TPU v7x, 32 devices: a whole 2x2x4 slice. The times are simulated.
32 devices in a mesh: groups: 2 (over y), blk: 4 (over z), tp: 4 (over x, core).
Axes of the slice: x: 2, y: 2, z: 4, core: 2. Of those that a mesh axis runs over, the one named last changes fastest.
Arguments:
- tokens: bfloat16 [3072, 4096], P(('groups', 'blk'), 'tp'), parts along dimension 0, may hold values from -6 to 6
- gate_weight: bfloat16 [4, 4096, 1024], P('blk', None, 'tp'), may hold values from -0.09375 to 0.09375
- up_weight: bfloat16 [4, 4096, 1024], P('blk', None, 'tp'), may hold values from -0.09375 to 0.09375
- down_weight: bfloat16 [4, 1024, 4096], P('blk', 'tp'), may hold values from -0.1875 to 0.1875
- route_gates: float32 [3072, 4], P(('groups', 'blk')), parts along dimension 0, may hold values from 0.1 to 1
- block_list: int32 [8, 4, 3], P(('groups', 'blk')), parts along dimension 0, may hold values from 0 to 2, as said below
- block_count: int32 [8, 4], P(('groups', 'blk')), parts along dimension 0, may hold values from 0 to 3, as said below
- owner_token: int32 [3072], P(('groups', 'blk')), parts along dimension 0, may hold values from 0 to 767, as said below
Outputs:
- combined: bfloat16 [1536, 4096], P(('groups', 'blk'), 'tp'), parts along dimension 0
There are 2 independent parts, one for each index of `groups`. A program takes and returns all parts, laid end to end along the dimension named above; an argument that names none is the same for every part. Nothing has to cross between parts.
Inputs may be any that keep to these rules, and one draw needn't show every extreme that they name: `block_list`: in each row of a device and offset the entries are the 3 block numbers, each once, the chosen ones first. `block_count`: every device has an offset at which all 3 of its blocks are chosen. `owner_token`: token t is owned by device t // 192; the rows of one device name tokens of one owner device at most 192 times, and each device's rows reach 192 for some owner.
All inputs are finite; a program needn't handle non-finite values.
Results may differ from a plain program's by a relative error of at most 0.011.
Values may be sent and summed in bfloat16 or wider, within the bound.
No kernel may reach another device: no remote copies, remote signals or barrier semaphores. Data moves between devices by JAX's collectives and lax.ppermute only.
A program may use at most 128 MiB of HBM per device.

v0:
```python
import jax
import jax.numpy as jnp
from jax import lax
from jax.sharding import PartitionSpec as P


def shifted(block, axis, distance):
    devices = range(lax.axis_size(axis))
    route = [((i - distance) % len(devices), i) for i in devices]
    return lax.ppermute(block, axis, route)


def on_device(
    tokens, gate_weight, up_weight, down_weight, route_gates, block_list, block_count, owner_token
):
    whole_rows = lax.all_gather(tokens, "tp", axis=1, tiled=True)
    row_count = whole_rows.shape[0]
    width = whole_rows.shape[1]
    offsets_all = block_list.shape[1]
    block_total = block_list.shape[2]
    block_size = row_count // block_total
    blocks = whole_rows.reshape(block_total, block_size, width)
    gate_blocks = route_gates.reshape(block_total, block_size, offsets_all)
    totals = jnp.zeros((block_total, block_size, width), jnp.float32)

    def apply(totals, weights, offset, block_id):
        w_gate, w_up, w_down = weights
        block_rows = lax.dynamic_index_in_dim(blocks, block_id, 0, keepdims=False)
        gate_out = jnp.dot(block_rows, w_gate, preferred_element_type=jnp.float32)
        up_out = jnp.dot(block_rows, w_up, preferred_element_type=jnp.float32)
        hidden = (jax.nn.silu(gate_out) * up_out).astype(jnp.bfloat16)
        block_gates = lax.dynamic_index_in_dim(gate_blocks, block_id, 0, keepdims=False)
        factor = lax.dynamic_index_in_dim(block_gates, offset, 1, keepdims=False)
        product = jnp.dot(hidden, w_down, preferred_element_type=jnp.float32) * factor[:, None]
        before = lax.dynamic_index_in_dim(totals, block_id, 0, keepdims=False)
        return lax.dynamic_update_index_in_dim(totals, before + product, block_id, 0)

    resident = (gate_weight[0], up_weight[0], down_weight[0])
    arrived = [resident]
    holding = resident
    for offset in range(1, offsets_all):
        holding = shifted((holding[0], holding[1], holding[2]), "blk", 1)
        arrived.append(holding)
    for offset in range(offsets_all):
        weights = arrived[offset]

        def visit_block(position, totals, weights=weights, offset=offset):
            return apply(totals, weights, offset, block_list[0, offset, position])

        totals = lax.fori_loop(0, block_count[0, offset], visit_block, totals)
    summed = lax.psum_scatter(
        totals.reshape(row_count, width).astype(jnp.bfloat16), "tp", scatter_dimension=1, tiled=True
    )
    feature_share = summed.shape[1]
    cycle_size = lax.axis_size("blk")
    owned = row_count // 2
    capacity = max(2, 2 * row_count // cycle_size)
    target = owner_token // owned
    local_token = owner_token % owned
    target_table = (target[:, None] == jnp.arange(cycle_size, dtype=jnp.int32)[None, :]).astype(
        jnp.int32
    )
    running = jnp.cumsum(target_table, axis=0)
    rank = jnp.sum((running - 1) * target_table, axis=1)
    slot = target * capacity + rank
    send_rows = jnp.zeros((cycle_size * capacity, feature_share), jnp.bfloat16).at[slot].set(summed)
    send_index = jnp.full((cycle_size * capacity,), -1, jnp.int32).at[slot].set(local_token)
    send_rows = send_rows.reshape(cycle_size, capacity, feature_share)
    send_index = send_index.reshape(cycle_size, capacity)
    got_rows, got_index = (
        lax.all_to_all(send_rows, "blk", split_axis=0, concat_axis=0, tiled=True),
        lax.all_to_all(send_index, "blk", split_axis=0, concat_axis=0, tiled=True),
    )
    got_rows = got_rows.reshape(cycle_size * capacity, feature_share)
    got_index = got_index.reshape(cycle_size * capacity)
    placing = (got_index[:, None] == jnp.arange(owned, dtype=jnp.int32)[None, :]).astype(
        jnp.bfloat16
    )
    combined = lax.dot_general(
        placing, got_rows, (((0,), (0,)), ((), ())), preferred_element_type=jnp.float32
    )
    return combined.astype(jnp.bfloat16)


def solution(mesh):
    return jax.shard_map(
        on_device,
        mesh=mesh,
        in_specs=(
            P(("groups", "blk"), "tp"),
            P("blk", None, "tp"),
            P("blk", None, "tp"),
            P("blk", "tp", None),
            P(("groups", "blk"), None),
            P(("groups", "blk"), None, None),
            P(("groups", "blk"), None),
            P(("groups", "blk")),
        ),
        out_specs=P(("groups", "blk"), "tp"),
        check_vma=False,
    )
```

profile of v0, /device:TPU:0, one launch (start us, length us, event | category | flops | bytes accessed | tf_op | source)
XLA Modules:
  0.0 555.3 jit_solution(1535682961444922162)
XLA Ops:
  13.5 45.6 %collective-permute-done = bf16[4096,256]{1,0:T(8,128)(2,1)} collective-permute-done((bf16[4096,256]{1,0:T(8,128)(2,1)}, bf16[4096,256]{1,0:T(8,128)(2,1)}, u32[]{:S(2)}, u32[]{:S(2)}) %collective-permute-start) | collective-permute-done | bytes 2097184 | tf_op jit(solution)/shard_map/ppermute | solution.py:10
  59.2 44.8 %collective-permute-done.1 = bf16[4096,256]{1,0:T(8,128)(2,1)S(1)} collective-permute-done((bf16[4096,256]{1,0:T(8,128)(2,1)}, bf16[4096,256]{1,0:T(8,128)(2,1)S(1)}, u32[]{:S(2)}, u32[]{:S(2)}) %collective-permute-start.1) | collective-permute-done | bytes 2097184 | tf_op jit(solution)/shard_map/ppermute | solution.py:10
  104.0 45.0 %collective-permute-done.2 = bf16[256,4096]{1,0:T(8,128)(2,1)} collective-permute-done((bf16[256,4096]{1,0:T(8,128)(2,1)}, bf16[256,4096]{1,0:T(8,128)(2,1)}, u32[]{:S(2)}, u32[]{:S(2)}) %collective-permute-start.2) | collective-permute-done | bytes 2097184 | tf_op jit(solution)/shard_map/ppermute | solution.py:10
  150.6 43.4 %collective-permute-done.3 = bf16[4096,256]{1,0:T(8,128)(2,1)} collective-permute-done((bf16[4096,256]{1,0:T(8,128)(2,1)}, bf16[4096,256]{1,0:T(8,128)(2,1)}, u32[]{:S(2)}, u32[]{:S(2)}) %collective-permute-start.3) | collective-permute-done | bytes 2097184 | tf_op jit(solution)/shard_map/ppermute | solution.py:10
  194.0 44.9 %collective-permute-done.4 = bf16[4096,256]{1,0:T(8,128)(2,1)} collective-permute-done((bf16[4096,256]{1,0:T(8,128)(2,1)S(1)}, bf16[4096,256]{1,0:T(8,128)(2,1)}, u32[]{:S(2)}, u32[]{:S(2)}) %collective-permute-start.4) | collective-permute-done | bytes 2097184 | tf_op jit(solution)/shard_map/ppermute | solution.py:10
  239.0 44.9 %collective-permute-done.5 = bf16[256,4096]{1,0:T(8,128)(2,1)} collective-permute-done((bf16[256,4096]{1,0:T(8,128)(2,1)}, bf16[256,4096]{1,0:T(8,128)(2,1)}, u32[]{:S(2)}, u32[]{:S(2)}) %collective-permute-start.5) | collective-permute-done | bytes 2097184 | tf_op jit(solution)/shard_map/ppermute | solution.py:10
  287.4 13.1 %while.40 = (s32[]{:T(128)}, f32[3,128,4096]{2,1,0:T(8,128)}, s32[]{:T(128)}, s32[1,4,3]{1,0,2:T(1,128)S(1)}, bf16[3,128,4096]{2,1,0:T(8,128)(2,1)S(1)}, /*index...) while((s32[]{:T(128)}, f32[3,128,4096]{2,1,0:T(8,128)}, ...), condition=%wide.region_5.6_spmd, body=%wide.region_4.5_spmd.sunk | while | flops 806551552 | bytes 25434860 | solution.py:50
  294.3 5.5 fusion.141
  300.4 28.6 %while.41 = (s32[]{:T(128)}, f32[3,128,4096]{2,1,0:T(8,128)}, s32[]{:T(128)}, s32[1,4,3]{1,0,2:T(1,128)S(1)}, bf16[3,128,4096]{2,1,0:T(8,128)(2,1)S(1)}, /*index...) while((s32[]{:T(128)}, f32[3,128,4096]{2,1,0:T(8,128)}, ...), condition=%wide.region_7.8_spmd, body=%wide.region_6.7_spmd.sunk | while | flops 806551552 | bytes 17046224 | solution.py:50
  308.9 5.5 fusion.148
  322.8 5.5 fusion.148
  329.0 42.1 %while.42 = (s32[]{:T(128)}, f32[3,128,4096]{2,1,0:T(8,128)}, s32[]{:T(128)}, s32[1,4,3]{1,0,2:T(1,128)S(1)}, bf16[3,128,4096]{2,1,0:T(8,128)(2,1)S(1)}, /*index...) while((s32[]{:T(128)}, f32[3,128,4096]{2,1,0:T(8,128)}, ...), condition=%wide.region_9.10_spmd, body=%wide.region_8.9_spmd.sunk | while | flops 806551552 | bytes 17046224 | solution.py:50
  337.4 5.5 fusion.155
  351.2 5.5 fusion.155
  365.1 5.5 fusion.155
  373.8 44.1 %collective-permute-done.8 = bf16[256,4096]{1,0:T(8,128)(2,1)} collective-permute-done((bf16[256,4096]{1,0:T(8,128)(2,1)}, bf16[256,4096]{1,0:T(8,128)(2,1)}, u32[]{:S(2)}, u32[]{:S(2)}) %collective-permute-start.8) | collective-permute-done | bytes 2097184 | tf_op jit(solution)/shard_map/ppermute | solution.py:10
  417.9 42.3 %while.43 = (s32[]{:T(128)}, f32[3,128,4096]{2,1,0:T(8,128)}, s32[]{:T(128)}, s32[1,4,3]{1,0,2:T(1,128)S(1)}, bf16[3,128,4096]{2,1,0:T(8,128)(2,1)S(1)}, /*index...) while((s32[]{:T(128)}, f32[3,128,4096]{2,1,0:T(8,128)}, ...), condition=%wide.region_11.12_spmd, body=%wide.region_10.11_spmd.sunk | while | flops 806551552 | bytes 17046224 | solution.py:50
  426.3 5.5 fusion.162
  440.2 5.5 fusion.162
  454.0 5.5 fusion.162
  460.2 4.9 convert_element_type.28
  474.6 26.9 %reduce-scatter.2.cloned.1.call-done = bf16[384,1024]{1,0:T(8,128)(2,1)} async-done(((bf16[384,4096]{1,0:T(8,128)(2,1)}), bf16[384,1024]{1,0:T(8,128)(2,1)}) %reduce-scatter.2.cloned.1.call-update) | async-done | bytes 786448 | tf_op jit(solution)/shard_map/reduce_scatter | solution.py:51
  505.4 4.6 all-to-all-start.1
  510.1 36.9 %all-to-all-done.1 = bf16[4,192,1024]{2,1,0:T(8,128)(2,1)S(1)} async-done(((bf16[4,192,1024]{2,1,0:T(8,128)(2,1)}), bf16[4,192,1024]{2,1,0:T(8,128)(2,1)S(1)}, u32[]{:S(2)}, u32[]{:S(2)}) %all-to-all-start.1) | async-done | bytes 1572896 | tf_op jit(solution)/shard_map/all_to_all | solution.py:71
  (91 shorter events, 80.4 us)
Async XLA Ops:
  6.5 277.4 %all-gather.2.cloned.1.call-start = ((), (), s32[]{:S(2)}) async-start(), calls=%async_computation.3 | async-start | bytes 3932160 | tf_op jit(solution)/shard_map/all_gather | solution.py:16
  7.3 494.2 %reduce-scatter.2.cloned.1.call-start = ((), (), s32[]{:S(2)}) async-start(), calls=%async_computation.4 | async-start | bytes 3932160 | tf_op jit(solution)/shard_map/reduce_scatter | solution.py:51
  7.3 51.9 %collective-permute-start = (bf16[4096,256]{1,0:T(8,128)(2,1)}, bf16[4096,256]{1,0:T(8,128)(2,1)}, u32[]{:S(2)}, u32[]{:S(2)}) collective-permute-start(bf16[4096,256]{1,0:T(8,128)(2,1)} %bitcast.178), channel_id=1, source_target_pairs={{12,0},{0,4},{4,8},{8,12},{13,1},{1,5},{5,9},{9,13},{14,2},{2,6},{... | collective-permute-start | bytes 6291464 | tf_op jit(solution)/shard_map/ppermute | solution.py:10
  10.4 93.6 %collective-permute-start.1 = (bf16[4096,256]{1,0:T(8,128)(2,1)}, bf16[4096,256]{1,0:T(8,128)(2,1)S(1)}, u32[]{:S(2)}, u32[]{:S(2)}) collective-permute-start(bf16[4096,256]{1,0:T(8,128)(2,1)} %bitcast.174), channel_id=1, source_target_pairs={{12,0},{0,4},{4,8},{8,12},{13,1},{1,5},{5,9},{9,13},{14,2},{2,6},{... | collective-permute-start | bytes 6291464 | tf_op jit(solution)/shard_map/ppermute | solution.py:10
  12.0 137.1 %collective-permute-start.2 = (bf16[256,4096]{1,0:T(8,128)(2,1)}, bf16[256,4096]{1,0:T(8,128)(2,1)}, u32[]{:S(2)}, u32[]{:S(2)}) collective-permute-start(bf16[256,4096]{1,0:T(8,128)(2,1)} %bitcast.176), channel_id=1, source_target_pairs={{12,0},{0,4},{4,8},{8,12},{13,1},{1,5},{5,9},{9,13},{14,2},{2,6},{... | collective-permute-start | bytes 6291464 | tf_op jit(solution)/shard_map/ppermute | solution.py:10
  59.2 134.8 %collective-permute-start.3 = (bf16[4096,256]{1,0:T(8,128)(2,1)}, bf16[4096,256]{1,0:T(8,128)(2,1)}, u32[]{:S(2)}, u32[]{:S(2)}) collective-permute-start(bf16[4096,256]{1,0:T(8,128)(2,1)} %collective-permute-done), channel_id=1, source_target_pairs={{12,0},{0,4},{4,8},{8,12},{13,1},{1,5},{5,9},{9,13},{14,2},{2,6},{... | collective-permute-start | bytes 6291464 | tf_op jit(solution)/shard_map/ppermute | solution.py:10
  104.0 179.9 %copy-start.1 = (bf16[4096,256]{1,0:T(8,128)(2,1)}, bf16[4096,256]{1,0:T(8,128)(2,1)S(1)}, u32[]{:S(2)}) copy-start(bf16[4096,256]{1,0:T(8,128)(2,1)S(1)} %collective-permute-done.1) | copy-start | bytes 6291460
  104.0 134.9 %collective-permute-start.4 = (bf16[4096,256]{1,0:T(8,128)(2,1)S(1)}, bf16[4096,256]{1,0:T(8,128)(2,1)}, u32[]{:S(2)}, u32[]{:S(2)}) collective-permute-start(bf16[4096,256]{1,0:T(8,128)(2,1)S(1)} %collective-permute-done.1), channel_id=1, source_target_pairs={{12,0},{0,4},{4,8},{8,12},{13,1},{1,5},{5,9},{9,13},{14,2},{2,6},{... | collective-permute-start | bytes 6291464 | tf_op jit(solution)/shard_map/ppermute | solution.py:10
  149.1 134.8 %collective-permute-start.5 = (bf16[256,4096]{1,0:T(8,128)(2,1)}, bf16[256,4096]{1,0:T(8,128)(2,1)}, u32[]{:S(2)}, u32[]{:S(2)}) collective-permute-start(bf16[256,4096]{1,0:T(8,128)(2,1)} %collective-permute-done.2), channel_id=1, source_target_pairs={{12,0},{0,4},{4,8},{8,12},{13,1},{1,5},{5,9},{9,13},{14,2},{2,6},{... | collective-permute-start | bytes 6291464 | tf_op jit(solution)/shard_map/ppermute | solution.py:10
  194.0 177.1 %collective-permute-start.6 = (bf16[4096,256]{1,0:T(8,128)(2,1)}, bf16[4096,256]{1,0:T(8,128)(2,1)}, u32[]{:S(2)}, u32[]{:S(2)}) collective-permute-start(bf16[4096,256]{1,0:T(8,128)(2,1)} %collective-permute-done.3), channel_id=1, source_target_pairs={{12,0},{0,4},{4,8},{8,12},{13,1},{1,5},{5,9},{9,13},{14,2},{2,6},{... | collective-permute-start | bytes 6291464 | tf_op jit(solution)/shard_map/ppermute | solution.py:10
  238.9 134.8 %collective-permute-start.7 = (bf16[4096,256]{1,0:T(8,128)(2,1)}, bf16[4096,256]{1,0:T(8,128)(2,1)}, u32[]{:S(2)}, u32[]{:S(2)}) collective-permute-start(bf16[4096,256]{1,0:T(8,128)(2,1)} %collective-permute-done.4), channel_id=1, source_target_pairs={{12,0},{0,4},{4,8},{8,12},{13,1},{1,5},{5,9},{9,13},{14,2},{2,6},{... | collective-permute-start | bytes 6291464 | tf_op jit(solution)/shard_map/ppermute | solution.py:10
  283.9 134.0 %collective-permute-start.8 = (bf16[256,4096]{1,0:T(8,128)(2,1)}, bf16[256,4096]{1,0:T(8,128)(2,1)}, u32[]{:S(2)}, u32[]{:S(2)}) collective-permute-start(bf16[256,4096]{1,0:T(8,128)(2,1)} %collective-permute-done.5), channel_id=1, source_target_pairs={{12,0},{0,4},{4,8},{8,12},{13,1},{1,5},{5,9},{9,13},{14,2},{2,6},{... | collective-permute-start | bytes 6291464 | tf_op jit(solution)/shard_map/ppermute | solution.py:10
  283.9 3.4 copy-start
  283.9 3.4 copy-start.3
  283.9 3.4 copy-start.5
  290.5 3.3 copy-start.2
  465.1 0.7 copy-start.4
  471.2 34.3 %all-to-all-start = ((s32[4,1,192]{2,1,0:T(1,128)}), s32[4,1,192]{2,1,0:T(1,128)S(1)}, u32[]{:S(2)}, u32[]{:S(2)}) async-start(s32[4,1,192]{2,1,0:T(1,128)} %all_to_all.9), calls=%async_computation | async-start | bytes 8192 | tf_op jit(solution)/shard_map/all_to_all | solution.py:72
  505.4 41.5 %all-to-all-start.1 = ((bf16[4,192,1024]{2,1,0:T(8,128)(2,1)}), bf16[4,192,1024]{2,1,0:T(8,128)(2,1)S(1)}, u32[]{:S(2)}, u32[]{:S(2)}) async-start(bf16[4,192,1024]{2,1,0:T(8,128)(2,1)} %bitcast.32), calls=%async_computation.2 | async-start | bytes 3145728 | tf_op jit(solution)/shard_map/all_to_all | solution.py:71
Sparse Core Ops, SparseCore 0:
  8.9 31.2 all-gather.1
  465.3 36.1 reduce-scatter.1
where the time goes:
time: 557 us; the launch traced here: 555 us
  waiting for transfers between devices  380 us (68%)
  matrix products  67.8 us (12%)
  local copies, waits for them, and re-layouts  47.4 us (9%)
  loops' own time  25.7 us (5%)
  starting transfers between devices  14.5 us (3%)
  between operations  13.5 us (2%)
  other arithmetic  6.49 us (1%)
    ppermute x9, waiting for transfers between devices, shifted(): return lax.ppermute(block, axis, route)  315 us
    dot_general x9, matrix products, apply(): jnp.dot(hidden, w_down, preferred_element_type=jnp.float32)  49.6 us
    all_to_all x1, waiting for transfers between devices, on_device(): lax.all_to_all(send_rows, 'blk', split_axis=0, concat_axis=0, tiled=True)  36.9 us
    dynamic_slice x9, local copies, waits for them, and re-layouts, apply(): before = lax.dynamic_index_in_dim(totals, block_id, 0, keepdims=False)  28.5 us
    reduce_scatter x1, waiting for transfers between devices, on_device(): lax.psum_scatter(totals.reshape(row_count, width).astype(jnp.bfloat16), '...  26.9 us
    another operation x4, loops' own time, on_device(): totals = lax.fori_loop(0, block_count[0, offset], visit_block, totals)  25.7 us
    dot_general x9, matrix products, apply(): gate_out = jnp.dot(block_rows, w_gate, preferred_element_type=jnp.float32)  16.7 us
  transfers between devices with their start and end apart: 13, of which 10 were waited for; matrix products, arithmetic and copies ran while one was open for 14% of the time, Pallas kernels for 0%

commit v1 on v0

--- a/solution.py
+++ b/solution.py
@@ -10,7 +10,7 @@
     return lax.ppermute(block, axis, route)
 
 
-def on_device(
+def weights_travel(
     tokens, gate_weight, up_weight, down_weight, route_gates, block_list, block_count, owner_token
 ):
     whole_rows = lax.all_gather(tokens, "tp", axis=1, tiled=True)
@@ -80,6 +80,123 @@
         placing, got_rows, (((0,), (0,)), ((), ())), preferred_element_type=jnp.float32
     )
     return combined.astype(jnp.bfloat16)
+
+
+BESIDE = [(0, 1), (1, 0), (2, 3), (3, 2)]
+MIDDLE = [(1, 2), (2, 1)]
+INWARD = [(0, 1), (3, 2)]
+OUTWARD = [(1, 0), (2, 3)]
+SLOT_POSITION = [[0, 1, 2, 3], [1, 0, 3, 2], [2, 2, 1, 1], [3, 3, 0, 0]]
+CHUNK_OWNER = [[3, 3, 0, 0], [2, 2, 1, 1], [1, 0, 3, 2], [0, 1, 2, 3]]
+
+
+def across_chips(block):
+    return lax.ppermute(block, "tp", [(i, i ^ 2) for i in range(4)])
+
+
+def across_cores(block):
+    return lax.ppermute(block, "tp", [(i, i ^ 1) for i in range(4)])
+
+
+def rows_travel(
+    tokens, gate_weight, up_weight, down_weight, route_gates, block_list, block_count, owner_token
+):
+    position = lax.axis_index("blk")
+    share = lax.axis_index("tp")
+    row_count, width = tokens.shape
+    units = gate_weight.shape[2]
+    offsets_all = block_list.shape[1]
+    block_total = block_list.shape[2]
+    owned = row_count // 2
+    inner = (position == 1) | (position == 2)
+
+    beside = lax.ppermute(tokens, "blk", BESIDE)
+    middle = lax.ppermute(tokens, "blk", MIDDLE)
+    inner_far = lax.ppermute(beside, "blk", MIDDLE)
+    outer_next = lax.ppermute(middle, "blk", OUTWARD)
+    outer_far = lax.ppermute(inner_far, "blk", OUTWARD)
+    slots = [
+        tokens,
+        beside,
+        jnp.where(inner, middle, outer_next),
+        jnp.where(inner, inner_far, outer_far),
+    ]
+
+    order = jnp.arange(block_total, dtype=jnp.int32)
+    valid = order[None, :, None] < block_count[0][:, None, None]
+    chosen = jnp.any(valid & (block_list[0][:, :, None] == order[None, None, :]), axis=1)
+    row_chosen = jnp.repeat(chosen.astype(jnp.float32), row_count // block_total, axis=1)
+    coef = route_gates.T * row_chosen
+    facts = jnp.concatenate(
+        [coef, jnp.broadcast_to(owner_token.astype(jnp.float32)[None], (4, row_count))], axis=0
+    )
+    facts = lax.all_gather(facts, "blk")
+
+    def by_arrival(weight):
+        quarters = weight.reshape(4, width, units)
+        return jnp.concatenate(
+            [lax.dynamic_index_in_dim(quarters, share ^ j, 0, keepdims=False) for j in range(4)]
+        )
+
+    w_gate = by_arrival(gate_weight[0])
+    w_up = by_arrival(up_weight[0])
+
+    pieces = [
+        lax.dynamic_slice_in_dim(down_weight[0], (share ^ j) * width, width, 1) for j in range(4)
+    ]
+    sibling = across_cores(jnp.concatenate([pieces[1], pieces[3]], axis=1))
+    w_down = jnp.concatenate([jnp.concatenate([pieces[0], pieces[2]], axis=1), sibling], axis=0)
+
+    token_of = (
+        jnp.asarray(CHUNK_OWNER, jnp.int32)[:, position][:, None] * owned
+        + jnp.arange(owned, dtype=jnp.int32)[None, :]
+    ).reshape(4 * owned)
+
+    collected = jnp.zeros((4 * owned, units), jnp.float32)
+    for index, near in enumerate(slots):
+        far = across_chips(near)
+        rows = jnp.concatenate([near, across_cores(near), far, across_cores(far)], axis=1)
+        gate_out = jnp.dot(rows, w_gate, preferred_element_type=jnp.float32)
+        up_out = jnp.dot(rows, w_up, preferred_element_type=jnp.float32)
+        hidden = (jax.nn.silu(gate_out) * up_out).astype(jnp.bfloat16)
+        source = jnp.asarray(SLOT_POSITION[index], jnp.int32)[position]
+        offset = (source - position) % offsets_all
+        facts_here = lax.dynamic_index_in_dim(facts, source, 0, keepdims=False)
+        factor = lax.dynamic_index_in_dim(facts_here, offset, 0, keepdims=False)
+        owner = facts_here[offsets_all].astype(jnp.int32)
+        placing = jnp.where(owner[None, :] == token_of[:, None], factor[None, :], 0.0)
+        collected = collected + jnp.dot(
+            placing.astype(jnp.bfloat16), hidden, preferred_element_type=jnp.float32
+        )
+    own_half = collected.astype(jnp.bfloat16)
+    both = jnp.concatenate([own_half, across_cores(own_half)], axis=1)
+
+    chunks = []
+    for index in range(4):
+        part = jnp.dot(
+            both[index * owned : (index + 1) * owned], w_down, preferred_element_type=jnp.float32
+        )
+        got = across_chips(part[:, width:].astype(jnp.bfloat16))
+        chunks.append(part[:, :width] + got.astype(jnp.float32))
+
+    def send(block, route):
+        return lax.ppermute(block.astype(jnp.bfloat16), "blk", route).astype(jnp.float32)
+
+    first_in = send(chunks[0], INWARD)
+    second_in = send(chunks[1], INWARD)
+    second_mid = send(chunks[0] + first_in, MIDDLE)
+    third_in = send(chunks[2], INWARD)
+    third_mid = send(chunks[1] + second_in, MIDDLE)
+    third_out = send(chunks[2] + second_mid, OUTWARD)
+    return (chunks[3] + third_in + third_mid + third_out).astype(jnp.bfloat16)
+
+
+def on_device(*args):
+    block_list = args[5]
+    sizes = (lax.axis_size("blk"), lax.axis_size("tp"), block_list.shape[1])
+    if sizes == (4, 4, 4):
+        return rows_travel(*args)
+    return weights_travel(*args)
 
 
 def solution(mesh):

time: 557 us -> 173 us (0.31)
  waiting for transfers between devices: 380 us -> 59.1 us
  local copies, waits for them, and re-layouts: 47.4 us -> 16.9 us
  matrix products: 67.8 us -> 41.4 us
  loops' own time: 25.7 us -> 0 us
  blocking collectives: 0 us -> 13.9 us
  starting transfers between devices: 14.5 us -> 28 us
    ppermute x9 -> x29, waiting for transfers between devices: 315 us -> 59.1 us  [the longest x8 18.7 us: across_chips(): return lax.ppermute(block, 'tp', [(i, i ^ 2) for i in range(4)])]
    all_to_all x2 -> x0, waiting for transfers between devices: 36.9 us -> none  [the longest x1 36.9 us: on_device(): lax.all_to_all(send_rows, 'blk', split_axis=0, concat_axis=0, tiled=True)]
    dynamic_slice x27 -> x5, local copies, waits for them, and re-layouts: 34 us -> 4.8 us  [the longest x1 2.92 us: rows_travel(): lax.dynamic_slice_in_dim(down_weight[0], (share ^ j) * width, width, 1)]
    reduce_scatter x1 -> x0, waiting for transfers between devices: 26.9 us -> none  [on_device(): lax.psum_scatter(totals.reshape(row_count, width).astype(jnp.bfloat16), '...]
    dot_general x19 -> x12, matrix products: 67.8 us -> 41.4 us  [the longest x4 20.4 us: rows_travel(): jnp.dot(placing.astype(jnp.bfloat16), hidden, preferred_element_type=jnp....]
    another operation x4 -> x0, loops' own time: 25.7 us -> none  [on_device(): totals = lax.fori_loop(0, block_count[0, offset], visit_block, totals)]
    ppermute x9 -> x29, starting transfers between devices: 6.41 us -> 28 us  [the longest x6 12.2 us: send(): lax.ppermute(block.astype(jnp.bfloat16), 'blk', route).astype(jnp.float32)]
    all_gather x0 -> x1, blocking collectives: none -> 13.9 us  [rows_travel(): facts = lax.all_gather(facts, 'blk')]
  transfers between devices with their start and end apart: 13 -> 29, of which waited for: 10 -> 10; matrix products, arithmetic and copies ran while one was open for 14% -> 34% of each run, Pallas kernels for 0% -> 0%
where the time goes in v1:
time: 173 us; the launch traced here: 172 us
  waiting for transfers between devices  59.1 us (34%)
  matrix products  41.4 us (24%)
  starting transfers between devices  28 us (16%)
  local copies, waits for them, and re-layouts  16.9 us (10%)
  blocking collectives  13.9 us (8%)
  between operations  8.33 us (5%)
  other arithmetic  4.23 us (2%)
    dot_general x4, matrix products, rows_travel(): jnp.dot(placing.astype(jnp.bfloat16), hidden, preferred_element_type=jnp....  20.4 us
    ppermute x8, waiting for transfers between devices, across_chips(): return lax.ppermute(block, 'tp', [(i, i ^ 2) for i in range(4)])  18.7 us
    ppermute x1, waiting for transfers between devices, rows_travel(): outer_far = lax.ppermute(inner_far, 'blk', OUTWARD)  17 us
    all_gather x1, blocking collectives, rows_travel(): facts = lax.all_gather(facts, 'blk')  13.9 us
    ppermute x6, starting transfers between devices, send(): lax.ppermute(block.astype(jnp.bfloat16), 'blk', route).astype(jnp.float32)  12.2 us
    ppermute x1, waiting for transfers between devices, rows_travel(): outer_next = lax.ppermute(middle, 'blk', OUTWARD)  10.9 us
    ppermute x6, waiting for transfers between devices, send(): lax.ppermute(block.astype(jnp.bfloat16), 'blk', route).astype(jnp.float32)  10.9 us
    unnamed x56, local copies, waits for them, and re-layouts  8.15 us
  transfers between devices with their start and end apart: 29, of which 10 were waited for; matrix products, arithmetic and copies ran while one was open for 34% of the time, Pallas kernels for 0%

profile of v1, /device:TPU:0, one launch (start us, length us, event | category | flops | bytes accessed | tf_op | source)
XLA Modules:
  0.0 171.8 jit_solution(2815446055601194304)
XLA Ops:
  0.5 2.5 %collective-permute-start.1 = (bf16[384,1024]{1,0:T(8,128)(2,1)}, bf16[384,1024]{1,0:T(8,128)(2,1)}, u32[]{:S(2)}, u32[]{:S(2)}) collective-permute-start(bf16[384,1024]{1,0:T(8,128)(2,1)} %param.13), channel_id=1, source_target_pairs={{0,2},{1,3},{2,0},{3,1},{4,6},{5,7},{6,4},{7,5},{8,10},{9,11},{10,... | collective-permute-start | bytes 2359304 | tf_op jit(solution)/shard_map/ppermute | solution.py:94
  6.1 2.9 %dynamic-slice_bitcast_fusion.3 = (bf16[256,1024]{1,0:T(8,128)(2,1)}, bf16[256,1024]{1,0:T(8,128)(2,1)}, bf16[256,1024]{1,0:T(8,128)(2,1)S(1)}, bf16[256,1024]{1,0:T(8,128)(2,1)S(1)}) fusion(bf16[1,256,4096]{2,1,0:T(8,128)(2,1)} %param.16, s32[]{:T(128)S(6)} %select_n.154, s32[]{:T(128)S(6)} %select_n.155, s32[]{:T(128)S(6)} %select_n.157, s32[]{:T(128)S(6)} %select_n.156), kind=kLoop, calls=%fused_computation.61 | loop fusion | bytes 4194320 | tf_op jit(solution)/shard_map/dynamic_slice | solution.py:145
  20.0 13.9 %all-gather = f32[32,384]{1,0:T(8,128)S(1)} all-gather(f32[8,384]{1,0:T(8,128)S(1)} %pad_maximum_fusion.20), channel_id=2, replica_groups=mesh['groups'=2,'blk'=4,'tp'=4] {'blk'}, dimensions={0}, use_global_device_ids=true | all-gather | bytes 61440 | tf_op jit(solution)/shard_map/all_gather | solution.py:133
  37.4 2.1 %constant_dynamic-update-slice_fusion.7 = bf16[384,4096]{1,0:T(8,128)(2,1)} fusion(bf16[384,1024]{1,0:T(8,128)(2,1)} %collective-permute-done.3), kind=kLoop, calls=%fused_computation.97 | loop fusion | bytes 1572864
  42.4 10.9 %collective-permute-done.8 = bf16[384,1024]{1,0:T(8,128)(2,1)S(1)} collective-permute-done((bf16[384,1024]{1,0:T(8,128)(2,1)}, bf16[384,1024]{1,0:T(8,128)(2,1)S(1)}, u32[]{:S(2)}, u32[]{:S(2)}) %collective-permute-start.8) | collective-permute-done | bytes 786464 | tf_op jit(solution)/shard_map/ppermute | solution.py:116
  56.6 3.5 %collective-permute-done.5 = bf16[384,1024]{1,0:T(8,128)(2,1)} collective-permute-done((bf16[384,1024]{1,0:T(8,128)(2,1)}, bf16[384,1024]{1,0:T(8,128)(2,1)}, u32[]{:S(2)}, u32[]{:S(2)}) %collective-permute-start.5) | collective-permute-done | bytes 786464 | tf_op jit(solution)/shard_map/ppermute | solution.py:94
  62.6 2.1 %constant_dynamic-update-slice_fusion.5 = bf16[384,4096]{1,0:T(8,128)(2,1)} fusion(bf16[384,4096]{1,0:T(8,128)(2,1)} %constant_dynamic-update-slice_fusion.6, bf16[384,1024]{1,0:T(8,128)(2,1)} %collective-permute-done.5), kind=kLoop, calls=%fused_computation.95 | loop fusion | bytes 1572864
  64.7 5.0 %fusion.5 = f32[768,256]{0,1:T(8,128)} fusion(bf16[384]{0:T(512)(128)(2,1)S(1)} %get-tuple-element.12, s32[384]{0:T(512)S(1)} %get-tuple-element.8, s32[768]{0:T(1024)S(1)} %add.167, f32[384,256]{1,0:T(8,128)} %fusion.81, bf16[384,4096]{1,0:T(8,128)(2,1)} %copy-done.16, bf16[1024,256]{1,0:T(8,128)(2,1)} %get-tuple-element.18, ...), kind=kOutput, calls=%fused_computation.37 | convolution fusion | flops 965869568 | bytes 6427904 | tf_op jit(solution)/shard_map/dot_general | solution.py:168
  69.7 17.0 %collective-permute-done.13 = bf16[384,1024]{1,0:T(8,128)(2,1)} collective-permute-done((bf16[384,1024]{1,0:T(8,128)(2,1)S(1)}, bf16[384,1024]{1,0:T(8,128)(2,1)}, u32[]{:S(2)}, u32[]{:S(2)}) %collective-permute-start.13) | collective-permute-done | bytes 786464 | tf_op jit(solution)/shard_map/ppermute | solution.py:117
  89.0 2.2 %constant_dynamic-update-slice_fusion.4 = bf16[384,4096]{1,0:T(8,128)(2,1)} fusion(bf16[384,4096]{1,0:T(8,128)(2,1)} %constant_dynamic-update-slice_fusion.5, bf16[384,1024]{1,0:T(8,128)(2,1)} %collective-permute-done.6), kind=kLoop, calls=%fused_computation.94 | loop fusion | bytes 1572864 | tf_op jit(solution)/shard_map/concatenate | solution.py:158
  91.2 3.7 %fusion.80 = f32[384,256]{1,0:T(8,128)} fusion(bf16[384,4096]{1,0:T(8,128)(2,1)} %constant_dynamic-update-slice_fusion.4, bf16[1024,256]{1,0:T(8,128)(2,1)S(1)} %copy-done.9, bf16[1024,256]{1,0:T(8,128)(2,1)S(1)} %copy-done.11, bf16[1024,256]{1,0:T(8,128)(2,1)S(1)} %copy-done.13, bf16[1024,256]{1,0:T(8,128)(2,1)S(1)} %copy-done.6), kind=kOutput, calls=%fused_computation.147 | convolution fusion | flops 813694976 | bytes 5636096 | tf_op jit(solution)/shard_map/dot_general | solution.py:159
  94.9 5.3 %convolution_add_fusion.2 = f32[768,256]{0,1:T(8,128)} fusion(f32[768,256]{0,1:T(8,128)} %fusion.5, bf16[384]{0:T(512)(128)(2,1)S(1)} %get-tuple-element.11, s32[384]{0:T(512)S(1)} %get-tuple-element.7, s32[768]{0:T(1024)S(1)} %add.167, f32[384,256]{1,0:T(8,128)} %fusion.80, bf16[384,4096]{1,0:T(8,128)(2,1)} %constant_dynamic-update-slice_fusion.4, ...), kind=kOutput, calls=%fused_computation.7 | convolution fusion | flops 966066176 | bytes 7214336 | tf_op jit(solution)/shard_map/dot_general | solution.py:168
  100.2 2.8 %collective-permute-done.15 = bf16[384,1024]{1,0:T(8,128)(2,1)} collective-permute-done((bf16[384,1024]{1,0:T(8,128)(2,1)S(1)}, bf16[384,1024]{1,0:T(8,128)(2,1)}, u32[]{:S(2)}, u32[]{:S(2)}) %collective-permute-start.15) | collective-permute-done | bytes 786464 | tf_op jit(solution)/shard_map/ppermute | solution.py:94
  103.1 4.0 %fusion.24 = f32[384,256]{1,0:T(8,128)} fusion(bf16[384,1024]{1,0:T(8,128)(2,1)} %collective-permute-done.11, bf16[384,1024]{1,0:T(8,128)(2,1)} %collective-permute-done.10, bf16[384,1024]{1,0:T(8,128)(2,1)} %collective-permute-done.9, bf16[384,1024]{1,0:T(8,128)(2,1)S(1)} %broadcast_select_fusion.1, bf16[1024,256]{1,0:T(8,128)(2,1)} %get-tuple-element.18, ...), kind=kOutput, calls=%fused_computation.56 | convolution fusion | flops 826277888 | bytes 5636096 | tf_op jit(solution)/shard_map/dot_general | solution.py:160
  107.0 5.1 %convolution_add_fusion.1 = f32[768,256]{0,1:T(8,128)} fusion(f32[768,256]{0,1:T(8,128)} %convolution_add_fusion.2, bf16[384]{0:T(512)(128)(2,1)S(1)} %get-tuple-element.10, s32[384]{0:T(512)S(1)} %get-tuple-element.6, s32[768]{0:T(1024)S(1)} %add.167, f32[384,256]{1,0:T(8,128)} %fusion.24, bf16[384,1024]{1,0:T(8,128)(2,1)} %collective-permute-done.11, ...), kind=kOutput, calls=%fused_computation.6 | convolution fusion | flops 978649088 | bytes 7214336 | tf_op jit(solution)/shard_map/dot_general | solution.py:168
  112.1 4.0 %fusion.22 = f32[384,256]{1,0:T(8,128)} fusion(bf16[384,1024]{1,0:T(8,128)(2,1)} %collective-permute-done.16, bf16[384,1024]{1,0:T(8,128)(2,1)} %collective-permute-done.15, bf16[384,1024]{1,0:T(8,128)(2,1)} %collective-permute-done.14, bf16[384,1024]{1,0:T(8,128)(2,1)S(1)} %broadcast_select_fusion, bf16[1024,256]{1,0:T(8,128)(2,1)} %get-tuple-element.18, ...), kind=kOutput, calls=%fused_computation.54 | convolution fusion | flops 826277888 | bytes 5636096 | tf_op jit(solution)/shard_map/dot_general | solution.py:160
  116.1 5.0 %fusion = bf16[768,256]{0,1:T(8,128)(2,1)} fusion(f32[768,256]{0,1:T(8,128)} %convolution_add_fusion.1, bf16[384]{0:T(512)(128)(2,1)S(1)} %get-tuple-element.9, s32[384]{0:T(512)S(1)} %get-tuple-element.5, s32[768]{0:T(1024)S(1)} %add.167, f32[384,256]{1,0:T(8,128)} %fusion.22, bf16[384,1024]{1,0:T(8,128)(2,1)} %collective-permute-done.16, ...), kind=kOutput, calls=%fused_computation.8 | convolution fusion | flops 978845696 | bytes 6821120 | tf_op jit(solution)/shard_map/dot_general | solution.py:168
  123.2 1.9 %fusion.38 = f32[192,2048]{1,0:T(8,128)S(1)} fusion(bf16[768,256]{0,1:T(8,128)(2,1)S(1)} %collective-permute-done.17, bf16[768,256]{0,1:T(8,128)(2,1)} %fusion, bf16[256,2048]{1,0:T(8,128)(2,1)} %collective-permute-done.18, bf16[256,1024]{1,0:T(8,128)(2,1)S(1)} %copy-done.4, bf16[256,1024]{1,0:T(8,128)(2,1)S(1)} %copy-done.3), kind=kOutput, calls=%fused_computation.84 | convolution fusion | flops 409337856 | bytes 4456448 | tf_op jit(solution)/shard_map/dot_general | solution.py:176
  125.8 1.9 %fusion.30 = f32[192,2048]{1,0:T(8,128)S(1)} fusion(bf16[768,256]{0,1:T(8,128)(2,1)S(1)} %copy-done.20, bf16[768,256]{0,1:T(8,128)(2,1)S(1)} %collective-permute-done.17, bf16[256,2048]{1,0:T(8,128)(2,1)} %collective-permute-done.18, bf16[256,1024]{1,0:T(8,128)(2,1)S(1)} %copy-done.4, bf16[256,1024]{1,0:T(8,128)(2,1)S(1)} %copy-done.3), kind=kOutput, calls=%fused_computation.78 | convolution fusion | flops 409337856 | bytes 4456448 | tf_op jit(solution)/shard_map/dot_general | solution.py:176
  129.3 7.9 %collective-permute-done.25 = bf16[192,1024]{1,0:T(8,128)(2,1)S(1)} collective-permute-done((bf16[192,1024]{1,0:T(8,128)(2,1)S(1)}, bf16[192,1024]{1,0:T(8,128)(2,1)S(1)}, u32[]{:S(2)}, u32[]{:S(2)}) %collective-permute-start.25) | collective-permute-done | bytes 393248 | tf_op jit(solution)/shard_map/ppermute | solution.py:94
  141.1 4.5 %collective-permute-done.22 = bf16[192,1024]{1,0:T(8,128)(2,1)S(1)} collective-permute-done((bf16[192,1024]{1,0:T(8,128)(2,1)S(1)}, bf16[192,1024]{1,0:T(8,128)(2,1)S(1)}, u32[]{:S(2)}, u32[]{:S(2)}) %collective-permute-start.22) | collective-permute-done | bytes 393248 | tf_op jit(solution)/shard_map/ppermute | solution.py:94
  150.5 4.3 %collective-permute-done.23 = bf16[192,1024]{1,0:T(8,128)(2,1)S(1)} collective-permute-done((bf16[192,1024]{1,0:T(8,128)(2,1)S(1)}, bf16[192,1024]{1,0:T(8,128)(2,1)S(1)}, u32[]{:S(2)}, u32[]{:S(2)}) %collective-permute-start.23) | collective-permute-done | bytes 393248 | tf_op jit(solution)/shard_map/ppermute | solution.py:183
  157.3 6.9 %collective-permute-start.21 = (bf16[192,1024]{1,0:T(8,128)(2,1)S(1)}, bf16[192,1024]{1,0:T(8,128)(2,1)S(1)}, u32[]{:S(2)}, u32[]{:S(2)}) collective-permute-start(bf16[192,1024]{1,0:T(8,128)(2,1)S(1)} %get-tuple-element.25), channel_id=1, source_target_pairs={{0,4},{12,8},{1,5},{13,9},{2,6},{14,10},{3,7},{15,11},{16,20},{28,... | collective-permute-start | bytes 1179656 | tf_op jit(solution)/shard_map/ppermute | solution.py:183
  164.2 5.4 %collective-permute-done.28 = bf16[192,1024]{1,0:T(8,128)(2,1)S(1)} collective-permute-done((bf16[192,1024]{1,0:T(8,128)(2,1)S(1)}, bf16[192,1024]{1,0:T(8,128)(2,1)S(1)}, u32[]{:S(2)}, u32[]{:S(2)}) %collective-permute-start.28) | collective-permute-done | bytes 393248 | tf_op jit(solution)/shard_map/ppermute | solution.py:183
  (138 shorter events, 38.7 us)
Async XLA Ops:
  0.0 39.5 %collective-permute-start = (bf16[384,1024]{1,0:T(8,128)(2,1)}, bf16[384,1024]{1,0:T(8,128)(2,1)}, u32[]{:S(2)}, u32[]{:S(2)}) collective-permute-start(bf16[384,1024]{1,0:T(8,128)(2,1)} %param.13), channel_id=1, source_target_pairs={{0,1},{1,0},{2,3},{3,2},{4,5},{5,4},{6,7},{7,6},{8,9},{9,8},{10,11... | collective-permute-start | bytes 2359304 | tf_op jit(solution)/shard_map/ppermute | solution.py:98
  0.5 36.3 %collective-permute-start.1 = (bf16[384,1024]{1,0:T(8,128)(2,1)}, bf16[384,1024]{1,0:T(8,128)(2,1)}, u32[]{:S(2)}, u32[]{:S(2)}) collective-permute-start(bf16[384,1024]{1,0:T(8,128)(2,1)} %param.13), channel_id=1, source_target_pairs={{0,2},{1,3},{2,0},{3,1},{4,6},{5,7},{6,4},{7,5},{8,10},{9,11},{10,... | collective-permute-start | bytes 2359304 | tf_op jit(solution)/shard_map/ppermute | solution.py:94
  2.9 34.3 %collective-permute-start.3 = (bf16[384,1024]{1,0:T(8,128)(2,1)}, bf16[384,1024]{1,0:T(8,128)(2,1)}, u32[]{:S(2)}, u32[]{:S(2)}) collective-permute-start(bf16[384,1024]{1,0:T(8,128)(2,1)} %param.13), channel_id=1, source_target_pairs={{0,4},{4,0},{8,12},{12,8},{1,5},{5,1},{9,13},{13,9},{2,6},{6,2},{1... | collective-permute-start | bytes 2359304 | tf_op jit(solution)/shard_map/ppermute | solution.py:113
  4.5 29.5 %collective-permute-start.7 = (bf16[384,1024]{1,0:T(8,128)(2,1)}, bf16[384,1024]{1,0:T(8,128)(2,1)}, u32[]{:S(2)}, u32[]{:S(2)}) collective-permute-start(bf16[384,1024]{1,0:T(8,128)(2,1)} %param.13), channel_id=1, source_target_pairs={{4,8},{8,4},{5,9},{9,5},{6,10},{10,6},{7,11},{11,7},{20,24},{24,20... | collective-permute-start | bytes 2359304 | tf_op jit(solution)/shard_map/ppermute | solution.py:114
  9.1 112.5 %collective-permute-start.18 = (bf16[256,2048]{1,0:T(8,128)(2,1)S(1)}, bf16[256,2048]{1,0:T(8,128)(2,1)}, u32[]{:S(2)}, u32[]{:S(2)}) collective-permute-start(bf16[256,2048]{1,0:T(8,128)(2,1)S(1)} %pad_maximum_fusion.5), channel_id=1, source_target_pairs={{0,1},{1,0},{2,3},{3,2},{4,5},{5,4},{6,7},{7,6},{8,9},{9,8},{10,11... | collective-permute-start | bytes 3145736 | tf_op jit(solution)/shard_map/ppermute | solution.py:98
  34.0 19.3 %collective-permute-start.8 = (bf16[384,1024]{1,0:T(8,128)(2,1)}, bf16[384,1024]{1,0:T(8,128)(2,1)S(1)}, u32[]{:S(2)}, u32[]{:S(2)}) collective-permute-start(bf16[384,1024]{1,0:T(8,128)(2,1)} %collective-permute-done.7), channel_id=1, source_target_pairs={{4,0},{8,12},{5,1},{9,13},{6,2},{10,14},{7,3},{11,15},{20,16},{24,... | collective-permute-start | bytes 2359304 | tf_op jit(solution)/shard_map/ppermute | solution.py:116
  36.7 17.4 %collective-permute-start.2 = (bf16[384,1024]{1,0:T(8,128)(2,1)}, bf16[384,1024]{1,0:T(8,128)(2,1)S(1)}, u32[]{:S(2)}, u32[]{:S(2)}) collective-permute-start(bf16[384,1024]{1,0:T(8,128)(2,1)} %collective-permute-done.1), channel_id=1, source_target_pairs={{0,1},{1,0},{2,3},{3,2},{4,5},{5,4},{6,7},{7,6},{8,9},{9,8},{10,11... | collective-permute-start | bytes 2359304 | tf_op jit(solution)/shard_map/ppermute | solution.py:98
  37.3 19.3 %collective-permute-start.4 = (bf16[384,1024]{1,0:T(8,128)(2,1)}, bf16[384,1024]{1,0:T(8,128)(2,1)S(1)}, u32[]{:S(2)}, u32[]{:S(2)}) collective-permute-start(bf16[384,1024]{1,0:T(8,128)(2,1)} %collective-permute-done.3), channel_id=1, source_target_pairs={{0,1},{1,0},{2,3},{3,2},{4,5},{5,4},{6,7},{7,6},{8,9},{9,8},{10,11... | collective-permute-start | bytes 2359304 | tf_op jit(solution)/shard_map/ppermute | solution.py:98
  39.5 20.7 %collective-permute-start.5 = (bf16[384,1024]{1,0:T(8,128)(2,1)}, bf16[384,1024]{1,0:T(8,128)(2,1)}, u32[]{:S(2)}, u32[]{:S(2)}) collective-permute-start(bf16[384,1024]{1,0:T(8,128)(2,1)} %collective-permute-done.3), channel_id=1, source_target_pairs={{0,2},{1,3},{2,0},{3,1},{4,6},{5,7},{6,4},{7,5},{8,10},{9,11},{10,... | collective-permute-start | bytes 2359304 | tf_op jit(solution)/shard_map/ppermute | solution.py:94
  54.1 34.4 %collective-permute-start.10 = (bf16[384,1024]{1,0:T(8,128)(2,1)S(1)}, bf16[384,1024]{1,0:T(8,128)(2,1)}, u32[]{:S(2)}, u32[]{:S(2)}) collective-permute-start(bf16[384,1024]{1,0:T(8,128)(2,1)S(1)} %broadcast_select_fusion.1), channel_id=1, source_target_pairs={{0,2},{1,3},{2,0},{3,1},{4,6},{5,7},{6,4},{7,5},{8,10},{9,11},{10,... | collective-permute-start | bytes 2359304 | tf_op jit(solution)/shard_map/ppermute | solution.py:94
  56.6 46.5 %collective-permute-start.9 = (bf16[384,1024]{1,0:T(8,128)(2,1)S(1)}, bf16[384,1024]{1,0:T(8,128)(2,1)}, u32[]{:S(2)}, u32[]{:S(2)}) collective-permute-start(bf16[384,1024]{1,0:T(8,128)(2,1)S(1)} %broadcast_select_fusion.1), channel_id=1, source_target_pairs={{0,1},{1,0},{2,3},{3,2},{4,5},{5,4},{6,7},{7,6},{8,9},{9,8},{10,11... | collective-permute-start | bytes 2359304 | tf_op jit(solution)/shard_map/ppermute | solution.py:98
  60.1 28.4 %collective-permute-start.6 = (bf16[384,1024]{1,0:T(8,128)(2,1)}, bf16[384,1024]{1,0:T(8,128)(2,1)}, u32[]{:S(2)}, u32[]{:S(2)}) collective-permute-start(bf16[384,1024]{1,0:T(8,128)(2,1)} %collective-permute-done.5), channel_id=1, source_target_pairs={{0,1},{1,0},{2,3},{3,2},{4,5},{5,4},{6,7},{7,6},{8,9},{9,8},{10,11... | collective-permute-start | bytes 2359304 | tf_op jit(solution)/shard_map/ppermute | solution.py:98
  60.1 26.6 %collective-permute-start.13 = (bf16[384,1024]{1,0:T(8,128)(2,1)S(1)}, bf16[384,1024]{1,0:T(8,128)(2,1)}, u32[]{:S(2)}, u32[]{:S(2)}) collective-permute-start(bf16[384,1024]{1,0:T(8,128)(2,1)S(1)} %collective-permute-done.12), channel_id=1, source_target_pairs={{4,0},{8,12},{5,1},{9,13},{6,2},{10,14},{7,3},{11,15},{20,16},{24,... | collective-permute-start | bytes 2359304 | tf_op jit(solution)/shard_map/ppermute | solution.py:117
  87.9 15.1 %collective-permute-start.15 = (bf16[384,1024]{1,0:T(8,128)(2,1)S(1)}, bf16[384,1024]{1,0:T(8,128)(2,1)}, u32[]{:S(2)}, u32[]{:S(2)}) collective-permute-start(bf16[384,1024]{1,0:T(8,128)(2,1)S(1)} %broadcast_select_fusion), channel_id=1, source_target_pairs={{0,2},{1,3},{2,0},{3,1},{4,6},{5,7},{6,4},{7,5},{8,10},{9,11},{10,... | collective-permute-start | bytes 2359304 | tf_op jit(solution)/shard_map/ppermute | solution.py:94
  88.5 23.6 %collective-permute-start.14 = (bf16[384,1024]{1,0:T(8,128)(2,1)S(1)}, bf16[384,1024]{1,0:T(8,128)(2,1)}, u32[]{:S(2)}, u32[]{:S(2)}) collective-permute-start(bf16[384,1024]{1,0:T(8,128)(2,1)S(1)} %broadcast_select_fusion), channel_id=1, source_target_pairs={{0,1},{1,0},{2,3},{3,2},{4,5},{5,4},{6,7},{7,6},{8,9},{9,8},{10,11... | collective-permute-start | bytes 2359304 | tf_op jit(solution)/shard_map/ppermute | solution.py:98
  88.5 14.5 %collective-permute-start.11 = (bf16[384,1024]{1,0:T(8,128)(2,1)}, bf16[384,1024]{1,0:T(8,128)(2,1)}, u32[]{:S(2)}, u32[]{:S(2)}) collective-permute-start(bf16[384,1024]{1,0:T(8,128)(2,1)} %collective-permute-done.10), channel_id=1, source_target_pairs={{0,1},{1,0},{2,3},{3,2},{4,5},{5,4},{6,7},{7,6},{8,9},{9,8},{10,11... | collective-permute-start | bytes 2359304 | tf_op jit(solution)/shard_map/ppermute | solution.py:98
  125.2 12.0 %collective-permute-start.25 = (bf16[192,1024]{1,0:T(8,128)(2,1)S(1)}, bf16[192,1024]{1,0:T(8,128)(2,1)S(1)}, u32[]{:S(2)}, u32[]{:S(2)}) collective-permute-start(bf16[192,1024]{1,0:T(8,128)(2,1)S(1)} %slice.138), channel_id=1, source_target_pairs={{0,2},{1,3},{2,0},{3,1},{4,6},{5,7},{6,4},{7,5},{8,10},{9,11},{10,... | collective-permute-start | bytes 1179656 | tf_op jit(solution)/shard_map/ppermute | solution.py:94
  127.8 17.8 %collective-permute-start.22 = (bf16[192,1024]{1,0:T(8,128)(2,1)S(1)}, bf16[192,1024]{1,0:T(8,128)(2,1)S(1)}, u32[]{:S(2)}, u32[]{:S(2)}) collective-permute-start(bf16[192,1024]{1,0:T(8,128)(2,1)S(1)} %slice.139), channel_id=1, source_target_pairs={{0,2},{1,3},{2,0},{3,1},{4,6},{5,7},{6,4},{7,5},{8,10},{9,11},{10,... | collective-permute-start | bytes 1179656 | tf_op jit(solution)/shard_map/ppermute | solution.py:94
  137.3 9.8 %collective-permute-start.26 = (bf16[192,1024]{1,0:T(8,128)(2,1)S(1)}, bf16[192,1024]{1,0:T(8,128)(2,1)S(1)}, u32[]{:S(2)}, u32[]{:S(2)}) collective-permute-start(bf16[192,1024]{1,0:T(8,128)(2,1)S(1)} %fusion.28), channel_id=1, source_target_pairs={{0,4},{12,8},{1,5},{13,9},{2,6},{14,10},{3,7},{15,11},{16,20},{28,... | collective-permute-start | bytes 1179656 | tf_op jit(solution)/shard_map/ppermute | solution.py:183
  140.5 15.2 %collective-permute-start.20 = (bf16[192,1024]{1,0:T(8,128)(2,1)S(1)}, bf16[192,1024]{1,0:T(8,128)(2,1)S(1)}, u32[]{:S(2)}, u32[]{:S(2)}) collective-permute-start(bf16[192,1024]{1,0:T(8,128)(2,1)S(1)} %slice.140), channel_id=1, source_target_pairs={{0,2},{1,3},{2,0},{3,1},{4,6},{5,7},{6,4},{7,5},{8,10},{9,11},{10,... | collective-permute-start | bytes 1179656 | tf_op jit(solution)/shard_map/ppermute | solution.py:94
  149.9 14.3 %collective-permute-start.19 = (bf16[192,1024]{1,0:T(8,128)(2,1)S(1)}, bf16[192,1024]{1,0:T(8,128)(2,1)S(1)}, u32[]{:S(2)}, u32[]{:S(2)}) collective-permute-start(bf16[192,1024]{1,0:T(8,128)(2,1)S(1)} %slice.141), channel_id=1, source_target_pairs={{0,2},{1,3},{2,0},{3,1},{4,6},{5,7},{6,4},{7,5},{8,10},{9,11},{10,... | collective-permute-start | bytes 1179656 | tf_op jit(solution)/shard_map/ppermute | solution.py:94
  155.0 9.2 %collective-permute-start.24 = (bf16[192,1024]{1,0:T(8,128)(2,1)S(1)}, bf16[192,1024]{1,0:T(8,128)(2,1)S(1)}, u32[]{:S(2)}, u32[]{:S(2)}) collective-permute-start(bf16[192,1024]{1,0:T(8,128)(2,1)S(1)} %add_convert_fusion.2), channel_id=1, source_target_pairs={{4,8},{8,4},{5,9},{9,5},{6,10},{10,6},{7,11},{11,7},{20,24},{24,20... | collective-permute-start | bytes 1179656 | tf_op jit(solution)/shard_map/ppermute | solution.py:183
  156.0 13.6 %collective-permute-start.28 = (bf16[192,1024]{1,0:T(8,128)(2,1)S(1)}, bf16[192,1024]{1,0:T(8,128)(2,1)S(1)}, u32[]{:S(2)}, u32[]{:S(2)}) collective-permute-start(bf16[192,1024]{1,0:T(8,128)(2,1)S(1)} %get-tuple-element.26), channel_id=1, source_target_pairs={{4,0},{8,12},{5,1},{9,13},{6,2},{10,14},{7,3},{11,15},{20,16},{24,... | collective-permute-start | bytes 1179656 | tf_op jit(solution)/shard_map/ppermute | solution.py:183
  157.3 13.5 %collective-permute-start.21 = (bf16[192,1024]{1,0:T(8,128)(2,1)S(1)}, bf16[192,1024]{1,0:T(8,128)(2,1)S(1)}, u32[]{:S(2)}, u32[]{:S(2)}) collective-permute-start(bf16[192,1024]{1,0:T(8,128)(2,1)S(1)} %get-tuple-element.25), channel_id=1, source_target_pairs={{0,4},{12,8},{1,5},{13,9},{2,6},{14,10},{3,7},{15,11},{16,20},{28,... | collective-permute-start | bytes 1179656 | tf_op jit(solution)/shard_map/ppermute | solution.py:183
  (30 other events, 344.4 us)

commit v2 on v1

--- a/solution.py
+++ b/solution.py
@@ -1,6 +1,8 @@
 import jax
 import jax.numpy as jnp
 from jax import lax
+from jax.experimental import pallas as pl
+from jax.experimental.pallas import tpu as pltpu
 from jax.sharding import PartitionSpec as P
 
 
@@ -98,6 +100,86 @@
     return lax.ppermute(block, "tp", [(i, i ^ 1) for i in range(4)])
 
 
+def all_there(*arrays):
+    anywhere = [pl.BlockSpec(memory_space=pl.ANY)] * len(arrays)
+    return pl.pallas_call(
+        lambda *refs: None,
+        out_shape=[jax.ShapeDtypeStruct(a.shape, a.dtype) for a in arrays],
+        in_specs=anywhere,
+        out_specs=anywhere,
+        input_output_aliases={i: i for i in range(len(arrays))},
+    )(*arrays)
+
+
+def collected_rows(owned, owners, sums, got, pair, before, chunk):
+    width = sums.shape[1]
+    quarter = width // 4
+    other = got[...].astype(jnp.float32)
+    swapped = [other[:, (k ^ 1) * quarter : ((k ^ 1) + 1) * quarter] for k in range(4)]
+    gate = sums[:, : width // 2] + jnp.concatenate(swapped[:2], axis=1)
+    up = sums[:, width // 2 :] + jnp.concatenate(swapped[2:], axis=1)
+    hidden = (gate / (1.0 + jnp.exp(-gate)) * up).astype(jnp.bfloat16)
+    factor, owner = pair[0:1, :], pair[1:2, :].astype(jnp.int32)
+    results = []
+    for index in range(chunk):
+        token = owners[index] * owned + lax.broadcasted_iota(jnp.int32, (owned, 1), 0)
+        placing = jnp.where(owner == token, factor, 0.0).astype(jnp.bfloat16)
+        rows = jnp.dot(placing, hidden, preferred_element_type=jnp.float32)
+        if before is not None:
+            rows = rows + before[index * owned : (index + 1) * owned, :]
+        results.append(rows)
+    return results
+
+
+def collect(owned, owners, sums, got, pair, before):
+    chunks = owners.shape[0]
+    vmem = pl.BlockSpec(memory_space=pltpu.VMEM)
+    operands = [owners, sums, got, pair] + ([] if before is None else [before])
+
+    def body(owners_ref, sums_ref, got_ref, pair_ref, *rest):
+        before_ref = rest[0] if before is not None else None
+        rows = collected_rows(
+            owned, owners_ref, sums_ref, got_ref, pair_ref, before_ref, chunks
+        )
+        for index in range(chunks):
+            rest[-1][index * owned : (index + 1) * owned, :] = rows[index]
+
+    return pl.pallas_call(
+        body,
+        out_shape=jax.ShapeDtypeStruct((chunks * owned, sums.shape[1] // 2), jnp.float32),
+        in_specs=[pl.BlockSpec(memory_space=pltpu.SMEM)] + [vmem] * (len(operands) - 1),
+        out_specs=vmem,
+        compiler_params=pltpu.CompilerParams(vmem_limit_bytes=40 * 2**20),
+    )(*operands)
+
+
+def finish(owned, owners, sums, got, pair, before, w_down):
+    chunks = owners.shape[0]
+    width = w_down.shape[1] // 2
+    vmem = pl.BlockSpec(memory_space=pltpu.VMEM)
+
+    def body(owners_ref, sums_ref, got_ref, pair_ref, before_ref, w_ref, *out_refs):
+        rows = collected_rows(
+            owned, owners_ref, sums_ref, got_ref, pair_ref, before_ref, chunks
+        )
+        for index in range(chunks):
+            held = rows[index].astype(jnp.bfloat16)
+            keep = jnp.dot(held, w_ref[:, :width], preferred_element_type=jnp.float32)
+            sent = jnp.dot(held, w_ref[:, width:], preferred_element_type=jnp.float32)
+            out_refs[index][...] = sent.astype(jnp.bfloat16)
+            out_refs[chunks + index][...] = keep
+
+    results = pl.pallas_call(
+        body,
+        out_shape=[jax.ShapeDtypeStruct((owned, width), jnp.bfloat16)] * chunks
+        + [jax.ShapeDtypeStruct((owned, width), jnp.float32)] * chunks,
+        in_specs=[pl.BlockSpec(memory_space=pltpu.SMEM)] + [vmem] * 5,
+        out_specs=[vmem] * (2 * chunks),
+        compiler_params=pltpu.CompilerParams(vmem_limit_bytes=40 * 2**20),
+    )(owners, sums, got, pair, before, w_down)
+    return results[:chunks], results[chunks:]
+
+
 def rows_travel(
     tokens, gate_weight, up_weight, down_weight, route_gates, block_list, block_count, owner_token
 ):
@@ -108,76 +190,106 @@
     offsets_all = block_list.shape[1]
     block_total = block_list.shape[2]
     owned = row_count // 2
+    half = row_count // 2
     inner = (position == 1) | (position == 2)
 
     beside = lax.ppermute(tokens, "blk", BESIDE)
     middle = lax.ppermute(tokens, "blk", MIDDLE)
-    inner_far = lax.ppermute(beside, "blk", MIDDLE)
-    outer_next = lax.ppermute(middle, "blk", OUTWARD)
-    outer_far = lax.ppermute(inner_far, "blk", OUTWARD)
-    slots = [
-        tokens,
-        beside,
-        jnp.where(inner, middle, outer_next),
-        jnp.where(inner, inner_far, outer_far),
-    ]
+    own_far = across_chips(tokens)
 
     order = jnp.arange(block_total, dtype=jnp.int32)
     valid = order[None, :, None] < block_count[0][:, None, None]
     chosen = jnp.any(valid & (block_list[0][:, :, None] == order[None, None, :]), axis=1)
     row_chosen = jnp.repeat(chosen.astype(jnp.float32), row_count // block_total, axis=1)
     coef = route_gates.T * row_chosen
-    facts = jnp.concatenate(
-        [coef, jnp.broadcast_to(owner_token.astype(jnp.float32)[None], (4, row_count))], axis=0
-    )
-    facts = lax.all_gather(facts, "blk")
-
-    def by_arrival(weight):
-        quarters = weight.reshape(4, width, units)
-        return jnp.concatenate(
-            [lax.dynamic_index_in_dim(quarters, share ^ j, 0, keepdims=False) for j in range(4)]
-        )
-
-    w_gate = by_arrival(gate_weight[0])
-    w_up = by_arrival(up_weight[0])
+    owner_float = owner_token.astype(jnp.float32)
+    facts = []
+    for offset in range(offsets_all):
+        pair = jnp.stack([coef[offset], owner_float])
+        if offset > 0:
+            pair = shifted(pair, "blk", offsets_all - offset)
+        facts.append(pair)
+    facts = jnp.stack(facts)
+
+    gate_quarters = gate_weight[0].reshape(4, width, units)
+    up_quarters = up_weight[0].reshape(4, width, units)
+
+    def quarter(j):
+        index = share ^ j
+        return [
+            lax.dynamic_index_in_dim(q, index, 0, keepdims=False)
+            for q in (gate_quarters, up_quarters)
+        ]
+
+    lend = jnp.concatenate([jnp.concatenate(quarter(j), axis=1) for j in (1, 3)])
 
     pieces = [
         lax.dynamic_slice_in_dim(down_weight[0], (share ^ j) * width, width, 1) for j in range(4)
     ]
-    sibling = across_cores(jnp.concatenate([pieces[1], pieces[3]], axis=1))
-    w_down = jnp.concatenate([jnp.concatenate([pieces[0], pieces[2]], axis=1), sibling], axis=0)
-
-    token_of = (
-        jnp.asarray(CHUNK_OWNER, jnp.int32)[:, position][:, None] * owned
-        + jnp.arange(owned, dtype=jnp.int32)[None, :]
-    ).reshape(4 * owned)
-
-    collected = jnp.zeros((4 * owned, units), jnp.float32)
-    for index, near in enumerate(slots):
-        far = across_chips(near)
-        rows = jnp.concatenate([near, across_cores(near), far, across_cores(far)], axis=1)
-        gate_out = jnp.dot(rows, w_gate, preferred_element_type=jnp.float32)
-        up_out = jnp.dot(rows, w_up, preferred_element_type=jnp.float32)
-        hidden = (jax.nn.silu(gate_out) * up_out).astype(jnp.bfloat16)
+    lend_down = jnp.concatenate([pieces[1], pieces[3]], axis=1)
+
+    owners = jnp.asarray(CHUNK_OWNER, jnp.int32)[:, position]
+
+    def partial(rows, weight):
+        return jnp.dot(rows, weight, preferred_element_type=jnp.float32)
+
+    def slot_pair(index):
         source = jnp.asarray(SLOT_POSITION[index], jnp.int32)[position]
         offset = (source - position) % offsets_all
-        facts_here = lax.dynamic_index_in_dim(facts, source, 0, keepdims=False)
-        factor = lax.dynamic_index_in_dim(facts_here, offset, 0, keepdims=False)
-        owner = facts_here[offsets_all].astype(jnp.int32)
-        placing = jnp.where(owner[None, :] == token_of[:, None], factor[None, :], 0.0)
-        collected = collected + jnp.dot(
-            placing.astype(jnp.bfloat16), hidden, preferred_element_type=jnp.float32
+        return lax.dynamic_index_in_dim(facts, offset, 0, keepdims=False)
+
+    def exchanged(sums):
+        return across_cores(sums.astype(jnp.bfloat16))
+
+    beside, middle, own_far, lend, lend_down = all_there(
+        beside, middle, own_far, lend, lend_down
+    )
+    inner_last = lax.ppermute(beside, "blk", MIDDLE)
+    outer_next = lax.ppermute(middle, "blk", OUTWARD)
+    inward_far = lax.ppermute(own_far[half:], "blk", INWARD)
+    beside_far = across_chips(beside)
+    lent = across_cores(lend)
+    w_in = []
+    for index, j in enumerate((0, 2)):
+        gate_own, up_own = quarter(j)
+        other = lent[index * width : (index + 1) * width]
+        w_in.append(
+            jnp.concatenate([gate_own, other[:, :units], up_own, other[:, units:]], axis=1)
         )
-    own_half = collected.astype(jnp.bfloat16)
-    both = jnp.concatenate([own_half, across_cores(own_half)], axis=1)
-
-    chunks = []
-    for index in range(4):
-        part = jnp.dot(
-            both[index * owned : (index + 1) * owned], w_down, preferred_element_type=jnp.float32
-        )
-        got = across_chips(part[:, width:].astype(jnp.bfloat16))
-        chunks.append(part[:, :width] + got.astype(jnp.float32))
+    w_near, w_far = w_in
+    sums_0 = partial(tokens, w_near) + partial(own_far, w_far)
+    got_0 = exchanged(sums_0)
+
+    inner_last, outer_next, inward_far, beside_far, sums_0, got_0 = all_there(
+        inner_last, outer_next, inward_far, beside_far, sums_0, got_0
+    )
+    outer_last = lax.ppermute(inner_last, "blk", OUTWARD)
+    middle_far = lax.ppermute(inward_far, "blk", MIDDLE)
+    second = jnp.where(inner, middle, outer_next)
+    second_far = across_chips(second)
+    lent_down = across_cores(lend_down)
+    w_down = jnp.concatenate([jnp.concatenate([pieces[0], pieces[2]], axis=1), lent_down], axis=0)
+    total = collect(owned, owners, sums_0, got_0, slot_pair(0), None)
+    sums_1 = partial(beside, w_near) + partial(beside_far, w_far)
+    got_1 = exchanged(sums_1)
+
+    outer_last, middle_far, second_far, total, sums_1, got_1, w_down = all_there(
+        outer_last, middle_far, second_far, total, sums_1, got_1, w_down
+    )
+    outward_far = lax.ppermute(middle_far, "blk", OUTWARD)
+    last = jnp.where(inner, inner_last, outer_last)
+    last_far = across_chips(last[:half])
+    total = collect(owned, owners, sums_1, got_1, slot_pair(1), total)
+    sums_2 = partial(second, w_near) + partial(second_far, w_far)
+    got_2 = exchanged(sums_2)
+    total = collect(owned, owners, sums_2, got_2, slot_pair(2), total)
+    last_sums = partial(last, w_near)
+
+    last_far, outward_far, total, last_sums = all_there(last_far, outward_far, total, last_sums)
+    last_far = jnp.concatenate([last_far, jnp.where(inner, middle_far, outward_far)])
+    sums_3 = last_sums + partial(last_far, w_far)
+    sent, kept = finish(owned, owners, sums_3, exchanged(sums_3), slot_pair(3), total, w_down)
+    chunks = [k + across_chips(s).astype(jnp.float32) for s, k in zip(sent, kept)]
 
     def send(block, route):
         return lax.ppermute(block.astype(jnp.bfloat16), "blk", route).astype(jnp.float32)

time: 173 us -> 176 us (1.017)
  matrix products: 41.4 us -> 20.2 us
  waiting for transfers between devices: 59.1 us -> 78.9 us
  blocking collectives: 13.9 us -> 0 us
  starting transfers between devices: 28 us -> 36.5 us
  other arithmetic: 4.23 us -> 11.6 us
  Pallas kernels: 0 us -> 7.05 us
  between operations: 8.33 us -> 2.9 us
    dot_general x12 -> x8, matrix products: 41.4 us -> 20.2 us  [partial(): return jnp.dot(rows, weight, preferred_element_type=jnp.float32)]
    all_gather x1 -> x0, blocking collectives: 13.9 us -> none  [rows_travel(): facts = lax.all_gather(facts, 'blk')]
    ppermute x2 -> x8, waiting for transfers between devices: 17 us -> 30.4 us  [the longest x3 17.4 us: shifted(): return lax.ppermute(block, axis, route)]
    ppermute x1, waiting for transfers between devices: 10.9 us -> 0.01 us  [rows_travel(): outer_next = lax.ppermute(middle, 'blk', OUTWARD)]
    ppermute x2 -> x8, starting transfers between devices: 2.16 us -> 10.6 us  [the longest x1 4.53 us: rows_travel(): inward_far = lax.ppermute(own_far[half:], 'blk', INWARD)]
    ppermute x1, waiting for transfers between devices: 0.01 us -> 7.6 us  [rows_travel(): beside = lax.ppermute(tokens, 'blk', BESIDE)]
    pallas_call x0 -> x8, Pallas kernels: none -> 7.05 us  [the longest x3 4.07 us: collect(): pl.pallas_call(body, out_shape=jax.ShapeDtypeStruct((chunks * owned, sums...]
    ppermute x8, waiting for transfers between devices: 18.7 us -> 25.6 us  [across_chips(): return lax.ppermute(block, 'tp', [(i, i ^ 2) for i in range(4)])]
  transfers between devices with their start and end apart: 29 -> 31, of which waited for: 10 -> 17; matrix products, arithmetic and copies ran while one was open for 34% -> 18% of each run, Pallas kernels for 0% -> 2%
where the time goes in v2:
time: 176 us
  waiting for transfers between devices  78.9 us (45%)
  starting transfers between devices  36.5 us (21%)
  matrix products  20.2 us (11%)
  local copies, waits for them, and re-layouts  18.6 us (11%)
  other arithmetic  11.6 us (7%)
  Pallas kernels  7.05 us (4%)
  between operations  2.9 us (2%)
    ppermute x8, waiting for transfers between devices, across_chips(): return lax.ppermute(block, 'tp', [(i, i ^ 2) for i in range(4)])  25.6 us
    dot_general x8, matrix products, partial(): return jnp.dot(rows, weight, preferred_element_type=jnp.float32)  20.2 us
    ppermute x3, waiting for transfers between devices, shifted(): return lax.ppermute(block, axis, route)  17.4 us
    ppermute x6, waiting for transfers between devices, send(): lax.ppermute(block.astype(jnp.bfloat16), 'blk', route).astype(jnp.float32)  12.3 us
    ppermute x8, starting transfers between devices, across_chips(): return lax.ppermute(block, 'tp', [(i, i ^ 2) for i in range(4)])  9.35 us
    ppermute x1, waiting for transfers between devices, rows_travel(): inward_far = lax.ppermute(own_far[half:], 'blk', INWARD)  8.29 us
    unnamed x110, local copies, waits for them, and re-layouts  8.22 us
    ppermute x6, starting transfers between devices, send(): lax.ppermute(block.astype(jnp.bfloat16), 'blk', route).astype(jnp.float32)  8.09 us
  transfers between devices with their start and end apart: 31, of which 17 were waited for; matrix products, arithmetic and copies ran while one was open for 18% of the time, Pallas kernels for 2%

profile of v2, /device:TPU:0, one launch (start us, length us, event | category | flops | bytes accessed | tf_op | source)
XLA Modules:
  0.0 175.8 jit_solution(3640205062087898431)
XLA Ops:
  0.7 5.9 %collective-permute-start = (bf16[384,1024]{1,0:T(8,128)(2,1)}, bf16[384,1024]{1,0:T(8,128)(2,1)}, u32[]{:S(2)}, u32[]{:S(2)}) collective-permute-start(bf16[384,1024]{1,0:T(8,128)(2,1)} %param.13), channel_id=1, source_target_pairs={{0,4},{4,0},{8,12},{12,8},{1,5},{5,1},{9,13},{13,9},{2,6},{6,2},{1... | collective-permute-start | bytes 2359304 | tf_op jit(solution)/shard_map/ppermute | solution.py:196
  8.1 2.9 %dynamic-slice_bitcast_fusion.1 = (bf16[256,1024]{1,0:T(8,128)(2,1)}, bf16[256,1024]{1,0:T(8,128)(2,1)S(1)}, bf16[256,1024]{1,0:T(8,128)(2,1)}, bf16[256,1024]{1,0:T(8,128)(2,1)}) fusion(bf16[1,256,4096]{2,1,0:T(8,128)(2,1)} %param.16, s32[]{:T(128)S(6)} %select_n.99, s32[]{:T(128)S(6)} %select_n.93, s32[]{:T(128)S(6)} %select_n.92, s32[]{:T(128)S(6)} %select_n.100), kind=kLoop, calls=%fused_computation.25 | loop fusion | bytes 4194320 | tf_op jit(solution)/shard_map/dynamic_slice | solution.py:227
  10.9 3.0 %dynamic-slice_bitcast_fusion.2 = (bf16[1024,256]{1,0:T(8,128)(2,1)}, bf16[1024,256]{1,0:T(8,128)(2,1)}, bf16[1024,256]{1,0:T(8,128)(2,1)S(1)}, bf16[1024,256]{1...) fusion(bf16[4,1024,256]{2,1,0:T(8,128)(2,1)S(1)} %bitcast.62, ...), kind=kLoop, calls=%fused_computation.26 | loop fusion | bytes 8388624 | tf_op jit(solution)/shard_map/jit(dynamic_index_in_dim)/squeeze | solution.py:220
  16.6 7.6 %collective-permute-done.refs_0_ = bf16[384,1024]{1,0:T(8,128)(2,1)} collective-permute-done((bf16[384,1024]{1,0:T(8,128)(2,1)}, bf16[384,1024]{1,0:T(8,128)(2,1)}, u32[]{:S(2)}, u32[]{:S(2)}) %collective-permute-start) | collective-permute-done | bytes 786464 | tf_op jit(solution)/shard_map/ppermute | solution.py:196
  32.1 3.6 %fusion.24 = (bf16[384,1024]{1,0:T(8,128)(2,1)}, f32[384,1024]{1,0:T(8,128)}) fusion(bf16[384,1024]{1,0:T(8,128)(2,1)} %get-tuple-element.37, bf16[1024,256]{1,0:T(8,128)(2,1)S(1)} %get-tuple-element.76, bf16[1024,256]{1,0:T(8,128)(2,1)S(1)} %copy-done.24, bf16[1024,256]{1,0:T(8,128)(2,1)S(1)} %get-tuple-element.75, bf16[1024,256]{1,0:T(8,128)(2,1)S(1)} %copy-done.28, ...), kind=kOutput, calls=%fused_computation.68 | convolution fusion | flops 814481408 | bytes 6815744 | tf_op jit(solution)/shard_map/dot_general | solution.py:234
  37.6 4.5 %collective-permute-start.5 = (bf16[192,1024]{1,0:T(8,128)(2,1)}, bf16[192,1024]{1,0:T(8,128)(2,1)}, u32[]{:S(2)}, u32[]{:S(2)}) collective-permute-start(bf16[192,1024]{1,0:T(8,128)(2,1)} %slice.36), channel_id=1, source_target_pairs={{0,4},{12,8},{1,5},{13,9},{2,6},{14,10},{3,7},{15,11},{16,20},{28,... | collective-permute-start | bytes 1179656 | tf_op jit(solution)/shard_map/ppermute | solution.py:249
  42.4 8.3 %collective-permute-done.5.refs_2_ = bf16[192,1024]{1,0:T(8,128)(2,1)} collective-permute-done((bf16[192,1024]{1,0:T(8,128)(2,1)}, bf16[192,1024]{1,0:T(8,128)(2,1)}, u32[]{:S(2)}, u32[]{:S(2)}) %collective-permute-start.5) | collective-permute-done | bytes 393248 | tf_op jit(solution)/shard_map/ppermute | solution.py:249
  56.3 2.4 %fusion.19 = f32[384,1024]{1,0:T(8,128)S(1)} fusion(bf16[384,1024]{1,0:T(8,128)(2,1)} %get-tuple-element.44, bf16[1024,256]{1,0:T(8,128)(2,1)} %copy-done.39, bf16[1024,256]{1,0:T(8,128)(2,1)S(1)} %copy-done.25, bf16[1024,256]{1,0:T(8,128)(2,1)S(1)} %copy-done.38, bf16[1024,256]{1,0:T(8,128)(2,1)S(1)} %copy-done.29), kind=kOutput, calls=%fused_computation.63 | convolution fusion | flops 813694976 | bytes 4456448 | tf_op jit(solution)/shard_map/dot_general | solution.py:234
  58.8 3.6 %fusion.25 = (bf16[384,1024]{1,0:T(8,128)(2,1)}, f32[384,1024]{1,0:T(8,128)}) fusion(f32[384,1024]{1,0:T(8,128)S(1)} %fusion.19, bf16[384,1024]{1,0:T(8,128)(2,1)} %get-tuple-element.35, bf16[1024,256]{1,0:T(8,128)(2,1)S(1)} %copy-done.41, bf16[1024,256]{1,0:T(8,128)(2,1)S(1)} %copy-done.32, bf16[1024,256]{1,0:T(8,128)(2,1)S(1)} %copy-done.44, ...), kind=kOutput, calls=%fused_computation.69 | convolution fusion | flops 814481408 | bytes 6815744 | tf_op jit(solution)/shard_map/dot_general | solution.py:234
  64.7 12.0 %collective-permute-done.12 = f32[2,384]{1,0:T(2,128)S(1)} collective-permute-done((f32[2,384]{1,0:T(2,128)S(1)}, f32[2,384]{1,0:T(2,128)S(1)}, u32[]{:S(2)}, u32[]{:S(2)}) %collective-permute-start.12) | collective-permute-done | bytes 3104 | tf_op jit(solution)/shard_map/ppermute | solution.py:12
  77.4 3.8 %collective-permute-done.13 = f32[2,384]{1,0:T(2,128)S(1)} collective-permute-done((f32[2,384]{1,0:T(2,128)S(1)}, f32[2,384]{1,0:T(2,128)S(1)}, u32[]{:S(2)}, u32[]{:S(2)}) %collective-permute-start.13) | collective-permute-done | bytes 3104 | tf_op jit(solution)/shard_map/ppermute | solution.py:12
  87.3 3.3 %pad_maximum_fusion.2.refs_6_ = bf16[512,2048]{1,0:T(8,128)(2,1)} fusion(bf16[256,2048]{1,0:T(8,128)(2,1)} %collective-permute-done.16, bf16[256,1024]{1,0:T(8,128)(2,1)} %get-tuple-element.70, bf16[256,1024]{1,0:T(8,128)(2,1)} %get-tuple-element.67), kind=kLoop, calls=%fused_computation.3 | loop fusion | flops 6291456 | bytes 4194304 | tf_op jit(solution)/shard_map/concatenate | solution.py:271
  96.0 2.6 %fusion.18 = f32[384,1024]{1,0:T(8,128)S(1)} fusion(bf16[384,1024]{1,0:T(8,128)(2,1)} %get-tuple-element.48, bf16[1024,256]{1,0:T(8,128)(2,1)} %copy-done.39, bf16[1024,256]{1,0:T(8,128)(2,1)S(1)} %copy-done.26, bf16[1024,256]{1,0:T(8,128)(2,1)} %copy-done.37, bf16[1024,256]{1,0:T(8,128)(2,1)S(1)} %copy-done.30), kind=kOutput, calls=%fused_computation.62 | convolution fusion | flops 813694976 | bytes 4456448 | tf_op jit(solution)/shard_map/dot_general | solution.py:234
  110.2 2.5 %collective-permute-done.17.refs_0_ = bf16[192,1024]{1,0:T(8,128)(2,1)S(1)} collective-permute-done((bf16[192,1024]{1,0:T(8,128)(2,1)S(1)}, bf16[192,1024]{1,0:T(8,128)(2,1)S(1)}, u32[]{:S(2)}, u32[]{:S(2)}) %collective-permute-start.17) | collective-permute-done | bytes 393248 | tf_op jit(solution)/shard_map/ppermute | solution.py:96
  112.7 4.7 %collective-permute-done.18.refs_1_ = bf16[192,1024]{1,0:T(8,128)(2,1)S(1)} collective-permute-done((bf16[192,1024]{1,0:T(8,128)(2,1)S(1)}, bf16[192,1024]{1,0:T(8,128)(2,1)S(1)}, u32[]{:S(2)}, u32[]{:S(2)}) %collective-permute-start.18) | collective-permute-done | bytes 393248 | tf_op jit(solution)/shard_map/ppermute | solution.py:279
  119.2 2.6 %fusion = f32[384,1024]{1,0:T(8,128)S(1)} fusion(bf16[192,1024]{1,0:T(8,128)(2,1)S(1)} %broadcast_select_fusion.2, bf16[192,1024]{1,0:T(8,128)(2,1)} %get-tuple-element.53, bf16[1024,256]{1,0:T(8,128)(2,1)} %copy-done.39, bf16[1024,256]{1,0:T(8,128)(2,1)S(1)} %copy-done.27, bf16[1024,256]{1,0:T(8,128)(2,1)} %copy-done.37, ...), kind=kOutput, calls=%fused_computation.8 | convolution fusion | flops 815267840 | bytes 4456448 | tf_op jit(solution)/shard_map/dot_general | solution.py:234
  124.5 3.0 %shard_map.134 = (bf16[192,1024]{1,0:T(8,128)(2,1)S(1)}, bf16[192,1024]{1,0:T(8,128)(2,1)S(1)}, bf16[192,1024]{1,0:T(8,128)(2,1)S(1)}, bf16[192,1024]{1,0:T(8,12...) custom-call(s32[4]{0:T(128)S(1)} %fusion.14.owners_ref, ...), custom_call_target="tpu_custom_call" | custom-call | tf_op jit(solution)/shard_map/pallas_call | solution.py:172
  129.7 9.9 %collective-permute-done.27 = bf16[192,1024]{1,0:T(8,128)(2,1)S(1)} collective-permute-done((bf16[192,1024]{1,0:T(8,128)(2,1)S(1)}, bf16[192,1024]{1,0:T(8,128)(2,1)S(1)}, u32[]{:S(2)}, u32[]{:S(2)}) %collective-permute-start.27) | collective-permute-done | bytes 393248 | tf_op jit(solution)/shard_map/ppermute | solution.py:96
  141.0 6.2 %collective-permute-done.24 = bf16[192,1024]{1,0:T(8,128)(2,1)S(1)} collective-permute-done((bf16[192,1024]{1,0:T(8,128)(2,1)S(1)}, bf16[192,1024]{1,0:T(8,128)(2,1)S(1)}, u32[]{:S(2)}, u32[]{:S(2)}) %collective-permute-start.24) | collective-permute-done | bytes 393248 | tf_op jit(solution)/shard_map/ppermute | solution.py:96
  151.6 5.0 %collective-permute-done.25 = bf16[192,1024]{1,0:T(8,128)(2,1)S(1)} collective-permute-done((bf16[192,1024]{1,0:T(8,128)(2,1)S(1)}, bf16[192,1024]{1,0:T(8,128)(2,1)S(1)}, u32[]{:S(2)}, u32[]{:S(2)}) %collective-permute-start.25) | collective-permute-done | bytes 393248 | tf_op jit(solution)/shard_map/ppermute | solution.py:295
  157.5 3.2 %collective-permute-done.22 = bf16[192,1024]{1,0:T(8,128)(2,1)S(1)} collective-permute-done((bf16[192,1024]{1,0:T(8,128)(2,1)S(1)}, bf16[192,1024]{1,0:T(8,128)(2,1)S(1)}, u32[]{:S(2)}, u32[]{:S(2)}) %collective-permute-start.22) | collective-permute-done | bytes 393248 | tf_op jit(solution)/shard_map/ppermute | solution.py:96
  161.0 2.8 %collective-permute-start.23 = (bf16[192,1024]{1,0:T(8,128)(2,1)S(1)}, bf16[192,1024]{1,0:T(8,128)(2,1)S(1)}, u32[]{:S(2)}, u32[]{:S(2)}) collective-permute-start(bf16[192,1024]{1,0:T(8,128)(2,1)S(1)} %get-tuple-element.83), channel_id=1, source_target_pairs={{0,4},{12,8},{1,5},{13,9},{2,6},{14,10},{3,7},{15,11},{16,20},{28,... | collective-permute-start | bytes 1179656 | tf_op jit(solution)/shard_map/ppermute | solution.py:295
  167.4 3.2 %collective-permute-done.23 = bf16[192,1024]{1,0:T(8,128)(2,1)S(1)} collective-permute-done((bf16[192,1024]{1,0:T(8,128)(2,1)S(1)}, bf16[192,1024]{1,0:T(8,128)(2,1)S(1)}, u32[]{:S(2)}, u32[]{:S(2)}) %collective-permute-start.23) | collective-permute-done | bytes 393248 | tf_op jit(solution)/shard_map/ppermute | solution.py:295
  170.6 4.1 %collective-permute-done.30 = bf16[192,1024]{1,0:T(8,128)(2,1)S(1)} collective-permute-done((bf16[192,1024]{1,0:T(8,128)(2,1)S(1)}, bf16[192,1024]{1,0:T(8,128)(2,1)S(1)}, u32[]{:S(2)}, u32[]{:S(2)}) %collective-permute-start.30) | collective-permute-done | bytes 393248 | tf_op jit(solution)/shard_map/ppermute | solution.py:295
  (198 shorter events, 62.2 us)
Async XLA Ops:
  0.0 16.6 %collective-permute-start.1 = (bf16[384,1024]{1,0:T(8,128)(2,1)}, bf16[384,1024]{1,0:T(8,128)(2,1)S(1)}, u32[]{:S(2)}, u32[]{:S(2)}) collective-permute-start(bf16[384,1024]{1,0:T(8,128)(2,1)} %param.13), channel_id=1, source_target_pairs={{4,8},{8,4},{5,9},{9,5},{6,10},{10,6},{7,11},{11,7},{20,24},{24,20... | collective-permute-start | bytes 2359304 | tf_op jit(solution)/shard_map/ppermute | solution.py:197
  0.7 23.4 %collective-permute-start = (bf16[384,1024]{1,0:T(8,128)(2,1)}, bf16[384,1024]{1,0:T(8,128)(2,1)}, u32[]{:S(2)}, u32[]{:S(2)}) collective-permute-start(bf16[384,1024]{1,0:T(8,128)(2,1)} %param.13), channel_id=1, source_target_pairs={{0,4},{4,0},{8,12},{12,8},{1,5},{5,1},{9,13},{13,9},{2,6},{6,2},{1... | collective-permute-start | bytes 2359304 | tf_op jit(solution)/shard_map/ppermute | solution.py:196
  6.6 19.0 %collective-permute-start.2 = (bf16[384,1024]{1,0:T(8,128)(2,1)}, bf16[384,1024]{1,0:T(8,128)(2,1)}, u32[]{:S(2)}, u32[]{:S(2)}) collective-permute-start(bf16[384,1024]{1,0:T(8,128)(2,1)} %param.13), channel_id=1, source_target_pairs={{0,2},{1,3},{2,0},{3,1},{4,6},{5,7},{6,4},{7,5},{8,10},{9,11},{10,... | collective-permute-start | bytes 2359304 | tf_op jit(solution)/shard_map/ppermute | solution.py:96
  25.6 25.2 %collective-permute-start.6 = (bf16[384,1024]{1,0:T(8,128)(2,1)}, bf16[384,1024]{1,0:T(8,128)(2,1)}, u32[]{:S(2)}, u32[]{:S(2)}) collective-permute-start(bf16[384,1024]{1,0:T(8,128)(2,1)} %get-tuple-element.35), channel_id=1, source_target_pairs={{0,2},{1,3},{2,0},{3,1},{4,6},{5,7},{6,4},{7,5},{8,10},{9,11},{10,... | collective-permute-start | bytes 2359304 | tf_op jit(solution)/shard_map/ppermute | solution.py:96
  27.1 23.7 %collective-permute-start.3 = (bf16[384,1024]{1,0:T(8,128)(2,1)}, bf16[384,1024]{1,0:T(8,128)(2,1)S(1)}, u32[]{:S(2)}, u32[]{:S(2)}) collective-permute-start(bf16[384,1024]{1,0:T(8,128)(2,1)} %get-tuple-element.35), channel_id=1, source_target_pairs={{4,8},{8,4},{5,9},{9,5},{6,10},{10,6},{7,11},{11,7},{20,24},{24,20... | collective-permute-start | bytes 2359304 | tf_op jit(solution)/shard_map/ppermute | solution.py:247
  27.8 22.9 %collective-permute-start.4 = (bf16[384,1024]{1,0:T(8,128)(2,1)}, bf16[384,1024]{1,0:T(8,128)(2,1)S(1)}, u32[]{:S(2)}, u32[]{:S(2)}) collective-permute-start(bf16[384,1024]{1,0:T(8,128)(2,1)} %get-tuple-element.36), channel_id=1, source_target_pairs={{4,0},{8,12},{5,1},{9,13},{6,2},{10,14},{7,3},{11,15},{20,16},{24,... | collective-permute-start | bytes 2359304 | tf_op jit(solution)/shard_map/ppermute | solution.py:248
  35.7 15.1 %collective-permute-start.8 = (bf16[384,1024]{1,0:T(8,128)(2,1)}, bf16[384,1024]{1,0:T(8,128)(2,1)S(1)}, u32[]{:S(2)}, u32[]{:S(2)}) collective-permute-start(bf16[384,1024]{1,0:T(8,128)(2,1)} %get-tuple-element.97), channel_id=1, source_target_pairs={{0,1},{1,0},{2,3},{3,2},{4,5},{5,4},{6,7},{7,6},{8,9},{9,8},{10,11... | collective-permute-start | bytes 2359304 | tf_op jit(solution)/shard_map/ppermute | solution.py:100
  37.6 13.1 %collective-permute-start.5 = (bf16[192,1024]{1,0:T(8,128)(2,1)}, bf16[192,1024]{1,0:T(8,128)(2,1)}, u32[]{:S(2)}, u32[]{:S(2)}) collective-permute-start(bf16[192,1024]{1,0:T(8,128)(2,1)} %slice.36), channel_id=1, source_target_pairs={{0,4},{12,8},{1,5},{13,9},{2,6},{14,10},{3,7},{15,11},{16,20},{28,... | collective-permute-start | bytes 1179656 | tf_op jit(solution)/shard_map/ppermute | solution.py:249
  50.7 36.6 %collective-permute-start.16 = (bf16[256,2048]{1,0:T(8,128)(2,1)S(1)}, bf16[256,2048]{1,0:T(8,128)(2,1)}, u32[]{:S(2)}, u32[]{:S(2)}) collective-permute-start(bf16[256,2048]{1,0:T(8,128)(2,1)S(1)} %copy-done.12), channel_id=1, source_target_pairs={{0,1},{1,0},{2,3},{3,2},{4,5},{5,4},{6,7},{7,6},{8,9},{9,8},{10,11... | collective-permute-start | bytes 3145736 | tf_op jit(solution)/shard_map/ppermute | solution.py:100
  54.4 38.7 %collective-permute-start.11 = (bf16[384,1024]{1,0:T(8,128)(2,1)}, bf16[384,1024]{1,0:T(8,128)(2,1)}, u32[]{:S(2)}, u32[]{:S(2)}) collective-permute-start(bf16[384,1024]{1,0:T(8,128)(2,1)} %broadcast_select_fusion.1), channel_id=1, source_target_pairs={{0,2},{1,3},{2,0},{3,1},{4,6},{5,7},{6,4},{7,5},{8,10},{9,11},{10,... | collective-permute-start | bytes 2359304 | tf_op jit(solution)/shard_map/ppermute | solution.py:96
  54.9 38.2 %collective-permute-start.9 = (bf16[384,1024]{1,0:T(8,128)(2,1)S(1)}, bf16[384,1024]{1,0:T(8,128)(2,1)S(1)}, u32[]{:S(2)}, u32[]{:S(2)}) collective-permute-start(bf16[384,1024]{1,0:T(8,128)(2,1)S(1)} %copy-done.14), channel_id=1, source_target_pairs={{4,0},{8,12},{5,1},{9,13},{6,2},{10,14},{7,3},{11,15},{20,16},{24,... | collective-permute-start | bytes 2359304 | tf_op jit(solution)/shard_map/ppermute | solution.py:266
  62.5 30.7 %collective-permute-start.15 = (bf16[384,1024]{1,0:T(8,128)(2,1)}, bf16[384,1024]{1,0:T(8,128)(2,1)S(1)}, u32[]{:S(2)}, u32[]{:S(2)}) collective-permute-start(bf16[384,1024]{1,0:T(8,128)(2,1)} %get-tuple-element.99), channel_id=1, source_target_pairs={{0,1},{1,0},{2,3},{3,2},{4,5},{5,4},{6,7},{7,6},{8,9},{9,8},{10,11... | collective-permute-start | bytes 2359304 | tf_op jit(solution)/shard_map/ppermute | solution.py:100
  62.8 13.9 %collective-permute-start.12 = (f32[2,384]{1,0:T(2,128)S(1)}, f32[2,384]{1,0:T(2,128)S(1)}, u32[]{:S(2)}, u32[]{:S(2)}) collective-permute-start(f32[2,384]{1,0:T(2,128)S(1)} %get-tuple-element.94), channel_id=1, source_target_pairs={{4,0},{8,4},{12,8},{0,12},{5,1},{9,5},{13,9},{1,13},{6,2},{10,6},{... | collective-permute-start | bytes 9224 | tf_op jit(solution)/shard_map/ppermute | solution.py:12
  101.1 11.6 %collective-permute-start.17 = (bf16[192,1024]{1,0:T(8,128)(2,1)S(1)}, bf16[192,1024]{1,0:T(8,128)(2,1)S(1)}, u32[]{:S(2)}, u32[]{:S(2)}) collective-permute-start(bf16[192,1024]{1,0:T(8,128)(2,1)S(1)} %slice.54), channel_id=1, source_target_pairs={{0,2},{1,3},{2,0},{3,1},{4,6},{5,7},{6,4},{7,5},{8,10},{9,11},{10,... | collective-permute-start | bytes 1179656 | tf_op jit(solution)/shard_map/ppermute | solution.py:96
  102.7 14.7 %collective-permute-start.18 = (bf16[192,1024]{1,0:T(8,128)(2,1)S(1)}, bf16[192,1024]{1,0:T(8,128)(2,1)S(1)}, u32[]{:S(2)}, u32[]{:S(2)}) collective-permute-start(bf16[192,1024]{1,0:T(8,128)(2,1)S(1)} %copy-done.22), channel_id=1, source_target_pairs={{4,0},{8,12},{5,1},{9,13},{6,2},{10,14},{7,3},{11,15},{20,16},{24,... | collective-permute-start | bytes 1179656 | tf_op jit(solution)/shard_map/ppermute | solution.py:279
  127.5 12.1 %collective-permute-start.27 = (bf16[192,1024]{1,0:T(8,128)(2,1)S(1)}, bf16[192,1024]{1,0:T(8,128)(2,1)S(1)}, u32[]{:S(2)}, u32[]{:S(2)}) collective-permute-start(bf16[192,1024]{1,0:T(8,128)(2,1)S(1)} %get-tuple-element.64), channel_id=1, source_target_pairs={{0,2},{1,3},{2,0},{3,1},{4,6},{5,7},{6,4},{7,5},{8,10},{9,11},{10,... | collective-permute-start | bytes 1179656 | tf_op jit(solution)/shard_map/ppermute | solution.py:96
  128.1 19.1 %collective-permute-start.24 = (bf16[192,1024]{1,0:T(8,128)(2,1)S(1)}, bf16[192,1024]{1,0:T(8,128)(2,1)S(1)}, u32[]{:S(2)}, u32[]{:S(2)}) collective-permute-start(bf16[192,1024]{1,0:T(8,128)(2,1)S(1)} %get-tuple-element.62), channel_id=1, source_target_pairs={{0,2},{1,3},{2,0},{3,1},{4,6},{5,7},{6,4},{7,5},{8,10},{9,11},{10,... | collective-permute-start | bytes 1179656 | tf_op jit(solution)/shard_map/ppermute | solution.py:96
  139.7 10.1 %collective-permute-start.28 = (bf16[192,1024]{1,0:T(8,128)(2,1)S(1)}, bf16[192,1024]{1,0:T(8,128)(2,1)S(1)}, u32[]{:S(2)}, u32[]{:S(2)}) collective-permute-start(bf16[192,1024]{1,0:T(8,128)(2,1)S(1)} %fusion.6), channel_id=1, source_target_pairs={{0,4},{12,8},{1,5},{13,9},{2,6},{14,10},{3,7},{15,11},{16,20},{28,... | collective-permute-start | bytes 1179656 | tf_op jit(solution)/shard_map/ppermute | solution.py:295
  148.6 12.1 %collective-permute-start.22 = (bf16[192,1024]{1,0:T(8,128)(2,1)S(1)}, bf16[192,1024]{1,0:T(8,128)(2,1)S(1)}, u32[]{:S(2)}, u32[]{:S(2)}) collective-permute-start(bf16[192,1024]{1,0:T(8,128)(2,1)S(1)} %get-tuple-element.60), channel_id=1, source_target_pairs={{0,2},{1,3},{2,0},{3,1},{4,6},{5,7},{6,4},{7,5},{8,10},{9,11},{10,... | collective-permute-start | bytes 1179656 | tf_op jit(solution)/shard_map/ppermute | solution.py:96
  150.0 10.8 %collective-permute-start.29 = (bf16[192,1024]{1,0:T(8,128)(2,1)S(1)}, bf16[192,1024]{1,0:T(8,128)(2,1)S(1)}, u32[]{:S(2)}, u32[]{:S(2)}) collective-permute-start(bf16[192,1024]{1,0:T(8,128)(2,1)S(1)} %add_convert_fusion.2), channel_id=1, source_target_pairs={{4,8},{8,4},{5,9},{9,5},{6,10},{10,6},{7,11},{11,7},{20,24},{24,20... | collective-permute-start | bytes 1179656 | tf_op jit(solution)/shard_map/ppermute | solution.py:295
  150.7 16.7 %collective-permute-start.21 = (bf16[192,1024]{1,0:T(8,128)(2,1)S(1)}, bf16[192,1024]{1,0:T(8,128)(2,1)S(1)}, u32[]{:S(2)}, u32[]{:S(2)}) collective-permute-start(bf16[192,1024]{1,0:T(8,128)(2,1)S(1)} %get-tuple-element.58), channel_id=1, source_target_pairs={{0,2},{1,3},{2,0},{3,1},{4,6},{5,7},{6,4},{7,5},{8,10},{9,11},{10,... | collective-permute-start | bytes 1179656 | tf_op jit(solution)/shard_map/ppermute | solution.py:96
  156.8 10.6 %collective-permute-start.26 = (bf16[192,1024]{1,0:T(8,128)(2,1)S(1)}, bf16[192,1024]{1,0:T(8,128)(2,1)S(1)}, u32[]{:S(2)}, u32[]{:S(2)}) collective-permute-start(bf16[192,1024]{1,0:T(8,128)(2,1)S(1)} %add_convert_fusion.3), channel_id=1, source_target_pairs={{4,8},{8,4},{5,9},{9,5},{6,10},{10,6},{7,11},{11,7},{20,24},{24,20... | collective-permute-start | bytes 1179656 | tf_op jit(solution)/shard_map/ppermute | solution.py:295
  161.0 9.6 %collective-permute-start.23 = (bf16[192,1024]{1,0:T(8,128)(2,1)S(1)}, bf16[192,1024]{1,0:T(8,128)(2,1)S(1)}, u32[]{:S(2)}, u32[]{:S(2)}) collective-permute-start(bf16[192,1024]{1,0:T(8,128)(2,1)S(1)} %get-tuple-element.83), channel_id=1, source_target_pairs={{0,4},{12,8},{1,5},{13,9},{2,6},{14,10},{3,7},{15,11},{16,20},{28,... | collective-permute-start | bytes 1179656 | tf_op jit(solution)/shard_map/ppermute | solution.py:295
  163.8 10.9 %collective-permute-start.30 = (bf16[192,1024]{1,0:T(8,128)(2,1)S(1)}, bf16[192,1024]{1,0:T(8,128)(2,1)S(1)}, u32[]{:S(2)}, u32[]{:S(2)}) collective-permute-start(bf16[192,1024]{1,0:T(8,128)(2,1)S(1)} %get-tuple-element.84), channel_id=1, source_target_pairs={{4,0},{8,12},{5,1},{9,13},{6,2},{10,14},{7,3},{11,15},{20,16},{24,... | collective-permute-start | bytes 1179656 | tf_op jit(solution)/shard_map/ppermute | solution.py:295
  (62 other events, 286.8 us)

commit v3 on v0

--- a/solution.py
+++ b/solution.py
@@ -1,6 +1,8 @@
 import jax
 import jax.numpy as jnp
 from jax import lax
+from jax.experimental import pallas as pl
+from jax.experimental.pallas import tpu as pltpu
 from jax.sharding import PartitionSpec as P
 
 
@@ -10,7 +12,7 @@
     return lax.ppermute(block, axis, route)
 
 
-def on_device(
+def weights_travel(
     tokens, gate_weight, up_weight, down_weight, route_gates, block_list, block_count, owner_token
 ):
     whole_rows = lax.all_gather(tokens, "tp", axis=1, tiled=True)
@@ -80,6 +82,333 @@
         placing, got_rows, (((0,), (0,)), ((), ())), preferred_element_type=jnp.float32
     )
     return combined.astype(jnp.bfloat16)
+
+
+BESIDE = [(0, 1), (1, 0), (2, 3), (3, 2)]
+MIDDLE = [(1, 2), (2, 1)]
+INWARD = [(0, 1), (3, 2)]
+OUTWARD = [(1, 0), (2, 3)]
+PLAN = [
+    [3, 2, 1, 0, 0, 1, 2, 3],
+    [3, 2, 0, 1, 0, 3, 1, 2],
+    [0, 1, 3, 2, 0, 1, 3, 2],
+    [0, 1, 2, 3, 0, 3, 2, 1],
+]
+FACT_ROWS = 16
+VMEM = pl.BlockSpec(memory_space=pltpu.VMEM)
+SMEM = pl.BlockSpec(memory_space=pltpu.SMEM)
+ANYWHERE = pl.BlockSpec(memory_space=pl.ANY)
+
+
+def across_chips(block):
+    return lax.ppermute(block, "tp", [(i, i ^ 2) for i in range(4)])
+
+
+def across_cores(block):
+    return lax.ppermute(block, "tp", [(i, i ^ 1) for i in range(4)])
+
+
+def along(block, route):
+    return lax.ppermute(block, "blk", route)
+
+
+def on_core(body, out_shape, in_specs, flops=1024):
+    return pl.pallas_call(
+        body,
+        out_shape=out_shape,
+        in_specs=in_specs,
+        out_specs=jax.tree.map(lambda _: VMEM, out_shape),
+        compiler_params=pltpu.CompilerParams(vmem_limit_bytes=40 * 2**20),
+        cost_estimate=pl.CostEstimate(flops=flops, bytes_accessed=1024, transcendentals=0),
+    )
+
+
+def all_there(*arrays):
+    return pl.pallas_call(
+        lambda *refs: None,
+        out_shape=[jax.ShapeDtypeStruct(a.shape, a.dtype) for a in arrays],
+        in_specs=[ANYWHERE] * len(arrays),
+        out_specs=[ANYWHERE] * len(arrays),
+        input_output_aliases={i: i for i in range(len(arrays))},
+    )(*arrays)
+
+
+def two_halves(tokens, gates, block_list, block_count, owner):
+    rows, width = tokens.shape
+    half = rows // 2
+    offsets, blocks = block_list.shape
+
+    def body(tokens_ref, gates_ref, list_ref, count_ref, owner_ref, a_ref, b_ref):
+        a_ref[...] = tokens_ref[:half, :]
+        b_ref[:half, :] = tokens_ref[half:, :]
+        block_of = lax.broadcasted_iota(jnp.int32, (1, rows), 1) // (rows // blocks)
+        facts = []
+        for offset in range(offsets):
+            mask = jnp.zeros((1, rows), jnp.float32)
+            for block in range(blocks):
+                used = jnp.int32(0)
+                for place in range(blocks):
+                    found = (list_ref[offset, place] == block) & (place < count_ref[offset])
+                    used = used | found.astype(jnp.int32)
+                mask = mask + jnp.where(block_of == block, used.astype(jnp.float32), 0.0)
+            facts.append(gates_ref[offset : offset + 1, :] * mask)
+        facts.append((owner_ref[...] >> 8).astype(jnp.float32))
+        facts.append((owner_ref[...] & 255).astype(jnp.float32))
+        facts.append(jnp.zeros((FACT_ROWS - len(facts), rows), jnp.float32))
+        b_ref[half:, :] = jnp.zeros((FACT_ROWS, width), jnp.bfloat16)
+        b_ref[half:, :rows] = jnp.concatenate(facts, axis=0).astype(jnp.bfloat16)
+
+    return on_core(
+        body,
+        [
+            jax.ShapeDtypeStruct((half, width), tokens.dtype),
+            jax.ShapeDtypeStruct((half + FACT_ROWS, width), tokens.dtype),
+        ],
+        [VMEM, VMEM, SMEM, SMEM, VMEM],
+    )(tokens, gates, block_list, block_count, owner)
+
+
+def partial_sums(rows, parts, weights, places, before=None, send=True, flops=1024):
+    width = parts[0][0].shape[1]
+    columns = weights[0].shape[1]
+    operands = [block for part in parts for block in part] + list(weights)
+    if before is not None:
+        operands.append(before)
+
+    def body(*refs):
+        blocks, results = refs[: len(parts) * len(places)], refs[len(operands) :]
+        weight_refs = refs[len(blocks) : len(blocks) + len(weights)]
+        for part in range(len(parts)):
+            span = slice(part * rows, (part + 1) * rows)
+            for side in range(2):
+                at = slice(side * columns, (side + 1) * columns)
+                total = None if before is None else refs[len(operands) - 1][span, at]
+                for index, place in enumerate(places):
+                    product = jnp.dot(
+                        blocks[part * len(places) + index][:rows, :],
+                        weight_refs[side][place * width : (place + 1) * width, :],
+                        preferred_element_type=jnp.float32,
+                    )
+                    total = product if total is None else total + product
+                results[0][span, at] = total
+                if send:
+                    results[1][span, at] = total.astype(jnp.bfloat16)
+
+    size = (len(parts) * rows, 2 * columns)
+    shapes = [jax.ShapeDtypeStruct(size, jnp.float32)]
+    if send:
+        shapes.append(jax.ShapeDtypeStruct(size, jnp.bfloat16))
+    return on_core(body, shapes, [VMEM] * len(operands), flops)(*operands)
+
+
+def collected_rows(owned, slot, plan, sums_parts, got_parts, facts, before):
+    units = sums_parts[0].shape[1] // 4
+    hidden = []
+    for sums, got in zip(sums_parts, got_parts):
+        part = []
+        for core in range(2):
+            here, there = 2 * core * units, 2 * (1 - core) * units
+            gate = sums[:, here : here + units] + got[:, there : there + units].astype(jnp.float32)
+            up = sums[:, here + units : here + 2 * units]
+            up = up + got[:, there + units : there + 2 * units].astype(jnp.float32)
+            part.append((gate / (1.0 + jnp.exp(-gate)) * up).astype(jnp.bfloat16))
+        hidden.append(jnp.concatenate(part, axis=1))
+    hidden = jnp.concatenate(hidden, axis=0)
+    values = facts[...].astype(jnp.float32)
+    kind = lax.broadcasted_iota(jnp.int32, (FACT_ROWS, 1), 0)
+    factor = jnp.sum(jnp.where(kind == plan[4 + slot], values, 0.0), axis=0, keepdims=True)
+    owner = (values[4:5, :] * 256.0 + values[5:6, :]).astype(jnp.int32)
+    results = []
+    for index in range(4):
+        token = plan[index] * owned + lax.broadcasted_iota(jnp.int32, (owned, 1), 0)
+        placing = jnp.where(owner == token, factor, 0.0).astype(jnp.bfloat16)
+        rows = jnp.dot(placing, hidden, preferred_element_type=jnp.float32)
+        if before is not None:
+            rows = rows + before[index * owned : (index + 1) * owned, :]
+        results.append(rows)
+    return results
+
+
+def collect(owned, slot, plan, sums, got, facts, before):
+    operands = [plan, sums, got, facts] + ([] if before is None else [before])
+
+    def body(plan_ref, sums_ref, got_ref, facts_ref, *rest):
+        before_ref = rest[0] if before is not None else None
+        rows = collected_rows(
+            owned, slot, plan_ref, [sums_ref], [got_ref], facts_ref, before_ref
+        )
+        for index in range(4):
+            rest[-1][index * owned : (index + 1) * owned, :] = rows[index]
+
+    shape = jax.ShapeDtypeStruct((4 * owned, sums.shape[1] // 2), jnp.float32)
+    return on_core(body, shape, [SMEM] + [VMEM] * (len(operands) - 1))(*operands)
+
+
+def finish(owned, slot, plan, sums, got, facts, before, down_own, down_lent):
+    units = down_own.shape[0]
+    width = down_own.shape[1] // 2
+    count = len(sums)
+
+    def body(plan_ref, *refs):
+        sums_refs, got_refs = refs[:count], refs[count : 2 * count]
+        facts_ref, before_ref, own_ref, lent_ref, *out_refs = refs[2 * count :]
+        rows = collected_rows(owned, slot, plan_ref, sums_refs, got_refs, facts_ref, before_ref)
+        for index in range(4):
+            held = rows[index].astype(jnp.bfloat16)
+            for out, at in ((4 + index, slice(0, width)), (index, slice(width, 2 * width))):
+                result = jnp.dot(
+                    held[:, :units], own_ref[:, at], preferred_element_type=jnp.float32
+                ) + jnp.dot(held[:, units:], lent_ref[:, at], preferred_element_type=jnp.float32)
+                out_refs[out][...] = result.astype(out_refs[out].dtype)
+
+    results = on_core(
+        body,
+        [jax.ShapeDtypeStruct((owned, width), jnp.bfloat16)] * 4
+        + [jax.ShapeDtypeStruct((owned, width), jnp.float32)] * 4,
+        [SMEM] + [VMEM] * (2 * count + 4),
+    )(plan, *sums, *got, facts, before, down_own, down_lent)
+    return results[:4], results[4:]
+
+
+def rows_travel(
+    tokens, gate_weight, up_weight, down_weight, route_gates, block_list, block_count, owner_token
+):
+    position = lax.axis_index("blk")
+    share = lax.axis_index("tp")
+    row_count, width = tokens.shape
+    units = gate_weight.shape[2]
+    owned = row_count // 2
+    half = row_count // 2
+    inner = (position == 1) | (position == 2)
+    plan = jnp.asarray(PLAN, jnp.int32)[position]
+
+    own_a, own_b = two_halves(
+        tokens, route_gates.T, block_list[0], block_count[0], owner_token[None]
+    )
+
+    gate_quarters = gate_weight[0].reshape(4, width, units)
+    up_quarters = up_weight[0].reshape(4, width, units)
+
+    def quarter(j):
+        pair = [
+            lax.dynamic_index_in_dim(q, share ^ j, 0, keepdims=False)
+            for q in (gate_quarters, up_quarters)
+        ]
+        return jnp.concatenate(pair, axis=1)
+
+    def down_part(j):
+        return lax.dynamic_slice_in_dim(down_weight[0], (share ^ j) * width, width, 1)
+
+    kept_in = jnp.concatenate([quarter(0), quarter(2)])
+    lend_in = jnp.concatenate([quarter(1), quarter(3)])
+    kept_down = jnp.concatenate([down_part(0), down_part(2)], axis=1)
+    lend_down = jnp.concatenate([down_part(1), down_part(3)], axis=1)
+
+    def facts_of(second_half):
+        return second_half[half:, :row_count]
+
+    beside_a = along(own_a, BESIDE)
+    middle_a = along(own_a, MIDDLE)
+    own_far_a = across_chips(own_a)
+    beside_b = along(own_b, BESIDE)
+    middle_b = along(own_b, MIDDLE)
+    own_far_b = across_chips(own_b)
+
+    beside_a, middle_a, own_far_a, lend_in, lend_down, kept_in, kept_down = all_there(
+        beside_a, middle_a, own_far_a, lend_in, lend_down, kept_in, kept_down
+    )
+    inner_last_a = along(beside_a, MIDDLE)
+    outer_next_a = along(middle_a, OUTWARD)
+    beside_far_a = across_chips(beside_a)
+    lent_in = across_cores(lend_in)
+    lent_down = across_cores(lend_down)
+
+    beside_b, middle_b, own_far_b = all_there(beside_b, middle_b, own_far_b)
+    inner_last_b = along(beside_b, MIDDLE)
+    outer_next_b = along(middle_b, OUTWARD)
+    beside_far_b = across_chips(beside_b)
+    inward_far = along(own_far_b, INWARD)
+
+    inner_last_a, outer_next_a, beside_far_a = all_there(inner_last_a, outer_next_a, beside_far_a)
+    outer_last_a = along(inner_last_a, OUTWARD)
+    second_a = jnp.where(inner, middle_a, outer_next_a)
+    second_far_a = across_chips(second_a)
+
+    inner_last_b, outer_next_b, beside_far_b, inward_far, lent_in, lent_down = all_there(
+        inner_last_b, outer_next_b, beside_far_b, inward_far, lent_in, lent_down
+    )
+    outer_last_b = along(inner_last_b, OUTWARD)
+    second_b = jnp.where(inner, middle_b, outer_next_b)
+    second_far_b = across_chips(second_b)
+    middle_far = along(inward_far, MIDDLE)
+    weights = (kept_in, lent_in)
+    sums_0, send_0 = partial_sums(half, [(own_a, own_far_a), (own_b, own_far_b)], weights, (0, 1))
+    got_0 = across_cores(send_0)
+
+    outer_last_a, second_far_a, sums_0, got_0 = all_there(
+        outer_last_a, second_far_a, sums_0, got_0
+    )
+    last_a = jnp.where(inner, inner_last_a, outer_last_a)
+    last_far_a = across_chips(last_a)
+    total = collect(owned, 0, plan, sums_0, got_0, facts_of(own_b), None)
+    sums_1, send_1 = partial_sums(
+        half, [(beside_a, beside_far_a), (beside_b, beside_far_b)], weights, (0, 1)
+    )
+    got_1 = across_cores(send_1)
+
+    outer_last_b, second_far_b, middle_far, total, sums_1, got_1 = all_there(
+        outer_last_b, second_far_b, middle_far, total, sums_1, got_1
+    )
+    outward_far = along(middle_far, OUTWARD)
+    last_b = jnp.where(inner, inner_last_b, outer_last_b)
+    total = collect(owned, 1, plan, sums_1, got_1, facts_of(beside_b), total)
+    sums_2, send_2 = partial_sums(
+        half, [(second_a, second_far_a), (second_b, second_far_b)], weights, (0, 1)
+    )
+    got_2 = across_cores(send_2)
+    near_a = partial_sums(half, [(last_a,)], weights, (0,), send=False)[0]
+    near_b = partial_sums(half, [(last_b,)], weights, (0,), send=False)[0]
+    total = collect(owned, 2, plan, sums_2, got_2, facts_of(second_b), total)
+
+    last_far_a, near_a, near_b, total = all_there(last_far_a, near_a, near_b, total)
+    sums_a, send_a = partial_sums(
+        half, [(last_far_a,)], weights, (1,), before=near_a, flops=3 * 2**30
+    )
+    sums_a, got_a, outward_far = all_there(sums_a, across_cores(send_a), outward_far)
+    last_far_b = jnp.where(inner, middle_far, outward_far)
+    sums_b, send_b = partial_sums(half, [(last_far_b,)], weights, (1,), before=near_b)
+    got_b = across_cores(send_b)
+    sent, kept = finish(
+        owned,
+        3,
+        plan,
+        (sums_a, sums_b),
+        (got_a, got_b),
+        facts_of(last_b),
+        total,
+        kept_down,
+        lent_down,
+    )
+    chunks = [k + across_chips(s).astype(jnp.float32) for s, k in zip(sent, kept)]
+
+    def send(block, route):
+        return along(block.astype(jnp.bfloat16), route).astype(jnp.float32)
+
+    first_in = send(chunks[0], INWARD)
+    second_in = send(chunks[1], INWARD)
+    second_mid = send(chunks[0] + first_in, MIDDLE)
+    third_in = send(chunks[2], INWARD)
+    third_mid = send(chunks[1] + second_in, MIDDLE)
+    third_out = send(chunks[2] + second_mid, OUTWARD)
+    return (chunks[3] + third_in + third_mid + third_out).astype(jnp.bfloat16)
+
+
+def on_device(*args):
+    block_list = args[5]
+    sizes = (lax.axis_size("blk"), lax.axis_size("tp"), block_list.shape[1])
+    if sizes == (4, 4, 4):
+        return rows_travel(*args)
+    return weights_travel(*args)
 
 
 def solution(mesh):

time: 557 us -> 195 us (0.35)
  waiting for transfers between devices: 380 us -> 70.4 us
  matrix products: 67.8 us -> 0 us
  starting transfers between devices: 14.5 us -> 52.1 us
  Pallas kernels: 0 us -> 30.4 us
  loops' own time: 25.7 us -> 0 us
  local copies, waits for them, and re-layouts: 47.4 us -> 28.5 us
  between operations: 13.5 us -> 0.6 us
  other arithmetic: 6.49 us -> 12.1 us
    ppermute x9 -> x37, waiting for transfers between devices: 315 us -> 70.4 us  [the longest x11 34.6 us: across_chips(): return lax.ppermute(block, 'tp', [(i, i ^ 2) for i in range(4)])]
    dot_general x19 -> x0, matrix products: 67.8 us -> none  [the longest x9 49.6 us: apply(): jnp.dot(hidden, w_down, preferred_element_type=jnp.float32)]
    ppermute x9 -> x37, starting transfers between devices: 6.41 us -> 52.1 us  [the longest x19 37.6 us: along(): return lax.ppermute(block, 'blk', route)]
    all_to_all x2 -> x0, waiting for transfers between devices: 36.9 us -> none  [the longest x1 36.9 us: on_device(): lax.all_to_all(send_rows, 'blk', split_axis=0, concat_axis=0, tiled=True)]
    dynamic_slice x27 -> x1, local copies, waits for them, and re-layouts: 34 us -> 1.69 us  [down_part(): lax.dynamic_slice_in_dim(down_weight[0], (share ^ j) * width, width, 1)]
    pallas_call x0 -> x20, Pallas kernels: none -> 30.4 us  [the longest x7 21.6 us: partial_sums(): return on_core(body, shapes, [VMEM] * len(operands), flops)(*operands)]
    reduce_scatter x1 -> x0, waiting for transfers between devices: 26.9 us -> none  [on_device(): lax.psum_scatter(totals.reshape(row_count, width).astype(jnp.bfloat16), '...]
    another operation x4 -> x0, loops' own time: 25.7 us -> none  [on_device(): totals = lax.fori_loop(0, block_count[0, offset], visit_block, totals)]
  transfers between devices with their start and end apart: 13 -> 37, of which waited for: 10 -> 17; matrix products, arithmetic and copies ran while one was open for 14% -> 7% of each run, Pallas kernels for 0% -> 10%
where the time goes in v3:
time: 195 us; the launch traced here: 194 us
  waiting for transfers between devices  70.4 us (36%)
  starting transfers between devices  52.1 us (27%)
  Pallas kernels  30.4 us (16%)
  local copies, waits for them, and re-layouts  28.5 us (15%)
  other arithmetic  12.1 us (6%)
    ppermute x19, starting transfers between devices, along(): return lax.ppermute(block, 'blk', route)  37.6 us
    ppermute x11, waiting for transfers between devices, across_chips(): return lax.ppermute(block, 'tp', [(i, i ^ 2) for i in range(4)])  34.6 us
    ppermute x19, waiting for transfers between devices, along(): return lax.ppermute(block, 'blk', route)  34.1 us
    unnamed x97, local copies, waits for them, and re-layouts  23.7 us
    pallas_call x7, Pallas kernels, partial_sums(): return on_core(body, shapes, [VMEM] * len(operands), flops)(*operands)  21.6 us
    ppermute x11, starting transfers between devices, across_chips(): return lax.ppermute(block, 'tp', [(i, i ^ 2) for i in range(4)])  13.7 us
    pallas_call x3, Pallas kernels, collect(): on_core(body, shape, [SMEM] + [VMEM] * (len(operands) - 1))(*operands)  4.69 us
  transfers between devices with their start and end apart: 37, of which 17 were waited for; matrix products, arithmetic and copies ran while one was open for 7% of the time, Pallas kernels for 10%

profile of v3, /device:TPU:0, one launch (start us, length us, event | category | flops | bytes accessed | tf_op | source)
XLA Modules:
  0.0 194.0 jit_solution(832755636117637540)
XLA Ops:
  4.6 3.0 %collective-permute-start.2 = (bf16[192,1024]{1,0:T(8,128)(2,1)S(1)}, bf16[192,1024]{1,0:T(8,128)(2,1)S(1)}, u32[]{:S(2)}, u32[]{:S(2)}) collective-permute-start(bf16[192,1024]{1,0:T(8,128)(2,1)S(1)} %get-tuple-element.61.refs_0_), channel_id=1, source_target_pairs={{0,2},{1,3},{2,0},{3,1},{4,6},{5,7},{6,4},{7,5},{8,10},{9,11},{10,... | collective-permute-start | bytes 1179656 | tf_op jit(solution)/shard_map/ppermute | solution.py:104
  9.0 3.7 %collective-permute-start = (bf16[192,1024]{1,0:T(8,128)(2,1)S(1)}, bf16[192,1024]{1,0:T(8,128)(2,1)S(1)}, u32[]{:S(2)}, u32[]{:S(2)}) collective-permute-start(bf16[192,1024]{1,0:T(8,128)(2,1)S(1)} %get-tuple-element.61.refs_0_), channel_id=1, source_target_pairs={{0,4},{4,0},{8,12},{12,8},{1,5},{5,1},{9,13},{13,9},{2,6},{6,2},{1... | collective-permute-start | bytes 1179656 | tf_op jit(solution)/shard_map/ppermute | solution.py:112
  23.2 3.5 %collective-permute-start.8 = (bf16[208,1024]{1,0:T(8,128)(2,1)S(1)}, bf16[208,1024]{1,0:T(8,128)(2,1)S(1)}, u32[]{:S(2)}, u32[]{:S(2)}) collective-permute-start(bf16[208,1024]{1,0:T(8,128)(2,1)S(1)} %get-tuple-element.67.refs_2_), channel_id=1, source_target_pairs={{0,4},{4,0},{8,12},{12,8},{1,5},{5,1},{9,13},{13,9},{2,6},{6,2},{1... | collective-permute-start | bytes 1277960 | tf_op jit(solution)/shard_map/ppermute | solution.py:112
  28.0 6.2 %collective-permute-done.10.refs_2_ = bf16[208,1024]{1,0:T(8,128)(2,1)S(1)} collective-permute-done((bf16[208,1024]{1,0:T(8,128)(2,1)S(1)}, bf16[208,1024]{1,0:T(8,128)(2,1)S(1)}, u32[]{:S(2)}, u32[]{:S(2)}) %collective-permute-start.10) | collective-permute-done | bytes 426016 | tf_op jit(solution)/shard_map/ppermute | solution.py:104
  34.3 3.1 %collective-permute-done.8.refs_0_ = bf16[208,1024]{1,0:T(8,128)(2,1)S(1)} collective-permute-done((bf16[208,1024]{1,0:T(8,128)(2,1)S(1)}, bf16[208,1024]{1,0:T(8,128)(2,1)S(1)}, u32[]{:S(2)}, u32[]{:S(2)}) %collective-permute-start.8) | collective-permute-done | bytes 426016 | tf_op jit(solution)/shard_map/ppermute | solution.py:112
  38.1 4.2 %collective-permute-start.14 = (bf16[208,1024]{1,0:T(8,128)(2,1)}, bf16[208,1024]{1,0:T(8,128)(2,1)}, u32[]{:S(2)}, u32[]{:S(2)}) collective-permute-start(bf16[208,1024]{1,0:T(8,128)(2,1)} %get-tuple-element.68.refs_3_), channel_id=1, source_target_pairs={{0,4},{12,8},{1,5},{13,9},{2,6},{14,10},{3,7},{15,11},{16,20},{28,... | collective-permute-start | bytes 1277960 | tf_op jit(solution)/shard_map/ppermute | solution.py:112
  45.8 6.9 %collective-permute-done.5.refs_2_ = bf16[192,1024]{1,0:T(8,128)(2,1)S(1)} collective-permute-done((bf16[192,1024]{1,0:T(8,128)(2,1)}, bf16[192,1024]{1,0:T(8,128)(2,1)S(1)}, u32[]{:S(2)}, u32[]{:S(2)}) %collective-permute-start.5) | collective-permute-done | bytes 393248 | tf_op jit(solution)/shard_map/ppermute | solution.py:104
  58.8 5.9 %collective-permute-done.12.refs_1_ = bf16[208,1024]{1,0:T(8,128)(2,1)S(1)} collective-permute-done((bf16[208,1024]{1,0:T(8,128)(2,1)}, bf16[208,1024]{1,0:T(8,128)(2,1)S(1)}, u32[]{:S(2)}, u32[]{:S(2)}) %collective-permute-start.12) | collective-permute-done | bytes 426016 | tf_op jit(solution)/shard_map/ppermute | solution.py:112
  72.5 4.4 %shard_map.96 = (f32[384,1024]{1,0:T(8,128)S(1)}, bf16[384,1024]{1,0:T(8,128)(2,1)}) custom-call(bf16[192,1024]{1,0:T(8,128)(2,1)S(1)} %get-tuple-element.61.refs_0_, bf16[192,1024]{1,0:T(8,128)(2,1)S(1)} %copy-done.27, bf16[208,1024]{1,0:T(8,128)(2,1)S(1)} %copy-done.34, bf16[208,1024]{1,0:T(8,128)(2,1)S(1)} %copy-done.25, bf16[2048,512]{1,0:T(8,128)(2,1)S(1)} %copy-done, ...), custom_call_target="tpu_custom_call" | custom-call | flops 1024 | bytes 1024 | tf_op jit(solution)/shard_map/pallas_call | solution.py:201
  78.2 4.3 %shard_map.100 = (f32[384,1024]{1,0:T(8,128)S(1)}, bf16[384,1024]{1,0:T(8,128)(2,1)}) custom-call(bf16[192,1024]{1,0:T(8,128)(2,1)S(1)} %copy-done.29, bf16[192,1024]{1,0:T(8,128)(2,1)S(1)} %copy-done.31, bf16[208,1024]{1,0:T(8,128)(2,1)S(1)} %copy-done.21, bf16[208,1024]{1,0:T(8,128)(2,1)S(1)} %copy-done.23, bf16[2048,512]{1,0:T(8,128)(2,1)S(1)} %copy-done, ...), custom_call_target="tpu_custom_call" | custom-call | flops 1024 | bytes 1024 | tf_op jit(solution)/shard_map/pallas_call | solution.py:201
  94.4 2.6 %collective-permute-done.20.refs_1_ = bf16[208,1024]{1,0:T(8,128)(2,1)} collective-permute-done((bf16[208,1024]{1,0:T(8,128)(2,1)}, bf16[208,1024]{1,0:T(8,128)(2,1)}, u32[]{:S(2)}, u32[]{:S(2)}) %collective-permute-start.20) | collective-permute-done | bytes 426016 | tf_op jit(solution)/shard_map/ppermute | solution.py:104
  97.1 8.7 %collective-permute-done.19.refs_0_ = bf16[208,1024]{1,0:T(8,128)(2,1)} collective-permute-done((bf16[208,1024]{1,0:T(8,128)(2,1)}, bf16[208,1024]{1,0:T(8,128)(2,1)}, u32[]{:S(2)}, u32[]{:S(2)}) %collective-permute-start.19) | collective-permute-done | bytes 426016 | tf_op jit(solution)/shard_map/ppermute | solution.py:112
  106.7 3.9 %shard_map.103 = (f32[384,1024]{1,0:T(8,128)S(1)}, bf16[384,1024]{1,0:T(8,128)(2,1)S(1)}) custom-call(bf16[192,1024]{1,0:T(8,128)(2,1)} %broadcast_select_fusion.4.refs_0_, bf16[192,1024]{1,0:T(8,128)(2,1)} %get-tuple-element.88.refs_1_, bf16[208,1024]{1,0:T(8,128)(2,1)} %broadcast_select_fusion.2.refs_2_, bf16[208,1024]{1,0:T(8,128)(2,1)} %get-tuple-element.89.refs_3_, ...), custom_call_target="tpu_custom_call" | custom-call | flops 1024 | bytes 1024 | tf_op jit(solution)/shard_map/pallas_call | solution.py:201
  132.0 2.6 %collective-permute-done.25.refs_2_ = bf16[208,1024]{1,0:T(8,128)(2,1)} collective-permute-done((bf16[208,1024]{1,0:T(8,128)(2,1)}, bf16[208,1024]{1,0:T(8,128)(2,1)}, u32[]{:S(2)}, u32[]{:S(2)}) %collective-permute-start.25) | collective-permute-done | bytes 426016 | tf_op jit(solution)/shard_map/ppermute | solution.py:112
  139.8 3.5 %shard_map.110 = (bf16[192,1024]{1,0:T(8,128)(2,1)S(1)}, bf16[192,1024]{1,0:T(8,128)(2,1)S(1)}, bf16[192,1024]{1,0:T(8,128)(2,1)S(1)}, bf16[192,1024]{1,0:T(8,12...) custom-call(s32[8]{0:T(128)S(1)} %fusion.3.plan_ref, ...), custom_call_target="tpu_custom_call" | custom-call | flops 1024 | bytes 1024 | tf_op jit(solution)/shard_map/pallas_call | solution.py:264
  145.4 9.9 %collective-permute-done.33 = bf16[192,1024]{1,0:T(8,128)(2,1)S(1)} collective-permute-done((bf16[192,1024]{1,0:T(8,128)(2,1)S(1)}, bf16[192,1024]{1,0:T(8,128)(2,1)S(1)}, u32[]{:S(2)}, u32[]{:S(2)}) %collective-permute-start.33) | collective-permute-done | bytes 393248 | tf_op jit(solution)/shard_map/ppermute | solution.py:104
  155.4 4.2 %collective-permute-start.34 = (bf16[192,1024]{1,0:T(8,128)(2,1)S(1)}, bf16[192,1024]{1,0:T(8,128)(2,1)S(1)}, u32[]{:S(2)}, u32[]{:S(2)}) collective-permute-start(bf16[192,1024]{1,0:T(8,128)(2,1)S(1)} %fusion.2), channel_id=1, source_target_pairs={{0,4},{12,8},{1,5},{13,9},{2,6},{14,10},{3,7},{15,11},{16,20},{28,... | collective-permute-start | bytes 1179656 | tf_op jit(solution)/shard_map/ppermute | solution.py:112
  159.6 3.3 %collective-permute-done.30 = bf16[192,1024]{1,0:T(8,128)(2,1)S(1)} collective-permute-done((bf16[192,1024]{1,0:T(8,128)(2,1)S(1)}, bf16[192,1024]{1,0:T(8,128)(2,1)S(1)}, u32[]{:S(2)}, u32[]{:S(2)}) %collective-permute-start.30) | collective-permute-done | bytes 393248 | tf_op jit(solution)/shard_map/ppermute | solution.py:104
  163.0 4.2 %collective-permute-start.31 = (bf16[192,1024]{1,0:T(8,128)(2,1)S(1)}, bf16[192,1024]{1,0:T(8,128)(2,1)S(1)}, u32[]{:S(2)}, u32[]{:S(2)}) collective-permute-start(bf16[192,1024]{1,0:T(8,128)(2,1)S(1)} %fusion.1), channel_id=1, source_target_pairs={{0,4},{12,8},{1,5},{13,9},{2,6},{14,10},{3,7},{15,11},{16,20},{28,... | collective-permute-start | bytes 1179656 | tf_op jit(solution)/shard_map/ppermute | solution.py:112
  170.3 4.8 %collective-permute-done.31 = bf16[192,1024]{1,0:T(8,128)(2,1)S(1)} collective-permute-done((bf16[192,1024]{1,0:T(8,128)(2,1)S(1)}, bf16[192,1024]{1,0:T(8,128)(2,1)S(1)}, u32[]{:S(2)}, u32[]{:S(2)}) %collective-permute-start.31) | collective-permute-done | bytes 393248 | tf_op jit(solution)/shard_map/ppermute | solution.py:112
  175.9 3.5 %collective-permute-done.28 = bf16[192,1024]{1,0:T(8,128)(2,1)S(1)} collective-permute-done((bf16[192,1024]{1,0:T(8,128)(2,1)S(1)}, bf16[192,1024]{1,0:T(8,128)(2,1)S(1)}, u32[]{:S(2)}, u32[]{:S(2)}) %collective-permute-start.28) | collective-permute-done | bytes 393248 | tf_op jit(solution)/shard_map/ppermute | solution.py:104
  179.6 2.8 %collective-permute-start.29 = (bf16[192,1024]{1,0:T(8,128)(2,1)S(1)}, bf16[192,1024]{1,0:T(8,128)(2,1)S(1)}, u32[]{:S(2)}, u32[]{:S(2)}) collective-permute-start(bf16[192,1024]{1,0:T(8,128)(2,1)S(1)} %get-tuple-element.129), channel_id=1, source_target_pairs={{0,4},{12,8},{1,5},{13,9},{2,6},{14,10},{3,7},{15,11},{16,20},{28,... | collective-permute-start | bytes 1179656 | tf_op jit(solution)/shard_map/ppermute | solution.py:112
  185.8 3.1 %collective-permute-done.29 = bf16[192,1024]{1,0:T(8,128)(2,1)S(1)} collective-permute-done((bf16[192,1024]{1,0:T(8,128)(2,1)S(1)}, bf16[192,1024]{1,0:T(8,128)(2,1)S(1)}, u32[]{:S(2)}, u32[]{:S(2)}) %collective-permute-start.29) | collective-permute-done | bytes 393248 | tf_op jit(solution)/shard_map/ppermute | solution.py:112
  188.8 4.1 %collective-permute-done.36 = bf16[192,1024]{1,0:T(8,128)(2,1)S(1)} collective-permute-done((bf16[192,1024]{1,0:T(8,128)(2,1)S(1)}, bf16[192,1024]{1,0:T(8,128)(2,1)S(1)}, u32[]{:S(2)}, u32[]{:S(2)}) %collective-permute-start.36) | collective-permute-done | bytes 393248 | tf_op jit(solution)/shard_map/ppermute | solution.py:112
  (189 shorter events, 86.9 us)
Async XLA Ops:
  4.6 16.1 %collective-permute-start.2 = (bf16[192,1024]{1,0:T(8,128)(2,1)S(1)}, bf16[192,1024]{1,0:T(8,128)(2,1)S(1)}, u32[]{:S(2)}, u32[]{:S(2)}) collective-permute-start(bf16[192,1024]{1,0:T(8,128)(2,1)S(1)} %get-tuple-element.61.refs_0_), channel_id=1, source_target_pairs={{0,2},{1,3},{2,0},{3,1},{4,6},{5,7},{6,4},{7,5},{8,10},{9,11},{10,... | collective-permute-start | bytes 1179656 | tf_op jit(solution)/shard_map/ppermute | solution.py:104
  7.6 13.1 %collective-permute-start.1 = (bf16[192,1024]{1,0:T(8,128)(2,1)S(1)}, bf16[192,1024]{1,0:T(8,128)(2,1)}, u32[]{:S(2)}, u32[]{:S(2)}) collective-permute-start(bf16[192,1024]{1,0:T(8,128)(2,1)S(1)} %get-tuple-element.61.refs_0_), channel_id=1, source_target_pairs={{4,8},{8,4},{5,9},{9,5},{6,10},{10,6},{7,11},{11,7},{20,24},{24,20... | collective-permute-start | bytes 1179656 | tf_op jit(solution)/shard_map/ppermute | solution.py:112
  9.0 12.3 %collective-permute-start = (bf16[192,1024]{1,0:T(8,128)(2,1)S(1)}, bf16[192,1024]{1,0:T(8,128)(2,1)S(1)}, u32[]{:S(2)}, u32[]{:S(2)}) collective-permute-start(bf16[192,1024]{1,0:T(8,128)(2,1)S(1)} %get-tuple-element.61.refs_0_), channel_id=1, source_target_pairs={{0,4},{4,0},{8,12},{12,8},{1,5},{5,1},{9,13},{13,9},{2,6},{6,2},{1... | collective-permute-start | bytes 1179656 | tf_op jit(solution)/shard_map/ppermute | solution.py:112
  22.0 46.4 %collective-permute-start.15 = (bf16[2048,512]{1,0:T(8,128)(2,1)}, bf16[2048,512]{1,0:T(8,128)(2,1)}, u32[]{:S(2)}, u32[]{:S(2)}) collective-permute-start(bf16[2048,512]{1,0:T(8,128)(2,1)} %get-tuple-element.72), channel_id=1, source_target_pairs={{0,1},{1,0},{2,3},{3,2},{4,5},{5,4},{6,7},{7,6},{8,9},{9,8},{10,11... | collective-permute-start | bytes 6291464 | tf_op jit(solution)/shard_map/ppermute | solution.py:108
  22.0 12.2 %collective-permute-start.10 = (bf16[208,1024]{1,0:T(8,128)(2,1)S(1)}, bf16[208,1024]{1,0:T(8,128)(2,1)S(1)}, u32[]{:S(2)}, u32[]{:S(2)}) collective-permute-start(bf16[208,1024]{1,0:T(8,128)(2,1)S(1)} %get-tuple-element.67.refs_2_), channel_id=1, source_target_pairs={{0,2},{1,3},{2,0},{3,1},{4,6},{5,7},{6,4},{7,5},{8,10},{9,11},{10,... | collective-permute-start | bytes 1277960 | tf_op jit(solution)/shard_map/ppermute | solution.py:104
  23.2 14.1 %collective-permute-start.8 = (bf16[208,1024]{1,0:T(8,128)(2,1)S(1)}, bf16[208,1024]{1,0:T(8,128)(2,1)S(1)}, u32[]{:S(2)}, u32[]{:S(2)}) collective-permute-start(bf16[208,1024]{1,0:T(8,128)(2,1)S(1)} %get-tuple-element.67.refs_2_), channel_id=1, source_target_pairs={{0,4},{4,0},{8,12},{12,8},{1,5},{5,1},{9,13},{13,9},{2,6},{6,2},{1... | collective-permute-start | bytes 1277960 | tf_op jit(solution)/shard_map/ppermute | solution.py:112
  26.7 18.4 %collective-permute-start.4 = (bf16[192,1024]{1,0:T(8,128)(2,1)}, bf16[192,1024]{1,0:T(8,128)(2,1)S(1)}, u32[]{:S(2)}, u32[]{:S(2)}) collective-permute-start(bf16[192,1024]{1,0:T(8,128)(2,1)} %get-tuple-element.63), channel_id=1, source_target_pairs={{4,0},{8,12},{5,1},{9,13},{6,2},{10,14},{7,3},{11,15},{20,16},{24,... | collective-permute-start | bytes 1179656 | tf_op jit(solution)/shard_map/ppermute | solution.py:112
  34.2 34.2 %collective-permute-start.16 = (bf16[256,2048]{1,0:T(8,128)(2,1)}, bf16[256,2048]{1,0:T(8,128)(2,1)S(1)}, u32[]{:S(2)}, u32[]{:S(2)}) collective-permute-start(bf16[256,2048]{1,0:T(8,128)(2,1)} %get-tuple-element.73), channel_id=1, source_target_pairs={{0,1},{1,0},{2,3},{3,2},{4,5},{5,4},{6,7},{7,6},{8,9},{9,8},{10,11... | collective-permute-start | bytes 3145736 | tf_op jit(solution)/shard_map/ppermute | solution.py:108
  38.1 17.4 %collective-permute-start.14 = (bf16[208,1024]{1,0:T(8,128)(2,1)}, bf16[208,1024]{1,0:T(8,128)(2,1)}, u32[]{:S(2)}, u32[]{:S(2)}) collective-permute-start(bf16[208,1024]{1,0:T(8,128)(2,1)} %get-tuple-element.68.refs_3_), channel_id=1, source_target_pairs={{0,4},{12,8},{1,5},{13,9},{2,6},{14,10},{3,7},{15,11},{16,20},{28,... | collective-permute-start | bytes 1277960 | tf_op jit(solution)/shard_map/ppermute | solution.py:112
  54.0 12.2 %collective-permute-start.13 = (bf16[208,1024]{1,0:T(8,128)(2,1)}, bf16[208,1024]{1,0:T(8,128)(2,1)S(1)}, u32[]{:S(2)}, u32[]{:S(2)}) collective-permute-start(bf16[208,1024]{1,0:T(8,128)(2,1)} %get-tuple-element.70.refs_2_), channel_id=1, source_target_pairs={{0,2},{1,3},{2,0},{3,1},{4,6},{5,7},{6,4},{7,5},{8,10},{9,11},{10,... | collective-permute-start | bytes 1277960 | tf_op jit(solution)/shard_map/ppermute | solution.py:104
  55.5 12.9 %collective-permute-start.11 = (bf16[208,1024]{1,0:T(8,128)(2,1)}, bf16[208,1024]{1,0:T(8,128)(2,1)}, u32[]{:S(2)}, u32[]{:S(2)}) collective-permute-start(bf16[208,1024]{1,0:T(8,128)(2,1)} %get-tuple-element.70.refs_2_), channel_id=1, source_target_pairs={{4,8},{8,4},{5,9},{9,5},{6,10},{10,6},{7,11},{11,7},{20,24},{24,20... | collective-permute-start | bytes 1277960 | tf_op jit(solution)/shard_map/ppermute | solution.py:112
  64.7 21.0 %collective-permute-start.7 = (bf16[192,1024]{1,0:T(8,128)(2,1)}, bf16[192,1024]{1,0:T(8,128)(2,1)}, u32[]{:S(2)}, u32[]{:S(2)}) collective-permute-start(bf16[192,1024]{1,0:T(8,128)(2,1)} %broadcast_select_fusion.4.refs_0_), channel_id=1, source_target_pairs={{0,2},{1,3},{2,0},{3,1},{4,6},{5,7},{6,4},{7,5},{8,10},{9,11},{10,... | collective-permute-start | bytes 1179656 | tf_op jit(solution)/shard_map/ppermute | solution.py:104
  67.0 20.2 %collective-permute-start.6 = (bf16[192,1024]{1,0:T(8,128)(2,1)}, bf16[192,1024]{1,0:T(8,128)(2,1)}, u32[]{:S(2)}, u32[]{:S(2)}) collective-permute-start(bf16[192,1024]{1,0:T(8,128)(2,1)} %get-tuple-element.64), channel_id=1, source_target_pairs={{4,0},{8,12},{5,1},{9,13},{6,2},{10,14},{7,3},{11,15},{20,16},{24,... | collective-permute-start | bytes 1179656 | tf_op jit(solution)/shard_map/ppermute | solution.py:112
  83.7 22.1 %collective-permute-start.22 = (bf16[384,1024]{1,0:T(8,128)(2,1)}, bf16[384,1024]{1,0:T(8,128)(2,1)S(1)}, u32[]{:S(2)}, u32[]{:S(2)}) collective-permute-start(bf16[384,1024]{1,0:T(8,128)(2,1)} %get-tuple-element.86), channel_id=1, source_target_pairs={{0,1},{1,0},{2,3},{3,2},{4,5},{5,4},{6,7},{7,6},{8,9},{9,8},{10,11... | collective-permute-start | bytes 2359304 | tf_op jit(solution)/shard_map/ppermute | solution.py:108
  85.0 12.1 %collective-permute-start.20 = (bf16[208,1024]{1,0:T(8,128)(2,1)}, bf16[208,1024]{1,0:T(8,128)(2,1)}, u32[]{:S(2)}, u32[]{:S(2)}) collective-permute-start(bf16[208,1024]{1,0:T(8,128)(2,1)} %broadcast_select_fusion.2.refs_2_), channel_id=1, source_target_pairs={{0,2},{1,3},{2,0},{3,1},{4,6},{5,7},{6,4},{7,5},{8,10},{9,11},{10,... | collective-permute-start | bytes 1277960 | tf_op jit(solution)/shard_map/ppermute | solution.py:104
  87.2 18.6 %collective-permute-start.19 = (bf16[208,1024]{1,0:T(8,128)(2,1)}, bf16[208,1024]{1,0:T(8,128)(2,1)}, u32[]{:S(2)}, u32[]{:S(2)}) collective-permute-start(bf16[208,1024]{1,0:T(8,128)(2,1)} %get-tuple-element.78), channel_id=1, source_target_pairs={{4,0},{8,12},{5,1},{9,13},{6,2},{10,14},{7,3},{11,15},{20,16},{24,... | collective-permute-start | bytes 1277960 | tf_op jit(solution)/shard_map/ppermute | solution.py:112
  110.6 12.7 %collective-permute-start.23 = (bf16[384,1024]{1,0:T(8,128)(2,1)S(1)}, bf16[384,1024]{1,0:T(8,128)(2,1)S(1)}, u32[]{:S(2)}, u32[]{:S(2)}) collective-permute-start(bf16[384,1024]{1,0:T(8,128)(2,1)S(1)} %get-tuple-element.91), channel_id=1, source_target_pairs={{0,1},{1,0},{2,3},{3,2},{4,5},{5,4},{6,7},{7,6},{8,9},{9,8},{10,11... | collective-permute-start | bytes 2359304 | tf_op jit(solution)/shard_map/ppermute | solution.py:108
  111.8 14.1 %collective-permute-start.18 = (bf16[192,1024]{1,0:T(8,128)(2,1)S(1)}, bf16[192,1024]{1,0:T(8,128)(2,1)S(1)}, u32[]{:S(2)}, u32[]{:S(2)}) collective-permute-start(bf16[192,1024]{1,0:T(8,128)(2,1)S(1)} %broadcast_select_fusion.3.refs_0_), channel_id=1, source_target_pairs={{0,2},{1,3},{2,0},{3,1},{4,6},{5,7},{6,4},{7,5},{8,10},{9,11},{10,... | collective-permute-start | bytes 1179656 | tf_op jit(solution)/shard_map/ppermute | solution.py:104
  120.4 14.1 %collective-permute-start.25 = (bf16[208,1024]{1,0:T(8,128)(2,1)}, bf16[208,1024]{1,0:T(8,128)(2,1)}, u32[]{:S(2)}, u32[]{:S(2)}) collective-permute-start(bf16[208,1024]{1,0:T(8,128)(2,1)} %get-tuple-element.99), channel_id=1, source_target_pairs={{4,0},{8,12},{5,1},{9,13},{6,2},{10,14},{7,3},{11,15},{20,16},{24,... | collective-permute-start | bytes 1277960 | tf_op jit(solution)/shard_map/ppermute | solution.py:112
  143.3 12.0 %collective-permute-start.33 = (bf16[192,1024]{1,0:T(8,128)(2,1)S(1)}, bf16[192,1024]{1,0:T(8,128)(2,1)S(1)}, u32[]{:S(2)}, u32[]{:S(2)}) collective-permute-start(bf16[192,1024]{1,0:T(8,128)(2,1)S(1)} %get-tuple-element.116), channel_id=1, source_target_pairs={{0,2},{1,3},{2,0},{3,1},{4,6},{5,7},{6,4},{7,5},{8,10},{9,11},{10,... | collective-permute-start | bytes 1179656 | tf_op jit(solution)/shard_map/ppermute | solution.py:104
  144.9 18.1 %collective-permute-start.30 = (bf16[192,1024]{1,0:T(8,128)(2,1)S(1)}, bf16[192,1024]{1,0:T(8,128)(2,1)S(1)}, u32[]{:S(2)}, u32[]{:S(2)}) collective-permute-start(bf16[192,1024]{1,0:T(8,128)(2,1)S(1)} %get-tuple-element.114), channel_id=1, source_target_pairs={{0,2},{1,3},{2,0},{3,1},{4,6},{5,7},{6,4},{7,5},{8,10},{9,11},{10,... | collective-permute-start | bytes 1179656 | tf_op jit(solution)/shard_map/ppermute | solution.py:104
  155.4 13.4 %collective-permute-start.34 = (bf16[192,1024]{1,0:T(8,128)(2,1)S(1)}, bf16[192,1024]{1,0:T(8,128)(2,1)S(1)}, u32[]{:S(2)}, u32[]{:S(2)}) collective-permute-start(bf16[192,1024]{1,0:T(8,128)(2,1)S(1)} %fusion.2), channel_id=1, source_target_pairs={{0,4},{12,8},{1,5},{13,9},{2,6},{14,10},{3,7},{15,11},{16,20},{28,... | collective-permute-start | bytes 1179656 | tf_op jit(solution)/shard_map/ppermute | solution.py:112
  167.2 12.1 %collective-permute-start.28 = (bf16[192,1024]{1,0:T(8,128)(2,1)S(1)}, bf16[192,1024]{1,0:T(8,128)(2,1)S(1)}, u32[]{:S(2)}, u32[]{:S(2)}) collective-permute-start(bf16[192,1024]{1,0:T(8,128)(2,1)S(1)} %get-tuple-element.112), channel_id=1, source_target_pairs={{0,2},{1,3},{2,0},{3,1},{4,6},{5,7},{6,4},{7,5},{8,10},{9,11},{10,... | collective-permute-start | bytes 1179656 | tf_op jit(solution)/shard_map/ppermute | solution.py:104
  169.7 16.1 %collective-permute-start.27 = (bf16[192,1024]{1,0:T(8,128)(2,1)S(1)}, bf16[192,1024]{1,0:T(8,128)(2,1)S(1)}, u32[]{:S(2)}, u32[]{:S(2)}) collective-permute-start(bf16[192,1024]{1,0:T(8,128)(2,1)S(1)} %get-tuple-element.110), channel_id=1, source_target_pairs={{0,2},{1,3},{2,0},{3,1},{4,6},{5,7},{6,4},{7,5},{8,10},{9,11},{10,... | collective-permute-start | bytes 1179656 | tf_op jit(solution)/shard_map/ppermute | solution.py:104
  (61 other events, 272.1 us)

commit v4 on v3

--- a/solution.py
+++ b/solution.py
@@ -84,16 +84,10 @@
     return combined.astype(jnp.bfloat16)
 
 
-BESIDE = [(0, 1), (1, 0), (2, 3), (3, 2)]
 MIDDLE = [(1, 2), (2, 1)]
 INWARD = [(0, 1), (3, 2)]
 OUTWARD = [(1, 0), (2, 3)]
-PLAN = [
-    [3, 2, 1, 0, 0, 1, 2, 3],
-    [3, 2, 0, 1, 0, 3, 1, 2],
-    [0, 1, 3, 2, 0, 1, 3, 2],
-    [0, 1, 2, 3, 0, 3, 2, 1],
-]
+CHUNK_OWNER = [[3, 2, 1, 0], [3, 2, 0, 1], [0, 1, 3, 2], [0, 1, 2, 3]]
 FACT_ROWS = 16
 VMEM = pl.BlockSpec(memory_space=pltpu.VMEM)
 SMEM = pl.BlockSpec(memory_space=pltpu.SMEM)
@@ -123,28 +117,28 @@
     )
 
 
-def all_there(*arrays):
+def after(block, *others):
     return pl.pallas_call(
         lambda *refs: None,
-        out_shape=[jax.ShapeDtypeStruct(a.shape, a.dtype) for a in arrays],
-        in_specs=[ANYWHERE] * len(arrays),
-        out_specs=[ANYWHERE] * len(arrays),
-        input_output_aliases={i: i for i in range(len(arrays))},
-    )(*arrays)
-
-
-def two_halves(tokens, gates, block_list, block_count, owner):
-    rows, width = tokens.shape
-    half = rows // 2
+        out_shape=jax.ShapeDtypeStruct(block.shape, block.dtype),
+        in_specs=[ANYWHERE] * (1 + len(others)),
+        out_specs=ANYWHERE,
+        input_output_aliases={0: 0},
+        cost_estimate=pl.CostEstimate(flops=16, bytes_accessed=16, transcendentals=0),
+    )(block, *others)
+
+
+def with_facts(rows, gates, block_list, block_count, owner):
+    count, width = rows.shape
     offsets, blocks = block_list.shape
-
-    def body(tokens_ref, gates_ref, list_ref, count_ref, owner_ref, a_ref, b_ref):
-        a_ref[...] = tokens_ref[:half, :]
-        b_ref[:half, :] = tokens_ref[half:, :]
-        block_of = lax.broadcasted_iota(jnp.int32, (1, rows), 1) // (rows // blocks)
+    total = owner.shape[1]
+
+    def body(rows_ref, gates_ref, list_ref, count_ref, owner_ref, out_ref):
+        out_ref[:count, :] = rows_ref[...]
+        block_of = lax.broadcasted_iota(jnp.int32, (1, total), 1) // (total // blocks)
         facts = []
         for offset in range(offsets):
-            mask = jnp.zeros((1, rows), jnp.float32)
+            mask = jnp.zeros((1, total), jnp.float32)
             for block in range(blocks):
                 used = jnp.int32(0)
                 for place in range(blocks):
@@ -154,18 +148,14 @@
             facts.append(gates_ref[offset : offset + 1, :] * mask)
         facts.append((owner_ref[...] >> 8).astype(jnp.float32))
         facts.append((owner_ref[...] & 255).astype(jnp.float32))
-        facts.append(jnp.zeros((FACT_ROWS - len(facts), rows), jnp.float32))
-        b_ref[half:, :] = jnp.zeros((FACT_ROWS, width), jnp.bfloat16)
-        b_ref[half:, :rows] = jnp.concatenate(facts, axis=0).astype(jnp.bfloat16)
-
-    return on_core(
-        body,
-        [
-            jax.ShapeDtypeStruct((half, width), tokens.dtype),
-            jax.ShapeDtypeStruct((half + FACT_ROWS, width), tokens.dtype),
-        ],
-        [VMEM, VMEM, SMEM, SMEM, VMEM],
-    )(tokens, gates, block_list, block_count, owner)
+        facts.append(jnp.zeros((FACT_ROWS - len(facts), total), jnp.float32))
+        out_ref[count:, :] = jnp.zeros((FACT_ROWS, width), jnp.bfloat16)
+        out_ref[count:, :total] = jnp.concatenate(facts, axis=0).astype(jnp.bfloat16)
+
+    shape = jax.ShapeDtypeStruct((count + FACT_ROWS, width), rows.dtype)
+    return on_core(body, shape, [VMEM, VMEM, SMEM, SMEM, VMEM])(
+        rows, gates, block_list, block_count, owner
+    )
 
 
 def partial_sums(rows, parts, weights, places, before=None, send=True, flops=1024):
@@ -201,23 +191,23 @@
     return on_core(body, shapes, [VMEM] * len(operands), flops)(*operands)
 
 
-def collected_rows(owned, slot, plan, sums_parts, got_parts, facts, before):
-    units = sums_parts[0].shape[1] // 4
+def collected_rows(owned, plan, sums, got, facts, picks, before):
+    units = sums.shape[1] // 4
     hidden = []
-    for sums, got in zip(sums_parts, got_parts):
-        part = []
-        for core in range(2):
-            here, there = 2 * core * units, 2 * (1 - core) * units
-            gate = sums[:, here : here + units] + got[:, there : there + units].astype(jnp.float32)
-            up = sums[:, here + units : here + 2 * units]
-            up = up + got[:, there + units : there + 2 * units].astype(jnp.float32)
-            part.append((gate / (1.0 + jnp.exp(-gate)) * up).astype(jnp.bfloat16))
-        hidden.append(jnp.concatenate(part, axis=1))
-    hidden = jnp.concatenate(hidden, axis=0)
-    values = facts[...].astype(jnp.float32)
-    kind = lax.broadcasted_iota(jnp.int32, (FACT_ROWS, 1), 0)
-    factor = jnp.sum(jnp.where(kind == plan[4 + slot], values, 0.0), axis=0, keepdims=True)
-    owner = (values[4:5, :] * 256.0 + values[5:6, :]).astype(jnp.int32)
+    for core in range(2):
+        here, there = 2 * core * units, 2 * (1 - core) * units
+        gate = sums[:, here : here + units] + got[:, there : there + units].astype(jnp.float32)
+        up = sums[:, here + units : here + 2 * units]
+        up = up + got[:, there + units : there + 2 * units].astype(jnp.float32)
+        hidden.append((gate / (1.0 + jnp.exp(-gate)) * up).astype(jnp.bfloat16))
+    hidden = jnp.concatenate(hidden, axis=1)
+    factor, owner = [], []
+    for offset, start, stop in picks:
+        values = facts[plan[4 + offset]].astype(jnp.float32)
+        factor.append(values[offset : offset + 1, start:stop])
+        owner.append(values[4:5, start:stop] * 256.0 + values[5:6, start:stop])
+    factor = jnp.concatenate(factor, axis=1)
+    owner = jnp.concatenate(owner, axis=1).astype(jnp.int32)
     results = []
     for index in range(4):
         token = plan[index] * owned + lax.broadcasted_iota(jnp.int32, (owned, 1), 0)
@@ -229,14 +219,12 @@
     return results
 
 
-def collect(owned, slot, plan, sums, got, facts, before):
+def collect(owned, plan, sums, got, facts, picks, before):
     operands = [plan, sums, got, facts] + ([] if before is None else [before])
 
     def body(plan_ref, sums_ref, got_ref, facts_ref, *rest):
         before_ref = rest[0] if before is not None else None
-        rows = collected_rows(
-            owned, slot, plan_ref, [sums_ref], [got_ref], facts_ref, before_ref
-        )
+        rows = collected_rows(owned, plan_ref, sums_ref, got_ref, facts_ref, picks, before_ref)
         for index in range(4):
             rest[-1][index * owned : (index + 1) * owned, :] = rows[index]
 
@@ -244,15 +232,12 @@
     return on_core(body, shape, [SMEM] + [VMEM] * (len(operands) - 1))(*operands)
 
 
-def finish(owned, slot, plan, sums, got, facts, before, down_own, down_lent):
+def finish(owned, plan, sums, got, facts, picks, before, down_own, down_lent):
     units = down_own.shape[0]
     width = down_own.shape[1] // 2
-    count = len(sums)
-
-    def body(plan_ref, *refs):
-        sums_refs, got_refs = refs[:count], refs[count : 2 * count]
-        facts_ref, before_ref, own_ref, lent_ref, *out_refs = refs[2 * count :]
-        rows = collected_rows(owned, slot, plan_ref, sums_refs, got_refs, facts_ref, before_ref)
+
+    def body(plan_ref, sums_ref, got_ref, facts_ref, before_ref, own_ref, lent_ref, *out_refs):
+        rows = collected_rows(owned, plan_ref, sums_ref, got_ref, facts_ref, picks, before_ref)
         for index in range(4):
             held = rows[index].astype(jnp.bfloat16)
             for out, at in ((4 + index, slice(0, width)), (index, slice(width, 2 * width))):
@@ -265,8 +250,8 @@
         body,
         [jax.ShapeDtypeStruct((owned, width), jnp.bfloat16)] * 4
         + [jax.ShapeDtypeStruct((owned, width), jnp.float32)] * 4,
-        [SMEM] + [VMEM] * (2 * count + 4),
-    )(plan, *sums, *got, facts, before, down_own, down_lent)
+        [SMEM] + [VMEM] * 6,
+    )(plan, sums, got, facts, before, down_own, down_lent)
     return results[:4], results[4:]
 
 
@@ -278,13 +263,36 @@
     row_count, width = tokens.shape
     units = gate_weight.shape[2]
     owned = row_count // 2
-    half = row_count // 2
-    inner = (position == 1) | (position == 2)
-    plan = jnp.asarray(PLAN, jnp.int32)[position]
-
-    own_a, own_b = two_halves(
-        tokens, route_gates.T, block_list[0], block_count[0], owner_token[None]
-    )
+    third = row_count // 3
+    cycle = 4
+    owners = jnp.asarray(CHUNK_OWNER, jnp.int32)[position]
+    plan = jnp.concatenate([owners, (position + jnp.arange(cycle, dtype=jnp.int32)) % cycle])
+
+    def others(gathered):
+        rows = [
+            lax.dynamic_slice(gathered, ((position + s) % cycle, 0, 0), (1, third, width))
+            for s in range(1, cycle)
+        ]
+        return jnp.concatenate(rows).reshape((cycle - 1) * third, width)
+
+    own_far = across_chips(tokens)
+    gathered_0 = lax.all_gather(tokens[:third], "blk")
+    marked = with_facts(
+        tokens[third : 2 * third],
+        route_gates.T,
+        block_list[0],
+        block_count[0],
+        owner_token[None],
+    )
+    gathered_1 = lax.all_gather(marked, "blk")
+    facts = gathered_1[:, third:, :row_count]
+    rows_0 = others(gathered_0)
+    far_0 = across_chips(rows_0)
+    rows_1 = others(gathered_1)
+    far_1 = across_chips(rows_1)
+    gathered_2 = lax.all_gather(after(tokens[2 * third :], gathered_1, own_far, far_0), "blk")
+    rows_2 = after(others(gathered_2), far_1)
+    far_2 = across_chips(rows_2)
 
     gate_quarters = gate_weight[0].reshape(4, width, units)
     up_quarters = up_weight[0].reshape(4, width, units)
@@ -304,91 +312,25 @@
     kept_down = jnp.concatenate([down_part(0), down_part(2)], axis=1)
     lend_down = jnp.concatenate([down_part(1), down_part(3)], axis=1)
 
-    def facts_of(second_half):
-        return second_half[half:, :row_count]
-
-    beside_a = along(own_a, BESIDE)
-    middle_a = along(own_a, MIDDLE)
-    own_far_a = across_chips(own_a)
-    beside_b = along(own_b, BESIDE)
-    middle_b = along(own_b, MIDDLE)
-    own_far_b = across_chips(own_b)
-
-    beside_a, middle_a, own_far_a, lend_in, lend_down, kept_in, kept_down = all_there(
-        beside_a, middle_a, own_far_a, lend_in, lend_down, kept_in, kept_down
-    )
-    inner_last_a = along(beside_a, MIDDLE)
-    outer_next_a = along(middle_a, OUTWARD)
-    beside_far_a = across_chips(beside_a)
     lent_in = across_cores(lend_in)
     lent_down = across_cores(lend_down)
-
-    beside_b, middle_b, own_far_b = all_there(beside_b, middle_b, own_far_b)
-    inner_last_b = along(beside_b, MIDDLE)
-    outer_next_b = along(middle_b, OUTWARD)
-    beside_far_b = across_chips(beside_b)
-    inward_far = along(own_far_b, INWARD)
-
-    inner_last_a, outer_next_a, beside_far_a = all_there(inner_last_a, outer_next_a, beside_far_a)
-    outer_last_a = along(inner_last_a, OUTWARD)
-    second_a = jnp.where(inner, middle_a, outer_next_a)
-    second_far_a = across_chips(second_a)
-
-    inner_last_b, outer_next_b, beside_far_b, inward_far, lent_in, lent_down = all_there(
-        inner_last_b, outer_next_b, beside_far_b, inward_far, lent_in, lent_down
-    )
-    outer_last_b = along(inner_last_b, OUTWARD)
-    second_b = jnp.where(inner, middle_b, outer_next_b)
-    second_far_b = across_chips(second_b)
-    middle_far = along(inward_far, MIDDLE)
     weights = (kept_in, lent_in)
-    sums_0, send_0 = partial_sums(half, [(own_a, own_far_a), (own_b, own_far_b)], weights, (0, 1))
-    got_0 = across_cores(send_0)
-
-    outer_last_a, second_far_a, sums_0, got_0 = all_there(
-        outer_last_a, second_far_a, sums_0, got_0
-    )
-    last_a = jnp.where(inner, inner_last_a, outer_last_a)
-    last_far_a = across_chips(last_a)
-    total = collect(owned, 0, plan, sums_0, got_0, facts_of(own_b), None)
-    sums_1, send_1 = partial_sums(
-        half, [(beside_a, beside_far_a), (beside_b, beside_far_b)], weights, (0, 1)
-    )
-    got_1 = across_cores(send_1)
-
-    outer_last_b, second_far_b, middle_far, total, sums_1, got_1 = all_there(
-        outer_last_b, second_far_b, middle_far, total, sums_1, got_1
-    )
-    outward_far = along(middle_far, OUTWARD)
-    last_b = jnp.where(inner, inner_last_b, outer_last_b)
-    total = collect(owned, 1, plan, sums_1, got_1, facts_of(beside_b), total)
-    sums_2, send_2 = partial_sums(
-        half, [(second_a, second_far_a), (second_b, second_far_b)], weights, (0, 1)
-    )
-    got_2 = across_cores(send_2)
-    near_a = partial_sums(half, [(last_a,)], weights, (0,), send=False)[0]
-    near_b = partial_sums(half, [(last_b,)], weights, (0,), send=False)[0]
-    total = collect(owned, 2, plan, sums_2, got_2, facts_of(second_b), total)
-
-    last_far_a, near_a, near_b, total = all_there(last_far_a, near_a, near_b, total)
-    sums_a, send_a = partial_sums(
-        half, [(last_far_a,)], weights, (1,), before=near_a, flops=3 * 2**30
-    )
-    sums_a, got_a, outward_far = all_there(sums_a, across_cores(send_a), outward_far)
-    last_far_b = jnp.where(inner, middle_far, outward_far)
-    sums_b, send_b = partial_sums(half, [(last_far_b,)], weights, (1,), before=near_b)
-    got_b = across_cores(send_b)
-    sent, kept = finish(
-        owned,
-        3,
-        plan,
-        (sums_a, sums_b),
-        (got_a, got_b),
-        facts_of(last_b),
-        total,
-        kept_down,
-        lent_down,
-    )
+
+    def sums_of(near, far):
+        sums, send = partial_sums(row_count, [(near, far)], weights, (0, 1))
+        return sums, across_cores(send)
+
+    def picks(index):
+        return [(s, index * third, (index + 1) * third) for s in range(1, cycle)]
+
+    sums, got = sums_of(tokens, own_far)
+    total = collect(owned, plan, sums, got, facts, [(0, 0, row_count)], None)
+    sums, got = sums_of(rows_0, far_0)
+    total = collect(owned, plan, sums, got, facts, picks(0), total)
+    sums, got = sums_of(rows_1, far_1)
+    total = collect(owned, plan, sums, got, facts, picks(1), total)
+    sums, got = sums_of(rows_2, far_2)
+    sent, kept = finish(owned, plan, sums, got, facts, picks(2), total, kept_down, lent_down)
     chunks = [k + across_chips(s).astype(jnp.float32) for s, k in zip(sent, kept)]
 
     def send(block, route):

time: 195 us -> 199 us (1.021)
  waiting for transfers between devices: 70.4 us -> 105 us
  starting transfers between devices: 52.1 us -> 25.5 us
  between operations: 0.6 us -> 13.4 us
  local copies, waits for them, and re-layouts: 28.5 us -> 21.5 us
  Pallas kernels: 30.4 us -> 25 us
  other arithmetic: 12.1 us -> 7.91 us
    all_gather x0 -> x3, waiting for transfers between devices: none -> 73.4 us  [the longest x1 28.7 us: rows_travel(): gathered_1 = lax.all_gather(marked, 'blk')]
    ppermute x19 -> x6, starting transfers between devices: 37.6 us -> 12.7 us  [along(): return lax.ppermute(block, 'blk', route)]
    ppermute x19 -> x6, waiting for transfers between devices: 34.1 us -> 12.6 us  [along(): return lax.ppermute(block, 'blk', route)]
    ppermute x11 -> x8, waiting for transfers between devices: 34.6 us -> 19.2 us  [across_chips(): return lax.ppermute(block, 'tp', [(i, i ^ 2) for i in range(4)])]
    unnamed x97 -> x41, local copies, waits for them, and re-layouts: 23.7 us -> 8.63 us
    pallas_call x7 -> x4, Pallas kernels: 21.6 us -> 14.4 us  [partial_sums(): return on_core(body, shapes, [VMEM] * len(operands), flops)(*operands)]
    select_n x5 -> x1, other arithmetic: 5.79 us -> 0.01 us  [rows_travel(): (position + jnp.arange(cycle, dtype=jnp.int32)) % cycle]
    concatenate x0 -> x5, other arithmetic: none -> 3.41 us  [the longest x3 2.04 us: others(): return jnp.concatenate(rows).reshape((cycle - 1) * third, width)]
  transfers between devices with their start and end apart: 37 -> 23, of which waited for: 17 -> 10; matrix products, arithmetic and copies ran while one was open for 7% -> 9% of each run, Pallas kernels for 10% -> 11%
where the time goes in v4:
time: 199 us
  waiting for transfers between devices  105 us (53%)
  starting transfers between devices  25.5 us (13%)
  Pallas kernels  25 us (13%)
  local copies, waits for them, and re-layouts  21.5 us (11%)
  between operations  13.4 us (7%)
  other arithmetic  7.91 us (4%)
    all_gather x1, waiting for transfers between devices, rows_travel(): gathered_1 = lax.all_gather(marked, 'blk')  28.7 us
    all_gather x1, waiting for transfers between devices, rows_travel(): gathered_0 = lax.all_gather(tokens[:third], 'blk')  23.7 us
    all_gather x1, waiting for transfers between devices, rows_travel(): lax.all_gather(after(tokens[2 * third:], gathered_1, own_far, far_0), 'blk')  21 us
    ppermute x8, waiting for transfers between devices, across_chips(): return lax.ppermute(block, 'tp', [(i, i ^ 2) for i in range(4)])  19.2 us
    pallas_call x4, Pallas kernels, partial_sums(): return on_core(body, shapes, [VMEM] * len(operands), flops)(*operands)  14.4 us
    ppermute x6, starting transfers between devices, along(): return lax.ppermute(block, 'blk', route)  12.7 us
    ppermute x6, waiting for transfers between devices, along(): return lax.ppermute(block, 'blk', route)  12.6 us
    ppermute x8, starting transfers between devices, across_chips(): return lax.ppermute(block, 'tp', [(i, i ^ 2) for i in range(4)])  11.7 us
  transfers between devices with their start and end apart: 23, of which 10 were waited for; matrix products, arithmetic and copies ran while one was open for 9% of the time, Pallas kernels for 11%

profile of v4, /device:TPU:0, one launch (start us, length us, event | category | flops | bytes accessed | tf_op | source)
XLA Modules:
  0.0 198.6 jit_solution(1120132741602997690)
XLA Ops:
  6.5 2.0 %fusion.5 = (bf16[128,1024]{1,0:T(8,128)(2,1)}, bf16[128,1024]{1,0:T(8,128)(2,1)S(1)}, bf16[128,1024]{1,0:T(8,128)(2,1)}) fusion(bf16[384,1024]{1,0:T(8,128)(2,1)} %refs_0_.1), kind=kLoop, calls=%fused_computation.45 | loop fusion | bytes 1572864 | tf_op jit(solution)/shard_map/slice | solution.py:279
  12.9 3.0 %collective-permute-start = (bf16[384,1024]{1,0:T(8,128)(2,1)S(1)}, bf16[384,1024]{1,0:T(8,128)(2,1)S(1)}, u32[]{:S(2)}, u32[]{:S(2)}) collective-permute-start(bf16[384,1024]{1,0:T(8,128)(2,1)S(1)} %copy-done.1), channel_id=1, source_target_pairs={{0,2},{1,3},{2,0},{3,1},{4,6},{5,7},{6,4},{7,5},{8,10},{9,11},{10,... | collective-permute-start | bytes 2359304 | tf_op jit(solution)/shard_map/ppermute | solution.py:98
  15.9 23.7 %all-gather.9.cloned.1.call-done = bf16[512,1024]{1,0:T(8,128)(2,1)} async-done(((bf16[128,1024]{1,0:T(8,128)(2,1)}), bf16[512,1024]{1,0:T(8,128)(2,1)}) %all-gather.9.cloned.1.call-update) | async-done | bytes 1048592 | tf_op jit(solution)/shard_map/all_gather | solution.py:279
  42.4 28.7 %all-gather.7.cloned.1.call-done = bf16[576,1024]{1,0:T(8,128)(2,1)} async-done(((bf16[144,1024]{1,0:T(8,128)(2,1)}), bf16[576,1024]{1,0:T(8,128)(2,1)}) %all-gather.7.cloned.1.call-update) | async-done | bytes 1179664 | tf_op jit(solution)/shard_map/all_gather | solution.py:287
  71.2 3.4 %dynamic-slice_bitcast_fusion.6 = (bf16[1024,256]{1,0:T(8,128)(2,1)S(1)}, bf16[1024,256]{1,0:T(8,128)(2,1)S(1)}, bf16[1024,256]{1,0:T(8,128)(2,1)S(1)}, bf16[102...) fusion(bf16[4,1024,256]{2,1,0:T(8,128)(2,1)} %bitcast.46, ...), kind=kLoop, calls=%fused_computation.23 | loop fusion | bytes 8388624 | tf_op jit(solution)/shard_map/jit(dynamic_index_in_dim)/squeeze | solution.py:302
  78.8 21.0 %all-gather.11.cloned.1.call-done = bf16[512,1024]{1,0:T(8,128)(2,1)} async-done(((bf16[128,1024]{1,0:T(8,128)(2,1)}), bf16[512,1024]{1,0:T(8,128)(2,1)}) %all-gather.11.cloned.1.call-update) | async-done | bytes 1048592 | tf_op jit(solution)/shard_map/all_gather | solution.py:293
  103.4 2.7 %dynamic-slice_bitcast_fusion.1 = (bf16[256,1024]{1,0:T(8,128)(2,1)S(1)}, bf16[256,1024]{1,0:T(8,128)(2,1)}, bf16[256,1024]{1,0:T(8,128)(2,1)}, bf16[256,1024]{1,0:T(8,128)(2,1)S(1)}) fusion(bf16[1,256,4096]{2,1,0:T(8,128)(2,1)} %param.12, s32[]{:T(128)S(6)} %select_n.94, s32[]{:T(128)S(6)} %select_n.93, s32[]{:T(128)S(6)} %select_n.92, s32[]{:T(128)S(6)} %select_n.95), kind=kLoop, calls=%fused_computation.18 | loop fusion | bytes 4194320 | tf_op jit(solution)/shard_map/dynamic_slice | solution.py:308
  109.0 2.7 %shard_map.97 = (f32[384,1024]{1,0:T(8,128)S(1)}, bf16[384,1024]{1,0:T(8,128)(2,1)}) custom-call(bf16[384,1024]{1,0:T(8,128)(2,1)S(1)} %copy-done.1, bf16[384,1024]{1,0:T(8,128)(2,1)S(1)} %copy-done.5, bf16[2048,512]{1,0:T(8,128)(2,1)S(1)} %maximum_maximum_fusion.refs_2_, bf16[2048,512]{1,0:T(8,128)(2,1)S(1)} %collective-permute-done.4.refs_3_), custom_call_target="tpu_custom_call" | custom-call | flops 1024 | bytes 1024 | tf_op jit(solution)/shard_map/pallas_call | solution.py:191
  112.8 3.8 %shard_map.96 = (f32[384,1024]{1,0:T(8,128)S(1)}, bf16[384,1024]{1,0:T(8,128)(2,1)}) custom-call(bf16[384,1024]{1,0:T(8,128)(2,1)S(1)} %bitcast.39, bf16[384,1024]{1,0:T(8,128)(2,1)} %collective-permute-done.1.refs_3_.refs_1_, bf16[2048,512]{1,0:T(8,128)(2,1)S(1)} %maximum_maximum_fusion.refs_2_, bf16[2048,512]{1,0:T(8,128)(2,1)S(1)} %collective-permute-done.4.refs_3_), custom_call_target="tpu_custom_call" | custom-call | flops 1024 | bytes 1024 | tf_op jit(solution)/shard_map/pallas_call | solution.py:191
  118.3 4.1 %shard_map.95 = (f32[384,1024]{1,0:T(8,128)S(1)}, bf16[384,1024]{1,0:T(8,128)(2,1)}) custom-call(bf16[384,1024]{1,0:T(8,128)(2,1)} %bitcast.9.refs_0_, bf16[384,1024]{1,0:T(8,128)(2,1)} %collective-permute-done.2.refs_1_, bf16[2048,512]{1,0:T(8,128)(2,1)S(1)} %maximum_maximum_fusion.refs_2_, bf16[2048,512]{1,0:T(8,128)(2,1)S(1)} %collective-permute-done.4.refs_3_), custom_call_target="tpu_custom_call" | custom-call | flops 1024 | bytes 1024 | tf_op jit(solution)/shard_map/pallas_call | solution.py:191
  123.7 3.8 %shard_map.94 = (f32[384,1024]{1,0:T(8,128)S(1)}, bf16[384,1024]{1,0:T(8,128)(2,1)}) custom-call(bf16[384,1024]{1,0:T(8,128)(2,1)S(1)} %copy-done, bf16[384,1024]{1,0:T(8,128)(2,1)} %collective-permute-done.3.refs_1_, bf16[2048,512]{1,0:T(8,128)(2,1)S(1)} %maximum_maximum_fusion.refs_2_, bf16[2048,512]{1,0:T(8,128)(2,1)S(1)} %collective-permute-done.4.refs_3_), custom_call_target="tpu_custom_call" | custom-call | flops 1024 | bytes 1024 | tf_op jit(solution)/shard_map/pallas_call | solution.py:191
  133.5 2.1 %shard_map.99.rest_0_ = f32[768,512]{1,0:T(8,128)S(1)} custom-call(s32[8]{0:T(128)S(1)} %pad_add_fusion.plan_ref, f32[384,1024]{1,0:T(8,128)S(1)} %copy-done.11, bf16[384,1024]{1,0:T(8,128)(2,1)} %collective-permute-done.7.got_ref, bf16[4,16,384]{2,1,0:T(8,128)(2,1)S(1)} %slice.16.facts_ref, f32[768,512]{1,0:T(8,128)S(1)} %shard_map.98.rest_0_), custom_call_target="tpu_custom_call" | custom-call | flops 1024 | bytes 1024 | tf_op jit(solution)/shard_map/pallas_call | solution.py:232
  135.7 2.1 %shard_map.100.before_ref = f32[768,512]{1,0:T(8,128)S(1)} custom-call(s32[8]{0:T(128)S(1)} %pad_add_fusion.plan_ref, f32[384,1024]{1,0:T(8,128)S(1)} %copy-done.13, bf16[384,1024]{1,0:T(8,128)(2,1)} %collective-permute-done.6.got_ref, bf16[4,16,384]{2,1,0:T(8,128)(2,1)S(1)} %slice.16.facts_ref, f32[768,512]{1,0:T(8,128)S(1)} %shard_map.99.rest_0_), custom_call_target="tpu_custom_call" | custom-call | flops 1024 | bytes 1024 | tf_op jit(solution)/shard_map/pallas_call | solution.py:232
  137.8 3.7 %shard_map.101 = (bf16[192,1024]{1,0:T(8,128)(2,1)S(1)}, bf16[192,1024]{1,0:T(8,128)(2,1)S(1)}, bf16[192,1024]{1,0:T(8,128)(2,1)S(1)}, bf16[192,1024]{1,0:T(8,12...) custom-call(s32[8]{0:T(128)S(1)} %pad_add_fusion.plan_ref, ...), custom_call_target="tpu_custom_call" | custom-call | flops 1024 | bytes 1024 | tf_op jit(solution)/shard_map/pallas_call | solution.py:249
  143.6 9.9 %collective-permute-done.16 = bf16[192,1024]{1,0:T(8,128)(2,1)S(1)} collective-permute-done((bf16[192,1024]{1,0:T(8,128)(2,1)S(1)}, bf16[192,1024]{1,0:T(8,128)(2,1)S(1)}, u32[]{:S(2)}, u32[]{:S(2)}) %collective-permute-start.16) | collective-permute-done | bytes 393248 | tf_op jit(solution)/shard_map/ppermute | solution.py:98
  153.7 3.4 %collective-permute-start.17 = (bf16[192,1024]{1,0:T(8,128)(2,1)S(1)}, bf16[192,1024]{1,0:T(8,128)(2,1)S(1)}, u32[]{:S(2)}, u32[]{:S(2)}) collective-permute-start(bf16[192,1024]{1,0:T(8,128)(2,1)S(1)} %fusion.2), channel_id=1, source_target_pairs={{0,4},{12,8},{1,5},{13,9},{2,6},{14,10},{3,7},{15,11},{16,20},{28,... | collective-permute-start | bytes 1179656 | tf_op jit(solution)/shard_map/ppermute | solution.py:106
  157.0 4.2 %collective-permute-done.13 = bf16[192,1024]{1,0:T(8,128)(2,1)S(1)} collective-permute-done((bf16[192,1024]{1,0:T(8,128)(2,1)S(1)}, bf16[192,1024]{1,0:T(8,128)(2,1)S(1)}, u32[]{:S(2)}, u32[]{:S(2)}) %collective-permute-start.13) | collective-permute-done | bytes 393248 | tf_op jit(solution)/shard_map/ppermute | solution.py:98
  161.3 3.4 %collective-permute-start.14 = (bf16[192,1024]{1,0:T(8,128)(2,1)S(1)}, bf16[192,1024]{1,0:T(8,128)(2,1)S(1)}, u32[]{:S(2)}, u32[]{:S(2)}) collective-permute-start(bf16[192,1024]{1,0:T(8,128)(2,1)S(1)} %fusion.1), channel_id=1, source_target_pairs={{0,4},{12,8},{1,5},{13,9},{2,6},{14,10},{3,7},{15,11},{16,20},{28,... | collective-permute-start | bytes 1179656 | tf_op jit(solution)/shard_map/ppermute | solution.py:106
  167.7 4.8 %collective-permute-done.14 = bf16[192,1024]{1,0:T(8,128)(2,1)S(1)} collective-permute-done((bf16[192,1024]{1,0:T(8,128)(2,1)S(1)}, bf16[192,1024]{1,0:T(8,128)(2,1)S(1)}, u32[]{:S(2)}, u32[]{:S(2)}) %collective-permute-start.14) | collective-permute-done | bytes 393248 | tf_op jit(solution)/shard_map/ppermute | solution.py:106
  173.4 3.4 %collective-permute-done.11 = bf16[192,1024]{1,0:T(8,128)(2,1)S(1)} collective-permute-done((bf16[192,1024]{1,0:T(8,128)(2,1)S(1)}, bf16[192,1024]{1,0:T(8,128)(2,1)S(1)}, u32[]{:S(2)}, u32[]{:S(2)}) %collective-permute-start.11) | collective-permute-done | bytes 393248 | tf_op jit(solution)/shard_map/ppermute | solution.py:98
  177.0 3.2 %collective-permute-start.12 = (bf16[192,1024]{1,0:T(8,128)(2,1)S(1)}, bf16[192,1024]{1,0:T(8,128)(2,1)S(1)}, u32[]{:S(2)}, u32[]{:S(2)}) collective-permute-start(bf16[192,1024]{1,0:T(8,128)(2,1)S(1)} %get-tuple-element.49), channel_id=1, source_target_pairs={{0,4},{12,8},{1,5},{13,9},{2,6},{14,10},{3,7},{15,11},{16,20},{28,... | collective-permute-start | bytes 1179656 | tf_op jit(solution)/shard_map/ppermute | solution.py:106
  181.6 1.7 collective-permute-done.10
  183.2 3.6 %collective-permute-done.12 = bf16[192,1024]{1,0:T(8,128)(2,1)S(1)} collective-permute-done((bf16[192,1024]{1,0:T(8,128)(2,1)S(1)}, bf16[192,1024]{1,0:T(8,128)(2,1)S(1)}, u32[]{:S(2)}, u32[]{:S(2)}) %collective-permute-start.12) | collective-permute-done | bytes 393248 | tf_op jit(solution)/shard_map/ppermute | solution.py:106
  186.9 4.1 %collective-permute-done.19 = bf16[192,1024]{1,0:T(8,128)(2,1)S(1)} collective-permute-done((bf16[192,1024]{1,0:T(8,128)(2,1)S(1)}, bf16[192,1024]{1,0:T(8,128)(2,1)S(1)}, u32[]{:S(2)}, u32[]{:S(2)}) %collective-permute-start.19) | collective-permute-done | bytes 393248 | tf_op jit(solution)/shard_map/ppermute | solution.py:106
  (101 shorter events, 36.5 us)
Async XLA Ops:
  6.5 33.1 %all-gather.9.cloned.1.call-start = ((), (), s32[]{:S(2)}) async-start(), calls=%async_computation.1 | async-start | bytes 1310720 | tf_op jit(solution)/shard_map/all_gather | solution.py:279
  8.6 62.5 %all-gather.7.cloned.1.call-start = ((), (), s32[]{:S(2)}) async-start(), calls=%async_computation | async-start | bytes 1474560 | tf_op jit(solution)/shard_map/all_gather | solution.py:287
  12.8 87.0 %all-gather.11.cloned.1.call-start = ((), (), s32[]{:S(2)}) async-start(), calls=%async_computation.2 | async-start | bytes 1310720 | tf_op jit(solution)/shard_map/all_gather | solution.py:293
  12.9 29.5 %collective-permute-start = (bf16[384,1024]{1,0:T(8,128)(2,1)S(1)}, bf16[384,1024]{1,0:T(8,128)(2,1)S(1)}, u32[]{:S(2)}, u32[]{:S(2)}) collective-permute-start(bf16[384,1024]{1,0:T(8,128)(2,1)S(1)} %copy-done.1), channel_id=1, source_target_pairs={{0,2},{1,3},{2,0},{3,1},{4,6},{5,7},{6,4},{7,5},{8,10},{9,11},{10,... | collective-permute-start | bytes 2359304 | tf_op jit(solution)/shard_map/ppermute | solution.py:98
  40.9 33.8 %copy-start.2 = (bf16[3,128,1024]{2,1,0:T(8,128)(2,1)}, bf16[3,128,1024]{2,1,0:T(8,128)(2,1)S(1)}, u32[]{:S(2)}) copy-start(bf16[3,128,1024]{2,1,0:T(8,128)(2,1)S(1)} %pad_maximum_fusion.2) | copy-start | bytes 2359300
  40.9 30.3 %collective-permute-start.1 = (bf16[384,1024]{1,0:T(8,128)(2,1)S(1)}, bf16[384,1024]{1,0:T(8,128)(2,1)}, u32[]{:S(2)}, u32[]{:S(2)}) collective-permute-start(bf16[384,1024]{1,0:T(8,128)(2,1)S(1)} %bitcast.38), channel_id=1, source_target_pairs={{0,2},{1,3},{2,0},{3,1},{4,6},{5,7},{6,4},{7,5},{8,10},{9,11},{10,... | collective-permute-start | bytes 2359304 | tf_op jit(solution)/shard_map/ppermute | solution.py:98
  76.1 31.9 %collective-permute-start.4 = (bf16[2048,512]{1,0:T(8,128)(2,1)}, bf16[2048,512]{1,0:T(8,128)(2,1)S(1)}, u32[]{:S(2)}, u32[]{:S(2)}) collective-permute-start(bf16[2048,512]{1,0:T(8,128)(2,1)} %maximum_maximum_fusion.1), channel_id=1, source_target_pairs={{0,1},{1,0},{2,3},{3,2},{4,5},{5,4},{6,7},{7,6},{8,9},{9,8},{10,11... | collective-permute-start | bytes 6291464 | tf_op jit(solution)/shard_map/ppermute | solution.py:102
  77.4 24.6 %collective-permute-start.2 = (bf16[384,1024]{1,0:T(8,128)(2,1)}, bf16[384,1024]{1,0:T(8,128)(2,1)}, u32[]{:S(2)}, u32[]{:S(2)}) collective-permute-start(bf16[384,1024]{1,0:T(8,128)(2,1)} %bitcast.9.refs_0_), channel_id=1, source_target_pairs={{0,2},{1,3},{2,0},{3,1},{4,6},{5,7},{6,4},{7,5},{8,10},{9,11},{10,... | collective-permute-start | bytes 2359304 | tf_op jit(solution)/shard_map/ppermute | solution.py:98
  101.9 21.7 %collective-permute-start.3 = (bf16[384,1024]{1,0:T(8,128)(2,1)}, bf16[384,1024]{1,0:T(8,128)(2,1)}, u32[]{:S(2)}, u32[]{:S(2)}) collective-permute-start(bf16[384,1024]{1,0:T(8,128)(2,1)} %shard_map.93.refs_0_), channel_id=1, source_target_pairs={{0,2},{1,3},{2,0},{3,1},{4,6},{5,7},{6,4},{7,5},{8,10},{9,11},{10,... | collective-permute-start | bytes 2359304 | tf_op jit(solution)/shard_map/ppermute | solution.py:98
  107.2 30.6 %collective-permute-start.9 = (bf16[256,2048]{1,0:T(8,128)(2,1)}, bf16[256,2048]{1,0:T(8,128)(2,1)}, u32[]{:S(2)}, u32[]{:S(2)}) collective-permute-start(bf16[256,2048]{1,0:T(8,128)(2,1)} %pad_maximum_fusion.1), channel_id=1, source_target_pairs={{0,1},{1,0},{2,3},{3,2},{4,5},{5,4},{6,7},{7,6},{8,9},{9,8},{10,11... | collective-permute-start | bytes 3145736 | tf_op jit(solution)/shard_map/ppermute | solution.py:102
  112.8 19.3 %collective-permute-start.8 = (bf16[384,1024]{1,0:T(8,128)(2,1)}, bf16[384,1024]{1,0:T(8,128)(2,1)S(1)}, u32[]{:S(2)}, u32[]{:S(2)}) collective-permute-start(bf16[384,1024]{1,0:T(8,128)(2,1)} %get-tuple-element.28), channel_id=1, source_target_pairs={{0,1},{1,0},{2,3},{3,2},{4,5},{5,4},{6,7},{7,6},{8,9},{9,8},{10,11... | collective-permute-start | bytes 2359304 | tf_op jit(solution)/shard_map/ppermute | solution.py:102
  117.8 15.7 %collective-permute-start.7 = (bf16[384,1024]{1,0:T(8,128)(2,1)}, bf16[384,1024]{1,0:T(8,128)(2,1)}, u32[]{:S(2)}, u32[]{:S(2)}) collective-permute-start(bf16[384,1024]{1,0:T(8,128)(2,1)} %get-tuple-element.26), channel_id=1, source_target_pairs={{0,1},{1,0},{2,3},{3,2},{4,5},{5,4},{6,7},{7,6},{8,9},{9,8},{10,11... | collective-permute-start | bytes 2359304 | tf_op jit(solution)/shard_map/ppermute | solution.py:102
  123.6 12.1 %collective-permute-start.6 = (bf16[384,1024]{1,0:T(8,128)(2,1)}, bf16[384,1024]{1,0:T(8,128)(2,1)}, u32[]{:S(2)}, u32[]{:S(2)}) collective-permute-start(bf16[384,1024]{1,0:T(8,128)(2,1)} %get-tuple-element.24), channel_id=1, source_target_pairs={{0,1},{1,0},{2,3},{3,2},{4,5},{5,4},{6,7},{7,6},{8,9},{9,8},{10,11... | collective-permute-start | bytes 2359304 | tf_op jit(solution)/shard_map/ppermute | solution.py:102
  128.7 9.1 %collective-permute-start.5 = (bf16[384,1024]{1,0:T(8,128)(2,1)}, bf16[384,1024]{1,0:T(8,128)(2,1)S(1)}, u32[]{:S(2)}, u32[]{:S(2)}) collective-permute-start(bf16[384,1024]{1,0:T(8,128)(2,1)} %get-tuple-element.22), channel_id=1, source_target_pairs={{0,1},{1,0},{2,3},{3,2},{4,5},{5,4},{6,7},{7,6},{8,9},{9,8},{10,11... | collective-permute-start | bytes 2359304 | tf_op jit(solution)/shard_map/ppermute | solution.py:102
  141.5 12.0 %collective-permute-start.16 = (bf16[192,1024]{1,0:T(8,128)(2,1)S(1)}, bf16[192,1024]{1,0:T(8,128)(2,1)S(1)}, u32[]{:S(2)}, u32[]{:S(2)}) collective-permute-start(bf16[192,1024]{1,0:T(8,128)(2,1)S(1)} %get-tuple-element.36), channel_id=1, source_target_pairs={{0,2},{1,3},{2,0},{3,1},{4,6},{5,7},{6,4},{7,5},{8,10},{9,11},{10,... | collective-permute-start | bytes 1179656 | tf_op jit(solution)/shard_map/ppermute | solution.py:98
  142.2 19.0 %collective-permute-start.13 = (bf16[192,1024]{1,0:T(8,128)(2,1)S(1)}, bf16[192,1024]{1,0:T(8,128)(2,1)S(1)}, u32[]{:S(2)}, u32[]{:S(2)}) collective-permute-start(bf16[192,1024]{1,0:T(8,128)(2,1)S(1)} %get-tuple-element.34), channel_id=1, source_target_pairs={{0,2},{1,3},{2,0},{3,1},{4,6},{5,7},{6,4},{7,5},{8,10},{9,11},{10,... | collective-permute-start | bytes 1179656 | tf_op jit(solution)/shard_map/ppermute | solution.py:98
  153.7 11.7 %collective-permute-start.17 = (bf16[192,1024]{1,0:T(8,128)(2,1)S(1)}, bf16[192,1024]{1,0:T(8,128)(2,1)S(1)}, u32[]{:S(2)}, u32[]{:S(2)}) collective-permute-start(bf16[192,1024]{1,0:T(8,128)(2,1)S(1)} %fusion.2), channel_id=1, source_target_pairs={{0,4},{12,8},{1,5},{13,9},{2,6},{14,10},{3,7},{15,11},{16,20},{28,... | collective-permute-start | bytes 1179656 | tf_op jit(solution)/shard_map/ppermute | solution.py:106
  161.3 11.2 %collective-permute-start.14 = (bf16[192,1024]{1,0:T(8,128)(2,1)S(1)}, bf16[192,1024]{1,0:T(8,128)(2,1)S(1)}, u32[]{:S(2)}, u32[]{:S(2)}) collective-permute-start(bf16[192,1024]{1,0:T(8,128)(2,1)S(1)} %fusion.1), channel_id=1, source_target_pairs={{0,4},{12,8},{1,5},{13,9},{2,6},{14,10},{3,7},{15,11},{16,20},{28,... | collective-permute-start | bytes 1179656 | tf_op jit(solution)/shard_map/ppermute | solution.py:106
  164.7 12.1 %collective-permute-start.11 = (bf16[192,1024]{1,0:T(8,128)(2,1)S(1)}, bf16[192,1024]{1,0:T(8,128)(2,1)S(1)}, u32[]{:S(2)}, u32[]{:S(2)}) collective-permute-start(bf16[192,1024]{1,0:T(8,128)(2,1)S(1)} %get-tuple-element.32), channel_id=1, source_target_pairs={{0,2},{1,3},{2,0},{3,1},{4,6},{5,7},{6,4},{7,5},{8,10},{9,11},{10,... | collective-permute-start | bytes 1179656 | tf_op jit(solution)/shard_map/ppermute | solution.py:98
  165.5 11.3 %collective-permute-start.18 = (bf16[192,1024]{1,0:T(8,128)(2,1)S(1)}, bf16[192,1024]{1,0:T(8,128)(2,1)S(1)}, u32[]{:S(2)}, u32[]{:S(2)}) collective-permute-start(bf16[192,1024]{1,0:T(8,128)(2,1)S(1)} %add_convert_fusion.2), channel_id=1, source_target_pairs={{4,8},{8,4},{5,9},{9,5},{6,10},{10,6},{7,11},{11,7},{20,24},{24,20... | collective-permute-start | bytes 1179656 | tf_op jit(solution)/shard_map/ppermute | solution.py:106
  166.2 17.0 %collective-permute-start.10 = (bf16[192,1024]{1,0:T(8,128)(2,1)S(1)}, bf16[192,1024]{1,0:T(8,128)(2,1)S(1)}, u32[]{:S(2)}, u32[]{:S(2)}) collective-permute-start(bf16[192,1024]{1,0:T(8,128)(2,1)S(1)} %get-tuple-element.30), channel_id=1, source_target_pairs={{0,2},{1,3},{2,0},{3,1},{4,6},{5,7},{6,4},{7,5},{8,10},{9,11},{10,... | collective-permute-start | bytes 1179656 | tf_op jit(solution)/shard_map/ppermute | solution.py:98
  172.7 10.6 %collective-permute-start.15 = (bf16[192,1024]{1,0:T(8,128)(2,1)S(1)}, bf16[192,1024]{1,0:T(8,128)(2,1)S(1)}, u32[]{:S(2)}, u32[]{:S(2)}) collective-permute-start(bf16[192,1024]{1,0:T(8,128)(2,1)S(1)} %add_convert_fusion.3), channel_id=1, source_target_pairs={{4,8},{8,4},{5,9},{9,5},{6,10},{10,6},{7,11},{11,7},{20,24},{24,20... | collective-permute-start | bytes 1179656 | tf_op jit(solution)/shard_map/ppermute | solution.py:106
  177.0 9.9 %collective-permute-start.12 = (bf16[192,1024]{1,0:T(8,128)(2,1)S(1)}, bf16[192,1024]{1,0:T(8,128)(2,1)S(1)}, u32[]{:S(2)}, u32[]{:S(2)}) collective-permute-start(bf16[192,1024]{1,0:T(8,128)(2,1)S(1)} %get-tuple-element.49), channel_id=1, source_target_pairs={{0,4},{12,8},{1,5},{13,9},{2,6},{14,10},{3,7},{15,11},{16,20},{28,... | collective-permute-start | bytes 1179656 | tf_op jit(solution)/shard_map/ppermute | solution.py:106
  180.3 10.7 %collective-permute-start.19 = (bf16[192,1024]{1,0:T(8,128)(2,1)S(1)}, bf16[192,1024]{1,0:T(8,128)(2,1)S(1)}, u32[]{:S(2)}, u32[]{:S(2)}) collective-permute-start(bf16[192,1024]{1,0:T(8,128)(2,1)S(1)} %get-tuple-element.50), channel_id=1, source_target_pairs={{4,0},{8,12},{5,1},{9,13},{6,2},{10,14},{7,3},{11,15},{20,16},{24,... | collective-permute-start | bytes 1179656 | tf_op jit(solution)/shard_map/ppermute | solution.py:106
  (19 other events, 69.2 us)
Sparse Core Ops, SparseCore 0:
  8.9 30.6 all-gather.8
  41.2 29.9 all-gather.6
  72.7 27.0 all-gather.10

commit v5 on v4

--- a/solution.py
+++ b/solution.py
@@ -84,11 +84,17 @@
     return combined.astype(jnp.bfloat16)
 
 
+BESIDE = [(0, 1), (1, 0), (2, 3), (3, 2)]
 MIDDLE = [(1, 2), (2, 1)]
 INWARD = [(0, 1), (3, 2)]
 OUTWARD = [(1, 0), (2, 3)]
-CHUNK_OWNER = [[3, 2, 1, 0], [3, 2, 0, 1], [0, 1, 3, 2], [0, 1, 2, 3]]
-FACT_ROWS = 16
+PLAN = [
+    [3, 2, 1, 0, 0, 1, 2, 3, 0],
+    [3, 2, 0, 1, 0, 3, 1, 2, 1],
+    [0, 1, 3, 2, 0, 1, 3, 2, 1],
+    [0, 1, 2, 3, 0, 3, 2, 1, 0],
+]
+OFFSETS_AT, INNER_AT = 4, 8
 VMEM = pl.BlockSpec(memory_space=pltpu.VMEM)
 SMEM = pl.BlockSpec(memory_space=pltpu.SMEM)
 ANYWHERE = pl.BlockSpec(memory_space=pl.ANY)
@@ -128,15 +134,12 @@
     )(block, *others)
 
 
-def with_facts(rows, gates, block_list, block_count, owner):
-    count, width = rows.shape
+def row_facts(gates, block_list, block_count, owner):
     offsets, blocks = block_list.shape
     total = owner.shape[1]
 
-    def body(rows_ref, gates_ref, list_ref, count_ref, owner_ref, out_ref):
-        out_ref[:count, :] = rows_ref[...]
+    def body(gates_ref, list_ref, count_ref, owner_ref, *out_refs):
         block_of = lax.broadcasted_iota(jnp.int32, (1, total), 1) // (total // blocks)
-        facts = []
         for offset in range(offsets):
             mask = jnp.zeros((1, total), jnp.float32)
             for block in range(blocks):
@@ -145,37 +148,47 @@
                     found = (list_ref[offset, place] == block) & (place < count_ref[offset])
                     used = used | found.astype(jnp.int32)
                 mask = mask + jnp.where(block_of == block, used.astype(jnp.float32), 0.0)
-            facts.append(gates_ref[offset : offset + 1, :] * mask)
-        facts.append((owner_ref[...] >> 8).astype(jnp.float32))
-        facts.append((owner_ref[...] & 255).astype(jnp.float32))
-        facts.append(jnp.zeros((FACT_ROWS - len(facts), total), jnp.float32))
-        out_ref[count:, :] = jnp.zeros((FACT_ROWS, width), jnp.bfloat16)
-        out_ref[count:, :total] = jnp.concatenate(facts, axis=0).astype(jnp.bfloat16)
-
-    shape = jax.ShapeDtypeStruct((count + FACT_ROWS, width), rows.dtype)
-    return on_core(body, shape, [VMEM, VMEM, SMEM, SMEM, VMEM])(
-        rows, gates, block_list, block_count, owner
-    )
-
-
-def partial_sums(rows, parts, weights, places, before=None, send=True, flops=1024):
-    width = parts[0][0].shape[1]
-    columns = weights[0].shape[1]
-    operands = [block for part in parts for block in part] + list(weights)
+            out_refs[offset][0:1, :] = gates_ref[offset : offset + 1, :] * mask
+            out_refs[offset][1:2, :] = owner_ref[...].astype(jnp.float32)
+
+    shapes = [jax.ShapeDtypeStruct((2, total), jnp.float32)] * offsets
+    return on_core(body, shapes, [VMEM, SMEM, SMEM, VMEM])(gates, block_list, block_count, owner)
+
+
+def partial_sums(parts, weights, places, before=None, send=True, choice=None, waits=()):
+    width, columns = weights[0].shape[0] // 2, weights[0].shape[1]
+    sizes = [part[0].shape[0] for part in parts]
+    blocks = [block for part in parts for block in part]
+    operands = blocks + list(weights)
+    specs = [VMEM] * len(operands)
     if before is not None:
         operands.append(before)
+        specs.append(VMEM)
+    if choice is not None:
+        operands += [choice[0], choice[1]]
+        specs += [SMEM, VMEM]
+    operands += waits
+    specs += [ANYWHERE] * len(waits)
 
     def body(*refs):
-        blocks, results = refs[: len(parts) * len(places)], refs[len(operands) :]
+        results = refs[len(operands) :]
         weight_refs = refs[len(blocks) : len(blocks) + len(weights)]
-        for part in range(len(parts)):
-            span = slice(part * rows, (part + 1) * rows)
+        next_ref = len(blocks) + len(weights)
+        before_ref = refs[next_ref] if before is not None else None
+        next_ref += before is not None
+        start = 0
+        for part, size in enumerate(sizes):
+            span = slice(start, start + size)
+            start += size
+            rows = [refs[part * len(places) + index][...] for index in range(len(places))]
+            if choice is not None and part == len(sizes) - 1:
+                rows[0] = jnp.where(refs[next_ref][INNER_AT] == 1, refs[next_ref + 1][...], rows[0])
             for side in range(2):
                 at = slice(side * columns, (side + 1) * columns)
-                total = None if before is None else refs[len(operands) - 1][span, at]
+                total = None if before is None else before_ref[span, at]
                 for index, place in enumerate(places):
                     product = jnp.dot(
-                        blocks[part * len(places) + index][:rows, :],
+                        rows[index],
                         weight_refs[side][place * width : (place + 1) * width, :],
                         preferred_element_type=jnp.float32,
                     )
@@ -184,14 +197,14 @@
                 if send:
                     results[1][span, at] = total.astype(jnp.bfloat16)
 
-    size = (len(parts) * rows, 2 * columns)
+    size = (sum(sizes), 2 * columns)
     shapes = [jax.ShapeDtypeStruct(size, jnp.float32)]
     if send:
         shapes.append(jax.ShapeDtypeStruct(size, jnp.bfloat16))
-    return on_core(body, shapes, [VMEM] * len(operands), flops)(*operands)
-
-
-def collected_rows(owned, plan, sums, got, facts, picks, before):
+    return on_core(body, shapes, specs)(*operands)
+
+
+def collected_rows(owned, slot, plan, sums, got, facts, before):
     units = sums.shape[1] // 4
     hidden = []
     for core in range(2):
@@ -201,13 +214,8 @@
         up = up + got[:, there + units : there + 2 * units].astype(jnp.float32)
         hidden.append((gate / (1.0 + jnp.exp(-gate)) * up).astype(jnp.bfloat16))
     hidden = jnp.concatenate(hidden, axis=1)
-    factor, owner = [], []
-    for offset, start, stop in picks:
-        values = facts[plan[4 + offset]].astype(jnp.float32)
-        factor.append(values[offset : offset + 1, start:stop])
-        owner.append(values[4:5, start:stop] * 256.0 + values[5:6, start:stop])
-    factor = jnp.concatenate(factor, axis=1)
-    owner = jnp.concatenate(owner, axis=1).astype(jnp.int32)
+    values = facts[plan[OFFSETS_AT + slot]]
+    factor, owner = values[0:1, :], values[1:2, :].astype(jnp.int32)
     results = []
     for index in range(4):
         token = plan[index] * owned + lax.broadcasted_iota(jnp.int32, (owned, 1), 0)
@@ -219,12 +227,12 @@
     return results
 
 
-def collect(owned, plan, sums, got, facts, picks, before):
+def collect(owned, slot, plan, sums, got, facts, before):
     operands = [plan, sums, got, facts] + ([] if before is None else [before])
 
     def body(plan_ref, sums_ref, got_ref, facts_ref, *rest):
         before_ref = rest[0] if before is not None else None
-        rows = collected_rows(owned, plan_ref, sums_ref, got_ref, facts_ref, picks, before_ref)
+        rows = collected_rows(owned, slot, plan_ref, sums_ref, got_ref, facts_ref, before_ref)
         for index in range(4):
             rest[-1][index * owned : (index + 1) * owned, :] = rows[index]
 
@@ -232,27 +240,39 @@
     return on_core(body, shape, [SMEM] + [VMEM] * (len(operands) - 1))(*operands)
 
 
-def finish(owned, plan, sums, got, facts, picks, before, down_own, down_lent):
+def down(held, own_ref, lent_ref, sent_ref, kept_ref):
+    units, width = own_ref.shape[0], kept_ref.shape[1]
+    for out, at in ((kept_ref, slice(0, width)), (sent_ref, slice(width, 2 * width))):
+        result = jnp.dot(held[:, :units], own_ref[:, at], preferred_element_type=jnp.float32)
+        result += jnp.dot(held[:, units:], lent_ref[:, at], preferred_element_type=jnp.float32)
+        out[...] = result.astype(out.dtype)
+
+
+def finish(owned, slot, plan, sums, got, facts, before, down_own, down_lent):
     units = down_own.shape[0]
     width = down_own.shape[1] // 2
-
-    def body(plan_ref, sums_ref, got_ref, facts_ref, before_ref, own_ref, lent_ref, *out_refs):
-        rows = collected_rows(owned, plan_ref, sums_ref, got_ref, facts_ref, picks, before_ref)
-        for index in range(4):
-            held = rows[index].astype(jnp.bfloat16)
-            for out, at in ((4 + index, slice(0, width)), (index, slice(width, 2 * width))):
-                result = jnp.dot(
-                    held[:, :units], own_ref[:, at], preferred_element_type=jnp.float32
-                ) + jnp.dot(held[:, units:], lent_ref[:, at], preferred_element_type=jnp.float32)
-                out_refs[out][...] = result.astype(out_refs[out].dtype)
-
-    results = on_core(
-        body,
-        [jax.ShapeDtypeStruct((owned, width), jnp.bfloat16)] * 4
-        + [jax.ShapeDtypeStruct((owned, width), jnp.float32)] * 4,
-        [SMEM] + [VMEM] * 6,
-    )(plan, sums, got, facts, before, down_own, down_lent)
-    return results[:4], results[4:]
+    pair = [
+        jax.ShapeDtypeStruct((owned, width), jnp.bfloat16),
+        jax.ShapeDtypeStruct((owned, width), jnp.float32),
+    ]
+
+    def first(plan_ref, sums_ref, got_ref, facts_ref, before_ref, own_ref, lent_ref, *out_refs):
+        rows = collected_rows(owned, slot, plan_ref, sums_ref, got_ref, facts_ref, before_ref)
+        down(rows[0].astype(jnp.bfloat16), own_ref, lent_ref, out_refs[0], out_refs[1])
+        for index in range(1, 4):
+            out_refs[2][(index - 1) * owned : index * owned, :] = rows[index].astype(jnp.bfloat16)
+
+    def others(held_ref, own_ref, lent_ref, *out_refs):
+        for index in range(3):
+            held = held_ref[index * owned : (index + 1) * owned, :]
+            down(held, own_ref, lent_ref, out_refs[2 * index], out_refs[2 * index + 1])
+
+    held_shape = jax.ShapeDtypeStruct((3 * owned, 2 * units), jnp.bfloat16)
+    sent, kept, held = on_core(first, pair + [held_shape], [SMEM] + [VMEM] * 6)(
+        plan, sums, got, facts, before, down_own, down_lent
+    )
+    rest = on_core(others, pair * 3, [VMEM] * 3)(held, down_own, down_lent)
+    return [sent, *rest[0::2]], [kept, *rest[1::2]]
 
 
 def rows_travel(
@@ -263,36 +283,20 @@
     row_count, width = tokens.shape
     units = gate_weight.shape[2]
     owned = row_count // 2
-    third = row_count // 3
-    cycle = 4
-    owners = jnp.asarray(CHUNK_OWNER, jnp.int32)[position]
-    plan = jnp.concatenate([owners, (position + jnp.arange(cycle, dtype=jnp.int32)) % cycle])
-
-    def others(gathered):
-        rows = [
-            lax.dynamic_slice(gathered, ((position + s) % cycle, 0, 0), (1, third, width))
-            for s in range(1, cycle)
-        ]
-        return jnp.concatenate(rows).reshape((cycle - 1) * third, width)
-
+    half = row_count // 2
+    offsets_all = block_list.shape[1]
+    plan = jnp.asarray(PLAN, jnp.int32)[position]
+    inner = plan[INNER_AT] == 1
+
+    beside = along(tokens, BESIDE)
+    middle = along(tokens, MIDDLE)
     own_far = across_chips(tokens)
-    gathered_0 = lax.all_gather(tokens[:third], "blk")
-    marked = with_facts(
-        tokens[third : 2 * third],
-        route_gates.T,
-        block_list[0],
-        block_count[0],
-        owner_token[None],
-    )
-    gathered_1 = lax.all_gather(marked, "blk")
-    facts = gathered_1[:, third:, :row_count]
-    rows_0 = others(gathered_0)
-    far_0 = across_chips(rows_0)
-    rows_1 = others(gathered_1)
-    far_1 = across_chips(rows_1)
-    gathered_2 = lax.all_gather(after(tokens[2 * third :], gathered_1, own_far, far_0), "blk")
-    rows_2 = after(others(gathered_2), far_1)
-    far_2 = across_chips(rows_2)
+    facts = row_facts(route_gates.T, block_list[0], block_count[0], owner_token[None])
+    facts = [
+        pair if offset == 0 else shifted(pair, "blk", offsets_all - offset)
+        for offset, pair in enumerate(facts)
+    ]
+    facts = jnp.stack(facts)
 
     gate_quarters = gate_weight[0].reshape(4, width, units)
     up_quarters = up_weight[0].reshape(4, width, units)
@@ -312,25 +316,54 @@
     kept_down = jnp.concatenate([down_part(0), down_part(2)], axis=1)
     lend_down = jnp.concatenate([down_part(1), down_part(3)], axis=1)
 
-    lent_in = across_cores(lend_in)
-    lent_down = across_cores(lend_down)
+
+    inner_last = along(beside, MIDDLE)
+    outer_next = along(middle, OUTWARD)
+    beside_far = across_chips(beside)
+    inward_far = along(own_far[half:], INWARD)
+    lent_in = across_cores(after(lend_in, beside, own_far, facts))
     weights = (kept_in, lent_in)
-
-    def sums_of(near, far):
-        sums, send = partial_sums(row_count, [(near, far)], weights, (0, 1))
-        return sums, across_cores(send)
-
-    def picks(index):
-        return [(s, index * third, (index + 1) * third) for s in range(1, cycle)]
-
-    sums, got = sums_of(tokens, own_far)
-    total = collect(owned, plan, sums, got, facts, [(0, 0, row_count)], None)
-    sums, got = sums_of(rows_0, far_0)
-    total = collect(owned, plan, sums, got, facts, picks(0), total)
-    sums, got = sums_of(rows_1, far_1)
-    total = collect(owned, plan, sums, got, facts, picks(1), total)
-    sums, got = sums_of(rows_2, far_2)
-    sent, kept = finish(owned, plan, sums, got, facts, picks(2), total, kept_down, lent_down)
+    sums_0, send_0 = partial_sums([(tokens, own_far)], weights, (0, 1))
+    got_0 = across_cores(send_0)
+
+    outer_last = along(inner_last, OUTWARD)
+    second = after(
+        jnp.where(inner, middle, outer_next), beside_far, inner_last, inward_far
+    )
+    second_far = across_chips(second)
+    middle_far = along(inward_far, MIDDLE)
+    lent_down = across_cores(after(lend_down, inner_last))
+    total = collect(owned, 0, plan, sums_0, got_0, facts, None)
+    sums_1, send_1 = partial_sums([(beside, beside_far)], weights, (0, 1))
+    got_1 = across_cores(send_1)
+
+    last_a = after(
+        jnp.where(inner, inner_last[:half], outer_last[:half]),
+        second_far,
+        middle_far,
+        sums_1,
+        total,
+    )
+    last_b = jnp.where(inner, inner_last[half:], outer_last[half:])
+    last_far_a = across_chips(last_a)
+    outward_far = along(middle_far, OUTWARD)
+    total = collect(owned, 1, plan, sums_1, got_1, facts, total)
+    sums_2, send_2 = partial_sums([(second, second_far)], weights, (0, 1))
+    got_2 = across_cores(send_2)
+    near = partial_sums([(last_a,), (last_b,)], weights, (0,), send=False)[0]
+    total = collect(owned, 2, plan, sums_2, got_2, facts, total)
+    sums_3, send_3 = partial_sums(
+        [(last_far_a,), (outward_far,)],
+        weights,
+        (1,),
+        before=near,
+        choice=(plan, middle_far),
+        waits=(total,),
+    )
+    got_3 = across_cores(send_3)
+    sent, kept = finish(
+        owned, 3, plan, sums_3, got_3, facts, total, kept_down, lent_down
+    )
     chunks = [k + across_chips(s).astype(jnp.float32) for s, k in zip(sent, kept)]
 
     def send(block, route):

time: 199 us -> 164 us (0.82)
  waiting for transfers between devices: 105 us -> 44.9 us
  starting transfers between devices: 25.5 us -> 55.6 us
  between operations: 13.4 us -> 1.15 us
  Pallas kernels: 25 us -> 28.8 us
  other arithmetic: 7.91 us -> 11.7 us
    all_gather x3 -> x0, waiting for transfers between devices: 73.4 us -> none  [the longest x1 28.7 us: rows_travel(): gathered_1 = lax.all_gather(marked, 'blk')]
    ppermute x6 -> x14, starting transfers between devices: 12.7 us -> 35.9 us  [along(): return lax.ppermute(block, 'blk', route)]
    ppermute x0 -> x3, starting transfers between devices: none -> 11.3 us  [shifted(): return lax.ppermute(block, axis, route)]
    ppermute x6 -> x14, waiting for transfers between devices: 12.6 us -> 23.1 us  [along(): return lax.ppermute(block, 'blk', route)]
    unnamed x41 -> x55, local copies, waits for them, and re-layouts: 8.63 us -> 13.8 us
    ppermute x8, starting transfers between devices: 11.7 us -> 7.38 us  [across_chips(): return lax.ppermute(block, 'tp', [(i, i ^ 2) for i in range(4)])]
    select_n x1 -> x2, other arithmetic: 0.01 us -> 4.13 us  [the longest x1 2.19 us: rows_travel(): jnp.where(inner, middle, outer_next)]
    pallas_call x6 -> x8, Pallas kernels: 19.5 us -> 22.8 us  [the longest x5 19 us: partial_sums(): return on_core(body, shapes, specs)(*operands)]
  transfers between devices with their start and end apart: 23 -> 31, of which waited for: 10 -> 11; matrix products, arithmetic and copies ran while one was open for 9% -> 12% of each run, Pallas kernels for 11% -> 17%
where the time goes in v5:
time: 164 us; the launch traced here: 163 us
  starting transfers between devices  55.6 us (34%)
  waiting for transfers between devices  44.9 us (27%)
  Pallas kernels  28.8 us (18%)
  local copies, waits for them, and re-layouts  21.4 us (13%)
  other arithmetic  11.7 us (7%)
    ppermute x14, starting transfers between devices, along(): return lax.ppermute(block, 'blk', route)  35.9 us
    ppermute x14, waiting for transfers between devices, along(): return lax.ppermute(block, 'blk', route)  23.1 us
    pallas_call x5, Pallas kernels, partial_sums(): return on_core(body, shapes, specs)(*operands)  19 us
    ppermute x8, waiting for transfers between devices, across_chips(): return lax.ppermute(block, 'tp', [(i, i ^ 2) for i in range(4)])  17.1 us
    unnamed x55, local copies, waits for them, and re-layouts  13.8 us
    ppermute x3, starting transfers between devices, shifted(): return lax.ppermute(block, axis, route)  11.3 us
    ppermute x8, starting transfers between devices, across_chips(): return lax.ppermute(block, 'tp', [(i, i ^ 2) for i in range(4)])  7.38 us
    pallas_call x3, Pallas kernels, collect(): on_core(body, shape, [SMEM] + [VMEM] * (len(operands) - 1))(*operands)  5.93 us
  transfers between devices with their start and end apart: 31, of which 11 were waited for; matrix products, arithmetic and copies ran while one was open for 12% of the time, Pallas kernels for 17%

profile of v5, /device:TPU:0, one launch (start us, length us, event | category | flops | bytes accessed | tf_op | source)
XLA Modules:
  0.0 163.4 jit_solution(14278532393917051827)
XLA Ops:
  0.0 3.0 %collective-permute-start = (bf16[384,1024]{1,0:T(8,128)(2,1)}, bf16[384,1024]{1,0:T(8,128)(2,1)S(1)}, u32[]{:S(2)}, u32[]{:S(2)}) collective-permute-start(bf16[384,1024]{1,0:T(8,128)(2,1)} %refs_0_.1), channel_id=1, source_target_pairs={{0,4},{4,0},{8,12},{12,8},{1,5},{5,1},{9,13},{13,9},{2,6},{6,2},{1... | collective-permute-start | bytes 2359304 | tf_op jit(solution)/shard_map/ppermute | solution.py:112
  9.5 2.5 %collective-permute-start.10 = (f32[2,384]{1,0:T(2,128)S(1)}, f32[2,384]{1,0:T(2,128)S(1)}, u32[]{:S(2)}, u32[]{:S(2)}) collective-permute-start(f32[2,384]{1,0:T(2,128)S(1)} %get-tuple-element.27), channel_id=1, source_target_pairs={{4,0},{8,4},{12,8},{0,12},{5,1},{9,5},{13,9},{1,13},{6,2},{10,6},{... | collective-permute-start | bytes 9224 | tf_op jit(solution)/shard_map/ppermute | solution.py:12
  12.0 2.5 %collective-permute-start.11 = (f32[2,384]{1,0:T(2,128)S(1)}, f32[2,384]{1,0:T(2,128)S(1)}, u32[]{:S(2)}, u32[]{:S(2)}) collective-permute-start(f32[2,384]{1,0:T(2,128)S(1)} %get-tuple-element.28), channel_id=1, source_target_pairs={{8,0},{12,4},{0,8},{4,12},{9,1},{13,5},{1,9},{5,13},{10,2},{14,6},... | collective-permute-start | bytes 9224 | tf_op jit(solution)/shard_map/ppermute | solution.py:12
  14.5 3.4 %dynamic-slice_bitcast_fusion.6 = (bf16[1024,256]{1,0:T(8,128)(2,1)S(1)}, bf16[1024,256]{1,0:T(8,128)(2,1)S(1)}, bf16[1024,256]{1,0:T(8,128)(2,1)S(1)}, bf16[102...) fusion(bf16[4,1024,256]{2,1,0:T(8,128)(2,1)} %bitcast.40, ...), kind=kLoop, calls=%fused_computation.21 | loop fusion | bytes 8388624 | tf_op jit(solution)/shard_map/jit(dynamic_index_in_dim)/squeeze | solution.py:306
  17.9 2.9 %collective-permute-done.10 = f32[2,384]{1,0:T(2,128)S(1)} collective-permute-done((f32[2,384]{1,0:T(2,128)S(1)}, f32[2,384]{1,0:T(2,128)S(1)}, u32[]{:S(2)}, u32[]{:S(2)}) %collective-permute-start.10) | collective-permute-done | bytes 3104 | tf_op jit(solution)/shard_map/ppermute | solution.py:12
  20.8 6.2 %collective-permute-start.12 = (f32[2,384]{1,0:T(2,128)S(1)}, f32[2,384]{1,0:T(2,128)S(1)}, u32[]{:S(2)}, u32[]{:S(2)}) collective-permute-start(f32[2,384]{1,0:T(2,128)S(1)} %get-tuple-element.29), channel_id=1, source_target_pairs={{12,0},{0,4},{4,8},{8,12},{13,1},{1,5},{5,9},{9,13},{14,2},{2,6},{... | collective-permute-start | bytes 9224 | tf_op jit(solution)/shard_map/ppermute | solution.py:12
  34.6 7.3 %collective-permute-start.7 = (bf16[192,1024]{1,0:T(8,128)(2,1)S(1)}, bf16[192,1024]{1,0:T(8,128)(2,1)}, u32[]{:S(2)}, u32[]{:S(2)}) collective-permute-start(bf16[192,1024]{1,0:T(8,128)(2,1)S(1)} %slice.27), channel_id=1, source_target_pairs={{0,4},{12,8},{1,5},{13,9},{2,6},{14,10},{3,7},{15,11},{16,20},{28,... | collective-permute-start | bytes 1179656 | tf_op jit(solution)/shard_map/ppermute | solution.py:112
  43.8 9.3 %collective-permute-done.4 = bf16[384,1024]{1,0:T(8,128)(2,1)} collective-permute-done((bf16[384,1024]{1,0:T(8,128)(2,1)}, bf16[384,1024]{1,0:T(8,128)(2,1)}, u32[]{:S(2)}, u32[]{:S(2)}) %collective-permute-start.4) | collective-permute-done | bytes 786464 | tf_op jit(solution)/shard_map/ppermute | solution.py:112
  53.1 2.2 %broadcast_select_fusion.refs_0_ = bf16[384,1024]{1,0:T(8,128)(2,1)} fusion(bf16[384,1024]{1,0:T(8,128)(2,1)} %collective-permute-done.3, bf16[384,1024]{1,0:T(8,128)(2,1)} %collective-permute-done.4, pred[]{:T(512)} %bitcast.1), kind=kLoop, calls=%fused_computation.11 | loop fusion | flops 393216 | bytes 2359297 | tf_op jit(solution)/shard_map/jit(_where)/select_n | solution.py:331
  60.6 4.4 %shard_map.95 = (f32[384,1024]{1,0:T(8,128)S(1)}, bf16[384,1024]{1,0:T(8,128)(2,1)}) custom-call(bf16[384,1024]{1,0:T(8,128)(2,1)S(1)} %copy-done.18, bf16[384,1024]{1,0:T(8,128)(2,1)S(1)} %copy-done.6, bf16[2048,512]{1,0:T(8,128)(2,1)S(1)} %maximum_maximum_fusion.refs_2_, bf16[2048,512]{1,0:T(8,128)(2,1)} %collective-permute-done.13.refs_3_), custom_call_target="tpu_custom_call" | custom-call | flops 1024 | bytes 1024 | tf_op jit(solution)/shard_map/pallas_call | solution.py:204
  67.9 4.4 %shard_map.94 = (f32[384,1024]{1,0:T(8,128)S(1)}, bf16[384,1024]{1,0:T(8,128)(2,1)}) custom-call(bf16[384,1024]{1,0:T(8,128)(2,1)S(1)} %copy-done.9, bf16[384,1024]{1,0:T(8,128)(2,1)S(1)} %copy-done.11, bf16[2048,512]{1,0:T(8,128)(2,1)S(1)} %maximum_maximum_fusion.refs_2_, bf16[2048,512]{1,0:T(8,128)(2,1)} %collective-permute-done.13.refs_3_), custom_call_target="tpu_custom_call" | custom-call | flops 1024 | bytes 1024 | tf_op jit(solution)/shard_map/pallas_call | solution.py:204
  74.0 2.6 %collective-permute-done.8.refs_1_ = bf16[384,1024]{1,0:T(8,128)(2,1)} collective-permute-done((bf16[384,1024]{1,0:T(8,128)(2,1)}, bf16[384,1024]{1,0:T(8,128)(2,1)}, u32[]{:S(2)}, u32[]{:S(2)}) %collective-permute-start.8) | collective-permute-done | bytes 786464 | tf_op jit(solution)/shard_map/ppermute | solution.py:104
  76.6 4.6 %shard_map.99 = (f32[384,1024]{1,0:T(8,128)S(1)}, bf16[384,1024]{1,0:T(8,128)(2,1)}) custom-call(bf16[384,1024]{1,0:T(8,128)(2,1)S(1)} %copy-done.2, bf16[384,1024]{1,0:T(8,128)(2,1)} %collective-permute-done.8.refs_1_, bf16[2048,512]{1,0:T(8,128)(2,1)S(1)} %maximum_maximum_fusion.refs_2_, bf16[2048,512]{1,0:T(8,128)(2,1)} %collective-permute-done.13.refs_3_), custom_call_target="tpu_custom_call" | custom-call | flops 1024 | bytes 1024 | tf_op jit(solution)/shard_map/pallas_call | solution.py:204
  90.1 2.1 %pad_maximum_fusion.1.refs_0_ = bf16[256,2048]{1,0:T(8,128)(2,1)} fusion(bf16[256,1024]{1,0:T(8,128)(2,1)} %get-tuple-element.50, bf16[256,1024]{1,0:T(8,128)(2,1)S(1)} %get-tuple-element.47), kind=kLoop, calls=%fused_computation.3 | loop fusion | flops 2097152 | bytes 2097152 | tf_op jit(solution)/shard_map/concatenate | solution.py:317
  97.1 2.7 %shard_map.98.refs_4_ = f32[384,1024]{1,0:T(8,128)S(1)} custom-call(bf16[192,1024]{1,0:T(8,128)(2,1)S(1)} %copy-done.7, bf16[192,1024]{1,0:T(8,128)(2,1)S(1)} %get-tuple-element.59.refs_1_, bf16[2048,512]{1,0:T(8,128)(2,1)S(1)} %maximum_maximum_fusion.refs_2_, bf16[2048,512]{1,0:T(8,128)(2,1)} %collective-permute-done.13.refs_3_), custom_call_target="tpu_custom_call" | custom-call | flops 1024 | bytes 1024 | tf_op jit(solution)/shard_map/pallas_call | solution.py:204
  101.9 3.0 %shard_map.102 = (f32[384,1024]{1,0:T(8,128)S(1)}, bf16[384,1024]{1,0:T(8,128)(2,1)S(1)}) custom-call(bf16[192,1024]{1,0:T(8,128)(2,1)} %collective-permute-done.15.refs_0_, bf16[192,1024]{1,0:T(8,128)(2,1)} %collective-permute-done.16.refs_1_, bf16[2048,512]{1,0:T(8,128)(2,1)S(1)} %maximum_maximum_fusion.refs_2_, ...), custom_call_target="tpu_custom_call" | custom-call | flops 1024 | bytes 1024 | tf_op jit(solution)/shard_map/pallas_call | solution.py:204
  112.7 8.4 %collective-permute-done.27 = bf16[192,1024]{1,0:T(8,128)(2,1)S(1)} collective-permute-done((bf16[192,1024]{1,0:T(8,128)(2,1)S(1)}, bf16[192,1024]{1,0:T(8,128)(2,1)S(1)}, u32[]{:S(2)}, u32[]{:S(2)}) %collective-permute-start.27) | collective-permute-done | bytes 393248 | tf_op jit(solution)/shard_map/ppermute | solution.py:104
  121.2 5.8 %collective-permute-start.28 = (bf16[192,1024]{1,0:T(8,128)(2,1)S(1)}, bf16[192,1024]{1,0:T(8,128)(2,1)S(1)}, u32[]{:S(2)}, u32[]{:S(2)}) collective-permute-start(bf16[192,1024]{1,0:T(8,128)(2,1)S(1)} %fusion.2), channel_id=1, source_target_pairs={{0,4},{12,8},{1,5},{13,9},{2,6},{14,10},{3,7},{15,11},{16,20},{28,... | collective-permute-start | bytes 1179656 | tf_op jit(solution)/shard_map/ppermute | solution.py:112
  129.0 5.8 %collective-permute-start.25 = (bf16[192,1024]{1,0:T(8,128)(2,1)S(1)}, bf16[192,1024]{1,0:T(8,128)(2,1)S(1)}, u32[]{:S(2)}, u32[]{:S(2)}) collective-permute-start(bf16[192,1024]{1,0:T(8,128)(2,1)S(1)} %fusion.1), channel_id=1, source_target_pairs={{0,4},{12,8},{1,5},{13,9},{2,6},{14,10},{3,7},{15,11},{16,20},{28,... | collective-permute-start | bytes 1179656 | tf_op jit(solution)/shard_map/ppermute | solution.py:112
  137.9 5.0 %collective-permute-done.25 = bf16[192,1024]{1,0:T(8,128)(2,1)S(1)} collective-permute-done((bf16[192,1024]{1,0:T(8,128)(2,1)S(1)}, bf16[192,1024]{1,0:T(8,128)(2,1)S(1)}, u32[]{:S(2)}, u32[]{:S(2)}) %collective-permute-start.25) | collective-permute-done | bytes 393248 | tf_op jit(solution)/shard_map/ppermute | solution.py:112
  143.8 3.2 %collective-permute-done.22 = bf16[192,1024]{1,0:T(8,128)(2,1)S(1)} collective-permute-done((bf16[192,1024]{1,0:T(8,128)(2,1)S(1)}, bf16[192,1024]{1,0:T(8,128)(2,1)S(1)}, u32[]{:S(2)}, u32[]{:S(2)}) %collective-permute-start.22) | collective-permute-done | bytes 393248 | tf_op jit(solution)/shard_map/ppermute | solution.py:104
  147.2 4.2 %collective-permute-start.23 = (bf16[192,1024]{1,0:T(8,128)(2,1)S(1)}, bf16[192,1024]{1,0:T(8,128)(2,1)S(1)}, u32[]{:S(2)}, u32[]{:S(2)}) collective-permute-start(bf16[192,1024]{1,0:T(8,128)(2,1)S(1)} %get-tuple-element.61), channel_id=1, source_target_pairs={{0,4},{12,8},{1,5},{13,9},{2,6},{14,10},{3,7},{15,11},{16,20},{28,... | collective-permute-start | bytes 1179656 | tf_op jit(solution)/shard_map/ppermute | solution.py:112
  153.6 4.6 %collective-permute-done.23 = bf16[192,1024]{1,0:T(8,128)(2,1)S(1)} collective-permute-done((bf16[192,1024]{1,0:T(8,128)(2,1)S(1)}, bf16[192,1024]{1,0:T(8,128)(2,1)S(1)}, u32[]{:S(2)}, u32[]{:S(2)}) %collective-permute-start.23) | collective-permute-done | bytes 393248 | tf_op jit(solution)/shard_map/ppermute | solution.py:112
  158.2 4.1 %collective-permute-done.30 = bf16[192,1024]{1,0:T(8,128)(2,1)S(1)} collective-permute-done((bf16[192,1024]{1,0:T(8,128)(2,1)S(1)}, bf16[192,1024]{1,0:T(8,128)(2,1)S(1)}, u32[]{:S(2)}, u32[]{:S(2)}) %collective-permute-start.30) | collective-permute-done | bytes 393248 | tf_op jit(solution)/shard_map/ppermute | solution.py:112
  (127 shorter events, 58.1 us)
Async XLA Ops:
  0.0 29.2 %collective-permute-start = (bf16[384,1024]{1,0:T(8,128)(2,1)}, bf16[384,1024]{1,0:T(8,128)(2,1)S(1)}, u32[]{:S(2)}, u32[]{:S(2)}) collective-permute-start(bf16[384,1024]{1,0:T(8,128)(2,1)} %refs_0_.1), channel_id=1, source_target_pairs={{0,4},{4,0},{8,12},{12,8},{1,5},{5,1},{9,13},{13,9},{2,6},{6,2},{1... | collective-permute-start | bytes 2359304 | tf_op jit(solution)/shard_map/ppermute | solution.py:112
  3.0 26.2 %collective-permute-start.6 = (bf16[384,1024]{1,0:T(8,128)(2,1)}, bf16[384,1024]{1,0:T(8,128)(2,1)S(1)}, u32[]{:S(2)}, u32[]{:S(2)}) collective-permute-start(bf16[384,1024]{1,0:T(8,128)(2,1)} %refs_0_.1), channel_id=1, source_target_pairs={{0,2},{1,3},{2,0},{3,1},{4,6},{5,7},{6,4},{7,5},{8,10},{9,11},{10,... | collective-permute-start | bytes 2359304 | tf_op jit(solution)/shard_map/ppermute | solution.py:104
  4.5 26.5 %collective-permute-start.3 = (bf16[384,1024]{1,0:T(8,128)(2,1)}, bf16[384,1024]{1,0:T(8,128)(2,1)}, u32[]{:S(2)}, u32[]{:S(2)}) collective-permute-start(bf16[384,1024]{1,0:T(8,128)(2,1)} %refs_0_.1), channel_id=1, source_target_pairs={{4,8},{8,4},{5,9},{9,5},{6,10},{10,6},{7,11},{11,7},{20,24},{24,20... | collective-permute-start | bytes 2359304 | tf_op jit(solution)/shard_map/ppermute | solution.py:112
  12.0 16.5 %collective-permute-start.11 = (f32[2,384]{1,0:T(2,128)S(1)}, f32[2,384]{1,0:T(2,128)S(1)}, u32[]{:S(2)}, u32[]{:S(2)}) collective-permute-start(f32[2,384]{1,0:T(2,128)S(1)} %get-tuple-element.28), channel_id=1, source_target_pairs={{8,0},{12,4},{0,8},{4,12},{9,1},{13,5},{1,9},{5,13},{10,2},{14,6},... | collective-permute-start | bytes 9224 | tf_op jit(solution)/shard_map/ppermute | solution.py:12
  31.0 29.4 %collective-permute-start.13 = (bf16[2048,512]{1,0:T(8,128)(2,1)}, bf16[2048,512]{1,0:T(8,128)(2,1)}, u32[]{:S(2)}, u32[]{:S(2)}) collective-permute-start(bf16[2048,512]{1,0:T(8,128)(2,1)} %shard_map.93), channel_id=1, source_target_pairs={{0,1},{1,0},{2,3},{3,2},{4,5},{5,4},{6,7},{7,6},{8,9},{9,8},{10,11... | collective-permute-start | bytes 6291464 | tf_op jit(solution)/shard_map/ppermute | solution.py:108
  31.0 22.2 %collective-permute-start.4 = (bf16[384,1024]{1,0:T(8,128)(2,1)}, bf16[384,1024]{1,0:T(8,128)(2,1)}, u32[]{:S(2)}, u32[]{:S(2)}) collective-permute-start(bf16[384,1024]{1,0:T(8,128)(2,1)} %collective-permute-done.3), channel_id=1, source_target_pairs={{4,0},{8,12},{5,1},{9,13},{6,2},{10,14},{7,3},{11,15},{20,16},{24,... | collective-permute-start | bytes 2359304 | tf_op jit(solution)/shard_map/ppermute | solution.py:112
  32.3 23.1 %collective-permute-start.5 = (bf16[384,1024]{1,0:T(8,128)(2,1)}, bf16[384,1024]{1,0:T(8,128)(2,1)S(1)}, u32[]{:S(2)}, u32[]{:S(2)}) collective-permute-start(bf16[384,1024]{1,0:T(8,128)(2,1)} %copy-done.8), channel_id=1, source_target_pairs={{0,2},{1,3},{2,0},{3,1},{4,6},{5,7},{6,4},{7,5},{8,10},{9,11},{10,... | collective-permute-start | bytes 2359304 | tf_op jit(solution)/shard_map/ppermute | solution.py:104
  32.8 22.5 %collective-permute-start.1 = (bf16[384,1024]{1,0:T(8,128)(2,1)}, bf16[384,1024]{1,0:T(8,128)(2,1)S(1)}, u32[]{:S(2)}, u32[]{:S(2)}) collective-permute-start(bf16[384,1024]{1,0:T(8,128)(2,1)} %copy-done.8), channel_id=1, source_target_pairs={{4,8},{8,4},{5,9},{9,5},{6,10},{10,6},{7,11},{11,7},{20,24},{24,20... | collective-permute-start | bytes 2359304 | tf_op jit(solution)/shard_map/ppermute | solution.py:112
  34.6 20.8 %collective-permute-start.7 = (bf16[192,1024]{1,0:T(8,128)(2,1)S(1)}, bf16[192,1024]{1,0:T(8,128)(2,1)}, u32[]{:S(2)}, u32[]{:S(2)}) collective-permute-start(bf16[192,1024]{1,0:T(8,128)(2,1)S(1)} %slice.27), channel_id=1, source_target_pairs={{0,4},{12,8},{1,5},{13,9},{2,6},{14,10},{3,7},{15,11},{16,20},{28,... | collective-permute-start | bytes 1179656 | tf_op jit(solution)/shard_map/ppermute | solution.py:112
  57.1 19.5 %collective-permute-start.8 = (bf16[384,1024]{1,0:T(8,128)(2,1)}, bf16[384,1024]{1,0:T(8,128)(2,1)}, u32[]{:S(2)}, u32[]{:S(2)}) collective-permute-start(bf16[384,1024]{1,0:T(8,128)(2,1)} %shard_map.91.refs_0_), channel_id=1, source_target_pairs={{0,2},{1,3},{2,0},{3,1},{4,6},{5,7},{6,4},{7,5},{8,10},{9,11},{10,... | collective-permute-start | bytes 2359304 | tf_op jit(solution)/shard_map/ppermute | solution.py:104
  57.6 26.9 %collective-permute-start.2 = (bf16[384,1024]{1,0:T(8,128)(2,1)}, bf16[384,1024]{1,0:T(8,128)(2,1)}, u32[]{:S(2)}, u32[]{:S(2)}) collective-permute-start(bf16[384,1024]{1,0:T(8,128)(2,1)} %copy-done.22), channel_id=1, source_target_pairs={{4,0},{8,12},{5,1},{9,13},{6,2},{10,14},{7,3},{11,15},{20,16},{24,... | collective-permute-start | bytes 2359304 | tf_op jit(solution)/shard_map/ppermute | solution.py:112
  66.1 20.4 %collective-permute-start.14 = (bf16[384,1024]{1,0:T(8,128)(2,1)}, bf16[384,1024]{1,0:T(8,128)(2,1)}, u32[]{:S(2)}, u32[]{:S(2)}) collective-permute-start(bf16[384,1024]{1,0:T(8,128)(2,1)} %get-tuple-element.32), channel_id=1, source_target_pairs={{0,1},{1,0},{2,3},{3,2},{4,5},{5,4},{6,7},{7,6},{8,9},{9,8},{10,11... | collective-permute-start | bytes 2359304 | tf_op jit(solution)/shard_map/ppermute | solution.py:108
  66.1 16.8 %collective-permute-start.9 = (bf16[192,1024]{1,0:T(8,128)(2,1)}, bf16[192,1024]{1,0:T(8,128)(2,1)S(1)}, u32[]{:S(2)}, u32[]{:S(2)}) collective-permute-start(bf16[192,1024]{1,0:T(8,128)(2,1)} %collective-permute-done.7.refs_3_), channel_id=1, source_target_pairs={{4,8},{8,4},{5,9},{9,5},{6,10},{10,6},{7,11},{11,7},{20,24},{24,20... | collective-permute-start | bytes 1179656 | tf_op jit(solution)/shard_map/ppermute | solution.py:112
  73.5 18.8 %collective-permute-start.18 = (bf16[384,1024]{1,0:T(8,128)(2,1)}, bf16[384,1024]{1,0:T(8,128)(2,1)}, u32[]{:S(2)}, u32[]{:S(2)}) collective-permute-start(bf16[384,1024]{1,0:T(8,128)(2,1)} %get-tuple-element.35), channel_id=1, source_target_pairs={{0,1},{1,0},{2,3},{3,2},{4,5},{5,4},{6,7},{7,6},{8,9},{9,8},{10,11... | collective-permute-start | bytes 2359304 | tf_op jit(solution)/shard_map/ppermute | solution.py:108
  81.1 18.7 %collective-permute-start.17 = (bf16[384,1024]{1,0:T(8,128)(2,1)}, bf16[384,1024]{1,0:T(8,128)(2,1)}, u32[]{:S(2)}, u32[]{:S(2)}) collective-permute-start(bf16[384,1024]{1,0:T(8,128)(2,1)} %get-tuple-element.34), channel_id=1, source_target_pairs={{0,1},{1,0},{2,3},{3,2},{4,5},{5,4},{6,7},{7,6},{8,9},{9,8},{10,11... | collective-permute-start | bytes 2359304 | tf_op jit(solution)/shard_map/ppermute | solution.py:108
  82.9 19.0 %collective-permute-start.16 = (bf16[192,1024]{1,0:T(8,128)(2,1)S(1)}, bf16[192,1024]{1,0:T(8,128)(2,1)}, u32[]{:S(2)}, u32[]{:S(2)}) collective-permute-start(bf16[192,1024]{1,0:T(8,128)(2,1)S(1)} %collective-permute-done.9.refs_2_.refs_6_), channel_id=1, source_target_pairs={{4,0},{8,12},{5,1},{9,13},{6,2},{10,14},{7,3},{11,15},{20,16},{24,... | collective-permute-start | bytes 1179656 | tf_op jit(solution)/shard_map/ppermute | solution.py:112
  89.6 12.3 %collective-permute-start.15 = (bf16[192,1024]{1,0:T(8,128)(2,1)}, bf16[192,1024]{1,0:T(8,128)(2,1)}, u32[]{:S(2)}, u32[]{:S(2)}) collective-permute-start(bf16[192,1024]{1,0:T(8,128)(2,1)} %shard_map.97.refs_0_), channel_id=1, source_target_pairs={{0,2},{1,3},{2,0},{3,1},{4,6},{5,7},{6,4},{7,5},{8,10},{9,11},{10,... | collective-permute-start | bytes 1179656 | tf_op jit(solution)/shard_map/ppermute | solution.py:104
  92.2 13.2 %collective-permute-start.20 = (bf16[256,2048]{1,0:T(8,128)(2,1)}, bf16[256,2048]{1,0:T(8,128)(2,1)S(1)}, u32[]{:S(2)}, u32[]{:S(2)}) collective-permute-start(bf16[256,2048]{1,0:T(8,128)(2,1)} %shard_map.103), channel_id=1, source_target_pairs={{0,1},{1,0},{2,3},{3,2},{4,5},{5,4},{6,7},{7,6},{8,9},{9,8},{10,11... | collective-permute-start | bytes 3145736 | tf_op jit(solution)/shard_map/ppermute | solution.py:108
  109.1 12.0 %collective-permute-start.27 = (bf16[192,1024]{1,0:T(8,128)(2,1)S(1)}, bf16[192,1024]{1,0:T(8,128)(2,1)S(1)}, u32[]{:S(2)}, u32[]{:S(2)}) collective-permute-start(bf16[192,1024]{1,0:T(8,128)(2,1)S(1)} %get-tuple-element.46), channel_id=1, source_target_pairs={{0,2},{1,3},{2,0},{3,1},{4,6},{5,7},{6,4},{7,5},{8,10},{9,11},{10,... | collective-permute-start | bytes 1179656 | tf_op jit(solution)/shard_map/ppermute | solution.py:104
  112.1 16.8 %collective-permute-start.24 = (bf16[192,1024]{1,0:T(8,128)(2,1)S(1)}, bf16[192,1024]{1,0:T(8,128)(2,1)S(1)}, u32[]{:S(2)}, u32[]{:S(2)}) collective-permute-start(bf16[192,1024]{1,0:T(8,128)(2,1)S(1)} %get-tuple-element.44), channel_id=1, source_target_pairs={{0,2},{1,3},{2,0},{3,1},{4,6},{5,7},{6,4},{7,5},{8,10},{9,11},{10,... | collective-permute-start | bytes 1179656 | tf_op jit(solution)/shard_map/ppermute | solution.py:104
  121.2 14.6 %collective-permute-start.28 = (bf16[192,1024]{1,0:T(8,128)(2,1)S(1)}, bf16[192,1024]{1,0:T(8,128)(2,1)S(1)}, u32[]{:S(2)}, u32[]{:S(2)}) collective-permute-start(bf16[192,1024]{1,0:T(8,128)(2,1)S(1)} %fusion.2), channel_id=1, source_target_pairs={{0,4},{12,8},{1,5},{13,9},{2,6},{14,10},{3,7},{15,11},{16,20},{28,... | collective-permute-start | bytes 1179656 | tf_op jit(solution)/shard_map/ppermute | solution.py:112
  129.0 13.9 %collective-permute-start.25 = (bf16[192,1024]{1,0:T(8,128)(2,1)S(1)}, bf16[192,1024]{1,0:T(8,128)(2,1)S(1)}, u32[]{:S(2)}, u32[]{:S(2)}) collective-permute-start(bf16[192,1024]{1,0:T(8,128)(2,1)S(1)} %fusion.1), channel_id=1, source_target_pairs={{0,4},{12,8},{1,5},{13,9},{2,6},{14,10},{3,7},{15,11},{16,20},{28,... | collective-permute-start | bytes 1179656 | tf_op jit(solution)/shard_map/ppermute | solution.py:112
  134.8 12.1 %collective-permute-start.22 = (bf16[192,1024]{1,0:T(8,128)(2,1)S(1)}, bf16[192,1024]{1,0:T(8,128)(2,1)S(1)}, u32[]{:S(2)}, u32[]{:S(2)}) collective-permute-start(bf16[192,1024]{1,0:T(8,128)(2,1)S(1)} %get-tuple-element.42), channel_id=1, source_target_pairs={{0,2},{1,3},{2,0},{3,1},{4,6},{5,7},{6,4},{7,5},{8,10},{9,11},{10,... | collective-permute-start | bytes 1179656 | tf_op jit(solution)/shard_map/ppermute | solution.py:104
  136.7 17.0 %collective-permute-start.21 = (bf16[192,1024]{1,0:T(8,128)(2,1)S(1)}, bf16[192,1024]{1,0:T(8,128)(2,1)S(1)}, u32[]{:S(2)}, u32[]{:S(2)}) collective-permute-start(bf16[192,1024]{1,0:T(8,128)(2,1)S(1)} %get-tuple-element.40), channel_id=1, source_target_pairs={{0,2},{1,3},{2,0},{3,1},{4,6},{5,7},{6,4},{7,5},{8,10},{9,11},{10,... | collective-permute-start | bytes 1179656 | tf_op jit(solution)/shard_map/ppermute | solution.py:104
  (34 other events, 138.0 us)

commit v6 on v5

--- a/solution.py
+++ b/solution.py
@@ -88,13 +88,15 @@
 MIDDLE = [(1, 2), (2, 1)]
 INWARD = [(0, 1), (3, 2)]
 OUTWARD = [(1, 0), (2, 3)]
+TWO_ON = [(0, 2), (3, 1), (1, 3), (2, 0)]
 PLAN = [
     [3, 2, 1, 0, 0, 1, 2, 3, 0],
-    [3, 2, 0, 1, 0, 3, 1, 2, 1],
-    [0, 1, 3, 2, 0, 1, 3, 2, 1],
+    [2, 3, 0, 1, 0, 3, 1, 2, 1],
+    [1, 0, 3, 2, 0, 1, 3, 2, 1],
     [0, 1, 2, 3, 0, 3, 2, 1, 0],
 ]
 OFFSETS_AT, INNER_AT = 4, 8
+FACT_ROWS = 16
 VMEM = pl.BlockSpec(memory_space=pltpu.VMEM)
 SMEM = pl.BlockSpec(memory_space=pltpu.SMEM)
 ANYWHERE = pl.BlockSpec(memory_space=pl.ANY)
@@ -134,12 +136,50 @@
     )(block, *others)
 
 
-def row_facts(gates, block_list, block_count, owner):
+def chosen(plan, if_inner, if_outer, spans, *others):
+    width = if_inner.shape[1]
+
+    def body(plan_ref, inner_ref, outer_ref, *rest):
+        out_refs, sems = rest[len(others) : -1], rest[-1]
+
+        def copy_from(source):
+            copies = [
+                pltpu.make_async_copy(source.at[pl.ds(start, size)], out, sems.at[index])
+                for index, ((start, size), out) in enumerate(zip(spans, out_refs))
+            ]
+            for copy in copies:
+                copy.start()
+            for copy in copies:
+                copy.wait()
+
+        @pl.when(plan_ref[INNER_AT] == 1)
+        def _():
+            copy_from(inner_ref)
+
+        @pl.when(plan_ref[INNER_AT] == 0)
+        def _():
+            copy_from(outer_ref)
+
+    return pl.pallas_call(
+        body,
+        out_shape=[jax.ShapeDtypeStruct((size, width), if_inner.dtype) for _, size in spans],
+        in_specs=[SMEM] + [ANYWHERE] * (2 + len(others)),
+        out_specs=[ANYWHERE] * len(spans),
+        scratch_shapes=[pltpu.SemaphoreType.DMA((len(spans),))],
+        cost_estimate=pl.CostEstimate(flops=16, bytes_accessed=16, transcendentals=0),
+    )(plan, if_inner, if_outer, *others)
+
+
+def with_facts(rows, gates, block_list, block_count, owner):
+    count, width = rows.shape
     offsets, blocks = block_list.shape
     total = owner.shape[1]
 
-    def body(gates_ref, list_ref, count_ref, owner_ref, *out_refs):
+    def body(rows_ref, gates_ref, list_ref, count_ref, owner_ref, out_ref, sem):
+        copy = pltpu.make_async_copy(rows_ref, out_ref.at[pl.ds(0, count)], sem)
+        copy.start()
         block_of = lax.broadcasted_iota(jnp.int32, (1, total), 1) // (total // blocks)
+        facts = []
         for offset in range(offsets):
             mask = jnp.zeros((1, total), jnp.float32)
             for block in range(blocks):
@@ -148,16 +188,29 @@
                     found = (list_ref[offset, place] == block) & (place < count_ref[offset])
                     used = used | found.astype(jnp.int32)
                 mask = mask + jnp.where(block_of == block, used.astype(jnp.float32), 0.0)
-            out_refs[offset][0:1, :] = gates_ref[offset : offset + 1, :] * mask
-            out_refs[offset][1:2, :] = owner_ref[...].astype(jnp.float32)
-
-    shapes = [jax.ShapeDtypeStruct((2, total), jnp.float32)] * offsets
-    return on_core(body, shapes, [VMEM, SMEM, SMEM, VMEM])(gates, block_list, block_count, owner)
-
-
-def partial_sums(parts, weights, places, before=None, send=True, choice=None, waits=()):
+            facts.append(gates_ref[offset : offset + 1, :] * mask)
+        facts.append((owner_ref[...] >> 8).astype(jnp.float32))
+        facts.append((owner_ref[...] & 255).astype(jnp.float32))
+        facts.append(jnp.zeros((FACT_ROWS - len(facts), total), jnp.float32))
+        out_ref[count:, :] = jnp.zeros((FACT_ROWS, width), jnp.bfloat16)
+        out_ref[count:, :total] = jnp.concatenate(facts, axis=0).astype(jnp.bfloat16)
+        copy.wait()
+
+    return pl.pallas_call(
+        body,
+        out_shape=jax.ShapeDtypeStruct((count + FACT_ROWS, width), rows.dtype),
+        in_specs=[ANYWHERE, VMEM, SMEM, SMEM, VMEM],
+        out_specs=VMEM,
+        scratch_shapes=[pltpu.SemaphoreType.DMA],
+        compiler_params=pltpu.CompilerParams(vmem_limit_bytes=40 * 2**20),
+        cost_estimate=pl.CostEstimate(flops=1024, bytes_accessed=1024, transcendentals=0),
+    )(rows, gates, block_list, block_count, owner)
+
+
+def partial_sums(
+    sizes, parts, weights, places, before=None, send=True, choice=None, waits=()
+):
     width, columns = weights[0].shape[0] // 2, weights[0].shape[1]
-    sizes = [part[0].shape[0] for part in parts]
     blocks = [block for part in parts for block in part]
     operands = blocks + list(weights)
     specs = [VMEM] * len(operands)
@@ -180,9 +233,9 @@
         for part, size in enumerate(sizes):
             span = slice(start, start + size)
             start += size
-            rows = [refs[part * len(places) + index][...] for index in range(len(places))]
+            rows = [refs[part * len(places) + index][:size, :] for index in range(len(places))]
             if choice is not None and part == len(sizes) - 1:
-                rows[0] = jnp.where(refs[next_ref][INNER_AT] == 1, refs[next_ref + 1][...], rows[0])
+                rows[0] = jnp.where(refs[next_ref][INNER_AT] == 1, refs[next_ref + 1][:size, :], rows[0])
             for side in range(2):
                 at = slice(side * columns, (side + 1) * columns)
                 total = None if before is None else before_ref[span, at]
@@ -214,8 +267,11 @@
         up = up + got[:, there + units : there + 2 * units].astype(jnp.float32)
         hidden.append((gate / (1.0 + jnp.exp(-gate)) * up).astype(jnp.bfloat16))
     hidden = jnp.concatenate(hidden, axis=1)
-    values = facts[plan[OFFSETS_AT + slot]]
-    factor, owner = values[0:1, :], values[1:2, :].astype(jnp.int32)
+    values = facts[:, : sums.shape[0]].astype(jnp.float32)
+    kind = lax.broadcasted_iota(jnp.int32, (FACT_ROWS, 1), 0)
+    mine = kind == plan[OFFSETS_AT + slot]
+    factor = jnp.sum(jnp.where(mine, values, 0.0), axis=0, keepdims=True)
+    owner = (values[4:5, :] * 256.0 + values[5:6, :]).astype(jnp.int32)
     results = []
     for index in range(4):
         token = plan[index] * owned + lax.broadcasted_iota(jnp.int32, (owned, 1), 0)
@@ -284,19 +340,14 @@
     units = gate_weight.shape[2]
     owned = row_count // 2
     half = row_count // 2
-    offsets_all = block_list.shape[1]
     plan = jnp.asarray(PLAN, jnp.int32)[position]
-    inner = plan[INNER_AT] == 1
-
-    beside = along(tokens, BESIDE)
-    middle = along(tokens, MIDDLE)
+
     own_far = across_chips(tokens)
-    facts = row_facts(route_gates.T, block_list[0], block_count[0], owner_token[None])
-    facts = [
-        pair if offset == 0 else shifted(pair, "blk", offsets_all - offset)
-        for offset, pair in enumerate(facts)
-    ]
-    facts = jnp.stack(facts)
+    own = with_facts(
+        tokens, route_gates.T, block_list[0], block_count[0], owner_token[None]
+    )
+    beside = along(own, BESIDE)
+    middle = along(own, MIDDLE)
 
     gate_quarters = gate_weight[0].reshape(4, width, units)
     up_quarters = up_weight[0].reshape(4, width, units)
@@ -321,38 +372,46 @@
     outer_next = along(middle, OUTWARD)
     beside_far = across_chips(beside)
     inward_far = along(own_far[half:], INWARD)
-    lent_in = across_cores(after(lend_in, beside, own_far, facts))
+    lent_in = across_cores(after(lend_in, beside, middle, own_far))
     weights = (kept_in, lent_in)
-    sums_0, send_0 = partial_sums([(tokens, own_far)], weights, (0, 1))
+    sums_0, send_0 = partial_sums([row_count], [(tokens, own_far)], weights, (0, 1))
     got_0 = across_cores(send_0)
 
     outer_last = along(inner_last, OUTWARD)
-    second = after(
-        jnp.where(inner, middle, outer_next), beside_far, inner_last, inward_far
+    (second, second_facts) = chosen(
+        plan,
+        middle,
+        outer_next,
+        [(0, row_count), (row_count, FACT_ROWS)],
+        beside_far,
+        inner_last,
+        inward_far,
     )
     second_far = across_chips(second)
     middle_far = along(inward_far, MIDDLE)
     lent_down = across_cores(after(lend_down, inner_last))
-    total = collect(owned, 0, plan, sums_0, got_0, facts, None)
-    sums_1, send_1 = partial_sums([(beside, beside_far)], weights, (0, 1))
+    sums_1, send_1 = partial_sums([row_count], [(beside, beside_far)], weights, (0, 1))
     got_1 = across_cores(send_1)
 
-    last_a = after(
-        jnp.where(inner, inner_last[:half], outer_last[:half]),
+    last_a, last_b, last_facts = chosen(
+        plan,
+        inner_last,
+        outer_last,
+        [(0, half), (half, half), (row_count, FACT_ROWS)],
         second_far,
         middle_far,
+        sums_0,
         sums_1,
-        total,
-    )
-    last_b = jnp.where(inner, inner_last[half:], outer_last[half:])
+    )
     last_far_a = across_chips(last_a)
     outward_far = along(middle_far, OUTWARD)
-    total = collect(owned, 1, plan, sums_1, got_1, facts, total)
-    sums_2, send_2 = partial_sums([(second, second_far)], weights, (0, 1))
+    total = collect(owned, 0, plan, sums_0, got_0, own[row_count:], None)
+    total = collect(owned, 1, plan, sums_1, got_1, beside[row_count:], total)
+    sums_2, send_2 = partial_sums([row_count], [(second, second_far)], weights, (0, 1))
     got_2 = across_cores(send_2)
-    near = partial_sums([(last_a,), (last_b,)], weights, (0,), send=False)[0]
-    total = collect(owned, 2, plan, sums_2, got_2, facts, total)
+    near = partial_sums([half, half], [(last_a,), (last_b,)], weights, (0,), send=False)[0]
     sums_3, send_3 = partial_sums(
+        [half, half],
         [(last_far_a,), (outward_far,)],
         weights,
         (1,),
@@ -361,21 +420,20 @@
         waits=(total,),
     )
     got_3 = across_cores(send_3)
+    total = collect(owned, 2, plan, sums_2, got_2, second_facts, total)
     sent, kept = finish(
-        owned, 3, plan, sums_3, got_3, facts, total, kept_down, lent_down
+        owned, 3, plan, sums_3, got_3, last_facts, total, kept_down, lent_down
     )
     chunks = [k + across_chips(s).astype(jnp.float32) for s, k in zip(sent, kept)]
 
     def send(block, route):
         return along(block.astype(jnp.bfloat16), route).astype(jnp.float32)
 
-    first_in = send(chunks[0], INWARD)
-    second_in = send(chunks[1], INWARD)
-    second_mid = send(chunks[0] + first_in, MIDDLE)
-    third_in = send(chunks[2], INWARD)
-    third_mid = send(chunks[1] + second_in, MIDDLE)
-    third_out = send(chunks[2] + second_mid, OUTWARD)
-    return (chunks[3] + third_in + third_mid + third_out).astype(jnp.bfloat16)
+    inward = send(chunks[0], INWARD)
+    middle = send(chunks[0], MIDDLE)
+    two_on = send(chunks[1] + inward, TWO_ON)
+    beside = send(chunks[2], BESIDE)
+    return (chunks[3] + middle + two_on + beside).astype(jnp.bfloat16)
 
 
 def on_device(*args):

time: 164 us -> 209 us (1.27)
  Pallas kernels: 28.8 us -> 81.8 us
  starting transfers between devices: 55.6 us -> 47.3 us
  waiting for transfers between devices: 44.9 us -> 52.3 us
  other arithmetic: 11.7 us -> 6.73 us
  local copies, waits for them, and re-layouts: 21.4 us -> 19.1 us
    pallas_call x1 -> x3, Pallas kernels: 0.63 us -> 54.9 us  [the longest x2 53.2 us: chosen(): pl.pallas_call(body, out_shape=[jax.ShapeDtypeStruct((size, width), if_in...]
    ppermute x3 -> x0, starting transfers between devices: 11.3 us -> none  [shifted(): return lax.ppermute(block, axis, route)]
    ppermute x8, waiting for transfers between devices: 17.1 us -> 25.4 us  [across_chips(): return lax.ppermute(block, 'tp', [(i, i ^ 2) for i in range(4)])]
    unnamed x55 -> x57, local copies, waits for them, and re-layouts: 13.8 us -> 9.04 us
    select_n x2 -> x0, other arithmetic: 4.13 us -> none  [the longest x1 2.19 us: rows_travel(): jnp.where(inner, middle, outer_next)]
    ppermute x14 -> x12, waiting for transfers between devices: 23.1 us -> 26.7 us  [along(): return lax.ppermute(block, 'blk', route)]
    ppermute x3 -> x0, waiting for transfers between devices: 2.92 us -> none  [shifted(): return lax.ppermute(block, axis, route)]
    ppermute x8, starting transfers between devices: 7.38 us -> 9.47 us  [across_chips(): return lax.ppermute(block, 'tp', [(i, i ^ 2) for i in range(4)])]
  transfers between devices with their start and end apart: 31 -> 26, of which waited for: 11 -> 10; matrix products, arithmetic and copies ran while one was open for 12% -> 7% of each run, Pallas kernels for 17% -> 38%
where the time goes in v6:
time: 209 us; the launch traced here: 208 us
  Pallas kernels  81.8 us (39%)
  waiting for transfers between devices  52.3 us (25%)
  starting transfers between devices  47.3 us (23%)
  local copies, waits for them, and re-layouts  19.1 us (9%)
  other arithmetic  6.73 us (3%)
    pallas_call x2, Pallas kernels, chosen(): pl.pallas_call(body, out_shape=[jax.ShapeDtypeStruct((size, width), if_in...  53.2 us
    ppermute x12, starting transfers between devices, along(): return lax.ppermute(block, 'blk', route)  36.6 us
    ppermute x12, waiting for transfers between devices, along(): return lax.ppermute(block, 'blk', route)  26.7 us
    ppermute x8, waiting for transfers between devices, across_chips(): return lax.ppermute(block, 'tp', [(i, i ^ 2) for i in range(4)])  25.4 us
    pallas_call x5, Pallas kernels, partial_sums(): return on_core(body, shapes, specs)(*operands)  18.3 us
    ppermute x8, starting transfers between devices, across_chips(): return lax.ppermute(block, 'tp', [(i, i ^ 2) for i in range(4)])  9.47 us
    unnamed x57, local copies, waits for them, and re-layouts  9.04 us
    pallas_call x3, Pallas kernels, collect(): on_core(body, shape, [SMEM] + [VMEM] * (len(operands) - 1))(*operands)  5.4 us
  transfers between devices with their start and end apart: 26, of which 10 were waited for; matrix products, arithmetic and copies ran while one was open for 7% of the time, Pallas kernels for 38%

profile of v6, /device:TPU:0, one launch (start us, length us, event | category | flops | bytes accessed | tf_op | source)
XLA Modules:
  0.0 207.8 jit_solution(5197592415570000179)
XLA Ops:
  4.5 3.1 %collective-permute-start = (bf16[400,1024]{1,0:T(8,128)(2,1)S(1)}, bf16[400,1024]{1,0:T(8,128)(2,1)S(1)}, u32[]{:S(2)}, u32[]{:S(2)}) collective-permute-start(bf16[400,1024]{1,0:T(8,128)(2,1)S(1)} %shard_map.91), channel_id=1, source_target_pairs={{0,4},{4,0},{8,12},{12,8},{1,5},{5,1},{9,13},{13,9},{2,6},{6,2},{1... | collective-permute-start | bytes 2457608 | tf_op jit(solution)/shard_map/ppermute | solution.py:114
  9.9 3.6 %dynamic-slice_bitcast_fusion.6 = (bf16[1024,256]{1,0:T(8,128)(2,1)S(1)}, bf16[1024,256]{1,0:T(8,128)(2,1)S(1)}, bf16[1024,256]{1,0:T(8,128)(2,1)}, bf16[1024,25...) fusion(bf16[4,1024,256]{2,1,0:T(8,128)(2,1)} %bitcast.34, ...), kind=kLoop, calls=%fused_computation.14 | loop fusion | bytes 8388624 | tf_op jit(solution)/shard_map/jit(dynamic_index_in_dim)/squeeze | solution.py:357
  15.0 12.6 %collective-permute-done.6.refs_3_.refs_1_ = bf16[384,1024]{1,0:T(8,128)(2,1)S(1)} collective-permute-done((bf16[384,1024]{1,0:T(8,128)(2,1)}, bf16[384,1024]{1,0:T(8,128)(2,1)S(1)}, u32[]{:S(2)}, u32[]{:S(2)}) %collective-permute-start.6) | collective-permute-done | bytes 786464 | tf_op jit(solution)/shard_map/ppermute | solution.py:106
  35.3 6.7 %collective-permute-start.7 = (bf16[192,1024]{1,0:T(8,128)(2,1)S(1)}, bf16[192,1024]{1,0:T(8,128)(2,1)S(1)}, u32[]{:S(2)}, u32[]{:S(2)}) collective-permute-start(bf16[192,1024]{1,0:T(8,128)(2,1)S(1)} %slice.12), channel_id=1, source_target_pairs={{0,4},{12,8},{1,5},{13,9},{2,6},{14,10},{3,7},{15,11},{16,20},{28,... | collective-permute-start | bytes 1179656 | tf_op jit(solution)/shard_map/ppermute | solution.py:114
  44.5 5.8 %collective-permute-done.7.rest_2_ = bf16[192,1024]{1,0:T(8,128)(2,1)S(1)} collective-permute-done((bf16[192,1024]{1,0:T(8,128)(2,1)S(1)}, bf16[192,1024]{1,0:T(8,128)(2,1)S(1)}, u32[]{:S(2)}, u32[]{:S(2)}) %collective-permute-start.7) | collective-permute-done | bytes 393248 | tf_op jit(solution)/shard_map/ppermute | solution.py:114
  50.3 1.9 collective-permute-done.5.rest_0_.refs_1_
  52.2 5.2 %collective-permute-done.4.outer_ref = bf16[400,1024]{1,0:T(8,128)(2,1)S(1)} collective-permute-done((bf16[400,1024]{1,0:T(8,128)(2,1)}, bf16[400,1024]{1,0:T(8,128)(2,1)S(1)}, u32[]{:S(2)}, u32[]{:S(2)}) %collective-permute-start.4) | collective-permute-done | bytes 819232 | tf_op jit(solution)/shard_map/ppermute | solution.py:114
  58.2 26.6 %shard_map.92 = (bf16[384,1024]{1,0:T(8,128)(2,1)}, bf16[16,1024]{1,0:T(8,128)(2,1)}) custom-call(s32[9]{0:T(128)} %fusion.plan_ref.refs_5_, bf16[400,1024]{1,0:T(8,128)(2,1)} %copy-done.21, bf16[400,1024]{1,0:T(8,128)(2,1)} %copy-done.26, bf16[400,1024]{1,0:T(8,128)(2,1)} %copy-done.8, bf16[400,1024]{1,0:T(8,128)(2,1)} %collective-permute-done.1.rest_1_.inner_ref.refs_1_, ...), custom_call_target="tpu_custom_call" | custom-call | flops 16 | bytes 16 | tf_op jit(solution)/shard_map/pallas_call | solution.py:163
  87.7 4.6 %shard_map.94 = (f32[384,1024]{1,0:T(8,128)S(1)}, bf16[384,1024]{1,0:T(8,128)(2,1)}) custom-call(bf16[384,1024]{1,0:T(8,128)(2,1)} %refs_0_.1, bf16[384,1024]{1,0:T(8,128)(2,1)S(1)} %copy-done.5, bf16[2048,512]{1,0:T(8,128)(2,1)S(1)} %maximum_maximum_fusion.refs_2_, bf16[2048,512]{1,0:T(8,128)(2,1)} %collective-permute-done.10.refs_3_), custom_call_target="tpu_custom_call" | custom-call | flops 1024 | bytes 1024 | tf_op jit(solution)/shard_map/pallas_call | solution.py:257
  93.4 4.3 %shard_map.95 = (f32[384,1024]{1,0:T(8,128)S(1)}, bf16[384,1024]{1,0:T(8,128)(2,1)}) custom-call(bf16[400,1024]{1,0:T(8,128)(2,1)S(1)} %copy-done.7, bf16[400,1024]{1,0:T(8,128)(2,1)S(1)} %copy-done.9, bf16[2048,512]{1,0:T(8,128)(2,1)S(1)} %maximum_maximum_fusion.refs_2_, bf16[2048,512]{1,0:T(8,128)(2,1)} %collective-permute-done.10.refs_3_), custom_call_target="tpu_custom_call" | custom-call | flops 1024 | bytes 1024 | tf_op jit(solution)/shard_map/pallas_call | solution.py:257
  99.4 2.8 %dynamic-slice_bitcast_fusion.1 = (bf16[256,1024]{1,0:T(8,128)(2,1)}, bf16[256,1024]{1,0:T(8,128)(2,1)}, bf16[256,1024]{1,0:T(8,128)(2,1)}, bf16[256,1024]{1,0:T(8,128)(2,1)}) fusion(bf16[1,256,4096]{2,1,0:T(8,128)(2,1)} %param.12, s32[]{:T(128)S(6)} %select_n.39, s32[]{:T(128)S(6)} %select_n.38, s32[]{:T(128)S(6)} %select_n.37, s32[]{:T(128)S(6)} %select_n.40), kind=kLoop, calls=%fused_computation.9 | loop fusion | bytes 4194320 | tf_op jit(solution)/shard_map/dynamic_slice | solution.py:363
  103.9 26.6 %shard_map.96 = (bf16[192,1024]{1,0:T(8,128)(2,1)}, bf16[192,1024]{1,0:T(8,128)(2,1)}, bf16[16,1024]{1,0:T(8,128)(2,1)}) custom-call(s32[9]{0:T(128)} %fusion.plan_ref.refs_5_, bf16[400,1024]{1,0:T(8,128)(2,1)} %collective-permute-done.1.rest_1_.inner_ref.refs_1_, bf16[400,1024]{1,0:T(8,128)(2,1)} %collective-permute-done.2.outer_ref, ...), custom_call_target="tpu_custom_call" | custom-call | flops 16 | bytes 16 | tf_op jit(solution)/shard_map/pallas_call | solution.py:163
  132.0 2.3 %pad_maximum_fusion.1.refs_0_ = bf16[256,2048]{1,0:T(8,128)(2,1)} fusion(bf16[256,1024]{1,0:T(8,128)(2,1)} %get-tuple-element.52, bf16[256,1024]{1,0:T(8,128)(2,1)} %get-tuple-element.49), kind=kLoop, calls=%fused_computation.3 | loop fusion | flops 2097152 | bytes 2097152 | tf_op jit(solution)/shard_map/concatenate | solution.py:368
  136.2 3.7 %shard_map.101 = (f32[384,1024]{1,0:T(8,128)S(1)}, bf16[384,1024]{1,0:T(8,128)(2,1)S(1)}) custom-call(bf16[384,1024]{1,0:T(8,128)(2,1)S(1)} %copy-done.13, bf16[384,1024]{1,0:T(8,128)(2,1)} %collective-permute-done.8.rest_0_.refs_1_, bf16[2048,512]{1,0:T(8,128)(2,1)S(1)} %maximum_maximum_fusion.refs_2_, bf16[2048,512]{1,0:T(8,128)(2,1)} %collective-permute-done.10.refs_3_), custom_call_target="tpu_custom_call" | custom-call | flops 1024 | bytes 1024 | tf_op jit(solution)/shard_map/pallas_call | solution.py:257
  139.9 2.7 %shard_map.97.refs_4_ = f32[384,1024]{1,0:T(8,128)S(1)} custom-call(bf16[192,1024]{1,0:T(8,128)(2,1)S(1)} %copy-done.14, bf16[192,1024]{1,0:T(8,128)(2,1)S(1)} %copy-done.15, bf16[2048,512]{1,0:T(8,128)(2,1)S(1)} %maximum_maximum_fusion.refs_2_, bf16[2048,512]{1,0:T(8,128)(2,1)} %collective-permute-done.10.refs_3_), custom_call_target="tpu_custom_call" | custom-call | flops 1024 | bytes 1024 | tf_op jit(solution)/shard_map/pallas_call | solution.py:257
  143.2 2.0 shard_map.98.rest_0_
  145.2 2.0 shard_map.99.refs_7_.rest_0_
  147.3 3.0 %shard_map.100 = (f32[384,1024]{1,0:T(8,128)S(1)}, bf16[384,1024]{1,0:T(8,128)(2,1)S(1)}) custom-call(bf16[192,1024]{1,0:T(8,128)(2,1)} %collective-permute-done.11.refs_0_, bf16[192,1024]{1,0:T(8,128)(2,1)} %collective-permute-done.12.refs_1_, bf16[2048,512]{1,0:T(8,128)(2,1)S(1)} %maximum_maximum_fusion.refs_2_, ...), custom_call_target="tpu_custom_call" | custom-call | flops 1024 | bytes 1024 | tf_op jit(solution)/shard_map/pallas_call | solution.py:257
  158.7 7.8 %collective-permute-done.19 = bf16[192,1024]{1,0:T(8,128)(2,1)S(1)} collective-permute-done((bf16[192,1024]{1,0:T(8,128)(2,1)S(1)}, bf16[192,1024]{1,0:T(8,128)(2,1)S(1)}, u32[]{:S(2)}, u32[]{:S(2)}) %collective-permute-start.19) | collective-permute-done | bytes 393248 | tf_op jit(solution)/shard_map/ppermute | solution.py:106
  166.6 7.7 %collective-permute-start.22 = (bf16[192,1024]{1,0:T(8,128)(2,1)S(1)}, bf16[192,1024]{1,0:T(8,128)(2,1)S(1)}, u32[]{:S(2)}, u32[]{:S(2)}) collective-permute-start(bf16[192,1024]{1,0:T(8,128)(2,1)S(1)} %add_convert_fusion.3), channel_id=1, source_target_pairs={{0,4},{12,8},{1,5},{13,9},{2,6},{14,10},{3,7},{15,11},{16,20},{28,... | collective-permute-start | bytes 1179656 | tf_op jit(solution)/shard_map/ppermute | solution.py:114
  176.7 4.2 %collective-permute-start.25 = (bf16[192,1024]{1,0:T(8,128)(2,1)S(1)}, bf16[192,1024]{1,0:T(8,128)(2,1)S(1)}, u32[]{:S(2)}, u32[]{:S(2)}) collective-permute-start(bf16[192,1024]{1,0:T(8,128)(2,1)S(1)} %add_convert_fusion.1), channel_id=1, source_target_pairs={{0,4},{4,0},{8,12},{12,8},{1,5},{5,1},{9,13},{13,9},{2,6},{6,2},{1... | collective-permute-start | bytes 1179656 | tf_op jit(solution)/shard_map/ppermute | solution.py:114
  180.9 2.5 %collective-permute-done.21 = bf16[192,1024]{1,0:T(8,128)(2,1)S(1)} collective-permute-done((bf16[192,1024]{1,0:T(8,128)(2,1)S(1)}, bf16[192,1024]{1,0:T(8,128)(2,1)S(1)}, u32[]{:S(2)}, u32[]{:S(2)}) %collective-permute-start.21) | collective-permute-done | bytes 393248 | tf_op jit(solution)/shard_map/ppermute | solution.py:106
  183.5 7.0 %collective-permute-start.23 = (bf16[192,1024]{1,0:T(8,128)(2,1)S(1)}, bf16[192,1024]{1,0:T(8,128)(2,1)S(1)}, u32[]{:S(2)}, u32[]{:S(2)}) collective-permute-start(bf16[192,1024]{1,0:T(8,128)(2,1)S(1)} %add_convert_fusion.2), channel_id=1, source_target_pairs={{0,8},{12,4},{4,12},{8,0},{1,9},{13,5},{5,13},{9,1},{2,10},{14,6},... | collective-permute-start | bytes 1179656 | tf_op jit(solution)/shard_map/ppermute | solution.py:114
  191.0 15.8 %collective-permute-done.23 = bf16[192,1024]{1,0:T(8,128)(2,1)S(1)} collective-permute-done((bf16[192,1024]{1,0:T(8,128)(2,1)S(1)}, bf16[192,1024]{1,0:T(8,128)(2,1)S(1)}, u32[]{:S(2)}, u32[]{:S(2)}) %collective-permute-start.23) | collective-permute-done | bytes 393248 | tf_op jit(solution)/shard_map/ppermute | solution.py:114
  (115 shorter events, 42.9 us)
Async XLA Ops:
  4.5 23.1 %collective-permute-start = (bf16[400,1024]{1,0:T(8,128)(2,1)S(1)}, bf16[400,1024]{1,0:T(8,128)(2,1)S(1)}, u32[]{:S(2)}, u32[]{:S(2)}) collective-permute-start(bf16[400,1024]{1,0:T(8,128)(2,1)S(1)} %shard_map.91), channel_id=1, source_target_pairs={{0,4},{4,0},{8,12},{12,8},{1,5},{5,1},{9,13},{13,9},{2,6},{6,2},{1... | collective-permute-start | bytes 2457608 | tf_op jit(solution)/shard_map/ppermute | solution.py:114
  7.6 20.0 %collective-permute-start.3 = (bf16[400,1024]{1,0:T(8,128)(2,1)S(1)}, bf16[400,1024]{1,0:T(8,128)(2,1)S(1)}, u32[]{:S(2)}, u32[]{:S(2)}) collective-permute-start(bf16[400,1024]{1,0:T(8,128)(2,1)S(1)} %shard_map.91), channel_id=1, source_target_pairs={{4,8},{8,4},{5,9},{9,5},{6,10},{10,6},{7,11},{11,7},{20,24},{24,20... | collective-permute-start | bytes 2457608 | tf_op jit(solution)/shard_map/ppermute | solution.py:114
  8.3 19.3 %collective-permute-start.6 = (bf16[384,1024]{1,0:T(8,128)(2,1)}, bf16[384,1024]{1,0:T(8,128)(2,1)S(1)}, u32[]{:S(2)}, u32[]{:S(2)}) collective-permute-start(bf16[384,1024]{1,0:T(8,128)(2,1)} %refs_0_.1), channel_id=1, source_target_pairs={{0,2},{1,3},{2,0},{3,1},{4,6},{5,7},{6,4},{7,5},{8,10},{9,11},{10,... | collective-permute-start | bytes 2359304 | tf_op jit(solution)/shard_map/ppermute | solution.py:106
  29.7 57.9 %collective-permute-start.10 = (bf16[2048,512]{1,0:T(8,128)(2,1)}, bf16[2048,512]{1,0:T(8,128)(2,1)}, u32[]{:S(2)}, u32[]{:S(2)}) collective-permute-start(bf16[2048,512]{1,0:T(8,128)(2,1)} %shard_map.93), channel_id=1, source_target_pairs={{0,1},{1,0},{2,3},{3,2},{4,5},{5,4},{6,7},{7,6},{8,9},{9,8},{10,11... | collective-permute-start | bytes 6291464 | tf_op jit(solution)/shard_map/ppermute | solution.py:110
  29.7 12.3 %collective-permute-start.1 = (bf16[400,1024]{1,0:T(8,128)(2,1)}, bf16[400,1024]{1,0:T(8,128)(2,1)}, u32[]{:S(2)}, u32[]{:S(2)}) collective-permute-start(bf16[400,1024]{1,0:T(8,128)(2,1)} %copy-done.6), channel_id=1, source_target_pairs={{4,8},{8,4},{5,9},{9,5},{6,10},{10,6},{7,11},{11,7},{20,24},{24,20... | collective-permute-start | bytes 2457608 | tf_op jit(solution)/shard_map/ppermute | solution.py:114
  31.5 20.7 %collective-permute-start.5 = (bf16[400,1024]{1,0:T(8,128)(2,1)}, bf16[400,1024]{1,0:T(8,128)(2,1)S(1)}, u32[]{:S(2)}, u32[]{:S(2)}) collective-permute-start(bf16[400,1024]{1,0:T(8,128)(2,1)} %copy-done.6), channel_id=1, source_target_pairs={{0,2},{1,3},{2,0},{3,1},{4,6},{5,7},{6,4},{7,5},{8,10},{9,11},{10,... | collective-permute-start | bytes 2457608 | tf_op jit(solution)/shard_map/ppermute | solution.py:106
  33.0 24.4 %collective-permute-start.4 = (bf16[400,1024]{1,0:T(8,128)(2,1)}, bf16[400,1024]{1,0:T(8,128)(2,1)S(1)}, u32[]{:S(2)}, u32[]{:S(2)}) collective-permute-start(bf16[400,1024]{1,0:T(8,128)(2,1)} %copy-done.21), channel_id=1, source_target_pairs={{4,0},{8,12},{5,1},{9,13},{6,2},{10,14},{7,3},{11,15},{20,16},{24,... | collective-permute-start | bytes 2457608 | tf_op jit(solution)/shard_map/ppermute | solution.py:114
  35.3 15.0 %collective-permute-start.7 = (bf16[192,1024]{1,0:T(8,128)(2,1)S(1)}, bf16[192,1024]{1,0:T(8,128)(2,1)S(1)}, u32[]{:S(2)}, u32[]{:S(2)}) collective-permute-start(bf16[192,1024]{1,0:T(8,128)(2,1)S(1)} %slice.12), channel_id=1, source_target_pairs={{0,4},{12,8},{1,5},{13,9},{2,6},{14,10},{3,7},{15,11},{16,20},{28,... | collective-permute-start | bytes 1179656 | tf_op jit(solution)/shard_map/ppermute | solution.py:114
  42.0 61.9 %collective-permute-start.2 = (bf16[400,1024]{1,0:T(8,128)(2,1)}, bf16[400,1024]{1,0:T(8,128)(2,1)}, u32[]{:S(2)}, u32[]{:S(2)}) collective-permute-start(bf16[400,1024]{1,0:T(8,128)(2,1)} %collective-permute-done.1.rest_1_.inner_ref.refs_1_), channel_id=1, source_target_pairs={{4,0},{8,12},{5,1},{9,13},{6,2},{10,14},{7,3},{11,15},{20,16},{24,... | collective-permute-start | bytes 2457608 | tf_op jit(solution)/shard_map/ppermute | solution.py:114
  84.9 19.1 %collective-permute-start.8 = (bf16[384,1024]{1,0:T(8,128)(2,1)}, bf16[384,1024]{1,0:T(8,128)(2,1)}, u32[]{:S(2)}, u32[]{:S(2)}) collective-permute-start(bf16[384,1024]{1,0:T(8,128)(2,1)} %get-tuple-element.27.refs_0_), channel_id=1, source_target_pairs={{0,2},{1,3},{2,0},{3,1},{4,6},{5,7},{6,4},{7,5},{8,10},{9,11},{10,... | collective-permute-start | bytes 2359304 | tf_op jit(solution)/shard_map/ppermute | solution.py:106
  85.5 16.8 %collective-permute-start.9 = (bf16[192,1024]{1,0:T(8,128)(2,1)}, bf16[192,1024]{1,0:T(8,128)(2,1)S(1)}, u32[]{:S(2)}, u32[]{:S(2)}) collective-permute-start(bf16[192,1024]{1,0:T(8,128)(2,1)} %copy-done.27), channel_id=1, source_target_pairs={{4,8},{8,4},{5,9},{9,5},{6,10},{10,6},{7,11},{11,7},{20,24},{24,20... | collective-permute-start | bytes 1179656 | tf_op jit(solution)/shard_map/ppermute | solution.py:114
  93.4 49.2 %collective-permute-start.14 = (bf16[384,1024]{1,0:T(8,128)(2,1)}, bf16[384,1024]{1,0:T(8,128)(2,1)}, u32[]{:S(2)}, u32[]{:S(2)}) collective-permute-start(bf16[384,1024]{1,0:T(8,128)(2,1)} %get-tuple-element.33), channel_id=1, source_target_pairs={{0,1},{1,0},{2,3},{3,2},{4,5},{5,4},{6,7},{7,6},{8,9},{9,8},{10,11... | collective-permute-start | bytes 2359304 | tf_op jit(solution)/shard_map/ppermute | solution.py:110
  98.9 46.3 %collective-permute-start.13 = (bf16[384,1024]{1,0:T(8,128)(2,1)}, bf16[384,1024]{1,0:T(8,128)(2,1)}, u32[]{:S(2)}, u32[]{:S(2)}) collective-permute-start(bf16[384,1024]{1,0:T(8,128)(2,1)} %get-tuple-element.32), channel_id=1, source_target_pairs={{0,1},{1,0},{2,3},{3,2},{4,5},{5,4},{6,7},{7,6},{8,9},{9,8},{10,11... | collective-permute-start | bytes 2359304 | tf_op jit(solution)/shard_map/ppermute | solution.py:110
  102.3 45.1 %collective-permute-start.12 = (bf16[192,1024]{1,0:T(8,128)(2,1)S(1)}, bf16[192,1024]{1,0:T(8,128)(2,1)}, u32[]{:S(2)}, u32[]{:S(2)}) collective-permute-start(bf16[192,1024]{1,0:T(8,128)(2,1)S(1)} %collective-permute-done.9.rest_1_.refs_6_), channel_id=1, source_target_pairs={{4,0},{8,12},{5,1},{9,13},{6,2},{10,14},{7,3},{11,15},{20,16},{24,... | collective-permute-start | bytes 1179656 | tf_op jit(solution)/shard_map/ppermute | solution.py:114
  130.5 16.8 %collective-permute-start.11 = (bf16[192,1024]{1,0:T(8,128)(2,1)}, bf16[192,1024]{1,0:T(8,128)(2,1)}, u32[]{:S(2)}, u32[]{:S(2)}) collective-permute-start(bf16[192,1024]{1,0:T(8,128)(2,1)} %get-tuple-element.30.refs_0_), channel_id=1, source_target_pairs={{0,2},{1,3},{2,0},{3,1},{4,6},{5,7},{6,4},{7,5},{8,10},{9,11},{10,... | collective-permute-start | bytes 1179656 | tf_op jit(solution)/shard_map/ppermute | solution.py:106
  134.3 18.2 %collective-permute-start.17 = (bf16[256,2048]{1,0:T(8,128)(2,1)}, bf16[256,2048]{1,0:T(8,128)(2,1)S(1)}, u32[]{:S(2)}, u32[]{:S(2)}) collective-permute-start(bf16[256,2048]{1,0:T(8,128)(2,1)} %shard_map.103), channel_id=1, source_target_pairs={{0,1},{1,0},{2,3},{3,2},{4,5},{5,4},{6,7},{7,6},{8,9},{9,8},{10,11... | collective-permute-start | bytes 3145736 | tf_op jit(solution)/shard_map/ppermute | solution.py:110
  154.5 12.0 %collective-permute-start.19 = (bf16[192,1024]{1,0:T(8,128)(2,1)S(1)}, bf16[192,1024]{1,0:T(8,128)(2,1)S(1)}, u32[]{:S(2)}, u32[]{:S(2)}) collective-permute-start(bf16[192,1024]{1,0:T(8,128)(2,1)S(1)} %get-tuple-element.44), channel_id=1, source_target_pairs={{0,2},{1,3},{2,0},{3,1},{4,6},{5,7},{6,4},{7,5},{8,10},{9,11},{10,... | collective-permute-start | bytes 1179656 | tf_op jit(solution)/shard_map/ppermute | solution.py:106
  156.6 19.9 %collective-permute-start.24 = (bf16[192,1024]{1,0:T(8,128)(2,1)S(1)}, bf16[192,1024]{1,0:T(8,128)(2,1)S(1)}, u32[]{:S(2)}, u32[]{:S(2)}) collective-permute-start(bf16[192,1024]{1,0:T(8,128)(2,1)S(1)} %get-tuple-element.48), channel_id=1, source_target_pairs={{0,2},{1,3},{2,0},{3,1},{4,6},{5,7},{6,4},{7,5},{8,10},{9,11},{10,... | collective-permute-start | bytes 1179656 | tf_op jit(solution)/shard_map/ppermute | solution.py:106
  158.0 25.3 %collective-permute-start.21 = (bf16[192,1024]{1,0:T(8,128)(2,1)S(1)}, bf16[192,1024]{1,0:T(8,128)(2,1)S(1)}, u32[]{:S(2)}, u32[]{:S(2)}) collective-permute-start(bf16[192,1024]{1,0:T(8,128)(2,1)S(1)} %get-tuple-element.46), channel_id=1, source_target_pairs={{0,2},{1,3},{2,0},{3,1},{4,6},{5,7},{6,4},{7,5},{8,10},{9,11},{10,... | collective-permute-start | bytes 1179656 | tf_op jit(solution)/shard_map/ppermute | solution.py:106
  166.6 16.8 %collective-permute-start.22 = (bf16[192,1024]{1,0:T(8,128)(2,1)S(1)}, bf16[192,1024]{1,0:T(8,128)(2,1)S(1)}, u32[]{:S(2)}, u32[]{:S(2)}) collective-permute-start(bf16[192,1024]{1,0:T(8,128)(2,1)S(1)} %add_convert_fusion.3), channel_id=1, source_target_pairs={{0,4},{12,8},{1,5},{13,9},{2,6},{14,10},{3,7},{15,11},{16,20},{28,... | collective-permute-start | bytes 1179656 | tf_op jit(solution)/shard_map/ppermute | solution.py:114
  174.3 16.6 %collective-permute-start.18 = (bf16[192,1024]{1,0:T(8,128)(2,1)S(1)}, bf16[192,1024]{1,0:T(8,128)(2,1)S(1)}, u32[]{:S(2)}, u32[]{:S(2)}) collective-permute-start(bf16[192,1024]{1,0:T(8,128)(2,1)S(1)} %get-tuple-element.42), channel_id=1, source_target_pairs={{0,2},{1,3},{2,0},{3,1},{4,6},{5,7},{6,4},{7,5},{8,10},{9,11},{10,... | collective-permute-start | bytes 1179656 | tf_op jit(solution)/shard_map/ppermute | solution.py:106
  175.9 15.1 %collective-permute-start.20 = (bf16[192,1024]{1,0:T(8,128)(2,1)S(1)}, bf16[192,1024]{1,0:T(8,128)(2,1)S(1)}, u32[]{:S(2)}, u32[]{:S(2)}) collective-permute-start(bf16[192,1024]{1,0:T(8,128)(2,1)S(1)} %add_convert_fusion.3), channel_id=1, source_target_pairs={{4,8},{8,4},{5,9},{9,5},{6,10},{10,6},{7,11},{11,7},{20,24},{24,20... | collective-permute-start | bytes 1179656 | tf_op jit(solution)/shard_map/ppermute | solution.py:114
  176.7 14.3 %collective-permute-start.25 = (bf16[192,1024]{1,0:T(8,128)(2,1)S(1)}, bf16[192,1024]{1,0:T(8,128)(2,1)S(1)}, u32[]{:S(2)}, u32[]{:S(2)}) collective-permute-start(bf16[192,1024]{1,0:T(8,128)(2,1)S(1)} %add_convert_fusion.1), channel_id=1, source_target_pairs={{0,4},{4,0},{8,12},{12,8},{1,5},{5,1},{9,13},{13,9},{2,6},{6,2},{1... | collective-permute-start | bytes 1179656 | tf_op jit(solution)/shard_map/ppermute | solution.py:114
  183.5 23.2 %collective-permute-start.23 = (bf16[192,1024]{1,0:T(8,128)(2,1)S(1)}, bf16[192,1024]{1,0:T(8,128)(2,1)S(1)}, u32[]{:S(2)}, u32[]{:S(2)}) collective-permute-start(bf16[192,1024]{1,0:T(8,128)(2,1)S(1)} %add_convert_fusion.2), channel_id=1, source_target_pairs={{0,8},{12,4},{4,12},{8,0},{1,9},{13,5},{5,13},{9,1},{2,10},{14,6},... | collective-permute-start | bytes 1179656 | tf_op jit(solution)/shard_map/ppermute | solution.py:114
  (30 other events, 195.4 us)

commit v7 on v6

--- a/solution.py
+++ b/solution.py
@@ -88,7 +88,8 @@
 MIDDLE = [(1, 2), (2, 1)]
 INWARD = [(0, 1), (3, 2)]
 OUTWARD = [(1, 0), (2, 3)]
-TWO_ON = [(0, 2), (3, 1), (1, 3), (2, 0)]
+TWO_IN = [(0, 2), (3, 1)]
+TWO_OUT = [(1, 3), (2, 0)]
 PLAN = [
     [3, 2, 1, 0, 0, 1, 2, 3, 0],
     [2, 3, 0, 1, 0, 3, 1, 2, 1],
@@ -136,6 +137,24 @@
     )(block, *others)
 
 
+def lower_half(block):
+    rows = block.shape[0] // 2
+
+    def body(block_ref, out_ref, sem):
+        copy = pltpu.make_async_copy(block_ref.at[pl.ds(rows, rows)], out_ref, sem)
+        copy.start()
+        copy.wait()
+
+    return pl.pallas_call(
+        body,
+        out_shape=jax.ShapeDtypeStruct((rows, block.shape[1]), block.dtype),
+        in_specs=[ANYWHERE],
+        out_specs=VMEM,
+        scratch_shapes=[pltpu.SemaphoreType.DMA],
+        cost_estimate=pl.CostEstimate(flops=1024, bytes_accessed=1024, transcendentals=0),
+    )(block)
+
+
 def chosen(plan, if_inner, if_outer, spans, *others):
     width = if_inner.shape[1]
 
@@ -164,7 +183,7 @@
         body,
         out_shape=[jax.ShapeDtypeStruct((size, width), if_inner.dtype) for _, size in spans],
         in_specs=[SMEM] + [ANYWHERE] * (2 + len(others)),
-        out_specs=[ANYWHERE] * len(spans),
+        out_specs=[VMEM] * len(spans),
         scratch_shapes=[pltpu.SemaphoreType.DMA((len(spans),))],
         cost_estimate=pl.CostEstimate(flops=16, bytes_accessed=16, transcendentals=0),
     )(plan, if_inner, if_outer, *others)
@@ -210,9 +229,10 @@
 def partial_sums(
     sizes, parts, weights, places, before=None, send=True, choice=None, waits=()
 ):
-    width, columns = weights[0].shape[0] // 2, weights[0].shape[1]
+    width, columns = weights[0].shape
     blocks = [block for part in parts for block in part]
-    operands = blocks + list(weights)
+    used = [weights[place] for place in places] + [weights[2]]
+    operands = blocks + used
     specs = [VMEM] * len(operands)
     if before is not None:
         operands.append(before)
@@ -225,8 +245,8 @@
 
     def body(*refs):
         results = refs[len(operands) :]
-        weight_refs = refs[len(blocks) : len(blocks) + len(weights)]
-        next_ref = len(blocks) + len(weights)
+        weight_refs = refs[len(blocks) : len(blocks) + len(used)]
+        next_ref = len(blocks) + len(used)
         before_ref = refs[next_ref] if before is not None else None
         next_ref += before is not None
         start = 0
@@ -240,11 +260,11 @@
                 at = slice(side * columns, (side + 1) * columns)
                 total = None if before is None else before_ref[span, at]
                 for index, place in enumerate(places):
-                    product = jnp.dot(
-                        rows[index],
-                        weight_refs[side][place * width : (place + 1) * width, :],
-                        preferred_element_type=jnp.float32,
-                    )
+                    if side == 0:
+                        weight = weight_refs[index][...]
+                    else:
+                        weight = weight_refs[-1][place * width : (place + 1) * width, :]
+                    product = jnp.dot(rows[index], weight, preferred_element_type=jnp.float32)
                     total = product if total is None else total + product
                 results[0][span, at] = total
                 if send:
@@ -318,17 +338,27 @@
         for index in range(1, 4):
             out_refs[2][(index - 1) * owned : index * owned, :] = rows[index].astype(jnp.bfloat16)
 
-    def others(held_ref, own_ref, lent_ref, *out_refs):
-        for index in range(3):
-            held = held_ref[index * owned : (index + 1) * owned, :]
-            down(held, own_ref, lent_ref, out_refs[2 * index], out_refs[2 * index + 1])
+    def others(indices, waits):
+        def body(held_ref, own_ref, lent_ref, *refs):
+            out_refs = refs[len(waits) :]
+            for place, index in enumerate(indices):
+                held = held_ref[(index - 1) * owned : index * owned, :]
+                down(held, own_ref, lent_ref, out_refs[2 * place], out_refs[2 * place + 1])
+
+        specs = [VMEM] * 3 + [ANYWHERE] * len(waits)
+        return on_core(body, pair * len(indices), specs)(held, down_own, down_lent, *waits)
+
+    def joined(sent, kept):
+        return kept + across_chips(sent).astype(jnp.float32)
 
     held_shape = jax.ShapeDtypeStruct((3 * owned, 2 * units), jnp.bfloat16)
     sent, kept, held = on_core(first, pair + [held_shape], [SMEM] + [VMEM] * 6)(
         plan, sums, got, facts, before, down_own, down_lent
     )
-    rest = on_core(others, pair * 3, [VMEM] * 3)(held, down_own, down_lent)
-    return [sent, *rest[0::2]], [kept, *rest[1::2]]
+    got_first = across_chips(sent)
+    chunks = [kept + got_first.astype(jnp.float32), joined(*others([1], []))]
+    rest = others([2, 3], [got_first])
+    return chunks + [joined(rest[0], rest[1]), joined(rest[2], rest[3])]
 
 
 def rows_travel(
@@ -362,8 +392,6 @@
     def down_part(j):
         return lax.dynamic_slice_in_dim(down_weight[0], (share ^ j) * width, width, 1)
 
-    kept_in = jnp.concatenate([quarter(0), quarter(2)])
-    lend_in = jnp.concatenate([quarter(1), quarter(3)])
     kept_down = jnp.concatenate([down_part(0), down_part(2)], axis=1)
     lend_down = jnp.concatenate([down_part(1), down_part(3)], axis=1)
 
@@ -371,11 +399,13 @@
     inner_last = along(beside, MIDDLE)
     outer_next = along(middle, OUTWARD)
     beside_far = across_chips(beside)
-    inward_far = along(own_far[half:], INWARD)
-    lent_in = across_cores(after(lend_in, beside, middle, own_far))
-    weights = (kept_in, lent_in)
+    inward_far = along(lower_half(own_far), INWARD)
+    lend = jnp.concatenate([quarter(1), quarter(3)])
+    lent = across_cores(after(lend, beside, middle, own_far))
+    weights = [quarter(0), quarter(2), lent]
     sums_0, send_0 = partial_sums([row_count], [(tokens, own_far)], weights, (0, 1))
     got_0 = across_cores(send_0)
+    lent_down = across_cores(lend_down)
 
     outer_last = along(inner_last, OUTWARD)
     (second, second_facts) = chosen(
@@ -386,10 +416,12 @@
         beside_far,
         inner_last,
         inward_far,
+        lend_down,
+        weights[0],
+        weights[1],
     )
     second_far = across_chips(second)
     middle_far = along(inward_far, MIDDLE)
-    lent_down = across_cores(after(lend_down, inner_last))
     sums_1, send_1 = partial_sums([row_count], [(beside, beside_far)], weights, (0, 1))
     got_1 = across_cores(send_1)
 
@@ -421,19 +453,19 @@
     )
     got_3 = across_cores(send_3)
     total = collect(owned, 2, plan, sums_2, got_2, second_facts, total)
-    sent, kept = finish(
+    chunks = finish(
         owned, 3, plan, sums_3, got_3, last_facts, total, kept_down, lent_down
     )
-    chunks = [k + across_chips(s).astype(jnp.float32) for s, k in zip(sent, kept)]
 
     def send(block, route):
         return along(block.astype(jnp.bfloat16), route).astype(jnp.float32)
 
     inward = send(chunks[0], INWARD)
     middle = send(chunks[0], MIDDLE)
-    two_on = send(chunks[1] + inward, TWO_ON)
+    two_in = send(chunks[1], TWO_IN)
+    two_out = send(chunks[1] + inward, TWO_OUT)
     beside = send(chunks[2], BESIDE)
-    return (chunks[3] + middle + two_on + beside).astype(jnp.bfloat16)
+    return (chunks[3] + middle + two_in + two_out + beside).astype(jnp.bfloat16)
 
 
 def on_device(*args):

time: 209 us -> 153 us (0.73)
  Pallas kernels: 81.8 us -> 31.4 us
  waiting for transfers between devices: 52.3 us -> 46.2 us
  starting transfers between devices: 47.3 us -> 45.2 us
  other arithmetic: 6.73 us -> 8.82 us
    pallas_call x2, Pallas kernels: 53.2 us -> 5.51 us  [chosen(): pl.pallas_call(body, out_shape=[jax.ShapeDtypeStruct((size, width), if_in...]
    ppermute x12 -> x13, waiting for transfers between devices: 26.7 us -> 18 us  [along(): return lax.ppermute(block, 'blk', route)]
    pallas_call x5, Pallas kernels: 18.3 us -> 13.7 us  [partial_sums(): return on_core(body, shapes, specs)(*operands)]
    ppermute x12 -> x13, starting transfers between devices: 36.6 us -> 33.2 us  [along(): return lax.ppermute(block, 'blk', route)]
    ppermute x8, waiting for transfers between devices: 25.4 us -> 28 us  [across_chips(): return lax.ppermute(block, 'tp', [(i, i ^ 2) for i in range(4)])]
    unnamed x57 -> x59, local copies, waits for them, and re-layouts: 9.04 us -> 11.4 us
    concatenate x2 -> x3, other arithmetic: 2.97 us -> 4.96 us  [the longest x2 3.46 us: quarter(): return jnp.concatenate(pair, axis=1)]
  transfers between devices with their start and end apart: 26 -> 27, of which waited for: 10 -> 12; matrix products, arithmetic and copies ran while one was open for 7% -> 10% of each run, Pallas kernels for 38% -> 18%
where the time goes in v7:
time: 153 us; the launch traced here: 152 us
  waiting for transfers between devices  46.2 us (30%)
  starting transfers between devices  45.2 us (30%)
  Pallas kernels  31.4 us (21%)
  local copies, waits for them, and re-layouts  19.9 us (13%)
  other arithmetic  8.82 us (6%)
    ppermute x13, starting transfers between devices, along(): return lax.ppermute(block, 'blk', route)  33.2 us
    ppermute x8, waiting for transfers between devices, across_chips(): return lax.ppermute(block, 'tp', [(i, i ^ 2) for i in range(4)])  28 us
    ppermute x13, waiting for transfers between devices, along(): return lax.ppermute(block, 'blk', route)  18 us
    pallas_call x5, Pallas kernels, partial_sums(): return on_core(body, shapes, specs)(*operands)  13.7 us
    unnamed x59, local copies, waits for them, and re-layouts  11.4 us
    ppermute x8, starting transfers between devices, across_chips(): return lax.ppermute(block, 'tp', [(i, i ^ 2) for i in range(4)])  10.5 us
    pallas_call x2, Pallas kernels, chosen(): pl.pallas_call(body, out_shape=[jax.ShapeDtypeStruct((size, width), if_in...  5.51 us
    pallas_call x3, Pallas kernels, collect(): on_core(body, shape, [SMEM] + [VMEM] * (len(operands) - 1))(*operands)  5.39 us
  transfers between devices with their start and end apart: 27, of which 12 were waited for; matrix products, arithmetic and copies ran while one was open for 10% of the time, Pallas kernels for 18%

profile of v7, /device:TPU:0, one launch (start us, length us, event | category | flops | bytes accessed | tf_op | source)
XLA Modules:
  0.0 152.0 jit_solution(2214393907674837168)
XLA Ops:
  5.2 5.9 %collective-permute-start = (bf16[400,1024]{1,0:T(8,128)(2,1)S(1)}, bf16[400,1024]{1,0:T(8,128)(2,1)S(1)}, u32[]{:S(2)}, u32[]{:S(2)}) collective-permute-start(bf16[400,1024]{1,0:T(8,128)(2,1)S(1)} %shard_map.91), channel_id=1, source_target_pairs={{0,4},{4,0},{8,12},{12,8},{1,5},{5,1},{9,13},{13,9},{2,6},{6,2},{1... | collective-permute-start | bytes 2457608 | tf_op jit(solution)/shard_map/ppermute | solution.py:115
  12.6 3.6 %dynamic-slice_bitcast_fusion.4 = (bf16[1024,256]{1,0:T(8,128)(2,1)S(1)}, bf16[1024,256]{1,0:T(8,128)(2,1)S(1)}, bf16[1024,256]{1,0:T(8,128)(2,1)}, bf16[1024,25...) fusion(bf16[4,1024,256]{2,1,0:T(8,128)(2,1)} %bitcast.34, ...), kind=kLoop, calls=%fused_computation.15 | loop fusion | bytes 8388624 | tf_op jit(solution)/shard_map/jit(dynamic_index_in_dim)/squeeze | solution.py:387
  17.7 12.4 %collective-permute-done.6.block_ref.refs_3_.refs_1_ = bf16[384,1024]{1,0:T(8,128)(2,1)S(1)} collective-permute-done((bf16[384,1024]{1,0:T(8,128)(2,1)}, bf16[384,1024]{1,0:T(8,128)(2,1)S(1)}, u32[]{:S(2)}, u32[]{:S(2)}) %collective-permute-start.6) | collective-permute-done | bytes 786464 | tf_op jit(solution)/shard_map/ppermute | solution.py:107
  36.6 2.4 %pad_maximum_fusion.2.rest_5_.refs_3_.refs_2_ = bf16[1024,512]{1,0:T(8,128)(2,1)} fusion(bf16[1024,256]{1,0:T(8,128)(2,1)} %get-tuple-element.59, bf16[1024,256]{1,0:T(8,128)(2,1)} %get-tuple-element.64), kind=kLoop, calls=%fused_computation.3 | loop fusion | flops 2097152 | bytes 2097152 | tf_op jit(solution)/shard_map/concatenate | solution.py:390
  42.1 6.1 %collective-permute-start.7 = (bf16[192,1024]{1,0:T(8,128)(2,1)}, bf16[192,1024]{1,0:T(8,128)(2,1)}, u32[]{:S(2)}, u32[]{:S(2)}) collective-permute-start(bf16[192,1024]{1,0:T(8,128)(2,1)} %shard_map.92), channel_id=1, source_target_pairs={{0,4},{12,8},{1,5},{13,9},{2,6},{14,10},{3,7},{15,11},{16,20},{28,... | collective-permute-start | bytes 1179656 | tf_op jit(solution)/shard_map/ppermute | solution.py:115
  49.3 2.3 %pad_maximum_fusion.rest_3_ = bf16[256,2048]{1,0:T(8,128)(2,1)} fusion(bf16[256,1024]{1,0:T(8,128)(2,1)} %get-tuple-element.50, bf16[256,1024]{1,0:T(8,128)(2,1)} %get-tuple-element.51), kind=kLoop, calls=%fused_computation.1 | loop fusion | flops 2097152 | bytes 2097152 | tf_op jit(solution)/shard_map/concatenate | solution.py:396
  54.2 2.1 %collective-permute-done.7.rest_2_ = bf16[192,1024]{1,0:T(8,128)(2,1)} collective-permute-done((bf16[192,1024]{1,0:T(8,128)(2,1)}, bf16[192,1024]{1,0:T(8,128)(2,1)}, u32[]{:S(2)}, u32[]{:S(2)}) %collective-permute-start.7) | collective-permute-done | bytes 393248 | tf_op jit(solution)/shard_map/ppermute | solution.py:115
  56.6 2.8 %shard_map.93 = (bf16[384,1024]{1,0:T(8,128)(2,1)}, bf16[16,1024]{1,0:T(8,128)(2,1)}) custom-call(s32[9]{0:T(128)} %fusion.1.plan_ref.refs_5_, bf16[400,1024]{1,0:T(8,128)(2,1)} %copy-done.23, bf16[400,1024]{1,0:T(8,128)(2,1)} %collective-permute-done.4.outer_ref, bf16[400,1024]{1,0:T(8,128)(2,1)} %collective-permute-done.5.rest_0_.refs_1_, ...), custom_call_target="tpu_custom_call" | custom-call | flops 16 | bytes 16 | tf_op jit(solution)/shard_map/pallas_call | solution.py:182
  64.0 3.9 %shard_map.95 = (f32[384,1024]{1,0:T(8,128)S(1)}, bf16[384,1024]{1,0:T(8,128)(2,1)}) custom-call(bf16[384,1024]{1,0:T(8,128)(2,1)} %refs_0_.1, bf16[384,1024]{1,0:T(8,128)(2,1)S(1)} %copy-done.5, bf16[1024,512]{1,0:T(8,128)(2,1)S(1)} %copy-done, bf16[1024,512]{1,0:T(8,128)(2,1)S(1)} %copy-done.1, bf16[2048,512]{1,0:T(8,128)(2,1)S(1)} %collective-permute-done.10.refs_4_.refs_3_), custom_call_target="tpu_custom_call" | custom-call | flops 1024 | bytes 1024 | tf_op jit(solution)/shard_map/pallas_call | solution.py:277
  69.1 3.8 %shard_map.96 = (f32[384,1024]{1,0:T(8,128)S(1)}, bf16[384,1024]{1,0:T(8,128)(2,1)}) custom-call(bf16[400,1024]{1,0:T(8,128)(2,1)S(1)} %copy-done.11, bf16[400,1024]{1,0:T(8,128)(2,1)} %collective-permute-done.5.rest_0_.refs_1_, bf16[1024,512]{1,0:T(8,128)(2,1)S(1)} %copy-done, bf16[1024,512]{1,0:T(8,128)(2,1)S(1)} %copy-done.1, ...), custom_call_target="tpu_custom_call" | custom-call | flops 1024 | bytes 1024 | tf_op jit(solution)/shard_map/pallas_call | solution.py:277
  75.8 3.1 %collective-permute-done.8.rest_0_.refs_1_ = bf16[384,1024]{1,0:T(8,128)(2,1)} collective-permute-done((bf16[384,1024]{1,0:T(8,128)(2,1)}, bf16[384,1024]{1,0:T(8,128)(2,1)}, u32[]{:S(2)}, u32[]{:S(2)}) %collective-permute-start.8) | collective-permute-done | bytes 786464 | tf_op jit(solution)/shard_map/ppermute | solution.py:107
  78.9 2.7 %shard_map.97 = (bf16[192,1024]{1,0:T(8,128)(2,1)}, bf16[192,1024]{1,0:T(8,128)(2,1)}, bf16[16,1024]{1,0:T(8,128)(2,1)}) custom-call(s32[9]{0:T(128)} %fusion.1.plan_ref.refs_5_, bf16[400,1024]{1,0:T(8,128)(2,1)} %collective-permute-done.1.rest_1_.inner_ref, bf16[400,1024]{1,0:T(8,128)(2,1)} %collective-permute-done.2.outer_ref, ...), custom_call_target="tpu_custom_call" | custom-call | flops 16 | bytes 16 | tf_op jit(solution)/shard_map/pallas_call | solution.py:182
  87.1 3.0 %shard_map.102 = (f32[384,1024]{1,0:T(8,128)S(1)}, bf16[384,1024]{1,0:T(8,128)(2,1)S(1)}) custom-call(bf16[384,1024]{1,0:T(8,128)(2,1)S(1)} %copy-done.15, bf16[384,1024]{1,0:T(8,128)(2,1)} %collective-permute-done.8.rest_0_.refs_1_, bf16[1024,512]{1,0:T(8,128)(2,1)S(1)} %copy-done, bf16[1024,512]{1,0:T(8,128)(2,1)S(1)} %copy-done.2, ...), custom_call_target="tpu_custom_call" | custom-call | flops 1024 | bytes 1024 | tf_op jit(solution)/shard_map/pallas_call | solution.py:277
  91.7 2.0 %shard_map.99.rest_0_ = f32[768,512]{1,0:T(8,128)S(1)} custom-call(s32[9]{0:T(128)S(1)} %copy-done.20, f32[384,1024]{1,0:T(8,128)S(1)} %copy-done.7, bf16[384,1024]{1,0:T(8,128)(2,1)} %collective-permute-done.14.got_ref, bf16[16,1024]{1,0:T(8,128)(2,1)S(1)} %slice.9.facts_ref), custom_call_target="tpu_custom_call" | custom-call | flops 1024 | bytes 1024 | tf_op jit(solution)/shard_map/pallas_call | solution.py:316
  93.7 2.1 %shard_map.100.refs_7_.rest_0_ = f32[768,512]{1,0:T(8,128)S(1)} custom-call(s32[9]{0:T(128)S(1)} %copy-done.20, f32[384,1024]{1,0:T(8,128)S(1)} %copy-done.9, bf16[384,1024]{1,0:T(8,128)(2,1)} %collective-permute-done.13.got_ref, bf16[16,1024]{1,0:T(8,128)(2,1)S(1)} %slice.8.facts_ref, f32[768,512]{1,0:T(8,128)S(1)} %shard_map.99.rest_0_), custom_call_target="tpu_custom_call" | custom-call | flops 1024 | bytes 1024 | tf_op jit(solution)/shard_map/pallas_call | solution.py:316
  95.9 2.1 %shard_map.101 = (f32[384,1024]{1,0:T(8,128)S(1)}, bf16[384,1024]{1,0:T(8,128)(2,1)S(1)}) custom-call(bf16[192,1024]{1,0:T(8,128)(2,1)S(1)} %collective-permute-done.11.refs_0_, bf16[192,1024]{1,0:T(8,128)(2,1)} %collective-permute-done.12.refs_1_, bf16[1024,512]{1,0:T(8,128)(2,1)S(1)} %copy-done.3, ...), custom_call_target="tpu_custom_call" | custom-call | flops 1024 | bytes 1024 | tf_op jit(solution)/shard_map/pallas_call | solution.py:277
  104.9 9.2 %collective-permute-done.18.refs_0_ = bf16[192,1024]{1,0:T(8,128)(2,1)S(1)} collective-permute-done((bf16[192,1024]{1,0:T(8,128)(2,1)S(1)}, bf16[192,1024]{1,0:T(8,128)(2,1)S(1)}, u32[]{:S(2)}, u32[]{:S(2)}) %collective-permute-start.18) | collective-permute-done | bytes 393248 | tf_op jit(solution)/shard_map/ppermute | solution.py:107
  114.2 4.4 %collective-permute-start.23 = (bf16[192,1024]{1,0:T(8,128)(2,1)S(1)}, bf16[192,1024]{1,0:T(8,128)(2,1)S(1)}, u32[]{:S(2)}, u32[]{:S(2)}) collective-permute-start(bf16[192,1024]{1,0:T(8,128)(2,1)S(1)} %add_convert_fusion.3), channel_id=1, source_target_pairs={{0,4},{12,8},{1,5},{13,9},{2,6},{14,10},{3,7},{15,11},{16,20},{28,... | collective-permute-start | bytes 1179656 | tf_op jit(solution)/shard_map/ppermute | solution.py:115
  122.6 3.5 %collective-permute-done.23 = bf16[192,1024]{1,0:T(8,128)(2,1)S(1)} collective-permute-done((bf16[192,1024]{1,0:T(8,128)(2,1)S(1)}, bf16[192,1024]{1,0:T(8,128)(2,1)S(1)}, u32[]{:S(2)}, u32[]{:S(2)}) %collective-permute-start.23) | collective-permute-done | bytes 393248 | tf_op jit(solution)/shard_map/ppermute | solution.py:115
  126.3 4.3 %collective-permute-start.22 = (bf16[192,1024]{1,0:T(8,128)(2,1)S(1)}, bf16[192,1024]{1,0:T(8,128)(2,1)S(1)}, u32[]{:S(2)}, u32[]{:S(2)}) collective-permute-start(bf16[192,1024]{1,0:T(8,128)(2,1)S(1)} %get-tuple-element.61), channel_id=1, source_target_pairs={{0,8},{12,4},{1,9},{13,5},{2,10},{14,6},{3,11},{15,7},{16,24},{28,... | collective-permute-start | bytes 1179656 | tf_op jit(solution)/shard_map/ppermute | solution.py:115
  132.0 3.7 %collective-permute-start.26 = (bf16[192,1024]{1,0:T(8,128)(2,1)S(1)}, bf16[192,1024]{1,0:T(8,128)(2,1)S(1)}, u32[]{:S(2)}, u32[]{:S(2)}) collective-permute-start(bf16[192,1024]{1,0:T(8,128)(2,1)S(1)} %add_convert_fusion.1), channel_id=1, source_target_pairs={{0,4},{4,0},{8,12},{12,8},{1,5},{5,1},{9,13},{13,9},{2,6},{6,2},{1... | collective-permute-start | bytes 1179656 | tf_op jit(solution)/shard_map/ppermute | solution.py:115
  135.7 3.1 %collective-permute-done.19 = bf16[192,1024]{1,0:T(8,128)(2,1)S(1)} collective-permute-done((bf16[192,1024]{1,0:T(8,128)(2,1)S(1)}, bf16[192,1024]{1,0:T(8,128)(2,1)S(1)}, u32[]{:S(2)}, u32[]{:S(2)}) %collective-permute-start.19) | collective-permute-done | bytes 393248 | tf_op jit(solution)/shard_map/ppermute | solution.py:107
  140.2 8.5 %collective-permute-done.24 = bf16[192,1024]{1,0:T(8,128)(2,1)S(1)} collective-permute-done((bf16[192,1024]{1,0:T(8,128)(2,1)S(1)}, bf16[192,1024]{1,0:T(8,128)(2,1)S(1)}, u32[]{:S(2)}, u32[]{:S(2)}) %collective-permute-start.24) | collective-permute-done | bytes 393248 | tf_op jit(solution)/shard_map/ppermute | solution.py:115
  148.6 2.3 %collective-permute-done.26 = bf16[192,1024]{1,0:T(8,128)(2,1)S(1)} collective-permute-done((bf16[192,1024]{1,0:T(8,128)(2,1)S(1)}, bf16[192,1024]{1,0:T(8,128)(2,1)S(1)}, u32[]{:S(2)}, u32[]{:S(2)}) %collective-permute-start.26) | collective-permute-done | bytes 393248 | tf_op jit(solution)/shard_map/ppermute | solution.py:115
  (120 shorter events, 52.5 us)
Async XLA Ops:
  4.5 25.5 %collective-permute-start.3 = (bf16[400,1024]{1,0:T(8,128)(2,1)S(1)}, bf16[400,1024]{1,0:T(8,128)(2,1)S(1)}, u32[]{:S(2)}, u32[]{:S(2)}) collective-permute-start(bf16[400,1024]{1,0:T(8,128)(2,1)S(1)} %shard_map.91), channel_id=1, source_target_pairs={{4,8},{8,4},{5,9},{9,5},{6,10},{10,6},{7,11},{11,7},{20,24},{24,20... | collective-permute-start | bytes 2457608 | tf_op jit(solution)/shard_map/ppermute | solution.py:115
  5.2 24.8 %collective-permute-start = (bf16[400,1024]{1,0:T(8,128)(2,1)S(1)}, bf16[400,1024]{1,0:T(8,128)(2,1)S(1)}, u32[]{:S(2)}, u32[]{:S(2)}) collective-permute-start(bf16[400,1024]{1,0:T(8,128)(2,1)S(1)} %shard_map.91), channel_id=1, source_target_pairs={{0,4},{4,0},{8,12},{12,8},{1,5},{5,1},{9,13},{13,9},{2,6},{6,2},{1... | collective-permute-start | bytes 2457608 | tf_op jit(solution)/shard_map/ppermute | solution.py:115
  11.1 18.9 %collective-permute-start.6 = (bf16[384,1024]{1,0:T(8,128)(2,1)}, bf16[384,1024]{1,0:T(8,128)(2,1)S(1)}, u32[]{:S(2)}, u32[]{:S(2)}) collective-permute-start(bf16[384,1024]{1,0:T(8,128)(2,1)} %refs_0_.1), channel_id=1, source_target_pairs={{0,2},{1,3},{2,0},{3,1},{4,6},{5,7},{6,4},{7,5},{8,10},{9,11},{10,... | collective-permute-start | bytes 2359304 | tf_op jit(solution)/shard_map/ppermute | solution.py:107
  32.1 29.5 %collective-permute-start.10 = (bf16[2048,512]{1,0:T(8,128)(2,1)}, bf16[2048,512]{1,0:T(8,128)(2,1)S(1)}, u32[]{:S(2)}, u32[]{:S(2)}) collective-permute-start(bf16[2048,512]{1,0:T(8,128)(2,1)} %shard_map.94), channel_id=1, source_target_pairs={{0,1},{1,0},{2,3},{3,2},{4,5},{5,4},{6,7},{7,6},{8,9},{9,8},{10,11... | collective-permute-start | bytes 6291464 | tf_op jit(solution)/shard_map/ppermute | solution.py:111
  32.1 19.5 %collective-permute-start.1 = (bf16[400,1024]{1,0:T(8,128)(2,1)}, bf16[400,1024]{1,0:T(8,128)(2,1)}, u32[]{:S(2)}, u32[]{:S(2)}) collective-permute-start(bf16[400,1024]{1,0:T(8,128)(2,1)} %copy-done.10), channel_id=1, source_target_pairs={{4,8},{8,4},{5,9},{9,5},{6,10},{10,6},{7,11},{11,7},{20,24},{24,20... | collective-permute-start | bytes 2457608 | tf_op jit(solution)/shard_map/ppermute | solution.py:115
  33.7 22.9 %collective-permute-start.4 = (bf16[400,1024]{1,0:T(8,128)(2,1)}, bf16[400,1024]{1,0:T(8,128)(2,1)}, u32[]{:S(2)}, u32[]{:S(2)}) collective-permute-start(bf16[400,1024]{1,0:T(8,128)(2,1)} %copy-done.23), channel_id=1, source_target_pairs={{4,0},{8,12},{5,1},{9,13},{6,2},{10,14},{7,3},{11,15},{20,16},{24,... | collective-permute-start | bytes 2457608 | tf_op jit(solution)/shard_map/ppermute | solution.py:115
  35.0 21.6 %collective-permute-start.5 = (bf16[400,1024]{1,0:T(8,128)(2,1)}, bf16[400,1024]{1,0:T(8,128)(2,1)}, u32[]{:S(2)}, u32[]{:S(2)}) collective-permute-start(bf16[400,1024]{1,0:T(8,128)(2,1)} %copy-done.10), channel_id=1, source_target_pairs={{0,2},{1,3},{2,0},{3,1},{4,6},{5,7},{6,4},{7,5},{8,10},{9,11},{10,... | collective-permute-start | bytes 2457608 | tf_op jit(solution)/shard_map/ppermute | solution.py:107
  42.1 14.1 %collective-permute-start.7 = (bf16[192,1024]{1,0:T(8,128)(2,1)}, bf16[192,1024]{1,0:T(8,128)(2,1)}, u32[]{:S(2)}, u32[]{:S(2)}) collective-permute-start(bf16[192,1024]{1,0:T(8,128)(2,1)} %shard_map.92), channel_id=1, source_target_pairs={{0,4},{12,8},{1,5},{13,9},{2,6},{14,10},{3,7},{15,11},{16,20},{28,... | collective-permute-start | bytes 1179656 | tf_op jit(solution)/shard_map/ppermute | solution.py:115
  51.6 27.3 %collective-permute-start.2 = (bf16[400,1024]{1,0:T(8,128)(2,1)}, bf16[400,1024]{1,0:T(8,128)(2,1)}, u32[]{:S(2)}, u32[]{:S(2)}) collective-permute-start(bf16[400,1024]{1,0:T(8,128)(2,1)} %collective-permute-done.1.rest_1_.inner_ref), channel_id=1, source_target_pairs={{4,0},{8,12},{5,1},{9,13},{6,2},{10,14},{7,3},{11,15},{20,16},{24,... | collective-permute-start | bytes 2457608 | tf_op jit(solution)/shard_map/ppermute | solution.py:115
  59.4 19.6 %collective-permute-start.8 = (bf16[384,1024]{1,0:T(8,128)(2,1)}, bf16[384,1024]{1,0:T(8,128)(2,1)}, u32[]{:S(2)}, u32[]{:S(2)}) collective-permute-start(bf16[384,1024]{1,0:T(8,128)(2,1)} %get-tuple-element.27.refs_0_), channel_id=1, source_target_pairs={{0,2},{1,3},{2,0},{3,1},{4,6},{5,7},{6,4},{7,5},{8,10},{9,11},{10,... | collective-permute-start | bytes 2359304 | tf_op jit(solution)/shard_map/ppermute | solution.py:107
  60.9 13.6 %collective-permute-start.9 = (bf16[192,1024]{1,0:T(8,128)(2,1)}, bf16[192,1024]{1,0:T(8,128)(2,1)S(1)}, u32[]{:S(2)}, u32[]{:S(2)}) collective-permute-start(bf16[192,1024]{1,0:T(8,128)(2,1)} %collective-permute-done.7.rest_2_), channel_id=1, source_target_pairs={{4,8},{8,4},{5,9},{9,5},{6,10},{10,6},{7,11},{11,7},{20,24},{24,20... | collective-permute-start | bytes 1179656 | tf_op jit(solution)/shard_map/ppermute | solution.py:115
  69.1 22.1 %collective-permute-start.14 = (bf16[384,1024]{1,0:T(8,128)(2,1)}, bf16[384,1024]{1,0:T(8,128)(2,1)}, u32[]{:S(2)}, u32[]{:S(2)}) collective-permute-start(bf16[384,1024]{1,0:T(8,128)(2,1)} %get-tuple-element.33), channel_id=1, source_target_pairs={{0,1},{1,0},{2,3},{3,2},{4,5},{5,4},{6,7},{7,6},{8,9},{9,8},{10,11... | collective-permute-start | bytes 2359304 | tf_op jit(solution)/shard_map/ppermute | solution.py:111
  74.0 19.7 %collective-permute-start.13 = (bf16[384,1024]{1,0:T(8,128)(2,1)}, bf16[384,1024]{1,0:T(8,128)(2,1)}, u32[]{:S(2)}, u32[]{:S(2)}) collective-permute-start(bf16[384,1024]{1,0:T(8,128)(2,1)} %get-tuple-element.32), channel_id=1, source_target_pairs={{0,1},{1,0},{2,3},{3,2},{4,5},{5,4},{6,7},{7,6},{8,9},{9,8},{10,11... | collective-permute-start | bytes 2359304 | tf_op jit(solution)/shard_map/ppermute | solution.py:111
  74.5 21.3 %collective-permute-start.12 = (bf16[192,1024]{1,0:T(8,128)(2,1)S(1)}, bf16[192,1024]{1,0:T(8,128)(2,1)}, u32[]{:S(2)}, u32[]{:S(2)}) collective-permute-start(bf16[192,1024]{1,0:T(8,128)(2,1)S(1)} %collective-permute-done.9.rest_1_.refs_6_), channel_id=1, source_target_pairs={{4,0},{8,12},{5,1},{9,13},{6,2},{10,14},{7,3},{11,15},{20,16},{24,... | collective-permute-start | bytes 1179656 | tf_op jit(solution)/shard_map/ppermute | solution.py:115
  81.7 14.2 %collective-permute-start.11 = (bf16[192,1024]{1,0:T(8,128)(2,1)}, bf16[192,1024]{1,0:T(8,128)(2,1)S(1)}, u32[]{:S(2)}, u32[]{:S(2)}) collective-permute-start(bf16[192,1024]{1,0:T(8,128)(2,1)} %get-tuple-element.30.refs_0_), channel_id=1, source_target_pairs={{0,2},{1,3},{2,0},{3,1},{4,6},{5,7},{6,4},{7,5},{8,10},{9,11},{10,... | collective-permute-start | bytes 1179656 | tf_op jit(solution)/shard_map/ppermute | solution.py:107
  83.2 16.9 %collective-permute-start.17 = (bf16[256,2048]{1,0:T(8,128)(2,1)}, bf16[256,2048]{1,0:T(8,128)(2,1)S(1)}, u32[]{:S(2)}, u32[]{:S(2)}) collective-permute-start(bf16[256,2048]{1,0:T(8,128)(2,1)} %pad_maximum_fusion.rest_3_), channel_id=1, source_target_pairs={{0,1},{1,0},{2,3},{3,2},{4,5},{5,4},{6,7},{7,6},{8,9},{9,8},{10,11... | collective-permute-start | bytes 3145736 | tf_op jit(solution)/shard_map/ppermute | solution.py:111
  102.1 12.0 %collective-permute-start.18 = (bf16[192,1024]{1,0:T(8,128)(2,1)S(1)}, bf16[192,1024]{1,0:T(8,128)(2,1)S(1)}, u32[]{:S(2)}, u32[]{:S(2)}) collective-permute-start(bf16[192,1024]{1,0:T(8,128)(2,1)S(1)} %get-tuple-element.41), channel_id=1, source_target_pairs={{0,2},{1,3},{2,0},{3,1},{4,6},{5,7},{6,4},{7,5},{8,10},{9,11},{10,... | collective-permute-start | bytes 1179656 | tf_op jit(solution)/shard_map/ppermute | solution.py:107
  103.3 19.2 %collective-permute-start.21 = (bf16[192,1024]{1,0:T(8,128)(2,1)S(1)}, bf16[192,1024]{1,0:T(8,128)(2,1)S(1)}, u32[]{:S(2)}, u32[]{:S(2)}) collective-permute-start(bf16[192,1024]{1,0:T(8,128)(2,1)S(1)} %get-tuple-element.46), channel_id=1, source_target_pairs={{0,2},{1,3},{2,0},{3,1},{4,6},{5,7},{6,4},{7,5},{8,10},{9,11},{10,... | collective-permute-start | bytes 1179656 | tf_op jit(solution)/shard_map/ppermute | solution.py:107
  119.6 12.3 %collective-permute-start.25 = (bf16[192,1024]{1,0:T(8,128)(2,1)S(1)}, bf16[192,1024]{1,0:T(8,128)(2,1)S(1)}, u32[]{:S(2)}, u32[]{:S(2)}) collective-permute-start(bf16[192,1024]{1,0:T(8,128)(2,1)S(1)} %get-tuple-element.48), channel_id=1, source_target_pairs={{0,2},{1,3},{2,0},{3,1},{4,6},{5,7},{6,4},{7,5},{8,10},{9,11},{10,... | collective-permute-start | bytes 1179656 | tf_op jit(solution)/shard_map/ppermute | solution.py:107
  120.2 15.6 %collective-permute-start.20 = (bf16[192,1024]{1,0:T(8,128)(2,1)S(1)}, bf16[192,1024]{1,0:T(8,128)(2,1)S(1)}, u32[]{:S(2)}, u32[]{:S(2)}) collective-permute-start(bf16[192,1024]{1,0:T(8,128)(2,1)S(1)} %add_convert_fusion.3), channel_id=1, source_target_pairs={{4,8},{8,4},{5,9},{9,5},{6,10},{10,6},{7,11},{11,7},{20,24},{24,20... | collective-permute-start | bytes 1179656 | tf_op jit(solution)/shard_map/ppermute | solution.py:115
  120.9 18.0 %collective-permute-start.19 = (bf16[192,1024]{1,0:T(8,128)(2,1)S(1)}, bf16[192,1024]{1,0:T(8,128)(2,1)S(1)}, u32[]{:S(2)}, u32[]{:S(2)}) collective-permute-start(bf16[192,1024]{1,0:T(8,128)(2,1)S(1)} %get-tuple-element.43), channel_id=1, source_target_pairs={{0,2},{1,3},{2,0},{3,1},{4,6},{5,7},{6,4},{7,5},{8,10},{9,11},{10,... | collective-permute-start | bytes 1179656 | tf_op jit(solution)/shard_map/ppermute | solution.py:107
  126.3 13.9 %collective-permute-start.22 = (bf16[192,1024]{1,0:T(8,128)(2,1)S(1)}, bf16[192,1024]{1,0:T(8,128)(2,1)S(1)}, u32[]{:S(2)}, u32[]{:S(2)}) collective-permute-start(bf16[192,1024]{1,0:T(8,128)(2,1)S(1)} %get-tuple-element.61), channel_id=1, source_target_pairs={{0,8},{12,4},{1,9},{13,5},{2,10},{14,6},{3,11},{15,7},{16,24},{28,... | collective-permute-start | bytes 1179656 | tf_op jit(solution)/shard_map/ppermute | solution.py:115
  130.6 18.0 %collective-permute-start.24 = (bf16[192,1024]{1,0:T(8,128)(2,1)S(1)}, bf16[192,1024]{1,0:T(8,128)(2,1)S(1)}, u32[]{:S(2)}, u32[]{:S(2)}) collective-permute-start(bf16[192,1024]{1,0:T(8,128)(2,1)S(1)} %get-tuple-element.62), channel_id=1, source_target_pairs={{4,12},{8,0},{5,13},{9,1},{6,14},{10,2},{7,15},{11,3},{20,28},{24,... | collective-permute-start | bytes 1179656 | tf_op jit(solution)/shard_map/ppermute | solution.py:115
  132.0 18.9 %collective-permute-start.26 = (bf16[192,1024]{1,0:T(8,128)(2,1)S(1)}, bf16[192,1024]{1,0:T(8,128)(2,1)S(1)}, u32[]{:S(2)}, u32[]{:S(2)}) collective-permute-start(bf16[192,1024]{1,0:T(8,128)(2,1)S(1)} %add_convert_fusion.1), channel_id=1, source_target_pairs={{0,4},{4,0},{8,12},{12,8},{1,5},{5,1},{9,13},{13,9},{2,6},{6,2},{1... | collective-permute-start | bytes 1179656 | tf_op jit(solution)/shard_map/ppermute | solution.py:115
  (32 other events, 106.1 us)

commit v8 on v7

--- a/solution.py
+++ b/solution.py
@@ -115,15 +115,36 @@
     return lax.ppermute(block, "blk", route)
 
 
-def on_core(body, out_shape, in_specs, flops=1024):
+def cheap():
+    return pl.CostEstimate(flops=1024, bytes_accessed=1024, transcendentals=0)
+
+
+TOKEN = jax.ShapeDtypeStruct((8, 128), jnp.float32)
+VMEM_LIMIT = 40 * 2**20
+
+
+def on_core(body, out_shape, in_specs, scratch=()):
     return pl.pallas_call(
         body,
         out_shape=out_shape,
         in_specs=in_specs,
         out_specs=jax.tree.map(lambda _: VMEM, out_shape),
-        compiler_params=pltpu.CompilerParams(vmem_limit_bytes=40 * 2**20),
-        cost_estimate=pl.CostEstimate(flops=flops, bytes_accessed=1024, transcendentals=0),
-    )
+        scratch_shapes=scratch,
+        compiler_params=pltpu.CompilerParams(vmem_limit_bytes=VMEM_LIMIT),
+        cost_estimate=cheap(),
+    )
+
+
+def copies(source, start, target, size, pieces, sems, first):
+    step = size // pieces
+    return [
+        pltpu.make_async_copy(
+            source.at[pl.ds(start + index * step, step)],
+            target.at[pl.ds(index * step, step)],
+            sems.at[first + index],
+        )
+        for index in range(pieces)
+    ]
 
 
 def after(block, *others):
@@ -133,70 +154,79 @@
         in_specs=[ANYWHERE] * (1 + len(others)),
         out_specs=ANYWHERE,
         input_output_aliases={0: 0},
-        cost_estimate=pl.CostEstimate(flops=16, bytes_accessed=16, transcendentals=0),
+        cost_estimate=cheap(),
     )(block, *others)
+
+
+def moved(sources_of, shapes_out, operands, specs, flag=False, flops=1024):
+    kinds = sources_of if flag else [sources_of]
+    total = sum(pieces for _, _, _, pieces in kinds[0])
+
+    def body(*refs):
+        out_refs = refs[len(operands) : len(operands) + len(shapes_out)]
+        buffers = refs[len(operands) + len(shapes_out) : -2]
+        in_sems, out_sems = refs[-2:]
+
+        def run(sources):
+            first, inward, outward = 0, [], []
+            for (index, start, size, pieces), out, buffer in zip(sources, out_refs, buffers):
+                inward += copies(refs[index], start, buffer, size, pieces, in_sems, first)
+                outward += copies(buffer, 0, out, size, pieces, out_sems, first)
+                first += pieces
+            for copy in inward:
+                copy.start()
+            for copy, next_copy in zip(inward, outward):
+                copy.wait()
+                next_copy.start()
+            for copy in outward:
+                copy.wait()
+
+        if flag:
+            for kind, sources in enumerate(kinds):
+
+                @pl.when(refs[0][INNER_AT] == kind)
+                def _(sources=sources):
+                    run(sources)
+
+        else:
+            run(kinds[0])
+
+    return pl.pallas_call(
+        body,
+        out_shape=shapes_out,
+        in_specs=specs,
+        out_specs=[ANYWHERE] * len(shapes_out),
+        scratch_shapes=[pltpu.VMEM(shape.shape, shape.dtype) for shape in shapes_out]
+        + [pltpu.SemaphoreType.DMA((total,))] * 2,
+        compiler_params=pltpu.CompilerParams(vmem_limit_bytes=VMEM_LIMIT),
+        cost_estimate=pl.CostEstimate(flops=flops, bytes_accessed=1024, transcendentals=0),
+    )(*operands)
 
 
 def lower_half(block):
     rows = block.shape[0] // 2
-
-    def body(block_ref, out_ref, sem):
-        copy = pltpu.make_async_copy(block_ref.at[pl.ds(rows, rows)], out_ref, sem)
-        copy.start()
-        copy.wait()
-
-    return pl.pallas_call(
-        body,
-        out_shape=jax.ShapeDtypeStruct((rows, block.shape[1]), block.dtype),
-        in_specs=[ANYWHERE],
-        out_specs=VMEM,
-        scratch_shapes=[pltpu.SemaphoreType.DMA],
-        cost_estimate=pl.CostEstimate(flops=1024, bytes_accessed=1024, transcendentals=0),
-    )(block)
+    shape = jax.ShapeDtypeStruct((rows, block.shape[1]), block.dtype)
+    return moved([(0, rows, rows, 4)], [shape], [block], [ANYWHERE], flops=8 * 2**30)[0]
 
 
 def chosen(plan, if_inner, if_outer, spans, *others):
-    width = if_inner.shape[1]
-
-    def body(plan_ref, inner_ref, outer_ref, *rest):
-        out_refs, sems = rest[len(others) : -1], rest[-1]
-
-        def copy_from(source):
-            copies = [
-                pltpu.make_async_copy(source.at[pl.ds(start, size)], out, sems.at[index])
-                for index, ((start, size), out) in enumerate(zip(spans, out_refs))
-            ]
-            for copy in copies:
-                copy.start()
-            for copy in copies:
-                copy.wait()
-
-        @pl.when(plan_ref[INNER_AT] == 1)
-        def _():
-            copy_from(inner_ref)
-
-        @pl.when(plan_ref[INNER_AT] == 0)
-        def _():
-            copy_from(outer_ref)
-
-    return pl.pallas_call(
-        body,
-        out_shape=[jax.ShapeDtypeStruct((size, width), if_inner.dtype) for _, size in spans],
-        in_specs=[SMEM] + [ANYWHERE] * (2 + len(others)),
-        out_specs=[VMEM] * len(spans),
-        scratch_shapes=[pltpu.SemaphoreType.DMA((len(spans),))],
-        cost_estimate=pl.CostEstimate(flops=16, bytes_accessed=16, transcendentals=0),
-    )(plan, if_inner, if_outer, *others)
+    shapes = [
+        jax.ShapeDtypeStruct((size, if_inner.shape[1]), if_inner.dtype) for _, size, _ in spans
+    ]
+    kinds = [[(index, *span) for span in spans] for index in (2, 1)]
+    operands = [plan, if_inner, if_outer, *others]
+    return moved(kinds, shapes, operands, [SMEM] + [ANYWHERE] * (len(operands) - 1), flag=True)
 
 
 def with_facts(rows, gates, block_list, block_count, owner):
     count, width = rows.shape
-    offsets, blocks = block_list.shape
-    total = owner.shape[1]
-
-    def body(rows_ref, gates_ref, list_ref, count_ref, owner_ref, out_ref, sem):
-        copy = pltpu.make_async_copy(rows_ref, out_ref.at[pl.ds(0, count)], sem)
-        copy.start()
+    blocks, _, offsets = block_list.shape
+    total = owner.shape[0]
+
+    def body(rows_ref, gates_ref, list_ref, count_ref, owner_ref, out_ref, sems):
+        moves = copies(rows_ref, 0, out_ref, count, 4, sems, 0)
+        for copy in moves:
+            copy.start()
         block_of = lax.broadcasted_iota(jnp.int32, (1, total), 1) // (total // blocks)
         facts = []
         for offset in range(offsets):
@@ -204,25 +234,22 @@
             for block in range(blocks):
                 used = jnp.int32(0)
                 for place in range(blocks):
-                    found = (list_ref[offset, place] == block) & (place < count_ref[offset])
+                    found = (list_ref[place, 0, offset] == block) & (place < count_ref[0, offset])
                     used = used | found.astype(jnp.int32)
                 mask = mask + jnp.where(block_of == block, used.astype(jnp.float32), 0.0)
             facts.append(gates_ref[offset : offset + 1, :] * mask)
-        facts.append((owner_ref[...] >> 8).astype(jnp.float32))
-        facts.append((owner_ref[...] & 255).astype(jnp.float32))
+        numbers = owner_ref[...].reshape(1, total)
+        facts.append((numbers >> 8).astype(jnp.float32))
+        facts.append((numbers & 255).astype(jnp.float32))
         facts.append(jnp.zeros((FACT_ROWS - len(facts), total), jnp.float32))
         out_ref[count:, :] = jnp.zeros((FACT_ROWS, width), jnp.bfloat16)
         out_ref[count:, :total] = jnp.concatenate(facts, axis=0).astype(jnp.bfloat16)
-        copy.wait()
-
-    return pl.pallas_call(
-        body,
-        out_shape=jax.ShapeDtypeStruct((count + FACT_ROWS, width), rows.dtype),
-        in_specs=[ANYWHERE, VMEM, SMEM, SMEM, VMEM],
-        out_specs=VMEM,
-        scratch_shapes=[pltpu.SemaphoreType.DMA],
-        compiler_params=pltpu.CompilerParams(vmem_limit_bytes=40 * 2**20),
-        cost_estimate=pl.CostEstimate(flops=1024, bytes_accessed=1024, transcendentals=0),
+        for copy in moves:
+            copy.wait()
+
+    shape = jax.ShapeDtypeStruct((count + FACT_ROWS, width), rows.dtype)
+    return on_core(
+        body, shape, [ANYWHERE, VMEM, SMEM, SMEM, VMEM], [pltpu.SemaphoreType.DMA((4,))]
     )(rows, gates, block_list, block_count, owner)
 
 
@@ -230,51 +257,90 @@
     sizes, parts, weights, places, before=None, send=True, choice=None, waits=()
 ):
     width, columns = weights[0].shape
+    rows, count = sum(sizes), len(places)
     blocks = [block for part in parts for block in part]
-    used = [weights[place] for place in places] + [weights[2]]
-    operands = blocks + used
-    specs = [VMEM] * len(operands)
+    operands = blocks + [weights[place] for place in places] + [weights[2]]
+    specs = [ANYWHERE] * len(operands)
+    flag_at = len(operands)
+    if choice is not None:
+        operands += [choice[0], choice[1]]
+        specs += [SMEM, ANYWHERE]
+    before_at = len(operands)
     if before is not None:
         operands.append(before)
         specs.append(VMEM)
-    if choice is not None:
-        operands += [choice[0], choice[1]]
-        specs += [SMEM, VMEM]
     operands += waits
-    specs += [ANYWHERE] * len(waits)
+    specs += [VMEM] * len(waits)
+    row_pieces, weight_pieces = 2, 2
+    row_sems = len(blocks) * row_pieces
 
     def body(*refs):
-        results = refs[len(operands) :]
-        weight_refs = refs[len(blocks) : len(blocks) + len(used)]
-        next_ref = len(blocks) + len(used)
-        before_ref = refs[next_ref] if before is not None else None
-        next_ref += before is not None
-        start = 0
+        results = refs[len(operands) : -4]
+        row_buffer, weight_buffer, sems, weight_sems = refs[-4:]
+        row_moves, weight_moves = [], [[], []]
         for part, size in enumerate(sizes):
-            span = slice(start, start + size)
-            start += size
-            rows = [refs[part * len(places) + index][:size, :] for index in range(len(places))]
-            if choice is not None and part == len(sizes) - 1:
-                rows[0] = jnp.where(refs[next_ref][INNER_AT] == 1, refs[next_ref + 1][:size, :], rows[0])
-            for side in range(2):
-                at = slice(side * columns, (side + 1) * columns)
-                total = None if before is None else before_ref[span, at]
-                for index, place in enumerate(places):
-                    if side == 0:
-                        weight = weight_refs[index][...]
-                    else:
-                        weight = weight_refs[-1][place * width : (place + 1) * width, :]
-                    product = jnp.dot(rows[index], weight, preferred_element_type=jnp.float32)
-                    total = product if total is None else total + product
-                results[0][span, at] = total
-                if send:
-                    results[1][span, at] = total.astype(jnp.bfloat16)
-
-    size = (sum(sizes), 2 * columns)
-    shapes = [jax.ShapeDtypeStruct(size, jnp.float32)]
+            for index in range(count):
+                block = part * count + index
+                target = row_buffer.at[index, pl.ds(sum(sizes[:part]), size)]
+                first = block * row_pieces
+                move = copies(refs[block], 0, target, size, row_pieces, sems, first)
+                if choice is not None and part == len(sizes) - 1:
+                    source = refs[flag_at + 1]
+                    other = copies(source, 0, target, size, row_pieces, sems, first)
+                    for kind, group in enumerate((move, other)):
+
+                        @pl.when(refs[flag_at][INNER_AT] == kind)
+                        def _(group=group):
+                            for copy in group:
+                                copy.start()
+
+                else:
+                    for copy in move:
+                        copy.start()
+                row_moves += move
+        for side in range(2):
+            for index, place in enumerate(places):
+                source = refs[len(blocks) + index] if side == 0 else refs[len(blocks) + count]
+                weight_moves[side] += copies(
+                    source,
+                    0 if side == 0 else place * width,
+                    weight_buffer.at[side, index],
+                    width,
+                    weight_pieces,
+                    weight_sems,
+                    (side * count + index) * weight_pieces,
+                )
+            for copy in weight_moves[side]:
+                copy.start()
+        for copy in row_moves:
+            copy.wait()
+        for side in range(2):
+            for copy in weight_moves[side]:
+                copy.wait()
+            at = slice(side * columns, (side + 1) * columns)
+            total = None if before is None else refs[before_at][:, at]
+            for index in range(count):
+                product = jnp.dot(
+                    row_buffer[index],
+                    weight_buffer[side, index],
+                    preferred_element_type=jnp.float32,
+                )
+                total = product if total is None else total + product
+            results[0][:, at] = total
+            if send:
+                results[1][:, at] = total.astype(jnp.bfloat16)
+        results[-1][...] = jnp.zeros(TOKEN.shape, TOKEN.dtype)
+
+    shapes = [jax.ShapeDtypeStruct((rows, 2 * columns), jnp.float32)]
     if send:
-        shapes.append(jax.ShapeDtypeStruct(size, jnp.bfloat16))
-    return on_core(body, shapes, specs)(*operands)
+        shapes.append(jax.ShapeDtypeStruct((rows, 2 * columns), jnp.bfloat16))
+    scratch = [
+        pltpu.VMEM((count, rows, width), jnp.bfloat16),
+        pltpu.VMEM((2, count, width, columns), jnp.bfloat16),
+        pltpu.SemaphoreType.DMA((row_sems,)),
+        pltpu.SemaphoreType.DMA((2 * count * weight_pieces,)),
+    ]
+    return on_core(body, shapes + [TOKEN], specs, scratch)(*operands)
 
 
 def collected_rows(owned, slot, plan, sums, got, facts, before):
@@ -303,17 +369,42 @@
     return results
 
 
+def fact_scratch(width):
+    return [pltpu.VMEM((FACT_ROWS, width), jnp.bfloat16), pltpu.SemaphoreType.DMA((1,))]
+
+
+def facts_of(facts_ref, buffer, sem):
+    last = facts_ref.shape[0] - FACT_ROWS
+    (copy,) = copies(facts_ref, last, buffer, FACT_ROWS, 1, sem, 0)
+    copy.start()
+    copy.wait()
+    return buffer
+
+
 def collect(owned, slot, plan, sums, got, facts, before):
     operands = [plan, sums, got, facts] + ([] if before is None else [before])
 
     def body(plan_ref, sums_ref, got_ref, facts_ref, *rest):
         before_ref = rest[0] if before is not None else None
-        rows = collected_rows(owned, slot, plan_ref, sums_ref, got_ref, facts_ref, before_ref)
+        out_ref, token_ref, buffer, sem = rest[-4:]
+        facts_here = facts_of(facts_ref, buffer, sem)
+        rows = collected_rows(owned, slot, plan_ref, sums_ref, got_ref, facts_here, before_ref)
         for index in range(4):
-            rest[-1][index * owned : (index + 1) * owned, :] = rows[index]
+            out_ref[index * owned : (index + 1) * owned, :] = rows[index]
+        token_ref[...] = jnp.zeros(TOKEN.shape, TOKEN.dtype)
 
     shape = jax.ShapeDtypeStruct((4 * owned, sums.shape[1] // 2), jnp.float32)
-    return on_core(body, shape, [SMEM] + [VMEM] * (len(operands) - 1))(*operands)
+    specs = [SMEM, VMEM, VMEM, ANYWHERE] + [VMEM] * (len(operands) - 4)
+    return on_core(body, [shape, TOKEN], specs, fact_scratch(facts.shape[1]))(*operands)
+
+
+def added(block, other, wait):
+    def body(block_ref, other_ref, _, out_ref):
+        total = block_ref[...].astype(jnp.float32) + other_ref[...].astype(jnp.float32)
+        out_ref[...] = total.astype(out_ref.dtype)
+
+    shape = jax.ShapeDtypeStruct(block.shape, block.dtype)
+    return on_core(body, shape, [VMEM, VMEM, ANYWHERE])(block, other, wait)
 
 
 def down(held, own_ref, lent_ref, sent_ref, kept_ref):
@@ -333,7 +424,8 @@
     ]
 
     def first(plan_ref, sums_ref, got_ref, facts_ref, before_ref, own_ref, lent_ref, *out_refs):
-        rows = collected_rows(owned, slot, plan_ref, sums_ref, got_ref, facts_ref, before_ref)
+        facts_here = facts_of(facts_ref, *out_refs[3:])
+        rows = collected_rows(owned, slot, plan_ref, sums_ref, got_ref, facts_here, before_ref)
         down(rows[0].astype(jnp.bfloat16), own_ref, lent_ref, out_refs[0], out_refs[1])
         for index in range(1, 4):
             out_refs[2][(index - 1) * owned : index * owned, :] = rows[index].astype(jnp.bfloat16)
@@ -352,7 +444,8 @@
         return kept + across_chips(sent).astype(jnp.float32)
 
     held_shape = jax.ShapeDtypeStruct((3 * owned, 2 * units), jnp.bfloat16)
-    sent, kept, held = on_core(first, pair + [held_shape], [SMEM] + [VMEM] * 6)(
+    specs = [SMEM, VMEM, VMEM, ANYWHERE] + [VMEM] * 3
+    sent, kept, held = on_core(first, pair + [held_shape], specs, fact_scratch(facts.shape[1]))(
         plan, sums, got, facts, before, down_own, down_lent
     )
     got_first = across_chips(sent)
@@ -374,7 +467,7 @@
 
     own_far = across_chips(tokens)
     own = with_facts(
-        tokens, route_gates.T, block_list[0], block_count[0], owner_token[None]
+        tokens, route_gates.T, jnp.transpose(block_list, (2, 0, 1)), block_count, owner_token
     )
     beside = along(own, BESIDE)
     middle = along(own, MIDDLE)
@@ -399,11 +492,12 @@
     inner_last = along(beside, MIDDLE)
     outer_next = along(middle, OUTWARD)
     beside_far = across_chips(beside)
-    inward_far = along(lower_half(own_far), INWARD)
+    own_far_half = lower_half(own_far)
+    inward_far = along(own_far_half, INWARD)
     lend = jnp.concatenate([quarter(1), quarter(3)])
-    lent = across_cores(after(lend, beside, middle, own_far))
+    lent = across_cores(after(lend, own))
     weights = [quarter(0), quarter(2), lent]
-    sums_0, send_0 = partial_sums([row_count], [(tokens, own_far)], weights, (0, 1))
+    sums_0, send_0, ready_0 = partial_sums([row_count], [(tokens, own_far)], weights, (0, 1))
     got_0 = across_cores(send_0)
     lent_down = across_cores(lend_down)
 
@@ -412,7 +506,7 @@
         plan,
         middle,
         outer_next,
-        [(0, row_count), (row_count, FACT_ROWS)],
+        [(0, row_count, 4), (row_count, FACT_ROWS, 1)],
         beside_far,
         inner_last,
         inward_far,
@@ -422,50 +516,50 @@
     )
     second_far = across_chips(second)
     middle_far = along(inward_far, MIDDLE)
-    sums_1, send_1 = partial_sums([row_count], [(beside, beside_far)], weights, (0, 1))
+    sums_1, send_1, ready_1 = partial_sums([row_count], [(beside, beside_far)], weights, (0, 1))
     got_1 = across_cores(send_1)
+
+    total, _ = collect(owned, 0, plan, sums_0, got_0, own, None)
 
     last_a, last_b, last_facts = chosen(
         plan,
         inner_last,
         outer_last,
-        [(0, half), (half, half), (row_count, FACT_ROWS)],
+        [(0, half, 4), (half, half, 4), (row_count, FACT_ROWS, 1)],
         second_far,
         middle_far,
-        sums_0,
-        sums_1,
+        ready_0,
+        ready_1,
     )
     last_far_a = across_chips(last_a)
     outward_far = along(middle_far, OUTWARD)
-    total = collect(owned, 0, plan, sums_0, got_0, own[row_count:], None)
-    total = collect(owned, 1, plan, sums_1, got_1, beside[row_count:], total)
-    sums_2, send_2 = partial_sums([row_count], [(second, second_far)], weights, (0, 1))
+    total, collected_1 = collect(owned, 1, plan, sums_1, got_1, beside, total)
+    sums_2, send_2, ready_2 = partial_sums([row_count], [(second, second_far)], weights, (0, 1))
     got_2 = across_cores(send_2)
     near = partial_sums([half, half], [(last_a,), (last_b,)], weights, (0,), send=False)[0]
-    sums_3, send_3 = partial_sums(
+    sums_3, send_3, _ = partial_sums(
         [half, half],
         [(last_far_a,), (outward_far,)],
         weights,
         (1,),
         before=near,
         choice=(plan, middle_far),
-        waits=(total,),
+        waits=[collected_1],
     )
     got_3 = across_cores(send_3)
-    total = collect(owned, 2, plan, sums_2, got_2, second_facts, total)
+    total, _ = collect(owned, 2, plan, sums_2, got_2, second_facts, total)
     chunks = finish(
         owned, 3, plan, sums_3, got_3, last_facts, total, kept_down, lent_down
     )
 
-    def send(block, route):
-        return along(block.astype(jnp.bfloat16), route).astype(jnp.float32)
-
-    inward = send(chunks[0], INWARD)
-    middle = send(chunks[0], MIDDLE)
-    two_in = send(chunks[1], TWO_IN)
-    two_out = send(chunks[1] + inward, TWO_OUT)
-    beside = send(chunks[2], BESIDE)
-    return (chunks[3] + middle + two_in + two_out + beside).astype(jnp.bfloat16)
+    first, second, third = [chunk.astype(jnp.bfloat16) for chunk in chunks[:3]]
+    middle = along(first, MIDDLE)
+    inward = along(first, INWARD)
+    two_in = along(second, TWO_IN)
+    two_out = along(added(second, inward, middle), TWO_OUT)
+    beside = along(third, BESIDE)
+    arrived = [block.astype(jnp.float32) for block in (middle, two_in, two_out, beside)]
+    return (chunks[3] + sum(arrived)).astype(jnp.bfloat16)
 
 
 def on_device(*args):

time: 153 us -> 145 us (0.948)
  local copies, waits for them, and re-layouts: 19.9 us -> 8.2 us
  waiting for transfers between devices: 46.2 us -> 53.5 us
  starting transfers between devices: 45.2 us -> 40 us
  Pallas kernels: 31.4 us -> 35.4 us
  other arithmetic: 8.82 us -> 6.65 us
    ppermute x13, waiting for transfers between devices: 18 us -> 32.8 us  [along(): return lax.ppermute(block, 'blk', route)]
    unnamed x59 -> x24, local copies, waits for them, and re-layouts: 11.4 us -> 2.74 us
    ppermute x8, waiting for transfers between devices: 28 us -> 20.5 us  [across_chips(): return lax.ppermute(block, 'tp', [(i, i ^ 2) for i in range(4)])]
    ppermute x8, starting transfers between devices: 10.5 us -> 6.19 us  [across_chips(): return lax.ppermute(block, 'tp', [(i, i ^ 2) for i in range(4)])]
    pallas_call x13 -> x14, Pallas kernels: 29.9 us -> 33.8 us  [the longest x5 17 us: partial_sums(): return on_core(body, shapes + [TOKEN], specs, scratch)(*operands)]
  transfers between devices with their start and end apart: 27 -> 27, of which waited for: 12 -> 13; matrix products, arithmetic and copies ran while one was open for 10% -> 8% of each run, Pallas kernels for 18% -> 22%
where the time goes in v8:
time: 145 us; the launch traced here: 144 us
  waiting for transfers between devices  53.5 us (37%)
  starting transfers between devices  40 us (28%)
  Pallas kernels  35.4 us (24%)
  local copies, waits for them, and re-layouts  8.2 us (6%)
  other arithmetic  6.65 us (5%)
    ppermute x13, waiting for transfers between devices, along(): return lax.ppermute(block, 'blk', route)  32.8 us
    ppermute x13, starting transfers between devices, along(): return lax.ppermute(block, 'blk', route)  32.6 us
    ppermute x8, waiting for transfers between devices, across_chips(): return lax.ppermute(block, 'tp', [(i, i ^ 2) for i in range(4)])  20.5 us
    pallas_call x5, Pallas kernels, partial_sums(): return on_core(body, shapes + [TOKEN], specs, scratch)(*operands)  17 us
    pallas_call x3, Pallas kernels, moved(): pl.pallas_call(body, out_shape=shapes_out, in_specs=specs, out_specs=[ANY...  7.18 us
    ppermute x8, starting transfers between devices, across_chips(): return lax.ppermute(block, 'tp', [(i, i ^ 2) for i in range(4)])  6.19 us
    pallas_call x3, Pallas kernels, collect(): on_core(body, [shape, TOKEN], specs, fact_scratch(facts.shape[1]))  5.93 us
    squeeze x1, local copies, waits for them, and re-layouts, quarter(): lax.dynamic_index_in_dim(q, share ^ j, 0, keepdims=False)  3.42 us
  transfers between devices with their start and end apart: 27, of which 13 were waited for; matrix products, arithmetic and copies ran while one was open for 8% of the time, Pallas kernels for 22%

profile of v8, /device:TPU:0, one launch (start us, length us, event | category | flops | bytes accessed | tf_op | source)
XLA Modules:
  0.0 144.3 jit_solution(13172297890845671027)
XLA Ops:
  4.5 3.1 %collective-permute-start = (bf16[400,1024]{1,0:T(8,128)(2,1)S(1)}, bf16[400,1024]{1,0:T(8,128)(2,1)}, u32[]{:S(2)}, u32[]{:S(2)}) collective-permute-start(bf16[400,1024]{1,0:T(8,128)(2,1)S(1)} %shard_map.91.refs_1_.facts_ref), channel_id=1, source_target_pairs={{0,4},{4,0},{8,12},{12,8},{1,5},{5,1},{9,13},{13,9},{2,6},{6,2},{1... | collective-permute-start | bytes 2457608 | tf_op jit(solution)/shard_map/ppermute | solution.py:115
  10.7 3.4 %dynamic-slice_bitcast_fusion.4 = (bf16[1024,256]{1,0:T(8,128)(2,1)S(1)}, bf16[1024,256]{1,0:T(8,128)(2,1)S(1)}, bf16[1024,256]{1,0:T(8,128)(2,1)}, bf16[1024,25...) fusion(bf16[4,1024,256]{2,1,0:T(8,128)(2,1)} %bitcast.32, ...), kind=kLoop, calls=%fused_computation.13 | loop fusion | bytes 8388624 | tf_op jit(solution)/shard_map/jit(dynamic_index_in_dim)/squeeze | solution.py:480
  15.6 2.2 %pad_maximum_fusion.1.refs_7_.refs_2_ = bf16[1024,512]{1,0:T(8,128)(2,1)} fusion(bf16[1024,256]{1,0:T(8,128)(2,1)S(1)} %get-tuple-element.74, bf16[1024,256]{1,0:T(8,128)(2,1)} %get-tuple-element.75), kind=kLoop, calls=%fused_computation.2 | loop fusion | flops 2097152 | bytes 2097152 | tf_op jit(solution)/shard_map/concatenate | solution.py:483
  19.2 6.8 %collective-permute-done.refs_0_.facts_ref = bf16[400,1024]{1,0:T(8,128)(2,1)} collective-permute-done((bf16[400,1024]{1,0:T(8,128)(2,1)S(1)}, bf16[400,1024]{1,0:T(8,128)(2,1)}, u32[]{:S(2)}, u32[]{:S(2)}) %collective-permute-start) | collective-permute-done | bytes 819232 | tf_op jit(solution)/shard_map/ppermute | solution.py:115
  32.3 6.4 %collective-permute-start.7 = (bf16[192,1024]{1,0:T(8,128)(2,1)}, bf16[192,1024]{1,0:T(8,128)(2,1)S(1)}, u32[]{:S(2)}, u32[]{:S(2)}) collective-permute-start(bf16[192,1024]{1,0:T(8,128)(2,1)} %shard_map.92), channel_id=1, source_target_pairs={{0,4},{12,8},{1,5},{13,9},{2,6},{14,10},{3,7},{15,11},{16,20},{28,... | collective-permute-start | bytes 1179656 | tf_op jit(solution)/shard_map/ppermute | solution.py:115
  42.2 3.7 %collective-permute-done.7.refs_5_ = bf16[192,1024]{1,0:T(8,128)(2,1)S(1)} collective-permute-done((bf16[192,1024]{1,0:T(8,128)(2,1)}, bf16[192,1024]{1,0:T(8,128)(2,1)S(1)}, u32[]{:S(2)}, u32[]{:S(2)}) %collective-permute-start.7) | collective-permute-done | bytes 393248 | tf_op jit(solution)/shard_map/ppermute | solution.py:115
  47.3 5.4 %collective-permute-done.4.refs_2_ = bf16[400,1024]{1,0:T(8,128)(2,1)} collective-permute-done((bf16[400,1024]{1,0:T(8,128)(2,1)}, bf16[400,1024]{1,0:T(8,128)(2,1)}, u32[]{:S(2)}, u32[]{:S(2)}) %collective-permute-start.4) | collective-permute-done | bytes 819232 | tf_op jit(solution)/shard_map/ppermute | solution.py:115
  52.7 2.6 %shard_map.93 = (bf16[384,1024]{1,0:T(8,128)(2,1)S(1)}, bf16[16,1024]{1,0:T(8,128)(2,1)S(1)}) custom-call(s32[9]{0:T(128)S(1)} %fusion.refs_0_.plan_ref.refs_4_, bf16[400,1024]{1,0:T(8,128)(2,1)} %collective-permute-done.3.refs_1_, bf16[400,1024]{1,0:T(8,128)(2,1)} %collective-permute-done.4.refs_2_, ...), custom_call_target="tpu_custom_call" | custom-call | flops 1024 | bytes 1024 | tf_op jit(solution)/shard_map/pallas_call | solution.py:194
  55.4 3.4 %shard_map.95 = (f32[384,1024]{1,0:T(8,128)S(1)}, bf16[384,1024]{1,0:T(8,128)(2,1)S(1)}, f32[8,128]{1,0:T(8,128)S(1)}) custom-call(bf16[384,1024]{1,0:T(8,128)(2,1)} %refs_0_.1, bf16[384,1024]{1,0:T(8,128)(2,1)} %collective-permute-done.6.refs_0_.refs_1_, bf16[1024,512]{1,0:T(8,128)(2,1)S(1)} %copy-done, ...), custom_call_target="tpu_custom_call" | custom-call | flops 1024 | bytes 1024 | tf_op jit(solution)/shard_map/pallas_call | solution.py:343
  59.6 3.4 %shard_map.96 = (f32[384,1024]{1,0:T(8,128)S(1)}, bf16[384,1024]{1,0:T(8,128)(2,1)S(1)}, f32[8,128]{1,0:T(8,128)S(1)}) custom-call(bf16[400,1024]{1,0:T(8,128)(2,1)} %collective-permute-done.refs_0_.facts_ref, bf16[400,1024]{1,0:T(8,128)(2,1)} %collective-permute-done.5.refs_3_.refs_1_, bf16[1024,512]{1,0:T(8,128)(2,1)S(1)} %copy-done, ...), custom_call_target="tpu_custom_call" | custom-call | flops 1024 | bytes 1024 | tf_op jit(solution)/shard_map/pallas_call | solution.py:343
  64.9 6.1 %collective-permute-done.8.refs_3_.refs_1_ = bf16[384,1024]{1,0:T(8,128)(2,1)S(1)} collective-permute-done((bf16[384,1024]{1,0:T(8,128)(2,1)S(1)}, bf16[384,1024]{1,0:T(8,128)(2,1)S(1)}, u32[]{:S(2)}, u32[]{:S(2)}) %collective-permute-start.8) | collective-permute-done | bytes 786464 | tf_op jit(solution)/shard_map/ppermute | solution.py:107
  71.0 2.8 %shard_map.97 = (bf16[192,1024]{1,0:T(8,128)(2,1)S(1)}, bf16[192,1024]{1,0:T(8,128)(2,1)S(1)}, bf16[16,1024]{1,0:T(8,128)(2,1)S(1)}) custom-call(s32[9]{0:T(128)S(1)} %fusion.refs_0_.plan_ref.refs_4_, bf16[400,1024]{1,0:T(8,128)(2,1)} %collective-permute-done.1.refs_4_.refs_1_, bf16[400,1024]{1,0:T(8,128)(2,1)S(1)} %collective-permute-done.2.refs_2_, ...), custom_call_target="tpu_custom_call" | custom-call | flops 1024 | bytes 1024 | tf_op jit(solution)/shard_map/pallas_call | solution.py:194
  74.5 3.6 %shard_map.102 = (f32[384,1024]{1,0:T(8,128)S(1)}, bf16[384,1024]{1,0:T(8,128)(2,1)S(1)}, f32[8,128]{1,0:T(8,128)}) custom-call(bf16[384,1024]{1,0:T(8,128)(2,1)S(1)} %get-tuple-element.34.refs_0_, bf16[384,1024]{1,0:T(8,128)(2,1)S(1)} %collective-permute-done.8.refs_3_.refs_1_, bf16[1024,512]{1,0:T(8,128)(2,1)S(1)} %copy-done, ...), custom_call_target="tpu_custom_call" | custom-call | flops 1024 | bytes 1024 | tf_op jit(solution)/shard_map/pallas_call | solution.py:343
  78.1 2.9 %shard_map.98 = (f32[384,1024]{1,0:T(8,128)S(1)}, f32[8,128]{1,0:T(8,128)}) custom-call(bf16[192,1024]{1,0:T(8,128)(2,1)S(1)} %get-tuple-element.37.refs_0_, bf16[192,1024]{1,0:T(8,128)(2,1)S(1)} %get-tuple-element.38.refs_1_, bf16[1024,512]{1,0:T(8,128)(2,1)S(1)} %copy-done, bf16[2048,512]{1,0:T(8,128)(2,1)S(1)} %collective-permute-done.10.refs_4_.refs_3_), custom_call_target="tpu_custom_call" | custom-call | flops 1024 | bytes 1024 | tf_op jit(solution)/shard_map/pallas_call | solution.py:343
  83.5 2.1 %shard_map.100 = (f32[768,512]{1,0:T(8,128)S(1)}, f32[8,128]{1,0:T(8,128)S(1)}) custom-call(s32[9]{0:T(128)S(1)} %fusion.refs_0_.plan_ref.refs_4_, f32[384,1024]{1,0:T(8,128)S(1)} %get-tuple-element.40.sums_ref, bf16[384,1024]{1,0:T(8,128)(2,1)S(1)} %collective-permute-done.13.got_ref, bf16[400,1024]{1,0:T(8,128)(2,1)} %collective-permute-done.refs_0_.facts_ref, ...), custom_call_target="tpu_custom_call" | custom-call | flops 1024 | bytes 1024 | tf_op jit(solution)/shard_map/pallas_call | solution.py:398
  85.7 3.6 %shard_map.101 = (f32[384,1024]{1,0:T(8,128)S(1)}, bf16[384,1024]{1,0:T(8,128)(2,1)S(1)}, f32[8,128]{1,0:T(8,128)}) custom-call(bf16[192,1024]{1,0:T(8,128)(2,1)S(1)} %collective-permute-done.11.refs_0_, bf16[192,1024]{1,0:T(8,128)(2,1)S(1)} %collective-permute-done.12.refs_1_, bf16[1024,512]{1,0:T(8,128)(2,1)S(1)} %pad_maximum_fusion.2.refs_8_.refs_3_.refs_2_, ...), custom_call_target="tpu_custom_call" | custom-call | flops 1024 | bytes 1024 | tf_op jit(solution)/shard_map/pallas_call | solution.py:343
  96.3 9.3 %collective-permute-done.18.refs_0_ = bf16[192,1024]{1,0:T(8,128)(2,1)S(1)} collective-permute-done((bf16[192,1024]{1,0:T(8,128)(2,1)S(1)}, bf16[192,1024]{1,0:T(8,128)(2,1)S(1)}, u32[]{:S(2)}, u32[]{:S(2)}) %collective-permute-start.18) | collective-permute-done | bytes 393248 | tf_op jit(solution)/shard_map/ppermute | solution.py:107
  106.3 8.6 %collective-permute-start.23 = (bf16[192,1024]{1,0:T(8,128)(2,1)S(1)}, bf16[192,1024]{1,0:T(8,128)(2,1)S(1)}, u32[]{:S(2)}, u32[]{:S(2)}) collective-permute-start(bf16[192,1024]{1,0:T(8,128)(2,1)S(1)} %add_convert_fusion.3), channel_id=1, source_target_pairs={{0,4},{12,8},{1,5},{13,9},{2,6},{14,10},{3,7},{15,11},{16,20},{28,... | collective-permute-start | bytes 1179656 | tf_op jit(solution)/shard_map/ppermute | solution.py:115
  116.1 4.7 %collective-permute-start.22 = (bf16[192,1024]{1,0:T(8,128)(2,1)S(1)}, bf16[192,1024]{1,0:T(8,128)(2,1)S(1)}, u32[]{:S(2)}, u32[]{:S(2)}) collective-permute-start(bf16[192,1024]{1,0:T(8,128)(2,1)S(1)} %add_convert_fusion.2.block_ref), channel_id=1, source_target_pairs={{0,8},{12,4},{1,9},{13,5},{2,10},{14,6},{3,11},{15,7},{16,24},{28,... | collective-permute-start | bytes 1179656 | tf_op jit(solution)/shard_map/ppermute | solution.py:115
  121.0 3.1 %collective-permute-done.23.other_ref = bf16[192,1024]{1,0:T(8,128)(2,1)S(1)} collective-permute-done((bf16[192,1024]{1,0:T(8,128)(2,1)S(1)}, bf16[192,1024]{1,0:T(8,128)(2,1)S(1)}, u32[]{:S(2)}, u32[]{:S(2)}) %collective-permute-start.23) | collective-permute-done | bytes 393248 | tf_op jit(solution)/shard_map/ppermute | solution.py:115
  125.5 2.6 %collective-permute-done.25 = bf16[192,1024]{1,0:T(8,128)(2,1)S(1)} collective-permute-done((bf16[192,1024]{1,0:T(8,128)(2,1)S(1)}, bf16[192,1024]{1,0:T(8,128)(2,1)S(1)}, u32[]{:S(2)}, u32[]{:S(2)}) %collective-permute-start.25) | collective-permute-done | bytes 393248 | tf_op jit(solution)/shard_map/ppermute | solution.py:107
  128.2 4.3 %collective-permute-done.22 = bf16[192,1024]{1,0:T(8,128)(2,1)S(1)} collective-permute-done((bf16[192,1024]{1,0:T(8,128)(2,1)S(1)}, bf16[192,1024]{1,0:T(8,128)(2,1)S(1)}, u32[]{:S(2)}, u32[]{:S(2)}) %collective-permute-start.22) | collective-permute-done | bytes 393248 | tf_op jit(solution)/shard_map/ppermute | solution.py:115
  133.7 6.6 %collective-permute-done.24 = bf16[192,1024]{1,0:T(8,128)(2,1)S(1)} collective-permute-done((bf16[192,1024]{1,0:T(8,128)(2,1)S(1)}, bf16[192,1024]{1,0:T(8,128)(2,1)S(1)}, u32[]{:S(2)}, u32[]{:S(2)}) %collective-permute-start.24) | collective-permute-done | bytes 393248 | tf_op jit(solution)/shard_map/ppermute | solution.py:115
  140.3 2.9 %collective-permute-done.26 = bf16[192,1024]{1,0:T(8,128)(2,1)S(1)} collective-permute-done((bf16[192,1024]{1,0:T(8,128)(2,1)S(1)}, bf16[192,1024]{1,0:T(8,128)(2,1)S(1)}, u32[]{:S(2)}, u32[]{:S(2)}) %collective-permute-start.26) | collective-permute-done | bytes 393248 | tf_op jit(solution)/shard_map/ppermute | solution.py:115
  (83 shorter events, 40.0 us)
Async XLA Ops:
  4.5 21.4 %collective-permute-start = (bf16[400,1024]{1,0:T(8,128)(2,1)S(1)}, bf16[400,1024]{1,0:T(8,128)(2,1)}, u32[]{:S(2)}, u32[]{:S(2)}) collective-permute-start(bf16[400,1024]{1,0:T(8,128)(2,1)S(1)} %shard_map.91.refs_1_.facts_ref), channel_id=1, source_target_pairs={{0,4},{4,0},{8,12},{12,8},{1,5},{5,1},{9,13},{13,9},{2,6},{6,2},{1... | collective-permute-start | bytes 2457608 | tf_op jit(solution)/shard_map/ppermute | solution.py:115
  7.6 21.6 %collective-permute-start.3 = (bf16[400,1024]{1,0:T(8,128)(2,1)S(1)}, bf16[400,1024]{1,0:T(8,128)(2,1)}, u32[]{:S(2)}, u32[]{:S(2)}) collective-permute-start(bf16[400,1024]{1,0:T(8,128)(2,1)S(1)} %shard_map.91.refs_1_.facts_ref), channel_id=1, source_target_pairs={{4,8},{8,4},{5,9},{9,5},{6,10},{10,6},{7,11},{11,7},{20,24},{24,20... | collective-permute-start | bytes 2457608 | tf_op jit(solution)/shard_map/ppermute | solution.py:115
  9.2 21.3 %collective-permute-start.6 = (bf16[384,1024]{1,0:T(8,128)(2,1)}, bf16[384,1024]{1,0:T(8,128)(2,1)}, u32[]{:S(2)}, u32[]{:S(2)}) collective-permute-start(bf16[384,1024]{1,0:T(8,128)(2,1)} %refs_0_.1), channel_id=1, source_target_pairs={{0,2},{1,3},{2,0},{3,1},{4,6},{5,7},{6,4},{7,5},{8,10},{9,11},{10,... | collective-permute-start | bytes 2359304 | tf_op jit(solution)/shard_map/ppermute | solution.py:107
  15.6 39.8 %collective-permute-start.10 = (bf16[2048,512]{1,0:T(8,128)(2,1)}, bf16[2048,512]{1,0:T(8,128)(2,1)S(1)}, u32[]{:S(2)}, u32[]{:S(2)}) collective-permute-start(bf16[2048,512]{1,0:T(8,128)(2,1)} %shard_map.94), channel_id=1, source_target_pairs={{0,1},{1,0},{2,3},{3,2},{4,5},{5,4},{6,7},{7,6},{8,9},{9,8},{10,11... | collective-permute-start | bytes 6291464 | tf_op jit(solution)/shard_map/ppermute | solution.py:111
  26.0 14.2 %collective-permute-start.1 = (bf16[400,1024]{1,0:T(8,128)(2,1)}, bf16[400,1024]{1,0:T(8,128)(2,1)}, u32[]{:S(2)}, u32[]{:S(2)}) collective-permute-start(bf16[400,1024]{1,0:T(8,128)(2,1)} %collective-permute-done.refs_0_.facts_ref), channel_id=1, source_target_pairs={{4,8},{8,4},{5,9},{9,5},{6,10},{10,6},{7,11},{11,7},{20,24},{24,20... | collective-permute-start | bytes 2457608 | tf_op jit(solution)/shard_map/ppermute | solution.py:115
  27.5 19.7 %collective-permute-start.5 = (bf16[400,1024]{1,0:T(8,128)(2,1)}, bf16[400,1024]{1,0:T(8,128)(2,1)}, u32[]{:S(2)}, u32[]{:S(2)}) collective-permute-start(bf16[400,1024]{1,0:T(8,128)(2,1)} %collective-permute-done.refs_0_.facts_ref), channel_id=1, source_target_pairs={{0,2},{1,3},{2,0},{3,1},{4,6},{5,7},{6,4},{7,5},{8,10},{9,11},{10,... | collective-permute-start | bytes 2457608 | tf_op jit(solution)/shard_map/ppermute | solution.py:107
  29.2 23.5 %collective-permute-start.4 = (bf16[400,1024]{1,0:T(8,128)(2,1)}, bf16[400,1024]{1,0:T(8,128)(2,1)}, u32[]{:S(2)}, u32[]{:S(2)}) collective-permute-start(bf16[400,1024]{1,0:T(8,128)(2,1)} %collective-permute-done.3.refs_1_), channel_id=1, source_target_pairs={{4,0},{8,12},{5,1},{9,13},{6,2},{10,14},{7,3},{11,15},{20,16},{24,... | collective-permute-start | bytes 2457608 | tf_op jit(solution)/shard_map/ppermute | solution.py:115
  32.3 13.7 %collective-permute-start.7 = (bf16[192,1024]{1,0:T(8,128)(2,1)}, bf16[192,1024]{1,0:T(8,128)(2,1)S(1)}, u32[]{:S(2)}, u32[]{:S(2)}) collective-permute-start(bf16[192,1024]{1,0:T(8,128)(2,1)} %shard_map.92), channel_id=1, source_target_pairs={{0,4},{12,8},{1,5},{13,9},{2,6},{14,10},{3,7},{15,11},{16,20},{28,... | collective-permute-start | bytes 1179656 | tf_op jit(solution)/shard_map/ppermute | solution.py:115
  40.2 30.8 %collective-permute-start.2 = (bf16[400,1024]{1,0:T(8,128)(2,1)}, bf16[400,1024]{1,0:T(8,128)(2,1)S(1)}, u32[]{:S(2)}, u32[]{:S(2)}) collective-permute-start(bf16[400,1024]{1,0:T(8,128)(2,1)} %collective-permute-done.1.refs_4_.refs_1_), channel_id=1, source_target_pairs={{4,0},{8,12},{5,1},{9,13},{6,2},{10,14},{7,3},{11,15},{20,16},{24,... | collective-permute-start | bytes 2457608 | tf_op jit(solution)/shard_map/ppermute | solution.py:115
  55.3 15.7 %collective-permute-start.8 = (bf16[384,1024]{1,0:T(8,128)(2,1)S(1)}, bf16[384,1024]{1,0:T(8,128)(2,1)S(1)}, u32[]{:S(2)}, u32[]{:S(2)}) collective-permute-start(bf16[384,1024]{1,0:T(8,128)(2,1)S(1)} %get-tuple-element.34.refs_0_), channel_id=1, source_target_pairs={{0,2},{1,3},{2,0},{3,1},{4,6},{5,7},{6,4},{7,5},{8,10},{9,11},{10,... | collective-permute-start | bytes 2359304 | tf_op jit(solution)/shard_map/ppermute | solution.py:107
  58.9 22.1 %collective-permute-start.14 = (bf16[384,1024]{1,0:T(8,128)(2,1)S(1)}, bf16[384,1024]{1,0:T(8,128)(2,1)S(1)}, u32[]{:S(2)}, u32[]{:S(2)}) collective-permute-start(bf16[384,1024]{1,0:T(8,128)(2,1)S(1)} %get-tuple-element.43), channel_id=1, source_target_pairs={{0,1},{1,0},{2,3},{3,2},{4,5},{5,4},{6,7},{7,6},{8,9},{9,8},{10,11... | collective-permute-start | bytes 2359304 | tf_op jit(solution)/shard_map/ppermute | solution.py:111
  63.1 20.4 %collective-permute-start.13 = (bf16[384,1024]{1,0:T(8,128)(2,1)S(1)}, bf16[384,1024]{1,0:T(8,128)(2,1)S(1)}, u32[]{:S(2)}, u32[]{:S(2)}) collective-permute-start(bf16[384,1024]{1,0:T(8,128)(2,1)S(1)} %get-tuple-element.41), channel_id=1, source_target_pairs={{0,1},{1,0},{2,3},{3,2},{4,5},{5,4},{6,7},{7,6},{8,9},{9,8},{10,11... | collective-permute-start | bytes 2359304 | tf_op jit(solution)/shard_map/ppermute | solution.py:111
  63.6 22.0 %collective-permute-start.12 = (bf16[192,1024]{1,0:T(8,128)(2,1)S(1)}, bf16[192,1024]{1,0:T(8,128)(2,1)S(1)}, u32[]{:S(2)}, u32[]{:S(2)}) collective-permute-start(bf16[192,1024]{1,0:T(8,128)(2,1)S(1)} %collective-permute-done.9.refs_4_.refs_5_), channel_id=1, source_target_pairs={{4,0},{8,12},{5,1},{9,13},{6,2},{10,14},{7,3},{11,15},{20,16},{24,... | collective-permute-start | bytes 1179656 | tf_op jit(solution)/shard_map/ppermute | solution.py:115
  73.9 11.8 %collective-permute-start.11 = (bf16[192,1024]{1,0:T(8,128)(2,1)S(1)}, bf16[192,1024]{1,0:T(8,128)(2,1)S(1)}, u32[]{:S(2)}, u32[]{:S(2)}) collective-permute-start(bf16[192,1024]{1,0:T(8,128)(2,1)S(1)} %get-tuple-element.37.refs_0_), channel_id=1, source_target_pairs={{0,2},{1,3},{2,0},{3,1},{4,6},{5,7},{6,4},{7,5},{8,10},{9,11},{10,... | collective-permute-start | bytes 1179656 | tf_op jit(solution)/shard_map/ppermute | solution.py:107
  74.5 17.0 %collective-permute-start.17 = (bf16[256,2048]{1,0:T(8,128)(2,1)S(1)}, bf16[256,2048]{1,0:T(8,128)(2,1)S(1)}, u32[]{:S(2)}, u32[]{:S(2)}) collective-permute-start(bf16[256,2048]{1,0:T(8,128)(2,1)S(1)} %pad_maximum_fusion.refs_6_), channel_id=1, source_target_pairs={{0,1},{1,0},{2,3},{3,2},{4,5},{5,4},{6,7},{7,6},{8,9},{9,8},{10,11... | collective-permute-start | bytes 3145736 | tf_op jit(solution)/shard_map/ppermute | solution.py:111
  93.5 12.0 %collective-permute-start.18 = (bf16[192,1024]{1,0:T(8,128)(2,1)S(1)}, bf16[192,1024]{1,0:T(8,128)(2,1)S(1)}, u32[]{:S(2)}, u32[]{:S(2)}) collective-permute-start(bf16[192,1024]{1,0:T(8,128)(2,1)S(1)} %get-tuple-element.55), channel_id=1, source_target_pairs={{0,2},{1,3},{2,0},{3,1},{4,6},{5,7},{6,4},{7,5},{8,10},{9,11},{10,... | collective-permute-start | bytes 1179656 | tf_op jit(solution)/shard_map/ppermute | solution.py:107
  95.7 20.4 %collective-permute-start.21 = (bf16[192,1024]{1,0:T(8,128)(2,1)S(1)}, bf16[192,1024]{1,0:T(8,128)(2,1)S(1)}, u32[]{:S(2)}, u32[]{:S(2)}) collective-permute-start(bf16[192,1024]{1,0:T(8,128)(2,1)S(1)} %get-tuple-element.60), channel_id=1, source_target_pairs={{0,2},{1,3},{2,0},{3,1},{4,6},{5,7},{6,4},{7,5},{8,10},{9,11},{10,... | collective-permute-start | bytes 1179656 | tf_op jit(solution)/shard_map/ppermute | solution.py:107
  105.6 15.4 %collective-permute-start.20 = (bf16[192,1024]{1,0:T(8,128)(2,1)S(1)}, bf16[192,1024]{1,0:T(8,128)(2,1)S(1)}, u32[]{:S(2)}, u32[]{:S(2)}) collective-permute-start(bf16[192,1024]{1,0:T(8,128)(2,1)S(1)} %add_convert_fusion.3), channel_id=1, source_target_pairs={{4,8},{8,4},{5,9},{9,5},{6,10},{10,6},{7,11},{11,7},{20,24},{24,20... | collective-permute-start | bytes 1179656 | tf_op jit(solution)/shard_map/ppermute | solution.py:115
  106.3 17.7 %collective-permute-start.23 = (bf16[192,1024]{1,0:T(8,128)(2,1)S(1)}, bf16[192,1024]{1,0:T(8,128)(2,1)S(1)}, u32[]{:S(2)}, u32[]{:S(2)}) collective-permute-start(bf16[192,1024]{1,0:T(8,128)(2,1)S(1)} %add_convert_fusion.3), channel_id=1, source_target_pairs={{0,4},{12,8},{1,5},{13,9},{2,6},{14,10},{3,7},{15,11},{16,20},{28,... | collective-permute-start | bytes 1179656 | tf_op jit(solution)/shard_map/ppermute | solution.py:115
  115.9 12.1 %collective-permute-start.25 = (bf16[192,1024]{1,0:T(8,128)(2,1)S(1)}, bf16[192,1024]{1,0:T(8,128)(2,1)S(1)}, u32[]{:S(2)}, u32[]{:S(2)}) collective-permute-start(bf16[192,1024]{1,0:T(8,128)(2,1)S(1)} %get-tuple-element.62), channel_id=1, source_target_pairs={{0,2},{1,3},{2,0},{3,1},{4,6},{5,7},{6,4},{7,5},{8,10},{9,11},{10,... | collective-permute-start | bytes 1179656 | tf_op jit(solution)/shard_map/ppermute | solution.py:107
  116.1 16.4 %collective-permute-start.22 = (bf16[192,1024]{1,0:T(8,128)(2,1)S(1)}, bf16[192,1024]{1,0:T(8,128)(2,1)S(1)}, u32[]{:S(2)}, u32[]{:S(2)}) collective-permute-start(bf16[192,1024]{1,0:T(8,128)(2,1)S(1)} %add_convert_fusion.2.block_ref), channel_id=1, source_target_pairs={{0,8},{12,4},{1,9},{13,5},{2,10},{14,6},{3,11},{15,7},{16,24},{28,... | collective-permute-start | bytes 1179656 | tf_op jit(solution)/shard_map/ppermute | solution.py:115
  120.9 12.8 %collective-permute-start.19 = (bf16[192,1024]{1,0:T(8,128)(2,1)S(1)}, bf16[192,1024]{1,0:T(8,128)(2,1)S(1)}, u32[]{:S(2)}, u32[]{:S(2)}) collective-permute-start(bf16[192,1024]{1,0:T(8,128)(2,1)S(1)} %get-tuple-element.57), channel_id=1, source_target_pairs={{0,2},{1,3},{2,0},{3,1},{4,6},{5,7},{6,4},{7,5},{8,10},{9,11},{10,... | collective-permute-start | bytes 1179656 | tf_op jit(solution)/shard_map/ppermute | solution.py:107
  124.2 16.1 %collective-permute-start.24 = (bf16[192,1024]{1,0:T(8,128)(2,1)S(1)}, bf16[192,1024]{1,0:T(8,128)(2,1)S(1)}, u32[]{:S(2)}, u32[]{:S(2)}) collective-permute-start(bf16[192,1024]{1,0:T(8,128)(2,1)S(1)} %shard_map.107), channel_id=1, source_target_pairs={{4,12},{8,0},{5,13},{9,1},{6,14},{10,2},{7,15},{11,3},{20,28},{24,... | collective-permute-start | bytes 1179656 | tf_op jit(solution)/shard_map/ppermute | solution.py:115
  128.1 15.0 %collective-permute-start.26 = (bf16[192,1024]{1,0:T(8,128)(2,1)S(1)}, bf16[192,1024]{1,0:T(8,128)(2,1)S(1)}, u32[]{:S(2)}, u32[]{:S(2)}) collective-permute-start(bf16[192,1024]{1,0:T(8,128)(2,1)S(1)} %add_convert_fusion.1), channel_id=1, source_target_pairs={{0,4},{4,0},{8,12},{12,8},{1,5},{5,1},{9,13},{13,9},{2,6},{6,2},{1... | collective-permute-start | bytes 1179656 | tf_op jit(solution)/shard_map/ppermute | solution.py:115
  (15 other events, 94.0 us)

commit v9 on v8

--- a/solution.py
+++ b/solution.py
@@ -147,32 +147,38 @@
     ]
 
 
-def after(block, *others):
+def after(block, *others, flops=1024):
     return pl.pallas_call(
         lambda *refs: None,
         out_shape=jax.ShapeDtypeStruct(block.shape, block.dtype),
         in_specs=[ANYWHERE] * (1 + len(others)),
         out_specs=ANYWHERE,
         input_output_aliases={0: 0},
-        cost_estimate=cheap(),
+        cost_estimate=pl.CostEstimate(flops=flops, bytes_accessed=1024, transcendentals=0),
     )(block, *others)
 
 
-def moved(sources_of, shapes_out, operands, specs, flag=False, flops=1024):
-    kinds = sources_of if flag else [sources_of]
-    total = sum(pieces for _, _, _, pieces in kinds[0])
-
-    def body(*refs):
-        out_refs = refs[len(operands) : len(operands) + len(shapes_out)]
-        buffers = refs[len(operands) + len(shapes_out) : -2]
-        in_sems, out_sems = refs[-2:]
-
-        def run(sources):
-            first, inward, outward = 0, [], []
-            for (index, start, size, pieces), out, buffer in zip(sources, out_refs, buffers):
-                inward += copies(refs[index], start, buffer, size, pieces, in_sems, first)
-                outward += copies(buffer, 0, out, size, pieces, out_sems, first)
-                first += pieces
+def by_kind(plan_ref, kinds, run):
+    if kinds[0] is kinds[1]:
+        run(kinds[0])
+        return
+    for kind, value in zip(kinds, (1, 0)):
+
+        @pl.when(plan_ref[INNER_AT] == value)
+        def _(kind=kind):
+            run(kind)
+
+
+def part_of(plan, if_inner, if_outer, start, size, *others, flops=1024):
+    shape = jax.ShapeDtypeStruct((size, if_inner.shape[1]), if_inner.dtype)
+    pieces = 4
+
+    def body(plan_ref, inner_ref, outer_ref, *rest):
+        out_ref, buffer, in_sems, out_sems = rest[len(others) :]
+
+        def run(source):
+            inward = copies(source, start, buffer, size, pieces, in_sems, 0)
+            outward = copies(buffer, 0, out_ref, size, pieces, out_sems, 0)
             for copy in inward:
                 copy.start()
             for copy, next_copy in zip(inward, outward):
@@ -181,41 +187,18 @@
             for copy in outward:
                 copy.wait()
 
-        if flag:
-            for kind, sources in enumerate(kinds):
-
-                @pl.when(refs[0][INNER_AT] == kind)
-                def _(sources=sources):
-                    run(sources)
-
-        else:
-            run(kinds[0])
+        by_kind(plan_ref, (inner_ref, inner_ref if if_outer is if_inner else outer_ref), run)
 
     return pl.pallas_call(
         body,
-        out_shape=shapes_out,
-        in_specs=specs,
-        out_specs=[ANYWHERE] * len(shapes_out),
-        scratch_shapes=[pltpu.VMEM(shape.shape, shape.dtype) for shape in shapes_out]
-        + [pltpu.SemaphoreType.DMA((total,))] * 2,
+        out_shape=shape,
+        in_specs=[SMEM] + [ANYWHERE] * (2 + len(others)),
+        out_specs=ANYWHERE,
+        scratch_shapes=[pltpu.VMEM(shape.shape, shape.dtype)]
+        + [pltpu.SemaphoreType.DMA((pieces,))] * 2,
         compiler_params=pltpu.CompilerParams(vmem_limit_bytes=VMEM_LIMIT),
         cost_estimate=pl.CostEstimate(flops=flops, bytes_accessed=1024, transcendentals=0),
-    )(*operands)
-
-
-def lower_half(block):
-    rows = block.shape[0] // 2
-    shape = jax.ShapeDtypeStruct((rows, block.shape[1]), block.dtype)
-    return moved([(0, rows, rows, 4)], [shape], [block], [ANYWHERE], flops=8 * 2**30)[0]
-
-
-def chosen(plan, if_inner, if_outer, spans, *others):
-    shapes = [
-        jax.ShapeDtypeStruct((size, if_inner.shape[1]), if_inner.dtype) for _, size, _ in spans
-    ]
-    kinds = [[(index, *span) for span in spans] for index in (2, 1)]
-    operands = [plan, if_inner, if_outer, *others]
-    return moved(kinds, shapes, operands, [SMEM] + [ANYWHERE] * (len(operands) - 1), flag=True)
+    )(plan, if_inner, if_outer, *others)
 
 
 def with_facts(rows, gates, block_list, block_count, owner):
@@ -223,10 +206,19 @@
     blocks, _, offsets = block_list.shape
     total = owner.shape[0]
 
-    def body(rows_ref, gates_ref, list_ref, count_ref, owner_ref, out_ref, sems):
+    def body(rows_ref, gates_hbm, list_hbm, count_hbm, owner_hbm, out_ref, *scratch):
+        gates_ref, list_ref, count_ref, owner_ref, sems, small_sems = scratch
         moves = copies(rows_ref, 0, out_ref, count, 4, sems, 0)
-        for copy in moves:
+        small = [
+            pltpu.make_async_copy(source, target, small_sems.at[index])
+            for index, (source, target) in enumerate(
+                zip((gates_hbm, list_hbm, count_hbm, owner_hbm), scratch[:4])
+            )
+        ]
+        for copy in small + moves:
             copy.start()
+        for copy in small:
+            copy.wait()
         block_of = lax.broadcasted_iota(jnp.int32, (1, total), 1) // (total // blocks)
         facts = []
         for offset in range(offsets):
@@ -248,61 +240,65 @@
             copy.wait()
 
     shape = jax.ShapeDtypeStruct((count + FACT_ROWS, width), rows.dtype)
-    return on_core(
-        body, shape, [ANYWHERE, VMEM, SMEM, SMEM, VMEM], [pltpu.SemaphoreType.DMA((4,))]
-    )(rows, gates, block_list, block_count, owner)
-
-
-def partial_sums(
-    sizes, parts, weights, places, before=None, send=True, choice=None, waits=()
-):
+    scratch = [
+        pltpu.VMEM(gates.shape, gates.dtype),
+        pltpu.SMEM(block_list.shape, block_list.dtype),
+        pltpu.SMEM(block_count.shape, block_count.dtype),
+        pltpu.VMEM(owner.shape, owner.dtype),
+        pltpu.SemaphoreType.DMA((4,)),
+        pltpu.SemaphoreType.DMA((4,)),
+    ]
+    return on_core(body, shape, [ANYWHERE] * 5, scratch)(
+        rows, gates, block_list, block_count, owner
+    )
+
+
+def partial_sums(plan, sizes, parts, weights, places, before=None, send=True, waits=()):
     width, columns = weights[0].shape
     rows, count = sum(sizes), len(places)
-    blocks = [block for part in parts for block in part]
-    operands = blocks + [weights[place] for place in places] + [weights[2]]
-    specs = [ANYWHERE] * len(operands)
-    flag_at = len(operands)
-    if choice is not None:
-        operands += [choice[0], choice[1]]
-        specs += [SMEM, ANYWHERE]
-    before_at = len(operands)
+    pairs = [
+        block if isinstance(block, tuple) else (block, block) for part in parts for block in part
+    ]
+    sources = [array for pair in pairs for array in pair]
+    operands = [plan] + sources + [weights[place] for place in places] + [weights[2]]
     if before is not None:
         operands.append(before)
-        specs.append(VMEM)
-    operands += waits
-    specs += [VMEM] * len(waits)
-    row_pieces, weight_pieces = 2, 2
-    row_sems = len(blocks) * row_pieces
-
-    def body(*refs):
-        results = refs[len(operands) : -4]
-        row_buffer, weight_buffer, sems, weight_sems = refs[-4:]
-        row_moves, weight_moves = [], [[], []]
+    specs = [SMEM] + [ANYWHERE] * (len(operands) - 1) + [VMEM] * len(waits)
+    row_pieces, weight_pieces, before_pieces = 2, 4, 4
+    has_before = before is not None
+
+    def body(plan_ref, *refs):
+        source_refs = refs[: len(sources)]
+        weight_refs = refs[len(sources) : len(sources) + count + 1]
+        before_ref = refs[len(sources) + count + 1] if has_before else None
+        scratch = refs[len(operands) - 1 + len(waits) :]
+        results = scratch[: 3 if send else 2]
+        row_buffer, weight_buffer, row_sems, weight_sems = scratch[len(results) :][:4]
+        row_moves, weight_moves, before_moves = [], [[], []], []
+
+        def start(moves):
+            for copy in moves:
+                copy.start()
+
         for part, size in enumerate(sizes):
             for index in range(count):
                 block = part * count + index
                 target = row_buffer.at[index, pl.ds(sum(sizes[:part]), size)]
                 first = block * row_pieces
-                move = copies(refs[block], 0, target, size, row_pieces, sems, first)
-                if choice is not None and part == len(sizes) - 1:
-                    source = refs[flag_at + 1]
-                    other = copies(source, 0, target, size, row_pieces, sems, first)
-                    for kind, group in enumerate((move, other)):
-
-                        @pl.when(refs[flag_at][INNER_AT] == kind)
-                        def _(group=group):
-                            for copy in group:
-                                copy.start()
-
+                kinds = [
+                    copies(source_refs[2 * block], 0, target, size, row_pieces, row_sems, first)
+                ]
+                if pairs[block][0] is pairs[block][1]:
+                    kinds.append(kinds[0])
                 else:
-                    for copy in move:
-                        copy.start()
-                row_moves += move
+                    source = source_refs[2 * block + 1]
+                    kinds.append(copies(source, 0, target, size, row_pieces, row_sems, first))
+                by_kind(plan_ref, kinds, start)
+                row_moves += kinds[0]
         for side in range(2):
             for index, place in enumerate(places):
-                source = refs[len(blocks) + index] if side == 0 else refs[len(blocks) + count]
                 weight_moves[side] += copies(
-                    source,
+                    weight_refs[index if side == 0 else count],
                     0 if side == 0 else place * width,
                     weight_buffer.at[side, index],
                     width,
@@ -310,15 +306,20 @@
                     weight_sems,
                     (side * count + index) * weight_pieces,
                 )
-            for copy in weight_moves[side]:
-                copy.start()
-        for copy in row_moves:
+            start(weight_moves[side])
+        if has_before:
+            before_buffer, before_sems = scratch[-2:]
+            before_moves = copies(
+                before_ref, 0, before_buffer, rows, before_pieces, before_sems, 0
+            )
+            start(before_moves)
+        for copy in row_moves + before_moves:
             copy.wait()
         for side in range(2):
             for copy in weight_moves[side]:
                 copy.wait()
             at = slice(side * columns, (side + 1) * columns)
-            total = None if before is None else refs[before_at][:, at]
+            total = before_buffer[:, at] if has_before else None
             for index in range(count):
                 product = jnp.dot(
                     row_buffer[index],
@@ -337,10 +338,15 @@
     scratch = [
         pltpu.VMEM((count, rows, width), jnp.bfloat16),
         pltpu.VMEM((2, count, width, columns), jnp.bfloat16),
-        pltpu.SemaphoreType.DMA((row_sems,)),
+        pltpu.SemaphoreType.DMA((len(pairs) * row_pieces,)),
         pltpu.SemaphoreType.DMA((2 * count * weight_pieces,)),
     ]
-    return on_core(body, shapes + [TOKEN], specs, scratch)(*operands)
+    if has_before:
+        scratch += [
+            pltpu.VMEM((rows, 2 * columns), jnp.float32),
+            pltpu.SemaphoreType.DMA((before_pieces,)),
+        ]
+    return on_core(body, shapes + [TOKEN], specs, scratch)(*operands, *waits)
 
 
 def collected_rows(owned, slot, plan, sums, got, facts, before):
@@ -373,38 +379,47 @@
     return [pltpu.VMEM((FACT_ROWS, width), jnp.bfloat16), pltpu.SemaphoreType.DMA((1,))]
 
 
-def facts_of(facts_ref, buffer, sem):
-    last = facts_ref.shape[0] - FACT_ROWS
-    (copy,) = copies(facts_ref, last, buffer, FACT_ROWS, 1, sem, 0)
-    copy.start()
-    copy.wait()
+def facts_of(plan_ref, inner_ref, outer_ref, buffer, sem):
+    last = inner_ref.shape[0] - FACT_ROWS
+
+    def run(source):
+        (copy,) = copies(source, last, buffer, FACT_ROWS, 1, sem, 0)
+        copy.start()
+        copy.wait()
+
+    by_kind(plan_ref, (inner_ref, outer_ref), run)
     return buffer
 
 
 def collect(owned, slot, plan, sums, got, facts, before):
-    operands = [plan, sums, got, facts] + ([] if before is None else [before])
-
-    def body(plan_ref, sums_ref, got_ref, facts_ref, *rest):
+    operands = [plan, sums, got, *facts] + ([] if before is None else [before])
+
+    def body(plan_ref, sums_ref, got_ref, inner_ref, outer_ref, *rest):
         before_ref = rest[0] if before is not None else None
         out_ref, token_ref, buffer, sem = rest[-4:]
-        facts_here = facts_of(facts_ref, buffer, sem)
+        facts_here = facts_of(plan_ref, inner_ref, outer_ref, buffer, sem)
         rows = collected_rows(owned, slot, plan_ref, sums_ref, got_ref, facts_here, before_ref)
         for index in range(4):
             out_ref[index * owned : (index + 1) * owned, :] = rows[index]
         token_ref[...] = jnp.zeros(TOKEN.shape, TOKEN.dtype)
 
     shape = jax.ShapeDtypeStruct((4 * owned, sums.shape[1] // 2), jnp.float32)
-    specs = [SMEM, VMEM, VMEM, ANYWHERE] + [VMEM] * (len(operands) - 4)
-    return on_core(body, [shape, TOKEN], specs, fact_scratch(facts.shape[1]))(*operands)
-
-
-def added(block, other, wait):
-    def body(block_ref, other_ref, _, out_ref):
+    specs = [SMEM, VMEM, VMEM, ANYWHERE, ANYWHERE] + [VMEM] * (len(operands) - 5)
+    return on_core(body, [shape, TOKEN], specs, fact_scratch(facts[0].shape[1]))(*operands)
+
+
+def added(block, other, *waits, flops=1024):
+    def body(block_ref, other_ref, *rest):
         total = block_ref[...].astype(jnp.float32) + other_ref[...].astype(jnp.float32)
-        out_ref[...] = total.astype(out_ref.dtype)
-
-    shape = jax.ShapeDtypeStruct(block.shape, block.dtype)
-    return on_core(body, shape, [VMEM, VMEM, ANYWHERE])(block, other, wait)
+        rest[-1][...] = total.astype(jnp.bfloat16)
+
+    return pl.pallas_call(
+        body,
+        out_shape=jax.ShapeDtypeStruct(block.shape, jnp.bfloat16),
+        in_specs=[VMEM, VMEM] + [ANYWHERE] * len(waits),
+        out_specs=VMEM,
+        cost_estimate=pl.CostEstimate(flops=flops, bytes_accessed=1024, transcendentals=0),
+    )(block, other, *waits)
 
 
 def down(held, own_ref, lent_ref, sent_ref, kept_ref):
@@ -423,35 +438,26 @@
         jax.ShapeDtypeStruct((owned, width), jnp.float32),
     ]
 
-    def first(plan_ref, sums_ref, got_ref, facts_ref, before_ref, own_ref, lent_ref, *out_refs):
-        facts_here = facts_of(facts_ref, *out_refs[3:])
+    def first(plan_ref, sums_ref, got_ref, inner_ref, outer_ref, before_ref, *refs):
+        own_ref, lent_ref, sent_ref, kept_ref, held_ref, buffer, sem = refs
+        facts_here = facts_of(plan_ref, inner_ref, outer_ref, buffer, sem)
         rows = collected_rows(owned, slot, plan_ref, sums_ref, got_ref, facts_here, before_ref)
-        down(rows[0].astype(jnp.bfloat16), own_ref, lent_ref, out_refs[0], out_refs[1])
+        down(rows[0].astype(jnp.bfloat16), own_ref, lent_ref, sent_ref, kept_ref)
         for index in range(1, 4):
-            out_refs[2][(index - 1) * owned : index * owned, :] = rows[index].astype(jnp.bfloat16)
-
-    def others(indices, waits):
-        def body(held_ref, own_ref, lent_ref, *refs):
-            out_refs = refs[len(waits) :]
-            for place, index in enumerate(indices):
-                held = held_ref[(index - 1) * owned : index * owned, :]
-                down(held, own_ref, lent_ref, out_refs[2 * place], out_refs[2 * place + 1])
-
-        specs = [VMEM] * 3 + [ANYWHERE] * len(waits)
-        return on_core(body, pair * len(indices), specs)(held, down_own, down_lent, *waits)
-
-    def joined(sent, kept):
-        return kept + across_chips(sent).astype(jnp.float32)
+            held_ref[(index - 1) * owned : index * owned, :] = rows[index].astype(jnp.bfloat16)
+
+    def others(held_ref, own_ref, lent_ref, *refs):
+        for index in range(3):
+            held = held_ref[index * owned : (index + 1) * owned, :]
+            down(held, own_ref, lent_ref, refs[2 * index], refs[2 * index + 1])
 
     held_shape = jax.ShapeDtypeStruct((3 * owned, 2 * units), jnp.bfloat16)
-    specs = [SMEM, VMEM, VMEM, ANYWHERE] + [VMEM] * 3
-    sent, kept, held = on_core(first, pair + [held_shape], specs, fact_scratch(facts.shape[1]))(
-        plan, sums, got, facts, before, down_own, down_lent
-    )
-    got_first = across_chips(sent)
-    chunks = [kept + got_first.astype(jnp.float32), joined(*others([1], []))]
-    rest = others([2, 3], [got_first])
-    return chunks + [joined(rest[0], rest[1]), joined(rest[2], rest[3])]
+    specs = [SMEM, VMEM, VMEM, ANYWHERE, ANYWHERE] + [VMEM] * 3
+    sent, kept, held = on_core(
+        first, pair + [held_shape], specs, fact_scratch(facts[0].shape[1])
+    )(plan, sums, got, *facts, before, down_own, down_lent)
+    rest = on_core(others, pair * 3, [VMEM] * 3)(held, down_own, down_lent)
+    return [sent, *rest[0::2]], [kept, *rest[1::2]]
 
 
 def rows_travel(
@@ -489,24 +495,29 @@
     lend_down = jnp.concatenate([down_part(1), down_part(3)], axis=1)
 
 
+    def at_kind(block, positions):
+        pairs = [(4 * p + i, 4 * p + (i ^ 2)) for p in positions for i in range(4)]
+        return lax.ppermute(block, ("blk", "tp"), pairs)
+
+    beside = after(beside, middle)
     inner_last = along(beside, MIDDLE)
-    outer_next = along(middle, OUTWARD)
+    outer_next = after(along(middle, OUTWARD), flops=3 * 2**30)
     beside_far = across_chips(beside)
-    own_far_half = lower_half(own_far)
+    own_far_half = part_of(plan, own_far, own_far, half, half, flops=6 * 2**30)
     inward_far = along(own_far_half, INWARD)
     lend = jnp.concatenate([quarter(1), quarter(3)])
     lent = across_cores(after(lend, own))
     weights = [quarter(0), quarter(2), lent]
-    sums_0, send_0, ready_0 = partial_sums([row_count], [(tokens, own_far)], weights, (0, 1))
+    whole = [row_count]
+    sums_0, send_0, ready_0 = partial_sums(
+        plan, whole, [(tokens, own_far)], weights, (0, 1)
+    )
     got_0 = across_cores(send_0)
     lent_down = across_cores(lend_down)
 
     outer_last = along(inner_last, OUTWARD)
-    (second, second_facts) = chosen(
-        plan,
-        middle,
+    outer_next = after(
         outer_next,
-        [(0, row_count, 4), (row_count, FACT_ROWS, 1)],
         beside_far,
         inner_last,
         inward_far,
@@ -514,52 +525,47 @@
         weights[0],
         weights[1],
     )
-    second_far = across_chips(second)
+    second = (middle, outer_next)
+    second_far = (at_kind(middle, (1, 2)), at_kind(outer_next, (0, 3)))
     middle_far = along(inward_far, MIDDLE)
-    sums_1, send_1, ready_1 = partial_sums([row_count], [(beside, beside_far)], weights, (0, 1))
+    sums_1, send_1, ready_1 = partial_sums(
+        plan, whole, [(beside, beside_far)], weights, (0, 1)
+    )
     got_1 = across_cores(send_1)
 
-    total, _ = collect(owned, 0, plan, sums_0, got_0, own, None)
-
-    last_a, last_b, last_facts = chosen(
+    last = (inner_last, outer_last)
+    last_far_a = across_chips(
+        part_of(plan, *last, 0, half, *second_far, middle_far, ready_0, ready_1)
+    )
+    outward_far = along(middle_far, OUTWARD)
+    total, _ = collect(owned, 0, plan, sums_0, got_0, (own, own), None)
+    total, collected_1 = collect(owned, 1, plan, sums_1, got_1, (beside, beside), total)
+    sums_2, send_2, _ = partial_sums(plan, whole, [(second, second_far)], weights, (0, 1))
+    got_2 = across_cores(send_2)
+    near, _ = partial_sums(plan, whole, [(last,)], weights, (0,), send=False)
+    sums_3, send_3, _ = partial_sums(
         plan,
-        inner_last,
-        outer_last,
-        [(0, half, 4), (half, half, 4), (row_count, FACT_ROWS, 1)],
-        second_far,
-        middle_far,
-        ready_0,
-        ready_1,
-    )
-    last_far_a = across_chips(last_a)
-    outward_far = along(middle_far, OUTWARD)
-    total, collected_1 = collect(owned, 1, plan, sums_1, got_1, beside, total)
-    sums_2, send_2, ready_2 = partial_sums([row_count], [(second, second_far)], weights, (0, 1))
-    got_2 = across_cores(send_2)
-    near = partial_sums([half, half], [(last_a,), (last_b,)], weights, (0,), send=False)[0]
-    sums_3, send_3, _ = partial_sums(
         [half, half],
-        [(last_far_a,), (outward_far,)],
+        [(last_far_a,), ((middle_far, outward_far),)],
         weights,
         (1,),
         before=near,
-        choice=(plan, middle_far),
         waits=[collected_1],
     )
     got_3 = across_cores(send_3)
-    total, _ = collect(owned, 2, plan, sums_2, got_2, second_facts, total)
-    chunks = finish(
-        owned, 3, plan, sums_3, got_3, last_facts, total, kept_down, lent_down
-    )
-
-    first, second, third = [chunk.astype(jnp.bfloat16) for chunk in chunks[:3]]
+    total, _ = collect(owned, 2, plan, sums_2, got_2, second, total)
+    sent, kept = finish(owned, 3, plan, sums_3, got_3, last, total, kept_down, lent_down)
+
+    far = [across_chips(block) for block in sent]
+    first = added(kept[0], far[0])
     middle = along(first, MIDDLE)
     inward = along(first, INWARD)
+    second = added(kept[1], far[1], flops=4 * 2**30)
     two_in = along(second, TWO_IN)
     two_out = along(added(second, inward, middle), TWO_OUT)
-    beside = along(third, BESIDE)
-    arrived = [block.astype(jnp.float32) for block in (middle, two_in, two_out, beside)]
-    return (chunks[3] + sum(arrived)).astype(jnp.bfloat16)
+    beside = along(added(kept[2], far[2], flops=4 * 2**30), BESIDE)
+    arrived = [block.astype(jnp.float32) for block in (far[3], middle, two_in, two_out, beside)]
+    return (kept[3] + sum(arrived)).astype(jnp.bfloat16)
 
 
 def on_device(*args):

time: 145 us -> 155 us (1.069)
  waiting for transfers between devices: 53.5 us -> 35.3 us
  starting transfers between devices: 40 us -> 49.8 us
  local copies, waits for them, and re-layouts: 8.2 us -> 16.6 us
  Pallas kernels: 35.4 us -> 43.7 us
    ppermute x8 -> x7, waiting for transfers between devices: 20.5 us -> 5.76 us  [across_chips(): return lax.ppermute(block, 'tp', [(i, i ^ 2) for i in range(4)])]
    unnamed x24 -> x46, local copies, waits for them, and re-layouts: 2.74 us -> 11.2 us
    pallas_call x16 -> x17, Pallas kernels: 35.4 us -> 43.7 us  [the longest x5 20 us: partial_sums(): return on_core(body, shapes + [TOKEN], specs, scratch)(*operands, *waits)]
    ppermute x13, waiting for transfers between devices: 32.8 us -> 26.8 us  [along(): return lax.ppermute(block, 'blk', route)]
    ppermute x0 -> x2, starting transfers between devices: none -> 3.97 us  [at_kind(): return lax.ppermute(block, ('blk', 'tp'), pairs)]
    ppermute x13, starting transfers between devices: 32.6 us -> 36.3 us  [along(): return lax.ppermute(block, 'blk', route)]
    ppermute x0 -> x2, waiting for transfers between devices: none -> 2.81 us  [at_kind(): return lax.ppermute(block, ('blk', 'tp'), pairs)]
    ppermute x8 -> x7, starting transfers between devices: 6.19 us -> 8.24 us  [across_chips(): return lax.ppermute(block, 'tp', [(i, i ^ 2) for i in range(4)])]
  transfers between devices with their start and end apart: 27 -> 28, of which waited for: 13 -> 8; matrix products, arithmetic and copies ran while one was open for 8% -> 7% of each run, Pallas kernels for 22% -> 27%
where the time goes in v9:
time: 155 us; the launch traced here: 154 us
  starting transfers between devices  49.8 us (32%)
  Pallas kernels  43.7 us (28%)
  waiting for transfers between devices  35.3 us (23%)
  local copies, waits for them, and re-layouts  16.6 us (11%)
  other arithmetic  8.11 us (5%)
    ppermute x13, starting transfers between devices, along(): return lax.ppermute(block, 'blk', route)  36.3 us
    ppermute x13, waiting for transfers between devices, along(): return lax.ppermute(block, 'blk', route)  26.8 us
    pallas_call x5, Pallas kernels, partial_sums(): return on_core(body, shapes + [TOKEN], specs, scratch)(*operands, *waits)  20 us
    unnamed x46, local copies, waits for them, and re-layouts  11.2 us
    ppermute x7, starting transfers between devices, across_chips(): return lax.ppermute(block, 'tp', [(i, i ^ 2) for i in range(4)])  8.24 us
    pallas_call x4, Pallas kernels, added(): pl.pallas_call(body, out_shape=jax.ShapeDtypeStruct(block.shape, jnp.bflo...  8.1 us
    pallas_call x3, Pallas kernels, collect(): on_core(body, [shape, TOKEN], specs, fact_scratch(facts[0].shape[1]))  6.67 us
    ppermute x7, waiting for transfers between devices, across_chips(): return lax.ppermute(block, 'tp', [(i, i ^ 2) for i in range(4)])  5.76 us
  transfers between devices with their start and end apart: 28, of which 8 were waited for; matrix products, arithmetic and copies ran while one was open for 7% of the time, Pallas kernels for 27%

profile of v9, /device:TPU:0, one launch (start us, length us, event | category | flops | bytes accessed | tf_op | source)
XLA Modules:
  0.0 154.0 jit_solution(7942438572341458622)
XLA Ops:
  0.0 2.9 %collective-permute-start.7 = (bf16[384,1024]{1,0:T(8,128)(2,1)}, bf16[384,1024]{1,0:T(8,128)(2,1)}, u32[]{:S(2)}, u32[]{:S(2)}) collective-permute-start(bf16[384,1024]{1,0:T(8,128)(2,1)} %refs_1_.1), channel_id=1, source_target_pairs={{0,2},{1,3},{2,0},{3,1},{4,6},{5,7},{6,4},{7,5},{8,10},{9,11},{10,... | collective-permute-start | bytes 2359304 | tf_op jit(solution)/shard_map/ppermute | solution.py:107
  10.4 3.6 %collective-permute-start = (bf16[400,1024]{1,0:T(8,128)(2,1)}, bf16[400,1024]{1,0:T(8,128)(2,1)S(1)}, u32[]{:S(2)}, u32[]{:S(2)}) collective-permute-start(bf16[400,1024]{1,0:T(8,128)(2,1)} %shard_map.91.refs_1_.inner_ref.outer_ref), channel_id=1, source_target_pairs={{0,4},{4,0},{8,12},{12,8},{1,5},{5,1},{9,13},{13,9},{2,6},{6,2},{1... | collective-permute-start | bytes 2457608 | tf_op jit(solution)/shard_map/ppermute | solution.py:115
  14.0 3.4 %dynamic-slice_bitcast_fusion.4 = (bf16[1024,256]{1,0:T(8,128)(2,1)S(1)}, bf16[1024,256]{1,0:T(8,128)(2,1)S(1)}, bf16[1024,256]{1,0:T(8,128)(2,1)}, bf16[1024,25...) fusion(bf16[4,1024,256]{2,1,0:T(8,128)(2,1)} %bitcast.32, ...), kind=kLoop, calls=%fused_computation.10 | loop fusion | bytes 8388624 | tf_op jit(solution)/shard_map/jit(dynamic_index_in_dim)/squeeze | solution.py:486
  19.0 2.3 %pad_maximum_fusion.1.refs_5_.refs_4_.refs_2_ = bf16[1024,512]{1,0:T(8,128)(2,1)} fusion(bf16[1024,256]{1,0:T(8,128)(2,1)S(1)} %get-tuple-element.64, bf16[1024,256]{1,0:T(8,128)(2,1)} %get-tuple-element.65), kind=kLoop, calls=%fused_computation.2 | loop fusion | flops 2097152 | bytes 2097152 | tf_op jit(solution)/shard_map/concatenate | solution.py:489
  25.5 6.4 %collective-permute-done.refs_0_ = bf16[400,1024]{1,0:T(8,128)(2,1)S(1)} collective-permute-done((bf16[400,1024]{1,0:T(8,128)(2,1)}, bf16[400,1024]{1,0:T(8,128)(2,1)S(1)}, u32[]{:S(2)}, u32[]{:S(2)}) %collective-permute-start) | collective-permute-done | bytes 819232 | tf_op jit(solution)/shard_map/ppermute | solution.py:115
  37.1 7.9 %collective-permute-start.8 = (bf16[192,1024]{1,0:T(8,128)(2,1)S(1)}, bf16[192,1024]{1,0:T(8,128)(2,1)}, u32[]{:S(2)}, u32[]{:S(2)}) collective-permute-start(bf16[192,1024]{1,0:T(8,128)(2,1)S(1)} %shard_map.94), channel_id=1, source_target_pairs={{0,4},{12,8},{1,5},{13,9},{2,6},{14,10},{3,7},{15,11},{16,20},{28,... | collective-permute-start | bytes 1179656 | tf_op jit(solution)/shard_map/ppermute | solution.py:115
  46.1 4.9 %collective-permute-done.5.refs_0_ = bf16[400,1024]{1,0:T(8,128)(2,1)} collective-permute-done((bf16[400,1024]{1,0:T(8,128)(2,1)}, bf16[400,1024]{1,0:T(8,128)(2,1)}, u32[]{:S(2)}, u32[]{:S(2)}) %collective-permute-start.5) | collective-permute-done | bytes 819232 | tf_op jit(solution)/shard_map/ppermute | solution.py:115
  53.7 2.4 %collective-permute-start.9 = (bf16[400,1024]{1,0:T(8,128)(2,1)}, bf16[400,1024]{1,0:T(8,128)(2,1)S(1)}, u32[]{:S(2)}, u32[]{:S(2)}) collective-permute-start(bf16[400,1024]{1,0:T(8,128)(2,1)} %shard_map.95.refs_1_.outer_ref), channel_id=1, source_target_pairs={{0,2},{1,3},{2,0},{3,1},{12,14},{13,15},{14,12},{15,13},{16,18},{1... | collective-permute-start | bytes 2457608 | tf_op jit(solution)/shard_map/ppermute | solution.py:500
  60.5 4.2 %shard_map.97 = (f32[384,1024]{1,0:T(8,128)S(1)}, bf16[384,1024]{1,0:T(8,128)(2,1)S(1)}, f32[8,128]{1,0:T(8,128)S(1)}) custom-call(s32[9]{0:T(128)S(1)} %fusion.plan_ref, bf16[384,1024]{1,0:T(8,128)(2,1)S(1)} %copy-done.6, bf16[384,1024]{1,0:T(8,128)(2,1)S(1)} %copy-done.6, bf16[384,1024]{1,0:T(8,128)(2,1)} %collective-permute-done.7.inner_ref.outer_ref.refs_2_.refs_3_, ...), custom_call_target="tpu_custom_call" | custom-call | flops 1024 | bytes 1024 | tf_op jit(solution)/shard_map/pallas_call | solution.py:349
  64.8 4.2 %shard_map.98 = (f32[384,1024]{1,0:T(8,128)S(1)}, bf16[384,1024]{1,0:T(8,128)(2,1)S(1)}, f32[8,128]{1,0:T(8,128)S(1)}) custom-call(s32[9]{0:T(128)S(1)} %fusion.plan_ref, bf16[400,1024]{1,0:T(8,128)(2,1)S(1)} %copy-done.4, bf16[400,1024]{1,0:T(8,128)(2,1)S(1)} %copy-done.4, bf16[400,1024]{1,0:T(8,128)(2,1)} %collective-permute-done.6.refs_1_.refs_2_.refs_3_, ...), custom_call_target="tpu_custom_call" | custom-call | flops 1024 | bytes 1024 | tf_op jit(solution)/shard_map/pallas_call | solution.py:349
  70.8 2.8 %collective-permute-done.9.rest_1_.refs_3_ = bf16[400,1024]{1,0:T(8,128)(2,1)S(1)} collective-permute-done((bf16[400,1024]{1,0:T(8,128)(2,1)}, bf16[400,1024]{1,0:T(8,128)(2,1)S(1)}, u32[]{:S(2)}, u32[]{:S(2)}) %collective-permute-start.9) | collective-permute-done | bytes 819232 | tf_op jit(solution)/shard_map/ppermute | solution.py:500
  73.6 3.1 %collective-permute-done.3.outer_ref.refs_1_ = bf16[400,1024]{1,0:T(8,128)(2,1)S(1)} collective-permute-done((bf16[400,1024]{1,0:T(8,128)(2,1)}, bf16[400,1024]{1,0:T(8,128)(2,1)S(1)}, u32[]{:S(2)}, u32[]{:S(2)}) %collective-permute-start.3) | collective-permute-done | bytes 819232 | tf_op jit(solution)/shard_map/ppermute | solution.py:115
  79.0 4.3 %shard_map.104 = (f32[384,1024]{1,0:T(8,128)S(1)}, bf16[384,1024]{1,0:T(8,128)(2,1)S(1)}, f32[8,128]{1,0:T(8,128)}) custom-call(s32[9]{0:T(128)S(1)} %fusion.plan_ref, bf16[400,1024]{1,0:T(8,128)(2,1)} %collective-permute-done.1.refs_1_.refs_0_.inner_ref, bf16[400,1024]{1,0:T(8,128)(2,1)} %shard_map.95.refs_1_.outer_ref, ...), custom_call_target="tpu_custom_call" | custom-call | flops 1024 | bytes 1024 | tf_op jit(solution)/shard_map/pallas_call | solution.py:349
  83.4 2.8 %shard_map.100 = (f32[384,1024]{1,0:T(8,128)S(1)}, f32[8,128]{1,0:T(8,128)}) custom-call(s32[9]{0:T(128)S(1)} %fusion.plan_ref, bf16[400,1024]{1,0:T(8,128)(2,1)} %collective-permute-done.2.refs_2_.inner_ref.refs_0_, bf16[400,1024]{1,0:T(8,128)(2,1)S(1)} %collective-permute-done.3.outer_ref.refs_1_, bf16[1024,512]{1,0:T(8,128)(2,1)S(1)} %copy-done, ...), custom_call_target="tpu_custom_call" | custom-call | flops 1024 | bytes 1024 | tf_op jit(solution)/shard_map/pallas_call | solution.py:349
  86.8 2.6 %shard_map.101 = (f32[768,512]{1,0:T(8,128)S(1)}, f32[8,128]{1,0:T(8,128)}) custom-call(s32[9]{0:T(128)S(1)} %fusion.plan_ref, f32[384,1024]{1,0:T(8,128)S(1)} %get-tuple-element.34.sums_ref, bf16[384,1024]{1,0:T(8,128)(2,1)S(1)} %collective-permute-done.15.got_ref, bf16[400,1024]{1,0:T(8,128)(2,1)} %shard_map.91.refs_1_.inner_ref.outer_ref, ...), custom_call_target="tpu_custom_call" | custom-call | flops 1024 | bytes 1024 | tf_op jit(solution)/shard_map/pallas_call | solution.py:408
  90.8 4.5 %shard_map.103 = (f32[384,1024]{1,0:T(8,128)S(1)}, bf16[384,1024]{1,0:T(8,128)(2,1)S(1)}, f32[8,128]{1,0:T(8,128)}) custom-call(s32[9]{0:T(128)S(1)} %fusion.plan_ref, bf16[192,1024]{1,0:T(8,128)(2,1)S(1)} %collective-permute-done.12.refs_0_.refs_1_, bf16[192,1024]{1,0:T(8,128)(2,1)S(1)} %collective-permute-done.12.refs_0_.refs_1_, ...), custom_call_target="tpu_custom_call" | custom-call | flops 1024 | bytes 1024 | tf_op jit(solution)/shard_map/pallas_call | solution.py:349
  95.5 2.6 %shard_map.105 = (f32[768,512]{1,0:T(8,128)S(1)}, f32[8,128]{1,0:T(8,128)}) custom-call(s32[9]{0:T(128)S(1)} %fusion.plan_ref, f32[384,1024]{1,0:T(8,128)S(1)} %get-tuple-element.40.sums_ref, bf16[384,1024]{1,0:T(8,128)(2,1)S(1)} %collective-permute-done.17.got_ref, bf16[400,1024]{1,0:T(8,128)(2,1)} %collective-permute-done.1.refs_1_.refs_0_.inner_ref, ...), custom_call_target="tpu_custom_call" | custom-call | flops 1024 | bytes 1024 | tf_op jit(solution)/shard_map/pallas_call | solution.py:408
  107.4 4.6 %collective-permute-done.20.other_ref = bf16[192,1024]{1,0:T(8,128)(2,1)S(1)} collective-permute-done((bf16[192,1024]{1,0:T(8,128)(2,1)S(1)}, bf16[192,1024]{1,0:T(8,128)(2,1)S(1)}, u32[]{:S(2)}, u32[]{:S(2)}) %collective-permute-start.20) | collective-permute-done | bytes 393248 | tf_op jit(solution)/shard_map/ppermute | solution.py:107
  115.5 8.4 %collective-permute-start.24 = (bf16[192,1024]{1,0:T(8,128)(2,1)}, bf16[192,1024]{1,0:T(8,128)(2,1)S(1)}, u32[]{:S(2)}, u32[]{:S(2)}) collective-permute-start(bf16[192,1024]{1,0:T(8,128)(2,1)} %shard_map.108), channel_id=1, source_target_pairs={{0,4},{12,8},{1,5},{13,9},{2,6},{14,10},{3,7},{15,11},{16,20},{28,... | collective-permute-start | bytes 1179656 | tf_op jit(solution)/shard_map/ppermute | solution.py:115
  125.9 3.2 %collective-permute-start.23 = (bf16[192,1024]{1,0:T(8,128)(2,1)}, bf16[192,1024]{1,0:T(8,128)(2,1)S(1)}, u32[]{:S(2)}, u32[]{:S(2)}) collective-permute-start(bf16[192,1024]{1,0:T(8,128)(2,1)} %shard_map.109.block_ref), channel_id=1, source_target_pairs={{0,8},{12,4},{1,9},{13,5},{2,10},{14,6},{3,11},{15,7},{16,24},{28,... | collective-permute-start | bytes 1179656 | tf_op jit(solution)/shard_map/ppermute | solution.py:115
  131.2 3.4 %collective-permute-start.27 = (bf16[192,1024]{1,0:T(8,128)(2,1)}, bf16[192,1024]{1,0:T(8,128)(2,1)S(1)}, u32[]{:S(2)}, u32[]{:S(2)}) collective-permute-start(bf16[192,1024]{1,0:T(8,128)(2,1)} %shard_map.111), channel_id=1, source_target_pairs={{0,4},{4,0},{8,12},{12,8},{1,5},{5,1},{9,13},{13,9},{2,6},{6,2},{1... | collective-permute-start | bytes 1179656 | tf_op jit(solution)/shard_map/ppermute | solution.py:115
  139.5 2.7 %collective-permute-done.23 = bf16[192,1024]{1,0:T(8,128)(2,1)S(1)} collective-permute-done((bf16[192,1024]{1,0:T(8,128)(2,1)}, bf16[192,1024]{1,0:T(8,128)(2,1)S(1)}, u32[]{:S(2)}, u32[]{:S(2)}) %collective-permute-start.23) | collective-permute-done | bytes 393248 | tf_op jit(solution)/shard_map/ppermute | solution.py:115
  142.1 9.7 %collective-permute-done.27 = bf16[192,1024]{1,0:T(8,128)(2,1)S(1)} collective-permute-done((bf16[192,1024]{1,0:T(8,128)(2,1)}, bf16[192,1024]{1,0:T(8,128)(2,1)S(1)}, u32[]{:S(2)}, u32[]{:S(2)}) %collective-permute-start.27) | collective-permute-done | bytes 393248 | tf_op jit(solution)/shard_map/ppermute | solution.py:115
  151.9 2.1 %add_convert_fusion = bf16[192,1024]{1,0:T(8,128)(2,1)} fusion(f32[192,1024]{1,0:T(8,128)S(1)} %get-tuple-element.45, bf16[192,1024]{1,0:T(8,128)(2,1)S(1)} %collective-permute-done.27, bf16[192,1024]{1,0:T(8,128)(2,1)S(1)} %collective-permute-done.25, bf16[192,1024]{1,0:T(8,128)(2,1)S(1)} %collective-permute-done.23, bf16[192,1024]{1,0:T(8,128)(2,1)} %copy-done.20, ...), kind=kLoop, calls=%fused_computation.5 | loop fusion | flops 2162688 | bytes 3145728 | tf_op jit(solution)/shard_map/convert_element_type | solution.py:568
  (108 shorter events, 54.5 us)
Async XLA Ops:
  0.0 35.1 %collective-permute-start.7 = (bf16[384,1024]{1,0:T(8,128)(2,1)}, bf16[384,1024]{1,0:T(8,128)(2,1)}, u32[]{:S(2)}, u32[]{:S(2)}) collective-permute-start(bf16[384,1024]{1,0:T(8,128)(2,1)} %refs_1_.1), channel_id=1, source_target_pairs={{0,2},{1,3},{2,0},{3,1},{4,6},{5,7},{6,4},{7,5},{8,10},{9,11},{10,... | collective-permute-start | bytes 2359304 | tf_op jit(solution)/shard_map/ppermute | solution.py:107
  8.9 14.7 %collective-permute-start.1 = (bf16[400,1024]{1,0:T(8,128)(2,1)}, bf16[400,1024]{1,0:T(8,128)(2,1)}, u32[]{:S(2)}, u32[]{:S(2)}) collective-permute-start(bf16[400,1024]{1,0:T(8,128)(2,1)} %shard_map.91.refs_1_.inner_ref.outer_ref), channel_id=1, source_target_pairs={{4,8},{8,4},{5,9},{9,5},{6,10},{10,6},{7,11},{11,7},{20,24},{24,20... | collective-permute-start | bytes 2457608 | tf_op jit(solution)/shard_map/ppermute | solution.py:115
  10.4 21.5 %collective-permute-start = (bf16[400,1024]{1,0:T(8,128)(2,1)}, bf16[400,1024]{1,0:T(8,128)(2,1)S(1)}, u32[]{:S(2)}, u32[]{:S(2)}) collective-permute-start(bf16[400,1024]{1,0:T(8,128)(2,1)} %shard_map.91.refs_1_.inner_ref.outer_ref), channel_id=1, source_target_pairs={{0,4},{4,0},{8,12},{12,8},{1,5},{5,1},{9,13},{13,9},{2,6},{6,2},{1... | collective-permute-start | bytes 2457608 | tf_op jit(solution)/shard_map/ppermute | solution.py:115
  19.0 39.2 %collective-permute-start.11 = (bf16[2048,512]{1,0:T(8,128)(2,1)}, bf16[2048,512]{1,0:T(8,128)(2,1)S(1)}, u32[]{:S(2)}, u32[]{:S(2)}) collective-permute-start(bf16[2048,512]{1,0:T(8,128)(2,1)} %shard_map.96), channel_id=1, source_target_pairs={{0,1},{1,0},{2,3},{3,2},{4,5},{5,4},{6,7},{7,6},{8,9},{9,8},{10,11... | collective-permute-start | bytes 6291464 | tf_op jit(solution)/shard_map/ppermute | solution.py:111
  23.6 27.4 %collective-permute-start.5 = (bf16[400,1024]{1,0:T(8,128)(2,1)}, bf16[400,1024]{1,0:T(8,128)(2,1)}, u32[]{:S(2)}, u32[]{:S(2)}) collective-permute-start(bf16[400,1024]{1,0:T(8,128)(2,1)} %collective-permute-done.1.refs_1_.refs_0_.inner_ref), channel_id=1, source_target_pairs={{4,0},{8,12},{5,1},{9,13},{6,2},{10,14},{7,3},{11,15},{20,16},{24,... | collective-permute-start | bytes 2457608 | tf_op jit(solution)/shard_map/ppermute | solution.py:115
  32.8 19.8 %collective-permute-start.2 = (bf16[400,1024]{1,0:T(8,128)(2,1)}, bf16[400,1024]{1,0:T(8,128)(2,1)}, u32[]{:S(2)}, u32[]{:S(2)}) collective-permute-start(bf16[400,1024]{1,0:T(8,128)(2,1)} %shard_map.92.refs_0_.refs_1_.inner_ref.outer_ref), channel_id=1, source_target_pairs={{4,8},{8,4},{5,9},{9,5},{6,10},{10,6},{7,11},{11,7},{20,24},{24,20... | collective-permute-start | bytes 2457608 | tf_op jit(solution)/shard_map/ppermute | solution.py:115
  34.6 19.1 %collective-permute-start.6 = (bf16[400,1024]{1,0:T(8,128)(2,1)}, bf16[400,1024]{1,0:T(8,128)(2,1)}, u32[]{:S(2)}, u32[]{:S(2)}) collective-permute-start(bf16[400,1024]{1,0:T(8,128)(2,1)} %shard_map.92.refs_0_.refs_1_.inner_ref.outer_ref), channel_id=1, source_target_pairs={{0,2},{1,3},{2,0},{3,1},{4,6},{5,7},{6,4},{7,5},{8,10},{9,11},{10,... | collective-permute-start | bytes 2457608 | tf_op jit(solution)/shard_map/ppermute | solution.py:107
  37.1 15.5 %collective-permute-start.8 = (bf16[192,1024]{1,0:T(8,128)(2,1)S(1)}, bf16[192,1024]{1,0:T(8,128)(2,1)}, u32[]{:S(2)}, u32[]{:S(2)}) collective-permute-start(bf16[192,1024]{1,0:T(8,128)(2,1)S(1)} %shard_map.94), channel_id=1, source_target_pairs={{0,4},{12,8},{1,5},{13,9},{2,6},{14,10},{3,7},{15,11},{16,20},{28,... | collective-permute-start | bytes 1179656 | tf_op jit(solution)/shard_map/ppermute | solution.py:115
  51.0 18.5 %collective-permute-start.4 = (bf16[400,1024]{1,0:T(8,128)(2,1)}, bf16[400,1024]{1,0:T(8,128)(2,1)}, u32[]{:S(2)}, u32[]{:S(2)}) collective-permute-start(bf16[400,1024]{1,0:T(8,128)(2,1)} %collective-permute-done.1.refs_1_.refs_0_.inner_ref), channel_id=1, source_target_pairs={{4,6},{5,7},{6,4},{7,5},{8,10},{9,11},{10,8},{11,9},{20,22},{21,23... | collective-permute-start | bytes 2457608 | tf_op jit(solution)/shard_map/ppermute | solution.py:500
  53.7 20.0 %collective-permute-start.9 = (bf16[400,1024]{1,0:T(8,128)(2,1)}, bf16[400,1024]{1,0:T(8,128)(2,1)S(1)}, u32[]{:S(2)}, u32[]{:S(2)}) collective-permute-start(bf16[400,1024]{1,0:T(8,128)(2,1)} %shard_map.95.refs_1_.outer_ref), channel_id=1, source_target_pairs={{0,2},{1,3},{2,0},{3,1},{12,14},{13,15},{14,12},{15,13},{16,18},{1... | collective-permute-start | bytes 2457608 | tf_op jit(solution)/shard_map/ppermute | solution.py:500
  56.1 20.6 %collective-permute-start.3 = (bf16[400,1024]{1,0:T(8,128)(2,1)}, bf16[400,1024]{1,0:T(8,128)(2,1)S(1)}, u32[]{:S(2)}, u32[]{:S(2)}) collective-permute-start(bf16[400,1024]{1,0:T(8,128)(2,1)} %collective-permute-done.2.refs_2_.inner_ref.refs_0_), channel_id=1, source_target_pairs={{4,0},{8,12},{5,1},{9,13},{6,2},{10,14},{7,3},{11,15},{20,16},{24,... | collective-permute-start | bytes 2457608 | tf_op jit(solution)/shard_map/ppermute | solution.py:115
  64.7 21.5 %collective-permute-start.15 = (bf16[384,1024]{1,0:T(8,128)(2,1)S(1)}, bf16[384,1024]{1,0:T(8,128)(2,1)S(1)}, u32[]{:S(2)}, u32[]{:S(2)}) collective-permute-start(bf16[384,1024]{1,0:T(8,128)(2,1)S(1)} %get-tuple-element.35), channel_id=1, source_target_pairs={{0,1},{1,0},{2,3},{3,2},{4,5},{5,4},{6,7},{7,6},{8,9},{9,8},{10,11... | collective-permute-start | bytes 2359304 | tf_op jit(solution)/shard_map/ppermute | solution.py:111
  69.0 20.4 %collective-permute-start.14 = (bf16[384,1024]{1,0:T(8,128)(2,1)S(1)}, bf16[384,1024]{1,0:T(8,128)(2,1)S(1)}, u32[]{:S(2)}, u32[]{:S(2)}) collective-permute-start(bf16[384,1024]{1,0:T(8,128)(2,1)S(1)} %get-tuple-element.33), channel_id=1, source_target_pairs={{0,1},{1,0},{2,3},{3,2},{4,5},{5,4},{6,7},{7,6},{8,9},{9,8},{10,11... | collective-permute-start | bytes 2359304 | tf_op jit(solution)/shard_map/ppermute | solution.py:111
  69.5 21.3 %collective-permute-start.13 = (bf16[192,1024]{1,0:T(8,128)(2,1)S(1)}, bf16[192,1024]{1,0:T(8,128)(2,1)S(1)}, u32[]{:S(2)}, u32[]{:S(2)}) collective-permute-start(bf16[192,1024]{1,0:T(8,128)(2,1)S(1)} %collective-permute-done.10.rest_2_.refs_2_), channel_id=1, source_target_pairs={{4,0},{8,12},{5,1},{9,13},{6,2},{10,14},{7,3},{11,15},{20,16},{24,... | collective-permute-start | bytes 1179656 | tf_op jit(solution)/shard_map/ppermute | solution.py:115
  78.4 12.5 %collective-permute-start.12 = (bf16[192,1024]{1,0:T(8,128)(2,1)S(1)}, bf16[192,1024]{1,0:T(8,128)(2,1)S(1)}, u32[]{:S(2)}, u32[]{:S(2)}) collective-permute-start(bf16[192,1024]{1,0:T(8,128)(2,1)S(1)} %shard_map.99), channel_id=1, source_target_pairs={{0,2},{1,3},{2,0},{3,1},{4,6},{5,7},{6,4},{7,5},{8,10},{9,11},{10,... | collective-permute-start | bytes 1179656 | tf_op jit(solution)/shard_map/ppermute | solution.py:107
  79.0 19.2 %collective-permute-start.18 = (bf16[256,2048]{1,0:T(8,128)(2,1)S(1)}, bf16[256,2048]{1,0:T(8,128)(2,1)S(1)}, u32[]{:S(2)}, u32[]{:S(2)}) collective-permute-start(bf16[256,2048]{1,0:T(8,128)(2,1)S(1)} %copy-done.14), channel_id=1, source_target_pairs={{0,1},{1,0},{2,3},{3,2},{4,5},{5,4},{6,7},{7,6},{8,9},{9,8},{10,11... | collective-permute-start | bytes 3145736 | tf_op jit(solution)/shard_map/ppermute | solution.py:111
  104.8 19.1 %collective-permute-start.22 = (bf16[192,1024]{1,0:T(8,128)(2,1)S(1)}, bf16[192,1024]{1,0:T(8,128)(2,1)}, u32[]{:S(2)}, u32[]{:S(2)}) collective-permute-start(bf16[192,1024]{1,0:T(8,128)(2,1)S(1)} %get-tuple-element.50), channel_id=1, source_target_pairs={{0,2},{1,3},{2,0},{3,1},{4,6},{5,7},{6,4},{7,5},{8,10},{9,11},{10,... | collective-permute-start | bytes 1179656 | tf_op jit(solution)/shard_map/ppermute | solution.py:107
  105.4 23.8 %collective-permute-start.26 = (bf16[192,1024]{1,0:T(8,128)(2,1)S(1)}, bf16[192,1024]{1,0:T(8,128)(2,1)}, u32[]{:S(2)}, u32[]{:S(2)}) collective-permute-start(bf16[192,1024]{1,0:T(8,128)(2,1)S(1)} %get-tuple-element.52), channel_id=1, source_target_pairs={{0,2},{1,3},{2,0},{3,1},{4,6},{5,7},{6,4},{7,5},{8,10},{9,11},{10,... | collective-permute-start | bytes 1179656 | tf_op jit(solution)/shard_map/ppermute | solution.py:107
  106.8 32.6 %collective-permute-start.19 = (bf16[192,1024]{1,0:T(8,128)(2,1)S(1)}, bf16[192,1024]{1,0:T(8,128)(2,1)S(1)}, u32[]{:S(2)}, u32[]{:S(2)}) collective-permute-start(bf16[192,1024]{1,0:T(8,128)(2,1)S(1)} %get-tuple-element.46), channel_id=1, source_target_pairs={{0,2},{1,3},{2,0},{3,1},{4,6},{5,7},{6,4},{7,5},{8,10},{9,11},{10,... | collective-permute-start | bytes 1179656 | tf_op jit(solution)/shard_map/ppermute | solution.py:107
  114.8 19.8 %collective-permute-start.21 = (bf16[192,1024]{1,0:T(8,128)(2,1)}, bf16[192,1024]{1,0:T(8,128)(2,1)S(1)}, u32[]{:S(2)}, u32[]{:S(2)}) collective-permute-start(bf16[192,1024]{1,0:T(8,128)(2,1)} %shard_map.108), channel_id=1, source_target_pairs={{4,8},{8,4},{5,9},{9,5},{6,10},{10,6},{7,11},{11,7},{20,24},{24,20... | collective-permute-start | bytes 1179656 | tf_op jit(solution)/shard_map/ppermute | solution.py:115
  115.5 19.2 %collective-permute-start.24 = (bf16[192,1024]{1,0:T(8,128)(2,1)}, bf16[192,1024]{1,0:T(8,128)(2,1)S(1)}, u32[]{:S(2)}, u32[]{:S(2)}) collective-permute-start(bf16[192,1024]{1,0:T(8,128)(2,1)} %shard_map.108), channel_id=1, source_target_pairs={{0,4},{12,8},{1,5},{13,9},{2,6},{14,10},{3,7},{15,11},{16,20},{28,... | collective-permute-start | bytes 1179656 | tf_op jit(solution)/shard_map/ppermute | solution.py:115
  125.9 16.2 %collective-permute-start.23 = (bf16[192,1024]{1,0:T(8,128)(2,1)}, bf16[192,1024]{1,0:T(8,128)(2,1)S(1)}, u32[]{:S(2)}, u32[]{:S(2)}) collective-permute-start(bf16[192,1024]{1,0:T(8,128)(2,1)} %shard_map.109.block_ref), channel_id=1, source_target_pairs={{0,8},{12,4},{1,9},{13,5},{2,10},{14,6},{3,11},{15,7},{16,24},{28,... | collective-permute-start | bytes 1179656 | tf_op jit(solution)/shard_map/ppermute | solution.py:115
  131.2 20.6 %collective-permute-start.27 = (bf16[192,1024]{1,0:T(8,128)(2,1)}, bf16[192,1024]{1,0:T(8,128)(2,1)S(1)}, u32[]{:S(2)}, u32[]{:S(2)}) collective-permute-start(bf16[192,1024]{1,0:T(8,128)(2,1)} %shard_map.111), channel_id=1, source_target_pairs={{0,4},{4,0},{8,12},{12,8},{1,5},{5,1},{9,13},{13,9},{2,6},{6,2},{1... | collective-permute-start | bytes 1179656 | tf_op jit(solution)/shard_map/ppermute | solution.py:115
  138.2 13.7 %collective-permute-start.25 = (bf16[192,1024]{1,0:T(8,128)(2,1)}, bf16[192,1024]{1,0:T(8,128)(2,1)S(1)}, u32[]{:S(2)}, u32[]{:S(2)}) collective-permute-start(bf16[192,1024]{1,0:T(8,128)(2,1)} %shard_map.110), channel_id=1, source_target_pairs={{4,12},{8,0},{5,13},{9,1},{6,14},{10,2},{7,15},{11,3},{20,28},{24,... | collective-permute-start | bytes 1179656 | tf_op jit(solution)/shard_map/ppermute | solution.py:115
  (27 other events, 109.9 us)

commit v10 on v9

--- a/solution.py
+++ b/solution.py
@@ -120,7 +120,7 @@
 
 
 TOKEN = jax.ShapeDtypeStruct((8, 128), jnp.float32)
-VMEM_LIMIT = 40 * 2**20
+VMEM_LIMIT = 18 * 2**20
 
 
 def on_core(body, out_shape, in_specs, scratch=()):
@@ -206,19 +206,10 @@
     blocks, _, offsets = block_list.shape
     total = owner.shape[0]
 
-    def body(rows_ref, gates_hbm, list_hbm, count_hbm, owner_hbm, out_ref, *scratch):
-        gates_ref, list_ref, count_ref, owner_ref, sems, small_sems = scratch
+    def body(rows_ref, gates_ref, list_ref, count_ref, owner_ref, out_ref, sems):
         moves = copies(rows_ref, 0, out_ref, count, 4, sems, 0)
-        small = [
-            pltpu.make_async_copy(source, target, small_sems.at[index])
-            for index, (source, target) in enumerate(
-                zip((gates_hbm, list_hbm, count_hbm, owner_hbm), scratch[:4])
-            )
-        ]
-        for copy in small + moves:
+        for copy in moves:
             copy.start()
-        for copy in small:
-            copy.wait()
         block_of = lax.broadcasted_iota(jnp.int32, (1, total), 1) // (total // blocks)
         facts = []
         for offset in range(offsets):
@@ -240,113 +231,60 @@
             copy.wait()
 
     shape = jax.ShapeDtypeStruct((count + FACT_ROWS, width), rows.dtype)
-    scratch = [
-        pltpu.VMEM(gates.shape, gates.dtype),
-        pltpu.SMEM(block_list.shape, block_list.dtype),
-        pltpu.SMEM(block_count.shape, block_count.dtype),
-        pltpu.VMEM(owner.shape, owner.dtype),
-        pltpu.SemaphoreType.DMA((4,)),
-        pltpu.SemaphoreType.DMA((4,)),
-    ]
-    return on_core(body, shape, [ANYWHERE] * 5, scratch)(
-        rows, gates, block_list, block_count, owner
-    )
+    return on_core(
+        body, shape, [ANYWHERE, VMEM, SMEM, SMEM, VMEM], [pltpu.SemaphoreType.DMA((4,))]
+    )(rows, gates, block_list, block_count, owner)
 
 
 def partial_sums(plan, sizes, parts, weights, places, before=None, send=True, waits=()):
     width, columns = weights[0].shape
-    rows, count = sum(sizes), len(places)
-    pairs = [
-        block if isinstance(block, tuple) else (block, block) for part in parts for block in part
+    blocks = [
+        block if isinstance(block, tuple) else (block,) for part in parts for block in part
     ]
-    sources = [array for pair in pairs for array in pair]
+    sources = [array for block in blocks for array in block]
     operands = [plan] + sources + [weights[place] for place in places] + [weights[2]]
     if before is not None:
         operands.append(before)
-    specs = [SMEM] + [ANYWHERE] * (len(operands) - 1) + [VMEM] * len(waits)
-    row_pieces, weight_pieces, before_pieces = 2, 4, 4
+    specs = [SMEM] + [VMEM] * (len(operands) - 1 + len(waits))
     has_before = before is not None
 
     def body(plan_ref, *refs):
-        source_refs = refs[: len(sources)]
-        weight_refs = refs[len(sources) : len(sources) + count + 1]
-        before_ref = refs[len(sources) + count + 1] if has_before else None
-        scratch = refs[len(operands) - 1 + len(waits) :]
-        results = scratch[: 3 if send else 2]
-        row_buffer, weight_buffer, row_sems, weight_sems = scratch[len(results) :][:4]
-        row_moves, weight_moves, before_moves = [], [[], []], []
-
-        def start(moves):
-            for copy in moves:
-                copy.start()
-
+        source_refs, refs = refs[: len(sources)], refs[len(sources) :]
+        weight_refs, refs = refs[: len(places) + 1], refs[len(places) + 1 :]
+        before_ref, refs = (refs[0], refs[1:]) if has_before else (None, refs)
+        results = refs[len(waits) :]
+        start, source = 0, 0
         for part, size in enumerate(sizes):
-            for index in range(count):
-                block = part * count + index
-                target = row_buffer.at[index, pl.ds(sum(sizes[:part]), size)]
-                first = block * row_pieces
-                kinds = [
-                    copies(source_refs[2 * block], 0, target, size, row_pieces, row_sems, first)
-                ]
-                if pairs[block][0] is pairs[block][1]:
-                    kinds.append(kinds[0])
-                else:
-                    source = source_refs[2 * block + 1]
-                    kinds.append(copies(source, 0, target, size, row_pieces, row_sems, first))
-                by_kind(plan_ref, kinds, start)
-                row_moves += kinds[0]
-        for side in range(2):
-            for index, place in enumerate(places):
-                weight_moves[side] += copies(
-                    weight_refs[index if side == 0 else count],
-                    0 if side == 0 else place * width,
-                    weight_buffer.at[side, index],
-                    width,
-                    weight_pieces,
-                    weight_sems,
-                    (side * count + index) * weight_pieces,
-                )
-            start(weight_moves[side])
-        if has_before:
-            before_buffer, before_sems = scratch[-2:]
-            before_moves = copies(
-                before_ref, 0, before_buffer, rows, before_pieces, before_sems, 0
-            )
-            start(before_moves)
-        for copy in row_moves + before_moves:
-            copy.wait()
-        for side in range(2):
-            for copy in weight_moves[side]:
-                copy.wait()
-            at = slice(side * columns, (side + 1) * columns)
-            total = before_buffer[:, at] if has_before else None
-            for index in range(count):
-                product = jnp.dot(
-                    row_buffer[index],
-                    weight_buffer[side, index],
-                    preferred_element_type=jnp.float32,
-                )
-                total = product if total is None else total + product
-            results[0][:, at] = total
-            if send:
-                results[1][:, at] = total.astype(jnp.bfloat16)
+            span = slice(start, start + size)
+            start += size
+            rows = []
+            for index in range(len(places)):
+                block = blocks[part * len(places) + index]
+                value = source_refs[source][:size, :]
+                if len(block) > 1:
+                    other = source_refs[source + 1][:size, :]
+                    value = jnp.where(plan_ref[INNER_AT] == 1, value, other)
+                source += len(block)
+                rows.append(value)
+            for side in range(2):
+                at = slice(side * columns, (side + 1) * columns)
+                total = before_ref[span, at] if has_before else None
+                for index, place in enumerate(places):
+                    if side == 0:
+                        weight = weight_refs[index][...]
+                    else:
+                        weight = weight_refs[-1][place * width : (place + 1) * width, :]
+                    product = jnp.dot(rows[index], weight, preferred_element_type=jnp.float32)
+                    total = product if total is None else total + product
+                results[0][span, at] = total
+                if send:
+                    results[1][span, at] = total.astype(jnp.bfloat16)
         results[-1][...] = jnp.zeros(TOKEN.shape, TOKEN.dtype)
 
-    shapes = [jax.ShapeDtypeStruct((rows, 2 * columns), jnp.float32)]
+    shapes = [jax.ShapeDtypeStruct((sum(sizes), 2 * columns), jnp.float32)]
     if send:
-        shapes.append(jax.ShapeDtypeStruct((rows, 2 * columns), jnp.bfloat16))
-    scratch = [
-        pltpu.VMEM((count, rows, width), jnp.bfloat16),
-        pltpu.VMEM((2, count, width, columns), jnp.bfloat16),
-        pltpu.SemaphoreType.DMA((len(pairs) * row_pieces,)),
-        pltpu.SemaphoreType.DMA((2 * count * weight_pieces,)),
-    ]
-    if has_before:
-        scratch += [
-            pltpu.VMEM((rows, 2 * columns), jnp.float32),
-            pltpu.SemaphoreType.DMA((before_pieces,)),
-        ]
-    return on_core(body, shapes + [TOKEN], specs, scratch)(*operands, *waits)
+        shapes.append(jax.ShapeDtypeStruct((sum(sizes), 2 * columns), jnp.bfloat16))
+    return on_core(body, shapes + [TOKEN], specs)(*operands, *waits)
 
 
 def collected_rows(owned, slot, plan, sums, got, facts, before):
@@ -516,15 +454,7 @@
     lent_down = across_cores(lend_down)
 
     outer_last = along(inner_last, OUTWARD)
-    outer_next = after(
-        outer_next,
-        beside_far,
-        inner_last,
-        inward_far,
-        lend_down,
-        weights[0],
-        weights[1],
-    )
+    outer_next = after(outer_next, beside_far, lend_down, weights[0], weights[1])
     second = (middle, outer_next)
     second_far = (at_kind(middle, (1, 2)), at_kind(outer_next, (0, 3)))
     middle_far = along(inward_far, MIDDLE)

time: 155 us -> 150 us (0.968)
  waiting for transfers between devices: 35.3 us -> 41.7 us
  Pallas kernels: 43.7 us -> 38.9 us
  starting transfers between devices: 49.8 us -> 46 us
  local copies, waits for them, and re-layouts: 16.6 us -> 14.1 us
    pallas_call x6, Pallas kernels: 22 us -> 16.9 us  [the longest x5 15.1 us: partial_sums(): return on_core(body, shapes + [TOKEN], specs)(*operands, *waits)]
    ppermute x13, starting transfers between devices: 36.3 us -> 32.1 us  [along(): return lax.ppermute(block, 'blk', route)]
    ppermute x2, waiting for transfers between devices: 2.81 us -> 5.5 us  [at_kind(): return lax.ppermute(block, ('blk', 'tp'), pairs)]
    ppermute x13, waiting for transfers between devices: 26.8 us -> 29.3 us  [along(): return lax.ppermute(block, 'blk', route)]
    unnamed x46 -> x44, local copies, waits for them, and re-layouts: 11.2 us -> 8.73 us
  transfers between devices with their start and end apart: 28 -> 28, of which waited for: 8 -> 8; matrix products, arithmetic and copies ran while one was open for 7% -> 8% of each run, Pallas kernels for 27% -> 23%
where the time goes in v10:
time: 150 us; the launch traced here: 149 us
  starting transfers between devices  46 us (31%)
  waiting for transfers between devices  41.7 us (28%)
  Pallas kernels  38.9 us (26%)
  local copies, waits for them, and re-layouts  14.1 us (9%)
  other arithmetic  8.11 us (5%)
    ppermute x13, starting transfers between devices, along(): return lax.ppermute(block, 'blk', route)  32.1 us
    ppermute x13, waiting for transfers between devices, along(): return lax.ppermute(block, 'blk', route)  29.3 us
    pallas_call x5, Pallas kernels, partial_sums(): return on_core(body, shapes + [TOKEN], specs)(*operands, *waits)  15.1 us
    unnamed x44, local copies, waits for them, and re-layouts  8.73 us
    pallas_call x4, Pallas kernels, added(): pl.pallas_call(body, out_shape=jax.ShapeDtypeStruct(block.shape, jnp.bflo...  8.14 us
    ppermute x7, starting transfers between devices, across_chips(): return lax.ppermute(block, 'tp', [(i, i ^ 2) for i in range(4)])  7.69 us
    ppermute x7, waiting for transfers between devices, across_chips(): return lax.ppermute(block, 'tp', [(i, i ^ 2) for i in range(4)])  6.86 us
    pallas_call x3, Pallas kernels, collect(): on_core(body, [shape, TOKEN], specs, fact_scratch(facts[0].shape[1]))  6.71 us
  transfers between devices with their start and end apart: 28, of which 8 were waited for; matrix products, arithmetic and copies ran while one was open for 8% of the time, Pallas kernels for 23%

profile of v10, /device:TPU:0, one launch (start us, length us, event | category | flops | bytes accessed | tf_op | source)
XLA Modules:
  0.0 149.2 jit_solution(16769780179583012509)
XLA Ops:
  6.1 5.0 %collective-permute-start = (bf16[400,1024]{1,0:T(8,128)(2,1)S(1)}, bf16[400,1024]{1,0:T(8,128)(2,1)}, u32[]{:S(2)}, u32[]{:S(2)}) collective-permute-start(bf16[400,1024]{1,0:T(8,128)(2,1)S(1)} %shard_map.91.refs_1_.inner_ref.outer_ref), channel_id=1, source_target_pairs={{0,4},{4,0},{8,12},{12,8},{1,5},{5,1},{9,13},{13,9},{2,6},{6,2},{1... | collective-permute-start | bytes 2457608 | tf_op jit(solution)/shard_map/ppermute | solution.py:115
  12.6 3.4 %dynamic-slice_bitcast_fusion.4 = (bf16[1024,256]{1,0:T(8,128)(2,1)S(1)}, bf16[1024,256]{1,0:T(8,128)(2,1)S(1)}, bf16[1024,256]{1,0:T(8,128)(2,1)}, bf16[1024,25...) fusion(bf16[4,1024,256]{2,1,0:T(8,128)(2,1)} %bitcast.32, ...), kind=kLoop, calls=%fused_computation.10 | loop fusion | bytes 8388624 | tf_op jit(solution)/shard_map/jit(dynamic_index_in_dim)/squeeze | solution.py:424
  17.6 2.2 %pad_maximum_fusion.1.refs_3_.refs_2_.refs_4_ = bf16[1024,512]{1,0:T(8,128)(2,1)} fusion(bf16[1024,256]{1,0:T(8,128)(2,1)S(1)} %get-tuple-element.64, bf16[1024,256]{1,0:T(8,128)(2,1)} %get-tuple-element.65), kind=kLoop, calls=%fused_computation.2 | loop fusion | flops 2097152 | bytes 2097152 | tf_op jit(solution)/shard_map/concatenate | solution.py:427
  24.2 5.0 %collective-permute-done.refs_0_ = bf16[400,1024]{1,0:T(8,128)(2,1)} collective-permute-done((bf16[400,1024]{1,0:T(8,128)(2,1)S(1)}, bf16[400,1024]{1,0:T(8,128)(2,1)}, u32[]{:S(2)}, u32[]{:S(2)}) %collective-permute-start) | collective-permute-done | bytes 819232 | tf_op jit(solution)/shard_map/ppermute | solution.py:115
  34.3 7.8 %collective-permute-start.9 = (bf16[192,1024]{1,0:T(8,128)(2,1)S(1)}, bf16[192,1024]{1,0:T(8,128)(2,1)}, u32[]{:S(2)}, u32[]{:S(2)}) collective-permute-start(bf16[192,1024]{1,0:T(8,128)(2,1)S(1)} %shard_map.95), channel_id=1, source_target_pairs={{0,4},{12,8},{1,5},{13,9},{2,6},{14,10},{3,7},{15,11},{16,20},{28,... | collective-permute-start | bytes 1179656 | tf_op jit(solution)/shard_map/ppermute | solution.py:115
  43.2 5.3 %collective-permute-done.5.refs_0_ = bf16[400,1024]{1,0:T(8,128)(2,1)} collective-permute-done((bf16[400,1024]{1,0:T(8,128)(2,1)}, bf16[400,1024]{1,0:T(8,128)(2,1)}, u32[]{:S(2)}, u32[]{:S(2)}) %collective-permute-start.5) | collective-permute-done | bytes 819232 | tf_op jit(solution)/shard_map/ppermute | solution.py:115
  50.1 3.5 %collective-permute-start.7 = (bf16[400,1024]{1,0:T(8,128)(2,1)}, bf16[400,1024]{1,0:T(8,128)(2,1)S(1)}, u32[]{:S(2)}, u32[]{:S(2)}) collective-permute-start(bf16[400,1024]{1,0:T(8,128)(2,1)} %shard_map.94.refs_1_.outer_ref), channel_id=1, source_target_pairs={{0,2},{1,3},{2,0},{3,1},{12,14},{13,15},{14,12},{15,13},{16,18},{1... | collective-permute-start | bytes 2457608 | tf_op jit(solution)/shard_map/ppermute | solution.py:438
  56.9 3.2 %shard_map.97 = (f32[384,1024]{1,0:T(8,128)S(1)}, bf16[384,1024]{1,0:T(8,128)(2,1)S(1)}, f32[8,128]{1,0:T(8,128)S(1)}) custom-call(s32[9]{0:T(128)S(1)} %fusion.plan_ref, bf16[384,1024]{1,0:T(8,128)(2,1)} %refs_0_.1, bf16[384,1024]{1,0:T(8,128)(2,1)} %collective-permute-done.8.inner_ref.outer_ref.refs_1_, bf16[1024,512]{1,0:T(8,128)(2,1)S(1)} %copy-done, ...), custom_call_target="tpu_custom_call" | custom-call | flops 1024 | bytes 1024 | tf_op jit(solution)/shard_map/pallas_call | solution.py:287
  60.2 3.2 %shard_map.98 = (f32[384,1024]{1,0:T(8,128)S(1)}, bf16[384,1024]{1,0:T(8,128)(2,1)S(1)}, f32[8,128]{1,0:T(8,128)S(1)}) custom-call(s32[9]{0:T(128)S(1)} %fusion.plan_ref, bf16[400,1024]{1,0:T(8,128)(2,1)} %shard_map.92.refs_0_.inner_ref.outer_ref, bf16[400,1024]{1,0:T(8,128)(2,1)} %collective-permute-done.6.refs_1_, bf16[1024,512]{1,0:T(8,128)(2,1)S(1)} %copy-done, ...), custom_call_target="tpu_custom_call" | custom-call | flops 1024 | bytes 1024 | tf_op jit(solution)/shard_map/pallas_call | solution.py:287
  65.3 5.5 %collective-permute-done.7.rest_1_.refs_3_ = bf16[400,1024]{1,0:T(8,128)(2,1)S(1)} collective-permute-done((bf16[400,1024]{1,0:T(8,128)(2,1)}, bf16[400,1024]{1,0:T(8,128)(2,1)S(1)}, u32[]{:S(2)}, u32[]{:S(2)}) %collective-permute-start.7) | collective-permute-done | bytes 819232 | tf_op jit(solution)/shard_map/ppermute | solution.py:438
  70.8 5.2 %collective-permute-done.3.outer_ref.refs_1_ = bf16[400,1024]{1,0:T(8,128)(2,1)S(1)} collective-permute-done((bf16[400,1024]{1,0:T(8,128)(2,1)}, bf16[400,1024]{1,0:T(8,128)(2,1)S(1)}, u32[]{:S(2)}, u32[]{:S(2)}) %collective-permute-start.3) | collective-permute-done | bytes 819232 | tf_op jit(solution)/shard_map/ppermute | solution.py:115
  78.3 4.0 %shard_map.104 = (f32[384,1024]{1,0:T(8,128)S(1)}, bf16[384,1024]{1,0:T(8,128)(2,1)S(1)}, f32[8,128]{1,0:T(8,128)}) custom-call(s32[9]{0:T(128)S(1)} %fusion.plan_ref, bf16[400,1024]{1,0:T(8,128)(2,1)} %collective-permute-done.1.refs_1_.refs_0_.inner_ref, bf16[400,1024]{1,0:T(8,128)(2,1)} %shard_map.94.refs_1_.outer_ref, ...), custom_call_target="tpu_custom_call" | custom-call | flops 1024 | bytes 1024 | tf_op jit(solution)/shard_map/pallas_call | solution.py:287
  82.2 2.7 %shard_map.100 = (f32[384,1024]{1,0:T(8,128)S(1)}, f32[8,128]{1,0:T(8,128)}) custom-call(s32[9]{0:T(128)S(1)} %fusion.plan_ref, bf16[400,1024]{1,0:T(8,128)(2,1)} %collective-permute-done.2.inner_ref.refs_0_, bf16[400,1024]{1,0:T(8,128)(2,1)S(1)} %collective-permute-done.3.outer_ref.refs_1_, bf16[1024,512]{1,0:T(8,128)(2,1)S(1)} %copy-done, ...), custom_call_target="tpu_custom_call" | custom-call | flops 1024 | bytes 1024 | tf_op jit(solution)/shard_map/pallas_call | solution.py:287
  87.3 2.2 %shard_map.102 = (f32[768,512]{1,0:T(8,128)S(1)}, f32[8,128]{1,0:T(8,128)S(1)}) custom-call(s32[9]{0:T(128)S(1)} %fusion.plan_ref, f32[384,1024]{1,0:T(8,128)S(1)} %get-tuple-element.32.sums_ref, bf16[384,1024]{1,0:T(8,128)(2,1)S(1)} %collective-permute-done.14.got_ref, bf16[400,1024]{1,0:T(8,128)(2,1)} %shard_map.92.refs_0_.inner_ref.outer_ref, ...), custom_call_target="tpu_custom_call" | custom-call | flops 1024 | bytes 1024 | tf_op jit(solution)/shard_map/pallas_call | solution.py:346
  91.7 2.6 %shard_map.105 = (f32[768,512]{1,0:T(8,128)S(1)}, f32[8,128]{1,0:T(8,128)}) custom-call(s32[9]{0:T(128)S(1)} %fusion.plan_ref, f32[384,1024]{1,0:T(8,128)S(1)} %get-tuple-element.40.sums_ref, bf16[384,1024]{1,0:T(8,128)(2,1)S(1)} %collective-permute-done.17.got_ref, bf16[400,1024]{1,0:T(8,128)(2,1)} %collective-permute-done.1.refs_1_.refs_0_.inner_ref, ...), custom_call_target="tpu_custom_call" | custom-call | flops 1024 | bytes 1024 | tf_op jit(solution)/shard_map/pallas_call | solution.py:346
  94.4 2.1 %shard_map.106 = (bf16[192,1024]{1,0:T(8,128)(2,1)S(1)}, f32[192,1024]{1,0:T(8,128)S(1)}, bf16[576,512]{1,0:T(8,128)(2,1)S(1)}) custom-call(s32[9]{0:T(128)S(1)} %fusion.plan_ref, f32[384,1024]{1,0:T(8,128)S(1)} %get-tuple-element.38.sums_ref, bf16[384,1024]{1,0:T(8,128)(2,1)S(1)} %collective-permute-done.16.got_ref, ...), custom_call_target="tpu_custom_call" | custom-call | flops 1024 | bytes 1024 | tf_op jit(solution)/shard_map/pallas_call | solution.py:394
  103.8 4.6 %collective-permute-done.20.other_ref = bf16[192,1024]{1,0:T(8,128)(2,1)S(1)} collective-permute-done((bf16[192,1024]{1,0:T(8,128)(2,1)S(1)}, bf16[192,1024]{1,0:T(8,128)(2,1)S(1)}, u32[]{:S(2)}, u32[]{:S(2)}) %collective-permute-start.20) | collective-permute-done | bytes 393248 | tf_op jit(solution)/shard_map/ppermute | solution.py:107
  111.9 5.9 %collective-permute-start.24 = (bf16[192,1024]{1,0:T(8,128)(2,1)}, bf16[192,1024]{1,0:T(8,128)(2,1)S(1)}, u32[]{:S(2)}, u32[]{:S(2)}) collective-permute-start(bf16[192,1024]{1,0:T(8,128)(2,1)} %shard_map.108), channel_id=1, source_target_pairs={{0,4},{12,8},{1,5},{13,9},{2,6},{14,10},{3,7},{15,11},{16,20},{28,... | collective-permute-start | bytes 1179656 | tf_op jit(solution)/shard_map/ppermute | solution.py:115
  119.8 3.2 %collective-permute-start.23 = (bf16[192,1024]{1,0:T(8,128)(2,1)}, bf16[192,1024]{1,0:T(8,128)(2,1)S(1)}, u32[]{:S(2)}, u32[]{:S(2)}) collective-permute-start(bf16[192,1024]{1,0:T(8,128)(2,1)} %shard_map.109.block_ref), channel_id=1, source_target_pairs={{0,8},{12,4},{1,9},{13,5},{2,10},{14,6},{3,11},{15,7},{16,24},{28,... | collective-permute-start | bytes 1179656 | tf_op jit(solution)/shard_map/ppermute | solution.py:115
  123.1 2.2 %collective-permute-done.26.other_ref = bf16[192,1024]{1,0:T(8,128)(2,1)S(1)} collective-permute-done((bf16[192,1024]{1,0:T(8,128)(2,1)S(1)}, bf16[192,1024]{1,0:T(8,128)(2,1)S(1)}, u32[]{:S(2)}, u32[]{:S(2)}) %collective-permute-start.26) | collective-permute-done | bytes 393248 | tf_op jit(solution)/shard_map/ppermute | solution.py:107
  126.0 2.1 %shard_map.111 = bf16[192,1024]{1,0:T(8,128)(2,1)} custom-call(f32[192,1024]{1,0:T(8,128)} %copy-done.10, bf16[192,1024]{1,0:T(8,128)(2,1)} %copy-done.21), custom_call_target="tpu_custom_call" | custom-call | flops 4294967296 | bytes 1024 | tf_op jit(solution)/shard_map/pallas_call | solution.py:354
  133.4 2.7 %collective-permute-done.23 = bf16[192,1024]{1,0:T(8,128)(2,1)S(1)} collective-permute-done((bf16[192,1024]{1,0:T(8,128)(2,1)}, bf16[192,1024]{1,0:T(8,128)(2,1)S(1)}, u32[]{:S(2)}, u32[]{:S(2)}) %collective-permute-start.23) | collective-permute-done | bytes 393248 | tf_op jit(solution)/shard_map/ppermute | solution.py:115
  136.0 11.0 %collective-permute-done.27 = bf16[192,1024]{1,0:T(8,128)(2,1)S(1)} collective-permute-done((bf16[192,1024]{1,0:T(8,128)(2,1)}, bf16[192,1024]{1,0:T(8,128)(2,1)S(1)}, u32[]{:S(2)}, u32[]{:S(2)}) %collective-permute-start.27) | collective-permute-done | bytes 393248 | tf_op jit(solution)/shard_map/ppermute | solution.py:115
  147.1 2.1 %add_convert_fusion = bf16[192,1024]{1,0:T(8,128)(2,1)} fusion(f32[192,1024]{1,0:T(8,128)S(1)} %get-tuple-element.45, bf16[192,1024]{1,0:T(8,128)(2,1)S(1)} %collective-permute-done.27, bf16[192,1024]{1,0:T(8,128)(2,1)S(1)} %collective-permute-done.25, bf16[192,1024]{1,0:T(8,128)(2,1)S(1)} %collective-permute-done.23, bf16[192,1024]{1,0:T(8,128)(2,1)} %copy-done.18, ...), kind=kLoop, calls=%fused_computation.5 | loop fusion | flops 2162688 | bytes 3145728 | tf_op jit(solution)/shard_map/convert_element_type | solution.py:498
  (106 shorter events, 51.9 us)
Async XLA Ops:
  4.5 17.6 %collective-permute-start.1 = (bf16[400,1024]{1,0:T(8,128)(2,1)S(1)}, bf16[400,1024]{1,0:T(8,128)(2,1)}, u32[]{:S(2)}, u32[]{:S(2)}) collective-permute-start(bf16[400,1024]{1,0:T(8,128)(2,1)S(1)} %shard_map.91.refs_1_.inner_ref.outer_ref), channel_id=1, source_target_pairs={{4,8},{8,4},{5,9},{9,5},{6,10},{10,6},{7,11},{11,7},{20,24},{24,20... | collective-permute-start | bytes 2457608 | tf_op jit(solution)/shard_map/ppermute | solution.py:115
  6.1 23.1 %collective-permute-start = (bf16[400,1024]{1,0:T(8,128)(2,1)S(1)}, bf16[400,1024]{1,0:T(8,128)(2,1)}, u32[]{:S(2)}, u32[]{:S(2)}) collective-permute-start(bf16[400,1024]{1,0:T(8,128)(2,1)S(1)} %shard_map.91.refs_1_.inner_ref.outer_ref), channel_id=1, source_target_pairs={{0,4},{4,0},{8,12},{12,8},{1,5},{5,1},{9,13},{13,9},{2,6},{6,2},{1... | collective-permute-start | bytes 2457608 | tf_op jit(solution)/shard_map/ppermute | solution.py:115
  11.1 21.2 %collective-permute-start.8 = (bf16[384,1024]{1,0:T(8,128)(2,1)}, bf16[384,1024]{1,0:T(8,128)(2,1)}, u32[]{:S(2)}, u32[]{:S(2)}) collective-permute-start(bf16[384,1024]{1,0:T(8,128)(2,1)} %refs_0_.1), channel_id=1, source_target_pairs={{0,2},{1,3},{2,0},{3,1},{4,6},{5,7},{6,4},{7,5},{8,10},{9,11},{10,... | collective-permute-start | bytes 2359304 | tf_op jit(solution)/shard_map/ppermute | solution.py:107
  17.6 38.0 %collective-permute-start.11 = (bf16[2048,512]{1,0:T(8,128)(2,1)}, bf16[2048,512]{1,0:T(8,128)(2,1)S(1)}, u32[]{:S(2)}, u32[]{:S(2)}) collective-permute-start(bf16[2048,512]{1,0:T(8,128)(2,1)} %shard_map.96), channel_id=1, source_target_pairs={{0,1},{1,0},{2,3},{3,2},{4,5},{5,4},{6,7},{7,6},{8,9},{9,8},{10,11... | collective-permute-start | bytes 6291464 | tf_op jit(solution)/shard_map/ppermute | solution.py:111
  22.2 26.3 %collective-permute-start.5 = (bf16[400,1024]{1,0:T(8,128)(2,1)}, bf16[400,1024]{1,0:T(8,128)(2,1)}, u32[]{:S(2)}, u32[]{:S(2)}) collective-permute-start(bf16[400,1024]{1,0:T(8,128)(2,1)} %collective-permute-done.1.refs_1_.refs_0_.inner_ref), channel_id=1, source_target_pairs={{4,0},{8,12},{5,1},{9,13},{6,2},{10,14},{7,3},{11,15},{20,16},{24,... | collective-permute-start | bytes 2457608 | tf_op jit(solution)/shard_map/ppermute | solution.py:115
  29.2 20.9 %collective-permute-start.6 = (bf16[400,1024]{1,0:T(8,128)(2,1)}, bf16[400,1024]{1,0:T(8,128)(2,1)}, u32[]{:S(2)}, u32[]{:S(2)}) collective-permute-start(bf16[400,1024]{1,0:T(8,128)(2,1)} %shard_map.92.refs_0_.inner_ref.outer_ref), channel_id=1, source_target_pairs={{0,2},{1,3},{2,0},{3,1},{4,6},{5,7},{6,4},{7,5},{8,10},{9,11},{10,... | collective-permute-start | bytes 2457608 | tf_op jit(solution)/shard_map/ppermute | solution.py:107
  30.7 22.9 %collective-permute-start.2 = (bf16[400,1024]{1,0:T(8,128)(2,1)}, bf16[400,1024]{1,0:T(8,128)(2,1)}, u32[]{:S(2)}, u32[]{:S(2)}) collective-permute-start(bf16[400,1024]{1,0:T(8,128)(2,1)} %shard_map.92.refs_0_.inner_ref.outer_ref), channel_id=1, source_target_pairs={{4,8},{8,4},{5,9},{9,5},{6,10},{10,6},{7,11},{11,7},{20,24},{24,20... | collective-permute-start | bytes 2457608 | tf_op jit(solution)/shard_map/ppermute | solution.py:115
  34.3 20.6 %collective-permute-start.9 = (bf16[192,1024]{1,0:T(8,128)(2,1)S(1)}, bf16[192,1024]{1,0:T(8,128)(2,1)}, u32[]{:S(2)}, u32[]{:S(2)}) collective-permute-start(bf16[192,1024]{1,0:T(8,128)(2,1)S(1)} %shard_map.95), channel_id=1, source_target_pairs={{0,4},{12,8},{1,5},{13,9},{2,6},{14,10},{3,7},{15,11},{16,20},{28,... | collective-permute-start | bytes 1179656 | tf_op jit(solution)/shard_map/ppermute | solution.py:115
  48.5 15.5 %collective-permute-start.4 = (bf16[400,1024]{1,0:T(8,128)(2,1)}, bf16[400,1024]{1,0:T(8,128)(2,1)}, u32[]{:S(2)}, u32[]{:S(2)}) collective-permute-start(bf16[400,1024]{1,0:T(8,128)(2,1)} %collective-permute-done.1.refs_1_.refs_0_.inner_ref), channel_id=1, source_target_pairs={{4,6},{5,7},{6,4},{7,5},{8,10},{9,11},{10,8},{11,9},{20,22},{21,23... | collective-permute-start | bytes 2457608 | tf_op jit(solution)/shard_map/ppermute | solution.py:438
  50.1 20.7 %collective-permute-start.7 = (bf16[400,1024]{1,0:T(8,128)(2,1)}, bf16[400,1024]{1,0:T(8,128)(2,1)S(1)}, u32[]{:S(2)}, u32[]{:S(2)}) collective-permute-start(bf16[400,1024]{1,0:T(8,128)(2,1)} %shard_map.94.refs_1_.outer_ref), channel_id=1, source_target_pairs={{0,2},{1,3},{2,0},{3,1},{12,14},{13,15},{14,12},{15,13},{16,18},{1... | collective-permute-start | bytes 2457608 | tf_op jit(solution)/shard_map/ppermute | solution.py:438
  53.6 22.4 %collective-permute-start.3 = (bf16[400,1024]{1,0:T(8,128)(2,1)}, bf16[400,1024]{1,0:T(8,128)(2,1)S(1)}, u32[]{:S(2)}, u32[]{:S(2)}) collective-permute-start(bf16[400,1024]{1,0:T(8,128)(2,1)} %collective-permute-done.2.inner_ref.refs_0_), channel_id=1, source_target_pairs={{4,0},{8,12},{5,1},{9,13},{6,2},{10,14},{7,3},{11,15},{20,16},{24,... | collective-permute-start | bytes 2457608 | tf_op jit(solution)/shard_map/ppermute | solution.py:115
  60.1 24.8 %collective-permute-start.15 = (bf16[384,1024]{1,0:T(8,128)(2,1)S(1)}, bf16[384,1024]{1,0:T(8,128)(2,1)S(1)}, u32[]{:S(2)}, u32[]{:S(2)}) collective-permute-start(bf16[384,1024]{1,0:T(8,128)(2,1)S(1)} %get-tuple-element.35), channel_id=1, source_target_pairs={{0,1},{1,0},{2,3},{3,2},{4,5},{5,4},{6,7},{7,6},{8,9},{9,8},{10,11... | collective-permute-start | bytes 2359304 | tf_op jit(solution)/shard_map/ppermute | solution.py:111
  63.4 23.9 %collective-permute-start.14 = (bf16[384,1024]{1,0:T(8,128)(2,1)S(1)}, bf16[384,1024]{1,0:T(8,128)(2,1)S(1)}, u32[]{:S(2)}, u32[]{:S(2)}) collective-permute-start(bf16[384,1024]{1,0:T(8,128)(2,1)S(1)} %get-tuple-element.33), channel_id=1, source_target_pairs={{0,1},{1,0},{2,3},{3,2},{4,5},{5,4},{6,7},{7,6},{8,9},{9,8},{10,11... | collective-permute-start | bytes 2359304 | tf_op jit(solution)/shard_map/ppermute | solution.py:111
  64.0 25.5 %collective-permute-start.13 = (bf16[192,1024]{1,0:T(8,128)(2,1)S(1)}, bf16[192,1024]{1,0:T(8,128)(2,1)S(1)}, u32[]{:S(2)}, u32[]{:S(2)}) collective-permute-start(bf16[192,1024]{1,0:T(8,128)(2,1)S(1)} %collective-permute-done.10.rest_2_.refs_1_), channel_id=1, source_target_pairs={{4,0},{8,12},{5,1},{9,13},{6,2},{10,14},{7,3},{11,15},{20,16},{24,... | collective-permute-start | bytes 1179656 | tf_op jit(solution)/shard_map/ppermute | solution.py:115
  78.3 16.1 %collective-permute-start.18 = (bf16[256,2048]{1,0:T(8,128)(2,1)S(1)}, bf16[256,2048]{1,0:T(8,128)(2,1)S(1)}, u32[]{:S(2)}, u32[]{:S(2)}) collective-permute-start(bf16[256,2048]{1,0:T(8,128)(2,1)S(1)} %copy-done.12), channel_id=1, source_target_pairs={{0,1},{1,0},{2,3},{3,2},{4,5},{5,4},{6,7},{7,6},{8,9},{9,8},{10,11... | collective-permute-start | bytes 3145736 | tf_op jit(solution)/shard_map/ppermute | solution.py:111
  96.5 12.0 %collective-permute-start.20 = (bf16[192,1024]{1,0:T(8,128)(2,1)S(1)}, bf16[192,1024]{1,0:T(8,128)(2,1)S(1)}, u32[]{:S(2)}, u32[]{:S(2)}) collective-permute-start(bf16[192,1024]{1,0:T(8,128)(2,1)S(1)} %get-tuple-element.48), channel_id=1, source_target_pairs={{0,2},{1,3},{2,0},{3,1},{4,6},{5,7},{6,4},{7,5},{8,10},{9,11},{10,... | collective-permute-start | bytes 1179656 | tf_op jit(solution)/shard_map/ppermute | solution.py:107
  101.2 16.5 %collective-permute-start.22 = (bf16[192,1024]{1,0:T(8,128)(2,1)S(1)}, bf16[192,1024]{1,0:T(8,128)(2,1)}, u32[]{:S(2)}, u32[]{:S(2)}) collective-permute-start(bf16[192,1024]{1,0:T(8,128)(2,1)S(1)} %get-tuple-element.50), channel_id=1, source_target_pairs={{0,2},{1,3},{2,0},{3,1},{4,6},{5,7},{6,4},{7,5},{8,10},{9,11},{10,... | collective-permute-start | bytes 1179656 | tf_op jit(solution)/shard_map/ppermute | solution.py:107
  101.8 23.5 %collective-permute-start.26 = (bf16[192,1024]{1,0:T(8,128)(2,1)S(1)}, bf16[192,1024]{1,0:T(8,128)(2,1)S(1)}, u32[]{:S(2)}, u32[]{:S(2)}) collective-permute-start(bf16[192,1024]{1,0:T(8,128)(2,1)S(1)} %get-tuple-element.52), channel_id=1, source_target_pairs={{0,2},{1,3},{2,0},{3,1},{4,6},{5,7},{6,4},{7,5},{8,10},{9,11},{10,... | collective-permute-start | bytes 1179656 | tf_op jit(solution)/shard_map/ppermute | solution.py:107
  103.3 30.1 %collective-permute-start.19 = (bf16[192,1024]{1,0:T(8,128)(2,1)S(1)}, bf16[192,1024]{1,0:T(8,128)(2,1)S(1)}, u32[]{:S(2)}, u32[]{:S(2)}) collective-permute-start(bf16[192,1024]{1,0:T(8,128)(2,1)S(1)} %get-tuple-element.46), channel_id=1, source_target_pairs={{0,2},{1,3},{2,0},{3,1},{4,6},{5,7},{6,4},{7,5},{8,10},{9,11},{10,... | collective-permute-start | bytes 1179656 | tf_op jit(solution)/shard_map/ppermute | solution.py:107
  111.2 17.4 %collective-permute-start.21 = (bf16[192,1024]{1,0:T(8,128)(2,1)}, bf16[192,1024]{1,0:T(8,128)(2,1)S(1)}, u32[]{:S(2)}, u32[]{:S(2)}) collective-permute-start(bf16[192,1024]{1,0:T(8,128)(2,1)} %shard_map.108), channel_id=1, source_target_pairs={{4,8},{8,4},{5,9},{9,5},{6,10},{10,6},{7,11},{11,7},{20,24},{24,20... | collective-permute-start | bytes 1179656 | tf_op jit(solution)/shard_map/ppermute | solution.py:115
  111.9 16.7 %collective-permute-start.24 = (bf16[192,1024]{1,0:T(8,128)(2,1)}, bf16[192,1024]{1,0:T(8,128)(2,1)S(1)}, u32[]{:S(2)}, u32[]{:S(2)}) collective-permute-start(bf16[192,1024]{1,0:T(8,128)(2,1)} %shard_map.108), channel_id=1, source_target_pairs={{0,4},{12,8},{1,5},{13,9},{2,6},{14,10},{3,7},{15,11},{16,20},{28,... | collective-permute-start | bytes 1179656 | tf_op jit(solution)/shard_map/ppermute | solution.py:115
  119.8 16.2 %collective-permute-start.23 = (bf16[192,1024]{1,0:T(8,128)(2,1)}, bf16[192,1024]{1,0:T(8,128)(2,1)S(1)}, u32[]{:S(2)}, u32[]{:S(2)}) collective-permute-start(bf16[192,1024]{1,0:T(8,128)(2,1)} %shard_map.109.block_ref), channel_id=1, source_target_pairs={{0,8},{12,4},{1,9},{13,5},{2,10},{14,6},{3,11},{15,7},{16,24},{28,... | collective-permute-start | bytes 1179656 | tf_op jit(solution)/shard_map/ppermute | solution.py:115
  128.1 19.0 %collective-permute-start.27 = (bf16[192,1024]{1,0:T(8,128)(2,1)}, bf16[192,1024]{1,0:T(8,128)(2,1)S(1)}, u32[]{:S(2)}, u32[]{:S(2)}) collective-permute-start(bf16[192,1024]{1,0:T(8,128)(2,1)} %shard_map.111), channel_id=1, source_target_pairs={{0,4},{4,0},{8,12},{12,8},{1,5},{5,1},{9,13},{13,9},{2,6},{6,2},{1... | collective-permute-start | bytes 1179656 | tf_op jit(solution)/shard_map/ppermute | solution.py:115
  132.1 15.0 %collective-permute-start.25 = (bf16[192,1024]{1,0:T(8,128)(2,1)}, bf16[192,1024]{1,0:T(8,128)(2,1)S(1)}, u32[]{:S(2)}, u32[]{:S(2)}) collective-permute-start(bf16[192,1024]{1,0:T(8,128)(2,1)} %shard_map.110), channel_id=1, source_target_pairs={{4,12},{8,0},{5,13},{9,1},{6,14},{10,2},{7,15},{11,3},{20,28},{24,... | collective-permute-start | bytes 1179656 | tf_op jit(solution)/shard_map/ppermute | solution.py:115
  (26 other events, 112.3 us)

commit v11 on v10

--- a/solution.py
+++ b/solution.py
@@ -120,7 +120,7 @@
 
 
 TOKEN = jax.ShapeDtypeStruct((8, 128), jnp.float32)
-VMEM_LIMIT = 18 * 2**20
+VMEM_LIMIT = 40 * 2**20
 
 
 def on_core(body, out_shape, in_specs, scratch=()):
@@ -437,11 +437,10 @@
         pairs = [(4 * p + i, 4 * p + (i ^ 2)) for p in positions for i in range(4)]
         return lax.ppermute(block, ("blk", "tp"), pairs)
 
-    beside = after(beside, middle)
     inner_last = along(beside, MIDDLE)
-    outer_next = after(along(middle, OUTWARD), flops=3 * 2**30)
+    outer_next = along(middle, OUTWARD)
     beside_far = across_chips(beside)
-    own_far_half = part_of(plan, own_far, own_far, half, half, flops=6 * 2**30)
+    own_far_half = part_of(plan, own_far, own_far, half, half, flops=12 * 2**30)
     inward_far = along(own_far_half, INWARD)
     lend = jnp.concatenate([quarter(1), quarter(3)])
     lent = across_cores(after(lend, own))
@@ -454,7 +453,9 @@
     lent_down = across_cores(lend_down)
 
     outer_last = along(inner_last, OUTWARD)
-    outer_next = after(outer_next, beside_far, lend_down, weights[0], weights[1])
+    outer_next = after(
+        outer_next, beside_far, inner_last, inward_far, lend_down, weights[0], weights[1]
+    )
     second = (middle, outer_next)
     second_far = (at_kind(middle, (1, 2)), at_kind(outer_next, (0, 3)))
     middle_far = along(inward_far, MIDDLE)
@@ -486,16 +487,15 @@
     total, _ = collect(owned, 2, plan, sums_2, got_2, second, total)
     sent, kept = finish(owned, 3, plan, sums_3, got_3, last, total, kept_down, lent_down)
 
-    far = [across_chips(block) for block in sent]
-    first = added(kept[0], far[0])
+    joined = [k + across_chips(s).astype(jnp.float32) for s, k in zip(sent, kept)]
+    first, second, third = [block.astype(jnp.bfloat16) for block in joined[:3]]
+    inward = along(first, INWARD)
     middle = along(first, MIDDLE)
-    inward = along(first, INWARD)
-    second = added(kept[1], far[1], flops=4 * 2**30)
     two_in = along(second, TWO_IN)
-    two_out = along(added(second, inward, middle), TWO_OUT)
-    beside = along(added(kept[2], far[2], flops=4 * 2**30), BESIDE)
-    arrived = [block.astype(jnp.float32) for block in (far[3], middle, two_in, two_out, beside)]
-    return (kept[3] + sum(arrived)).astype(jnp.bfloat16)
+    two_out = along(added(second, inward), TWO_OUT)
+    beside = along(third, BESIDE)
+    arrived = [block.astype(jnp.float32) for block in (middle, two_in, two_out, beside)]
+    return (joined[3] + sum(arrived)).astype(jnp.bfloat16)
 
 
 def on_device(*args):

time: 150 us -> 147 us (0.980)
  waiting for transfers between devices: 41.7 us -> 52.1 us
  Pallas kernels: 38.9 us -> 32.5 us
  starting transfers between devices: 46 us -> 42.3 us
  local copies, waits for them, and re-layouts: 14.1 us -> 11.5 us
    ppermute x7, waiting for transfers between devices: 6.86 us -> 17.4 us  [across_chips(): return lax.ppermute(block, 'tp', [(i, i ^ 2) for i in range(4)])]
    pallas_call x4 -> x1, Pallas kernels: 8.14 us -> 1.95 us  [added(): pl.pallas_call(body, out_shape=jax.ShapeDtypeStruct(block.shape, jnp.bflo...]
    unnamed x44 -> x36, local copies, waits for them, and re-layouts: 8.73 us -> 4.72 us
    ppermute x13, starting transfers between devices: 32.1 us -> 28.2 us  [along(): return lax.ppermute(block, 'blk', route)]
  transfers between devices with their start and end apart: 28 -> 28, of which waited for: 8 -> 10; matrix products, arithmetic and copies ran while one was open for 8% -> 9% of each run, Pallas kernels for 23% -> 20%
where the time goes in v11:
time: 147 us; the launch traced here: 146 us
  waiting for transfers between devices  52.1 us (35%)
  starting transfers between devices  42.3 us (29%)
  Pallas kernels  32.5 us (22%)
  local copies, waits for them, and re-layouts  11.5 us (8%)
  other arithmetic  6.9 us (5%)
    ppermute x13, waiting for transfers between devices, along(): return lax.ppermute(block, 'blk', route)  28.8 us
    ppermute x13, starting transfers between devices, along(): return lax.ppermute(block, 'blk', route)  28.2 us
    ppermute x7, waiting for transfers between devices, across_chips(): return lax.ppermute(block, 'tp', [(i, i ^ 2) for i in range(4)])  17.4 us
    pallas_call x5, Pallas kernels, partial_sums(): return on_core(body, shapes + [TOKEN], specs)(*operands, *waits)  15.1 us
    ppermute x7, starting transfers between devices, across_chips(): return lax.ppermute(block, 'tp', [(i, i ^ 2) for i in range(4)])  8.91 us
    pallas_call x3, Pallas kernels, collect(): on_core(body, [shape, TOKEN], specs, fact_scratch(facts[0].shape[1]))  6.65 us
    ppermute x2, waiting for transfers between devices, at_kind(): return lax.ppermute(block, ('blk', 'tp'), pairs)  5.84 us
    unnamed x36, local copies, waits for them, and re-layouts  4.72 us
  transfers between devices with their start and end apart: 28, of which 10 were waited for; matrix products, arithmetic and copies ran while one was open for 9% of the time, Pallas kernels for 20%

profile of v11, /device:TPU:0, one launch (start us, length us, event | category | flops | bytes accessed | tf_op | source)
XLA Modules:
  0.0 145.7 jit_solution(18392540350107429498)
XLA Ops:
  4.5 3.1 %collective-permute-start = (bf16[400,1024]{1,0:T(8,128)(2,1)S(1)}, bf16[400,1024]{1,0:T(8,128)(2,1)}, u32[]{:S(2)}, u32[]{:S(2)}) collective-permute-start(bf16[400,1024]{1,0:T(8,128)(2,1)S(1)} %shard_map.91.refs_1_.inner_ref.outer_ref), channel_id=1, source_target_pairs={{0,4},{4,0},{8,12},{12,8},{1,5},{5,1},{9,13},{13,9},{2,6},{6,2},{1... | collective-permute-start | bytes 2457608 | tf_op jit(solution)/shard_map/ppermute | solution.py:115
  10.7 3.4 %dynamic-slice_bitcast_fusion.4 = (bf16[1024,256]{1,0:T(8,128)(2,1)S(1)}, bf16[1024,256]{1,0:T(8,128)(2,1)S(1)}, bf16[1024,256]{1,0:T(8,128)(2,1)S(1)}, bf16[102...) fusion(bf16[4,1024,256]{2,1,0:T(8,128)(2,1)} %bitcast.32, ...), kind=kLoop, calls=%fused_computation.13 | loop fusion | bytes 8388624 | tf_op jit(solution)/shard_map/jit(dynamic_index_in_dim)/squeeze | solution.py:424
  16.3 2.7 %dynamic-slice_bitcast_fusion.1 = (bf16[256,1024]{1,0:T(8,128)(2,1)}, bf16[256,1024]{1,0:T(8,128)(2,1)S(1)}, bf16[256,1024]{1,0:T(8,128)(2,1)S(1)}, bf16[256,1024]{1,0:T(8,128)(2,1)}) fusion(bf16[1,256,4096]{2,1,0:T(8,128)(2,1)} %param.12, s32[]{:T(128)S(6)} %select_n.39, s32[]{:T(128)S(6)} %select_n.34, s32[]{:T(128)S(6)} %select_n.33, s32[]{:T(128)S(6)} %select_n.40), kind=kLoop, calls=%fused_computation.10 | loop fusion | bytes 4194320 | tf_op jit(solution)/shard_map/dynamic_slice | solution.py:430
  19.0 7.0 %collective-permute-done.refs_0_.inner_ref.outer_ref = bf16[400,1024]{1,0:T(8,128)(2,1)} collective-permute-done((bf16[400,1024]{1,0:T(8,128)(2,1)S(1)}, bf16[400,1024]{1,0:T(8,128)(2,1)}, u32[]{:S(2)}, u32[]{:S(2)}) %collective-permute-start) | collective-permute-done | bytes 819232 | tf_op jit(solution)/shard_map/ppermute | solution.py:115
  32.6 6.4 %collective-permute-start.8 = (bf16[192,1024]{1,0:T(8,128)(2,1)S(1)}, bf16[192,1024]{1,0:T(8,128)(2,1)S(1)}, u32[]{:S(2)}, u32[]{:S(2)}) collective-permute-start(bf16[192,1024]{1,0:T(8,128)(2,1)S(1)} %shard_map.92), channel_id=1, source_target_pairs={{0,4},{12,8},{1,5},{13,9},{2,6},{14,10},{3,7},{15,11},{16,20},{28,... | collective-permute-start | bytes 1179656 | tf_op jit(solution)/shard_map/ppermute | solution.py:115
  42.2 3.7 %collective-permute-done.8.refs_3_ = bf16[192,1024]{1,0:T(8,128)(2,1)S(1)} collective-permute-done((bf16[192,1024]{1,0:T(8,128)(2,1)S(1)}, bf16[192,1024]{1,0:T(8,128)(2,1)S(1)}, u32[]{:S(2)}, u32[]{:S(2)}) %collective-permute-start.8) | collective-permute-done | bytes 393248 | tf_op jit(solution)/shard_map/ppermute | solution.py:115
  48.3 2.9 %collective-permute-done.5.refs_0_ = bf16[400,1024]{1,0:T(8,128)(2,1)} collective-permute-done((bf16[400,1024]{1,0:T(8,128)(2,1)}, bf16[400,1024]{1,0:T(8,128)(2,1)}, u32[]{:S(2)}, u32[]{:S(2)}) %collective-permute-start.5) | collective-permute-done | bytes 819232 | tf_op jit(solution)/shard_map/ppermute | solution.py:115
  51.2 2.4 %collective-permute-start.9 = (bf16[400,1024]{1,0:T(8,128)(2,1)}, bf16[400,1024]{1,0:T(8,128)(2,1)S(1)}, u32[]{:S(2)}, u32[]{:S(2)}) collective-permute-start(bf16[400,1024]{1,0:T(8,128)(2,1)} %shard_map.93.refs_1_.outer_ref), channel_id=1, source_target_pairs={{0,2},{1,3},{2,0},{3,1},{12,14},{13,15},{14,12},{15,13},{16,18},{1... | collective-permute-start | bytes 2457608 | tf_op jit(solution)/shard_map/ppermute | solution.py:438
  56.8 3.2 %shard_map.95 = (f32[384,1024]{1,0:T(8,128)S(1)}, bf16[384,1024]{1,0:T(8,128)(2,1)S(1)}, f32[8,128]{1,0:T(8,128)S(1)}) custom-call(s32[9]{0:T(128)S(1)} %fusion.plan_ref, bf16[384,1024]{1,0:T(8,128)(2,1)} %refs_0_.1, bf16[384,1024]{1,0:T(8,128)(2,1)} %collective-permute-done.7.inner_ref.outer_ref.refs_1_, bf16[1024,512]{1,0:T(8,128)(2,1)S(1)} %copy-done.1, ...), custom_call_target="tpu_custom_call" | custom-call | flops 1024 | bytes 1024 | tf_op jit(solution)/shard_map/pallas_call | solution.py:287
  60.1 3.2 %shard_map.96 = (f32[384,1024]{1,0:T(8,128)S(1)}, bf16[384,1024]{1,0:T(8,128)(2,1)S(1)}, f32[8,128]{1,0:T(8,128)S(1)}) custom-call(s32[9]{0:T(128)S(1)} %fusion.plan_ref, bf16[400,1024]{1,0:T(8,128)(2,1)} %collective-permute-done.refs_0_.inner_ref.outer_ref, bf16[400,1024]{1,0:T(8,128)(2,1)} %collective-permute-done.6.refs_1_, ...), custom_call_target="tpu_custom_call" | custom-call | flops 1024 | bytes 1024 | tf_op jit(solution)/shard_map/pallas_call | solution.py:287
  65.3 5.8 %collective-permute-done.9.rest_1_.refs_3_ = bf16[400,1024]{1,0:T(8,128)(2,1)S(1)} collective-permute-done((bf16[400,1024]{1,0:T(8,128)(2,1)}, bf16[400,1024]{1,0:T(8,128)(2,1)S(1)}, u32[]{:S(2)}, u32[]{:S(2)}) %collective-permute-start.9) | collective-permute-done | bytes 819232 | tf_op jit(solution)/shard_map/ppermute | solution.py:438
  71.2 3.5 %collective-permute-done.2.outer_ref.refs_1_ = bf16[400,1024]{1,0:T(8,128)(2,1)S(1)} collective-permute-done((bf16[400,1024]{1,0:T(8,128)(2,1)}, bf16[400,1024]{1,0:T(8,128)(2,1)S(1)}, u32[]{:S(2)}, u32[]{:S(2)}) %collective-permute-start.2) | collective-permute-done | bytes 819232 | tf_op jit(solution)/shard_map/ppermute | solution.py:115
  77.9 4.0 %shard_map.102 = (f32[384,1024]{1,0:T(8,128)S(1)}, bf16[384,1024]{1,0:T(8,128)(2,1)S(1)}, f32[8,128]{1,0:T(8,128)}) custom-call(s32[9]{0:T(128)S(1)} %fusion.plan_ref, bf16[400,1024]{1,0:T(8,128)(2,1)} %collective-permute-done.3.refs_0_.inner_ref, bf16[400,1024]{1,0:T(8,128)(2,1)} %shard_map.93.refs_1_.outer_ref, ...), custom_call_target="tpu_custom_call" | custom-call | flops 1024 | bytes 1024 | tf_op jit(solution)/shard_map/pallas_call | solution.py:287
  81.8 2.7 %shard_map.98 = (f32[384,1024]{1,0:T(8,128)S(1)}, f32[8,128]{1,0:T(8,128)}) custom-call(s32[9]{0:T(128)S(1)} %fusion.plan_ref, bf16[400,1024]{1,0:T(8,128)(2,1)} %collective-permute-done.1.refs_2_.inner_ref.refs_0_, bf16[400,1024]{1,0:T(8,128)(2,1)S(1)} %collective-permute-done.2.outer_ref.refs_1_, bf16[1024,512]{1,0:T(8,128)(2,1)S(1)} %copy-done.2, ...), custom_call_target="tpu_custom_call" | custom-call | flops 1024 | bytes 1024 | tf_op jit(solution)/shard_map/pallas_call | solution.py:287
  87.0 2.1 %shard_map.100 = (f32[768,512]{1,0:T(8,128)S(1)}, f32[8,128]{1,0:T(8,128)S(1)}) custom-call(s32[9]{0:T(128)S(1)} %fusion.plan_ref, f32[384,1024]{1,0:T(8,128)S(1)} %get-tuple-element.32.sums_ref, bf16[384,1024]{1,0:T(8,128)(2,1)S(1)} %collective-permute-done.14.got_ref, bf16[400,1024]{1,0:T(8,128)(2,1)} %collective-permute-done.refs_0_.inner_ref.outer_ref, ...), custom_call_target="tpu_custom_call" | custom-call | flops 1024 | bytes 1024 | tf_op jit(solution)/shard_map/pallas_call | solution.py:346
  89.1 2.0 %shard_map.101 = (f32[384,1024]{1,0:T(8,128)S(1)}, bf16[384,1024]{1,0:T(8,128)(2,1)S(1)}, f32[8,128]{1,0:T(8,128)}) custom-call(s32[9]{0:T(128)S(1)} %fusion.plan_ref, bf16[192,1024]{1,0:T(8,128)(2,1)S(1)} %collective-permute-done.12.refs_0_, bf16[192,1024]{1,0:T(8,128)(2,1)S(1)} %collective-permute-done.10.rest_2_.refs_1_, ...), custom_call_target="tpu_custom_call" | custom-call | flops 1024 | bytes 1024 | tf_op jit(solution)/shard_map/pallas_call | solution.py:287
  91.3 2.6 %shard_map.103 = (f32[768,512]{1,0:T(8,128)S(1)}, f32[8,128]{1,0:T(8,128)}) custom-call(s32[9]{0:T(128)S(1)} %fusion.plan_ref, f32[384,1024]{1,0:T(8,128)S(1)} %get-tuple-element.40.sums_ref, bf16[384,1024]{1,0:T(8,128)(2,1)S(1)} %collective-permute-done.17.got_ref, bf16[400,1024]{1,0:T(8,128)(2,1)} %collective-permute-done.3.refs_0_.inner_ref, ...), custom_call_target="tpu_custom_call" | custom-call | flops 1024 | bytes 1024 | tf_op jit(solution)/shard_map/pallas_call | solution.py:346
  101.6 6.4 %collective-permute-done.20 = bf16[192,1024]{1,0:T(8,128)(2,1)S(1)} collective-permute-done((bf16[192,1024]{1,0:T(8,128)(2,1)S(1)}, bf16[192,1024]{1,0:T(8,128)(2,1)S(1)}, u32[]{:S(2)}, u32[]{:S(2)}) %collective-permute-start.20) | collective-permute-done | bytes 393248 | tf_op jit(solution)/shard_map/ppermute | solution.py:107
  108.0 3.2 %collective-permute-start.24 = (bf16[192,1024]{1,0:T(8,128)(2,1)S(1)}, bf16[192,1024]{1,0:T(8,128)(2,1)}, u32[]{:S(2)}, u32[]{:S(2)}) collective-permute-start(bf16[192,1024]{1,0:T(8,128)(2,1)S(1)} %add_convert_fusion.3), channel_id=1, source_target_pairs={{0,4},{12,8},{1,5},{13,9},{2,6},{14,10},{3,7},{15,11},{16,20},{28,... | collective-permute-start | bytes 1179656 | tf_op jit(solution)/shard_map/ppermute | solution.py:115
  111.9 4.5 %collective-permute-done.22 = bf16[192,1024]{1,0:T(8,128)(2,1)S(1)} collective-permute-done((bf16[192,1024]{1,0:T(8,128)(2,1)S(1)}, bf16[192,1024]{1,0:T(8,128)(2,1)S(1)}, u32[]{:S(2)}, u32[]{:S(2)}) %collective-permute-start.22) | collective-permute-done | bytes 393248 | tf_op jit(solution)/shard_map/ppermute | solution.py:107
  116.5 5.2 %collective-permute-start.23 = (bf16[192,1024]{1,0:T(8,128)(2,1)S(1)}, bf16[192,1024]{1,0:T(8,128)(2,1)S(1)}, u32[]{:S(2)}, u32[]{:S(2)}) collective-permute-start(bf16[192,1024]{1,0:T(8,128)(2,1)S(1)} %add_convert_fusion.2.block_ref), channel_id=1, source_target_pairs={{0,8},{12,4},{1,9},{13,5},{2,10},{14,6},{3,11},{15,7},{16,24},{28,... | collective-permute-start | bytes 1179656 | tf_op jit(solution)/shard_map/ppermute | solution.py:115
  121.7 3.1 %collective-permute-done.26 = bf16[192,1024]{1,0:T(8,128)(2,1)S(1)} collective-permute-done((bf16[192,1024]{1,0:T(8,128)(2,1)S(1)}, bf16[192,1024]{1,0:T(8,128)(2,1)S(1)}, u32[]{:S(2)}, u32[]{:S(2)}) %collective-permute-start.26) | collective-permute-done | bytes 393248 | tf_op jit(solution)/shard_map/ppermute | solution.py:107
  129.4 3.4 %collective-permute-done.19 = bf16[192,1024]{1,0:T(8,128)(2,1)S(1)} collective-permute-done((bf16[192,1024]{1,0:T(8,128)(2,1)S(1)}, bf16[192,1024]{1,0:T(8,128)(2,1)S(1)}, u32[]{:S(2)}, u32[]{:S(2)}) %collective-permute-start.19) | collective-permute-done | bytes 393248 | tf_op jit(solution)/shard_map/ppermute | solution.py:107
  132.8 11.8 %collective-permute-done.27 = bf16[192,1024]{1,0:T(8,128)(2,1)S(1)} collective-permute-done((bf16[192,1024]{1,0:T(8,128)(2,1)}, bf16[192,1024]{1,0:T(8,128)(2,1)S(1)}, u32[]{:S(2)}, u32[]{:S(2)}) %collective-permute-start.27) | collective-permute-done | bytes 393248 | tf_op jit(solution)/shard_map/ppermute | solution.py:115
  (96 shorter events, 47.0 us)
Async XLA Ops:
  4.5 21.4 %collective-permute-start = (bf16[400,1024]{1,0:T(8,128)(2,1)S(1)}, bf16[400,1024]{1,0:T(8,128)(2,1)}, u32[]{:S(2)}, u32[]{:S(2)}) collective-permute-start(bf16[400,1024]{1,0:T(8,128)(2,1)S(1)} %shard_map.91.refs_1_.inner_ref.outer_ref), channel_id=1, source_target_pairs={{0,4},{4,0},{8,12},{12,8},{1,5},{5,1},{9,13},{13,9},{2,6},{6,2},{1... | collective-permute-start | bytes 2457608 | tf_op jit(solution)/shard_map/ppermute | solution.py:115
  7.6 21.6 %collective-permute-start.3 = (bf16[400,1024]{1,0:T(8,128)(2,1)S(1)}, bf16[400,1024]{1,0:T(8,128)(2,1)}, u32[]{:S(2)}, u32[]{:S(2)}) collective-permute-start(bf16[400,1024]{1,0:T(8,128)(2,1)S(1)} %shard_map.91.refs_1_.inner_ref.outer_ref), channel_id=1, source_target_pairs={{4,8},{8,4},{5,9},{9,5},{6,10},{10,6},{7,11},{11,7},{20,24},{24,20... | collective-permute-start | bytes 2457608 | tf_op jit(solution)/shard_map/ppermute | solution.py:115
  9.2 21.4 %collective-permute-start.7 = (bf16[384,1024]{1,0:T(8,128)(2,1)}, bf16[384,1024]{1,0:T(8,128)(2,1)}, u32[]{:S(2)}, u32[]{:S(2)}) collective-permute-start(bf16[384,1024]{1,0:T(8,128)(2,1)} %refs_0_.1), channel_id=1, source_target_pairs={{0,2},{1,3},{2,0},{3,1},{4,6},{5,7},{6,4},{7,5},{8,10},{9,11},{10,... | collective-permute-start | bytes 2359304 | tf_op jit(solution)/shard_map/ppermute | solution.py:107
  15.6 40.0 %collective-permute-start.11 = (bf16[2048,512]{1,0:T(8,128)(2,1)}, bf16[2048,512]{1,0:T(8,128)(2,1)S(1)}, u32[]{:S(2)}, u32[]{:S(2)}) collective-permute-start(bf16[2048,512]{1,0:T(8,128)(2,1)} %shard_map.94), channel_id=1, source_target_pairs={{0,1},{1,0},{2,3},{3,2},{4,5},{5,4},{6,7},{7,6},{8,9},{9,8},{10,11... | collective-permute-start | bytes 6291464 | tf_op jit(solution)/shard_map/ppermute | solution.py:111
  26.0 22.3 %collective-permute-start.1 = (bf16[400,1024]{1,0:T(8,128)(2,1)}, bf16[400,1024]{1,0:T(8,128)(2,1)}, u32[]{:S(2)}, u32[]{:S(2)}) collective-permute-start(bf16[400,1024]{1,0:T(8,128)(2,1)} %collective-permute-done.refs_0_.inner_ref.outer_ref), channel_id=1, source_target_pairs={{4,8},{8,4},{5,9},{9,5},{6,10},{10,6},{7,11},{11,7},{20,24},{24,20... | collective-permute-start | bytes 2457608 | tf_op jit(solution)/shard_map/ppermute | solution.py:115
  27.6 20.6 %collective-permute-start.6 = (bf16[400,1024]{1,0:T(8,128)(2,1)}, bf16[400,1024]{1,0:T(8,128)(2,1)}, u32[]{:S(2)}, u32[]{:S(2)}) collective-permute-start(bf16[400,1024]{1,0:T(8,128)(2,1)} %collective-permute-done.refs_0_.inner_ref.outer_ref), channel_id=1, source_target_pairs={{0,2},{1,3},{2,0},{3,1},{4,6},{5,7},{6,4},{7,5},{8,10},{9,11},{10,... | collective-permute-start | bytes 2457608 | tf_op jit(solution)/shard_map/ppermute | solution.py:107
  29.3 21.9 %collective-permute-start.5 = (bf16[400,1024]{1,0:T(8,128)(2,1)}, bf16[400,1024]{1,0:T(8,128)(2,1)}, u32[]{:S(2)}, u32[]{:S(2)}) collective-permute-start(bf16[400,1024]{1,0:T(8,128)(2,1)} %collective-permute-done.3.refs_0_.inner_ref), channel_id=1, source_target_pairs={{4,0},{8,12},{5,1},{9,13},{6,2},{10,14},{7,3},{11,15},{20,16},{24,... | collective-permute-start | bytes 2457608 | tf_op jit(solution)/shard_map/ppermute | solution.py:115
  32.6 13.4 %collective-permute-start.8 = (bf16[192,1024]{1,0:T(8,128)(2,1)S(1)}, bf16[192,1024]{1,0:T(8,128)(2,1)S(1)}, u32[]{:S(2)}, u32[]{:S(2)}) collective-permute-start(bf16[192,1024]{1,0:T(8,128)(2,1)S(1)} %shard_map.92), channel_id=1, source_target_pairs={{0,4},{12,8},{1,5},{13,9},{2,6},{14,10},{3,7},{15,11},{16,20},{28,... | collective-permute-start | bytes 1179656 | tf_op jit(solution)/shard_map/ppermute | solution.py:115
  46.7 17.2 %collective-permute-start.4 = (bf16[400,1024]{1,0:T(8,128)(2,1)}, bf16[400,1024]{1,0:T(8,128)(2,1)}, u32[]{:S(2)}, u32[]{:S(2)}) collective-permute-start(bf16[400,1024]{1,0:T(8,128)(2,1)} %collective-permute-done.3.refs_0_.inner_ref), channel_id=1, source_target_pairs={{4,6},{5,7},{6,4},{7,5},{8,10},{9,11},{10,8},{11,9},{20,22},{21,23... | collective-permute-start | bytes 2457608 | tf_op jit(solution)/shard_map/ppermute | solution.py:438
  51.2 20.0 %collective-permute-start.9 = (bf16[400,1024]{1,0:T(8,128)(2,1)}, bf16[400,1024]{1,0:T(8,128)(2,1)S(1)}, u32[]{:S(2)}, u32[]{:S(2)}) collective-permute-start(bf16[400,1024]{1,0:T(8,128)(2,1)} %shard_map.93.refs_1_.outer_ref), channel_id=1, source_target_pairs={{0,2},{1,3},{2,0},{3,1},{12,14},{13,15},{14,12},{15,13},{16,18},{1... | collective-permute-start | bytes 2457608 | tf_op jit(solution)/shard_map/ppermute | solution.py:438
  53.6 21.0 %collective-permute-start.2 = (bf16[400,1024]{1,0:T(8,128)(2,1)}, bf16[400,1024]{1,0:T(8,128)(2,1)S(1)}, u32[]{:S(2)}, u32[]{:S(2)}) collective-permute-start(bf16[400,1024]{1,0:T(8,128)(2,1)} %collective-permute-done.1.refs_2_.inner_ref.refs_0_), channel_id=1, source_target_pairs={{4,0},{8,12},{5,1},{9,13},{6,2},{10,14},{7,3},{11,15},{20,16},{24,... | collective-permute-start | bytes 2457608 | tf_op jit(solution)/shard_map/ppermute | solution.py:115
  60.0 24.5 %collective-permute-start.15 = (bf16[384,1024]{1,0:T(8,128)(2,1)S(1)}, bf16[384,1024]{1,0:T(8,128)(2,1)S(1)}, u32[]{:S(2)}, u32[]{:S(2)}) collective-permute-start(bf16[384,1024]{1,0:T(8,128)(2,1)S(1)} %get-tuple-element.35), channel_id=1, source_target_pairs={{0,1},{1,0},{2,3},{3,2},{4,5},{5,4},{6,7},{7,6},{8,9},{9,8},{10,11... | collective-permute-start | bytes 2359304 | tf_op jit(solution)/shard_map/ppermute | solution.py:111
  63.3 23.6 %collective-permute-start.14 = (bf16[384,1024]{1,0:T(8,128)(2,1)S(1)}, bf16[384,1024]{1,0:T(8,128)(2,1)S(1)}, u32[]{:S(2)}, u32[]{:S(2)}) collective-permute-start(bf16[384,1024]{1,0:T(8,128)(2,1)S(1)} %get-tuple-element.33), channel_id=1, source_target_pairs={{0,1},{1,0},{2,3},{3,2},{4,5},{5,4},{6,7},{7,6},{8,9},{9,8},{10,11... | collective-permute-start | bytes 2359304 | tf_op jit(solution)/shard_map/ppermute | solution.py:111
  63.9 25.2 %collective-permute-start.13 = (bf16[192,1024]{1,0:T(8,128)(2,1)S(1)}, bf16[192,1024]{1,0:T(8,128)(2,1)S(1)}, u32[]{:S(2)}, u32[]{:S(2)}) collective-permute-start(bf16[192,1024]{1,0:T(8,128)(2,1)S(1)} %collective-permute-done.10.rest_2_.refs_1_), channel_id=1, source_target_pairs={{4,0},{8,12},{5,1},{9,13},{6,2},{10,14},{7,3},{11,15},{20,16},{24,... | collective-permute-start | bytes 1179656 | tf_op jit(solution)/shard_map/ppermute | solution.py:115
  76.3 12.8 %collective-permute-start.12 = (bf16[192,1024]{1,0:T(8,128)(2,1)S(1)}, bf16[192,1024]{1,0:T(8,128)(2,1)S(1)}, u32[]{:S(2)}, u32[]{:S(2)}) collective-permute-start(bf16[192,1024]{1,0:T(8,128)(2,1)S(1)} %shard_map.97), channel_id=1, source_target_pairs={{0,2},{1,3},{2,0},{3,1},{4,6},{5,7},{6,4},{7,5},{8,10},{9,11},{10,... | collective-permute-start | bytes 1179656 | tf_op jit(solution)/shard_map/ppermute | solution.py:107
  77.9 16.0 %collective-permute-start.18 = (bf16[256,2048]{1,0:T(8,128)(2,1)S(1)}, bf16[256,2048]{1,0:T(8,128)(2,1)S(1)}, u32[]{:S(2)}, u32[]{:S(2)}) collective-permute-start(bf16[256,2048]{1,0:T(8,128)(2,1)S(1)} %copy-done.9), channel_id=1, source_target_pairs={{0,1},{1,0},{2,3},{3,2},{4,5},{5,4},{6,7},{7,6},{8,9},{9,8},{10,11... | collective-permute-start | bytes 3145736 | tf_op jit(solution)/shard_map/ppermute | solution.py:111
  98.0 18.4 %collective-permute-start.22 = (bf16[192,1024]{1,0:T(8,128)(2,1)S(1)}, bf16[192,1024]{1,0:T(8,128)(2,1)S(1)}, u32[]{:S(2)}, u32[]{:S(2)}) collective-permute-start(bf16[192,1024]{1,0:T(8,128)(2,1)S(1)} %get-tuple-element.50), channel_id=1, source_target_pairs={{0,2},{1,3},{2,0},{3,1},{4,6},{5,7},{6,4},{7,5},{8,10},{9,11},{10,... | collective-permute-start | bytes 1179656 | tf_op jit(solution)/shard_map/ppermute | solution.py:107
  99.5 25.3 %collective-permute-start.26 = (bf16[192,1024]{1,0:T(8,128)(2,1)S(1)}, bf16[192,1024]{1,0:T(8,128)(2,1)S(1)}, u32[]{:S(2)}, u32[]{:S(2)}) collective-permute-start(bf16[192,1024]{1,0:T(8,128)(2,1)S(1)} %get-tuple-element.52), channel_id=1, source_target_pairs={{0,2},{1,3},{2,0},{3,1},{4,6},{5,7},{6,4},{7,5},{8,10},{9,11},{10,... | collective-permute-start | bytes 1179656 | tf_op jit(solution)/shard_map/ppermute | solution.py:107
  100.1 32.8 %collective-permute-start.19 = (bf16[192,1024]{1,0:T(8,128)(2,1)S(1)}, bf16[192,1024]{1,0:T(8,128)(2,1)S(1)}, u32[]{:S(2)}, u32[]{:S(2)}) collective-permute-start(bf16[192,1024]{1,0:T(8,128)(2,1)S(1)} %get-tuple-element.46), channel_id=1, source_target_pairs={{0,2},{1,3},{2,0},{3,1},{4,6},{5,7},{6,4},{7,5},{8,10},{9,11},{10,... | collective-permute-start | bytes 1179656 | tf_op jit(solution)/shard_map/ppermute | solution.py:107
  108.0 18.1 %collective-permute-start.24 = (bf16[192,1024]{1,0:T(8,128)(2,1)S(1)}, bf16[192,1024]{1,0:T(8,128)(2,1)}, u32[]{:S(2)}, u32[]{:S(2)}) collective-permute-start(bf16[192,1024]{1,0:T(8,128)(2,1)S(1)} %add_convert_fusion.3), channel_id=1, source_target_pairs={{0,4},{12,8},{1,5},{13,9},{2,6},{14,10},{3,7},{15,11},{16,20},{28,... | collective-permute-start | bytes 1179656 | tf_op jit(solution)/shard_map/ppermute | solution.py:115
  111.2 21.6 %collective-permute-start.21 = (bf16[192,1024]{1,0:T(8,128)(2,1)S(1)}, bf16[192,1024]{1,0:T(8,128)(2,1)S(1)}, u32[]{:S(2)}, u32[]{:S(2)}) collective-permute-start(bf16[192,1024]{1,0:T(8,128)(2,1)S(1)} %add_convert_fusion.3), channel_id=1, source_target_pairs={{4,8},{8,4},{5,9},{9,5},{6,10},{10,6},{7,11},{11,7},{20,24},{24,20... | collective-permute-start | bytes 1179656 | tf_op jit(solution)/shard_map/ppermute | solution.py:115
  116.5 16.4 %collective-permute-start.23 = (bf16[192,1024]{1,0:T(8,128)(2,1)S(1)}, bf16[192,1024]{1,0:T(8,128)(2,1)S(1)}, u32[]{:S(2)}, u32[]{:S(2)}) collective-permute-start(bf16[192,1024]{1,0:T(8,128)(2,1)S(1)} %add_convert_fusion.2.block_ref), channel_id=1, source_target_pairs={{0,8},{12,4},{1,9},{13,5},{2,10},{14,6},{3,11},{15,7},{16,24},{28,... | collective-permute-start | bytes 1179656 | tf_op jit(solution)/shard_map/ppermute | solution.py:115
  125.6 19.0 %collective-permute-start.27 = (bf16[192,1024]{1,0:T(8,128)(2,1)}, bf16[192,1024]{1,0:T(8,128)(2,1)S(1)}, u32[]{:S(2)}, u32[]{:S(2)}) collective-permute-start(bf16[192,1024]{1,0:T(8,128)(2,1)} %add_convert_fusion.1), channel_id=1, source_target_pairs={{0,4},{4,0},{8,12},{12,8},{1,5},{5,1},{9,13},{13,9},{2,6},{6,2},{1... | collective-permute-start | bytes 1179656 | tf_op jit(solution)/shard_map/ppermute | solution.py:115
  128.1 16.5 %collective-permute-start.25 = (bf16[192,1024]{1,0:T(8,128)(2,1)}, bf16[192,1024]{1,0:T(8,128)(2,1)S(1)}, u32[]{:S(2)}, u32[]{:S(2)}) collective-permute-start(bf16[192,1024]{1,0:T(8,128)(2,1)} %shard_map.106), channel_id=1, source_target_pairs={{4,12},{8,0},{5,13},{9,1},{6,14},{10,2},{7,15},{11,3},{20,28},{24,... | collective-permute-start | bytes 1179656 | tf_op jit(solution)/shard_map/ppermute | solution.py:115
  (22 other events, 157.9 us)

commit v12 on v11

--- a/solution.py
+++ b/solution.py
@@ -346,20 +346,6 @@
     return on_core(body, [shape, TOKEN], specs, fact_scratch(facts[0].shape[1]))(*operands)
 
 
-def added(block, other, *waits, flops=1024):
-    def body(block_ref, other_ref, *rest):
-        total = block_ref[...].astype(jnp.float32) + other_ref[...].astype(jnp.float32)
-        rest[-1][...] = total.astype(jnp.bfloat16)
-
-    return pl.pallas_call(
-        body,
-        out_shape=jax.ShapeDtypeStruct(block.shape, jnp.bfloat16),
-        in_specs=[VMEM, VMEM] + [ANYWHERE] * len(waits),
-        out_specs=VMEM,
-        cost_estimate=pl.CostEstimate(flops=flops, bytes_accessed=1024, transcendentals=0),
-    )(block, other, *waits)
-
-
 def down(held, own_ref, lent_ref, sent_ref, kept_ref):
     units, width = own_ref.shape[0], kept_ref.shape[1]
     for out, at in ((kept_ref, slice(0, width)), (sent_ref, slice(width, 2 * width))):
@@ -440,7 +426,7 @@
     inner_last = along(beside, MIDDLE)
     outer_next = along(middle, OUTWARD)
     beside_far = across_chips(beside)
-    own_far_half = part_of(plan, own_far, own_far, half, half, flops=12 * 2**30)
+    own_far_half = part_of(plan, own_far, own_far, half, half, flops=16 * 2**30)
     inward_far = along(own_far_half, INWARD)
     lend = jnp.concatenate([quarter(1), quarter(3)])
     lent = across_cores(after(lend, own))
@@ -454,7 +440,7 @@
 
     outer_last = along(inner_last, OUTWARD)
     outer_next = after(
-        outer_next, beside_far, inner_last, inward_far, lend_down, weights[0], weights[1]
+        outer_next, beside_far, inner_last, inward_far, lend_down, weights[0], weights[1], ready_0
     )
     second = (middle, outer_next)
     second_far = (at_kind(middle, (1, 2)), at_kind(outer_next, (0, 3)))
@@ -489,13 +475,16 @@
 
     joined = [k + across_chips(s).astype(jnp.float32) for s, k in zip(sent, kept)]
     first, second, third = [block.astype(jnp.bfloat16) for block in joined[:3]]
+    second = lax.optimization_barrier(second)
     inward = along(first, INWARD)
     middle = along(first, MIDDLE)
     two_in = along(second, TWO_IN)
-    two_out = along(added(second, inward), TWO_OUT)
+    passed = second.astype(jnp.float32) + inward.astype(jnp.float32)
+    two_out = along(passed.astype(jnp.bfloat16), TWO_OUT)
     beside = along(third, BESIDE)
-    arrived = [block.astype(jnp.float32) for block in (middle, two_in, two_out, beside)]
-    return (joined[3] + sum(arrived)).astype(jnp.bfloat16)
+    arrived = [block.astype(jnp.float32) for block in (middle, two_in, two_out)]
+    total = lax.optimization_barrier(joined[3] + sum(arrived))
+    return (total + beside.astype(jnp.float32)).astype(jnp.bfloat16)
 
 
 def on_device(*args):

time: 147 us -> 144 us (0.980)
  waiting for transfers between devices: 52.1 us -> 45.2 us
  starting transfers between devices: 42.3 us -> 47 us
  local copies, waits for them, and re-layouts: 11.5 us -> 15.5 us
  other arithmetic: 6.9 us -> 4.48 us
  Pallas kernels: 32.5 us -> 30.7 us
    ppermute x13, starting transfers between devices: 28.2 us -> 33.8 us  [along(): return lax.ppermute(block, 'blk', route)]
    unnamed x36 -> x56, local copies, waits for them, and re-layouts: 4.72 us -> 8.75 us
    ppermute x7, waiting for transfers between devices: 17.4 us -> 13.4 us  [across_chips(): return lax.ppermute(block, 'tp', [(i, i ^ 2) for i in range(4)])]
    ppermute x2, waiting for transfers between devices: 5.84 us -> 1.9 us  [at_kind(): return lax.ppermute(block, ('blk', 'tp'), pairs)]
    concatenate x2, other arithmetic: 2.14 us -> 0.15 us  [quarter(): return jnp.concatenate(pair, axis=1)]
    pallas_call x1 -> x0, Pallas kernels: 1.95 us -> none  [added(): pl.pallas_call(body, out_shape=jax.ShapeDtypeStruct(block.shape, jnp.bflo...]
  transfers between devices with their start and end apart: 28 -> 28, of which waited for: 10 -> 10; matrix products, arithmetic and copies ran while one was open for 9% -> 7% of each run, Pallas kernels for 20% -> 18%
where the time goes in v12:
time: 144 us; the launch traced here: 143 us
  starting transfers between devices  47 us (33%)
  waiting for transfers between devices  45.2 us (31%)
  Pallas kernels  30.7 us (21%)
  local copies, waits for them, and re-layouts  15.5 us (11%)
  other arithmetic  4.48 us (3%)
    ppermute x13, starting transfers between devices, along(): return lax.ppermute(block, 'blk', route)  33.8 us
    ppermute x13, waiting for transfers between devices, along(): return lax.ppermute(block, 'blk', route)  29.9 us
    pallas_call x5, Pallas kernels, partial_sums(): return on_core(body, shapes + [TOKEN], specs)(*operands, *waits)  14.8 us
    ppermute x7, waiting for transfers between devices, across_chips(): return lax.ppermute(block, 'tp', [(i, i ^ 2) for i in range(4)])  13.4 us
    unnamed x56, local copies, waits for them, and re-layouts  8.75 us
    ppermute x7, starting transfers between devices, across_chips(): return lax.ppermute(block, 'tp', [(i, i ^ 2) for i in range(4)])  8 us
    pallas_call x3, Pallas kernels, collect(): on_core(body, [shape, TOKEN], specs, fact_scratch(facts[0].shape[1]))  6.13 us
    ppermute x2, starting transfers between devices, at_kind(): return lax.ppermute(block, ('blk', 'tp'), pairs)  4.11 us
  transfers between devices with their start and end apart: 28, of which 10 were waited for; matrix products, arithmetic and copies ran while one was open for 7% of the time, Pallas kernels for 18%

profile of v12, /device:TPU:0, one launch (start us, length us, event | category | flops | bytes accessed | tf_op | source)
XLA Modules:
  0.0 143.4 jit_solution(15735170187369533662)
XLA Ops:
  4.5 3.1 %collective-permute-start = (bf16[400,1024]{1,0:T(8,128)(2,1)S(1)}, bf16[400,1024]{1,0:T(8,128)(2,1)}, u32[]{:S(2)}, u32[]{:S(2)}) collective-permute-start(bf16[400,1024]{1,0:T(8,128)(2,1)S(1)} %shard_map.91.refs_1_.inner_ref.outer_ref), channel_id=1, source_target_pairs={{0,4},{4,0},{8,12},{12,8},{1,5},{5,1},{9,13},{13,9},{2,6},{6,2},{1... | collective-permute-start | bytes 2457608 | tf_op jit(solution)/shard_map/ppermute | solution.py:115
  10.7 3.4 %dynamic-slice_bitcast_fusion.4 = (bf16[1024,256]{1,0:T(8,128)(2,1)S(1)}, bf16[1024,256]{1,0:T(8,128)(2,1)S(1)}, bf16[1024,256]{1,0:T(8,128)(2,1)S(1)}, bf16[102...) fusion(bf16[4,1024,256]{2,1,0:T(8,128)(2,1)} %bitcast.32, ...), kind=kLoop, calls=%fused_computation.15 | loop fusion | bytes 8388624 | tf_op jit(solution)/shard_map/jit(dynamic_index_in_dim)/squeeze | solution.py:410
  16.2 2.7 %dynamic-slice_bitcast_fusion.1 = (bf16[256,1024]{1,0:T(8,128)(2,1)}, bf16[256,1024]{1,0:T(8,128)(2,1)S(1)}, bf16[256,1024]{1,0:T(8,128)(2,1)S(1)}, bf16[256,1024]{1,0:T(8,128)(2,1)}) fusion(bf16[1,256,4096]{2,1,0:T(8,128)(2,1)} %param.12, s32[]{:T(128)S(6)} %select_n.39, s32[]{:T(128)S(6)} %select_n.34, s32[]{:T(128)S(6)} %select_n.33, s32[]{:T(128)S(6)} %select_n.40), kind=kLoop, calls=%fused_computation.12 | loop fusion | bytes 4194320 | tf_op jit(solution)/shard_map/dynamic_slice | solution.py:416
  18.9 7.1 %collective-permute-done.refs_0_.inner_ref.outer_ref = bf16[400,1024]{1,0:T(8,128)(2,1)} collective-permute-done((bf16[400,1024]{1,0:T(8,128)(2,1)S(1)}, bf16[400,1024]{1,0:T(8,128)(2,1)}, u32[]{:S(2)}, u32[]{:S(2)}) %collective-permute-start) | collective-permute-done | bytes 819232 | tf_op jit(solution)/shard_map/ppermute | solution.py:115
  32.6 5.6 %collective-permute-start.8 = (bf16[192,1024]{1,0:T(8,128)(2,1)S(1)}, bf16[192,1024]{1,0:T(8,128)(2,1)S(1)}, u32[]{:S(2)}, u32[]{:S(2)}) collective-permute-start(bf16[192,1024]{1,0:T(8,128)(2,1)S(1)} %shard_map.92), channel_id=1, source_target_pairs={{0,4},{12,8},{1,5},{13,9},{2,6},{14,10},{3,7},{15,11},{16,20},{28,... | collective-permute-start | bytes 1179656 | tf_op jit(solution)/shard_map/ppermute | solution.py:115
  42.5 3.2 %shard_map.94 = (f32[384,1024]{1,0:T(8,128)S(1)}, bf16[384,1024]{1,0:T(8,128)(2,1)S(1)}, f32[8,128]{1,0:T(8,128)S(1)}) custom-call(s32[9]{0:T(128)S(1)} %fusion.plan_ref, bf16[384,1024]{1,0:T(8,128)(2,1)} %refs_0_.1, bf16[384,1024]{1,0:T(8,128)(2,1)} %collective-permute-done.7.inner_ref.outer_ref.refs_1_, ...), custom_call_target="tpu_custom_call" | custom-call | flops 1024 | bytes 1024 | tf_op jit(solution)/shard_map/pallas_call | solution.py:287
  48.4 2.6 %collective-permute-done.5.refs_0_ = bf16[400,1024]{1,0:T(8,128)(2,1)S(1)} collective-permute-done((bf16[400,1024]{1,0:T(8,128)(2,1)}, bf16[400,1024]{1,0:T(8,128)(2,1)S(1)}, u32[]{:S(2)}, u32[]{:S(2)}) %collective-permute-start.5) | collective-permute-done | bytes 819232 | tf_op jit(solution)/shard_map/ppermute | solution.py:115
  52.0 2.6 %collective-permute-start.10 = (bf16[400,1024]{1,0:T(8,128)(2,1)}, bf16[400,1024]{1,0:T(8,128)(2,1)S(1)}, u32[]{:S(2)}, u32[]{:S(2)}) collective-permute-start(bf16[400,1024]{1,0:T(8,128)(2,1)} %shard_map.95.refs_1_.outer_ref), channel_id=1, source_target_pairs={{0,2},{1,3},{2,0},{3,1},{12,14},{13,15},{14,12},{15,13},{16,18},{1... | collective-permute-start | bytes 2457608 | tf_op jit(solution)/shard_map/ppermute | solution.py:424
  57.7 3.0 %shard_map.96 = (f32[384,1024]{1,0:T(8,128)S(1)}, bf16[384,1024]{1,0:T(8,128)(2,1)S(1)}, f32[8,128]{1,0:T(8,128)S(1)}) custom-call(s32[9]{0:T(128)S(1)} %fusion.plan_ref, bf16[400,1024]{1,0:T(8,128)(2,1)} %collective-permute-done.refs_0_.inner_ref.outer_ref, bf16[400,1024]{1,0:T(8,128)(2,1)S(1)} %copy-done.10, bf16[1024,512]{1,0:T(8,128)(2,1)S(1)} %copy-done.3, ...), custom_call_target="tpu_custom_call" | custom-call | flops 1024 | bytes 1024 | tf_op jit(solution)/shard_map/pallas_call | solution.py:287
  62.7 7.5 %collective-permute-done.2.outer_ref.refs_1_ = bf16[400,1024]{1,0:T(8,128)(2,1)} collective-permute-done((bf16[400,1024]{1,0:T(8,128)(2,1)}, bf16[400,1024]{1,0:T(8,128)(2,1)}, u32[]{:S(2)}, u32[]{:S(2)}) %collective-permute-start.2) | collective-permute-done | bytes 819232 | tf_op jit(solution)/shard_map/ppermute | solution.py:115
  72.1 2.0 %shard_map.97 = bf16[192,1024]{1,0:T(8,128)(2,1)S(1)} custom-call(s32[9]{0:T(128)S(1)} %fusion.plan_ref, bf16[400,1024]{1,0:T(8,128)(2,1)} %collective-permute-done.1.refs_2_.inner_ref.refs_0_, bf16[400,1024]{1,0:T(8,128)(2,1)} %collective-permute-done.2.outer_ref.refs_1_, bf16[400,1024]{1,0:T(8,128)(2,1)} %collective-permute-done.4.rest_0_.refs_2_, ...), custom_call_target="tpu_custom_call" | custom-call | flops 1024 | bytes 1024 | tf_op jit(solution)/shard_map/pallas_call | solution.py:192
  74.7 3.0 %shard_map.98 = (f32[384,1024]{1,0:T(8,128)S(1)}, f32[8,128]{1,0:T(8,128)}) custom-call(s32[9]{0:T(128)S(1)} %fusion.plan_ref, bf16[400,1024]{1,0:T(8,128)(2,1)} %collective-permute-done.1.refs_2_.inner_ref.refs_0_, bf16[400,1024]{1,0:T(8,128)(2,1)} %collective-permute-done.2.outer_ref.refs_1_, bf16[1024,512]{1,0:T(8,128)(2,1)S(1)} %copy-done.4, ...), custom_call_target="tpu_custom_call" | custom-call | flops 1024 | bytes 1024 | tf_op jit(solution)/shard_map/pallas_call | solution.py:287
  79.6 2.2 %shard_map.100 = (f32[768,512]{1,0:T(8,128)S(1)}, f32[8,128]{1,0:T(8,128)S(1)}) custom-call(s32[9]{0:T(128)S(1)} %fusion.plan_ref, f32[384,1024]{1,0:T(8,128)S(1)} %get-tuple-element.32.sums_ref, bf16[384,1024]{1,0:T(8,128)(2,1)S(1)} %collective-permute-done.14.got_ref, bf16[400,1024]{1,0:T(8,128)(2,1)} %collective-permute-done.refs_0_.inner_ref.outer_ref, ...), custom_call_target="tpu_custom_call" | custom-call | flops 1024 | bytes 1024 | tf_op jit(solution)/shard_map/pallas_call | solution.py:346
  81.8 3.7 %shard_map.102 = (f32[384,1024]{1,0:T(8,128)S(1)}, bf16[384,1024]{1,0:T(8,128)(2,1)S(1)}, f32[8,128]{1,0:T(8,128)}) custom-call(s32[9]{0:T(128)S(1)} %fusion.plan_ref, bf16[400,1024]{1,0:T(8,128)(2,1)} %collective-permute-done.3.refs_0_.inner_ref, bf16[400,1024]{1,0:T(8,128)(2,1)S(1)} %copy-done.8, bf16[400,1024]{1,0:T(8,128)(2,1)} %collective-permute-done.4.rest_0_.refs_2_, ...), custom_call_target="tpu_custom_call" | custom-call | flops 1024 | bytes 1024 | tf_op jit(solution)/shard_map/pallas_call | solution.py:287
  85.9 2.0 %shard_map.101 = (f32[384,1024]{1,0:T(8,128)S(1)}, bf16[384,1024]{1,0:T(8,128)(2,1)S(1)}, f32[8,128]{1,0:T(8,128)}) custom-call(s32[9]{0:T(128)S(1)} %fusion.plan_ref, bf16[192,1024]{1,0:T(8,128)(2,1)S(1)} %collective-permute-done.12.refs_0_, bf16[192,1024]{1,0:T(8,128)(2,1)S(1)} %collective-permute-done.11.rest_2_.refs_1_, ...), custom_call_target="tpu_custom_call" | custom-call | flops 1024 | bytes 1024 | tf_op jit(solution)/shard_map/pallas_call | solution.py:287
  88.2 2.1 %shard_map.103 = (f32[768,512]{1,0:T(8,128)S(1)}, f32[8,128]{1,0:T(8,128)}) custom-call(s32[9]{0:T(128)S(1)} %fusion.plan_ref, f32[384,1024]{1,0:T(8,128)S(1)} %get-tuple-element.40.sums_ref, bf16[384,1024]{1,0:T(8,128)(2,1)S(1)} %collective-permute-done.17.got_ref, bf16[400,1024]{1,0:T(8,128)(2,1)} %collective-permute-done.3.refs_0_.inner_ref, ...), custom_call_target="tpu_custom_call" | custom-call | flops 1024 | bytes 1024 | tf_op jit(solution)/shard_map/pallas_call | solution.py:346
  90.3 2.6 %shard_map.104 = (bf16[192,1024]{1,0:T(8,128)(2,1)S(1)}, f32[192,1024]{1,0:T(8,128)S(1)}, bf16[576,512]{1,0:T(8,128)(2,1)S(1)}) custom-call(s32[9]{0:T(128)S(1)} %fusion.plan_ref, f32[384,1024]{1,0:T(8,128)S(1)} %get-tuple-element.38.sums_ref, bf16[384,1024]{1,0:T(8,128)(2,1)S(1)} %collective-permute-done.16.got_ref, ...), custom_call_target="tpu_custom_call" | custom-call | flops 1024 | bytes 1024 | tf_op jit(solution)/shard_map/pallas_call | solution.py:380
  96.4 8.4 %collective-permute-done.20 = bf16[192,1024]{1,0:T(8,128)(2,1)S(1)} collective-permute-done((bf16[192,1024]{1,0:T(8,128)(2,1)S(1)}, bf16[192,1024]{1,0:T(8,128)(2,1)S(1)}, u32[]{:S(2)}, u32[]{:S(2)}) %collective-permute-start.20) | collective-permute-done | bytes 393248 | tf_op jit(solution)/shard_map/ppermute | solution.py:107
  104.9 6.0 %collective-permute-start.24 = (bf16[192,1024]{1,0:T(8,128)(2,1)S(1)}, bf16[192,1024]{1,0:T(8,128)(2,1)S(1)}, u32[]{:S(2)}, u32[]{:S(2)}) collective-permute-start(bf16[192,1024]{1,0:T(8,128)(2,1)S(1)} %add_convert_fusion.4), channel_id=1, source_target_pairs={{0,4},{12,8},{1,5},{13,9},{2,6},{14,10},{3,7},{15,11},{16,20},{28,... | collective-permute-start | bytes 1179656 | tf_op jit(solution)/shard_map/ppermute | solution.py:115
  113.8 6.6 %collective-permute-start.23 = (bf16[192,1024]{1,0:T(8,128)(2,1)S(1)}, bf16[192,1024]{1,0:T(8,128)(2,1)S(1)}, u32[]{:S(2)}, u32[]{:S(2)}) collective-permute-start(bf16[192,1024]{1,0:T(8,128)(2,1)S(1)} %add_convert_fusion.3), channel_id=1, source_target_pairs={{0,8},{12,4},{1,9},{13,5},{2,10},{14,6},{3,11},{15,7},{16,24},{28,... | collective-permute-start | bytes 1179656 | tf_op jit(solution)/shard_map/ppermute | solution.py:115
  123.1 2.8 %collective-permute-start.27 = (bf16[192,1024]{1,0:T(8,128)(2,1)S(1)}, bf16[192,1024]{1,0:T(8,128)(2,1)S(1)}, u32[]{:S(2)}, u32[]{:S(2)}) collective-permute-start(bf16[192,1024]{1,0:T(8,128)(2,1)S(1)} %add_convert_fusion.1), channel_id=1, source_target_pairs={{0,4},{4,0},{8,12},{12,8},{1,5},{5,1},{9,13},{13,9},{2,6},{6,2},{1... | collective-permute-start | bytes 1179656 | tf_op jit(solution)/shard_map/ppermute | solution.py:115
  125.9 3.8 %collective-permute-done.19 = bf16[192,1024]{1,0:T(8,128)(2,1)S(1)} collective-permute-done((bf16[192,1024]{1,0:T(8,128)(2,1)S(1)}, bf16[192,1024]{1,0:T(8,128)(2,1)S(1)}, u32[]{:S(2)}, u32[]{:S(2)}) %collective-permute-start.19) | collective-permute-done | bytes 393248 | tf_op jit(solution)/shard_map/ppermute | solution.py:107
  129.9 10.2 %collective-permute-done.25 = bf16[192,1024]{1,0:T(8,128)(2,1)S(1)} collective-permute-done((bf16[192,1024]{1,0:T(8,128)(2,1)S(1)}, bf16[192,1024]{1,0:T(8,128)(2,1)S(1)}, u32[]{:S(2)}, u32[]{:S(2)}) %collective-permute-start.25) | collective-permute-done | bytes 393248 | tf_op jit(solution)/shard_map/ppermute | solution.py:115
  140.4 2.2 %collective-permute-done.27 = bf16[192,1024]{1,0:T(8,128)(2,1)S(1)} collective-permute-done((bf16[192,1024]{1,0:T(8,128)(2,1)S(1)}, bf16[192,1024]{1,0:T(8,128)(2,1)S(1)}, u32[]{:S(2)}, u32[]{:S(2)}) %collective-permute-start.27) | collective-permute-done | bytes 393248 | tf_op jit(solution)/shard_map/ppermute | solution.py:115
  (117 shorter events, 44.9 us)
Async XLA Ops:
  4.5 21.4 %collective-permute-start = (bf16[400,1024]{1,0:T(8,128)(2,1)S(1)}, bf16[400,1024]{1,0:T(8,128)(2,1)}, u32[]{:S(2)}, u32[]{:S(2)}) collective-permute-start(bf16[400,1024]{1,0:T(8,128)(2,1)S(1)} %shard_map.91.refs_1_.inner_ref.outer_ref), channel_id=1, source_target_pairs={{0,4},{4,0},{8,12},{12,8},{1,5},{5,1},{9,13},{13,9},{2,6},{6,2},{1... | collective-permute-start | bytes 2457608 | tf_op jit(solution)/shard_map/ppermute | solution.py:115
  7.6 21.7 %collective-permute-start.3 = (bf16[400,1024]{1,0:T(8,128)(2,1)S(1)}, bf16[400,1024]{1,0:T(8,128)(2,1)}, u32[]{:S(2)}, u32[]{:S(2)}) collective-permute-start(bf16[400,1024]{1,0:T(8,128)(2,1)S(1)} %shard_map.91.refs_1_.inner_ref.outer_ref), channel_id=1, source_target_pairs={{4,8},{8,4},{5,9},{9,5},{6,10},{10,6},{7,11},{11,7},{20,24},{24,20... | collective-permute-start | bytes 2457608 | tf_op jit(solution)/shard_map/ppermute | solution.py:115
  9.2 21.4 %collective-permute-start.7 = (bf16[384,1024]{1,0:T(8,128)(2,1)}, bf16[384,1024]{1,0:T(8,128)(2,1)}, u32[]{:S(2)}, u32[]{:S(2)}) collective-permute-start(bf16[384,1024]{1,0:T(8,128)(2,1)} %refs_0_.1), channel_id=1, source_target_pairs={{0,2},{1,3},{2,0},{3,1},{4,6},{5,7},{6,4},{7,5},{8,10},{9,11},{10,... | collective-permute-start | bytes 2359304 | tf_op jit(solution)/shard_map/ppermute | solution.py:107
  15.6 25.7 %collective-permute-start.9 = (bf16[2048,512]{1,0:T(8,128)(2,1)}, bf16[2048,512]{1,0:T(8,128)(2,1)S(1)}, u32[]{:S(2)}, u32[]{:S(2)}) collective-permute-start(bf16[2048,512]{1,0:T(8,128)(2,1)} %shard_map.93), channel_id=1, source_target_pairs={{0,1},{1,0},{2,3},{3,2},{4,5},{5,4},{6,7},{7,6},{8,9},{9,8},{10,11... | collective-permute-start | bytes 6291464 | tf_op jit(solution)/shard_map/ppermute | solution.py:111
  26.0 13.7 %collective-permute-start.1 = (bf16[400,1024]{1,0:T(8,128)(2,1)}, bf16[400,1024]{1,0:T(8,128)(2,1)}, u32[]{:S(2)}, u32[]{:S(2)}) collective-permute-start(bf16[400,1024]{1,0:T(8,128)(2,1)} %collective-permute-done.refs_0_.inner_ref.outer_ref), channel_id=1, source_target_pairs={{4,8},{8,4},{5,9},{9,5},{6,10},{10,6},{7,11},{11,7},{20,24},{24,20... | collective-permute-start | bytes 2457608 | tf_op jit(solution)/shard_map/ppermute | solution.py:115
  27.6 20.8 %collective-permute-start.6 = (bf16[400,1024]{1,0:T(8,128)(2,1)}, bf16[400,1024]{1,0:T(8,128)(2,1)S(1)}, u32[]{:S(2)}, u32[]{:S(2)}) collective-permute-start(bf16[400,1024]{1,0:T(8,128)(2,1)} %collective-permute-done.refs_0_.inner_ref.outer_ref), channel_id=1, source_target_pairs={{0,2},{1,3},{2,0},{3,1},{4,6},{5,7},{6,4},{7,5},{8,10},{9,11},{10,... | collective-permute-start | bytes 2457608 | tf_op jit(solution)/shard_map/ppermute | solution.py:107
  29.3 21.8 %collective-permute-start.5 = (bf16[400,1024]{1,0:T(8,128)(2,1)}, bf16[400,1024]{1,0:T(8,128)(2,1)S(1)}, u32[]{:S(2)}, u32[]{:S(2)}) collective-permute-start(bf16[400,1024]{1,0:T(8,128)(2,1)} %collective-permute-done.3.refs_0_.inner_ref), channel_id=1, source_target_pairs={{4,0},{8,12},{5,1},{9,13},{6,2},{10,14},{7,3},{11,15},{20,16},{24,... | collective-permute-start | bytes 2457608 | tf_op jit(solution)/shard_map/ppermute | solution.py:115
  32.6 15.8 %collective-permute-start.8 = (bf16[192,1024]{1,0:T(8,128)(2,1)S(1)}, bf16[192,1024]{1,0:T(8,128)(2,1)S(1)}, u32[]{:S(2)}, u32[]{:S(2)}) collective-permute-start(bf16[192,1024]{1,0:T(8,128)(2,1)S(1)} %shard_map.92), channel_id=1, source_target_pairs={{0,4},{12,8},{1,5},{13,9},{2,6},{14,10},{3,7},{15,11},{16,20},{28,... | collective-permute-start | bytes 1179656 | tf_op jit(solution)/shard_map/ppermute | solution.py:115
  39.7 21.6 %collective-permute-start.4 = (bf16[400,1024]{1,0:T(8,128)(2,1)}, bf16[400,1024]{1,0:T(8,128)(2,1)}, u32[]{:S(2)}, u32[]{:S(2)}) collective-permute-start(bf16[400,1024]{1,0:T(8,128)(2,1)} %collective-permute-done.3.refs_0_.inner_ref), channel_id=1, source_target_pairs={{4,6},{5,7},{6,4},{7,5},{8,10},{9,11},{10,8},{11,9},{20,22},{21,23... | collective-permute-start | bytes 2457608 | tf_op jit(solution)/shard_map/ppermute | solution.py:424
  41.2 29.0 %collective-permute-start.2 = (bf16[400,1024]{1,0:T(8,128)(2,1)}, bf16[400,1024]{1,0:T(8,128)(2,1)}, u32[]{:S(2)}, u32[]{:S(2)}) collective-permute-start(bf16[400,1024]{1,0:T(8,128)(2,1)} %collective-permute-done.1.refs_2_.inner_ref.refs_0_), channel_id=1, source_target_pairs={{4,0},{8,12},{5,1},{9,13},{6,2},{10,14},{7,3},{11,15},{20,16},{24,... | collective-permute-start | bytes 2457608 | tf_op jit(solution)/shard_map/ppermute | solution.py:115
  52.0 20.1 %collective-permute-start.10 = (bf16[400,1024]{1,0:T(8,128)(2,1)}, bf16[400,1024]{1,0:T(8,128)(2,1)S(1)}, u32[]{:S(2)}, u32[]{:S(2)}) collective-permute-start(bf16[400,1024]{1,0:T(8,128)(2,1)} %shard_map.95.refs_1_.outer_ref), channel_id=1, source_target_pairs={{0,2},{1,3},{2,0},{3,1},{12,14},{13,15},{14,12},{15,13},{16,18},{1... | collective-permute-start | bytes 2457608 | tf_op jit(solution)/shard_map/ppermute | solution.py:424
  55.2 22.5 %collective-permute-start.15 = (bf16[384,1024]{1,0:T(8,128)(2,1)}, bf16[384,1024]{1,0:T(8,128)(2,1)S(1)}, u32[]{:S(2)}, u32[]{:S(2)}) collective-permute-start(bf16[384,1024]{1,0:T(8,128)(2,1)} %copy-done.19), channel_id=1, source_target_pairs={{0,1},{1,0},{2,3},{3,2},{4,5},{5,4},{6,7},{7,6},{8,9},{9,8},{10,11... | collective-permute-start | bytes 2359304 | tf_op jit(solution)/shard_map/ppermute | solution.py:111
  60.7 18.9 %collective-permute-start.14 = (bf16[384,1024]{1,0:T(8,128)(2,1)S(1)}, bf16[384,1024]{1,0:T(8,128)(2,1)S(1)}, u32[]{:S(2)}, u32[]{:S(2)}) collective-permute-start(bf16[384,1024]{1,0:T(8,128)(2,1)S(1)} %get-tuple-element.33), channel_id=1, source_target_pairs={{0,1},{1,0},{2,3},{3,2},{4,5},{5,4},{6,7},{7,6},{8,9},{9,8},{10,11... | collective-permute-start | bytes 2359304 | tf_op jit(solution)/shard_map/ppermute | solution.py:111
  61.2 24.7 %collective-permute-start.13 = (bf16[192,1024]{1,0:T(8,128)(2,1)S(1)}, bf16[192,1024]{1,0:T(8,128)(2,1)S(1)}, u32[]{:S(2)}, u32[]{:S(2)}) collective-permute-start(bf16[192,1024]{1,0:T(8,128)(2,1)S(1)} %collective-permute-done.11.rest_2_.refs_1_), channel_id=1, source_target_pairs={{4,0},{8,12},{5,1},{9,13},{6,2},{10,14},{7,3},{11,15},{20,16},{24,... | collective-permute-start | bytes 1179656 | tf_op jit(solution)/shard_map/ppermute | solution.py:115
  74.7 15.6 %collective-permute-start.18 = (bf16[256,2048]{1,0:T(8,128)(2,1)S(1)}, bf16[256,2048]{1,0:T(8,128)(2,1)S(1)}, u32[]{:S(2)}, u32[]{:S(2)}) collective-permute-start(bf16[256,2048]{1,0:T(8,128)(2,1)S(1)} %copy-done.20), channel_id=1, source_target_pairs={{0,1},{1,0},{2,3},{3,2},{4,5},{5,4},{6,7},{7,6},{8,9},{9,8},{10,11... | collective-permute-start | bytes 3145736 | tf_op jit(solution)/shard_map/ppermute | solution.py:111
  92.9 12.0 %collective-permute-start.20 = (bf16[192,1024]{1,0:T(8,128)(2,1)S(1)}, bf16[192,1024]{1,0:T(8,128)(2,1)S(1)}, u32[]{:S(2)}, u32[]{:S(2)}) collective-permute-start(bf16[192,1024]{1,0:T(8,128)(2,1)S(1)} %get-tuple-element.48), channel_id=1, source_target_pairs={{0,2},{1,3},{2,0},{3,1},{4,6},{5,7},{6,4},{7,5},{8,10},{9,11},{10,... | collective-permute-start | bytes 1179656 | tf_op jit(solution)/shard_map/ppermute | solution.py:107
  95.8 17.9 %collective-permute-start.22 = (bf16[192,1024]{1,0:T(8,128)(2,1)S(1)}, bf16[192,1024]{1,0:T(8,128)(2,1)S(1)}, u32[]{:S(2)}, u32[]{:S(2)}) collective-permute-start(bf16[192,1024]{1,0:T(8,128)(2,1)S(1)} %get-tuple-element.50), channel_id=1, source_target_pairs={{0,2},{1,3},{2,0},{3,1},{4,6},{5,7},{6,4},{7,5},{8,10},{9,11},{10,... | collective-permute-start | bytes 1179656 | tf_op jit(solution)/shard_map/ppermute | solution.py:107
  104.9 15.4 %collective-permute-start.24 = (bf16[192,1024]{1,0:T(8,128)(2,1)S(1)}, bf16[192,1024]{1,0:T(8,128)(2,1)S(1)}, u32[]{:S(2)}, u32[]{:S(2)}) collective-permute-start(bf16[192,1024]{1,0:T(8,128)(2,1)S(1)} %add_convert_fusion.4), channel_id=1, source_target_pairs={{0,4},{12,8},{1,5},{13,9},{2,6},{14,10},{3,7},{15,11},{16,20},{28,... | collective-permute-start | bytes 1179656 | tf_op jit(solution)/shard_map/ppermute | solution.py:115
  110.9 12.1 %collective-permute-start.26 = (bf16[192,1024]{1,0:T(8,128)(2,1)S(1)}, bf16[192,1024]{1,0:T(8,128)(2,1)S(1)}, u32[]{:S(2)}, u32[]{:S(2)}) collective-permute-start(bf16[192,1024]{1,0:T(8,128)(2,1)S(1)} %get-tuple-element.52), channel_id=1, source_target_pairs={{0,2},{1,3},{2,0},{3,1},{4,6},{5,7},{6,4},{7,5},{8,10},{9,11},{10,... | collective-permute-start | bytes 1179656 | tf_op jit(solution)/shard_map/ppermute | solution.py:107
  112.5 17.2 %collective-permute-start.19 = (bf16[192,1024]{1,0:T(8,128)(2,1)S(1)}, bf16[192,1024]{1,0:T(8,128)(2,1)S(1)}, u32[]{:S(2)}, u32[]{:S(2)}) collective-permute-start(bf16[192,1024]{1,0:T(8,128)(2,1)S(1)} %get-tuple-element.46), channel_id=1, source_target_pairs={{0,2},{1,3},{2,0},{3,1},{4,6},{5,7},{6,4},{7,5},{8,10},{9,11},{10,... | collective-permute-start | bytes 1179656 | tf_op jit(solution)/shard_map/ppermute | solution.py:107
  113.0 16.9 %collective-permute-start.21 = (bf16[192,1024]{1,0:T(8,128)(2,1)S(1)}, bf16[192,1024]{1,0:T(8,128)(2,1)S(1)}, u32[]{:S(2)}, u32[]{:S(2)}) collective-permute-start(bf16[192,1024]{1,0:T(8,128)(2,1)S(1)} %add_convert_fusion.4), channel_id=1, source_target_pairs={{4,8},{8,4},{5,9},{9,5},{6,10},{10,6},{7,11},{11,7},{20,24},{24,20... | collective-permute-start | bytes 1179656 | tf_op jit(solution)/shard_map/ppermute | solution.py:115
  113.8 16.1 %collective-permute-start.23 = (bf16[192,1024]{1,0:T(8,128)(2,1)S(1)}, bf16[192,1024]{1,0:T(8,128)(2,1)S(1)}, u32[]{:S(2)}, u32[]{:S(2)}) collective-permute-start(bf16[192,1024]{1,0:T(8,128)(2,1)S(1)} %add_convert_fusion.3), channel_id=1, source_target_pairs={{0,8},{12,4},{1,9},{13,5},{2,10},{14,6},{3,11},{15,7},{16,24},{28,... | collective-permute-start | bytes 1179656 | tf_op jit(solution)/shard_map/ppermute | solution.py:115
  120.5 19.6 %collective-permute-start.25 = (bf16[192,1024]{1,0:T(8,128)(2,1)S(1)}, bf16[192,1024]{1,0:T(8,128)(2,1)S(1)}, u32[]{:S(2)}, u32[]{:S(2)}) collective-permute-start(bf16[192,1024]{1,0:T(8,128)(2,1)S(1)} %add_convert_fusion.2), channel_id=1, source_target_pairs={{4,12},{8,0},{5,13},{9,1},{6,14},{10,2},{7,15},{11,3},{20,28},{24,... | collective-permute-start | bytes 1179656 | tf_op jit(solution)/shard_map/ppermute | solution.py:115
  123.1 19.5 %collective-permute-start.27 = (bf16[192,1024]{1,0:T(8,128)(2,1)S(1)}, bf16[192,1024]{1,0:T(8,128)(2,1)S(1)}, u32[]{:S(2)}, u32[]{:S(2)}) collective-permute-start(bf16[192,1024]{1,0:T(8,128)(2,1)S(1)} %add_convert_fusion.1), channel_id=1, source_target_pairs={{0,4},{4,0},{8,12},{12,8},{1,5},{5,1},{9,13},{13,9},{2,6},{6,2},{1... | collective-permute-start | bytes 1179656 | tf_op jit(solution)/shard_map/ppermute | solution.py:115
  (32 other events, 164.3 us)

commit v13 on v12

--- a/solution.py
+++ b/solution.py
@@ -363,10 +363,12 @@
     ]
 
     def first(plan_ref, sums_ref, got_ref, inner_ref, outer_ref, before_ref, *refs):
-        own_ref, lent_ref, sent_ref, kept_ref, held_ref, buffer, sem = refs
+        own_ref, lent_ref, sent_ref, kept_ref, both_ref, held_ref, buffer, sem = refs
         facts_here = facts_of(plan_ref, inner_ref, outer_ref, buffer, sem)
         rows = collected_rows(owned, slot, plan_ref, sums_ref, got_ref, facts_here, before_ref)
         down(rows[0].astype(jnp.bfloat16), own_ref, lent_ref, sent_ref, kept_ref)
+        both_ref[:, :width] = kept_ref[...].astype(jnp.bfloat16)
+        both_ref[:, width:] = sent_ref[...]
         for index in range(1, 4):
             held_ref[(index - 1) * owned : index * owned, :] = rows[index].astype(jnp.bfloat16)
 
@@ -377,11 +379,12 @@
 
     held_shape = jax.ShapeDtypeStruct((3 * owned, 2 * units), jnp.bfloat16)
     specs = [SMEM, VMEM, VMEM, ANYWHERE, ANYWHERE] + [VMEM] * 3
-    sent, kept, held = on_core(
-        first, pair + [held_shape], specs, fact_scratch(facts[0].shape[1])
+    both_shape = jax.ShapeDtypeStruct((owned, 2 * width), jnp.bfloat16)
+    sent, kept, both, held = on_core(
+        first, pair + [both_shape, held_shape], specs, fact_scratch(facts[0].shape[1])
     )(plan, sums, got, *facts, before, down_own, down_lent)
     rest = on_core(others, pair * 3, [VMEM] * 3)(held, down_own, down_lent)
-    return [sent, *rest[0::2]], [kept, *rest[1::2]]
+    return [sent, *rest[0::2]], [kept, *rest[1::2]], both
 
 
 def rows_travel(
@@ -471,19 +474,23 @@
     )
     got_3 = across_cores(send_3)
     total, _ = collect(owned, 2, plan, sums_2, got_2, second, total)
-    sent, kept = finish(owned, 3, plan, sums_3, got_3, last, total, kept_down, lent_down)
-
-    joined = [k + across_chips(s).astype(jnp.float32) for s, k in zip(sent, kept)]
-    first, second, third = [block.astype(jnp.bfloat16) for block in joined[:3]]
-    second = lax.optimization_barrier(second)
-    inward = along(first, INWARD)
-    middle = along(first, MIDDLE)
+    sent, kept, both = finish(owned, 3, plan, sums_3, got_3, last, total, kept_down, lent_down)
+
+    def joined(kept_part, sent_part):
+        return kept_part + across_chips(sent_part).astype(jnp.float32)
+
+    middle = along(both, MIDDLE).astype(jnp.float32)
+    first = kept[0] + at_kind(sent[0], (0, 3)).astype(jnp.float32)
+    inward = along(first.astype(jnp.bfloat16), INWARD)
+    second = lax.optimization_barrier(joined(kept[1], sent[1]).astype(jnp.bfloat16))
     two_in = along(second, TWO_IN)
     passed = second.astype(jnp.float32) + inward.astype(jnp.float32)
     two_out = along(passed.astype(jnp.bfloat16), TWO_OUT)
-    beside = along(third, BESIDE)
-    arrived = [block.astype(jnp.float32) for block in (middle, two_in, two_out)]
-    total = lax.optimization_barrier(joined[3] + sum(arrived))
+    beside = along(joined(kept[2], sent[2]).astype(jnp.bfloat16), BESIDE)
+    own_sent = (sent[3].astype(jnp.float32) + middle[:, width:]).astype(jnp.bfloat16)
+    own_sum = joined(kept[3] + middle[:, :width], own_sent)
+    arrived = [block.astype(jnp.float32) for block in (two_in, two_out)]
+    total = lax.optimization_barrier(own_sum + sum(arrived))
     return (total + beside.astype(jnp.float32)).astype(jnp.bfloat16)
 
 

time: 144 us -> 149 us (1.035)
  waiting for transfers between devices: 45.2 us -> 52.4 us
  starting transfers between devices: 47 us -> 44 us
    ppermute x2 -> x3, waiting for transfers between devices: 1.9 us -> 7.94 us  [at_kind(): return lax.ppermute(block, ('blk', 'tp'), pairs)]
    ppermute x13, starting transfers between devices: 33.8 us -> 28 us  [along(): return lax.ppermute(block, 'blk', route)]
    ppermute x2 -> x3, starting transfers between devices: 4.11 us -> 7.51 us  [at_kind(): return lax.ppermute(block, ('blk', 'tp'), pairs)]
    ppermute x13, waiting for transfers between devices: 29.9 us -> 32.6 us  [along(): return lax.ppermute(block, 'blk', route)]
    ppermute x7 -> x6, waiting for transfers between devices: 13.4 us -> 11.7 us  [across_chips(): return lax.ppermute(block, 'tp', [(i, i ^ 2) for i in range(4)])]
    ppermute x7 -> x6, starting transfers between devices: 8 us -> 7.39 us  [across_chips(): return lax.ppermute(block, 'tp', [(i, i ^ 2) for i in range(4)])]
  transfers between devices with their start and end apart: 28 -> 28, of which waited for: 10 -> 11; matrix products, arithmetic and copies ran while one was open for 7% -> 7% of each run, Pallas kernels for 18% -> 18%
where the time goes in v13:
time: 149 us; the launch traced here: 148 us
  waiting for transfers between devices  52.4 us (35%)
  starting transfers between devices  44 us (30%)
  Pallas kernels  30.5 us (20%)
  local copies, waits for them, and re-layouts  15.5 us (10%)
  other arithmetic  4.77 us (3%)
    ppermute x13, waiting for transfers between devices, along(): return lax.ppermute(block, 'blk', route)  32.6 us
    ppermute x13, starting transfers between devices, along(): return lax.ppermute(block, 'blk', route)  28 us
    pallas_call x5, Pallas kernels, partial_sums(): return on_core(body, shapes + [TOKEN], specs)(*operands, *waits)  14.8 us
    ppermute x6, waiting for transfers between devices, across_chips(): return lax.ppermute(block, 'tp', [(i, i ^ 2) for i in range(4)])  11.7 us
    unnamed x56, local copies, waits for them, and re-layouts  8.75 us
    ppermute x3, waiting for transfers between devices, at_kind(): return lax.ppermute(block, ('blk', 'tp'), pairs)  7.94 us
    ppermute x3, starting transfers between devices, at_kind(): return lax.ppermute(block, ('blk', 'tp'), pairs)  7.51 us
    ppermute x6, starting transfers between devices, across_chips(): return lax.ppermute(block, 'tp', [(i, i ^ 2) for i in range(4)])  7.39 us
  transfers between devices with their start and end apart: 28, of which 11 were waited for; matrix products, arithmetic and copies ran while one was open for 7% of the time, Pallas kernels for 18%

profile of v13, /device:TPU:0, one launch (start us, length us, event | category | flops | bytes accessed | tf_op | source)
XLA Modules:
  0.0 147.8 jit_solution(10534540606290557994)
XLA Ops:
  4.5 3.1 %collective-permute-start = (bf16[400,1024]{1,0:T(8,128)(2,1)S(1)}, bf16[400,1024]{1,0:T(8,128)(2,1)}, u32[]{:S(2)}, u32[]{:S(2)}) collective-permute-start(bf16[400,1024]{1,0:T(8,128)(2,1)S(1)} %shard_map.91.refs_1_.inner_ref.outer_ref), channel_id=1, source_target_pairs={{0,4},{4,0},{8,12},{12,8},{1,5},{5,1},{9,13},{13,9},{2,6},{6,2},{1... | collective-permute-start | bytes 2457608 | tf_op jit(solution)/shard_map/ppermute | solution.py:115
  10.7 3.4 %dynamic-slice_bitcast_fusion.4 = (bf16[1024,256]{1,0:T(8,128)(2,1)S(1)}, bf16[1024,256]{1,0:T(8,128)(2,1)S(1)}, bf16[1024,256]{1,0:T(8,128)(2,1)S(1)}, bf16[102...) fusion(bf16[4,1024,256]{2,1,0:T(8,128)(2,1)} %bitcast.32, ...), kind=kLoop, calls=%fused_computation.19 | loop fusion | bytes 8388624 | tf_op jit(solution)/shard_map/jit(dynamic_index_in_dim)/squeeze | solution.py:413
  16.2 2.7 %dynamic-slice_bitcast_fusion.1 = (bf16[256,1024]{1,0:T(8,128)(2,1)}, bf16[256,1024]{1,0:T(8,128)(2,1)S(1)}, bf16[256,1024]{1,0:T(8,128)(2,1)S(1)}, bf16[256,1024]{1,0:T(8,128)(2,1)}) fusion(bf16[1,256,4096]{2,1,0:T(8,128)(2,1)} %param.12, s32[]{:T(128)S(6)} %select_n.39, s32[]{:T(128)S(6)} %select_n.34, s32[]{:T(128)S(6)} %select_n.33, s32[]{:T(128)S(6)} %select_n.40), kind=kLoop, calls=%fused_computation.16 | loop fusion | bytes 4194320 | tf_op jit(solution)/shard_map/dynamic_slice | solution.py:419
  18.9 7.1 %collective-permute-done.refs_0_.inner_ref.outer_ref = bf16[400,1024]{1,0:T(8,128)(2,1)} collective-permute-done((bf16[400,1024]{1,0:T(8,128)(2,1)S(1)}, bf16[400,1024]{1,0:T(8,128)(2,1)}, u32[]{:S(2)}, u32[]{:S(2)}) %collective-permute-start) | collective-permute-done | bytes 819232 | tf_op jit(solution)/shard_map/ppermute | solution.py:115
  30.6 2.0 %shard_map.92 = bf16[192,1024]{1,0:T(8,128)(2,1)S(1)} custom-call(s32[9]{0:T(128)S(1)} %fusion.3.plan_ref, bf16[384,1024]{1,0:T(8,128)(2,1)} %collective-permute-done.7.inner_ref.outer_ref.refs_1_, bf16[384,1024]{1,0:T(8,128)(2,1)} %collective-permute-done.7.inner_ref.outer_ref.refs_1_), custom_call_target="tpu_custom_call" | custom-call | flops 17179869184 | bytes 1024 | tf_op jit(solution)/shard_map/pallas_call | solution.py:192
  32.6 5.6 %collective-permute-start.8 = (bf16[192,1024]{1,0:T(8,128)(2,1)S(1)}, bf16[192,1024]{1,0:T(8,128)(2,1)S(1)}, u32[]{:S(2)}, u32[]{:S(2)}) collective-permute-start(bf16[192,1024]{1,0:T(8,128)(2,1)S(1)} %shard_map.92), channel_id=1, source_target_pairs={{0,4},{12,8},{1,5},{13,9},{2,6},{14,10},{3,7},{15,11},{16,20},{28,... | collective-permute-start | bytes 1179656 | tf_op jit(solution)/shard_map/ppermute | solution.py:115
  42.5 3.2 %shard_map.94 = (f32[384,1024]{1,0:T(8,128)S(1)}, bf16[384,1024]{1,0:T(8,128)(2,1)S(1)}, f32[8,128]{1,0:T(8,128)S(1)}) custom-call(s32[9]{0:T(128)S(1)} %fusion.3.plan_ref, bf16[384,1024]{1,0:T(8,128)(2,1)} %refs_0_.1, bf16[384,1024]{1,0:T(8,128)(2,1)} %collective-permute-done.7.inner_ref.outer_ref.refs_1_, ...), custom_call_target="tpu_custom_call" | custom-call | flops 1024 | bytes 1024 | tf_op jit(solution)/shard_map/pallas_call | solution.py:287
  48.4 2.6 %collective-permute-done.5.refs_0_ = bf16[400,1024]{1,0:T(8,128)(2,1)S(1)} collective-permute-done((bf16[400,1024]{1,0:T(8,128)(2,1)}, bf16[400,1024]{1,0:T(8,128)(2,1)S(1)}, u32[]{:S(2)}, u32[]{:S(2)}) %collective-permute-start.5) | collective-permute-done | bytes 819232 | tf_op jit(solution)/shard_map/ppermute | solution.py:115
  52.0 2.6 %collective-permute-start.10 = (bf16[400,1024]{1,0:T(8,128)(2,1)}, bf16[400,1024]{1,0:T(8,128)(2,1)S(1)}, u32[]{:S(2)}, u32[]{:S(2)}) collective-permute-start(bf16[400,1024]{1,0:T(8,128)(2,1)} %shard_map.95.refs_1_.outer_ref), channel_id=1, source_target_pairs={{0,2},{1,3},{2,0},{3,1},{12,14},{13,15},{14,12},{15,13},{16,18},{1... | collective-permute-start | bytes 2457608 | tf_op jit(solution)/shard_map/ppermute | solution.py:427
  57.7 3.0 %shard_map.96 = (f32[384,1024]{1,0:T(8,128)S(1)}, bf16[384,1024]{1,0:T(8,128)(2,1)S(1)}, f32[8,128]{1,0:T(8,128)S(1)}) custom-call(s32[9]{0:T(128)S(1)} %fusion.3.plan_ref, bf16[400,1024]{1,0:T(8,128)(2,1)} %collective-permute-done.refs_0_.inner_ref.outer_ref, bf16[400,1024]{1,0:T(8,128)(2,1)S(1)} %copy-done.10, bf16[1024,512]{1,0:T(8,128)(2,1)S(1)} %copy-done.3, ...), custom_call_target="tpu_custom_call" | custom-call | flops 1024 | bytes 1024 | tf_op jit(solution)/shard_map/pallas_call | solution.py:287
  62.7 7.5 %collective-permute-done.2.outer_ref.refs_1_ = bf16[400,1024]{1,0:T(8,128)(2,1)} collective-permute-done((bf16[400,1024]{1,0:T(8,128)(2,1)}, bf16[400,1024]{1,0:T(8,128)(2,1)}, u32[]{:S(2)}, u32[]{:S(2)}) %collective-permute-start.2) | collective-permute-done | bytes 819232 | tf_op jit(solution)/shard_map/ppermute | solution.py:115
  72.1 2.0 %shard_map.97 = bf16[192,1024]{1,0:T(8,128)(2,1)S(1)} custom-call(s32[9]{0:T(128)S(1)} %fusion.3.plan_ref, bf16[400,1024]{1,0:T(8,128)(2,1)} %collective-permute-done.1.refs_2_.inner_ref.refs_0_, bf16[400,1024]{1,0:T(8,128)(2,1)} %collective-permute-done.2.outer_ref.refs_1_, bf16[400,1024]{1,0:T(8,128)(2,1)} %collective-permute-done.4.rest_0_.refs_2_, ...), custom_call_target="tpu_custom_call" | custom-call | flops 1024 | bytes 1024 | tf_op jit(solution)/shard_map/pallas_call | solution.py:192
  74.7 3.0 %shard_map.98 = (f32[384,1024]{1,0:T(8,128)S(1)}, f32[8,128]{1,0:T(8,128)}) custom-call(s32[9]{0:T(128)S(1)} %fusion.3.plan_ref, bf16[400,1024]{1,0:T(8,128)(2,1)} %collective-permute-done.1.refs_2_.inner_ref.refs_0_, bf16[400,1024]{1,0:T(8,128)(2,1)} %collective-permute-done.2.outer_ref.refs_1_, bf16[1024,512]{1,0:T(8,128)(2,1)S(1)} %copy-done.4, ...), custom_call_target="tpu_custom_call" | custom-call | flops 1024 | bytes 1024 | tf_op jit(solution)/shard_map/pallas_call | solution.py:287
  79.6 2.2 %shard_map.100 = (f32[768,512]{1,0:T(8,128)S(1)}, f32[8,128]{1,0:T(8,128)S(1)}) custom-call(s32[9]{0:T(128)S(1)} %fusion.3.plan_ref, f32[384,1024]{1,0:T(8,128)S(1)} %get-tuple-element.33.sums_ref, bf16[384,1024]{1,0:T(8,128)(2,1)S(1)} %collective-permute-done.14.got_ref, bf16[400,1024]{1,0:T(8,128)(2,1)} %collective-permute-done.refs_0_.inner_ref.outer_ref, ...), custom_call_target="tpu_custom_call" | custom-call | flops 1024 | bytes 1024 | tf_op jit(solution)/shard_map/pallas_call | solution.py:346
  81.8 3.7 %shard_map.102 = (f32[384,1024]{1,0:T(8,128)S(1)}, bf16[384,1024]{1,0:T(8,128)(2,1)S(1)}, f32[8,128]{1,0:T(8,128)}) custom-call(s32[9]{0:T(128)S(1)} %fusion.3.plan_ref, bf16[400,1024]{1,0:T(8,128)(2,1)} %collective-permute-done.3.refs_0_.inner_ref, bf16[400,1024]{1,0:T(8,128)(2,1)S(1)} %copy-done.8, ...), custom_call_target="tpu_custom_call" | custom-call | flops 1024 | bytes 1024 | tf_op jit(solution)/shard_map/pallas_call | solution.py:287
  85.9 2.0 %shard_map.101 = (f32[384,1024]{1,0:T(8,128)S(1)}, bf16[384,1024]{1,0:T(8,128)(2,1)S(1)}, f32[8,128]{1,0:T(8,128)}) custom-call(s32[9]{0:T(128)S(1)} %fusion.3.plan_ref, bf16[192,1024]{1,0:T(8,128)(2,1)S(1)} %collective-permute-done.12.refs_0_, bf16[192,1024]{1,0:T(8,128)(2,1)S(1)} %collective-permute-done.11.rest_2_.refs_1_, ...), custom_call_target="tpu_custom_call" | custom-call | flops 1024 | bytes 1024 | tf_op jit(solution)/shard_map/pallas_call | solution.py:287
  90.3 2.5 %shard_map.104 = (bf16[192,1024]{1,0:T(8,128)(2,1)S(1)}, f32[192,1024]{1,0:T(8,128)S(1)}, bf16[192,2048]{1,0:T(8,128)(2,1)S(1)}, bf16[576,512]{1,0:T(8,128)(2,1)S(1)}) custom-call(s32[9]{0:T(128)S(1)} %fusion.3.plan_ref, f32[384,1024]{1,0:T(8,128)S(1)} %get-tuple-element.39.sums_ref, bf16[384,1024]{1,0:T(8,128)(2,1)S(1)} %collective-permute-done.16.got_ref, ...), custom_call_target="tpu_custom_call" | custom-call | flops 1024 | bytes 1024 | tf_op jit(solution)/shard_map/pallas_call | solution.py:383
  92.8 3.4 %collective-permute-start.23 = (bf16[192,1024]{1,0:T(8,128)(2,1)S(1)}, bf16[192,1024]{1,0:T(8,128)(2,1)S(1)}, u32[]{:S(2)}, u32[]{:S(2)}) collective-permute-start(bf16[192,1024]{1,0:T(8,128)(2,1)S(1)} %get-tuple-element.52), channel_id=1, source_target_pairs={{0,2},{1,3},{2,0},{3,1},{12,14},{13,15},{14,12},{15,13},{16,18},{1... | collective-permute-start | bytes 1179656 | tf_op jit(solution)/shard_map/ppermute | solution.py:427
  100.6 6.0 %collective-permute-done.23 = bf16[192,1024]{1,0:T(8,128)(2,1)S(1)} collective-permute-done((bf16[192,1024]{1,0:T(8,128)(2,1)S(1)}, bf16[192,1024]{1,0:T(8,128)(2,1)S(1)}, u32[]{:S(2)}, u32[]{:S(2)}) %collective-permute-start.23) | collective-permute-done | bytes 393248 | tf_op jit(solution)/shard_map/ppermute | solution.py:427
  108.1 7.0 %collective-permute-done.21 = bf16[192,1024]{1,0:T(8,128)(2,1)S(1)} collective-permute-done((bf16[192,1024]{1,0:T(8,128)(2,1)S(1)}, bf16[192,1024]{1,0:T(8,128)(2,1)S(1)}, u32[]{:S(2)}, u32[]{:S(2)}) %collective-permute-start.21) | collective-permute-done | bytes 393248 | tf_op jit(solution)/shard_map/ppermute | solution.py:107
  119.9 3.6 %collective-permute-done.26 = bf16[192,1024]{1,0:T(8,128)(2,1)S(1)} collective-permute-done((bf16[192,1024]{1,0:T(8,128)(2,1)S(1)}, bf16[192,1024]{1,0:T(8,128)(2,1)S(1)}, u32[]{:S(2)}, u32[]{:S(2)}) %collective-permute-start.26) | collective-permute-done | bytes 393248 | tf_op jit(solution)/shard_map/ppermute | solution.py:107
  123.6 6.6 %collective-permute-start.27 = (bf16[192,1024]{1,0:T(8,128)(2,1)S(1)}, bf16[192,1024]{1,0:T(8,128)(2,1)S(1)}, u32[]{:S(2)}, u32[]{:S(2)}) collective-permute-start(bf16[192,1024]{1,0:T(8,128)(2,1)S(1)} %add_convert_fusion.1), channel_id=1, source_target_pairs={{0,4},{4,0},{8,12},{12,8},{1,5},{5,1},{9,13},{13,9},{2,6},{6,2},{1... | collective-permute-start | bytes 1179656 | tf_op jit(solution)/shard_map/ppermute | solution.py:115
  131.3 9.2 %collective-permute-done.25 = bf16[192,1024]{1,0:T(8,128)(2,1)S(1)} collective-permute-done((bf16[192,1024]{1,0:T(8,128)(2,1)S(1)}, bf16[192,1024]{1,0:T(8,128)(2,1)S(1)}, u32[]{:S(2)}, u32[]{:S(2)}) %collective-permute-start.25) | collective-permute-done | bytes 393248 | tf_op jit(solution)/shard_map/ppermute | solution.py:115
  140.7 6.2 %collective-permute-done.27 = bf16[192,1024]{1,0:T(8,128)(2,1)S(1)} collective-permute-done((bf16[192,1024]{1,0:T(8,128)(2,1)S(1)}, bf16[192,1024]{1,0:T(8,128)(2,1)S(1)}, u32[]{:S(2)}, u32[]{:S(2)}) %collective-permute-start.27) | collective-permute-done | bytes 393248 | tf_op jit(solution)/shard_map/ppermute | solution.py:115
  (119 shorter events, 47.3 us)
Async XLA Ops:
  4.5 21.4 %collective-permute-start = (bf16[400,1024]{1,0:T(8,128)(2,1)S(1)}, bf16[400,1024]{1,0:T(8,128)(2,1)}, u32[]{:S(2)}, u32[]{:S(2)}) collective-permute-start(bf16[400,1024]{1,0:T(8,128)(2,1)S(1)} %shard_map.91.refs_1_.inner_ref.outer_ref), channel_id=1, source_target_pairs={{0,4},{4,0},{8,12},{12,8},{1,5},{5,1},{9,13},{13,9},{2,6},{6,2},{1... | collective-permute-start | bytes 2457608 | tf_op jit(solution)/shard_map/ppermute | solution.py:115
  7.6 21.7 %collective-permute-start.3 = (bf16[400,1024]{1,0:T(8,128)(2,1)S(1)}, bf16[400,1024]{1,0:T(8,128)(2,1)}, u32[]{:S(2)}, u32[]{:S(2)}) collective-permute-start(bf16[400,1024]{1,0:T(8,128)(2,1)S(1)} %shard_map.91.refs_1_.inner_ref.outer_ref), channel_id=1, source_target_pairs={{4,8},{8,4},{5,9},{9,5},{6,10},{10,6},{7,11},{11,7},{20,24},{24,20... | collective-permute-start | bytes 2457608 | tf_op jit(solution)/shard_map/ppermute | solution.py:115
  9.2 21.4 %collective-permute-start.7 = (bf16[384,1024]{1,0:T(8,128)(2,1)}, bf16[384,1024]{1,0:T(8,128)(2,1)}, u32[]{:S(2)}, u32[]{:S(2)}) collective-permute-start(bf16[384,1024]{1,0:T(8,128)(2,1)} %refs_0_.1), channel_id=1, source_target_pairs={{0,2},{1,3},{2,0},{3,1},{4,6},{5,7},{6,4},{7,5},{8,10},{9,11},{10,... | collective-permute-start | bytes 2359304 | tf_op jit(solution)/shard_map/ppermute | solution.py:107
  15.6 25.7 %collective-permute-start.9 = (bf16[2048,512]{1,0:T(8,128)(2,1)}, bf16[2048,512]{1,0:T(8,128)(2,1)S(1)}, u32[]{:S(2)}, u32[]{:S(2)}) collective-permute-start(bf16[2048,512]{1,0:T(8,128)(2,1)} %shard_map.93), channel_id=1, source_target_pairs={{0,1},{1,0},{2,3},{3,2},{4,5},{5,4},{6,7},{7,6},{8,9},{9,8},{10,11... | collective-permute-start | bytes 6291464 | tf_op jit(solution)/shard_map/ppermute | solution.py:111
  26.0 13.7 %collective-permute-start.1 = (bf16[400,1024]{1,0:T(8,128)(2,1)}, bf16[400,1024]{1,0:T(8,128)(2,1)}, u32[]{:S(2)}, u32[]{:S(2)}) collective-permute-start(bf16[400,1024]{1,0:T(8,128)(2,1)} %collective-permute-done.refs_0_.inner_ref.outer_ref), channel_id=1, source_target_pairs={{4,8},{8,4},{5,9},{9,5},{6,10},{10,6},{7,11},{11,7},{20,24},{24,20... | collective-permute-start | bytes 2457608 | tf_op jit(solution)/shard_map/ppermute | solution.py:115
  27.6 20.8 %collective-permute-start.6 = (bf16[400,1024]{1,0:T(8,128)(2,1)}, bf16[400,1024]{1,0:T(8,128)(2,1)S(1)}, u32[]{:S(2)}, u32[]{:S(2)}) collective-permute-start(bf16[400,1024]{1,0:T(8,128)(2,1)} %collective-permute-done.refs_0_.inner_ref.outer_ref), channel_id=1, source_target_pairs={{0,2},{1,3},{2,0},{3,1},{4,6},{5,7},{6,4},{7,5},{8,10},{9,11},{10,... | collective-permute-start | bytes 2457608 | tf_op jit(solution)/shard_map/ppermute | solution.py:107
  29.3 21.8 %collective-permute-start.5 = (bf16[400,1024]{1,0:T(8,128)(2,1)}, bf16[400,1024]{1,0:T(8,128)(2,1)S(1)}, u32[]{:S(2)}, u32[]{:S(2)}) collective-permute-start(bf16[400,1024]{1,0:T(8,128)(2,1)} %collective-permute-done.3.refs_0_.inner_ref), channel_id=1, source_target_pairs={{4,0},{8,12},{5,1},{9,13},{6,2},{10,14},{7,3},{11,15},{20,16},{24,... | collective-permute-start | bytes 2457608 | tf_op jit(solution)/shard_map/ppermute | solution.py:115
  32.6 15.8 %collective-permute-start.8 = (bf16[192,1024]{1,0:T(8,128)(2,1)S(1)}, bf16[192,1024]{1,0:T(8,128)(2,1)S(1)}, u32[]{:S(2)}, u32[]{:S(2)}) collective-permute-start(bf16[192,1024]{1,0:T(8,128)(2,1)S(1)} %shard_map.92), channel_id=1, source_target_pairs={{0,4},{12,8},{1,5},{13,9},{2,6},{14,10},{3,7},{15,11},{16,20},{28,... | collective-permute-start | bytes 1179656 | tf_op jit(solution)/shard_map/ppermute | solution.py:115
  39.7 21.6 %collective-permute-start.4 = (bf16[400,1024]{1,0:T(8,128)(2,1)}, bf16[400,1024]{1,0:T(8,128)(2,1)}, u32[]{:S(2)}, u32[]{:S(2)}) collective-permute-start(bf16[400,1024]{1,0:T(8,128)(2,1)} %collective-permute-done.3.refs_0_.inner_ref), channel_id=1, source_target_pairs={{4,6},{5,7},{6,4},{7,5},{8,10},{9,11},{10,8},{11,9},{20,22},{21,23... | collective-permute-start | bytes 2457608 | tf_op jit(solution)/shard_map/ppermute | solution.py:427
  41.2 29.0 %collective-permute-start.2 = (bf16[400,1024]{1,0:T(8,128)(2,1)}, bf16[400,1024]{1,0:T(8,128)(2,1)}, u32[]{:S(2)}, u32[]{:S(2)}) collective-permute-start(bf16[400,1024]{1,0:T(8,128)(2,1)} %collective-permute-done.1.refs_2_.inner_ref.refs_0_), channel_id=1, source_target_pairs={{4,0},{8,12},{5,1},{9,13},{6,2},{10,14},{7,3},{11,15},{20,16},{24,... | collective-permute-start | bytes 2457608 | tf_op jit(solution)/shard_map/ppermute | solution.py:115
  52.0 20.1 %collective-permute-start.10 = (bf16[400,1024]{1,0:T(8,128)(2,1)}, bf16[400,1024]{1,0:T(8,128)(2,1)S(1)}, u32[]{:S(2)}, u32[]{:S(2)}) collective-permute-start(bf16[400,1024]{1,0:T(8,128)(2,1)} %shard_map.95.refs_1_.outer_ref), channel_id=1, source_target_pairs={{0,2},{1,3},{2,0},{3,1},{12,14},{13,15},{14,12},{15,13},{16,18},{1... | collective-permute-start | bytes 2457608 | tf_op jit(solution)/shard_map/ppermute | solution.py:427
  55.2 22.5 %collective-permute-start.15 = (bf16[384,1024]{1,0:T(8,128)(2,1)}, bf16[384,1024]{1,0:T(8,128)(2,1)S(1)}, u32[]{:S(2)}, u32[]{:S(2)}) collective-permute-start(bf16[384,1024]{1,0:T(8,128)(2,1)} %copy-done.19), channel_id=1, source_target_pairs={{0,1},{1,0},{2,3},{3,2},{4,5},{5,4},{6,7},{7,6},{8,9},{9,8},{10,11... | collective-permute-start | bytes 2359304 | tf_op jit(solution)/shard_map/ppermute | solution.py:111
  60.7 18.9 %collective-permute-start.14 = (bf16[384,1024]{1,0:T(8,128)(2,1)S(1)}, bf16[384,1024]{1,0:T(8,128)(2,1)S(1)}, u32[]{:S(2)}, u32[]{:S(2)}) collective-permute-start(bf16[384,1024]{1,0:T(8,128)(2,1)S(1)} %get-tuple-element.34), channel_id=1, source_target_pairs={{0,1},{1,0},{2,3},{3,2},{4,5},{5,4},{6,7},{7,6},{8,9},{9,8},{10,11... | collective-permute-start | bytes 2359304 | tf_op jit(solution)/shard_map/ppermute | solution.py:111
  61.2 24.7 %collective-permute-start.13 = (bf16[192,1024]{1,0:T(8,128)(2,1)S(1)}, bf16[192,1024]{1,0:T(8,128)(2,1)S(1)}, u32[]{:S(2)}, u32[]{:S(2)}) collective-permute-start(bf16[192,1024]{1,0:T(8,128)(2,1)S(1)} %collective-permute-done.11.rest_2_.refs_1_), channel_id=1, source_target_pairs={{4,0},{8,12},{5,1},{9,13},{6,2},{10,14},{7,3},{11,15},{20,16},{24,... | collective-permute-start | bytes 1179656 | tf_op jit(solution)/shard_map/ppermute | solution.py:115
  74.1 11.8 %collective-permute-start.12 = (bf16[192,1024]{1,0:T(8,128)(2,1)S(1)}, bf16[192,1024]{1,0:T(8,128)(2,1)S(1)}, u32[]{:S(2)}, u32[]{:S(2)}) collective-permute-start(bf16[192,1024]{1,0:T(8,128)(2,1)S(1)} %shard_map.97), channel_id=1, source_target_pairs={{0,2},{1,3},{2,0},{3,1},{4,6},{5,7},{6,4},{7,5},{8,10},{9,11},{10,... | collective-permute-start | bytes 1179656 | tf_op jit(solution)/shard_map/ppermute | solution.py:107
  74.7 15.4 %collective-permute-start.18 = (bf16[256,2048]{1,0:T(8,128)(2,1)S(1)}, bf16[256,2048]{1,0:T(8,128)(2,1)S(1)}, u32[]{:S(2)}, u32[]{:S(2)}) collective-permute-start(bf16[256,2048]{1,0:T(8,128)(2,1)S(1)} %copy-done.20), channel_id=1, source_target_pairs={{0,1},{1,0},{2,3},{3,2},{4,5},{5,4},{6,7},{7,6},{8,9},{9,8},{10,11... | collective-permute-start | bytes 3145736 | tf_op jit(solution)/shard_map/ppermute | solution.py:111
  92.8 13.8 %collective-permute-start.23 = (bf16[192,1024]{1,0:T(8,128)(2,1)S(1)}, bf16[192,1024]{1,0:T(8,128)(2,1)S(1)}, u32[]{:S(2)}, u32[]{:S(2)}) collective-permute-start(bf16[192,1024]{1,0:T(8,128)(2,1)S(1)} %get-tuple-element.52), channel_id=1, source_target_pairs={{0,2},{1,3},{2,0},{3,1},{12,14},{13,15},{14,12},{15,13},{16,18},{1... | collective-permute-start | bytes 1179656 | tf_op jit(solution)/shard_map/ppermute | solution.py:427
  96.2 20.4 %collective-permute-start.19 = (bf16[192,2048]{1,0:T(8,128)(2,1)S(1)}, bf16[192,2048]{1,0:T(8,128)(2,1)S(1)}, u32[]{:S(2)}, u32[]{:S(2)}) collective-permute-start(bf16[192,2048]{1,0:T(8,128)(2,1)S(1)} %get-tuple-element.47), channel_id=1, source_target_pairs={{4,8},{8,4},{5,9},{9,5},{6,10},{10,6},{7,11},{11,7},{20,24},{24,20... | collective-permute-start | bytes 2359304 | tf_op jit(solution)/shard_map/ppermute | solution.py:115
  98.5 16.6 %collective-permute-start.21 = (bf16[192,1024]{1,0:T(8,128)(2,1)S(1)}, bf16[192,1024]{1,0:T(8,128)(2,1)S(1)}, u32[]{:S(2)}, u32[]{:S(2)}) collective-permute-start(bf16[192,1024]{1,0:T(8,128)(2,1)S(1)} %get-tuple-element.50), channel_id=1, source_target_pairs={{0,2},{1,3},{2,0},{3,1},{4,6},{5,7},{6,4},{7,5},{8,10},{9,11},{10,... | collective-permute-start | bytes 1179656 | tf_op jit(solution)/shard_map/ppermute | solution.py:107
  99.1 24.4 %collective-permute-start.26 = (bf16[192,1024]{1,0:T(8,128)(2,1)S(1)}, bf16[192,1024]{1,0:T(8,128)(2,1)S(1)}, u32[]{:S(2)}, u32[]{:S(2)}) collective-permute-start(bf16[192,1024]{1,0:T(8,128)(2,1)S(1)} %get-tuple-element.54), channel_id=1, source_target_pairs={{0,2},{1,3},{2,0},{3,1},{4,6},{5,7},{6,4},{7,5},{8,10},{9,11},{10,... | collective-permute-start | bytes 1179656 | tf_op jit(solution)/shard_map/ppermute | solution.py:107
  115.2 15.0 %collective-permute-start.22 = (bf16[192,1024]{1,0:T(8,128)(2,1)S(1)}, bf16[192,1024]{1,0:T(8,128)(2,1)S(1)}, u32[]{:S(2)}, u32[]{:S(2)}) collective-permute-start(bf16[192,1024]{1,0:T(8,128)(2,1)S(1)} %add_convert_fusion.4), channel_id=1, source_target_pairs={{0,8},{12,4},{1,9},{13,5},{2,10},{14,6},{3,11},{15,7},{16,24},{28,... | collective-permute-start | bytes 1179656 | tf_op jit(solution)/shard_map/ppermute | solution.py:115
  116.9 14.4 %collective-permute-start.20 = (bf16[192,1024]{1,0:T(8,128)(2,1)S(1)}, bf16[192,1024]{1,0:T(8,128)(2,1)S(1)}, u32[]{:S(2)}, u32[]{:S(2)}) collective-permute-start(bf16[192,1024]{1,0:T(8,128)(2,1)S(1)} %fusion), channel_id=1, source_target_pairs={{0,2},{1,3},{2,0},{3,1},{4,6},{5,7},{6,4},{7,5},{8,10},{9,11},{10,... | collective-permute-start | bytes 1179656 | tf_op jit(solution)/shard_map/ppermute | solution.py:107
  118.6 21.8 %collective-permute-start.25 = (bf16[192,1024]{1,0:T(8,128)(2,1)S(1)}, bf16[192,1024]{1,0:T(8,128)(2,1)S(1)}, u32[]{:S(2)}, u32[]{:S(2)}) collective-permute-start(bf16[192,1024]{1,0:T(8,128)(2,1)S(1)} %add_convert_fusion.2), channel_id=1, source_target_pairs={{4,12},{8,0},{5,13},{9,1},{6,14},{10,2},{7,15},{11,3},{20,28},{24,... | collective-permute-start | bytes 1179656 | tf_op jit(solution)/shard_map/ppermute | solution.py:115
  123.6 23.3 %collective-permute-start.27 = (bf16[192,1024]{1,0:T(8,128)(2,1)S(1)}, bf16[192,1024]{1,0:T(8,128)(2,1)S(1)}, u32[]{:S(2)}, u32[]{:S(2)}) collective-permute-start(bf16[192,1024]{1,0:T(8,128)(2,1)S(1)} %add_convert_fusion.1), channel_id=1, source_target_pairs={{0,4},{4,0},{8,12},{12,8},{1,5},{5,1},{9,13},{13,9},{2,6},{6,2},{1... | collective-permute-start | bytes 1179656 | tf_op jit(solution)/shard_map/ppermute | solution.py:115
  (32 other events, 164.2 us)

commit v14 on v13

--- a/solution.py
+++ b/solution.py
@@ -489,9 +489,8 @@
     beside = along(joined(kept[2], sent[2]).astype(jnp.bfloat16), BESIDE)
     own_sent = (sent[3].astype(jnp.float32) + middle[:, width:]).astype(jnp.bfloat16)
     own_sum = joined(kept[3] + middle[:, :width], own_sent)
-    arrived = [block.astype(jnp.float32) for block in (two_in, two_out)]
-    total = lax.optimization_barrier(own_sum + sum(arrived))
-    return (total + beside.astype(jnp.float32)).astype(jnp.bfloat16)
+    total = lax.optimization_barrier(two_in.astype(jnp.float32) + two_out.astype(jnp.float32))
+    return (total + own_sum + beside.astype(jnp.float32)).astype(jnp.bfloat16)
 
 
 def on_device(*args):

time: 149 us -> 146 us (0.980)
  starting transfers between devices: 44 us -> 37.5 us
  waiting for transfers between devices: 52.4 us -> 56.5 us
    ppermute x13, starting transfers between devices: 28 us -> 21.2 us  [along(): return lax.ppermute(block, 'blk', route)]
    ppermute x6, waiting for transfers between devices: 11.7 us -> 14.6 us  [across_chips(): return lax.ppermute(block, 'tp', [(i, i ^ 2) for i in range(4)])]
  transfers between devices with their start and end apart: 28 -> 28, of which waited for: 11 -> 10; matrix products, arithmetic and copies ran while one was open for 7% -> 7% of each run, Pallas kernels for 18% -> 18%
where the time goes in v14:
time: 146 us; the launch traced here: 145 us
  waiting for transfers between devices  56.5 us (39%)
  starting transfers between devices  37.5 us (26%)
  Pallas kernels  30.5 us (21%)
  local copies, waits for them, and re-layouts  15.5 us (11%)
  other arithmetic  4.8 us (3%)
    ppermute x13, waiting for transfers between devices, along(): return lax.ppermute(block, 'blk', route)  33.8 us
    ppermute x13, starting transfers between devices, along(): return lax.ppermute(block, 'blk', route)  21.2 us
    pallas_call x5, Pallas kernels, partial_sums(): return on_core(body, shapes + [TOKEN], specs)(*operands, *waits)  14.8 us
    ppermute x6, waiting for transfers between devices, across_chips(): return lax.ppermute(block, 'tp', [(i, i ^ 2) for i in range(4)])  14.6 us
    unnamed x56, local copies, waits for them, and re-layouts  8.75 us
    ppermute x3, waiting for transfers between devices, at_kind(): return lax.ppermute(block, ('blk', 'tp'), pairs)  7.89 us
    ppermute x3, starting transfers between devices, at_kind(): return lax.ppermute(block, ('blk', 'tp'), pairs)  7.69 us
    ppermute x6, starting transfers between devices, across_chips(): return lax.ppermute(block, 'tp', [(i, i ^ 2) for i in range(4)])  7.46 us
  transfers between devices with their start and end apart: 28, of which 10 were waited for; matrix products, arithmetic and copies ran while one was open for 7% of the time, Pallas kernels for 18%

profile of v14, /device:TPU:0, one launch (start us, length us, event | category | flops | bytes accessed | tf_op | source)
XLA Modules:
  0.0 145.4 jit_solution(5135618214490924988)
XLA Ops:
  4.5 3.1 %collective-permute-start = (bf16[400,1024]{1,0:T(8,128)(2,1)S(1)}, bf16[400,1024]{1,0:T(8,128)(2,1)}, u32[]{:S(2)}, u32[]{:S(2)}) collective-permute-start(bf16[400,1024]{1,0:T(8,128)(2,1)S(1)} %shard_map.91.refs_1_.inner_ref.outer_ref), channel_id=1, source_target_pairs={{0,4},{4,0},{8,12},{12,8},{1,5},{5,1},{9,13},{13,9},{2,6},{6,2},{1... | collective-permute-start | bytes 2457608 | tf_op jit(solution)/shard_map/ppermute | solution.py:115
  10.7 3.4 %dynamic-slice_bitcast_fusion.4 = (bf16[1024,256]{1,0:T(8,128)(2,1)S(1)}, bf16[1024,256]{1,0:T(8,128)(2,1)S(1)}, bf16[1024,256]{1,0:T(8,128)(2,1)S(1)}, bf16[102...) fusion(bf16[4,1024,256]{2,1,0:T(8,128)(2,1)} %bitcast.32, ...), kind=kLoop, calls=%fused_computation.21 | loop fusion | bytes 8388624 | tf_op jit(solution)/shard_map/jit(dynamic_index_in_dim)/squeeze | solution.py:413
  16.2 2.7 %dynamic-slice_bitcast_fusion.1 = (bf16[256,1024]{1,0:T(8,128)(2,1)}, bf16[256,1024]{1,0:T(8,128)(2,1)S(1)}, bf16[256,1024]{1,0:T(8,128)(2,1)S(1)}, bf16[256,1024]{1,0:T(8,128)(2,1)}) fusion(bf16[1,256,4096]{2,1,0:T(8,128)(2,1)} %param.12, s32[]{:T(128)S(6)} %select_n.39, s32[]{:T(128)S(6)} %select_n.34, s32[]{:T(128)S(6)} %select_n.33, s32[]{:T(128)S(6)} %select_n.40), kind=kLoop, calls=%fused_computation.18 | loop fusion | bytes 4194320 | tf_op jit(solution)/shard_map/dynamic_slice | solution.py:419
  18.9 7.1 %collective-permute-done.refs_0_.inner_ref.outer_ref = bf16[400,1024]{1,0:T(8,128)(2,1)} collective-permute-done((bf16[400,1024]{1,0:T(8,128)(2,1)S(1)}, bf16[400,1024]{1,0:T(8,128)(2,1)}, u32[]{:S(2)}, u32[]{:S(2)}) %collective-permute-start) | collective-permute-done | bytes 819232 | tf_op jit(solution)/shard_map/ppermute | solution.py:115
  30.6 2.0 %shard_map.92 = bf16[192,1024]{1,0:T(8,128)(2,1)S(1)} custom-call(s32[9]{0:T(128)S(1)} %fusion.5.plan_ref, bf16[384,1024]{1,0:T(8,128)(2,1)} %collective-permute-done.7.inner_ref.outer_ref.refs_1_, bf16[384,1024]{1,0:T(8,128)(2,1)} %collective-permute-done.7.inner_ref.outer_ref.refs_1_), custom_call_target="tpu_custom_call" | custom-call | flops 17179869184 | bytes 1024 | tf_op jit(solution)/shard_map/pallas_call | solution.py:192
  32.6 5.6 %collective-permute-start.8 = (bf16[192,1024]{1,0:T(8,128)(2,1)S(1)}, bf16[192,1024]{1,0:T(8,128)(2,1)S(1)}, u32[]{:S(2)}, u32[]{:S(2)}) collective-permute-start(bf16[192,1024]{1,0:T(8,128)(2,1)S(1)} %shard_map.92), channel_id=1, source_target_pairs={{0,4},{12,8},{1,5},{13,9},{2,6},{14,10},{3,7},{15,11},{16,20},{28,... | collective-permute-start | bytes 1179656 | tf_op jit(solution)/shard_map/ppermute | solution.py:115
  42.5 3.2 %shard_map.94 = (f32[384,1024]{1,0:T(8,128)S(1)}, bf16[384,1024]{1,0:T(8,128)(2,1)S(1)}, f32[8,128]{1,0:T(8,128)S(1)}) custom-call(s32[9]{0:T(128)S(1)} %fusion.5.plan_ref, bf16[384,1024]{1,0:T(8,128)(2,1)} %refs_0_.1, bf16[384,1024]{1,0:T(8,128)(2,1)} %collective-permute-done.7.inner_ref.outer_ref.refs_1_, ...), custom_call_target="tpu_custom_call" | custom-call | flops 1024 | bytes 1024 | tf_op jit(solution)/shard_map/pallas_call | solution.py:287
  48.4 2.6 %collective-permute-done.5.refs_0_ = bf16[400,1024]{1,0:T(8,128)(2,1)S(1)} collective-permute-done((bf16[400,1024]{1,0:T(8,128)(2,1)}, bf16[400,1024]{1,0:T(8,128)(2,1)S(1)}, u32[]{:S(2)}, u32[]{:S(2)}) %collective-permute-start.5) | collective-permute-done | bytes 819232 | tf_op jit(solution)/shard_map/ppermute | solution.py:115
  52.0 2.6 %collective-permute-start.10 = (bf16[400,1024]{1,0:T(8,128)(2,1)}, bf16[400,1024]{1,0:T(8,128)(2,1)S(1)}, u32[]{:S(2)}, u32[]{:S(2)}) collective-permute-start(bf16[400,1024]{1,0:T(8,128)(2,1)} %shard_map.95.refs_1_.outer_ref), channel_id=1, source_target_pairs={{0,2},{1,3},{2,0},{3,1},{12,14},{13,15},{14,12},{15,13},{16,18},{1... | collective-permute-start | bytes 2457608 | tf_op jit(solution)/shard_map/ppermute | solution.py:427
  57.7 3.0 %shard_map.96 = (f32[384,1024]{1,0:T(8,128)S(1)}, bf16[384,1024]{1,0:T(8,128)(2,1)S(1)}, f32[8,128]{1,0:T(8,128)S(1)}) custom-call(s32[9]{0:T(128)S(1)} %fusion.5.plan_ref, bf16[400,1024]{1,0:T(8,128)(2,1)} %collective-permute-done.refs_0_.inner_ref.outer_ref, bf16[400,1024]{1,0:T(8,128)(2,1)S(1)} %copy-done.10, bf16[1024,512]{1,0:T(8,128)(2,1)S(1)} %copy-done.3, ...), custom_call_target="tpu_custom_call" | custom-call | flops 1024 | bytes 1024 | tf_op jit(solution)/shard_map/pallas_call | solution.py:287
  62.7 7.5 %collective-permute-done.2.outer_ref.refs_1_ = bf16[400,1024]{1,0:T(8,128)(2,1)} collective-permute-done((bf16[400,1024]{1,0:T(8,128)(2,1)}, bf16[400,1024]{1,0:T(8,128)(2,1)}, u32[]{:S(2)}, u32[]{:S(2)}) %collective-permute-start.2) | collective-permute-done | bytes 819232 | tf_op jit(solution)/shard_map/ppermute | solution.py:115
  72.1 2.0 %shard_map.97 = bf16[192,1024]{1,0:T(8,128)(2,1)S(1)} custom-call(s32[9]{0:T(128)S(1)} %fusion.5.plan_ref, bf16[400,1024]{1,0:T(8,128)(2,1)} %collective-permute-done.1.refs_2_.inner_ref.refs_0_, bf16[400,1024]{1,0:T(8,128)(2,1)} %collective-permute-done.2.outer_ref.refs_1_, bf16[400,1024]{1,0:T(8,128)(2,1)} %collective-permute-done.4.rest_0_.refs_2_, ...), custom_call_target="tpu_custom_call" | custom-call | flops 1024 | bytes 1024 | tf_op jit(solution)/shard_map/pallas_call | solution.py:192
  74.7 3.0 %shard_map.98 = (f32[384,1024]{1,0:T(8,128)S(1)}, f32[8,128]{1,0:T(8,128)}) custom-call(s32[9]{0:T(128)S(1)} %fusion.5.plan_ref, bf16[400,1024]{1,0:T(8,128)(2,1)} %collective-permute-done.1.refs_2_.inner_ref.refs_0_, bf16[400,1024]{1,0:T(8,128)(2,1)} %collective-permute-done.2.outer_ref.refs_1_, bf16[1024,512]{1,0:T(8,128)(2,1)S(1)} %copy-done.4, ...), custom_call_target="tpu_custom_call" | custom-call | flops 1024 | bytes 1024 | tf_op jit(solution)/shard_map/pallas_call | solution.py:287
  79.6 2.2 %shard_map.100 = (f32[768,512]{1,0:T(8,128)S(1)}, f32[8,128]{1,0:T(8,128)S(1)}) custom-call(s32[9]{0:T(128)S(1)} %fusion.5.plan_ref, f32[384,1024]{1,0:T(8,128)S(1)} %get-tuple-element.33.sums_ref, bf16[384,1024]{1,0:T(8,128)(2,1)S(1)} %collective-permute-done.14.got_ref, bf16[400,1024]{1,0:T(8,128)(2,1)} %collective-permute-done.refs_0_.inner_ref.outer_ref, ...), custom_call_target="tpu_custom_call" | custom-call | flops 1024 | bytes 1024 | tf_op jit(solution)/shard_map/pallas_call | solution.py:346
  81.8 3.7 %shard_map.102 = (f32[384,1024]{1,0:T(8,128)S(1)}, bf16[384,1024]{1,0:T(8,128)(2,1)S(1)}, f32[8,128]{1,0:T(8,128)}) custom-call(s32[9]{0:T(128)S(1)} %fusion.5.plan_ref, bf16[400,1024]{1,0:T(8,128)(2,1)} %collective-permute-done.3.refs_0_.inner_ref, bf16[400,1024]{1,0:T(8,128)(2,1)S(1)} %copy-done.8, ...), custom_call_target="tpu_custom_call" | custom-call | flops 1024 | bytes 1024 | tf_op jit(solution)/shard_map/pallas_call | solution.py:287
  85.9 2.0 %shard_map.101 = (f32[384,1024]{1,0:T(8,128)S(1)}, bf16[384,1024]{1,0:T(8,128)(2,1)S(1)}, f32[8,128]{1,0:T(8,128)}) custom-call(s32[9]{0:T(128)S(1)} %fusion.5.plan_ref, bf16[192,1024]{1,0:T(8,128)(2,1)S(1)} %collective-permute-done.12.refs_0_, bf16[192,1024]{1,0:T(8,128)(2,1)S(1)} %collective-permute-done.11.rest_2_.refs_1_, ...), custom_call_target="tpu_custom_call" | custom-call | flops 1024 | bytes 1024 | tf_op jit(solution)/shard_map/pallas_call | solution.py:287
  88.2 1.9 %shard_map.103 = (f32[768,512]{1,0:T(8,128)S(1)}, f32[8,128]{1,0:T(8,128)}) custom-call(s32[9]{0:T(128)S(1)} %fusion.5.plan_ref, f32[384,1024]{1,0:T(8,128)S(1)} %get-tuple-element.41.sums_ref, bf16[384,1024]{1,0:T(8,128)(2,1)S(1)} %collective-permute-done.17.got_ref, bf16[400,1024]{1,0:T(8,128)(2,1)} %collective-permute-done.3.refs_0_.inner_ref, ...), custom_call_target="tpu_custom_call" | custom-call | flops 1024 | bytes 1024 | tf_op jit(solution)/shard_map/pallas_call | solution.py:346
  90.3 2.5 %shard_map.104 = (bf16[192,1024]{1,0:T(8,128)(2,1)S(1)}, f32[192,1024]{1,0:T(8,128)S(1)}, bf16[192,2048]{1,0:T(8,128)(2,1)S(1)}, bf16[576,512]{1,0:T(8,128)(2,1)S(1)}) custom-call(s32[9]{0:T(128)S(1)} %fusion.5.plan_ref, f32[384,1024]{1,0:T(8,128)S(1)} %get-tuple-element.39.sums_ref, bf16[384,1024]{1,0:T(8,128)(2,1)S(1)} %collective-permute-done.16.got_ref, ...), custom_call_target="tpu_custom_call" | custom-call | flops 1024 | bytes 1024 | tf_op jit(solution)/shard_map/pallas_call | solution.py:383
  92.8 3.6 %collective-permute-start.21 = (bf16[192,1024]{1,0:T(8,128)(2,1)S(1)}, bf16[192,1024]{1,0:T(8,128)(2,1)S(1)}, u32[]{:S(2)}, u32[]{:S(2)}) collective-permute-start(bf16[192,1024]{1,0:T(8,128)(2,1)S(1)} %get-tuple-element.49), channel_id=1, source_target_pairs={{0,2},{1,3},{2,0},{3,1},{12,14},{13,15},{14,12},{15,13},{16,18},{1... | collective-permute-start | bytes 1179656 | tf_op jit(solution)/shard_map/ppermute | solution.py:427
  100.7 6.0 %collective-permute-done.21 = bf16[192,1024]{1,0:T(8,128)(2,1)S(1)} collective-permute-done((bf16[192,1024]{1,0:T(8,128)(2,1)S(1)}, bf16[192,1024]{1,0:T(8,128)(2,1)S(1)}, u32[]{:S(2)}, u32[]{:S(2)}) %collective-permute-start.21) | collective-permute-done | bytes 393248 | tf_op jit(solution)/shard_map/ppermute | solution.py:427
  108.1 7.0 %collective-permute-done.26 = bf16[192,1024]{1,0:T(8,128)(2,1)S(1)} collective-permute-done((bf16[192,1024]{1,0:T(8,128)(2,1)S(1)}, bf16[192,1024]{1,0:T(8,128)(2,1)S(1)}, u32[]{:S(2)}, u32[]{:S(2)}) %collective-permute-start.26) | collective-permute-done | bytes 393248 | tf_op jit(solution)/shard_map/ppermute | solution.py:107
  115.3 7.6 %collective-permute-done.19 = bf16[192,1024]{1,0:T(8,128)(2,1)S(1)} collective-permute-done((bf16[192,1024]{1,0:T(8,128)(2,1)S(1)}, bf16[192,1024]{1,0:T(8,128)(2,1)S(1)}, u32[]{:S(2)}, u32[]{:S(2)}) %collective-permute-start.19) | collective-permute-done | bytes 393248 | tf_op jit(solution)/shard_map/ppermute | solution.py:107
  127.6 5.0 %collective-permute-done.20 = bf16[192,1024]{1,0:T(8,128)(2,1)S(1)} collective-permute-done((bf16[192,1024]{1,0:T(8,128)(2,1)S(1)}, bf16[192,1024]{1,0:T(8,128)(2,1)S(1)}, u32[]{:S(2)}, u32[]{:S(2)}) %collective-permute-start.20) | collective-permute-done | bytes 393248 | tf_op jit(solution)/shard_map/ppermute | solution.py:115
  132.5 11.6 %collective-permute-done.23 = bf16[192,1024]{1,0:T(8,128)(2,1)S(1)} collective-permute-done((bf16[192,1024]{1,0:T(8,128)(2,1)S(1)}, bf16[192,1024]{1,0:T(8,128)(2,1)S(1)}, u32[]{:S(2)}, u32[]{:S(2)}) %collective-permute-start.23) | collective-permute-done | bytes 393248 | tf_op jit(solution)/shard_map/ppermute | solution.py:115
  (119 shorter events, 44.1 us)
Async XLA Ops:
  4.5 21.4 %collective-permute-start = (bf16[400,1024]{1,0:T(8,128)(2,1)S(1)}, bf16[400,1024]{1,0:T(8,128)(2,1)}, u32[]{:S(2)}, u32[]{:S(2)}) collective-permute-start(bf16[400,1024]{1,0:T(8,128)(2,1)S(1)} %shard_map.91.refs_1_.inner_ref.outer_ref), channel_id=1, source_target_pairs={{0,4},{4,0},{8,12},{12,8},{1,5},{5,1},{9,13},{13,9},{2,6},{6,2},{1... | collective-permute-start | bytes 2457608 | tf_op jit(solution)/shard_map/ppermute | solution.py:115
  7.6 21.7 %collective-permute-start.3 = (bf16[400,1024]{1,0:T(8,128)(2,1)S(1)}, bf16[400,1024]{1,0:T(8,128)(2,1)}, u32[]{:S(2)}, u32[]{:S(2)}) collective-permute-start(bf16[400,1024]{1,0:T(8,128)(2,1)S(1)} %shard_map.91.refs_1_.inner_ref.outer_ref), channel_id=1, source_target_pairs={{4,8},{8,4},{5,9},{9,5},{6,10},{10,6},{7,11},{11,7},{20,24},{24,20... | collective-permute-start | bytes 2457608 | tf_op jit(solution)/shard_map/ppermute | solution.py:115
  9.2 21.4 %collective-permute-start.7 = (bf16[384,1024]{1,0:T(8,128)(2,1)}, bf16[384,1024]{1,0:T(8,128)(2,1)}, u32[]{:S(2)}, u32[]{:S(2)}) collective-permute-start(bf16[384,1024]{1,0:T(8,128)(2,1)} %refs_0_.1), channel_id=1, source_target_pairs={{0,2},{1,3},{2,0},{3,1},{4,6},{5,7},{6,4},{7,5},{8,10},{9,11},{10,... | collective-permute-start | bytes 2359304 | tf_op jit(solution)/shard_map/ppermute | solution.py:107
  15.6 25.7 %collective-permute-start.9 = (bf16[2048,512]{1,0:T(8,128)(2,1)}, bf16[2048,512]{1,0:T(8,128)(2,1)S(1)}, u32[]{:S(2)}, u32[]{:S(2)}) collective-permute-start(bf16[2048,512]{1,0:T(8,128)(2,1)} %shard_map.93), channel_id=1, source_target_pairs={{0,1},{1,0},{2,3},{3,2},{4,5},{5,4},{6,7},{7,6},{8,9},{9,8},{10,11... | collective-permute-start | bytes 6291464 | tf_op jit(solution)/shard_map/ppermute | solution.py:111
  26.0 13.7 %collective-permute-start.1 = (bf16[400,1024]{1,0:T(8,128)(2,1)}, bf16[400,1024]{1,0:T(8,128)(2,1)}, u32[]{:S(2)}, u32[]{:S(2)}) collective-permute-start(bf16[400,1024]{1,0:T(8,128)(2,1)} %collective-permute-done.refs_0_.inner_ref.outer_ref), channel_id=1, source_target_pairs={{4,8},{8,4},{5,9},{9,5},{6,10},{10,6},{7,11},{11,7},{20,24},{24,20... | collective-permute-start | bytes 2457608 | tf_op jit(solution)/shard_map/ppermute | solution.py:115
  27.6 20.8 %collective-permute-start.6 = (bf16[400,1024]{1,0:T(8,128)(2,1)}, bf16[400,1024]{1,0:T(8,128)(2,1)S(1)}, u32[]{:S(2)}, u32[]{:S(2)}) collective-permute-start(bf16[400,1024]{1,0:T(8,128)(2,1)} %collective-permute-done.refs_0_.inner_ref.outer_ref), channel_id=1, source_target_pairs={{0,2},{1,3},{2,0},{3,1},{4,6},{5,7},{6,4},{7,5},{8,10},{9,11},{10,... | collective-permute-start | bytes 2457608 | tf_op jit(solution)/shard_map/ppermute | solution.py:107
  29.3 21.8 %collective-permute-start.5 = (bf16[400,1024]{1,0:T(8,128)(2,1)}, bf16[400,1024]{1,0:T(8,128)(2,1)S(1)}, u32[]{:S(2)}, u32[]{:S(2)}) collective-permute-start(bf16[400,1024]{1,0:T(8,128)(2,1)} %collective-permute-done.3.refs_0_.inner_ref), channel_id=1, source_target_pairs={{4,0},{8,12},{5,1},{9,13},{6,2},{10,14},{7,3},{11,15},{20,16},{24,... | collective-permute-start | bytes 2457608 | tf_op jit(solution)/shard_map/ppermute | solution.py:115
  32.6 15.8 %collective-permute-start.8 = (bf16[192,1024]{1,0:T(8,128)(2,1)S(1)}, bf16[192,1024]{1,0:T(8,128)(2,1)S(1)}, u32[]{:S(2)}, u32[]{:S(2)}) collective-permute-start(bf16[192,1024]{1,0:T(8,128)(2,1)S(1)} %shard_map.92), channel_id=1, source_target_pairs={{0,4},{12,8},{1,5},{13,9},{2,6},{14,10},{3,7},{15,11},{16,20},{28,... | collective-permute-start | bytes 1179656 | tf_op jit(solution)/shard_map/ppermute | solution.py:115
  39.7 21.6 %collective-permute-start.4 = (bf16[400,1024]{1,0:T(8,128)(2,1)}, bf16[400,1024]{1,0:T(8,128)(2,1)}, u32[]{:S(2)}, u32[]{:S(2)}) collective-permute-start(bf16[400,1024]{1,0:T(8,128)(2,1)} %collective-permute-done.3.refs_0_.inner_ref), channel_id=1, source_target_pairs={{4,6},{5,7},{6,4},{7,5},{8,10},{9,11},{10,8},{11,9},{20,22},{21,23... | collective-permute-start | bytes 2457608 | tf_op jit(solution)/shard_map/ppermute | solution.py:427
  41.2 29.0 %collective-permute-start.2 = (bf16[400,1024]{1,0:T(8,128)(2,1)}, bf16[400,1024]{1,0:T(8,128)(2,1)}, u32[]{:S(2)}, u32[]{:S(2)}) collective-permute-start(bf16[400,1024]{1,0:T(8,128)(2,1)} %collective-permute-done.1.refs_2_.inner_ref.refs_0_), channel_id=1, source_target_pairs={{4,0},{8,12},{5,1},{9,13},{6,2},{10,14},{7,3},{11,15},{20,16},{24,... | collective-permute-start | bytes 2457608 | tf_op jit(solution)/shard_map/ppermute | solution.py:115
  52.0 20.1 %collective-permute-start.10 = (bf16[400,1024]{1,0:T(8,128)(2,1)}, bf16[400,1024]{1,0:T(8,128)(2,1)S(1)}, u32[]{:S(2)}, u32[]{:S(2)}) collective-permute-start(bf16[400,1024]{1,0:T(8,128)(2,1)} %shard_map.95.refs_1_.outer_ref), channel_id=1, source_target_pairs={{0,2},{1,3},{2,0},{3,1},{12,14},{13,15},{14,12},{15,13},{16,18},{1... | collective-permute-start | bytes 2457608 | tf_op jit(solution)/shard_map/ppermute | solution.py:427
  55.2 22.5 %collective-permute-start.15 = (bf16[384,1024]{1,0:T(8,128)(2,1)}, bf16[384,1024]{1,0:T(8,128)(2,1)S(1)}, u32[]{:S(2)}, u32[]{:S(2)}) collective-permute-start(bf16[384,1024]{1,0:T(8,128)(2,1)} %copy-done.19), channel_id=1, source_target_pairs={{0,1},{1,0},{2,3},{3,2},{4,5},{5,4},{6,7},{7,6},{8,9},{9,8},{10,11... | collective-permute-start | bytes 2359304 | tf_op jit(solution)/shard_map/ppermute | solution.py:111
  60.7 18.9 %collective-permute-start.14 = (bf16[384,1024]{1,0:T(8,128)(2,1)S(1)}, bf16[384,1024]{1,0:T(8,128)(2,1)S(1)}, u32[]{:S(2)}, u32[]{:S(2)}) collective-permute-start(bf16[384,1024]{1,0:T(8,128)(2,1)S(1)} %get-tuple-element.34), channel_id=1, source_target_pairs={{0,1},{1,0},{2,3},{3,2},{4,5},{5,4},{6,7},{7,6},{8,9},{9,8},{10,11... | collective-permute-start | bytes 2359304 | tf_op jit(solution)/shard_map/ppermute | solution.py:111
  61.2 24.7 %collective-permute-start.13 = (bf16[192,1024]{1,0:T(8,128)(2,1)S(1)}, bf16[192,1024]{1,0:T(8,128)(2,1)S(1)}, u32[]{:S(2)}, u32[]{:S(2)}) collective-permute-start(bf16[192,1024]{1,0:T(8,128)(2,1)S(1)} %collective-permute-done.11.rest_2_.refs_1_), channel_id=1, source_target_pairs={{4,0},{8,12},{5,1},{9,13},{6,2},{10,14},{7,3},{11,15},{20,16},{24,... | collective-permute-start | bytes 1179656 | tf_op jit(solution)/shard_map/ppermute | solution.py:115
  74.1 11.8 %collective-permute-start.12 = (bf16[192,1024]{1,0:T(8,128)(2,1)S(1)}, bf16[192,1024]{1,0:T(8,128)(2,1)S(1)}, u32[]{:S(2)}, u32[]{:S(2)}) collective-permute-start(bf16[192,1024]{1,0:T(8,128)(2,1)S(1)} %shard_map.97), channel_id=1, source_target_pairs={{0,2},{1,3},{2,0},{3,1},{4,6},{5,7},{6,4},{7,5},{8,10},{9,11},{10,... | collective-permute-start | bytes 1179656 | tf_op jit(solution)/shard_map/ppermute | solution.py:107
  74.7 15.4 %collective-permute-start.18 = (bf16[256,2048]{1,0:T(8,128)(2,1)S(1)}, bf16[256,2048]{1,0:T(8,128)(2,1)S(1)}, u32[]{:S(2)}, u32[]{:S(2)}) collective-permute-start(bf16[256,2048]{1,0:T(8,128)(2,1)S(1)} %copy-done.20), channel_id=1, source_target_pairs={{0,1},{1,0},{2,3},{3,2},{4,5},{5,4},{6,7},{7,6},{8,9},{9,8},{10,11... | collective-permute-start | bytes 3145736 | tf_op jit(solution)/shard_map/ppermute | solution.py:111
  92.8 13.8 %collective-permute-start.21 = (bf16[192,1024]{1,0:T(8,128)(2,1)S(1)}, bf16[192,1024]{1,0:T(8,128)(2,1)S(1)}, u32[]{:S(2)}, u32[]{:S(2)}) collective-permute-start(bf16[192,1024]{1,0:T(8,128)(2,1)S(1)} %get-tuple-element.49), channel_id=1, source_target_pairs={{0,2},{1,3},{2,0},{3,1},{12,14},{13,15},{14,12},{15,13},{16,18},{1... | collective-permute-start | bytes 1179656 | tf_op jit(solution)/shard_map/ppermute | solution.py:427
  97.8 17.3 %collective-permute-start.26 = (bf16[192,1024]{1,0:T(8,128)(2,1)S(1)}, bf16[192,1024]{1,0:T(8,128)(2,1)S(1)}, u32[]{:S(2)}, u32[]{:S(2)}) collective-permute-start(bf16[192,1024]{1,0:T(8,128)(2,1)S(1)} %get-tuple-element.54), channel_id=1, source_target_pairs={{0,2},{1,3},{2,0},{3,1},{4,6},{5,7},{6,4},{7,5},{8,10},{9,11},{10,... | collective-permute-start | bytes 1179656 | tf_op jit(solution)/shard_map/ppermute | solution.py:107
  98.4 27.3 %collective-permute-start.24 = (bf16[192,2048]{1,0:T(8,128)(2,1)S(1)}, bf16[192,2048]{1,0:T(8,128)(2,1)S(1)}, u32[]{:S(2)}, u32[]{:S(2)}) collective-permute-start(bf16[192,2048]{1,0:T(8,128)(2,1)S(1)} %get-tuple-element.51), channel_id=1, source_target_pairs={{4,8},{8,4},{5,9},{9,5},{6,10},{10,6},{7,11},{11,7},{20,24},{24,20... | collective-permute-start | bytes 2359304 | tf_op jit(solution)/shard_map/ppermute | solution.py:115
  99.1 23.7 %collective-permute-start.19 = (bf16[192,1024]{1,0:T(8,128)(2,1)S(1)}, bf16[192,1024]{1,0:T(8,128)(2,1)S(1)}, u32[]{:S(2)}, u32[]{:S(2)}) collective-permute-start(bf16[192,1024]{1,0:T(8,128)(2,1)S(1)} %get-tuple-element.47), channel_id=1, source_target_pairs={{0,2},{1,3},{2,0},{3,1},{4,6},{5,7},{6,4},{7,5},{8,10},{9,11},{10,... | collective-permute-start | bytes 1179656 | tf_op jit(solution)/shard_map/ppermute | solution.py:107
  106.8 17.5 %collective-permute-start.22 = (bf16[192,1024]{1,0:T(8,128)(2,1)S(1)}, bf16[192,1024]{1,0:T(8,128)(2,1)S(1)}, u32[]{:S(2)}, u32[]{:S(2)}) collective-permute-start(bf16[192,1024]{1,0:T(8,128)(2,1)S(1)} %add_convert_fusion.2), channel_id=1, source_target_pairs={{0,4},{12,8},{1,5},{13,9},{2,6},{14,10},{3,7},{15,11},{16,20},{28,... | collective-permute-start | bytes 1179656 | tf_op jit(solution)/shard_map/ppermute | solution.py:115
  115.2 29.1 %collective-permute-start.27 = (bf16[192,1024]{1,0:T(8,128)(2,1)S(1)}, bf16[192,1024]{1,0:T(8,128)(2,1)S(1)}, u32[]{:S(2)}, u32[]{:S(2)}) collective-permute-start(bf16[192,1024]{1,0:T(8,128)(2,1)S(1)} %add_convert_fusion), channel_id=1, source_target_pairs={{0,4},{4,0},{8,12},{12,8},{1,5},{5,1},{9,13},{13,9},{2,6},{6,2},{1... | collective-permute-start | bytes 1179656 | tf_op jit(solution)/shard_map/ppermute | solution.py:115
  124.4 19.7 %collective-permute-start.23 = (bf16[192,1024]{1,0:T(8,128)(2,1)S(1)}, bf16[192,1024]{1,0:T(8,128)(2,1)S(1)}, u32[]{:S(2)}, u32[]{:S(2)}) collective-permute-start(bf16[192,1024]{1,0:T(8,128)(2,1)S(1)} %add_convert_fusion.1), channel_id=1, source_target_pairs={{4,12},{8,0},{5,13},{9,1},{6,14},{10,2},{7,15},{11,3},{20,28},{24,... | collective-permute-start | bytes 1179656 | tf_op jit(solution)/shard_map/ppermute | solution.py:115
  126.0 18.3 %collective-permute-start.25 = (bf16[192,1024]{1,0:T(8,128)(2,1)S(1)}, bf16[192,1024]{1,0:T(8,128)(2,1)S(1)}, u32[]{:S(2)}, u32[]{:S(2)}) collective-permute-start(bf16[192,1024]{1,0:T(8,128)(2,1)S(1)} %fusion), channel_id=1, source_target_pairs={{0,2},{1,3},{2,0},{3,1},{4,6},{5,7},{6,4},{7,5},{8,10},{9,11},{10,... | collective-permute-start | bytes 1179656 | tf_op jit(solution)/shard_map/ppermute | solution.py:107
  (32 other events, 162.1 us)

commit v15 on v12

--- a/solution.py
+++ b/solution.py
@@ -363,25 +363,32 @@
     ]
 
     def first(plan_ref, sums_ref, got_ref, inner_ref, outer_ref, before_ref, *refs):
-        own_ref, lent_ref, sent_ref, kept_ref, held_ref, buffer, sem = refs
+        own_ref, lent_ref, sent_ref, kept_ref, again_ref, held_ref, buffer, sem = refs
         facts_here = facts_of(plan_ref, inner_ref, outer_ref, buffer, sem)
         rows = collected_rows(owned, slot, plan_ref, sums_ref, got_ref, facts_here, before_ref)
         down(rows[0].astype(jnp.bfloat16), own_ref, lent_ref, sent_ref, kept_ref)
+        again_ref[...] = kept_ref[...]
         for index in range(1, 4):
             held_ref[(index - 1) * owned : index * owned, :] = rows[index].astype(jnp.bfloat16)
 
-    def others(held_ref, own_ref, lent_ref, *refs):
-        for index in range(3):
-            held = held_ref[index * owned : (index + 1) * owned, :]
-            down(held, own_ref, lent_ref, refs[2 * index], refs[2 * index + 1])
+    def others(indices, *waits):
+        def body(held_ref, own_ref, lent_ref, *refs):
+            out_refs = refs[len(waits) :]
+            for place, index in enumerate(indices):
+                held = held_ref[(index - 1) * owned : index * owned, :]
+                down(held, own_ref, lent_ref, out_refs[2 * place], out_refs[2 * place + 1])
+
+        operands = [held, down_own, down_lent, *waits]
+        return on_core(body, pair * len(indices), [VMEM] * len(operands))(*operands)
 
     held_shape = jax.ShapeDtypeStruct((3 * owned, 2 * units), jnp.bfloat16)
     specs = [SMEM, VMEM, VMEM, ANYWHERE, ANYWHERE] + [VMEM] * 3
-    sent, kept, held = on_core(
-        first, pair + [held_shape], specs, fact_scratch(facts[0].shape[1])
+    sent, kept, again, held = on_core(
+        first, pair + [pair[1], held_shape], specs, fact_scratch(facts[0].shape[1])
     )(plan, sums, got, *facts, before, down_own, down_lent)
-    rest = on_core(others, pair * 3, [VMEM] * 3)(held, down_own, down_lent)
-    return [sent, *rest[0::2]], [kept, *rest[1::2]]
+    rest = others([1, 2])
+    chunks = [(sent, kept), (rest[0], rest[1]), (rest[2], rest[3])]
+    return chunks, again, lambda *waits: others([3], *waits)
 
 
 def rows_travel(
@@ -450,12 +457,13 @@
     )
     got_1 = across_cores(send_1)
 
+    total, collected_0 = collect(owned, 0, plan, sums_0, got_0, (own, own), None)
+
     last = (inner_last, outer_last)
     last_far_a = across_chips(
-        part_of(plan, *last, 0, half, *second_far, middle_far, ready_0, ready_1)
+        part_of(plan, *last, 0, half, *second_far, middle_far, collected_0, ready_1)
     )
     outward_far = along(middle_far, OUTWARD)
-    total, _ = collect(owned, 0, plan, sums_0, got_0, (own, own), None)
     total, collected_1 = collect(owned, 1, plan, sums_1, got_1, (beside, beside), total)
     sums_2, send_2, _ = partial_sums(plan, whole, [(second, second_far)], weights, (0, 1))
     got_2 = across_cores(send_2)
@@ -471,19 +479,27 @@
     )
     got_3 = across_cores(send_3)
     total, _ = collect(owned, 2, plan, sums_2, got_2, second, total)
-    sent, kept = finish(owned, 3, plan, sums_3, got_3, last, total, kept_down, lent_down)
-
-    joined = [k + across_chips(s).astype(jnp.float32) for s, k in zip(sent, kept)]
-    first, second, third = [block.astype(jnp.bfloat16) for block in joined[:3]]
-    second = lax.optimization_barrier(second)
-    inward = along(first, INWARD)
-    middle = along(first, MIDDLE)
+    chunks, again, last_chunk = finish(owned, 3, plan, sums_3, got_3, last, total, kept_down, lent_down)
+
+    def joined(sent, kept, exchange=across_chips):
+        return kept + exchange(sent).astype(jnp.float32)
+
+    def rounded(block):
+        return lax.optimization_barrier(block.astype(jnp.bfloat16))
+
+    sent, kept = chunks[0]
+    first_outer = rounded(joined(sent, kept, lambda block: at_kind(block, (0, 3))))
+    first_inner = rounded(joined(sent, again, lambda block: at_kind(block, (1, 2))))
+    second = rounded(joined(*chunks[1]))
+    third = rounded(joined(*chunks[2]))
+    inward = along(first_outer, INWARD)
+    middle = along(first_inner, MIDDLE)
     two_in = along(second, TWO_IN)
     passed = second.astype(jnp.float32) + inward.astype(jnp.float32)
     two_out = along(passed.astype(jnp.bfloat16), TWO_OUT)
     beside = along(third, BESIDE)
     arrived = [block.astype(jnp.float32) for block in (middle, two_in, two_out)]
-    total = lax.optimization_barrier(joined[3] + sum(arrived))
+    total = lax.optimization_barrier(joined(*last_chunk(second)) + sum(arrived))
     return (total + beside.astype(jnp.float32)).astype(jnp.bfloat16)
 
 

time: 144 us -> 151 us (1.049)
  waiting for transfers between devices: 45.2 us -> 49.8 us
  starting transfers between devices: 47 us -> 48.7 us
    ppermute x2 -> x4, waiting for transfers between devices: 1.9 us -> 9.21 us  [at_kind(): return lax.ppermute(block, ('blk', 'tp'), pairs)]
    ppermute x2 -> x4, starting transfers between devices: 4.11 us -> 8.38 us  [at_kind(): return lax.ppermute(block, ('blk', 'tp'), pairs)]
    ppermute x7 -> x6, waiting for transfers between devices: 13.4 us -> 10.6 us  [across_chips(): return lax.ppermute(block, 'tp', [(i, i ^ 2) for i in range(4)])]
    ppermute x13, starting transfers between devices: 33.8 us -> 31.8 us  [along(): return lax.ppermute(block, 'blk', route)]
    unnamed x56 -> x54, local copies, waits for them, and re-layouts: 8.75 us -> 9.67 us
    ppermute x7 -> x6, starting transfers between devices: 8 us -> 7.41 us  [across_chips(): return lax.ppermute(block, 'tp', [(i, i ^ 2) for i in range(4)])]
    pallas_call x2 -> x3, Pallas kernels: 3.95 us -> 4.11 us  [the longest x1 2.55 us: finish(): on_core(first, pair + [pair[1], held_shape], specs, fact_scratch(facts[0]...]
  transfers between devices with their start and end apart: 28 -> 29, of which waited for: 10 -> 11; matrix products, arithmetic and copies ran while one was open for 7% -> 7% of each run, Pallas kernels for 18% -> 17%
where the time goes in v15:
time: 151 us; the launch traced here: 150 us
  waiting for transfers between devices  49.8 us (33%)
  starting transfers between devices  48.7 us (32%)
  Pallas kernels  30.3 us (20%)
  local copies, waits for them, and re-layouts  16.4 us (11%)
  other arithmetic  4.65 us (3%)
    ppermute x13, starting transfers between devices, along(): return lax.ppermute(block, 'blk', route)  31.8 us
    ppermute x13, waiting for transfers between devices, along(): return lax.ppermute(block, 'blk', route)  29.7 us
    pallas_call x5, Pallas kernels, partial_sums(): return on_core(body, shapes + [TOKEN], specs)(*operands, *waits)  14.9 us
    ppermute x6, waiting for transfers between devices, across_chips(): return lax.ppermute(block, 'tp', [(i, i ^ 2) for i in range(4)])  10.6 us
    unnamed x54, local copies, waits for them, and re-layouts  9.67 us
    ppermute x4, waiting for transfers between devices, at_kind(): return lax.ppermute(block, ('blk', 'tp'), pairs)  9.21 us
    ppermute x4, starting transfers between devices, at_kind(): return lax.ppermute(block, ('blk', 'tp'), pairs)  8.38 us
    ppermute x6, starting transfers between devices, across_chips(): return lax.ppermute(block, 'tp', [(i, i ^ 2) for i in range(4)])  7.41 us
  transfers between devices with their start and end apart: 29, of which 11 were waited for; matrix products, arithmetic and copies ran while one was open for 7% of the time, Pallas kernels for 17%

profile of v15, /device:TPU:0, one launch (start us, length us, event | category | flops | bytes accessed | tf_op | source)
XLA Modules:
  0.0 150.3 jit_solution(7959609643272983751)
XLA Ops:
  4.5 3.1 %collective-permute-start = (bf16[400,1024]{1,0:T(8,128)(2,1)S(1)}, bf16[400,1024]{1,0:T(8,128)(2,1)}, u32[]{:S(2)}, u32[]{:S(2)}) collective-permute-start(bf16[400,1024]{1,0:T(8,128)(2,1)S(1)} %shard_map.91.refs_1_.inner_ref.outer_ref), channel_id=1, source_target_pairs={{0,4},{4,0},{8,12},{12,8},{1,5},{5,1},{9,13},{13,9},{2,6},{6,2},{1... | collective-permute-start | bytes 2457608 | tf_op jit(solution)/shard_map/ppermute | solution.py:115
  10.7 3.4 %dynamic-slice_bitcast_fusion.4 = (bf16[1024,256]{1,0:T(8,128)(2,1)S(1)}, bf16[1024,256]{1,0:T(8,128)(2,1)S(1)}, bf16[1024,256]{1,0:T(8,128)(2,1)}, bf16[1024,25...) fusion(bf16[4,1024,256]{2,1,0:T(8,128)(2,1)} %bitcast.32, ...), kind=kLoop, calls=%fused_computation.16 | loop fusion | bytes 8388624 | tf_op jit(solution)/shard_map/jit(dynamic_index_in_dim)/squeeze | solution.py:417
  16.3 2.7 %dynamic-slice_bitcast_fusion.1 = (bf16[256,1024]{1,0:T(8,128)(2,1)}, bf16[256,1024]{1,0:T(8,128)(2,1)S(1)}, bf16[256,1024]{1,0:T(8,128)(2,1)S(1)}, bf16[256,1024]{1,0:T(8,128)(2,1)}) fusion(bf16[1,256,4096]{2,1,0:T(8,128)(2,1)} %param.12, s32[]{:T(128)S(6)} %select_n.39, s32[]{:T(128)S(6)} %select_n.34, s32[]{:T(128)S(6)} %select_n.33, s32[]{:T(128)S(6)} %select_n.40), kind=kLoop, calls=%fused_computation.13 | loop fusion | bytes 4194320 | tf_op jit(solution)/shard_map/dynamic_slice | solution.py:423
  19.0 7.0 %collective-permute-done.refs_0_.inner_ref.outer_ref = bf16[400,1024]{1,0:T(8,128)(2,1)} collective-permute-done((bf16[400,1024]{1,0:T(8,128)(2,1)S(1)}, bf16[400,1024]{1,0:T(8,128)(2,1)}, u32[]{:S(2)}, u32[]{:S(2)}) %collective-permute-start) | collective-permute-done | bytes 819232 | tf_op jit(solution)/shard_map/ppermute | solution.py:115
  32.5 5.6 %collective-permute-start.8 = (bf16[192,1024]{1,0:T(8,128)(2,1)S(1)}, bf16[192,1024]{1,0:T(8,128)(2,1)S(1)}, u32[]{:S(2)}, u32[]{:S(2)}) collective-permute-start(bf16[192,1024]{1,0:T(8,128)(2,1)S(1)} %shard_map.92), channel_id=1, source_target_pairs={{0,4},{12,8},{1,5},{13,9},{2,6},{14,10},{3,7},{15,11},{16,20},{28,... | collective-permute-start | bytes 1179656 | tf_op jit(solution)/shard_map/ppermute | solution.py:115
  42.5 3.2 %shard_map.94 = (f32[384,1024]{1,0:T(8,128)S(1)}, bf16[384,1024]{1,0:T(8,128)(2,1)S(1)}, f32[8,128]{1,0:T(8,128)S(1)}) custom-call(s32[9]{0:T(128)S(1)} %fusion.plan_ref, bf16[384,1024]{1,0:T(8,128)(2,1)} %refs_0_.1, bf16[384,1024]{1,0:T(8,128)(2,1)} %collective-permute-done.7.inner_ref.outer_ref.refs_1_, ...), custom_call_target="tpu_custom_call" | custom-call | flops 1024 | bytes 1024 | tf_op jit(solution)/shard_map/pallas_call | solution.py:287
  48.5 2.5 %collective-permute-done.5.refs_0_ = bf16[400,1024]{1,0:T(8,128)(2,1)S(1)} collective-permute-done((bf16[400,1024]{1,0:T(8,128)(2,1)}, bf16[400,1024]{1,0:T(8,128)(2,1)S(1)}, u32[]{:S(2)}, u32[]{:S(2)}) %collective-permute-start.5) | collective-permute-done | bytes 819232 | tf_op jit(solution)/shard_map/ppermute | solution.py:115
  52.8 2.6 %collective-permute-start.10 = (bf16[400,1024]{1,0:T(8,128)(2,1)}, bf16[400,1024]{1,0:T(8,128)(2,1)S(1)}, u32[]{:S(2)}, u32[]{:S(2)}) collective-permute-start(bf16[400,1024]{1,0:T(8,128)(2,1)} %shard_map.95.refs_1_.outer_ref), channel_id=1, source_target_pairs={{0,2},{1,3},{2,0},{3,1},{12,14},{13,15},{14,12},{15,13},{16,18},{1... | collective-permute-start | bytes 2457608 | tf_op jit(solution)/shard_map/ppermute | solution.py:431
  58.5 3.1 %shard_map.97 = (f32[384,1024]{1,0:T(8,128)S(1)}, bf16[384,1024]{1,0:T(8,128)(2,1)S(1)}, f32[8,128]{1,0:T(8,128)S(1)}) custom-call(s32[9]{0:T(128)S(1)} %fusion.plan_ref, bf16[400,1024]{1,0:T(8,128)(2,1)} %collective-permute-done.refs_0_.inner_ref.outer_ref, bf16[400,1024]{1,0:T(8,128)(2,1)S(1)} %copy-done.10, bf16[1024,512]{1,0:T(8,128)(2,1)S(1)} %copy-done.3, ...), custom_call_target="tpu_custom_call" | custom-call | flops 1024 | bytes 1024 | tf_op jit(solution)/shard_map/pallas_call | solution.py:287
  65.0 5.2 %collective-permute-done.2.outer_ref.refs_1_ = bf16[400,1024]{1,0:T(8,128)(2,1)} collective-permute-done((bf16[400,1024]{1,0:T(8,128)(2,1)}, bf16[400,1024]{1,0:T(8,128)(2,1)}, u32[]{:S(2)}, u32[]{:S(2)}) %collective-permute-start.2) | collective-permute-done | bytes 819232 | tf_op jit(solution)/shard_map/ppermute | solution.py:115
  70.2 2.7 %collective-permute-done.10.rest_1_.refs_3_ = bf16[400,1024]{1,0:T(8,128)(2,1)S(1)} collective-permute-done((bf16[400,1024]{1,0:T(8,128)(2,1)}, bf16[400,1024]{1,0:T(8,128)(2,1)S(1)}, u32[]{:S(2)}, u32[]{:S(2)}) %collective-permute-start.10) | collective-permute-done | bytes 819232 | tf_op jit(solution)/shard_map/ppermute | solution.py:431
  75.5 2.9 %shard_map.99 = (f32[384,1024]{1,0:T(8,128)S(1)}, f32[8,128]{1,0:T(8,128)}) custom-call(s32[9]{0:T(128)S(1)} %fusion.plan_ref, bf16[400,1024]{1,0:T(8,128)(2,1)} %collective-permute-done.1.refs_2_.inner_ref.refs_0_, bf16[400,1024]{1,0:T(8,128)(2,1)} %collective-permute-done.2.outer_ref.refs_1_, bf16[1024,512]{1,0:T(8,128)(2,1)S(1)} %copy-done.4, ...), custom_call_target="tpu_custom_call" | custom-call | flops 1024 | bytes 1024 | tf_op jit(solution)/shard_map/pallas_call | solution.py:287
  78.4 2.1 %shard_map.100 = (f32[768,512]{1,0:T(8,128)S(1)}, f32[8,128]{1,0:T(8,128)S(1)}) custom-call(s32[9]{0:T(128)S(1)} %fusion.plan_ref, f32[384,1024]{1,0:T(8,128)S(1)} %get-tuple-element.37.sums_ref, bf16[384,1024]{1,0:T(8,128)(2,1)S(1)} %collective-permute-done.15.got_ref, bf16[400,1024]{1,0:T(8,128)(2,1)} %collective-permute-done.refs_0_.inner_ref.outer_ref, ...), custom_call_target="tpu_custom_call" | custom-call | flops 1024 | bytes 1024 | tf_op jit(solution)/shard_map/pallas_call | solution.py:346
  80.6 3.7 %shard_map.102 = (f32[384,1024]{1,0:T(8,128)S(1)}, bf16[384,1024]{1,0:T(8,128)(2,1)S(1)}, f32[8,128]{1,0:T(8,128)}) custom-call(s32[9]{0:T(128)S(1)} %fusion.plan_ref, bf16[400,1024]{1,0:T(8,128)(2,1)} %collective-permute-done.3.refs_0_.inner_ref, bf16[400,1024]{1,0:T(8,128)(2,1)S(1)} %copy-done.8, bf16[400,1024]{1,0:T(8,128)(2,1)} %collective-permute-done.4.rest_0_.refs_2_, ...), custom_call_target="tpu_custom_call" | custom-call | flops 1024 | bytes 1024 | tf_op jit(solution)/shard_map/pallas_call | solution.py:287
  84.8 3.4 %collective-permute-done.14.refs_2_ = bf16[192,1024]{1,0:T(8,128)(2,1)S(1)} collective-permute-done((bf16[192,1024]{1,0:T(8,128)(2,1)S(1)}, bf16[192,1024]{1,0:T(8,128)(2,1)S(1)}, u32[]{:S(2)}, u32[]{:S(2)}) %collective-permute-start.14) | collective-permute-done | bytes 393248 | tf_op jit(solution)/shard_map/ppermute | solution.py:115
  92.5 2.5 %shard_map.104 = (bf16[192,1024]{1,0:T(8,128)(2,1)S(1)}, f32[192,1024]{1,0:T(8,128)S(1)}, f32[192,1024]{1,0:T(8,128)S(1)}, bf16[576,512]{1,0:T(8,128)(2,1)S(1)}) custom-call(s32[9]{0:T(128)S(1)} %fusion.plan_ref, f32[384,1024]{1,0:T(8,128)S(1)} %get-tuple-element.41.sums_ref, bf16[384,1024]{1,0:T(8,128)(2,1)S(1)} %collective-permute-done.16.got_ref, ...), custom_call_target="tpu_custom_call" | custom-call | flops 1024 | bytes 1024 | tf_op jit(solution)/shard_map/pallas_call | solution.py:386
  95.1 3.4 %collective-permute-start.24 = (bf16[192,1024]{1,0:T(8,128)(2,1)S(1)}, bf16[192,1024]{1,0:T(8,128)(2,1)S(1)}, u32[]{:S(2)}, u32[]{:S(2)}) collective-permute-start(bf16[192,1024]{1,0:T(8,128)(2,1)S(1)} %get-tuple-element.53), channel_id=1, source_target_pairs={{0,2},{1,3},{2,0},{3,1},{12,14},{13,15},{14,12},{15,13},{16,18},{1... | collective-permute-start | bytes 1179656 | tf_op jit(solution)/shard_map/ppermute | solution.py:431
  102.5 6.5 %collective-permute-done.24 = bf16[192,1024]{1,0:T(8,128)(2,1)S(1)} collective-permute-done((bf16[192,1024]{1,0:T(8,128)(2,1)S(1)}, bf16[192,1024]{1,0:T(8,128)(2,1)S(1)}, u32[]{:S(2)}, u32[]{:S(2)}) %collective-permute-start.24) | collective-permute-done | bytes 393248 | tf_op jit(solution)/shard_map/ppermute | solution.py:431
  111.1 6.2 %collective-permute-done.19 = bf16[192,1024]{1,0:T(8,128)(2,1)S(1)} collective-permute-done((bf16[192,1024]{1,0:T(8,128)(2,1)S(1)}, bf16[192,1024]{1,0:T(8,128)(2,1)S(1)}, u32[]{:S(2)}, u32[]{:S(2)}) %collective-permute-start.19) | collective-permute-done | bytes 393248 | tf_op jit(solution)/shard_map/ppermute | solution.py:107
  117.4 9.5 %collective-permute-start.23 = (bf16[192,1024]{1,0:T(8,128)(2,1)S(1)}, bf16[192,1024]{1,0:T(8,128)(2,1)S(1)}, u32[]{:S(2)}, u32[]{:S(2)}) collective-permute-start(bf16[192,1024]{1,0:T(8,128)(2,1)S(1)} %add_convert_fusion.5.refs_0_), channel_id=1, source_target_pairs={{0,8},{12,4},{1,9},{13,5},{2,10},{14,6},{3,11},{15,7},{16,24},{28,... | collective-permute-start | bytes 1179656 | tf_op jit(solution)/shard_map/ppermute | solution.py:115
  130.6 2.6 %collective-permute-start.28 = (bf16[192,1024]{1,0:T(8,128)(2,1)S(1)}, bf16[192,1024]{1,0:T(8,128)(2,1)S(1)}, u32[]{:S(2)}, u32[]{:S(2)}) collective-permute-start(bf16[192,1024]{1,0:T(8,128)(2,1)S(1)} %add_convert_fusion.1), channel_id=1, source_target_pairs={{0,4},{4,0},{8,12},{12,8},{1,5},{5,1},{9,13},{13,9},{2,6},{6,2},{1... | collective-permute-start | bytes 1179656 | tf_op jit(solution)/shard_map/ppermute | solution.py:115
  133.2 4.4 %collective-permute-done.20 = bf16[192,1024]{1,0:T(8,128)(2,1)S(1)} collective-permute-done((bf16[192,1024]{1,0:T(8,128)(2,1)S(1)}, bf16[192,1024]{1,0:T(8,128)(2,1)S(1)}, u32[]{:S(2)}, u32[]{:S(2)}) %collective-permute-start.20) | collective-permute-done | bytes 393248 | tf_op jit(solution)/shard_map/ppermute | solution.py:107
  137.7 7.4 %collective-permute-done.26 = bf16[192,1024]{1,0:T(8,128)(2,1)S(1)} collective-permute-done((bf16[192,1024]{1,0:T(8,128)(2,1)S(1)}, bf16[192,1024]{1,0:T(8,128)(2,1)S(1)}, u32[]{:S(2)}, u32[]{:S(2)}) %collective-permute-start.26) | collective-permute-done | bytes 393248 | tf_op jit(solution)/shard_map/ppermute | solution.py:115
  145.4 4.1 %collective-permute-done.28 = bf16[192,1024]{1,0:T(8,128)(2,1)S(1)} collective-permute-done((bf16[192,1024]{1,0:T(8,128)(2,1)S(1)}, bf16[192,1024]{1,0:T(8,128)(2,1)S(1)}, u32[]{:S(2)}, u32[]{:S(2)}) %collective-permute-start.28) | collective-permute-done | bytes 393248 | tf_op jit(solution)/shard_map/ppermute | solution.py:115
  (119 shorter events, 50.0 us)
Async XLA Ops:
  4.5 21.4 %collective-permute-start = (bf16[400,1024]{1,0:T(8,128)(2,1)S(1)}, bf16[400,1024]{1,0:T(8,128)(2,1)}, u32[]{:S(2)}, u32[]{:S(2)}) collective-permute-start(bf16[400,1024]{1,0:T(8,128)(2,1)S(1)} %shard_map.91.refs_1_.inner_ref.outer_ref), channel_id=1, source_target_pairs={{0,4},{4,0},{8,12},{12,8},{1,5},{5,1},{9,13},{13,9},{2,6},{6,2},{1... | collective-permute-start | bytes 2457608 | tf_op jit(solution)/shard_map/ppermute | solution.py:115
  7.6 21.6 %collective-permute-start.3 = (bf16[400,1024]{1,0:T(8,128)(2,1)S(1)}, bf16[400,1024]{1,0:T(8,128)(2,1)}, u32[]{:S(2)}, u32[]{:S(2)}) collective-permute-start(bf16[400,1024]{1,0:T(8,128)(2,1)S(1)} %shard_map.91.refs_1_.inner_ref.outer_ref), channel_id=1, source_target_pairs={{4,8},{8,4},{5,9},{9,5},{6,10},{10,6},{7,11},{11,7},{20,24},{24,20... | collective-permute-start | bytes 2457608 | tf_op jit(solution)/shard_map/ppermute | solution.py:115
  9.2 21.3 %collective-permute-start.7 = (bf16[384,1024]{1,0:T(8,128)(2,1)}, bf16[384,1024]{1,0:T(8,128)(2,1)}, u32[]{:S(2)}, u32[]{:S(2)}) collective-permute-start(bf16[384,1024]{1,0:T(8,128)(2,1)} %refs_0_.1), channel_id=1, source_target_pairs={{0,2},{1,3},{2,0},{3,1},{4,6},{5,7},{6,4},{7,5},{8,10},{9,11},{10,... | collective-permute-start | bytes 2359304 | tf_op jit(solution)/shard_map/ppermute | solution.py:107
  15.6 25.6 %collective-permute-start.9 = (bf16[2048,512]{1,0:T(8,128)(2,1)}, bf16[2048,512]{1,0:T(8,128)(2,1)S(1)}, u32[]{:S(2)}, u32[]{:S(2)}) collective-permute-start(bf16[2048,512]{1,0:T(8,128)(2,1)} %shard_map.93), channel_id=1, source_target_pairs={{0,1},{1,0},{2,3},{3,2},{4,5},{5,4},{6,7},{7,6},{8,9},{9,8},{10,11... | collective-permute-start | bytes 6291464 | tf_op jit(solution)/shard_map/ppermute | solution.py:111
  26.0 25.0 %collective-permute-start.6 = (bf16[400,1024]{1,0:T(8,128)(2,1)}, bf16[400,1024]{1,0:T(8,128)(2,1)S(1)}, u32[]{:S(2)}, u32[]{:S(2)}) collective-permute-start(bf16[400,1024]{1,0:T(8,128)(2,1)} %collective-permute-done.refs_0_.inner_ref.outer_ref), channel_id=1, source_target_pairs={{0,2},{1,3},{2,0},{3,1},{4,6},{5,7},{6,4},{7,5},{8,10},{9,11},{10,... | collective-permute-start | bytes 2457608 | tf_op jit(solution)/shard_map/ppermute | solution.py:107
  27.6 12.0 %collective-permute-start.1 = (bf16[400,1024]{1,0:T(8,128)(2,1)}, bf16[400,1024]{1,0:T(8,128)(2,1)}, u32[]{:S(2)}, u32[]{:S(2)}) collective-permute-start(bf16[400,1024]{1,0:T(8,128)(2,1)} %collective-permute-done.refs_0_.inner_ref.outer_ref), channel_id=1, source_target_pairs={{4,8},{8,4},{5,9},{9,5},{6,10},{10,6},{7,11},{11,7},{20,24},{24,20... | collective-permute-start | bytes 2457608 | tf_op jit(solution)/shard_map/ppermute | solution.py:115
  29.2 21.8 %collective-permute-start.5 = (bf16[400,1024]{1,0:T(8,128)(2,1)}, bf16[400,1024]{1,0:T(8,128)(2,1)S(1)}, u32[]{:S(2)}, u32[]{:S(2)}) collective-permute-start(bf16[400,1024]{1,0:T(8,128)(2,1)} %collective-permute-done.3.refs_0_.inner_ref), channel_id=1, source_target_pairs={{4,0},{8,12},{5,1},{9,13},{6,2},{10,14},{7,3},{11,15},{20,16},{24,... | collective-permute-start | bytes 2457608 | tf_op jit(solution)/shard_map/ppermute | solution.py:115
  32.5 16.0 %collective-permute-start.8 = (bf16[192,1024]{1,0:T(8,128)(2,1)S(1)}, bf16[192,1024]{1,0:T(8,128)(2,1)S(1)}, u32[]{:S(2)}, u32[]{:S(2)}) collective-permute-start(bf16[192,1024]{1,0:T(8,128)(2,1)S(1)} %shard_map.92), channel_id=1, source_target_pairs={{0,4},{12,8},{1,5},{13,9},{2,6},{14,10},{3,7},{15,11},{16,20},{28,... | collective-permute-start | bytes 1179656 | tf_op jit(solution)/shard_map/ppermute | solution.py:115
  39.7 25.3 %collective-permute-start.4 = (bf16[400,1024]{1,0:T(8,128)(2,1)}, bf16[400,1024]{1,0:T(8,128)(2,1)}, u32[]{:S(2)}, u32[]{:S(2)}) collective-permute-start(bf16[400,1024]{1,0:T(8,128)(2,1)} %collective-permute-done.3.refs_0_.inner_ref), channel_id=1, source_target_pairs={{4,6},{5,7},{6,4},{7,5},{8,10},{9,11},{10,8},{11,9},{20,22},{21,23... | collective-permute-start | bytes 2457608 | tf_op jit(solution)/shard_map/ppermute | solution.py:431
  41.2 29.0 %collective-permute-start.2 = (bf16[400,1024]{1,0:T(8,128)(2,1)}, bf16[400,1024]{1,0:T(8,128)(2,1)}, u32[]{:S(2)}, u32[]{:S(2)}) collective-permute-start(bf16[400,1024]{1,0:T(8,128)(2,1)} %collective-permute-done.1.refs_2_.inner_ref.refs_0_), channel_id=1, source_target_pairs={{4,0},{8,12},{5,1},{9,13},{6,2},{10,14},{7,3},{11,15},{20,16},{24,... | collective-permute-start | bytes 2457608 | tf_op jit(solution)/shard_map/ppermute | solution.py:115
  52.8 20.1 %collective-permute-start.10 = (bf16[400,1024]{1,0:T(8,128)(2,1)}, bf16[400,1024]{1,0:T(8,128)(2,1)S(1)}, u32[]{:S(2)}, u32[]{:S(2)}) collective-permute-start(bf16[400,1024]{1,0:T(8,128)(2,1)} %shard_map.95.refs_1_.outer_ref), channel_id=1, source_target_pairs={{0,2},{1,3},{2,0},{3,1},{12,14},{13,15},{14,12},{15,13},{16,18},{1... | collective-permute-start | bytes 2457608 | tf_op jit(solution)/shard_map/ppermute | solution.py:431
  61.7 16.8 %collective-permute-start.15 = (bf16[384,1024]{1,0:T(8,128)(2,1)S(1)}, bf16[384,1024]{1,0:T(8,128)(2,1)S(1)}, u32[]{:S(2)}, u32[]{:S(2)}) collective-permute-start(bf16[384,1024]{1,0:T(8,128)(2,1)S(1)} %get-tuple-element.38), channel_id=1, source_target_pairs={{0,1},{1,0},{2,3},{3,2},{4,5},{5,4},{6,7},{7,6},{8,9},{9,8},{10,11... | collective-permute-start | bytes 2359304 | tf_op jit(solution)/shard_map/ppermute | solution.py:111
  62.2 26.0 %collective-permute-start.14 = (bf16[192,1024]{1,0:T(8,128)(2,1)S(1)}, bf16[192,1024]{1,0:T(8,128)(2,1)S(1)}, u32[]{:S(2)}, u32[]{:S(2)}) collective-permute-start(bf16[192,1024]{1,0:T(8,128)(2,1)S(1)} %collective-permute-done.11.rest_2_.refs_1_), channel_id=1, source_target_pairs={{4,0},{8,12},{5,1},{9,13},{6,2},{10,14},{7,3},{11,15},{20,16},{24,... | collective-permute-start | bytes 1179656 | tf_op jit(solution)/shard_map/ppermute | solution.py:115
  74.9 13.3 %collective-permute-start.13 = (bf16[192,1024]{1,0:T(8,128)(2,1)S(1)}, bf16[192,1024]{1,0:T(8,128)(2,1)S(1)}, u32[]{:S(2)}, u32[]{:S(2)}) collective-permute-start(bf16[192,1024]{1,0:T(8,128)(2,1)S(1)} %shard_map.98), channel_id=1, source_target_pairs={{0,2},{1,3},{2,0},{3,1},{4,6},{5,7},{6,4},{7,5},{8,10},{9,11},{10,... | collective-permute-start | bytes 1179656 | tf_op jit(solution)/shard_map/ppermute | solution.py:107
  75.5 16.7 %collective-permute-start.18 = (bf16[256,2048]{1,0:T(8,128)(2,1)S(1)}, bf16[256,2048]{1,0:T(8,128)(2,1)S(1)}, u32[]{:S(2)}, u32[]{:S(2)}) collective-permute-start(bf16[256,2048]{1,0:T(8,128)(2,1)S(1)} %copy-done.19), channel_id=1, source_target_pairs={{0,1},{1,0},{2,3},{3,2},{4,5},{5,4},{6,7},{7,6},{8,9},{9,8},{10,11... | collective-permute-start | bytes 3145736 | tf_op jit(solution)/shard_map/ppermute | solution.py:111
  95.1 13.8 %collective-permute-start.24 = (bf16[192,1024]{1,0:T(8,128)(2,1)S(1)}, bf16[192,1024]{1,0:T(8,128)(2,1)S(1)}, u32[]{:S(2)}, u32[]{:S(2)}) collective-permute-start(bf16[192,1024]{1,0:T(8,128)(2,1)S(1)} %get-tuple-element.53), channel_id=1, source_target_pairs={{0,2},{1,3},{2,0},{3,1},{12,14},{13,15},{14,12},{15,13},{16,18},{1... | collective-permute-start | bytes 1179656 | tf_op jit(solution)/shard_map/ppermute | solution.py:431
  98.5 11.9 %collective-permute-start.21 = (bf16[192,1024]{1,0:T(8,128)(2,1)S(1)}, bf16[192,1024]{1,0:T(8,128)(2,1)S(1)}, u32[]{:S(2)}, u32[]{:S(2)}) collective-permute-start(bf16[192,1024]{1,0:T(8,128)(2,1)S(1)} %get-tuple-element.53), channel_id=1, source_target_pairs={{4,6},{5,7},{6,4},{7,5},{8,10},{9,11},{10,8},{11,9},{20,22},{21,23... | collective-permute-start | bytes 1179656 | tf_op jit(solution)/shard_map/ppermute | solution.py:431
  100.4 17.0 %collective-permute-start.19 = (bf16[192,1024]{1,0:T(8,128)(2,1)S(1)}, bf16[192,1024]{1,0:T(8,128)(2,1)S(1)}, u32[]{:S(2)}, u32[]{:S(2)}) collective-permute-start(bf16[192,1024]{1,0:T(8,128)(2,1)S(1)} %get-tuple-element.49), channel_id=1, source_target_pairs={{0,2},{1,3},{2,0},{3,1},{4,6},{5,7},{6,4},{7,5},{8,10},{9,11},{10,... | collective-permute-start | bytes 1179656 | tf_op jit(solution)/shard_map/ppermute | solution.py:107
  101.0 29.5 %collective-permute-start.27 = (bf16[192,1024]{1,0:T(8,128)(2,1)S(1)}, bf16[192,1024]{1,0:T(8,128)(2,1)S(1)}, u32[]{:S(2)}, u32[]{:S(2)}) collective-permute-start(bf16[192,1024]{1,0:T(8,128)(2,1)S(1)} %get-tuple-element.56), channel_id=1, source_target_pairs={{0,2},{1,3},{2,0},{3,1},{4,6},{5,7},{6,4},{7,5},{8,10},{9,11},{10,... | collective-permute-start | bytes 1179656 | tf_op jit(solution)/shard_map/ppermute | solution.py:107
  109.0 20.1 %collective-permute-start.25 = (bf16[192,1024]{1,0:T(8,128)(2,1)S(1)}, bf16[192,1024]{1,0:T(8,128)(2,1)S(1)}, u32[]{:S(2)}, u32[]{:S(2)}) collective-permute-start(bf16[192,1024]{1,0:T(8,128)(2,1)S(1)} %add_convert_fusion.3), channel_id=1, source_target_pairs={{0,4},{12,8},{1,5},{13,9},{2,6},{14,10},{3,7},{15,11},{16,20},{28,... | collective-permute-start | bytes 1179656 | tf_op jit(solution)/shard_map/ppermute | solution.py:115
  110.5 22.8 %collective-permute-start.22 = (bf16[192,1024]{1,0:T(8,128)(2,1)S(1)}, bf16[192,1024]{1,0:T(8,128)(2,1)S(1)}, u32[]{:S(2)}, u32[]{:S(2)}) collective-permute-start(bf16[192,1024]{1,0:T(8,128)(2,1)S(1)} %add_convert_fusion.4), channel_id=1, source_target_pairs={{4,8},{8,4},{5,9},{9,5},{6,10},{10,6},{7,11},{11,7},{20,24},{24,20... | collective-permute-start | bytes 1179656 | tf_op jit(solution)/shard_map/ppermute | solution.py:115
  117.4 20.2 %collective-permute-start.23 = (bf16[192,1024]{1,0:T(8,128)(2,1)S(1)}, bf16[192,1024]{1,0:T(8,128)(2,1)S(1)}, u32[]{:S(2)}, u32[]{:S(2)}) collective-permute-start(bf16[192,1024]{1,0:T(8,128)(2,1)S(1)} %add_convert_fusion.5.refs_0_), channel_id=1, source_target_pairs={{0,8},{12,4},{1,9},{13,5},{2,10},{14,6},{3,11},{15,7},{16,24},{28,... | collective-permute-start | bytes 1179656 | tf_op jit(solution)/shard_map/ppermute | solution.py:115
  129.2 15.9 %collective-permute-start.26 = (bf16[192,1024]{1,0:T(8,128)(2,1)S(1)}, bf16[192,1024]{1,0:T(8,128)(2,1)S(1)}, u32[]{:S(2)}, u32[]{:S(2)}) collective-permute-start(bf16[192,1024]{1,0:T(8,128)(2,1)S(1)} %add_convert_fusion.2), channel_id=1, source_target_pairs={{4,12},{8,0},{5,13},{9,1},{6,14},{10,2},{7,15},{11,3},{20,28},{24,... | collective-permute-start | bytes 1179656 | tf_op jit(solution)/shard_map/ppermute | solution.py:115
  130.6 18.9 %collective-permute-start.28 = (bf16[192,1024]{1,0:T(8,128)(2,1)S(1)}, bf16[192,1024]{1,0:T(8,128)(2,1)S(1)}, u32[]{:S(2)}, u32[]{:S(2)}) collective-permute-start(bf16[192,1024]{1,0:T(8,128)(2,1)S(1)} %add_convert_fusion.1), channel_id=1, source_target_pairs={{0,4},{4,0},{8,12},{12,8},{1,5},{5,1},{9,13},{13,9},{2,6},{6,2},{1... | collective-permute-start | bytes 1179656 | tf_op jit(solution)/shard_map/ppermute | solution.py:115
  (32 other events, 152.3 us)

commit v16 on v12

--- a/solution.py
+++ b/solution.py
@@ -423,7 +423,6 @@
         pairs = [(4 * p + i, 4 * p + (i ^ 2)) for p in positions for i in range(4)]
         return lax.ppermute(block, ("blk", "tp"), pairs)
 
-    inner_last = along(beside, MIDDLE)
     outer_next = along(middle, OUTWARD)
     beside_far = across_chips(beside)
     own_far_half = part_of(plan, own_far, own_far, half, half, flops=16 * 2**30)
@@ -436,11 +435,12 @@
         plan, whole, [(tokens, own_far)], weights, (0, 1)
     )
     got_0 = across_cores(send_0)
+    inner_last = after(along(beside, MIDDLE), ready_0)
     lent_down = across_cores(lend_down)
 
-    outer_last = along(inner_last, OUTWARD)
+    outer_last = after(along(inner_last, OUTWARD), flops=5 * 2**30)
     outer_next = after(
-        outer_next, beside_far, inner_last, inward_far, lend_down, weights[0], weights[1], ready_0
+        outer_next, beside_far, inner_last, inward_far, lend_down, weights[0], weights[1]
     )
     second = (middle, outer_next)
     second_far = (at_kind(middle, (1, 2)), at_kind(outer_next, (0, 3)))
@@ -450,12 +450,13 @@
     )
     got_1 = across_cores(send_1)
 
+    total, collected_0 = collect(owned, 0, plan, sums_0, got_0, (own, own), None)
+
     last = (inner_last, outer_last)
     last_far_a = across_chips(
-        part_of(plan, *last, 0, half, *second_far, middle_far, ready_0, ready_1)
+        part_of(plan, *last, 0, half, *second_far, collected_0, ready_1)
     )
     outward_far = along(middle_far, OUTWARD)
-    total, _ = collect(owned, 0, plan, sums_0, got_0, (own, own), None)
     total, collected_1 = collect(owned, 1, plan, sums_1, got_1, (beside, beside), total)
     sums_2, send_2, _ = partial_sums(plan, whole, [(second, second_far)], weights, (0, 1))
     got_2 = across_cores(send_2)

time: 144 us -> 159 us (1.10)
  Pallas kernels: 30.7 us -> 37.5 us
  waiting for transfers between devices: 45.2 us -> 50.7 us
    ppermute x2, waiting for transfers between devices: 1.9 us -> 8.9 us  [at_kind(): return lax.ppermute(block, ('blk', 'tp'), pairs)]
    ppermute x13, waiting for transfers between devices: 29.9 us -> 24.4 us  [along(): return lax.ppermute(block, 'blk', route)]
    ppermute x7, waiting for transfers between devices: 13.4 us -> 17.4 us  [across_chips(): return lax.ppermute(block, 'tp', [(i, i ^ 2) for i in range(4)])]
    pallas_call x5, Pallas kernels: 14.8 us -> 17.7 us  [partial_sums(): return on_core(body, shapes + [TOKEN], specs)(*operands, *waits)]
    pallas_call x3, Pallas kernels: 6.13 us -> 8.61 us  [collect(): on_core(body, [shape, TOKEN], specs, fact_scratch(facts[0].shape[1]))]
    ppermute x13, starting transfers between devices: 33.8 us -> 35.5 us  [along(): return lax.ppermute(block, 'blk', route)]
    unnamed x56 -> x52, local copies, waits for them, and re-layouts: 8.75 us -> 9.95 us
  transfers between devices with their start and end apart: 28 -> 28, of which waited for: 10 -> 7; matrix products, arithmetic and copies ran while one was open for 7% -> 7% of each run, Pallas kernels for 18% -> 20%
where the time goes in v16:
time: 159 us; the launch traced here: 158 us
  waiting for transfers between devices  50.7 us (32%)
  starting transfers between devices  48.4 us (30%)
  Pallas kernels  37.5 us (24%)
  local copies, waits for them, and re-layouts  17 us (11%)
  other arithmetic  4.34 us (3%)
    ppermute x13, starting transfers between devices, along(): return lax.ppermute(block, 'blk', route)  35.5 us
    ppermute x13, waiting for transfers between devices, along(): return lax.ppermute(block, 'blk', route)  24.4 us
    pallas_call x5, Pallas kernels, partial_sums(): return on_core(body, shapes + [TOKEN], specs)(*operands, *waits)  17.7 us
    ppermute x7, waiting for transfers between devices, across_chips(): return lax.ppermute(block, 'tp', [(i, i ^ 2) for i in range(4)])  17.4 us
    unnamed x52, local copies, waits for them, and re-layouts  9.95 us
    ppermute x2, waiting for transfers between devices, at_kind(): return lax.ppermute(block, ('blk', 'tp'), pairs)  8.9 us
    pallas_call x3, Pallas kernels, collect(): on_core(body, [shape, TOKEN], specs, fact_scratch(facts[0].shape[1]))  8.61 us
    ppermute x7, starting transfers between devices, across_chips(): return lax.ppermute(block, 'tp', [(i, i ^ 2) for i in range(4)])  7.99 us
  transfers between devices with their start and end apart: 28, of which 7 were waited for; matrix products, arithmetic and copies ran while one was open for 7% of the time, Pallas kernels for 20%

profile of v16, /device:TPU:0, one launch (start us, length us, event | category | flops | bytes accessed | tf_op | source)
XLA Modules:
  0.0 158.4 jit_solution(9044479484990180478)
XLA Ops:
  2.7 2.8 %shard_map.91.refs_1_.inner_ref.outer_ref = bf16[400,1024]{1,0:T(8,128)(2,1)} custom-call(bf16[384,1024]{1,0:T(8,128)(2,1)} %refs_0_.1, f32[4,384]{1,0:T(4,128)S(1)} %bitcast.30, s32[3,1,4]{2,1,0:T(1,128)S(1)} %bitcast.31, s32[1,4]{1,0:T(1,128)S(1)} %copy-done.18, s32[384]{0:T(512)S(1)} %copy-done.16), custom_call_target="tpu_custom_call" | custom-call | flops 1024 | bytes 1024 | tf_op jit(solution)/shard_map/pallas_call | solution.py:234
  5.5 3.1 %collective-permute-start = (bf16[400,1024]{1,0:T(8,128)(2,1)}, bf16[400,1024]{1,0:T(8,128)(2,1)}, u32[]{:S(2)}, u32[]{:S(2)}) collective-permute-start(bf16[400,1024]{1,0:T(8,128)(2,1)} %shard_map.91.refs_1_.inner_ref.outer_ref), channel_id=1, source_target_pairs={{0,4},{4,0},{8,12},{12,8},{1,5},{5,1},{9,13},{13,9},{2,6},{6,2},{1... | collective-permute-start | bytes 2457608 | tf_op jit(solution)/shard_map/ppermute | solution.py:115
  11.6 3.6 %dynamic-slice_bitcast_fusion.6 = (bf16[1024,256]{1,0:T(8,128)(2,1)S(1)}, bf16[1024,256]{1,0:T(8,128)(2,1)S(1)}, bf16[1024,256]{1,0:T(8,128)(2,1)}, bf16[1024,25...) fusion(bf16[4,1024,256]{2,1,0:T(8,128)(2,1)} %bitcast.32, ...), kind=kLoop, calls=%fused_computation.17 | loop fusion | bytes 8388624 | tf_op jit(solution)/shard_map/jit(dynamic_index_in_dim)/squeeze | solution.py:410
  17.5 9.7 %collective-permute-done.refs_0_.inner_ref.outer_ref = bf16[400,1024]{1,0:T(8,128)(2,1)} collective-permute-done((bf16[400,1024]{1,0:T(8,128)(2,1)}, bf16[400,1024]{1,0:T(8,128)(2,1)}, u32[]{:S(2)}, u32[]{:S(2)}) %collective-permute-start) | collective-permute-done | bytes 819232 | tf_op jit(solution)/shard_map/ppermute | solution.py:115
  32.9 8.0 %collective-permute-start.9 = (bf16[192,1024]{1,0:T(8,128)(2,1)S(1)}, bf16[192,1024]{1,0:T(8,128)(2,1)}, u32[]{:S(2)}, u32[]{:S(2)}) collective-permute-start(bf16[192,1024]{1,0:T(8,128)(2,1)S(1)} %shard_map.96), channel_id=1, source_target_pairs={{0,4},{12,8},{1,5},{13,9},{2,6},{14,10},{3,7},{15,11},{16,20},{28,... | collective-permute-start | bytes 1179656 | tf_op jit(solution)/shard_map/ppermute | solution.py:115
  41.1 3.8 %shard_map.93 = (f32[384,1024]{1,0:T(8,128)S(1)}, bf16[384,1024]{1,0:T(8,128)(2,1)S(1)}, f32[8,128]{1,0:T(8,128)S(1)}) custom-call(s32[9]{0:T(128)S(1)} %fusion.plan_ref, bf16[384,1024]{1,0:T(8,128)(2,1)} %refs_0_.1, bf16[384,1024]{1,0:T(8,128)(2,1)} %collective-permute-done.2.refs_1_.inner_ref.outer_ref, ...), custom_call_target="tpu_custom_call" | custom-call | flops 1024 | bytes 1024 | tf_op jit(solution)/shard_map/pallas_call | solution.py:287
  50.0 2.7 %dynamic-slice_bitcast_fusion.1 = (bf16[256,1024]{1,0:T(8,128)(2,1)}, bf16[256,1024]{1,0:T(8,128)(2,1)S(1)}, bf16[256,1024]{1,0:T(8,128)(2,1)S(1)}, bf16[256,1024]{1,0:T(8,128)(2,1)}) fusion(bf16[1,256,4096]{2,1,0:T(8,128)(2,1)} %param.12, s32[]{:T(128)S(6)} %select_n.39, s32[]{:T(128)S(6)} %select_n.38, s32[]{:T(128)S(6)} %select_n.37, s32[]{:T(128)S(6)} %select_n.40), kind=kLoop, calls=%fused_computation.12 | loop fusion | bytes 4194320 | tf_op jit(solution)/shard_map/dynamic_slice | solution.py:416
  56.2 2.4 %collective-permute-start.10 = (bf16[400,1024]{1,0:T(8,128)(2,1)}, bf16[400,1024]{1,0:T(8,128)(2,1)}, u32[]{:S(2)}, u32[]{:S(2)}) collective-permute-start(bf16[400,1024]{1,0:T(8,128)(2,1)} %shard_map.97.refs_1_.outer_ref), channel_id=1, source_target_pairs={{0,2},{1,3},{2,0},{3,1},{12,14},{13,15},{14,12},{15,13},{16,18},{1... | collective-permute-start | bytes 2457608 | tf_op jit(solution)/shard_map/ppermute | solution.py:424
  61.2 4.3 %shard_map.99 = (f32[384,1024]{1,0:T(8,128)S(1)}, bf16[384,1024]{1,0:T(8,128)(2,1)}, f32[8,128]{1,0:T(8,128)S(1)}) custom-call(s32[9]{0:T(128)S(1)} %fusion.plan_ref, bf16[400,1024]{1,0:T(8,128)(2,1)} %collective-permute-done.refs_0_.inner_ref.outer_ref, bf16[400,1024]{1,0:T(8,128)(2,1)} %collective-permute-done.8.refs_1_, bf16[1024,512]{1,0:T(8,128)(2,1)S(1)} %copy-done.3, ...), custom_call_target="tpu_custom_call" | custom-call | flops 1024 | bytes 1024 | tf_op jit(solution)/shard_map/pallas_call | solution.py:287
  65.7 3.1 %shard_map.98 = (f32[768,512]{1,0:T(8,128)S(1)}, f32[8,128]{1,0:T(8,128)S(1)}) custom-call(s32[9]{0:T(128)S(1)} %fusion.plan_ref, f32[384,1024]{1,0:T(8,128)S(1)} %copy-done.9, bf16[384,1024]{1,0:T(8,128)(2,1)} %collective-permute-done.11.got_ref, bf16[400,1024]{1,0:T(8,128)(2,1)} %shard_map.91.refs_1_.inner_ref.outer_ref, ...), custom_call_target="tpu_custom_call" | custom-call | flops 1024 | bytes 1024 | tf_op jit(solution)/shard_map/pallas_call | solution.py:346
  70.1 8.9 %collective-permute-done.10.rest_1_.refs_3_ = bf16[400,1024]{1,0:T(8,128)(2,1)} collective-permute-done((bf16[400,1024]{1,0:T(8,128)(2,1)}, bf16[400,1024]{1,0:T(8,128)(2,1)}, u32[]{:S(2)}, u32[]{:S(2)}) %collective-permute-start.10) | collective-permute-done | bytes 819232 | tf_op jit(solution)/shard_map/ppermute | solution.py:424
  83.1 2.8 %shard_map.102 = (f32[768,512]{1,0:T(8,128)S(1)}, f32[8,128]{1,0:T(8,128)S(1)}) custom-call(s32[9]{0:T(128)S(1)} %fusion.plan_ref, f32[384,1024]{1,0:T(8,128)S(1)} %copy-done.11, bf16[384,1024]{1,0:T(8,128)(2,1)} %collective-permute-done.15.got_ref, bf16[400,1024]{1,0:T(8,128)(2,1)} %collective-permute-done.refs_0_.inner_ref.outer_ref, ...), custom_call_target="tpu_custom_call" | custom-call | flops 1024 | bytes 1024 | tf_op jit(solution)/shard_map/pallas_call | solution.py:346
  86.0 4.3 %shard_map.104 = (f32[384,1024]{1,0:T(8,128)S(1)}, bf16[384,1024]{1,0:T(8,128)(2,1)S(1)}, f32[8,128]{1,0:T(8,128)}) custom-call(s32[9]{0:T(128)S(1)} %fusion.plan_ref, bf16[400,1024]{1,0:T(8,128)(2,1)} %collective-permute-done.5.refs_0_.inner_ref, bf16[400,1024]{1,0:T(8,128)(2,1)} %shard_map.97.refs_1_.outer_ref, ...), custom_call_target="tpu_custom_call" | custom-call | flops 1024 | bytes 1024 | tf_op jit(solution)/shard_map/pallas_call | solution.py:287
  90.8 2.7 %shard_map.101 = (f32[384,1024]{1,0:T(8,128)S(1)}, f32[8,128]{1,0:T(8,128)}) custom-call(s32[9]{0:T(128)S(1)} %fusion.plan_ref, bf16[400,1024]{1,0:T(8,128)(2,1)S(1)} %copy-done.7, bf16[400,1024]{1,0:T(8,128)(2,1)} %shard_map.95.outer_ref.refs_1_, bf16[1024,512]{1,0:T(8,128)(2,1)S(1)} %copy-done.4, ...), custom_call_target="tpu_custom_call" | custom-call | flops 1024 | bytes 1024 | tf_op jit(solution)/shard_map/pallas_call | solution.py:287
  93.5 2.6 %shard_map.103 = (f32[384,1024]{1,0:T(8,128)S(1)}, bf16[384,1024]{1,0:T(8,128)(2,1)S(1)}, f32[8,128]{1,0:T(8,128)}) custom-call(s32[9]{0:T(128)S(1)} %fusion.plan_ref, bf16[192,1024]{1,0:T(8,128)(2,1)S(1)} %collective-permute-done.12.refs_0_, bf16[192,1024]{1,0:T(8,128)(2,1)S(1)} %collective-permute-done.13.refs_1_, ...), custom_call_target="tpu_custom_call" | custom-call | flops 1024 | bytes 1024 | tf_op jit(solution)/shard_map/pallas_call | solution.py:287
  96.2 2.6 %shard_map.105 = (f32[768,512]{1,0:T(8,128)S(1)}, f32[8,128]{1,0:T(8,128)}) custom-call(s32[9]{0:T(128)S(1)} %fusion.plan_ref, f32[384,1024]{1,0:T(8,128)S(1)} %get-tuple-element.42.sums_ref, bf16[384,1024]{1,0:T(8,128)(2,1)S(1)} %collective-permute-done.17.got_ref, bf16[400,1024]{1,0:T(8,128)(2,1)} %collective-permute-done.5.refs_0_.inner_ref, ...), custom_call_target="tpu_custom_call" | custom-call | flops 1024 | bytes 1024 | tf_op jit(solution)/shard_map/pallas_call | solution.py:346
  98.8 2.7 %shard_map.106 = (bf16[192,1024]{1,0:T(8,128)(2,1)S(1)}, f32[192,1024]{1,0:T(8,128)S(1)}, bf16[576,512]{1,0:T(8,128)(2,1)S(1)}) custom-call(s32[9]{0:T(128)S(1)} %fusion.plan_ref, f32[384,1024]{1,0:T(8,128)S(1)} %get-tuple-element.40.sums_ref, bf16[384,1024]{1,0:T(8,128)(2,1)S(1)} %collective-permute-done.16.got_ref, bf16[400,1024]{1,0:T(8,128)(2,1)S(1)} %copy-done.7, ...), custom_call_target="tpu_custom_call" | custom-call | flops 1024 | bytes 1024 | tf_op jit(solution)/shard_map/pallas_call | solution.py:380
  105.2 8.4 %collective-permute-done.20 = bf16[192,1024]{1,0:T(8,128)(2,1)S(1)} collective-permute-done((bf16[192,1024]{1,0:T(8,128)(2,1)S(1)}, bf16[192,1024]{1,0:T(8,128)(2,1)S(1)}, u32[]{:S(2)}, u32[]{:S(2)}) %collective-permute-start.20) | collective-permute-done | bytes 393248 | tf_op jit(solution)/shard_map/ppermute | solution.py:107
  113.7 6.0 %collective-permute-start.24 = (bf16[192,1024]{1,0:T(8,128)(2,1)S(1)}, bf16[192,1024]{1,0:T(8,128)(2,1)S(1)}, u32[]{:S(2)}, u32[]{:S(2)}) collective-permute-start(bf16[192,1024]{1,0:T(8,128)(2,1)S(1)} %add_convert_fusion.4), channel_id=1, source_target_pairs={{0,4},{12,8},{1,5},{13,9},{2,6},{14,10},{3,7},{15,11},{16,20},{28,... | collective-permute-start | bytes 1179656 | tf_op jit(solution)/shard_map/ppermute | solution.py:115
  122.6 5.4 %collective-permute-start.23 = (bf16[192,1024]{1,0:T(8,128)(2,1)S(1)}, bf16[192,1024]{1,0:T(8,128)(2,1)S(1)}, u32[]{:S(2)}, u32[]{:S(2)}) collective-permute-start(bf16[192,1024]{1,0:T(8,128)(2,1)S(1)} %add_convert_fusion.3), channel_id=1, source_target_pairs={{0,8},{12,4},{1,9},{13,5},{2,10},{14,6},{3,11},{15,7},{16,24},{28,... | collective-permute-start | bytes 1179656 | tf_op jit(solution)/shard_map/ppermute | solution.py:115
  129.5 9.0 %collective-permute-done.26 = bf16[192,1024]{1,0:T(8,128)(2,1)S(1)} collective-permute-done((bf16[192,1024]{1,0:T(8,128)(2,1)S(1)}, bf16[192,1024]{1,0:T(8,128)(2,1)S(1)}, u32[]{:S(2)}, u32[]{:S(2)}) %collective-permute-start.26) | collective-permute-done | bytes 393248 | tf_op jit(solution)/shard_map/ppermute | solution.py:107
  138.6 4.2 %collective-permute-start.27 = (bf16[192,1024]{1,0:T(8,128)(2,1)S(1)}, bf16[192,1024]{1,0:T(8,128)(2,1)S(1)}, u32[]{:S(2)}, u32[]{:S(2)}) collective-permute-start(bf16[192,1024]{1,0:T(8,128)(2,1)S(1)} %add_convert_fusion.1), channel_id=1, source_target_pairs={{0,4},{4,0},{8,12},{12,8},{1,5},{5,1},{9,13},{13,9},{2,6},{6,2},{1... | collective-permute-start | bytes 1179656 | tf_op jit(solution)/shard_map/ppermute | solution.py:115
  142.7 6.5 %collective-permute-done.25 = bf16[192,1024]{1,0:T(8,128)(2,1)S(1)} collective-permute-done((bf16[192,1024]{1,0:T(8,128)(2,1)S(1)}, bf16[192,1024]{1,0:T(8,128)(2,1)S(1)}, u32[]{:S(2)}, u32[]{:S(2)}) %collective-permute-start.25) | collective-permute-done | bytes 393248 | tf_op jit(solution)/shard_map/ppermute | solution.py:115
  149.5 8.0 %collective-permute-done.27 = bf16[192,1024]{1,0:T(8,128)(2,1)S(1)} collective-permute-done((bf16[192,1024]{1,0:T(8,128)(2,1)S(1)}, bf16[192,1024]{1,0:T(8,128)(2,1)S(1)}, u32[]{:S(2)}, u32[]{:S(2)}) %collective-permute-start.27) | collective-permute-done | bytes 393248 | tf_op jit(solution)/shard_map/ppermute | solution.py:115
  (115 shorter events, 40.0 us)
Async XLA Ops:
  5.5 21.6 %collective-permute-start = (bf16[400,1024]{1,0:T(8,128)(2,1)}, bf16[400,1024]{1,0:T(8,128)(2,1)}, u32[]{:S(2)}, u32[]{:S(2)}) collective-permute-start(bf16[400,1024]{1,0:T(8,128)(2,1)} %shard_map.91.refs_1_.inner_ref.outer_ref), channel_id=1, source_target_pairs={{0,4},{4,0},{8,12},{12,8},{1,5},{5,1},{9,13},{13,9},{2,6},{6,2},{1... | collective-permute-start | bytes 2457608 | tf_op jit(solution)/shard_map/ppermute | solution.py:115
  8.6 20.9 %collective-permute-start.5 = (bf16[400,1024]{1,0:T(8,128)(2,1)}, bf16[400,1024]{1,0:T(8,128)(2,1)}, u32[]{:S(2)}, u32[]{:S(2)}) collective-permute-start(bf16[400,1024]{1,0:T(8,128)(2,1)} %shard_map.91.refs_1_.inner_ref.outer_ref), channel_id=1, source_target_pairs={{4,8},{8,4},{5,9},{9,5},{6,10},{10,6},{7,11},{11,7},{20,24},{24,20... | collective-permute-start | bytes 2457608 | tf_op jit(solution)/shard_map/ppermute | solution.py:115
  10.2 20.7 %collective-permute-start.2 = (bf16[384,1024]{1,0:T(8,128)(2,1)}, bf16[384,1024]{1,0:T(8,128)(2,1)}, u32[]{:S(2)}, u32[]{:S(2)}) collective-permute-start(bf16[384,1024]{1,0:T(8,128)(2,1)} %refs_0_.1), channel_id=1, source_target_pairs={{0,2},{1,3},{2,0},{3,1},{4,6},{5,7},{6,4},{7,5},{8,10},{9,11},{10,... | collective-permute-start | bytes 2359304 | tf_op jit(solution)/shard_map/ppermute | solution.py:107
  16.8 24.3 %collective-permute-start.3 = (bf16[2048,512]{1,0:T(8,128)(2,1)}, bf16[2048,512]{1,0:T(8,128)(2,1)S(1)}, u32[]{:S(2)}, u32[]{:S(2)}) collective-permute-start(bf16[2048,512]{1,0:T(8,128)(2,1)} %shard_map.92), channel_id=1, source_target_pairs={{0,1},{1,0},{2,3},{3,2},{4,5},{5,4},{6,7},{7,6},{8,9},{9,8},{10,11... | collective-permute-start | bytes 6291464 | tf_op jit(solution)/shard_map/ppermute | solution.py:111
  27.2 29.1 %collective-permute-start.8 = (bf16[400,1024]{1,0:T(8,128)(2,1)}, bf16[400,1024]{1,0:T(8,128)(2,1)}, u32[]{:S(2)}, u32[]{:S(2)}) collective-permute-start(bf16[400,1024]{1,0:T(8,128)(2,1)} %collective-permute-done.refs_0_.inner_ref.outer_ref), channel_id=1, source_target_pairs={{0,2},{1,3},{2,0},{3,1},{4,6},{5,7},{6,4},{7,5},{8,10},{9,11},{10,... | collective-permute-start | bytes 2457608 | tf_op jit(solution)/shard_map/ppermute | solution.py:107
  28.8 18.8 %collective-permute-start.1 = (bf16[400,1024]{1,0:T(8,128)(2,1)}, bf16[400,1024]{1,0:T(8,128)(2,1)S(1)}, u32[]{:S(2)}, u32[]{:S(2)}) collective-permute-start(bf16[400,1024]{1,0:T(8,128)(2,1)} %collective-permute-done.refs_0_.inner_ref.outer_ref), channel_id=1, source_target_pairs={{4,8},{8,4},{5,9},{9,5},{6,10},{10,6},{7,11},{11,7},{20,24},{24,20... | collective-permute-start | bytes 2457608 | tf_op jit(solution)/shard_map/ppermute | solution.py:115
  29.5 25.0 %collective-permute-start.7 = (bf16[400,1024]{1,0:T(8,128)(2,1)}, bf16[400,1024]{1,0:T(8,128)(2,1)}, u32[]{:S(2)}, u32[]{:S(2)}) collective-permute-start(bf16[400,1024]{1,0:T(8,128)(2,1)} %collective-permute-done.5.refs_0_.inner_ref), channel_id=1, source_target_pairs={{4,0},{8,12},{5,1},{9,13},{6,2},{10,14},{7,3},{11,15},{20,16},{24,... | collective-permute-start | bytes 2457608 | tf_op jit(solution)/shard_map/ppermute | solution.py:115
  32.9 19.9 %collective-permute-start.9 = (bf16[192,1024]{1,0:T(8,128)(2,1)S(1)}, bf16[192,1024]{1,0:T(8,128)(2,1)}, u32[]{:S(2)}, u32[]{:S(2)}) collective-permute-start(bf16[192,1024]{1,0:T(8,128)(2,1)S(1)} %shard_map.96), channel_id=1, source_target_pairs={{0,4},{12,8},{1,5},{13,9},{2,6},{14,10},{3,7},{15,11},{16,20},{28,... | collective-permute-start | bytes 1179656 | tf_op jit(solution)/shard_map/ppermute | solution.py:115
  48.6 21.5 %collective-permute-start.4 = (bf16[400,1024]{1,0:T(8,128)(2,1)}, bf16[400,1024]{1,0:T(8,128)(2,1)}, u32[]{:S(2)}, u32[]{:S(2)}) collective-permute-start(bf16[400,1024]{1,0:T(8,128)(2,1)} %shard_map.94.refs_2_.inner_ref.refs_0_), channel_id=1, source_target_pairs={{4,0},{8,12},{5,1},{9,13},{6,2},{10,14},{7,3},{11,15},{20,16},{24,... | collective-permute-start | bytes 2457608 | tf_op jit(solution)/shard_map/ppermute | solution.py:115
  49.9 15.6 %collective-permute-start.11 = (bf16[384,1024]{1,0:T(8,128)(2,1)}, bf16[384,1024]{1,0:T(8,128)(2,1)}, u32[]{:S(2)}, u32[]{:S(2)}) collective-permute-start(bf16[384,1024]{1,0:T(8,128)(2,1)} %copy-done.19), channel_id=1, source_target_pairs={{0,1},{1,0},{2,3},{3,2},{4,5},{5,4},{6,7},{7,6},{8,9},{9,8},{10,11... | collective-permute-start | bytes 2359304 | tf_op jit(solution)/shard_map/ppermute | solution.py:111
  54.5 15.6 %collective-permute-start.6 = (bf16[400,1024]{1,0:T(8,128)(2,1)}, bf16[400,1024]{1,0:T(8,128)(2,1)}, u32[]{:S(2)}, u32[]{:S(2)}) collective-permute-start(bf16[400,1024]{1,0:T(8,128)(2,1)} %collective-permute-done.5.refs_0_.inner_ref), channel_id=1, source_target_pairs={{4,6},{5,7},{6,4},{7,5},{8,10},{9,11},{10,8},{11,9},{20,22},{21,23... | collective-permute-start | bytes 2457608 | tf_op jit(solution)/shard_map/ppermute | solution.py:424
  56.2 22.8 %collective-permute-start.10 = (bf16[400,1024]{1,0:T(8,128)(2,1)}, bf16[400,1024]{1,0:T(8,128)(2,1)}, u32[]{:S(2)}, u32[]{:S(2)}) collective-permute-start(bf16[400,1024]{1,0:T(8,128)(2,1)} %shard_map.97.refs_1_.outer_ref), channel_id=1, source_target_pairs={{0,2},{1,3},{2,0},{3,1},{12,14},{13,15},{14,12},{15,13},{16,18},{1... | collective-permute-start | bytes 2457608 | tf_op jit(solution)/shard_map/ppermute | solution.py:424
  58.7 34.8 %collective-permute-start.14 = (bf16[192,1024]{1,0:T(8,128)(2,1)S(1)}, bf16[192,1024]{1,0:T(8,128)(2,1)}, u32[]{:S(2)}, u32[]{:S(2)}) collective-permute-start(bf16[192,1024]{1,0:T(8,128)(2,1)S(1)} %collective-permute-done.13.refs_1_), channel_id=1, source_target_pairs={{4,0},{8,12},{5,1},{9,13},{6,2},{10,14},{7,3},{11,15},{20,16},{24,... | collective-permute-start | bytes 1179656 | tf_op jit(solution)/shard_map/ppermute | solution.py:115
  65.5 17.6 %collective-permute-start.15 = (bf16[384,1024]{1,0:T(8,128)(2,1)}, bf16[384,1024]{1,0:T(8,128)(2,1)}, u32[]{:S(2)}, u32[]{:S(2)}) collective-permute-start(bf16[384,1024]{1,0:T(8,128)(2,1)} %get-tuple-element.37), channel_id=1, source_target_pairs={{0,1},{1,0},{2,3},{3,2},{4,5},{5,4},{6,7},{7,6},{8,9},{9,8},{10,11... | collective-permute-start | bytes 2359304 | tf_op jit(solution)/shard_map/ppermute | solution.py:111
  83.1 15.8 %collective-permute-start.18 = (bf16[256,2048]{1,0:T(8,128)(2,1)}, bf16[256,2048]{1,0:T(8,128)(2,1)S(1)}, u32[]{:S(2)}, u32[]{:S(2)}) collective-permute-start(bf16[256,2048]{1,0:T(8,128)(2,1)} %pad_maximum_fusion.2.refs_4_), channel_id=1, source_target_pairs={{0,1},{1,0},{2,3},{3,2},{4,5},{5,4},{6,7},{7,6},{8,9},{9,8},{10,11... | collective-permute-start | bytes 3145736 | tf_op jit(solution)/shard_map/ppermute | solution.py:111
  101.6 12.0 %collective-permute-start.20 = (bf16[192,1024]{1,0:T(8,128)(2,1)S(1)}, bf16[192,1024]{1,0:T(8,128)(2,1)S(1)}, u32[]{:S(2)}, u32[]{:S(2)}) collective-permute-start(bf16[192,1024]{1,0:T(8,128)(2,1)S(1)} %get-tuple-element.50), channel_id=1, source_target_pairs={{0,2},{1,3},{2,0},{3,1},{4,6},{5,7},{6,4},{7,5},{8,10},{9,11},{10,... | collective-permute-start | bytes 1179656 | tf_op jit(solution)/shard_map/ppermute | solution.py:107
  104.6 17.9 %collective-permute-start.22 = (bf16[192,1024]{1,0:T(8,128)(2,1)S(1)}, bf16[192,1024]{1,0:T(8,128)(2,1)S(1)}, u32[]{:S(2)}, u32[]{:S(2)}) collective-permute-start(bf16[192,1024]{1,0:T(8,128)(2,1)S(1)} %get-tuple-element.52), channel_id=1, source_target_pairs={{0,2},{1,3},{2,0},{3,1},{4,6},{5,7},{6,4},{7,5},{8,10},{9,11},{10,... | collective-permute-start | bytes 1179656 | tf_op jit(solution)/shard_map/ppermute | solution.py:107
  113.7 14.4 %collective-permute-start.24 = (bf16[192,1024]{1,0:T(8,128)(2,1)S(1)}, bf16[192,1024]{1,0:T(8,128)(2,1)S(1)}, u32[]{:S(2)}, u32[]{:S(2)}) collective-permute-start(bf16[192,1024]{1,0:T(8,128)(2,1)S(1)} %add_convert_fusion.4), channel_id=1, source_target_pairs={{0,4},{12,8},{1,5},{13,9},{2,6},{14,10},{3,7},{15,11},{16,20},{28,... | collective-permute-start | bytes 1179656 | tf_op jit(solution)/shard_map/ppermute | solution.py:115
  119.7 23.0 %collective-permute-start.19 = (bf16[192,1024]{1,0:T(8,128)(2,1)S(1)}, bf16[192,1024]{1,0:T(8,128)(2,1)S(1)}, u32[]{:S(2)}, u32[]{:S(2)}) collective-permute-start(bf16[192,1024]{1,0:T(8,128)(2,1)S(1)} %get-tuple-element.48), channel_id=1, source_target_pairs={{0,2},{1,3},{2,0},{3,1},{4,6},{5,7},{6,4},{7,5},{8,10},{9,11},{10,... | collective-permute-start | bytes 1179656 | tf_op jit(solution)/shard_map/ppermute | solution.py:107
  121.3 17.2 %collective-permute-start.26 = (bf16[192,1024]{1,0:T(8,128)(2,1)S(1)}, bf16[192,1024]{1,0:T(8,128)(2,1)S(1)}, u32[]{:S(2)}, u32[]{:S(2)}) collective-permute-start(bf16[192,1024]{1,0:T(8,128)(2,1)S(1)} %get-tuple-element.54), channel_id=1, source_target_pairs={{0,2},{1,3},{2,0},{3,1},{4,6},{5,7},{6,4},{7,5},{8,10},{9,11},{10,... | collective-permute-start | bytes 1179656 | tf_op jit(solution)/shard_map/ppermute | solution.py:107
  121.8 20.9 %collective-permute-start.21 = (bf16[192,1024]{1,0:T(8,128)(2,1)S(1)}, bf16[192,1024]{1,0:T(8,128)(2,1)S(1)}, u32[]{:S(2)}, u32[]{:S(2)}) collective-permute-start(bf16[192,1024]{1,0:T(8,128)(2,1)S(1)} %add_convert_fusion.4), channel_id=1, source_target_pairs={{4,8},{8,4},{5,9},{9,5},{6,10},{10,6},{7,11},{11,7},{20,24},{24,20... | collective-permute-start | bytes 1179656 | tf_op jit(solution)/shard_map/ppermute | solution.py:115
  122.6 20.1 %collective-permute-start.23 = (bf16[192,1024]{1,0:T(8,128)(2,1)S(1)}, bf16[192,1024]{1,0:T(8,128)(2,1)S(1)}, u32[]{:S(2)}, u32[]{:S(2)}) collective-permute-start(bf16[192,1024]{1,0:T(8,128)(2,1)S(1)} %add_convert_fusion.3), channel_id=1, source_target_pairs={{0,8},{12,4},{1,9},{13,5},{2,10},{14,6},{3,11},{15,7},{16,24},{28,... | collective-permute-start | bytes 1179656 | tf_op jit(solution)/shard_map/ppermute | solution.py:115
  128.2 21.1 %collective-permute-start.25 = (bf16[192,1024]{1,0:T(8,128)(2,1)S(1)}, bf16[192,1024]{1,0:T(8,128)(2,1)S(1)}, u32[]{:S(2)}, u32[]{:S(2)}) collective-permute-start(bf16[192,1024]{1,0:T(8,128)(2,1)S(1)} %add_convert_fusion.2), channel_id=1, source_target_pairs={{4,12},{8,0},{5,13},{9,1},{6,14},{10,2},{7,15},{11,3},{20,28},{24,... | collective-permute-start | bytes 1179656 | tf_op jit(solution)/shard_map/ppermute | solution.py:115
  138.6 19.0 %collective-permute-start.27 = (bf16[192,1024]{1,0:T(8,128)(2,1)S(1)}, bf16[192,1024]{1,0:T(8,128)(2,1)S(1)}, u32[]{:S(2)}, u32[]{:S(2)}) collective-permute-start(bf16[192,1024]{1,0:T(8,128)(2,1)S(1)} %add_convert_fusion.1), channel_id=1, source_target_pairs={{0,4},{4,0},{8,12},{12,8},{1,5},{5,1},{9,13},{13,9},{2,6},{6,2},{1... | collective-permute-start | bytes 1179656 | tf_op jit(solution)/shard_map/ppermute | solution.py:115
  (30 other events, 138.4 us)

commit v17 on v12

--- a/solution.py
+++ b/solution.py
@@ -120,7 +120,7 @@
 
 
 TOKEN = jax.ShapeDtypeStruct((8, 128), jnp.float32)
-VMEM_LIMIT = 40 * 2**20
+VMEM_LIMIT = 18 * 2**20
 
 
 def on_core(body, out_shape, in_specs, scratch=()):

time: 144 us -> 144 us (level)
  no operation moved by 1% of the time
where the time goes in v17:
time: 144 us; the launch traced here: 143 us
  starting transfers between devices  47 us (33%)
  waiting for transfers between devices  45.2 us (31%)
  Pallas kernels  30.7 us (21%)
  local copies, waits for them, and re-layouts  15.5 us (11%)
  other arithmetic  4.49 us (3%)
    ppermute x13, starting transfers between devices, along(): return lax.ppermute(block, 'blk', route)  33.8 us
    ppermute x13, waiting for transfers between devices, along(): return lax.ppermute(block, 'blk', route)  29.9 us
    pallas_call x5, Pallas kernels, partial_sums(): return on_core(body, shapes + [TOKEN], specs)(*operands, *waits)  14.8 us
    ppermute x7, waiting for transfers between devices, across_chips(): return lax.ppermute(block, 'tp', [(i, i ^ 2) for i in range(4)])  13.4 us
    unnamed x56, local copies, waits for them, and re-layouts  8.75 us
    ppermute x7, starting transfers between devices, across_chips(): return lax.ppermute(block, 'tp', [(i, i ^ 2) for i in range(4)])  8 us
    pallas_call x3, Pallas kernels, collect(): on_core(body, [shape, TOKEN], specs, fact_scratch(facts[0].shape[1]))  6.13 us
    ppermute x2, starting transfers between devices, at_kind(): return lax.ppermute(block, ('blk', 'tp'), pairs)  4.11 us
  transfers between devices with their start and end apart: 28, of which 10 were waited for; matrix products, arithmetic and copies ran while one was open for 7% of the time, Pallas kernels for 18%

profile of v17, /device:TPU:0, one launch (start us, length us, event | category | flops | bytes accessed | tf_op | source)
XLA Modules:
  0.0 143.4 jit_solution(1447488250219774846)
XLA Ops:
  4.5 3.1 %collective-permute-start = (bf16[400,1024]{1,0:T(8,128)(2,1)S(1)}, bf16[400,1024]{1,0:T(8,128)(2,1)}, u32[]{:S(2)}, u32[]{:S(2)}) collective-permute-start(bf16[400,1024]{1,0:T(8,128)(2,1)S(1)} %shard_map.91.refs_1_.inner_ref.outer_ref), channel_id=1, source_target_pairs={{0,4},{4,0},{8,12},{12,8},{1,5},{5,1},{9,13},{13,9},{2,6},{6,2},{1... | collective-permute-start | bytes 2457608 | tf_op jit(solution)/shard_map/ppermute | solution.py:115
  10.7 3.4 %dynamic-slice_bitcast_fusion.4 = (bf16[1024,256]{1,0:T(8,128)(2,1)S(1)}, bf16[1024,256]{1,0:T(8,128)(2,1)S(1)}, bf16[1024,256]{1,0:T(8,128)(2,1)S(1)}, bf16[102...) fusion(bf16[4,1024,256]{2,1,0:T(8,128)(2,1)} %bitcast.32, ...), kind=kLoop, calls=%fused_computation.15 | loop fusion | bytes 8388624 | tf_op jit(solution)/shard_map/jit(dynamic_index_in_dim)/squeeze | solution.py:410
  16.2 2.7 %dynamic-slice_bitcast_fusion.1 = (bf16[256,1024]{1,0:T(8,128)(2,1)}, bf16[256,1024]{1,0:T(8,128)(2,1)S(1)}, bf16[256,1024]{1,0:T(8,128)(2,1)S(1)}, bf16[256,1024]{1,0:T(8,128)(2,1)}) fusion(bf16[1,256,4096]{2,1,0:T(8,128)(2,1)} %param.12, s32[]{:T(128)S(6)} %select_n.39, s32[]{:T(128)S(6)} %select_n.34, s32[]{:T(128)S(6)} %select_n.33, s32[]{:T(128)S(6)} %select_n.40), kind=kLoop, calls=%fused_computation.12 | loop fusion | bytes 4194320 | tf_op jit(solution)/shard_map/dynamic_slice | solution.py:416
  18.9 7.1 %collective-permute-done.refs_0_.inner_ref.outer_ref = bf16[400,1024]{1,0:T(8,128)(2,1)} collective-permute-done((bf16[400,1024]{1,0:T(8,128)(2,1)S(1)}, bf16[400,1024]{1,0:T(8,128)(2,1)}, u32[]{:S(2)}, u32[]{:S(2)}) %collective-permute-start) | collective-permute-done | bytes 819232 | tf_op jit(solution)/shard_map/ppermute | solution.py:115
  32.6 5.6 %collective-permute-start.8 = (bf16[192,1024]{1,0:T(8,128)(2,1)S(1)}, bf16[192,1024]{1,0:T(8,128)(2,1)S(1)}, u32[]{:S(2)}, u32[]{:S(2)}) collective-permute-start(bf16[192,1024]{1,0:T(8,128)(2,1)S(1)} %shard_map.92), channel_id=1, source_target_pairs={{0,4},{12,8},{1,5},{13,9},{2,6},{14,10},{3,7},{15,11},{16,20},{28,... | collective-permute-start | bytes 1179656 | tf_op jit(solution)/shard_map/ppermute | solution.py:115
  42.5 3.2 %shard_map.94 = (f32[384,1024]{1,0:T(8,128)S(1)}, bf16[384,1024]{1,0:T(8,128)(2,1)S(1)}, f32[8,128]{1,0:T(8,128)S(1)}) custom-call(s32[9]{0:T(128)S(1)} %fusion.plan_ref, bf16[384,1024]{1,0:T(8,128)(2,1)} %refs_0_.1, bf16[384,1024]{1,0:T(8,128)(2,1)} %collective-permute-done.7.inner_ref.outer_ref.refs_1_, ...), custom_call_target="tpu_custom_call" | custom-call | flops 1024 | bytes 1024 | tf_op jit(solution)/shard_map/pallas_call | solution.py:287
  48.4 2.6 %collective-permute-done.5.refs_0_ = bf16[400,1024]{1,0:T(8,128)(2,1)S(1)} collective-permute-done((bf16[400,1024]{1,0:T(8,128)(2,1)}, bf16[400,1024]{1,0:T(8,128)(2,1)S(1)}, u32[]{:S(2)}, u32[]{:S(2)}) %collective-permute-start.5) | collective-permute-done | bytes 819232 | tf_op jit(solution)/shard_map/ppermute | solution.py:115
  52.0 2.6 %collective-permute-start.10 = (bf16[400,1024]{1,0:T(8,128)(2,1)}, bf16[400,1024]{1,0:T(8,128)(2,1)S(1)}, u32[]{:S(2)}, u32[]{:S(2)}) collective-permute-start(bf16[400,1024]{1,0:T(8,128)(2,1)} %shard_map.95.refs_1_.outer_ref), channel_id=1, source_target_pairs={{0,2},{1,3},{2,0},{3,1},{12,14},{13,15},{14,12},{15,13},{16,18},{1... | collective-permute-start | bytes 2457608 | tf_op jit(solution)/shard_map/ppermute | solution.py:424
  57.7 3.0 %shard_map.96 = (f32[384,1024]{1,0:T(8,128)S(1)}, bf16[384,1024]{1,0:T(8,128)(2,1)S(1)}, f32[8,128]{1,0:T(8,128)S(1)}) custom-call(s32[9]{0:T(128)S(1)} %fusion.plan_ref, bf16[400,1024]{1,0:T(8,128)(2,1)} %collective-permute-done.refs_0_.inner_ref.outer_ref, bf16[400,1024]{1,0:T(8,128)(2,1)S(1)} %copy-done.10, bf16[1024,512]{1,0:T(8,128)(2,1)S(1)} %copy-done.3, ...), custom_call_target="tpu_custom_call" | custom-call | flops 1024 | bytes 1024 | tf_op jit(solution)/shard_map/pallas_call | solution.py:287
  62.7 7.5 %collective-permute-done.2.outer_ref.refs_1_ = bf16[400,1024]{1,0:T(8,128)(2,1)} collective-permute-done((bf16[400,1024]{1,0:T(8,128)(2,1)}, bf16[400,1024]{1,0:T(8,128)(2,1)}, u32[]{:S(2)}, u32[]{:S(2)}) %collective-permute-start.2) | collective-permute-done | bytes 819232 | tf_op jit(solution)/shard_map/ppermute | solution.py:115
  72.1 2.0 %shard_map.97 = bf16[192,1024]{1,0:T(8,128)(2,1)S(1)} custom-call(s32[9]{0:T(128)S(1)} %fusion.plan_ref, bf16[400,1024]{1,0:T(8,128)(2,1)} %collective-permute-done.1.refs_2_.inner_ref.refs_0_, bf16[400,1024]{1,0:T(8,128)(2,1)} %collective-permute-done.2.outer_ref.refs_1_, bf16[400,1024]{1,0:T(8,128)(2,1)} %collective-permute-done.4.rest_0_.refs_2_, ...), custom_call_target="tpu_custom_call" | custom-call | flops 1024 | bytes 1024 | tf_op jit(solution)/shard_map/pallas_call | solution.py:192
  74.7 3.0 %shard_map.98 = (f32[384,1024]{1,0:T(8,128)S(1)}, f32[8,128]{1,0:T(8,128)}) custom-call(s32[9]{0:T(128)S(1)} %fusion.plan_ref, bf16[400,1024]{1,0:T(8,128)(2,1)} %collective-permute-done.1.refs_2_.inner_ref.refs_0_, bf16[400,1024]{1,0:T(8,128)(2,1)} %collective-permute-done.2.outer_ref.refs_1_, bf16[1024,512]{1,0:T(8,128)(2,1)S(1)} %copy-done.4, ...), custom_call_target="tpu_custom_call" | custom-call | flops 1024 | bytes 1024 | tf_op jit(solution)/shard_map/pallas_call | solution.py:287
  79.6 2.2 %shard_map.100 = (f32[768,512]{1,0:T(8,128)S(1)}, f32[8,128]{1,0:T(8,128)S(1)}) custom-call(s32[9]{0:T(128)S(1)} %fusion.plan_ref, f32[384,1024]{1,0:T(8,128)S(1)} %get-tuple-element.32.sums_ref, bf16[384,1024]{1,0:T(8,128)(2,1)S(1)} %collective-permute-done.14.got_ref, bf16[400,1024]{1,0:T(8,128)(2,1)} %collective-permute-done.refs_0_.inner_ref.outer_ref, ...), custom_call_target="tpu_custom_call" | custom-call | flops 1024 | bytes 1024 | tf_op jit(solution)/shard_map/pallas_call | solution.py:346
  81.8 3.7 %shard_map.102 = (f32[384,1024]{1,0:T(8,128)S(1)}, bf16[384,1024]{1,0:T(8,128)(2,1)S(1)}, f32[8,128]{1,0:T(8,128)}) custom-call(s32[9]{0:T(128)S(1)} %fusion.plan_ref, bf16[400,1024]{1,0:T(8,128)(2,1)} %collective-permute-done.3.refs_0_.inner_ref, bf16[400,1024]{1,0:T(8,128)(2,1)S(1)} %copy-done.8, bf16[400,1024]{1,0:T(8,128)(2,1)} %collective-permute-done.4.rest_0_.refs_2_, ...), custom_call_target="tpu_custom_call" | custom-call | flops 1024 | bytes 1024 | tf_op jit(solution)/shard_map/pallas_call | solution.py:287
  85.9 2.0 %shard_map.101 = (f32[384,1024]{1,0:T(8,128)S(1)}, bf16[384,1024]{1,0:T(8,128)(2,1)S(1)}, f32[8,128]{1,0:T(8,128)}) custom-call(s32[9]{0:T(128)S(1)} %fusion.plan_ref, bf16[192,1024]{1,0:T(8,128)(2,1)S(1)} %collective-permute-done.12.refs_0_, bf16[192,1024]{1,0:T(8,128)(2,1)S(1)} %collective-permute-done.11.rest_2_.refs_1_, ...), custom_call_target="tpu_custom_call" | custom-call | flops 1024 | bytes 1024 | tf_op jit(solution)/shard_map/pallas_call | solution.py:287
  88.2 2.1 %shard_map.103 = (f32[768,512]{1,0:T(8,128)S(1)}, f32[8,128]{1,0:T(8,128)}) custom-call(s32[9]{0:T(128)S(1)} %fusion.plan_ref, f32[384,1024]{1,0:T(8,128)S(1)} %get-tuple-element.40.sums_ref, bf16[384,1024]{1,0:T(8,128)(2,1)S(1)} %collective-permute-done.17.got_ref, bf16[400,1024]{1,0:T(8,128)(2,1)} %collective-permute-done.3.refs_0_.inner_ref, ...), custom_call_target="tpu_custom_call" | custom-call | flops 1024 | bytes 1024 | tf_op jit(solution)/shard_map/pallas_call | solution.py:346
  90.3 2.6 %shard_map.104 = (bf16[192,1024]{1,0:T(8,128)(2,1)S(1)}, f32[192,1024]{1,0:T(8,128)S(1)}, bf16[576,512]{1,0:T(8,128)(2,1)S(1)}) custom-call(s32[9]{0:T(128)S(1)} %fusion.plan_ref, f32[384,1024]{1,0:T(8,128)S(1)} %get-tuple-element.38.sums_ref, bf16[384,1024]{1,0:T(8,128)(2,1)S(1)} %collective-permute-done.16.got_ref, ...), custom_call_target="tpu_custom_call" | custom-call | flops 1024 | bytes 1024 | tf_op jit(solution)/shard_map/pallas_call | solution.py:380
  96.4 8.4 %collective-permute-done.20 = bf16[192,1024]{1,0:T(8,128)(2,1)S(1)} collective-permute-done((bf16[192,1024]{1,0:T(8,128)(2,1)S(1)}, bf16[192,1024]{1,0:T(8,128)(2,1)S(1)}, u32[]{:S(2)}, u32[]{:S(2)}) %collective-permute-start.20) | collective-permute-done | bytes 393248 | tf_op jit(solution)/shard_map/ppermute | solution.py:107
  104.9 6.0 %collective-permute-start.24 = (bf16[192,1024]{1,0:T(8,128)(2,1)S(1)}, bf16[192,1024]{1,0:T(8,128)(2,1)S(1)}, u32[]{:S(2)}, u32[]{:S(2)}) collective-permute-start(bf16[192,1024]{1,0:T(8,128)(2,1)S(1)} %add_convert_fusion.4), channel_id=1, source_target_pairs={{0,4},{12,8},{1,5},{13,9},{2,6},{14,10},{3,7},{15,11},{16,20},{28,... | collective-permute-start | bytes 1179656 | tf_op jit(solution)/shard_map/ppermute | solution.py:115
  113.8 6.6 %collective-permute-start.23 = (bf16[192,1024]{1,0:T(8,128)(2,1)S(1)}, bf16[192,1024]{1,0:T(8,128)(2,1)S(1)}, u32[]{:S(2)}, u32[]{:S(2)}) collective-permute-start(bf16[192,1024]{1,0:T(8,128)(2,1)S(1)} %add_convert_fusion.3), channel_id=1, source_target_pairs={{0,8},{12,4},{1,9},{13,5},{2,10},{14,6},{3,11},{15,7},{16,24},{28,... | collective-permute-start | bytes 1179656 | tf_op jit(solution)/shard_map/ppermute | solution.py:115
  123.1 2.8 %collective-permute-start.27 = (bf16[192,1024]{1,0:T(8,128)(2,1)S(1)}, bf16[192,1024]{1,0:T(8,128)(2,1)S(1)}, u32[]{:S(2)}, u32[]{:S(2)}) collective-permute-start(bf16[192,1024]{1,0:T(8,128)(2,1)S(1)} %add_convert_fusion.1), channel_id=1, source_target_pairs={{0,4},{4,0},{8,12},{12,8},{1,5},{5,1},{9,13},{13,9},{2,6},{6,2},{1... | collective-permute-start | bytes 1179656 | tf_op jit(solution)/shard_map/ppermute | solution.py:115
  125.9 3.8 %collective-permute-done.19 = bf16[192,1024]{1,0:T(8,128)(2,1)S(1)} collective-permute-done((bf16[192,1024]{1,0:T(8,128)(2,1)S(1)}, bf16[192,1024]{1,0:T(8,128)(2,1)S(1)}, u32[]{:S(2)}, u32[]{:S(2)}) %collective-permute-start.19) | collective-permute-done | bytes 393248 | tf_op jit(solution)/shard_map/ppermute | solution.py:107
  129.9 10.2 %collective-permute-done.25 = bf16[192,1024]{1,0:T(8,128)(2,1)S(1)} collective-permute-done((bf16[192,1024]{1,0:T(8,128)(2,1)S(1)}, bf16[192,1024]{1,0:T(8,128)(2,1)S(1)}, u32[]{:S(2)}, u32[]{:S(2)}) %collective-permute-start.25) | collective-permute-done | bytes 393248 | tf_op jit(solution)/shard_map/ppermute | solution.py:115
  140.4 2.2 %collective-permute-done.27 = bf16[192,1024]{1,0:T(8,128)(2,1)S(1)} collective-permute-done((bf16[192,1024]{1,0:T(8,128)(2,1)S(1)}, bf16[192,1024]{1,0:T(8,128)(2,1)S(1)}, u32[]{:S(2)}, u32[]{:S(2)}) %collective-permute-start.27) | collective-permute-done | bytes 393248 | tf_op jit(solution)/shard_map/ppermute | solution.py:115
  (117 shorter events, 44.9 us)
Async XLA Ops:
  4.5 21.4 %collective-permute-start = (bf16[400,1024]{1,0:T(8,128)(2,1)S(1)}, bf16[400,1024]{1,0:T(8,128)(2,1)}, u32[]{:S(2)}, u32[]{:S(2)}) collective-permute-start(bf16[400,1024]{1,0:T(8,128)(2,1)S(1)} %shard_map.91.refs_1_.inner_ref.outer_ref), channel_id=1, source_target_pairs={{0,4},{4,0},{8,12},{12,8},{1,5},{5,1},{9,13},{13,9},{2,6},{6,2},{1... | collective-permute-start | bytes 2457608 | tf_op jit(solution)/shard_map/ppermute | solution.py:115
  7.6 21.7 %collective-permute-start.3 = (bf16[400,1024]{1,0:T(8,128)(2,1)S(1)}, bf16[400,1024]{1,0:T(8,128)(2,1)}, u32[]{:S(2)}, u32[]{:S(2)}) collective-permute-start(bf16[400,1024]{1,0:T(8,128)(2,1)S(1)} %shard_map.91.refs_1_.inner_ref.outer_ref), channel_id=1, source_target_pairs={{4,8},{8,4},{5,9},{9,5},{6,10},{10,6},{7,11},{11,7},{20,24},{24,20... | collective-permute-start | bytes 2457608 | tf_op jit(solution)/shard_map/ppermute | solution.py:115
  9.2 21.4 %collective-permute-start.7 = (bf16[384,1024]{1,0:T(8,128)(2,1)}, bf16[384,1024]{1,0:T(8,128)(2,1)}, u32[]{:S(2)}, u32[]{:S(2)}) collective-permute-start(bf16[384,1024]{1,0:T(8,128)(2,1)} %refs_0_.1), channel_id=1, source_target_pairs={{0,2},{1,3},{2,0},{3,1},{4,6},{5,7},{6,4},{7,5},{8,10},{9,11},{10,... | collective-permute-start | bytes 2359304 | tf_op jit(solution)/shard_map/ppermute | solution.py:107
  15.6 25.7 %collective-permute-start.9 = (bf16[2048,512]{1,0:T(8,128)(2,1)}, bf16[2048,512]{1,0:T(8,128)(2,1)S(1)}, u32[]{:S(2)}, u32[]{:S(2)}) collective-permute-start(bf16[2048,512]{1,0:T(8,128)(2,1)} %shard_map.93), channel_id=1, source_target_pairs={{0,1},{1,0},{2,3},{3,2},{4,5},{5,4},{6,7},{7,6},{8,9},{9,8},{10,11... | collective-permute-start | bytes 6291464 | tf_op jit(solution)/shard_map/ppermute | solution.py:111
  26.0 13.7 %collective-permute-start.1 = (bf16[400,1024]{1,0:T(8,128)(2,1)}, bf16[400,1024]{1,0:T(8,128)(2,1)}, u32[]{:S(2)}, u32[]{:S(2)}) collective-permute-start(bf16[400,1024]{1,0:T(8,128)(2,1)} %collective-permute-done.refs_0_.inner_ref.outer_ref), channel_id=1, source_target_pairs={{4,8},{8,4},{5,9},{9,5},{6,10},{10,6},{7,11},{11,7},{20,24},{24,20... | collective-permute-start | bytes 2457608 | tf_op jit(solution)/shard_map/ppermute | solution.py:115
  27.6 20.8 %collective-permute-start.6 = (bf16[400,1024]{1,0:T(8,128)(2,1)}, bf16[400,1024]{1,0:T(8,128)(2,1)S(1)}, u32[]{:S(2)}, u32[]{:S(2)}) collective-permute-start(bf16[400,1024]{1,0:T(8,128)(2,1)} %collective-permute-done.refs_0_.inner_ref.outer_ref), channel_id=1, source_target_pairs={{0,2},{1,3},{2,0},{3,1},{4,6},{5,7},{6,4},{7,5},{8,10},{9,11},{10,... | collective-permute-start | bytes 2457608 | tf_op jit(solution)/shard_map/ppermute | solution.py:107
  29.3 21.8 %collective-permute-start.5 = (bf16[400,1024]{1,0:T(8,128)(2,1)}, bf16[400,1024]{1,0:T(8,128)(2,1)S(1)}, u32[]{:S(2)}, u32[]{:S(2)}) collective-permute-start(bf16[400,1024]{1,0:T(8,128)(2,1)} %collective-permute-done.3.refs_0_.inner_ref), channel_id=1, source_target_pairs={{4,0},{8,12},{5,1},{9,13},{6,2},{10,14},{7,3},{11,15},{20,16},{24,... | collective-permute-start | bytes 2457608 | tf_op jit(solution)/shard_map/ppermute | solution.py:115
  32.6 15.8 %collective-permute-start.8 = (bf16[192,1024]{1,0:T(8,128)(2,1)S(1)}, bf16[192,1024]{1,0:T(8,128)(2,1)S(1)}, u32[]{:S(2)}, u32[]{:S(2)}) collective-permute-start(bf16[192,1024]{1,0:T(8,128)(2,1)S(1)} %shard_map.92), channel_id=1, source_target_pairs={{0,4},{12,8},{1,5},{13,9},{2,6},{14,10},{3,7},{15,11},{16,20},{28,... | collective-permute-start | bytes 1179656 | tf_op jit(solution)/shard_map/ppermute | solution.py:115
  39.7 21.6 %collective-permute-start.4 = (bf16[400,1024]{1,0:T(8,128)(2,1)}, bf16[400,1024]{1,0:T(8,128)(2,1)}, u32[]{:S(2)}, u32[]{:S(2)}) collective-permute-start(bf16[400,1024]{1,0:T(8,128)(2,1)} %collective-permute-done.3.refs_0_.inner_ref), channel_id=1, source_target_pairs={{4,6},{5,7},{6,4},{7,5},{8,10},{9,11},{10,8},{11,9},{20,22},{21,23... | collective-permute-start | bytes 2457608 | tf_op jit(solution)/shard_map/ppermute | solution.py:424
  41.2 29.0 %collective-permute-start.2 = (bf16[400,1024]{1,0:T(8,128)(2,1)}, bf16[400,1024]{1,0:T(8,128)(2,1)}, u32[]{:S(2)}, u32[]{:S(2)}) collective-permute-start(bf16[400,1024]{1,0:T(8,128)(2,1)} %collective-permute-done.1.refs_2_.inner_ref.refs_0_), channel_id=1, source_target_pairs={{4,0},{8,12},{5,1},{9,13},{6,2},{10,14},{7,3},{11,15},{20,16},{24,... | collective-permute-start | bytes 2457608 | tf_op jit(solution)/shard_map/ppermute | solution.py:115
  52.0 20.1 %collective-permute-start.10 = (bf16[400,1024]{1,0:T(8,128)(2,1)}, bf16[400,1024]{1,0:T(8,128)(2,1)S(1)}, u32[]{:S(2)}, u32[]{:S(2)}) collective-permute-start(bf16[400,1024]{1,0:T(8,128)(2,1)} %shard_map.95.refs_1_.outer_ref), channel_id=1, source_target_pairs={{0,2},{1,3},{2,0},{3,1},{12,14},{13,15},{14,12},{15,13},{16,18},{1... | collective-permute-start | bytes 2457608 | tf_op jit(solution)/shard_map/ppermute | solution.py:424
  55.2 22.5 %collective-permute-start.15 = (bf16[384,1024]{1,0:T(8,128)(2,1)}, bf16[384,1024]{1,0:T(8,128)(2,1)S(1)}, u32[]{:S(2)}, u32[]{:S(2)}) collective-permute-start(bf16[384,1024]{1,0:T(8,128)(2,1)} %copy-done.19), channel_id=1, source_target_pairs={{0,1},{1,0},{2,3},{3,2},{4,5},{5,4},{6,7},{7,6},{8,9},{9,8},{10,11... | collective-permute-start | bytes 2359304 | tf_op jit(solution)/shard_map/ppermute | solution.py:111
  60.7 18.9 %collective-permute-start.14 = (bf16[384,1024]{1,0:T(8,128)(2,1)S(1)}, bf16[384,1024]{1,0:T(8,128)(2,1)S(1)}, u32[]{:S(2)}, u32[]{:S(2)}) collective-permute-start(bf16[384,1024]{1,0:T(8,128)(2,1)S(1)} %get-tuple-element.33), channel_id=1, source_target_pairs={{0,1},{1,0},{2,3},{3,2},{4,5},{5,4},{6,7},{7,6},{8,9},{9,8},{10,11... | collective-permute-start | bytes 2359304 | tf_op jit(solution)/shard_map/ppermute | solution.py:111
  61.2 24.7 %collective-permute-start.13 = (bf16[192,1024]{1,0:T(8,128)(2,1)S(1)}, bf16[192,1024]{1,0:T(8,128)(2,1)S(1)}, u32[]{:S(2)}, u32[]{:S(2)}) collective-permute-start(bf16[192,1024]{1,0:T(8,128)(2,1)S(1)} %collective-permute-done.11.rest_2_.refs_1_), channel_id=1, source_target_pairs={{4,0},{8,12},{5,1},{9,13},{6,2},{10,14},{7,3},{11,15},{20,16},{24,... | collective-permute-start | bytes 1179656 | tf_op jit(solution)/shard_map/ppermute | solution.py:115
  74.7 15.6 %collective-permute-start.18 = (bf16[256,2048]{1,0:T(8,128)(2,1)S(1)}, bf16[256,2048]{1,0:T(8,128)(2,1)S(1)}, u32[]{:S(2)}, u32[]{:S(2)}) collective-permute-start(bf16[256,2048]{1,0:T(8,128)(2,1)S(1)} %copy-done.20), channel_id=1, source_target_pairs={{0,1},{1,0},{2,3},{3,2},{4,5},{5,4},{6,7},{7,6},{8,9},{9,8},{10,11... | collective-permute-start | bytes 3145736 | tf_op jit(solution)/shard_map/ppermute | solution.py:111
  92.9 12.0 %collective-permute-start.20 = (bf16[192,1024]{1,0:T(8,128)(2,1)S(1)}, bf16[192,1024]{1,0:T(8,128)(2,1)S(1)}, u32[]{:S(2)}, u32[]{:S(2)}) collective-permute-start(bf16[192,1024]{1,0:T(8,128)(2,1)S(1)} %get-tuple-element.48), channel_id=1, source_target_pairs={{0,2},{1,3},{2,0},{3,1},{4,6},{5,7},{6,4},{7,5},{8,10},{9,11},{10,... | collective-permute-start | bytes 1179656 | tf_op jit(solution)/shard_map/ppermute | solution.py:107
  95.8 17.9 %collective-permute-start.22 = (bf16[192,1024]{1,0:T(8,128)(2,1)S(1)}, bf16[192,1024]{1,0:T(8,128)(2,1)S(1)}, u32[]{:S(2)}, u32[]{:S(2)}) collective-permute-start(bf16[192,1024]{1,0:T(8,128)(2,1)S(1)} %get-tuple-element.50), channel_id=1, source_target_pairs={{0,2},{1,3},{2,0},{3,1},{4,6},{5,7},{6,4},{7,5},{8,10},{9,11},{10,... | collective-permute-start | bytes 1179656 | tf_op jit(solution)/shard_map/ppermute | solution.py:107
  104.9 15.4 %collective-permute-start.24 = (bf16[192,1024]{1,0:T(8,128)(2,1)S(1)}, bf16[192,1024]{1,0:T(8,128)(2,1)S(1)}, u32[]{:S(2)}, u32[]{:S(2)}) collective-permute-start(bf16[192,1024]{1,0:T(8,128)(2,1)S(1)} %add_convert_fusion.4), channel_id=1, source_target_pairs={{0,4},{12,8},{1,5},{13,9},{2,6},{14,10},{3,7},{15,11},{16,20},{28,... | collective-permute-start | bytes 1179656 | tf_op jit(solution)/shard_map/ppermute | solution.py:115
  110.9 12.1 %collective-permute-start.26 = (bf16[192,1024]{1,0:T(8,128)(2,1)S(1)}, bf16[192,1024]{1,0:T(8,128)(2,1)S(1)}, u32[]{:S(2)}, u32[]{:S(2)}) collective-permute-start(bf16[192,1024]{1,0:T(8,128)(2,1)S(1)} %get-tuple-element.52), channel_id=1, source_target_pairs={{0,2},{1,3},{2,0},{3,1},{4,6},{5,7},{6,4},{7,5},{8,10},{9,11},{10,... | collective-permute-start | bytes 1179656 | tf_op jit(solution)/shard_map/ppermute | solution.py:107
  112.5 17.2 %collective-permute-start.19 = (bf16[192,1024]{1,0:T(8,128)(2,1)S(1)}, bf16[192,1024]{1,0:T(8,128)(2,1)S(1)}, u32[]{:S(2)}, u32[]{:S(2)}) collective-permute-start(bf16[192,1024]{1,0:T(8,128)(2,1)S(1)} %get-tuple-element.46), channel_id=1, source_target_pairs={{0,2},{1,3},{2,0},{3,1},{4,6},{5,7},{6,4},{7,5},{8,10},{9,11},{10,... | collective-permute-start | bytes 1179656 | tf_op jit(solution)/shard_map/ppermute | solution.py:107
  113.0 16.9 %collective-permute-start.21 = (bf16[192,1024]{1,0:T(8,128)(2,1)S(1)}, bf16[192,1024]{1,0:T(8,128)(2,1)S(1)}, u32[]{:S(2)}, u32[]{:S(2)}) collective-permute-start(bf16[192,1024]{1,0:T(8,128)(2,1)S(1)} %add_convert_fusion.4), channel_id=1, source_target_pairs={{4,8},{8,4},{5,9},{9,5},{6,10},{10,6},{7,11},{11,7},{20,24},{24,20... | collective-permute-start | bytes 1179656 | tf_op jit(solution)/shard_map/ppermute | solution.py:115
  113.8 16.1 %collective-permute-start.23 = (bf16[192,1024]{1,0:T(8,128)(2,1)S(1)}, bf16[192,1024]{1,0:T(8,128)(2,1)S(1)}, u32[]{:S(2)}, u32[]{:S(2)}) collective-permute-start(bf16[192,1024]{1,0:T(8,128)(2,1)S(1)} %add_convert_fusion.3), channel_id=1, source_target_pairs={{0,8},{12,4},{1,9},{13,5},{2,10},{14,6},{3,11},{15,7},{16,24},{28,... | collective-permute-start | bytes 1179656 | tf_op jit(solution)/shard_map/ppermute | solution.py:115
  120.5 19.6 %collective-permute-start.25 = (bf16[192,1024]{1,0:T(8,128)(2,1)S(1)}, bf16[192,1024]{1,0:T(8,128)(2,1)S(1)}, u32[]{:S(2)}, u32[]{:S(2)}) collective-permute-start(bf16[192,1024]{1,0:T(8,128)(2,1)S(1)} %add_convert_fusion.2), channel_id=1, source_target_pairs={{4,12},{8,0},{5,13},{9,1},{6,14},{10,2},{7,15},{11,3},{20,28},{24,... | collective-permute-start | bytes 1179656 | tf_op jit(solution)/shard_map/ppermute | solution.py:115
  123.1 19.5 %collective-permute-start.27 = (bf16[192,1024]{1,0:T(8,128)(2,1)S(1)}, bf16[192,1024]{1,0:T(8,128)(2,1)S(1)}, u32[]{:S(2)}, u32[]{:S(2)}) collective-permute-start(bf16[192,1024]{1,0:T(8,128)(2,1)S(1)} %add_convert_fusion.1), channel_id=1, source_target_pairs={{0,4},{4,0},{8,12},{12,8},{1,5},{5,1},{9,13},{13,9},{2,6},{6,2},{1... | collective-permute-start | bytes 1179656 | tf_op jit(solution)/shard_map/ppermute | solution.py:115
  (32 other events, 164.3 us)

commit v18 on v17

--- a/solution.py
+++ b/solution.py
@@ -433,15 +433,13 @@
     weights = [quarter(0), quarter(2), lent]
     whole = [row_count]
     sums_0, send_0, ready_0 = partial_sums(
-        plan, whole, [(tokens, own_far)], weights, (0, 1)
+        plan, whole, [(tokens, own_far)], weights, (0, 1), waits=[lend_down]
     )
     got_0 = across_cores(send_0)
     lent_down = across_cores(lend_down)
 
     outer_last = along(inner_last, OUTWARD)
-    outer_next = after(
-        outer_next, beside_far, inner_last, inward_far, lend_down, weights[0], weights[1], ready_0
-    )
+    outer_next = after(outer_next, beside_far, inner_last, inward_far, ready_0)
     second = (middle, outer_next)
     second_far = (at_kind(middle, (1, 2)), at_kind(outer_next, (0, 3)))
     middle_far = along(inward_far, MIDDLE)
@@ -477,7 +475,7 @@
     first, second, third = [block.astype(jnp.bfloat16) for block in joined[:3]]
     second = lax.optimization_barrier(second)
     inward = along(first, INWARD)
-    middle = along(first, MIDDLE)
+    middle = after(along(first, MIDDLE), flops=8 * 2**30)
     two_in = along(second, TWO_IN)
     passed = second.astype(jnp.float32) + inward.astype(jnp.float32)
     two_out = along(passed.astype(jnp.bfloat16), TWO_OUT)

time: 144 us -> 150 us (1.042)
  waiting for transfers between devices: 45.2 us -> 49 us
  other arithmetic: 4.49 us -> 6.08 us
    ppermute x13, waiting for transfers between devices: 29.9 us -> 34.1 us  [along(): return lax.ppermute(block, 'blk', route)]
    unnamed x56 -> x48, local copies, waits for them, and re-layouts: 8.75 us -> 7.39 us
  transfers between devices with their start and end apart: 28 -> 28, of which waited for: 10 -> 9; matrix products, arithmetic and copies ran while one was open for 7% -> 8% of each run, Pallas kernels for 18% -> 18%
where the time goes in v18:
time: 150 us; the launch traced here: 149 us
  waiting for transfers between devices  49 us (33%)
  starting transfers between devices  47 us (31%)
  Pallas kernels  31.9 us (21%)
  local copies, waits for them, and re-layouts  14.5 us (10%)
  other arithmetic  6.08 us (4%)
    ppermute x13, waiting for transfers between devices, along(): return lax.ppermute(block, 'blk', route)  34.1 us
    ppermute x13, starting transfers between devices, along(): return lax.ppermute(block, 'blk', route)  33.9 us
    pallas_call x5, Pallas kernels, partial_sums(): return on_core(body, shapes + [TOKEN], specs)(*operands, *waits)  15.3 us
    ppermute x7, waiting for transfers between devices, across_chips(): return lax.ppermute(block, 'tp', [(i, i ^ 2) for i in range(4)])  13.9 us
    ppermute x7, starting transfers between devices, across_chips(): return lax.ppermute(block, 'tp', [(i, i ^ 2) for i in range(4)])  7.94 us
    unnamed x48, local copies, waits for them, and re-layouts  7.39 us
    pallas_call x3, Pallas kernels, collect(): on_core(body, [shape, TOKEN], specs, fact_scratch(facts[0].shape[1]))  6.84 us
    ppermute x2, starting transfers between devices, at_kind(): return lax.ppermute(block, ('blk', 'tp'), pairs)  4 us
  transfers between devices with their start and end apart: 28, of which 9 were waited for; matrix products, arithmetic and copies ran while one was open for 8% of the time, Pallas kernels for 18%

profile of v18, /device:TPU:0, one launch (start us, length us, event | category | flops | bytes accessed | tf_op | source)
XLA Modules:
  0.0 149.0 jit_solution(7530947220283857277)
XLA Ops:
  4.5 3.1 %collective-permute-start = (bf16[400,1024]{1,0:T(8,128)(2,1)S(1)}, bf16[400,1024]{1,0:T(8,128)(2,1)}, u32[]{:S(2)}, u32[]{:S(2)}) collective-permute-start(bf16[400,1024]{1,0:T(8,128)(2,1)S(1)} %shard_map.91.refs_1_.inner_ref.outer_ref), channel_id=1, source_target_pairs={{0,4},{4,0},{8,12},{12,8},{1,5},{5,1},{9,13},{13,9},{2,6},{6,2},{1... | collective-permute-start | bytes 2457608 | tf_op jit(solution)/shard_map/ppermute | solution.py:115
  10.7 3.6 %dynamic-slice_bitcast_fusion.6 = (bf16[1024,256]{1,0:T(8,128)(2,1)S(1)}, bf16[1024,256]{1,0:T(8,128)(2,1)S(1)}, bf16[1024,256]{1,0:T(8,128)(2,1)}, bf16[1024,25...) fusion(bf16[4,1024,256]{2,1,0:T(8,128)(2,1)} %bitcast.32, ...), kind=kLoop, calls=%fused_computation.17 | loop fusion | bytes 8388624 | tf_op jit(solution)/shard_map/jit(dynamic_index_in_dim)/squeeze | solution.py:410
  16.5 2.8 %dynamic-slice_bitcast_fusion.1 = (bf16[256,1024]{1,0:T(8,128)(2,1)}, bf16[256,1024]{1,0:T(8,128)(2,1)S(1)}, bf16[256,1024]{1,0:T(8,128)(2,1)S(1)}, bf16[256,1024]{1,0:T(8,128)(2,1)}) fusion(bf16[1,256,4096]{2,1,0:T(8,128)(2,1)} %param.12, s32[]{:T(128)S(6)} %select_n.39, s32[]{:T(128)S(6)} %select_n.38, s32[]{:T(128)S(6)} %select_n.37, s32[]{:T(128)S(6)} %select_n.40), kind=kLoop, calls=%fused_computation.12 | loop fusion | bytes 4194320 | tf_op jit(solution)/shard_map/dynamic_slice | solution.py:416
  19.3 6.7 %collective-permute-done.refs_0_.inner_ref.outer_ref = bf16[400,1024]{1,0:T(8,128)(2,1)} collective-permute-done((bf16[400,1024]{1,0:T(8,128)(2,1)S(1)}, bf16[400,1024]{1,0:T(8,128)(2,1)}, u32[]{:S(2)}, u32[]{:S(2)}) %collective-permute-start) | collective-permute-done | bytes 819232 | tf_op jit(solution)/shard_map/ppermute | solution.py:115
  32.5 6.5 %collective-permute-start.8 = (bf16[192,1024]{1,0:T(8,128)(2,1)S(1)}, bf16[192,1024]{1,0:T(8,128)(2,1)S(1)}, u32[]{:S(2)}, u32[]{:S(2)}) collective-permute-start(bf16[192,1024]{1,0:T(8,128)(2,1)S(1)} %shard_map.92), channel_id=1, source_target_pairs={{0,4},{12,8},{1,5},{13,9},{2,6},{14,10},{3,7},{15,11},{16,20},{28,... | collective-permute-start | bytes 1179656 | tf_op jit(solution)/shard_map/ppermute | solution.py:115
  42.2 3.2 %shard_map.94 = (f32[384,1024]{1,0:T(8,128)S(1)}, bf16[384,1024]{1,0:T(8,128)(2,1)S(1)}, f32[8,128]{1,0:T(8,128)S(1)}) custom-call(s32[9]{0:T(128)S(1)} %fusion.plan_ref, bf16[384,1024]{1,0:T(8,128)(2,1)} %refs_0_.1, bf16[384,1024]{1,0:T(8,128)(2,1)} %collective-permute-done.7.inner_ref.outer_ref.refs_1_, ...), custom_call_target="tpu_custom_call" | custom-call | flops 1024 | bytes 1024 | tf_op jit(solution)/shard_map/pallas_call | solution.py:287
  48.1 3.0 %collective-permute-done.5.refs_0_ = bf16[400,1024]{1,0:T(8,128)(2,1)} collective-permute-done((bf16[400,1024]{1,0:T(8,128)(2,1)}, bf16[400,1024]{1,0:T(8,128)(2,1)}, u32[]{:S(2)}, u32[]{:S(2)}) %collective-permute-start.5) | collective-permute-done | bytes 819232 | tf_op jit(solution)/shard_map/ppermute | solution.py:115
  51.2 2.4 %collective-permute-start.10 = (bf16[400,1024]{1,0:T(8,128)(2,1)}, bf16[400,1024]{1,0:T(8,128)(2,1)S(1)}, u32[]{:S(2)}, u32[]{:S(2)}) collective-permute-start(bf16[400,1024]{1,0:T(8,128)(2,1)} %shard_map.95.refs_1_.outer_ref), channel_id=1, source_target_pairs={{0,2},{1,3},{2,0},{3,1},{12,14},{13,15},{14,12},{15,13},{16,18},{1... | collective-permute-start | bytes 2457608 | tf_op jit(solution)/shard_map/ppermute | solution.py:424
  55.6 3.2 %shard_map.96 = (f32[384,1024]{1,0:T(8,128)S(1)}, bf16[384,1024]{1,0:T(8,128)(2,1)S(1)}, f32[8,128]{1,0:T(8,128)S(1)}) custom-call(s32[9]{0:T(128)S(1)} %fusion.plan_ref, bf16[400,1024]{1,0:T(8,128)(2,1)} %collective-permute-done.refs_0_.inner_ref.outer_ref, bf16[400,1024]{1,0:T(8,128)(2,1)} %collective-permute-done.6.refs_1_, ...), custom_call_target="tpu_custom_call" | custom-call | flops 1024 | bytes 1024 | tf_op jit(solution)/shard_map/pallas_call | solution.py:287
  60.7 9.5 %collective-permute-done.2.outer_ref.refs_1_ = bf16[400,1024]{1,0:T(8,128)(2,1)} collective-permute-done((bf16[400,1024]{1,0:T(8,128)(2,1)}, bf16[400,1024]{1,0:T(8,128)(2,1)}, u32[]{:S(2)}, u32[]{:S(2)}) %collective-permute-start.2) | collective-permute-done | bytes 819232 | tf_op jit(solution)/shard_map/ppermute | solution.py:115
  73.8 3.0 %shard_map.98 = (f32[384,1024]{1,0:T(8,128)S(1)}, f32[8,128]{1,0:T(8,128)}) custom-call(s32[9]{0:T(128)S(1)} %fusion.plan_ref, bf16[400,1024]{1,0:T(8,128)(2,1)} %collective-permute-done.1.refs_2_.inner_ref.refs_0_, bf16[400,1024]{1,0:T(8,128)(2,1)} %collective-permute-done.2.outer_ref.refs_1_, bf16[1024,512]{1,0:T(8,128)(2,1)S(1)} %pad_maximum_fusion.refs_2_.refs_4_, ...), custom_call_target="tpu_custom_call" | custom-call | flops 1024 | bytes 1024 | tf_op jit(solution)/shard_map/pallas_call | solution.py:287
  76.8 2.1 %shard_map.99 = (f32[768,512]{1,0:T(8,128)S(1)}, f32[8,128]{1,0:T(8,128)}) custom-call(s32[9]{0:T(128)S(1)} %fusion.plan_ref, f32[384,1024]{1,0:T(8,128)S(1)} %copy-done.8, bf16[384,1024]{1,0:T(8,128)(2,1)S(1)} %collective-permute-done.15.got_ref, bf16[400,1024]{1,0:T(8,128)(2,1)S(1)} %copy-done.4, bf16[400,1024]{1,0:T(8,128)(2,1)S(1)} %copy-done.4), custom_call_target="tpu_custom_call" | custom-call | flops 1024 | bytes 1024 | tf_op jit(solution)/shard_map/pallas_call | solution.py:346
  78.9 2.2 %shard_map.100 = (f32[768,512]{1,0:T(8,128)S(1)}, f32[8,128]{1,0:T(8,128)S(1)}) custom-call(s32[9]{0:T(128)S(1)} %fusion.plan_ref, f32[384,1024]{1,0:T(8,128)S(1)} %get-tuple-element.32.sums_ref, bf16[384,1024]{1,0:T(8,128)(2,1)S(1)} %collective-permute-done.14.got_ref, bf16[400,1024]{1,0:T(8,128)(2,1)} %collective-permute-done.refs_0_.inner_ref.outer_ref, ...), custom_call_target="tpu_custom_call" | custom-call | flops 1024 | bytes 1024 | tf_op jit(solution)/shard_map/pallas_call | solution.py:346
  81.1 4.0 %shard_map.102 = (f32[384,1024]{1,0:T(8,128)S(1)}, bf16[384,1024]{1,0:T(8,128)(2,1)S(1)}, f32[8,128]{1,0:T(8,128)}) custom-call(s32[9]{0:T(128)S(1)} %fusion.plan_ref, bf16[400,1024]{1,0:T(8,128)(2,1)} %collective-permute-done.3.refs_0_.inner_ref, bf16[400,1024]{1,0:T(8,128)(2,1)} %shard_map.95.refs_1_.outer_ref, ...), custom_call_target="tpu_custom_call" | custom-call | flops 1024 | bytes 1024 | tf_op jit(solution)/shard_map/pallas_call | solution.py:287
  87.6 2.6 %shard_map.103 = (f32[768,512]{1,0:T(8,128)S(1)}, f32[8,128]{1,0:T(8,128)}) custom-call(s32[9]{0:T(128)S(1)} %fusion.plan_ref, f32[384,1024]{1,0:T(8,128)S(1)} %get-tuple-element.40.sums_ref, bf16[384,1024]{1,0:T(8,128)(2,1)S(1)} %collective-permute-done.17.got_ref, bf16[400,1024]{1,0:T(8,128)(2,1)} %collective-permute-done.3.refs_0_.inner_ref, ...), custom_call_target="tpu_custom_call" | custom-call | flops 1024 | bytes 1024 | tf_op jit(solution)/shard_map/pallas_call | solution.py:346
  90.3 2.6 %shard_map.104 = (bf16[192,1024]{1,0:T(8,128)(2,1)S(1)}, f32[192,1024]{1,0:T(8,128)S(1)}, bf16[576,512]{1,0:T(8,128)(2,1)S(1)}) custom-call(s32[9]{0:T(128)S(1)} %fusion.plan_ref, f32[384,1024]{1,0:T(8,128)S(1)} %get-tuple-element.38.sums_ref, bf16[384,1024]{1,0:T(8,128)(2,1)S(1)} %collective-permute-done.16.got_ref, ...), custom_call_target="tpu_custom_call" | custom-call | flops 1024 | bytes 1024 | tf_op jit(solution)/shard_map/pallas_call | solution.py:380
  98.5 6.4 %collective-permute-done.20 = bf16[192,1024]{1,0:T(8,128)(2,1)S(1)} collective-permute-done((bf16[192,1024]{1,0:T(8,128)(2,1)S(1)}, bf16[192,1024]{1,0:T(8,128)(2,1)S(1)}, u32[]{:S(2)}, u32[]{:S(2)}) %collective-permute-start.20) | collective-permute-done | bytes 393248 | tf_op jit(solution)/shard_map/ppermute | solution.py:107
  104.9 5.2 %collective-permute-start.24 = (bf16[192,1024]{1,0:T(8,128)(2,1)S(1)}, bf16[192,1024]{1,0:T(8,128)(2,1)S(1)}, u32[]{:S(2)}, u32[]{:S(2)}) collective-permute-start(bf16[192,1024]{1,0:T(8,128)(2,1)S(1)} %add_convert_fusion.4), channel_id=1, source_target_pairs={{0,4},{12,8},{1,5},{13,9},{2,6},{14,10},{3,7},{15,11},{16,20},{28,... | collective-permute-start | bytes 1179656 | tf_op jit(solution)/shard_map/ppermute | solution.py:115
  110.8 2.5 %collective-permute-done.26 = bf16[192,1024]{1,0:T(8,128)(2,1)S(1)} collective-permute-done((bf16[192,1024]{1,0:T(8,128)(2,1)S(1)}, bf16[192,1024]{1,0:T(8,128)(2,1)S(1)}, u32[]{:S(2)}, u32[]{:S(2)}) %collective-permute-start.26) | collective-permute-done | bytes 393248 | tf_op jit(solution)/shard_map/ppermute | solution.py:107
  113.4 3.3 %collective-permute-start.27 = (bf16[192,1024]{1,0:T(8,128)(2,1)S(1)}, bf16[192,1024]{1,0:T(8,128)(2,1)}, u32[]{:S(2)}, u32[]{:S(2)}) collective-permute-start(bf16[192,1024]{1,0:T(8,128)(2,1)S(1)} %add_convert_fusion.1), channel_id=1, source_target_pairs={{0,4},{4,0},{8,12},{12,8},{1,5},{5,1},{9,13},{13,9},{2,6},{6,2},{1... | collective-permute-start | bytes 1179656 | tf_op jit(solution)/shard_map/ppermute | solution.py:115
  116.7 5.0 %collective-permute-done.22 = bf16[192,1024]{1,0:T(8,128)(2,1)S(1)} collective-permute-done((bf16[192,1024]{1,0:T(8,128)(2,1)S(1)}, bf16[192,1024]{1,0:T(8,128)(2,1)S(1)}, u32[]{:S(2)}, u32[]{:S(2)}) %collective-permute-start.22) | collective-permute-done | bytes 393248 | tf_op jit(solution)/shard_map/ppermute | solution.py:107
  121.8 6.2 %collective-permute-start.23 = (bf16[192,1024]{1,0:T(8,128)(2,1)S(1)}, bf16[192,1024]{1,0:T(8,128)(2,1)S(1)}, u32[]{:S(2)}, u32[]{:S(2)}) collective-permute-start(bf16[192,1024]{1,0:T(8,128)(2,1)S(1)} %add_convert_fusion.3), channel_id=1, source_target_pairs={{0,8},{12,4},{1,9},{13,5},{2,10},{14,6},{3,11},{15,7},{16,24},{28,... | collective-permute-start | bytes 1179656 | tf_op jit(solution)/shard_map/ppermute | solution.py:115
  130.9 4.7 %collective-permute-done.23 = bf16[192,1024]{1,0:T(8,128)(2,1)S(1)} collective-permute-done((bf16[192,1024]{1,0:T(8,128)(2,1)S(1)}, bf16[192,1024]{1,0:T(8,128)(2,1)S(1)}, u32[]{:S(2)}, u32[]{:S(2)}) %collective-permute-start.23) | collective-permute-done | bytes 393248 | tf_op jit(solution)/shard_map/ppermute | solution.py:115
  135.6 10.2 %collective-permute-done.25 = bf16[192,1024]{1,0:T(8,128)(2,1)S(1)} collective-permute-done((bf16[192,1024]{1,0:T(8,128)(2,1)}, bf16[192,1024]{1,0:T(8,128)(2,1)S(1)}, u32[]{:S(2)}, u32[]{:S(2)}) %collective-permute-start.25) | collective-permute-done | bytes 393248 | tf_op jit(solution)/shard_map/ppermute | solution.py:115
  (110 shorter events, 44.7 us)
Async XLA Ops:
  4.5 21.4 %collective-permute-start = (bf16[400,1024]{1,0:T(8,128)(2,1)S(1)}, bf16[400,1024]{1,0:T(8,128)(2,1)}, u32[]{:S(2)}, u32[]{:S(2)}) collective-permute-start(bf16[400,1024]{1,0:T(8,128)(2,1)S(1)} %shard_map.91.refs_1_.inner_ref.outer_ref), channel_id=1, source_target_pairs={{0,4},{4,0},{8,12},{12,8},{1,5},{5,1},{9,13},{13,9},{2,6},{6,2},{1... | collective-permute-start | bytes 2457608 | tf_op jit(solution)/shard_map/ppermute | solution.py:115
  7.6 21.6 %collective-permute-start.3 = (bf16[400,1024]{1,0:T(8,128)(2,1)S(1)}, bf16[400,1024]{1,0:T(8,128)(2,1)}, u32[]{:S(2)}, u32[]{:S(2)}) collective-permute-start(bf16[400,1024]{1,0:T(8,128)(2,1)S(1)} %shard_map.91.refs_1_.inner_ref.outer_ref), channel_id=1, source_target_pairs={{4,8},{8,4},{5,9},{9,5},{6,10},{10,6},{7,11},{11,7},{20,24},{24,20... | collective-permute-start | bytes 2457608 | tf_op jit(solution)/shard_map/ppermute | solution.py:115
  9.2 21.3 %collective-permute-start.7 = (bf16[384,1024]{1,0:T(8,128)(2,1)}, bf16[384,1024]{1,0:T(8,128)(2,1)}, u32[]{:S(2)}, u32[]{:S(2)}) collective-permute-start(bf16[384,1024]{1,0:T(8,128)(2,1)} %refs_0_.1), channel_id=1, source_target_pairs={{0,2},{1,3},{2,0},{3,1},{4,6},{5,7},{6,4},{7,5},{8,10},{9,11},{10,... | collective-permute-start | bytes 2359304 | tf_op jit(solution)/shard_map/ppermute | solution.py:107
  15.8 25.1 %collective-permute-start.9 = (bf16[2048,512]{1,0:T(8,128)(2,1)}, bf16[2048,512]{1,0:T(8,128)(2,1)S(1)}, u32[]{:S(2)}, u32[]{:S(2)}) collective-permute-start(bf16[2048,512]{1,0:T(8,128)(2,1)} %shard_map.93), channel_id=1, source_target_pairs={{0,1},{1,0},{2,3},{3,2},{4,5},{5,4},{6,7},{7,6},{8,9},{9,8},{10,11... | collective-permute-start | bytes 6291464 | tf_op jit(solution)/shard_map/ppermute | solution.py:111
  26.0 13.4 %collective-permute-start.1 = (bf16[400,1024]{1,0:T(8,128)(2,1)}, bf16[400,1024]{1,0:T(8,128)(2,1)}, u32[]{:S(2)}, u32[]{:S(2)}) collective-permute-start(bf16[400,1024]{1,0:T(8,128)(2,1)} %collective-permute-done.refs_0_.inner_ref.outer_ref), channel_id=1, source_target_pairs={{4,8},{8,4},{5,9},{9,5},{6,10},{10,6},{7,11},{11,7},{20,24},{24,20... | collective-permute-start | bytes 2457608 | tf_op jit(solution)/shard_map/ppermute | solution.py:115
  27.6 20.5 %collective-permute-start.6 = (bf16[400,1024]{1,0:T(8,128)(2,1)}, bf16[400,1024]{1,0:T(8,128)(2,1)}, u32[]{:S(2)}, u32[]{:S(2)}) collective-permute-start(bf16[400,1024]{1,0:T(8,128)(2,1)} %collective-permute-done.refs_0_.inner_ref.outer_ref), channel_id=1, source_target_pairs={{0,2},{1,3},{2,0},{3,1},{4,6},{5,7},{6,4},{7,5},{8,10},{9,11},{10,... | collective-permute-start | bytes 2457608 | tf_op jit(solution)/shard_map/ppermute | solution.py:107
  29.2 21.9 %collective-permute-start.5 = (bf16[400,1024]{1,0:T(8,128)(2,1)}, bf16[400,1024]{1,0:T(8,128)(2,1)}, u32[]{:S(2)}, u32[]{:S(2)}) collective-permute-start(bf16[400,1024]{1,0:T(8,128)(2,1)} %collective-permute-done.3.refs_0_.inner_ref), channel_id=1, source_target_pairs={{4,0},{8,12},{5,1},{9,13},{6,2},{10,14},{7,3},{11,15},{20,16},{24,... | collective-permute-start | bytes 2457608 | tf_op jit(solution)/shard_map/ppermute | solution.py:115
  32.5 15.6 %collective-permute-start.8 = (bf16[192,1024]{1,0:T(8,128)(2,1)S(1)}, bf16[192,1024]{1,0:T(8,128)(2,1)S(1)}, u32[]{:S(2)}, u32[]{:S(2)}) collective-permute-start(bf16[192,1024]{1,0:T(8,128)(2,1)S(1)} %shard_map.92), channel_id=1, source_target_pairs={{0,4},{12,8},{1,5},{13,9},{2,6},{14,10},{3,7},{15,11},{16,20},{28,... | collective-permute-start | bytes 1179656 | tf_op jit(solution)/shard_map/ppermute | solution.py:115
  39.4 20.0 %collective-permute-start.4 = (bf16[400,1024]{1,0:T(8,128)(2,1)}, bf16[400,1024]{1,0:T(8,128)(2,1)}, u32[]{:S(2)}, u32[]{:S(2)}) collective-permute-start(bf16[400,1024]{1,0:T(8,128)(2,1)} %collective-permute-done.3.refs_0_.inner_ref), channel_id=1, source_target_pairs={{4,6},{5,7},{6,4},{7,5},{8,10},{9,11},{10,8},{11,9},{20,22},{21,23... | collective-permute-start | bytes 2457608 | tf_op jit(solution)/shard_map/ppermute | solution.py:424
  40.9 29.3 %collective-permute-start.2 = (bf16[400,1024]{1,0:T(8,128)(2,1)}, bf16[400,1024]{1,0:T(8,128)(2,1)}, u32[]{:S(2)}, u32[]{:S(2)}) collective-permute-start(bf16[400,1024]{1,0:T(8,128)(2,1)} %collective-permute-done.1.refs_2_.inner_ref.refs_0_), channel_id=1, source_target_pairs={{4,0},{8,12},{5,1},{9,13},{6,2},{10,14},{7,3},{11,15},{20,16},{24,... | collective-permute-start | bytes 2457608 | tf_op jit(solution)/shard_map/ppermute | solution.py:115
  51.2 20.0 %collective-permute-start.10 = (bf16[400,1024]{1,0:T(8,128)(2,1)}, bf16[400,1024]{1,0:T(8,128)(2,1)S(1)}, u32[]{:S(2)}, u32[]{:S(2)}) collective-permute-start(bf16[400,1024]{1,0:T(8,128)(2,1)} %shard_map.95.refs_1_.outer_ref), channel_id=1, source_target_pairs={{0,2},{1,3},{2,0},{3,1},{12,14},{13,15},{14,12},{15,13},{16,18},{1... | collective-permute-start | bytes 2457608 | tf_op jit(solution)/shard_map/ppermute | solution.py:424
  54.3 22.5 %collective-permute-start.15 = (bf16[384,1024]{1,0:T(8,128)(2,1)}, bf16[384,1024]{1,0:T(8,128)(2,1)S(1)}, u32[]{:S(2)}, u32[]{:S(2)}) collective-permute-start(bf16[384,1024]{1,0:T(8,128)(2,1)} %copy-done.15), channel_id=1, source_target_pairs={{0,1},{1,0},{2,3},{3,2},{4,5},{5,4},{6,7},{7,6},{8,9},{9,8},{10,11... | collective-permute-start | bytes 2359304 | tf_op jit(solution)/shard_map/ppermute | solution.py:111
  58.8 20.0 %collective-permute-start.14 = (bf16[384,1024]{1,0:T(8,128)(2,1)S(1)}, bf16[384,1024]{1,0:T(8,128)(2,1)S(1)}, u32[]{:S(2)}, u32[]{:S(2)}) collective-permute-start(bf16[384,1024]{1,0:T(8,128)(2,1)S(1)} %get-tuple-element.33), channel_id=1, source_target_pairs={{0,1},{1,0},{2,3},{3,2},{4,5},{5,4},{6,7},{7,6},{8,9},{9,8},{10,11... | collective-permute-start | bytes 2359304 | tf_op jit(solution)/shard_map/ppermute | solution.py:111
  59.4 26.0 %collective-permute-start.13 = (bf16[192,1024]{1,0:T(8,128)(2,1)S(1)}, bf16[192,1024]{1,0:T(8,128)(2,1)S(1)}, u32[]{:S(2)}, u32[]{:S(2)}) collective-permute-start(bf16[192,1024]{1,0:T(8,128)(2,1)S(1)} %collective-permute-done.11.rest_2_.refs_1_), channel_id=1, source_target_pairs={{4,0},{8,12},{5,1},{9,13},{6,2},{10,14},{7,3},{11,15},{20,16},{24,... | collective-permute-start | bytes 1179656 | tf_op jit(solution)/shard_map/ppermute | solution.py:115
  73.2 12.3 %collective-permute-start.12 = (bf16[192,1024]{1,0:T(8,128)(2,1)S(1)}, bf16[192,1024]{1,0:T(8,128)(2,1)S(1)}, u32[]{:S(2)}, u32[]{:S(2)}) collective-permute-start(bf16[192,1024]{1,0:T(8,128)(2,1)S(1)} %shard_map.97), channel_id=1, source_target_pairs={{0,2},{1,3},{2,0},{3,1},{4,6},{5,7},{6,4},{7,5},{8,10},{9,11},{10,... | collective-permute-start | bytes 1179656 | tf_op jit(solution)/shard_map/ppermute | solution.py:107
  73.8 16.5 %collective-permute-start.18 = (bf16[256,2048]{1,0:T(8,128)(2,1)S(1)}, bf16[256,2048]{1,0:T(8,128)(2,1)S(1)}, u32[]{:S(2)}, u32[]{:S(2)}) collective-permute-start(bf16[256,2048]{1,0:T(8,128)(2,1)S(1)} %copy-done.6), channel_id=1, source_target_pairs={{0,1},{1,0},{2,3},{3,2},{4,5},{5,4},{6,7},{7,6},{8,9},{9,8},{10,11... | collective-permute-start | bytes 3145736 | tf_op jit(solution)/shard_map/ppermute | solution.py:111
  95.7 17.5 %collective-permute-start.26 = (bf16[192,1024]{1,0:T(8,128)(2,1)S(1)}, bf16[192,1024]{1,0:T(8,128)(2,1)S(1)}, u32[]{:S(2)}, u32[]{:S(2)}) collective-permute-start(bf16[192,1024]{1,0:T(8,128)(2,1)S(1)} %get-tuple-element.52), channel_id=1, source_target_pairs={{0,2},{1,3},{2,0},{3,1},{4,6},{5,7},{6,4},{7,5},{8,10},{9,11},{10,... | collective-permute-start | bytes 1179656 | tf_op jit(solution)/shard_map/ppermute | solution.py:107
  96.4 25.3 %collective-permute-start.22 = (bf16[192,1024]{1,0:T(8,128)(2,1)S(1)}, bf16[192,1024]{1,0:T(8,128)(2,1)S(1)}, u32[]{:S(2)}, u32[]{:S(2)}) collective-permute-start(bf16[192,1024]{1,0:T(8,128)(2,1)S(1)} %get-tuple-element.50), channel_id=1, source_target_pairs={{0,2},{1,3},{2,0},{3,1},{4,6},{5,7},{6,4},{7,5},{8,10},{9,11},{10,... | collective-permute-start | bytes 1179656 | tf_op jit(solution)/shard_map/ppermute | solution.py:107
  97.8 33.1 %collective-permute-start.19 = (bf16[192,1024]{1,0:T(8,128)(2,1)S(1)}, bf16[192,1024]{1,0:T(8,128)(2,1)S(1)}, u32[]{:S(2)}, u32[]{:S(2)}) collective-permute-start(bf16[192,1024]{1,0:T(8,128)(2,1)S(1)} %get-tuple-element.46), channel_id=1, source_target_pairs={{0,2},{1,3},{2,0},{3,1},{4,6},{5,7},{6,4},{7,5},{8,10},{9,11},{10,... | collective-permute-start | bytes 1179656 | tf_op jit(solution)/shard_map/ppermute | solution.py:107
  104.9 23.1 %collective-permute-start.24 = (bf16[192,1024]{1,0:T(8,128)(2,1)S(1)}, bf16[192,1024]{1,0:T(8,128)(2,1)S(1)}, u32[]{:S(2)}, u32[]{:S(2)}) collective-permute-start(bf16[192,1024]{1,0:T(8,128)(2,1)S(1)} %add_convert_fusion.4), channel_id=1, source_target_pairs={{0,4},{12,8},{1,5},{13,9},{2,6},{14,10},{3,7},{15,11},{16,20},{28,... | collective-permute-start | bytes 1179656 | tf_op jit(solution)/shard_map/ppermute | solution.py:115
  110.1 20.1 %collective-permute-start.21 = (bf16[192,1024]{1,0:T(8,128)(2,1)S(1)}, bf16[192,1024]{1,0:T(8,128)(2,1)S(1)}, u32[]{:S(2)}, u32[]{:S(2)}) collective-permute-start(bf16[192,1024]{1,0:T(8,128)(2,1)S(1)} %add_convert_fusion.4), channel_id=1, source_target_pairs={{4,8},{8,4},{5,9},{9,5},{6,10},{10,6},{7,11},{11,7},{20,24},{24,20... | collective-permute-start | bytes 1179656 | tf_op jit(solution)/shard_map/ppermute | solution.py:115
  113.4 33.8 %collective-permute-start.27 = (bf16[192,1024]{1,0:T(8,128)(2,1)S(1)}, bf16[192,1024]{1,0:T(8,128)(2,1)}, u32[]{:S(2)}, u32[]{:S(2)}) collective-permute-start(bf16[192,1024]{1,0:T(8,128)(2,1)S(1)} %add_convert_fusion.1), channel_id=1, source_target_pairs={{0,4},{4,0},{8,12},{12,8},{1,5},{5,1},{9,13},{13,9},{2,6},{6,2},{1... | collective-permute-start | bytes 1179656 | tf_op jit(solution)/shard_map/ppermute | solution.py:115
  121.8 13.9 %collective-permute-start.23 = (bf16[192,1024]{1,0:T(8,128)(2,1)S(1)}, bf16[192,1024]{1,0:T(8,128)(2,1)S(1)}, u32[]{:S(2)}, u32[]{:S(2)}) collective-permute-start(bf16[192,1024]{1,0:T(8,128)(2,1)S(1)} %add_convert_fusion.3), channel_id=1, source_target_pairs={{0,8},{12,4},{1,9},{13,5},{2,10},{14,6},{3,11},{15,7},{16,24},{28,... | collective-permute-start | bytes 1179656 | tf_op jit(solution)/shard_map/ppermute | solution.py:115
  128.9 17.0 %collective-permute-start.25 = (bf16[192,1024]{1,0:T(8,128)(2,1)}, bf16[192,1024]{1,0:T(8,128)(2,1)S(1)}, u32[]{:S(2)}, u32[]{:S(2)}) collective-permute-start(bf16[192,1024]{1,0:T(8,128)(2,1)} %add_convert_fusion.2), channel_id=1, source_target_pairs={{4,12},{8,0},{5,13},{9,1},{6,14},{10,2},{7,15},{11,3},{20,28},{24,... | collective-permute-start | bytes 1179656 | tf_op jit(solution)/shard_map/ppermute | solution.py:115
  (28 other events, 152.0 us)

commit v19 on v18

--- a/solution.py
+++ b/solution.py
@@ -287,7 +287,7 @@
     return on_core(body, shapes + [TOKEN], specs)(*operands, *waits)
 
 
-def collected_rows(owned, slot, plan, sums, got, facts, before):
+def hidden_rows(sums, got):
     units = sums.shape[1] // 4
     hidden = []
     for core in range(2):
@@ -296,25 +296,31 @@
         up = sums[:, here + units : here + 2 * units]
         up = up + got[:, there + units : there + 2 * units].astype(jnp.float32)
         hidden.append((gate / (1.0 + jnp.exp(-gate)) * up).astype(jnp.bfloat16))
-    hidden = jnp.concatenate(hidden, axis=1)
-    values = facts[:, : sums.shape[0]].astype(jnp.float32)
+    return jnp.concatenate(hidden, axis=1)
+
+
+def hide(sums, got):
+    def body(sums_ref, got_ref, out_ref, token_ref):
+        out_ref[...] = hidden_rows(sums_ref, got_ref)
+        token_ref[...] = jnp.zeros(TOKEN.shape, TOKEN.dtype)
+
+    shape = jax.ShapeDtypeStruct((sums.shape[0], sums.shape[1] // 2), jnp.bfloat16)
+    return on_core(body, [shape, TOKEN], [VMEM, VMEM])(sums, got)
+
+
+def factors_of(slot, plan, facts, rows):
+    values = facts[:, :rows].astype(jnp.float32)
     kind = lax.broadcasted_iota(jnp.int32, (FACT_ROWS, 1), 0)
     mine = kind == plan[OFFSETS_AT + slot]
     factor = jnp.sum(jnp.where(mine, values, 0.0), axis=0, keepdims=True)
-    owner = (values[4:5, :] * 256.0 + values[5:6, :]).astype(jnp.int32)
-    results = []
-    for index in range(4):
-        token = plan[index] * owned + lax.broadcasted_iota(jnp.int32, (owned, 1), 0)
-        placing = jnp.where(owner == token, factor, 0.0).astype(jnp.bfloat16)
-        rows = jnp.dot(placing, hidden, preferred_element_type=jnp.float32)
-        if before is not None:
-            rows = rows + before[index * owned : (index + 1) * owned, :]
-        results.append(rows)
-    return results
-
-
-def fact_scratch(width):
-    return [pltpu.VMEM((FACT_ROWS, width), jnp.bfloat16), pltpu.SemaphoreType.DMA((1,))]
+    return factor, values[4:5, :] * 256.0 + values[5:6, :]
+
+
+def chunk_rows(owned, index, plan, factor, owner, hidden):
+    first = (plan[index] * owned).astype(jnp.float32)
+    token = first + lax.broadcasted_iota(jnp.int32, (owned, 1), 0).astype(jnp.float32)
+    placing = jnp.where(owner == token, factor, 0.0).astype(jnp.bfloat16)
+    return jnp.dot(placing, hidden, preferred_element_type=jnp.float32).astype(jnp.bfloat16)
 
 
 def facts_of(plan_ref, inner_ref, outer_ref, buffer, sem):
@@ -327,23 +333,6 @@
 
     by_kind(plan_ref, (inner_ref, outer_ref), run)
     return buffer
-
-
-def collect(owned, slot, plan, sums, got, facts, before):
-    operands = [plan, sums, got, *facts] + ([] if before is None else [before])
-
-    def body(plan_ref, sums_ref, got_ref, inner_ref, outer_ref, *rest):
-        before_ref = rest[0] if before is not None else None
-        out_ref, token_ref, buffer, sem = rest[-4:]
-        facts_here = facts_of(plan_ref, inner_ref, outer_ref, buffer, sem)
-        rows = collected_rows(owned, slot, plan_ref, sums_ref, got_ref, facts_here, before_ref)
-        for index in range(4):
-            out_ref[index * owned : (index + 1) * owned, :] = rows[index]
-        token_ref[...] = jnp.zeros(TOKEN.shape, TOKEN.dtype)
-
-    shape = jax.ShapeDtypeStruct((4 * owned, sums.shape[1] // 2), jnp.float32)
-    specs = [SMEM, VMEM, VMEM, ANYWHERE, ANYWHERE] + [VMEM] * (len(operands) - 5)
-    return on_core(body, [shape, TOKEN], specs, fact_scratch(facts[0].shape[1]))(*operands)
 
 
 def down(held, own_ref, lent_ref, sent_ref, kept_ref):
@@ -354,33 +343,53 @@
         out[...] = result.astype(out.dtype)
 
 
-def finish(owned, slot, plan, sums, got, facts, before, down_own, down_lent):
-    units = down_own.shape[0]
+def finish(owned, plan, hidden, sums, got, facts, down_own, down_lent):
+    rows, units = hidden[0].shape
     width = down_own.shape[1] // 2
+    slots = len(facts)
     pair = [
         jax.ShapeDtypeStruct((owned, width), jnp.bfloat16),
         jax.ShapeDtypeStruct((owned, width), jnp.float32),
     ]
 
-    def first(plan_ref, sums_ref, got_ref, inner_ref, outer_ref, before_ref, *refs):
-        own_ref, lent_ref, sent_ref, kept_ref, held_ref, buffer, sem = refs
-        facts_here = facts_of(plan_ref, inner_ref, outer_ref, buffer, sem)
-        rows = collected_rows(owned, slot, plan_ref, sums_ref, got_ref, facts_here, before_ref)
-        down(rows[0].astype(jnp.bfloat16), own_ref, lent_ref, sent_ref, kept_ref)
+    def first(plan_ref, *refs):
+        hidden_refs, refs = refs[:2], refs[2:]
+        sums_refs, got_refs, refs = refs[:2], refs[2:4], refs[4:]
+        fact_refs, refs = refs[: 2 * slots], refs[2 * slots :]
+        own_ref, lent_ref, sent_ref, kept_ref, all_ref, by_row_ref, buffer, sem = refs
+        for slot in range(slots):
+            facts_of(plan_ref, *fact_refs[2 * slot : 2 * slot + 2], buffer, sem)
+            factor, owner = factors_of(slot, plan_ref, buffer, rows)
+            by_row_ref[0:1, slot * rows : (slot + 1) * rows] = factor
+            by_row_ref[1:2, slot * rows : (slot + 1) * rows] = owner
+        for slot in range(2):
+            all_ref[slot * rows : (slot + 1) * rows, :] = hidden_refs[slot][...]
+            made = hidden_rows(sums_refs[slot], got_refs[slot])
+            all_ref[(slot + 2) * rows : (slot + 3) * rows, :] = made
+        factor, owner = by_row_ref[0:1, :], by_row_ref[1:2, :]
+        held = chunk_rows(owned, 0, plan_ref, factor, owner, all_ref[...])
+        down(held, own_ref, lent_ref, sent_ref, kept_ref)
+
+    def others(plan_ref, all_ref, by_row_ref, own_ref, lent_ref, *refs):
+        factor, owner = by_row_ref[0:1, :], by_row_ref[1:2, :]
         for index in range(1, 4):
-            held_ref[(index - 1) * owned : index * owned, :] = rows[index].astype(jnp.bfloat16)
-
-    def others(held_ref, own_ref, lent_ref, *refs):
-        for index in range(3):
-            held = held_ref[index * owned : (index + 1) * owned, :]
-            down(held, own_ref, lent_ref, refs[2 * index], refs[2 * index + 1])
-
-    held_shape = jax.ShapeDtypeStruct((3 * owned, 2 * units), jnp.bfloat16)
-    specs = [SMEM, VMEM, VMEM, ANYWHERE, ANYWHERE] + [VMEM] * 3
-    sent, kept, held = on_core(
-        first, pair + [held_shape], specs, fact_scratch(facts[0].shape[1])
-    )(plan, sums, got, *facts, before, down_own, down_lent)
-    rest = on_core(others, pair * 3, [VMEM] * 3)(held, down_own, down_lent)
+            held = chunk_rows(owned, index, plan_ref, factor, owner, all_ref[...])
+            down(held, own_ref, lent_ref, refs[2 * index - 2], refs[2 * index - 1])
+
+    all_shape = jax.ShapeDtypeStruct((slots * rows, units), jnp.bfloat16)
+    by_row_shape = jax.ShapeDtypeStruct((2, slots * rows), jnp.float32)
+    scratch = [
+        pltpu.VMEM((FACT_ROWS, facts[0][0].shape[1]), jnp.bfloat16),
+        pltpu.SemaphoreType.DMA((1,)),
+    ]
+    fact_blocks = [block for pair_of in facts for block in pair_of]
+    specs = [SMEM] + [VMEM] * 6 + [ANYWHERE] * len(fact_blocks) + [VMEM] * 2
+    sent, kept, every, by_row = on_core(
+        first, pair + [all_shape, by_row_shape], specs, scratch
+    )(plan, *hidden, *sums, *got, *fact_blocks, down_own, down_lent)
+    rest = on_core(others, pair * 3, [SMEM] + [VMEM] * 4)(
+        plan, every, by_row, down_own, down_lent
+    )
     return [sent, *rest[0::2]], [kept, *rest[1::2]]
 
 
@@ -453,8 +462,8 @@
         part_of(plan, *last, 0, half, *second_far, middle_far, ready_0, ready_1)
     )
     outward_far = along(middle_far, OUTWARD)
-    total, _ = collect(owned, 0, plan, sums_0, got_0, (own, own), None)
-    total, collected_1 = collect(owned, 1, plan, sums_1, got_1, (beside, beside), total)
+    hidden_0, hidden_here = hide(sums_0, got_0)
+    hidden_1, hidden_there = hide(sums_1, got_1)
     sums_2, send_2, _ = partial_sums(plan, whole, [(second, second_far)], weights, (0, 1))
     got_2 = across_cores(send_2)
     near, _ = partial_sums(plan, whole, [(last,)], weights, (0,), send=False)
@@ -465,17 +474,25 @@
         weights,
         (1,),
         before=near,
-        waits=[collected_1],
+        waits=[hidden_here, hidden_there],
     )
     got_3 = across_cores(send_3)
-    total, _ = collect(owned, 2, plan, sums_2, got_2, second, total)
-    sent, kept = finish(owned, 3, plan, sums_3, got_3, last, total, kept_down, lent_down)
+    sent, kept = finish(
+        owned,
+        plan,
+        (hidden_0, hidden_1),
+        (sums_2, sums_3),
+        (got_2, got_3),
+        [(own, own), (beside, beside), second, last],
+        kept_down,
+        lent_down,
+    )
 
     joined = [k + across_chips(s).astype(jnp.float32) for s, k in zip(sent, kept)]
     first, second, third = [block.astype(jnp.bfloat16) for block in joined[:3]]
     second = lax.optimization_barrier(second)
     inward = along(first, INWARD)
-    middle = after(along(first, MIDDLE), flops=8 * 2**30)
+    middle = along(first, MIDDLE)
     two_in = along(second, TWO_IN)
     passed = second.astype(jnp.float32) + inward.astype(jnp.float32)
     two_out = along(passed.astype(jnp.bfloat16), TWO_OUT)

time: 150 us -> 150 us (level)
  waiting for transfers between devices: 49 us -> 52.5 us
  other arithmetic: 6.08 us -> 3.34 us
  Pallas kernels: 31.9 us -> 29.4 us
  starting transfers between devices: 47 us -> 48.6 us
    pallas_call x5 -> x4, Pallas kernels: 10.8 us -> 8.34 us  [the longest x1 4.58 us: finish(): on_core(first, pair + [all_shape, by_row_shape], specs, scratch)]
    ppermute x6, waiting for transfers between devices: 0.02 us -> 2.17 us  [across_cores(): return lax.ppermute(block, 'tp', [(i, i ^ 1) for i in range(4)])]
    ppermute x13, starting transfers between devices: 33.9 us -> 35.5 us  [along(): return lax.ppermute(block, 'blk', route)]
    unnamed x48 -> x46, local copies, waits for them, and re-layouts: 7.39 us -> 7.21 us
  transfers between devices with their start and end apart: 28 -> 28, of which waited for: 9 -> 10; matrix products, arithmetic and copies ran while one was open for 8% -> 6% of each run, Pallas kernels for 18% -> 15%
where the time goes in v19:
time: 150 us; the launch traced here: 149 us
  waiting for transfers between devices  52.5 us (35%)
  starting transfers between devices  48.6 us (32%)
  Pallas kernels  29.4 us (20%)
  local copies, waits for them, and re-layouts  14.3 us (10%)
  other arithmetic  3.34 us (2%)
    ppermute x13, starting transfers between devices, along(): return lax.ppermute(block, 'blk', route)  35.5 us
    ppermute x13, waiting for transfers between devices, along(): return lax.ppermute(block, 'blk', route)  35 us
    pallas_call x5, Pallas kernels, partial_sums(): return on_core(body, shapes + [TOKEN], specs)(*operands, *waits)  15.2 us
    ppermute x7, waiting for transfers between devices, across_chips(): return lax.ppermute(block, 'tp', [(i, i ^ 2) for i in range(4)])  14.4 us
    ppermute x7, starting transfers between devices, across_chips(): return lax.ppermute(block, 'tp', [(i, i ^ 2) for i in range(4)])  8.01 us
    unnamed x46, local copies, waits for them, and re-layouts  7.21 us
    pallas_call x1, Pallas kernels, finish(): on_core(first, pair + [all_shape, by_row_shape], specs, scratch)  4.58 us
    ppermute x2, starting transfers between devices, at_kind(): return lax.ppermute(block, ('blk', 'tp'), pairs)  4 us
  transfers between devices with their start and end apart: 28, of which 10 were waited for; matrix products, arithmetic and copies ran while one was open for 6% of the time, Pallas kernels for 15%

profile of v19, /device:TPU:0, one launch (start us, length us, event | category | flops | bytes accessed | tf_op | source)
XLA Modules:
  0.0 148.6 jit_solution(15489971923291964937)
XLA Ops:
  4.5 3.1 %collective-permute-start.3 = (bf16[400,1024]{1,0:T(8,128)(2,1)S(1)}, bf16[400,1024]{1,0:T(8,128)(2,1)}, u32[]{:S(2)}, u32[]{:S(2)}) collective-permute-start(bf16[400,1024]{1,0:T(8,128)(2,1)S(1)} %shard_map.91.refs_1_.refs_6_.refs_7_), channel_id=1, source_target_pairs={{0,4},{4,0},{8,12},{12,8},{1,5},{5,1},{9,13},{13,9},{2,6},{6,2},{1... | collective-permute-start | bytes 2457608 | tf_op jit(solution)/shard_map/ppermute | solution.py:115
  10.7 3.6 %dynamic-slice_bitcast_fusion.6 = (bf16[1024,256]{1,0:T(8,128)(2,1)S(1)}, bf16[1024,256]{1,0:T(8,128)(2,1)S(1)}, bf16[1024,256]{1,0:T(8,128)(2,1)}, bf16[1024,25...) fusion(bf16[4,1024,256]{2,1,0:T(8,128)(2,1)} %bitcast.32, ...), kind=kLoop, calls=%fused_computation.17 | loop fusion | bytes 8388624 | tf_op jit(solution)/shard_map/jit(dynamic_index_in_dim)/squeeze | solution.py:419
  16.5 2.8 %dynamic-slice_bitcast_fusion.1 = (bf16[256,1024]{1,0:T(8,128)(2,1)}, bf16[256,1024]{1,0:T(8,128)(2,1)S(1)}, bf16[256,1024]{1,0:T(8,128)(2,1)S(1)}, bf16[256,1024]{1,0:T(8,128)(2,1)}) fusion(bf16[1,256,4096]{2,1,0:T(8,128)(2,1)} %param.12, s32[]{:T(128)S(6)} %select_n.39, s32[]{:T(128)S(6)} %select_n.38, s32[]{:T(128)S(6)} %select_n.37, s32[]{:T(128)S(6)} %select_n.40), kind=kLoop, calls=%fused_computation.12 | loop fusion | bytes 4194320 | tf_op jit(solution)/shard_map/dynamic_slice | solution.py:425
  19.3 6.7 %collective-permute-done.3.refs_0_.refs_8_.refs_9_ = bf16[400,1024]{1,0:T(8,128)(2,1)} collective-permute-done((bf16[400,1024]{1,0:T(8,128)(2,1)S(1)}, bf16[400,1024]{1,0:T(8,128)(2,1)}, u32[]{:S(2)}, u32[]{:S(2)}) %collective-permute-start.3) | collective-permute-done | bytes 819232 | tf_op jit(solution)/shard_map/ppermute | solution.py:115
  32.5 6.4 %collective-permute-start.9 = (bf16[192,1024]{1,0:T(8,128)(2,1)S(1)}, bf16[192,1024]{1,0:T(8,128)(2,1)S(1)}, u32[]{:S(2)}, u32[]{:S(2)}) collective-permute-start(bf16[192,1024]{1,0:T(8,128)(2,1)S(1)} %shard_map.97), channel_id=1, source_target_pairs={{0,4},{12,8},{1,5},{13,9},{2,6},{14,10},{3,7},{15,11},{16,20},{28,... | collective-permute-start | bytes 1179656 | tf_op jit(solution)/shard_map/ppermute | solution.py:115
  42.2 3.2 %shard_map.93 = (f32[384,1024]{1,0:T(8,128)S(1)}, bf16[384,1024]{1,0:T(8,128)(2,1)S(1)}, f32[8,128]{1,0:T(8,128)S(1)}) custom-call(s32[9]{0:T(128)S(1)} %fusion.plan_ref, bf16[384,1024]{1,0:T(8,128)(2,1)} %refs_0_.1, bf16[384,1024]{1,0:T(8,128)(2,1)} %collective-permute-done.refs_1_.inner_ref.outer_ref, ...), custom_call_target="tpu_custom_call" | custom-call | flops 1024 | bytes 1024 | tf_op jit(solution)/shard_map/pallas_call | solution.py:287
  48.1 3.0 %collective-permute-done.7.refs_0_ = bf16[400,1024]{1,0:T(8,128)(2,1)} collective-permute-done((bf16[400,1024]{1,0:T(8,128)(2,1)}, bf16[400,1024]{1,0:T(8,128)(2,1)}, u32[]{:S(2)}, u32[]{:S(2)}) %collective-permute-start.7) | collective-permute-done | bytes 819232 | tf_op jit(solution)/shard_map/ppermute | solution.py:115
  51.1 2.4 %collective-permute-start.11 = (bf16[400,1024]{1,0:T(8,128)(2,1)}, bf16[400,1024]{1,0:T(8,128)(2,1)S(1)}, u32[]{:S(2)}, u32[]{:S(2)}) collective-permute-start(bf16[400,1024]{1,0:T(8,128)(2,1)} %shard_map.98.refs_1_.refs_11_), channel_id=1, source_target_pairs={{0,2},{1,3},{2,0},{3,1},{12,14},{13,15},{14,12},{15,13},{16,18},{1... | collective-permute-start | bytes 2457608 | tf_op jit(solution)/shard_map/ppermute | solution.py:433
  55.5 3.2 %shard_map.95 = (f32[384,1024]{1,0:T(8,128)S(1)}, bf16[384,1024]{1,0:T(8,128)(2,1)S(1)}, f32[8,128]{1,0:T(8,128)S(1)}) custom-call(s32[9]{0:T(128)S(1)} %fusion.plan_ref, bf16[400,1024]{1,0:T(8,128)(2,1)} %collective-permute-done.3.refs_0_.refs_8_.refs_9_, bf16[400,1024]{1,0:T(8,128)(2,1)} %collective-permute-done.4.refs_1_, ...), custom_call_target="tpu_custom_call" | custom-call | flops 1024 | bytes 1024 | tf_op jit(solution)/shard_map/pallas_call | solution.py:287
  60.6 9.5 %collective-permute-done.12.outer_ref.refs_1_.refs_13_ = bf16[400,1024]{1,0:T(8,128)(2,1)} collective-permute-done((bf16[400,1024]{1,0:T(8,128)(2,1)}, bf16[400,1024]{1,0:T(8,128)(2,1)}, u32[]{:S(2)}, u32[]{:S(2)}) %collective-permute-start.12) | collective-permute-done | bytes 819232 | tf_op jit(solution)/shard_map/ppermute | solution.py:115
  71.1 2.0 %shard_map.100 = bf16[192,1024]{1,0:T(8,128)(2,1)S(1)} custom-call(s32[9]{0:T(128)S(1)} %fusion.plan_ref, bf16[400,1024]{1,0:T(8,128)(2,1)} %collective-permute-done.8.refs_2_.inner_ref.refs_0_.refs_12_, bf16[400,1024]{1,0:T(8,128)(2,1)} %collective-permute-done.12.outer_ref.refs_1_.refs_13_, bf16[400,1024]{1,0:T(8,128)(2,1)} %collective-permute-done.10.refs_2_.rest_0_, ...), custom_call_target="tpu_custom_call" | custom-call | flops 1024 | bytes 1024 | tf_op jit(solution)/shard_map/pallas_call | solution.py:192
  73.8 2.9 %shard_map.101 = (f32[384,1024]{1,0:T(8,128)S(1)}, f32[8,128]{1,0:T(8,128)}) custom-call(s32[9]{0:T(128)S(1)} %fusion.plan_ref, bf16[400,1024]{1,0:T(8,128)(2,1)} %collective-permute-done.8.refs_2_.inner_ref.refs_0_.refs_12_, bf16[400,1024]{1,0:T(8,128)(2,1)} %collective-permute-done.12.outer_ref.refs_1_.refs_13_, ...), custom_call_target="tpu_custom_call" | custom-call | flops 1024 | bytes 1024 | tf_op jit(solution)/shard_map/pallas_call | solution.py:287
  77.9 4.0 %shard_map.99 = (f32[384,1024]{1,0:T(8,128)S(1)}, bf16[384,1024]{1,0:T(8,128)(2,1)S(1)}, f32[8,128]{1,0:T(8,128)}) custom-call(s32[9]{0:T(128)S(1)} %fusion.plan_ref, bf16[400,1024]{1,0:T(8,128)(2,1)} %collective-permute-done.6.refs_0_.refs_10_, bf16[400,1024]{1,0:T(8,128)(2,1)} %shard_map.98.refs_1_.refs_11_, ...), custom_call_target="tpu_custom_call" | custom-call | flops 1024 | bytes 1024 | tf_op jit(solution)/shard_map/pallas_call | solution.py:287
  83.9 2.0 %shard_map.102 = (f32[384,1024]{1,0:T(8,128)S(1)}, bf16[384,1024]{1,0:T(8,128)(2,1)S(1)}, f32[8,128]{1,0:T(8,128)}) custom-call(s32[9]{0:T(128)S(1)} %fusion.plan_ref, bf16[192,1024]{1,0:T(8,128)(2,1)S(1)} %collective-permute-done.14.refs_0_, bf16[192,1024]{1,0:T(8,128)(2,1)S(1)} %collective-permute-done.13.rest_2_.refs_1_, ...), custom_call_target="tpu_custom_call" | custom-call | flops 1024 | bytes 1024 | tf_op jit(solution)/shard_map/pallas_call | solution.py:287
  86.1 2.2 %collective-permute-done.17.refs_5_ = bf16[384,1024]{1,0:T(8,128)(2,1)S(1)} collective-permute-done((bf16[384,1024]{1,0:T(8,128)(2,1)S(1)}, bf16[384,1024]{1,0:T(8,128)(2,1)S(1)}, u32[]{:S(2)}, u32[]{:S(2)}) %collective-permute-start.17) | collective-permute-done | bytes 786464 | tf_op jit(solution)/shard_map/ppermute | solution.py:111
  88.2 4.6 %shard_map.103 = (bf16[192,1024]{1,0:T(8,128)(2,1)S(1)}, f32[192,1024]{1,0:T(8,128)S(1)}, bf16[1536,512]{1,0:T(8,128)(2,1)S(1)}, f32[2,1536]{1,0:T(2,128)S(1)}) custom-call(s32[9]{0:T(128)S(1)} %fusion.plan_ref, bf16[384,512]{1,0:T(8,128)(2,1)S(1)} %get-tuple-element.32.refs_0_, bf16[384,512]{1,0:T(8,128)(2,1)S(1)} %get-tuple-element.35.refs_1_, ...), custom_call_target="tpu_custom_call" | custom-call | flops 1024 | bytes 1024 | tf_op jit(solution)/shard_map/pallas_call | solution.py:387
  94.4 3.1 %shard_map.104 = (bf16[192,1024]{1,0:T(8,128)(2,1)S(1)}, f32[192,1024]{1,0:T(8,128)S(1)}, bf16[192,1024]{1,0:T(8,128)(2,1)S(1)}, f32[192,1024]{1,0:T(8,128)S(1)}...) custom-call(s32[9]{0:T(128)S(1)} %fusion.plan_ref, bf16[1536,512]{1,0:T(8,128)(2,1)S(1)} %get-tuple-element.45.all_ref, ...), custom_call_target="tpu_custom_call" | custom-call | flops 1024 | bytes 1024 | tf_op jit(solution)/shard_map/pallas_call | solution.py:390
  98.1 6.7 %collective-permute-done.20 = bf16[192,1024]{1,0:T(8,128)(2,1)S(1)} collective-permute-done((bf16[192,1024]{1,0:T(8,128)(2,1)S(1)}, bf16[192,1024]{1,0:T(8,128)(2,1)S(1)}, u32[]{:S(2)}, u32[]{:S(2)}) %collective-permute-start.20) | collective-permute-done | bytes 393248 | tf_op jit(solution)/shard_map/ppermute | solution.py:107
  104.9 5.8 %collective-permute-start.24 = (bf16[192,1024]{1,0:T(8,128)(2,1)S(1)}, bf16[192,1024]{1,0:T(8,128)(2,1)S(1)}, u32[]{:S(2)}, u32[]{:S(2)}) collective-permute-start(bf16[192,1024]{1,0:T(8,128)(2,1)S(1)} %add_convert_fusion.4), channel_id=1, source_target_pairs={{0,4},{12,8},{1,5},{13,9},{2,6},{14,10},{3,7},{15,11},{16,20},{28,... | collective-permute-start | bytes 1179656 | tf_op jit(solution)/shard_map/ppermute | solution.py:115
  113.6 6.6 %collective-permute-start.23 = (bf16[192,1024]{1,0:T(8,128)(2,1)S(1)}, bf16[192,1024]{1,0:T(8,128)(2,1)S(1)}, u32[]{:S(2)}, u32[]{:S(2)}) collective-permute-start(bf16[192,1024]{1,0:T(8,128)(2,1)S(1)} %add_convert_fusion.3), channel_id=1, source_target_pairs={{0,8},{12,4},{1,9},{13,5},{2,10},{14,6},{3,11},{15,7},{16,24},{28,... | collective-permute-start | bytes 1179656 | tf_op jit(solution)/shard_map/ppermute | solution.py:115
  121.6 7.7 %collective-permute-done.26 = bf16[192,1024]{1,0:T(8,128)(2,1)S(1)} collective-permute-done((bf16[192,1024]{1,0:T(8,128)(2,1)S(1)}, bf16[192,1024]{1,0:T(8,128)(2,1)S(1)}, u32[]{:S(2)}, u32[]{:S(2)}) %collective-permute-start.26) | collective-permute-done | bytes 393248 | tf_op jit(solution)/shard_map/ppermute | solution.py:107
  129.4 3.9 %collective-permute-start.27 = (bf16[192,1024]{1,0:T(8,128)(2,1)S(1)}, bf16[192,1024]{1,0:T(8,128)(2,1)S(1)}, u32[]{:S(2)}, u32[]{:S(2)}) collective-permute-start(bf16[192,1024]{1,0:T(8,128)(2,1)S(1)} %add_convert_fusion.1), channel_id=1, source_target_pairs={{0,4},{4,0},{8,12},{12,8},{1,5},{5,1},{9,13},{13,9},{2,6},{6,2},{1... | collective-permute-start | bytes 1179656 | tf_op jit(solution)/shard_map/ppermute | solution.py:115
  133.3 6.1 %collective-permute-done.25 = bf16[192,1024]{1,0:T(8,128)(2,1)S(1)} collective-permute-done((bf16[192,1024]{1,0:T(8,128)(2,1)S(1)}, bf16[192,1024]{1,0:T(8,128)(2,1)S(1)}, u32[]{:S(2)}, u32[]{:S(2)}) %collective-permute-start.25) | collective-permute-done | bytes 393248 | tf_op jit(solution)/shard_map/ppermute | solution.py:115
  139.7 8.0 %collective-permute-done.27 = bf16[192,1024]{1,0:T(8,128)(2,1)S(1)} collective-permute-done((bf16[192,1024]{1,0:T(8,128)(2,1)S(1)}, bf16[192,1024]{1,0:T(8,128)(2,1)S(1)}, u32[]{:S(2)}, u32[]{:S(2)}) %collective-permute-start.27) | collective-permute-done | bytes 393248 | tf_op jit(solution)/shard_map/ppermute | solution.py:115
  (106 shorter events, 38.6 us)
Async XLA Ops:
  4.5 21.4 %collective-permute-start.3 = (bf16[400,1024]{1,0:T(8,128)(2,1)S(1)}, bf16[400,1024]{1,0:T(8,128)(2,1)}, u32[]{:S(2)}, u32[]{:S(2)}) collective-permute-start(bf16[400,1024]{1,0:T(8,128)(2,1)S(1)} %shard_map.91.refs_1_.refs_6_.refs_7_), channel_id=1, source_target_pairs={{0,4},{4,0},{8,12},{12,8},{1,5},{5,1},{9,13},{13,9},{2,6},{6,2},{1... | collective-permute-start | bytes 2457608 | tf_op jit(solution)/shard_map/ppermute | solution.py:115
  7.6 21.6 %collective-permute-start.6 = (bf16[400,1024]{1,0:T(8,128)(2,1)S(1)}, bf16[400,1024]{1,0:T(8,128)(2,1)}, u32[]{:S(2)}, u32[]{:S(2)}) collective-permute-start(bf16[400,1024]{1,0:T(8,128)(2,1)S(1)} %shard_map.91.refs_1_.refs_6_.refs_7_), channel_id=1, source_target_pairs={{4,8},{8,4},{5,9},{9,5},{6,10},{10,6},{7,11},{11,7},{20,24},{24,20... | collective-permute-start | bytes 2457608 | tf_op jit(solution)/shard_map/ppermute | solution.py:115
  9.2 21.3 %collective-permute-start = (bf16[384,1024]{1,0:T(8,128)(2,1)}, bf16[384,1024]{1,0:T(8,128)(2,1)}, u32[]{:S(2)}, u32[]{:S(2)}) collective-permute-start(bf16[384,1024]{1,0:T(8,128)(2,1)} %refs_0_.1), channel_id=1, source_target_pairs={{0,2},{1,3},{2,0},{3,1},{4,6},{5,7},{6,4},{7,5},{8,10},{9,11},{10,... | collective-permute-start | bytes 2359304 | tf_op jit(solution)/shard_map/ppermute | solution.py:107
  15.8 25.1 %collective-permute-start.1 = (bf16[2048,512]{1,0:T(8,128)(2,1)}, bf16[2048,512]{1,0:T(8,128)(2,1)S(1)}, u32[]{:S(2)}, u32[]{:S(2)}) collective-permute-start(bf16[2048,512]{1,0:T(8,128)(2,1)} %shard_map.92), channel_id=1, source_target_pairs={{0,1},{1,0},{2,3},{3,2},{4,5},{5,4},{6,7},{7,6},{8,9},{9,8},{10,11... | collective-permute-start | bytes 6291464 | tf_op jit(solution)/shard_map/ppermute | solution.py:111
  26.0 22.1 %collective-permute-start.4 = (bf16[400,1024]{1,0:T(8,128)(2,1)}, bf16[400,1024]{1,0:T(8,128)(2,1)}, u32[]{:S(2)}, u32[]{:S(2)}) collective-permute-start(bf16[400,1024]{1,0:T(8,128)(2,1)} %collective-permute-done.3.refs_0_.refs_8_.refs_9_), channel_id=1, source_target_pairs={{0,2},{1,3},{2,0},{3,1},{4,6},{5,7},{6,4},{7,5},{8,10},{9,11},{10,... | collective-permute-start | bytes 2457608 | tf_op jit(solution)/shard_map/ppermute | solution.py:107
  27.6 11.7 %collective-permute-start.8 = (bf16[400,1024]{1,0:T(8,128)(2,1)}, bf16[400,1024]{1,0:T(8,128)(2,1)}, u32[]{:S(2)}, u32[]{:S(2)}) collective-permute-start(bf16[400,1024]{1,0:T(8,128)(2,1)} %collective-permute-done.3.refs_0_.refs_8_.refs_9_), channel_id=1, source_target_pairs={{4,8},{8,4},{5,9},{9,5},{6,10},{10,6},{7,11},{11,7},{20,24},{24,20... | collective-permute-start | bytes 2457608 | tf_op jit(solution)/shard_map/ppermute | solution.py:115
  29.2 21.9 %collective-permute-start.7 = (bf16[400,1024]{1,0:T(8,128)(2,1)}, bf16[400,1024]{1,0:T(8,128)(2,1)}, u32[]{:S(2)}, u32[]{:S(2)}) collective-permute-start(bf16[400,1024]{1,0:T(8,128)(2,1)} %collective-permute-done.6.refs_0_.refs_10_), channel_id=1, source_target_pairs={{4,0},{8,12},{5,1},{9,13},{6,2},{10,14},{7,3},{11,15},{20,16},{24,... | collective-permute-start | bytes 2457608 | tf_op jit(solution)/shard_map/ppermute | solution.py:115
  32.5 15.5 %collective-permute-start.9 = (bf16[192,1024]{1,0:T(8,128)(2,1)S(1)}, bf16[192,1024]{1,0:T(8,128)(2,1)S(1)}, u32[]{:S(2)}, u32[]{:S(2)}) collective-permute-start(bf16[192,1024]{1,0:T(8,128)(2,1)S(1)} %shard_map.97), channel_id=1, source_target_pairs={{0,4},{12,8},{1,5},{13,9},{2,6},{14,10},{3,7},{15,11},{16,20},{28,... | collective-permute-start | bytes 1179656 | tf_op jit(solution)/shard_map/ppermute | solution.py:115
  39.3 20.0 %collective-permute-start.10 = (bf16[400,1024]{1,0:T(8,128)(2,1)}, bf16[400,1024]{1,0:T(8,128)(2,1)}, u32[]{:S(2)}, u32[]{:S(2)}) collective-permute-start(bf16[400,1024]{1,0:T(8,128)(2,1)} %collective-permute-done.6.refs_0_.refs_10_), channel_id=1, source_target_pairs={{4,6},{5,7},{6,4},{7,5},{8,10},{9,11},{10,8},{11,9},{20,22},{21,23... | collective-permute-start | bytes 2457608 | tf_op jit(solution)/shard_map/ppermute | solution.py:433
  40.9 29.3 %collective-permute-start.12 = (bf16[400,1024]{1,0:T(8,128)(2,1)}, bf16[400,1024]{1,0:T(8,128)(2,1)}, u32[]{:S(2)}, u32[]{:S(2)}) collective-permute-start(bf16[400,1024]{1,0:T(8,128)(2,1)} %collective-permute-done.8.refs_2_.inner_ref.refs_0_.refs_12_), channel_id=1, source_target_pairs={{4,0},{8,12},{5,1},{9,13},{6,2},{10,14},{7,3},{11,15},{20,16},{24,... | collective-permute-start | bytes 2457608 | tf_op jit(solution)/shard_map/ppermute | solution.py:115
  51.1 20.0 %collective-permute-start.11 = (bf16[400,1024]{1,0:T(8,128)(2,1)}, bf16[400,1024]{1,0:T(8,128)(2,1)S(1)}, u32[]{:S(2)}, u32[]{:S(2)}) collective-permute-start(bf16[400,1024]{1,0:T(8,128)(2,1)} %shard_map.98.refs_1_.refs_11_), channel_id=1, source_target_pairs={{0,2},{1,3},{2,0},{3,1},{12,14},{13,15},{14,12},{15,13},{16,18},{1... | collective-permute-start | bytes 2457608 | tf_op jit(solution)/shard_map/ppermute | solution.py:433
  54.2 22.4 %collective-permute-start.2 = (bf16[384,1024]{1,0:T(8,128)(2,1)}, bf16[384,1024]{1,0:T(8,128)(2,1)S(1)}, u32[]{:S(2)}, u32[]{:S(2)}) collective-permute-start(bf16[384,1024]{1,0:T(8,128)(2,1)} %copy-done.15), channel_id=1, source_target_pairs={{0,1},{1,0},{2,3},{3,2},{4,5},{5,4},{6,7},{7,6},{8,9},{9,8},{10,11... | collective-permute-start | bytes 2359304 | tf_op jit(solution)/shard_map/ppermute | solution.py:111
  58.8 18.2 %collective-permute-start.5 = (bf16[384,1024]{1,0:T(8,128)(2,1)S(1)}, bf16[384,1024]{1,0:T(8,128)(2,1)S(1)}, u32[]{:S(2)}, u32[]{:S(2)}) collective-permute-start(bf16[384,1024]{1,0:T(8,128)(2,1)S(1)} %get-tuple-element.34), channel_id=1, source_target_pairs={{0,1},{1,0},{2,3},{3,2},{4,5},{5,4},{6,7},{7,6},{8,9},{9,8},{10,11... | collective-permute-start | bytes 2359304 | tf_op jit(solution)/shard_map/ppermute | solution.py:111
  59.3 24.6 %collective-permute-start.15 = (bf16[192,1024]{1,0:T(8,128)(2,1)S(1)}, bf16[192,1024]{1,0:T(8,128)(2,1)S(1)}, u32[]{:S(2)}, u32[]{:S(2)}) collective-permute-start(bf16[192,1024]{1,0:T(8,128)(2,1)S(1)} %collective-permute-done.13.rest_2_.refs_1_), channel_id=1, source_target_pairs={{4,0},{8,12},{5,1},{9,13},{6,2},{10,14},{7,3},{11,15},{20,16},{24,... | collective-permute-start | bytes 1179656 | tf_op jit(solution)/shard_map/ppermute | solution.py:115
  73.8 12.3 %collective-permute-start.18 = (bf16[256,2048]{1,0:T(8,128)(2,1)S(1)}, bf16[256,2048]{1,0:T(8,128)(2,1)S(1)}, u32[]{:S(2)}, u32[]{:S(2)}) collective-permute-start(bf16[256,2048]{1,0:T(8,128)(2,1)S(1)} %copy-done.6), channel_id=1, source_target_pairs={{0,1},{1,0},{2,3},{3,2},{4,5},{5,4},{6,7},{7,6},{8,9},{9,8},{10,11... | collective-permute-start | bytes 3145736 | tf_op jit(solution)/shard_map/ppermute | solution.py:111
  92.8 12.0 %collective-permute-start.20 = (bf16[192,1024]{1,0:T(8,128)(2,1)S(1)}, bf16[192,1024]{1,0:T(8,128)(2,1)S(1)}, u32[]{:S(2)}, u32[]{:S(2)}) collective-permute-start(bf16[192,1024]{1,0:T(8,128)(2,1)S(1)} %get-tuple-element.50), channel_id=1, source_target_pairs={{0,2},{1,3},{2,0},{3,1},{4,6},{5,7},{6,4},{7,5},{8,10},{9,11},{10,... | collective-permute-start | bytes 1179656 | tf_op jit(solution)/shard_map/ppermute | solution.py:107
  97.5 16.0 %collective-permute-start.22 = (bf16[192,1024]{1,0:T(8,128)(2,1)S(1)}, bf16[192,1024]{1,0:T(8,128)(2,1)S(1)}, u32[]{:S(2)}, u32[]{:S(2)}) collective-permute-start(bf16[192,1024]{1,0:T(8,128)(2,1)S(1)} %get-tuple-element.52), channel_id=1, source_target_pairs={{0,2},{1,3},{2,0},{3,1},{4,6},{5,7},{6,4},{7,5},{8,10},{9,11},{10,... | collective-permute-start | bytes 1179656 | tf_op jit(solution)/shard_map/ppermute | solution.py:107
  104.9 15.3 %collective-permute-start.24 = (bf16[192,1024]{1,0:T(8,128)(2,1)S(1)}, bf16[192,1024]{1,0:T(8,128)(2,1)S(1)}, u32[]{:S(2)}, u32[]{:S(2)}) collective-permute-start(bf16[192,1024]{1,0:T(8,128)(2,1)S(1)} %add_convert_fusion.4), channel_id=1, source_target_pairs={{0,4},{12,8},{1,5},{13,9},{2,6},{14,10},{3,7},{15,11},{16,20},{28,... | collective-permute-start | bytes 1179656 | tf_op jit(solution)/shard_map/ppermute | solution.py:115
  110.7 22.6 %collective-permute-start.19 = (bf16[192,1024]{1,0:T(8,128)(2,1)S(1)}, bf16[192,1024]{1,0:T(8,128)(2,1)S(1)}, u32[]{:S(2)}, u32[]{:S(2)}) collective-permute-start(bf16[192,1024]{1,0:T(8,128)(2,1)S(1)} %get-tuple-element.48), channel_id=1, source_target_pairs={{0,2},{1,3},{2,0},{3,1},{4,6},{5,7},{6,4},{7,5},{8,10},{9,11},{10,... | collective-permute-start | bytes 1179656 | tf_op jit(solution)/shard_map/ppermute | solution.py:107
  112.3 17.0 %collective-permute-start.26 = (bf16[192,1024]{1,0:T(8,128)(2,1)S(1)}, bf16[192,1024]{1,0:T(8,128)(2,1)S(1)}, u32[]{:S(2)}, u32[]{:S(2)}) collective-permute-start(bf16[192,1024]{1,0:T(8,128)(2,1)S(1)} %get-tuple-element.54), channel_id=1, source_target_pairs={{0,2},{1,3},{2,0},{3,1},{4,6},{5,7},{6,4},{7,5},{8,10},{9,11},{10,... | collective-permute-start | bytes 1179656 | tf_op jit(solution)/shard_map/ppermute | solution.py:107
  112.8 20.5 %collective-permute-start.21 = (bf16[192,1024]{1,0:T(8,128)(2,1)S(1)}, bf16[192,1024]{1,0:T(8,128)(2,1)S(1)}, u32[]{:S(2)}, u32[]{:S(2)}) collective-permute-start(bf16[192,1024]{1,0:T(8,128)(2,1)S(1)} %add_convert_fusion.4), channel_id=1, source_target_pairs={{4,8},{8,4},{5,9},{9,5},{6,10},{10,6},{7,11},{11,7},{20,24},{24,20... | collective-permute-start | bytes 1179656 | tf_op jit(solution)/shard_map/ppermute | solution.py:115
  113.6 19.7 %collective-permute-start.23 = (bf16[192,1024]{1,0:T(8,128)(2,1)S(1)}, bf16[192,1024]{1,0:T(8,128)(2,1)S(1)}, u32[]{:S(2)}, u32[]{:S(2)}) collective-permute-start(bf16[192,1024]{1,0:T(8,128)(2,1)S(1)} %add_convert_fusion.3), channel_id=1, source_target_pairs={{0,8},{12,4},{1,9},{13,5},{2,10},{14,6},{3,11},{15,7},{16,24},{28,... | collective-permute-start | bytes 1179656 | tf_op jit(solution)/shard_map/ppermute | solution.py:115
  120.3 19.1 %collective-permute-start.25 = (bf16[192,1024]{1,0:T(8,128)(2,1)S(1)}, bf16[192,1024]{1,0:T(8,128)(2,1)S(1)}, u32[]{:S(2)}, u32[]{:S(2)}) collective-permute-start(bf16[192,1024]{1,0:T(8,128)(2,1)S(1)} %add_convert_fusion.2), channel_id=1, source_target_pairs={{4,12},{8,0},{5,13},{9,1},{6,14},{10,2},{7,15},{11,3},{20,28},{24,... | collective-permute-start | bytes 1179656 | tf_op jit(solution)/shard_map/ppermute | solution.py:115
  129.4 18.3 %collective-permute-start.27 = (bf16[192,1024]{1,0:T(8,128)(2,1)S(1)}, bf16[192,1024]{1,0:T(8,128)(2,1)S(1)}, u32[]{:S(2)}, u32[]{:S(2)}) collective-permute-start(bf16[192,1024]{1,0:T(8,128)(2,1)S(1)} %add_convert_fusion.1), channel_id=1, source_target_pairs={{0,4},{4,0},{8,12},{12,8},{1,5},{5,1},{9,13},{13,9},{2,6},{6,2},{1... | collective-permute-start | bytes 1179656 | tf_op jit(solution)/shard_map/ppermute | solution.py:115
  (27 other events, 148.5 us)

commit v20 on v19

--- a/solution.py
+++ b/solution.py
@@ -320,7 +320,7 @@
     first = (plan[index] * owned).astype(jnp.float32)
     token = first + lax.broadcasted_iota(jnp.int32, (owned, 1), 0).astype(jnp.float32)
     placing = jnp.where(owner == token, factor, 0.0).astype(jnp.bfloat16)
-    return jnp.dot(placing, hidden, preferred_element_type=jnp.float32).astype(jnp.bfloat16)
+    return jnp.dot(placing, hidden, preferred_element_type=jnp.float32)
 
 
 def facts_of(plan_ref, inner_ref, outer_ref, buffer, sem):
@@ -343,54 +343,78 @@
         out[...] = result.astype(out.dtype)
 
 
-def finish(owned, plan, hidden, sums, got, facts, down_own, down_lent):
+def fact_scratch(width):
+    return [pltpu.VMEM((FACT_ROWS, width), jnp.bfloat16), pltpu.SemaphoreType.DMA((1,))]
+
+
+def collect(owned, plan, hidden, sums, got, facts):
     rows, units = hidden[0].shape
+    slots = len(facts)
+
+    def body(plan_ref, *refs):
+        hidden_refs, refs = refs[: slots - 1], refs[slots - 1 :]
+        sums_ref, got_ref, refs = refs[0], refs[1], refs[2:]
+        fact_refs, (out_ref, buffer, sem) = refs[: 2 * slots], refs[2 * slots :]
+        factors = []
+        for slot in range(slots):
+            facts_of(plan_ref, *fact_refs[2 * slot : 2 * slot + 2], buffer, sem)
+            factors.append(factors_of(slot, plan_ref, buffer, rows))
+        factor = jnp.concatenate([pair[0] for pair in factors], axis=1)
+        owner = jnp.concatenate([pair[1] for pair in factors], axis=1)
+        every = [ref[...] for ref in hidden_refs] + [hidden_rows(sums_ref, got_ref)]
+        every = jnp.concatenate(every, axis=0)
+        for index in range(4):
+            span = slice(index * owned, (index + 1) * owned)
+            out_ref[span, :] = chunk_rows(owned, index, plan_ref, factor, owner, every)
+
+    fact_blocks = [block for pair_of in facts for block in pair_of]
+    specs = [SMEM] + [VMEM] * (slots + 1) + [ANYWHERE] * len(fact_blocks)
+    shape = jax.ShapeDtypeStruct((4 * owned, units), jnp.float32)
+    return on_core(body, shape, specs, fact_scratch(facts[0][0].shape[1]))(
+        plan, *hidden, sums, got, *fact_blocks
+    )
+
+
+def finish(owned, slot, plan, sums, got, facts, before, down_own, down_lent):
+    units = down_own.shape[0]
     width = down_own.shape[1] // 2
-    slots = len(facts)
     pair = [
         jax.ShapeDtypeStruct((owned, width), jnp.bfloat16),
         jax.ShapeDtypeStruct((owned, width), jnp.float32),
     ]
 
-    def first(plan_ref, *refs):
-        hidden_refs, refs = refs[:2], refs[2:]
-        sums_refs, got_refs, refs = refs[:2], refs[2:4], refs[4:]
-        fact_refs, refs = refs[: 2 * slots], refs[2 * slots :]
-        own_ref, lent_ref, sent_ref, kept_ref, all_ref, by_row_ref, buffer, sem = refs
-        for slot in range(slots):
-            facts_of(plan_ref, *fact_refs[2 * slot : 2 * slot + 2], buffer, sem)
-            factor, owner = factors_of(slot, plan_ref, buffer, rows)
-            by_row_ref[0:1, slot * rows : (slot + 1) * rows] = factor
-            by_row_ref[1:2, slot * rows : (slot + 1) * rows] = owner
-        for slot in range(2):
-            all_ref[slot * rows : (slot + 1) * rows, :] = hidden_refs[slot][...]
-            made = hidden_rows(sums_refs[slot], got_refs[slot])
-            all_ref[(slot + 2) * rows : (slot + 3) * rows, :] = made
-        factor, owner = by_row_ref[0:1, :], by_row_ref[1:2, :]
-        held = chunk_rows(owned, 0, plan_ref, factor, owner, all_ref[...])
-        down(held, own_ref, lent_ref, sent_ref, kept_ref)
-
-    def others(plan_ref, all_ref, by_row_ref, own_ref, lent_ref, *refs):
-        factor, owner = by_row_ref[0:1, :], by_row_ref[1:2, :]
-        for index in range(1, 4):
-            held = chunk_rows(owned, index, plan_ref, factor, owner, all_ref[...])
-            down(held, own_ref, lent_ref, refs[2 * index - 2], refs[2 * index - 1])
-
-    all_shape = jax.ShapeDtypeStruct((slots * rows, units), jnp.bfloat16)
-    by_row_shape = jax.ShapeDtypeStruct((2, slots * rows), jnp.float32)
-    scratch = [
-        pltpu.VMEM((FACT_ROWS, facts[0][0].shape[1]), jnp.bfloat16),
-        pltpu.SemaphoreType.DMA((1,)),
-    ]
-    fact_blocks = [block for pair_of in facts for block in pair_of]
-    specs = [SMEM] + [VMEM] * 6 + [ANYWHERE] * len(fact_blocks) + [VMEM] * 2
-    sent, kept, every, by_row = on_core(
-        first, pair + [all_shape, by_row_shape], specs, scratch
-    )(plan, *hidden, *sums, *got, *fact_blocks, down_own, down_lent)
-    rest = on_core(others, pair * 3, [SMEM] + [VMEM] * 4)(
-        plan, every, by_row, down_own, down_lent
-    )
-    return [sent, *rest[0::2]], [kept, *rest[1::2]]
+    def first(plan_ref, sums_ref, got_ref, inner_ref, outer_ref, before_ref, *refs):
+        own_ref, lent_ref, sent_ref, kept_ref, held_ref, buffer, sem = refs
+        facts_of(plan_ref, inner_ref, outer_ref, buffer, sem)
+        factor, owner = factors_of(slot, plan_ref, buffer, sums_ref.shape[0])
+        hidden = hidden_rows(sums_ref, got_ref)
+        for index in range(4):
+            rows = chunk_rows(owned, index, plan_ref, factor, owner, hidden)
+            rows = rows + before_ref[index * owned : (index + 1) * owned, :]
+            held = rows.astype(jnp.bfloat16)
+            if index == 0:
+                down(held, own_ref, lent_ref, sent_ref, kept_ref)
+            else:
+                held_ref[(index - 1) * owned : index * owned, :] = held
+
+    def others(indices, *waits):
+        def body(held_ref, own_ref, lent_ref, *refs):
+            out_refs = refs[len(waits) :]
+            for place, index in enumerate(indices):
+                held = held_ref[(index - 1) * owned : index * owned, :]
+                down(held, own_ref, lent_ref, out_refs[2 * place], out_refs[2 * place + 1])
+
+        operands = [held, down_own, down_lent, *waits]
+        return on_core(body, pair * len(indices), [VMEM] * len(operands))(*operands)
+
+    held_shape = jax.ShapeDtypeStruct((3 * owned, 2 * units), jnp.bfloat16)
+    specs = [SMEM, VMEM, VMEM, ANYWHERE, ANYWHERE] + [VMEM] * 3
+    sent, kept, held = on_core(
+        first, pair + [held_shape], specs, fact_scratch(facts[0].shape[1])
+    )(plan, sums, got, *facts, before, down_own, down_lent)
+    rest = others([1, 2])
+    chunks = [(sent, kept), (rest[0], rest[1]), (rest[2], rest[3])]
+    return chunks, lambda *waits: others([3], *waits)
 
 
 def rows_travel(
@@ -477,19 +501,22 @@
         waits=[hidden_here, hidden_there],
     )
     got_3 = across_cores(send_3)
-    sent, kept = finish(
+    total = collect(
         owned,
         plan,
         (hidden_0, hidden_1),
-        (sums_2, sums_3),
-        (got_2, got_3),
-        [(own, own), (beside, beside), second, last],
-        kept_down,
-        lent_down,
-    )
-
-    joined = [k + across_chips(s).astype(jnp.float32) for s, k in zip(sent, kept)]
-    first, second, third = [block.astype(jnp.bfloat16) for block in joined[:3]]
+        sums_2,
+        got_2,
+        [(own, own), (beside, beside), second],
+    )
+    chunks, last_chunk = finish(
+        owned, 3, plan, sums_3, got_3, last, total, kept_down, lent_down
+    )
+
+    def joined(sent, kept):
+        return kept + across_chips(sent).astype(jnp.float32)
+
+    first, second, third = [joined(*chunk).astype(jnp.bfloat16) for chunk in chunks]
     second = lax.optimization_barrier(second)
     inward = along(first, INWARD)
     middle = along(first, MIDDLE)
@@ -498,7 +525,7 @@
     two_out = along(passed.astype(jnp.bfloat16), TWO_OUT)
     beside = along(third, BESIDE)
     arrived = [block.astype(jnp.float32) for block in (middle, two_in, two_out)]
-    total = lax.optimization_barrier(joined[3] + sum(arrived))
+    total = lax.optimization_barrier(joined(*last_chunk(second)) + sum(arrived))
     return (total + beside.astype(jnp.float32)).astype(jnp.bfloat16)
 
 

time: 150 us -> 143 us (0.953)
  waiting for transfers between devices: 52.5 us -> 44.6 us
  local copies, waits for them, and re-layouts: 14.3 us -> 15.9 us
    ppermute x13, waiting for transfers between devices: 35 us -> 31.7 us  [along(): return lax.ppermute(block, 'blk', route)]
    ppermute x7, waiting for transfers between devices: 14.4 us -> 11.8 us  [across_chips(): return lax.ppermute(block, 'tp', [(i, i ^ 2) for i in range(4)])]
    ppermute x6, waiting for transfers between devices: 2.17 us -> 0.02 us  [across_cores(): return lax.ppermute(block, 'tp', [(i, i ^ 1) for i in range(4)])]
    unnamed x46, local copies, waits for them, and re-layouts: 7.21 us -> 9 us
    pallas_call x2 -> x4, Pallas kernels: 7.73 us -> 7.73 us  [the longest x1 3.54 us: collect(): on_core(body, shape, specs, fact_scratch(facts[0][0].shape[1]))]
  transfers between devices with their start and end apart: 28 -> 28, of which waited for: 10 -> 10; matrix products, arithmetic and copies ran while one was open for 6% -> 7% of each run, Pallas kernels for 15% -> 18%
where the time goes in v20:
time: 143 us; the launch traced here: 142 us
  starting transfers between devices  48.8 us (34%)
  waiting for transfers between devices  44.6 us (31%)
  Pallas kernels  29.4 us (21%)
  local copies, waits for them, and re-layouts  15.9 us (11%)
  other arithmetic  3.32 us (2%)
    ppermute x13, starting transfers between devices, along(): return lax.ppermute(block, 'blk', route)  34.5 us
    ppermute x13, waiting for transfers between devices, along(): return lax.ppermute(block, 'blk', route)  31.7 us
    pallas_call x5, Pallas kernels, partial_sums(): return on_core(body, shapes + [TOKEN], specs)(*operands, *waits)  15.2 us
    ppermute x7, waiting for transfers between devices, across_chips(): return lax.ppermute(block, 'tp', [(i, i ^ 2) for i in range(4)])  11.8 us
    unnamed x46, local copies, waits for them, and re-layouts  9 us
    ppermute x7, starting transfers between devices, across_chips(): return lax.ppermute(block, 'tp', [(i, i ^ 2) for i in range(4)])  9 us
    ppermute x2, starting transfers between devices, at_kind(): return lax.ppermute(block, ('blk', 'tp'), pairs)  4.14 us
    pallas_call x2, Pallas kernels, part_of(): pl.pallas_call(body, out_shape=shape, in_specs=[SMEM] + [ANYWHERE] * (2 +...  3.98 us
  transfers between devices with their start and end apart: 28, of which 10 were waited for; matrix products, arithmetic and copies ran while one was open for 7% of the time, Pallas kernels for 18%

profile of v20, /device:TPU:0, one launch (start us, length us, event | category | flops | bytes accessed | tf_op | source)
XLA Modules:
  0.0 142.4 jit_solution(7815934097013381719)
XLA Ops:
  4.5 3.1 %collective-permute-start = (bf16[400,1024]{1,0:T(8,128)(2,1)S(1)}, bf16[400,1024]{1,0:T(8,128)(2,1)}, u32[]{:S(2)}, u32[]{:S(2)}) collective-permute-start(bf16[400,1024]{1,0:T(8,128)(2,1)S(1)} %shard_map.91.refs_1_.refs_4_.refs_5_), channel_id=1, source_target_pairs={{0,4},{4,0},{8,12},{12,8},{1,5},{5,1},{9,13},{13,9},{2,6},{6,2},{1... | collective-permute-start | bytes 2457608 | tf_op jit(solution)/shard_map/ppermute | solution.py:115
  10.7 3.4 %dynamic-slice_bitcast_fusion.6 = (bf16[1024,256]{1,0:T(8,128)(2,1)S(1)}, bf16[1024,256]{1,0:T(8,128)(2,1)S(1)}, bf16[1024,256]{1,0:T(8,128)(2,1)S(1)}, bf16[102...) fusion(bf16[4,1024,256]{2,1,0:T(8,128)(2,1)} %bitcast.32, ...), kind=kLoop, calls=%fused_computation.17 | loop fusion | bytes 8388624 | tf_op jit(solution)/shard_map/jit(dynamic_index_in_dim)/squeeze | solution.py:443
  16.3 2.8 %dynamic-slice_bitcast_fusion.1 = (bf16[256,1024]{1,0:T(8,128)(2,1)}, bf16[256,1024]{1,0:T(8,128)(2,1)S(1)}, bf16[256,1024]{1,0:T(8,128)(2,1)S(1)}, bf16[256,1024]{1,0:T(8,128)(2,1)}) fusion(bf16[1,256,4096]{2,1,0:T(8,128)(2,1)} %param.12, s32[]{:T(128)S(6)} %select_n.39, s32[]{:T(128)S(6)} %select_n.38, s32[]{:T(128)S(6)} %select_n.37, s32[]{:T(128)S(6)} %select_n.40), kind=kLoop, calls=%fused_computation.12 | loop fusion | bytes 4194320 | tf_op jit(solution)/shard_map/dynamic_slice | solution.py:449
  19.1 6.9 %collective-permute-done.refs_0_.refs_6_.refs_7_ = bf16[400,1024]{1,0:T(8,128)(2,1)} collective-permute-done((bf16[400,1024]{1,0:T(8,128)(2,1)S(1)}, bf16[400,1024]{1,0:T(8,128)(2,1)}, u32[]{:S(2)}, u32[]{:S(2)}) %collective-permute-start) | collective-permute-done | bytes 819232 | tf_op jit(solution)/shard_map/ppermute | solution.py:115
  30.5 2.0 %shard_map.92 = bf16[192,1024]{1,0:T(8,128)(2,1)S(1)} custom-call(s32[9]{0:T(128)S(1)} %fusion.plan_ref, bf16[384,1024]{1,0:T(8,128)(2,1)} %collective-permute-done.7.inner_ref.outer_ref.refs_1_, bf16[384,1024]{1,0:T(8,128)(2,1)} %collective-permute-done.7.inner_ref.outer_ref.refs_1_), custom_call_target="tpu_custom_call" | custom-call | flops 17179869184 | bytes 1024 | tf_op jit(solution)/shard_map/pallas_call | solution.py:192
  32.5 6.5 %collective-permute-start.8 = (bf16[192,1024]{1,0:T(8,128)(2,1)S(1)}, bf16[192,1024]{1,0:T(8,128)(2,1)S(1)}, u32[]{:S(2)}, u32[]{:S(2)}) collective-permute-start(bf16[192,1024]{1,0:T(8,128)(2,1)S(1)} %shard_map.92), channel_id=1, source_target_pairs={{0,4},{12,8},{1,5},{13,9},{2,6},{14,10},{3,7},{15,11},{16,20},{28,... | collective-permute-start | bytes 1179656 | tf_op jit(solution)/shard_map/ppermute | solution.py:115
  42.2 3.2 %shard_map.94 = (f32[384,1024]{1,0:T(8,128)S(1)}, bf16[384,1024]{1,0:T(8,128)(2,1)S(1)}, f32[8,128]{1,0:T(8,128)S(1)}) custom-call(s32[9]{0:T(128)S(1)} %fusion.plan_ref, bf16[384,1024]{1,0:T(8,128)(2,1)} %refs_0_.1, bf16[384,1024]{1,0:T(8,128)(2,1)} %collective-permute-done.7.inner_ref.outer_ref.refs_1_, ...), custom_call_target="tpu_custom_call" | custom-call | flops 1024 | bytes 1024 | tf_op jit(solution)/shard_map/pallas_call | solution.py:287
  48.8 2.3 %collective-permute-done.5.refs_0_ = bf16[400,1024]{1,0:T(8,128)(2,1)} collective-permute-done((bf16[400,1024]{1,0:T(8,128)(2,1)}, bf16[400,1024]{1,0:T(8,128)(2,1)}, u32[]{:S(2)}, u32[]{:S(2)}) %collective-permute-start.5) | collective-permute-done | bytes 819232 | tf_op jit(solution)/shard_map/ppermute | solution.py:115
  51.1 2.6 %collective-permute-start.10 = (bf16[400,1024]{1,0:T(8,128)(2,1)}, bf16[400,1024]{1,0:T(8,128)(2,1)S(1)}, u32[]{:S(2)}, u32[]{:S(2)}) collective-permute-start(bf16[400,1024]{1,0:T(8,128)(2,1)} %shard_map.95.refs_1_.refs_9_), channel_id=1, source_target_pairs={{0,2},{1,3},{2,0},{3,1},{12,14},{13,15},{14,12},{15,13},{16,18},{1... | collective-permute-start | bytes 2457608 | tf_op jit(solution)/shard_map/ppermute | solution.py:457
  55.7 3.2 %shard_map.96 = (f32[384,1024]{1,0:T(8,128)S(1)}, bf16[384,1024]{1,0:T(8,128)(2,1)S(1)}, f32[8,128]{1,0:T(8,128)S(1)}) custom-call(s32[9]{0:T(128)S(1)} %fusion.plan_ref, bf16[400,1024]{1,0:T(8,128)(2,1)} %collective-permute-done.refs_0_.refs_6_.refs_7_, bf16[400,1024]{1,0:T(8,128)(2,1)} %collective-permute-done.6.refs_1_, ...), custom_call_target="tpu_custom_call" | custom-call | flops 1024 | bytes 1024 | tf_op jit(solution)/shard_map/pallas_call | solution.py:287
  60.8 9.4 %collective-permute-done.2.outer_ref.refs_1_ = bf16[400,1024]{1,0:T(8,128)(2,1)} collective-permute-done((bf16[400,1024]{1,0:T(8,128)(2,1)}, bf16[400,1024]{1,0:T(8,128)(2,1)}, u32[]{:S(2)}, u32[]{:S(2)}) %collective-permute-start.2) | collective-permute-done | bytes 819232 | tf_op jit(solution)/shard_map/ppermute | solution.py:115
  71.3 2.0 %shard_map.97 = bf16[192,1024]{1,0:T(8,128)(2,1)S(1)} custom-call(s32[9]{0:T(128)S(1)} %fusion.plan_ref, bf16[400,1024]{1,0:T(8,128)(2,1)} %collective-permute-done.1.refs_2_.inner_ref.refs_0_, bf16[400,1024]{1,0:T(8,128)(2,1)} %collective-permute-done.2.outer_ref.refs_1_, bf16[400,1024]{1,0:T(8,128)(2,1)} %collective-permute-done.4.rest_0_.refs_2_, ...), custom_call_target="tpu_custom_call" | custom-call | flops 1024 | bytes 1024 | tf_op jit(solution)/shard_map/pallas_call | solution.py:192
  73.9 2.9 %shard_map.98 = (f32[384,1024]{1,0:T(8,128)S(1)}, f32[8,128]{1,0:T(8,128)}) custom-call(s32[9]{0:T(128)S(1)} %fusion.plan_ref, bf16[400,1024]{1,0:T(8,128)(2,1)} %collective-permute-done.1.refs_2_.inner_ref.refs_0_, bf16[400,1024]{1,0:T(8,128)(2,1)} %collective-permute-done.2.outer_ref.refs_1_, bf16[1024,512]{1,0:T(8,128)(2,1)S(1)} %pad_maximum_fusion.refs_2_.refs_4_, ...), custom_call_target="tpu_custom_call" | custom-call | flops 1024 | bytes 1024 | tf_op jit(solution)/shard_map/pallas_call | solution.py:287
  78.0 4.0 %shard_map.102 = (f32[384,1024]{1,0:T(8,128)S(1)}, bf16[384,1024]{1,0:T(8,128)(2,1)S(1)}, f32[8,128]{1,0:T(8,128)}) custom-call(s32[9]{0:T(128)S(1)} %fusion.plan_ref, bf16[400,1024]{1,0:T(8,128)(2,1)} %collective-permute-done.3.refs_0_.refs_8_, bf16[400,1024]{1,0:T(8,128)(2,1)} %shard_map.95.refs_1_.refs_9_, ...), custom_call_target="tpu_custom_call" | custom-call | flops 1024 | bytes 1024 | tf_op jit(solution)/shard_map/pallas_call | solution.py:287
  84.0 2.0 %shard_map.101 = (f32[384,1024]{1,0:T(8,128)S(1)}, bf16[384,1024]{1,0:T(8,128)(2,1)S(1)}, f32[8,128]{1,0:T(8,128)}) custom-call(s32[9]{0:T(128)S(1)} %fusion.plan_ref, bf16[192,1024]{1,0:T(8,128)(2,1)S(1)} %collective-permute-done.12.refs_0_, bf16[192,1024]{1,0:T(8,128)(2,1)S(1)} %collective-permute-done.11.rest_2_.refs_1_, ...), custom_call_target="tpu_custom_call" | custom-call | flops 1024 | bytes 1024 | tf_op jit(solution)/shard_map/pallas_call | solution.py:287
  87.2 3.5 %shard_map.103.before_ref = f32[768,512]{1,0:T(8,128)S(1)} custom-call(s32[9]{0:T(128)S(1)} %fusion.plan_ref, bf16[384,512]{1,0:T(8,128)(2,1)S(1)} %get-tuple-element.40.refs_0_, bf16[384,512]{1,0:T(8,128)(2,1)S(1)} %get-tuple-element.41.refs_1_, f32[384,1024]{1,0:T(8,128)S(1)} %get-tuple-element.42.refs_2_, ...), custom_call_target="tpu_custom_call" | custom-call | flops 1024 | bytes 1024 | tf_op jit(solution)/shard_map/pallas_call | solution.py:373
  90.7 2.6 %shard_map.104 = (bf16[192,1024]{1,0:T(8,128)(2,1)S(1)}, f32[192,1024]{1,0:T(8,128)S(1)}, bf16[576,512]{1,0:T(8,128)(2,1)S(1)}) custom-call(s32[9]{0:T(128)S(1)} %fusion.plan_ref, f32[384,1024]{1,0:T(8,128)S(1)} %get-tuple-element.38.sums_ref, bf16[384,1024]{1,0:T(8,128)(2,1)S(1)} %collective-permute-done.16.got_ref, ...), custom_call_target="tpu_custom_call" | custom-call | flops 1024 | bytes 1024 | tf_op jit(solution)/shard_map/pallas_call | solution.py:412
  96.5 8.9 %collective-permute-done.21 = bf16[192,1024]{1,0:T(8,128)(2,1)S(1)} collective-permute-done((bf16[192,1024]{1,0:T(8,128)(2,1)S(1)}, bf16[192,1024]{1,0:T(8,128)(2,1)S(1)}, u32[]{:S(2)}, u32[]{:S(2)}) %collective-permute-start.21) | collective-permute-done | bytes 393248 | tf_op jit(solution)/shard_map/ppermute | solution.py:107
  105.5 5.8 %collective-permute-start.24 = (bf16[192,1024]{1,0:T(8,128)(2,1)S(1)}, bf16[192,1024]{1,0:T(8,128)(2,1)S(1)}, u32[]{:S(2)}, u32[]{:S(2)}) collective-permute-start(bf16[192,1024]{1,0:T(8,128)(2,1)S(1)} %add_convert_fusion.3), channel_id=1, source_target_pairs={{0,4},{12,8},{1,5},{13,9},{2,6},{14,10},{3,7},{15,11},{16,20},{28,... | collective-permute-start | bytes 1179656 | tf_op jit(solution)/shard_map/ppermute | solution.py:115
  113.9 6.8 %collective-permute-start.23 = (bf16[192,1024]{1,0:T(8,128)(2,1)S(1)}, bf16[192,1024]{1,0:T(8,128)(2,1)S(1)}, u32[]{:S(2)}, u32[]{:S(2)}) collective-permute-start(bf16[192,1024]{1,0:T(8,128)(2,1)S(1)} %add_convert_fusion.4.refs_0_), channel_id=1, source_target_pairs={{0,8},{12,4},{1,9},{13,5},{2,10},{14,6},{3,11},{15,7},{16,24},{28,... | collective-permute-start | bytes 1179656 | tf_op jit(solution)/shard_map/ppermute | solution.py:115
  124.5 2.6 %collective-permute-start.27 = (bf16[192,1024]{1,0:T(8,128)(2,1)S(1)}, bf16[192,1024]{1,0:T(8,128)(2,1)S(1)}, u32[]{:S(2)}, u32[]{:S(2)}) collective-permute-start(bf16[192,1024]{1,0:T(8,128)(2,1)S(1)} %add_convert_fusion.1), channel_id=1, source_target_pairs={{0,4},{4,0},{8,12},{12,8},{1,5},{5,1},{9,13},{13,9},{2,6},{6,2},{1... | collective-permute-start | bytes 1179656 | tf_op jit(solution)/shard_map/ppermute | solution.py:115
  127.1 2.6 %collective-permute-done.20 = bf16[192,1024]{1,0:T(8,128)(2,1)S(1)} collective-permute-done((bf16[192,1024]{1,0:T(8,128)(2,1)S(1)}, bf16[192,1024]{1,0:T(8,128)(2,1)S(1)}, u32[]{:S(2)}, u32[]{:S(2)}) %collective-permute-start.20) | collective-permute-done | bytes 393248 | tf_op jit(solution)/shard_map/ppermute | solution.py:107
  129.7 9.1 %collective-permute-done.25 = bf16[192,1024]{1,0:T(8,128)(2,1)S(1)} collective-permute-done((bf16[192,1024]{1,0:T(8,128)(2,1)S(1)}, bf16[192,1024]{1,0:T(8,128)(2,1)S(1)}, u32[]{:S(2)}, u32[]{:S(2)}) %collective-permute-start.25) | collective-permute-done | bytes 393248 | tf_op jit(solution)/shard_map/ppermute | solution.py:115
  139.1 2.5 %collective-permute-done.27 = bf16[192,1024]{1,0:T(8,128)(2,1)S(1)} collective-permute-done((bf16[192,1024]{1,0:T(8,128)(2,1)S(1)}, bf16[192,1024]{1,0:T(8,128)(2,1)S(1)}, u32[]{:S(2)}, u32[]{:S(2)}) %collective-permute-start.27) | collective-permute-done | bytes 393248 | tf_op jit(solution)/shard_map/ppermute | solution.py:115
  (108 shorter events, 41.3 us)
Async XLA Ops:
  4.5 21.4 %collective-permute-start = (bf16[400,1024]{1,0:T(8,128)(2,1)S(1)}, bf16[400,1024]{1,0:T(8,128)(2,1)}, u32[]{:S(2)}, u32[]{:S(2)}) collective-permute-start(bf16[400,1024]{1,0:T(8,128)(2,1)S(1)} %shard_map.91.refs_1_.refs_4_.refs_5_), channel_id=1, source_target_pairs={{0,4},{4,0},{8,12},{12,8},{1,5},{5,1},{9,13},{13,9},{2,6},{6,2},{1... | collective-permute-start | bytes 2457608 | tf_op jit(solution)/shard_map/ppermute | solution.py:115
  7.6 21.6 %collective-permute-start.3 = (bf16[400,1024]{1,0:T(8,128)(2,1)S(1)}, bf16[400,1024]{1,0:T(8,128)(2,1)}, u32[]{:S(2)}, u32[]{:S(2)}) collective-permute-start(bf16[400,1024]{1,0:T(8,128)(2,1)S(1)} %shard_map.91.refs_1_.refs_4_.refs_5_), channel_id=1, source_target_pairs={{4,8},{8,4},{5,9},{9,5},{6,10},{10,6},{7,11},{11,7},{20,24},{24,20... | collective-permute-start | bytes 2457608 | tf_op jit(solution)/shard_map/ppermute | solution.py:115
  9.2 21.3 %collective-permute-start.7 = (bf16[384,1024]{1,0:T(8,128)(2,1)}, bf16[384,1024]{1,0:T(8,128)(2,1)}, u32[]{:S(2)}, u32[]{:S(2)}) collective-permute-start(bf16[384,1024]{1,0:T(8,128)(2,1)} %refs_0_.1), channel_id=1, source_target_pairs={{0,2},{1,3},{2,0},{3,1},{4,6},{5,7},{6,4},{7,5},{8,10},{9,11},{10,... | collective-permute-start | bytes 2359304 | tf_op jit(solution)/shard_map/ppermute | solution.py:107
  15.7 25.2 %collective-permute-start.9 = (bf16[2048,512]{1,0:T(8,128)(2,1)}, bf16[2048,512]{1,0:T(8,128)(2,1)S(1)}, u32[]{:S(2)}, u32[]{:S(2)}) collective-permute-start(bf16[2048,512]{1,0:T(8,128)(2,1)} %shard_map.93), channel_id=1, source_target_pairs={{0,1},{1,0},{2,3},{3,2},{4,5},{5,4},{6,7},{7,6},{8,9},{9,8},{10,11... | collective-permute-start | bytes 6291464 | tf_op jit(solution)/shard_map/ppermute | solution.py:111
  26.0 25.1 %collective-permute-start.6 = (bf16[400,1024]{1,0:T(8,128)(2,1)}, bf16[400,1024]{1,0:T(8,128)(2,1)}, u32[]{:S(2)}, u32[]{:S(2)}) collective-permute-start(bf16[400,1024]{1,0:T(8,128)(2,1)} %collective-permute-done.refs_0_.refs_6_.refs_7_), channel_id=1, source_target_pairs={{0,2},{1,3},{2,0},{3,1},{4,6},{5,7},{6,4},{7,5},{8,10},{9,11},{10,... | collective-permute-start | bytes 2457608 | tf_op jit(solution)/shard_map/ppermute | solution.py:107
  27.6 11.7 %collective-permute-start.1 = (bf16[400,1024]{1,0:T(8,128)(2,1)}, bf16[400,1024]{1,0:T(8,128)(2,1)}, u32[]{:S(2)}, u32[]{:S(2)}) collective-permute-start(bf16[400,1024]{1,0:T(8,128)(2,1)} %collective-permute-done.refs_0_.refs_6_.refs_7_), channel_id=1, source_target_pairs={{4,8},{8,4},{5,9},{9,5},{6,10},{10,6},{7,11},{11,7},{20,24},{24,20... | collective-permute-start | bytes 2457608 | tf_op jit(solution)/shard_map/ppermute | solution.py:115
  29.2 21.9 %collective-permute-start.5 = (bf16[400,1024]{1,0:T(8,128)(2,1)}, bf16[400,1024]{1,0:T(8,128)(2,1)}, u32[]{:S(2)}, u32[]{:S(2)}) collective-permute-start(bf16[400,1024]{1,0:T(8,128)(2,1)} %collective-permute-done.3.refs_0_.refs_8_), channel_id=1, source_target_pairs={{4,0},{8,12},{5,1},{9,13},{6,2},{10,14},{7,3},{11,15},{20,16},{24,... | collective-permute-start | bytes 2457608 | tf_op jit(solution)/shard_map/ppermute | solution.py:115
  32.5 15.5 %collective-permute-start.8 = (bf16[192,1024]{1,0:T(8,128)(2,1)S(1)}, bf16[192,1024]{1,0:T(8,128)(2,1)S(1)}, u32[]{:S(2)}, u32[]{:S(2)}) collective-permute-start(bf16[192,1024]{1,0:T(8,128)(2,1)S(1)} %shard_map.92), channel_id=1, source_target_pairs={{0,4},{12,8},{1,5},{13,9},{2,6},{14,10},{3,7},{15,11},{16,20},{28,... | collective-permute-start | bytes 1179656 | tf_op jit(solution)/shard_map/ppermute | solution.py:115
  39.3 20.2 %collective-permute-start.4 = (bf16[400,1024]{1,0:T(8,128)(2,1)}, bf16[400,1024]{1,0:T(8,128)(2,1)}, u32[]{:S(2)}, u32[]{:S(2)}) collective-permute-start(bf16[400,1024]{1,0:T(8,128)(2,1)} %collective-permute-done.3.refs_0_.refs_8_), channel_id=1, source_target_pairs={{4,6},{5,7},{6,4},{7,5},{8,10},{9,11},{10,8},{11,9},{20,22},{21,23... | collective-permute-start | bytes 2457608 | tf_op jit(solution)/shard_map/ppermute | solution.py:457
  40.9 29.3 %collective-permute-start.2 = (bf16[400,1024]{1,0:T(8,128)(2,1)}, bf16[400,1024]{1,0:T(8,128)(2,1)}, u32[]{:S(2)}, u32[]{:S(2)}) collective-permute-start(bf16[400,1024]{1,0:T(8,128)(2,1)} %collective-permute-done.1.refs_2_.inner_ref.refs_0_), channel_id=1, source_target_pairs={{4,0},{8,12},{5,1},{9,13},{6,2},{10,14},{7,3},{11,15},{20,16},{24,... | collective-permute-start | bytes 2457608 | tf_op jit(solution)/shard_map/ppermute | solution.py:115
  51.1 20.1 %collective-permute-start.10 = (bf16[400,1024]{1,0:T(8,128)(2,1)}, bf16[400,1024]{1,0:T(8,128)(2,1)S(1)}, u32[]{:S(2)}, u32[]{:S(2)}) collective-permute-start(bf16[400,1024]{1,0:T(8,128)(2,1)} %shard_map.95.refs_1_.refs_9_), channel_id=1, source_target_pairs={{0,2},{1,3},{2,0},{3,1},{12,14},{13,15},{14,12},{15,13},{16,18},{1... | collective-permute-start | bytes 2457608 | tf_op jit(solution)/shard_map/ppermute | solution.py:457
  54.4 22.4 %collective-permute-start.14 = (bf16[384,1024]{1,0:T(8,128)(2,1)}, bf16[384,1024]{1,0:T(8,128)(2,1)S(1)}, u32[]{:S(2)}, u32[]{:S(2)}) collective-permute-start(bf16[384,1024]{1,0:T(8,128)(2,1)} %copy-done.15), channel_id=1, source_target_pairs={{0,1},{1,0},{2,3},{3,2},{4,5},{5,4},{6,7},{7,6},{8,9},{9,8},{10,11... | collective-permute-start | bytes 2359304 | tf_op jit(solution)/shard_map/ppermute | solution.py:111
  58.9 18.2 %collective-permute-start.15 = (bf16[384,1024]{1,0:T(8,128)(2,1)S(1)}, bf16[384,1024]{1,0:T(8,128)(2,1)S(1)}, u32[]{:S(2)}, u32[]{:S(2)}) collective-permute-start(bf16[384,1024]{1,0:T(8,128)(2,1)S(1)} %get-tuple-element.36), channel_id=1, source_target_pairs={{0,1},{1,0},{2,3},{3,2},{4,5},{5,4},{6,7},{7,6},{8,9},{9,8},{10,11... | collective-permute-start | bytes 2359304 | tf_op jit(solution)/shard_map/ppermute | solution.py:111
  59.5 24.5 %collective-permute-start.13 = (bf16[192,1024]{1,0:T(8,128)(2,1)S(1)}, bf16[192,1024]{1,0:T(8,128)(2,1)S(1)}, u32[]{:S(2)}, u32[]{:S(2)}) collective-permute-start(bf16[192,1024]{1,0:T(8,128)(2,1)S(1)} %collective-permute-done.11.rest_2_.refs_1_), channel_id=1, source_target_pairs={{4,0},{8,12},{5,1},{9,13},{6,2},{10,14},{7,3},{11,15},{20,16},{24,... | collective-permute-start | bytes 1179656 | tf_op jit(solution)/shard_map/ppermute | solution.py:115
  73.3 10.8 %collective-permute-start.12 = (bf16[192,1024]{1,0:T(8,128)(2,1)S(1)}, bf16[192,1024]{1,0:T(8,128)(2,1)S(1)}, u32[]{:S(2)}, u32[]{:S(2)}) collective-permute-start(bf16[192,1024]{1,0:T(8,128)(2,1)S(1)} %shard_map.97), channel_id=1, source_target_pairs={{0,2},{1,3},{2,0},{3,1},{4,6},{5,7},{6,4},{7,5},{8,10},{9,11},{10,... | collective-permute-start | bytes 1179656 | tf_op jit(solution)/shard_map/ppermute | solution.py:107
  73.9 16.9 %collective-permute-start.18 = (bf16[256,2048]{1,0:T(8,128)(2,1)S(1)}, bf16[256,2048]{1,0:T(8,128)(2,1)S(1)}, u32[]{:S(2)}, u32[]{:S(2)}) collective-permute-start(bf16[256,2048]{1,0:T(8,128)(2,1)S(1)} %copy-done.6), channel_id=1, source_target_pairs={{0,1},{1,0},{2,3},{3,2},{4,5},{5,4},{6,7},{7,6},{8,9},{9,8},{10,11... | collective-permute-start | bytes 3145736 | tf_op jit(solution)/shard_map/ppermute | solution.py:111
  93.3 12.1 %collective-permute-start.21 = (bf16[192,1024]{1,0:T(8,128)(2,1)S(1)}, bf16[192,1024]{1,0:T(8,128)(2,1)S(1)}, u32[]{:S(2)}, u32[]{:S(2)}) collective-permute-start(bf16[192,1024]{1,0:T(8,128)(2,1)S(1)} %get-tuple-element.50), channel_id=1, source_target_pairs={{0,2},{1,3},{2,0},{3,1},{4,6},{5,7},{6,4},{7,5},{8,10},{9,11},{10,... | collective-permute-start | bytes 1179656 | tf_op jit(solution)/shard_map/ppermute | solution.py:107
  95.9 17.9 %collective-permute-start.19 = (bf16[192,1024]{1,0:T(8,128)(2,1)S(1)}, bf16[192,1024]{1,0:T(8,128)(2,1)S(1)}, u32[]{:S(2)}, u32[]{:S(2)}) collective-permute-start(bf16[192,1024]{1,0:T(8,128)(2,1)S(1)} %get-tuple-element.46), channel_id=1, source_target_pairs={{0,2},{1,3},{2,0},{3,1},{4,6},{5,7},{6,4},{7,5},{8,10},{9,11},{10,... | collective-permute-start | bytes 1179656 | tf_op jit(solution)/shard_map/ppermute | solution.py:107
  105.5 17.4 %collective-permute-start.24 = (bf16[192,1024]{1,0:T(8,128)(2,1)S(1)}, bf16[192,1024]{1,0:T(8,128)(2,1)S(1)}, u32[]{:S(2)}, u32[]{:S(2)}) collective-permute-start(bf16[192,1024]{1,0:T(8,128)(2,1)S(1)} %add_convert_fusion.3), channel_id=1, source_target_pairs={{0,4},{12,8},{1,5},{13,9},{2,6},{14,10},{3,7},{15,11},{16,20},{28,... | collective-permute-start | bytes 1179656 | tf_op jit(solution)/shard_map/ppermute | solution.py:115
  111.3 13.0 %collective-permute-start.26 = (bf16[192,1024]{1,0:T(8,128)(2,1)S(1)}, bf16[192,1024]{1,0:T(8,128)(2,1)S(1)}, u32[]{:S(2)}, u32[]{:S(2)}) collective-permute-start(bf16[192,1024]{1,0:T(8,128)(2,1)S(1)} %get-tuple-element.52), channel_id=1, source_target_pairs={{0,2},{1,3},{2,0},{3,1},{4,6},{5,7},{6,4},{7,5},{8,10},{9,11},{10,... | collective-permute-start | bytes 1179656 | tf_op jit(solution)/shard_map/ppermute | solution.py:107
  112.9 14.2 %collective-permute-start.22 = (bf16[192,1024]{1,0:T(8,128)(2,1)S(1)}, bf16[192,1024]{1,0:T(8,128)(2,1)S(1)}, u32[]{:S(2)}, u32[]{:S(2)}) collective-permute-start(bf16[192,1024]{1,0:T(8,128)(2,1)S(1)} %add_convert_fusion.3), channel_id=1, source_target_pairs={{4,8},{8,4},{5,9},{9,5},{6,10},{10,6},{7,11},{11,7},{20,24},{24,20... | collective-permute-start | bytes 1179656 | tf_op jit(solution)/shard_map/ppermute | solution.py:115
  113.9 15.8 %collective-permute-start.23 = (bf16[192,1024]{1,0:T(8,128)(2,1)S(1)}, bf16[192,1024]{1,0:T(8,128)(2,1)S(1)}, u32[]{:S(2)}, u32[]{:S(2)}) collective-permute-start(bf16[192,1024]{1,0:T(8,128)(2,1)S(1)} %add_convert_fusion.4.refs_0_), channel_id=1, source_target_pairs={{0,8},{12,4},{1,9},{13,5},{2,10},{14,6},{3,11},{15,7},{16,24},{28,... | collective-permute-start | bytes 1179656 | tf_op jit(solution)/shard_map/ppermute | solution.py:115
  123.1 15.8 %collective-permute-start.25 = (bf16[192,1024]{1,0:T(8,128)(2,1)S(1)}, bf16[192,1024]{1,0:T(8,128)(2,1)S(1)}, u32[]{:S(2)}, u32[]{:S(2)}) collective-permute-start(bf16[192,1024]{1,0:T(8,128)(2,1)S(1)} %add_convert_fusion.2), channel_id=1, source_target_pairs={{4,12},{8,0},{5,13},{9,1},{6,14},{10,2},{7,15},{11,3},{20,28},{24,... | collective-permute-start | bytes 1179656 | tf_op jit(solution)/shard_map/ppermute | solution.py:115
  124.5 17.1 %collective-permute-start.27 = (bf16[192,1024]{1,0:T(8,128)(2,1)S(1)}, bf16[192,1024]{1,0:T(8,128)(2,1)S(1)}, u32[]{:S(2)}, u32[]{:S(2)}) collective-permute-start(bf16[192,1024]{1,0:T(8,128)(2,1)S(1)} %add_convert_fusion.1), channel_id=1, source_target_pairs={{0,4},{4,0},{8,12},{12,8},{1,5},{5,1},{9,13},{13,9},{2,6},{6,2},{1... | collective-permute-start | bytes 1179656 | tf_op jit(solution)/shard_map/ppermute | solution.py:115
  (27 other events, 124.7 us)

commit v21 on v20

--- a/solution.py
+++ b/solution.py
@@ -147,11 +147,15 @@
     ]
 
 
+def waits_of(block, others):
+    return [VMEM if other.shape[0] < block.shape[0] else ANYWHERE for other in others]
+
+
 def after(block, *others, flops=1024):
     return pl.pallas_call(
         lambda *refs: None,
         out_shape=jax.ShapeDtypeStruct(block.shape, block.dtype),
-        in_specs=[ANYWHERE] * (1 + len(others)),
+        in_specs=[ANYWHERE] + waits_of(block, others),
         out_specs=ANYWHERE,
         input_output_aliases={0: 0},
         cost_estimate=pl.CostEstimate(flops=flops, bytes_accessed=1024, transcendentals=0),
@@ -192,7 +196,7 @@
     return pl.pallas_call(
         body,
         out_shape=shape,
-        in_specs=[SMEM] + [ANYWHERE] * (2 + len(others)),
+        in_specs=[SMEM] + [ANYWHERE] * 2 + waits_of(if_inner, others),
         out_specs=ANYWHERE,
         scratch_shapes=[pltpu.VMEM(shape.shape, shape.dtype)]
         + [pltpu.SemaphoreType.DMA((pieces,))] * 2,

time: 143 us -> 144 us (level)
  Pallas kernels: 29.4 us -> 31.6 us
    ppermute x13, waiting for transfers between devices: 31.7 us -> 29.5 us  [along(): return lax.ppermute(block, 'blk', route)]
    pallas_call x2, Pallas kernels: 0.01 us -> 2.21 us  [after(): pl.pallas_call(lambda *refs: None, out_shape=jax.ShapeDtypeStruct(block.s...]
  transfers between devices with their start and end apart: 28 -> 28, of which waited for: 10 -> 10; matrix products, arithmetic and copies ran while one was open for 7% -> 7% of each run, Pallas kernels for 18% -> 19%
where the time goes in v21:
time: 144 us; the launch traced here: 143 us
  starting transfers between devices  48.6 us (34%)
  waiting for transfers between devices  43.4 us (30%)
  Pallas kernels  31.6 us (22%)
  local copies, waits for them, and re-layouts  15.9 us (11%)
  other arithmetic  3.32 us (2%)
    ppermute x13, starting transfers between devices, along(): return lax.ppermute(block, 'blk', route)  34.5 us
    ppermute x13, waiting for transfers between devices, along(): return lax.ppermute(block, 'blk', route)  29.5 us
    pallas_call x5, Pallas kernels, partial_sums(): return on_core(body, shapes + [TOKEN], specs)(*operands, *waits)  15.2 us
    ppermute x7, waiting for transfers between devices, across_chips(): return lax.ppermute(block, 'tp', [(i, i ^ 2) for i in range(4)])  11.8 us
    ppermute x7, starting transfers between devices, across_chips(): return lax.ppermute(block, 'tp', [(i, i ^ 2) for i in range(4)])  9.01 us
    unnamed x46, local copies, waits for them, and re-layouts  9 us
    ppermute x2, starting transfers between devices, at_kind(): return lax.ppermute(block, ('blk', 'tp'), pairs)  4.01 us
    pallas_call x2, Pallas kernels, part_of(): pl.pallas_call(body, out_shape=shape, in_specs=[SMEM] + [ANYWHERE] * 2 +...  3.98 us
  transfers between devices with their start and end apart: 28, of which 10 were waited for; matrix products, arithmetic and copies ran while one was open for 7% of the time, Pallas kernels for 19%

profile of v21, /device:TPU:0, one launch (start us, length us, event | category | flops | bytes accessed | tf_op | source)
XLA Modules:
  0.0 143.2 jit_solution(4330226121095632549)
XLA Ops:
  4.5 3.1 %collective-permute-start = (bf16[400,1024]{1,0:T(8,128)(2,1)S(1)}, bf16[400,1024]{1,0:T(8,128)(2,1)}, u32[]{:S(2)}, u32[]{:S(2)}) collective-permute-start(bf16[400,1024]{1,0:T(8,128)(2,1)S(1)} %shard_map.91.refs_1_.refs_4_.refs_5_), channel_id=1, source_target_pairs={{0,4},{4,0},{8,12},{12,8},{1,5},{5,1},{9,13},{13,9},{2,6},{6,2},{1... | collective-permute-start | bytes 2457608 | tf_op jit(solution)/shard_map/ppermute | solution.py:115
  10.7 3.4 %dynamic-slice_bitcast_fusion.6 = (bf16[1024,256]{1,0:T(8,128)(2,1)S(1)}, bf16[1024,256]{1,0:T(8,128)(2,1)S(1)}, bf16[1024,256]{1,0:T(8,128)(2,1)S(1)}, bf16[102...) fusion(bf16[4,1024,256]{2,1,0:T(8,128)(2,1)} %bitcast.32, ...), kind=kLoop, calls=%fused_computation.17 | loop fusion | bytes 8388624 | tf_op jit(solution)/shard_map/jit(dynamic_index_in_dim)/squeeze | solution.py:447
  17.5 2.8 %dynamic-slice_bitcast_fusion.1 = (bf16[256,1024]{1,0:T(8,128)(2,1)}, bf16[256,1024]{1,0:T(8,128)(2,1)S(1)}, bf16[256,1024]{1,0:T(8,128)(2,1)S(1)}, bf16[256,1024]{1,0:T(8,128)(2,1)}) fusion(bf16[1,256,4096]{2,1,0:T(8,128)(2,1)} %param.12, s32[]{:T(128)S(6)} %select_n.39, s32[]{:T(128)S(6)} %select_n.38, s32[]{:T(128)S(6)} %select_n.37, s32[]{:T(128)S(6)} %select_n.40), kind=kLoop, calls=%fused_computation.12 | loop fusion | bytes 4194320 | tf_op jit(solution)/shard_map/dynamic_slice | solution.py:453
  20.2 5.7 %collective-permute-done.refs_0_.refs_6_.refs_7_ = bf16[400,1024]{1,0:T(8,128)(2,1)} collective-permute-done((bf16[400,1024]{1,0:T(8,128)(2,1)S(1)}, bf16[400,1024]{1,0:T(8,128)(2,1)}, u32[]{:S(2)}, u32[]{:S(2)}) %collective-permute-start) | collective-permute-done | bytes 819232 | tf_op jit(solution)/shard_map/ppermute | solution.py:115
  32.5 6.5 %collective-permute-start.8 = (bf16[192,1024]{1,0:T(8,128)(2,1)S(1)}, bf16[192,1024]{1,0:T(8,128)(2,1)S(1)}, u32[]{:S(2)}, u32[]{:S(2)}) collective-permute-start(bf16[192,1024]{1,0:T(8,128)(2,1)S(1)} %shard_map.92), channel_id=1, source_target_pairs={{0,4},{12,8},{1,5},{13,9},{2,6},{14,10},{3,7},{15,11},{16,20},{28,... | collective-permute-start | bytes 1179656 | tf_op jit(solution)/shard_map/ppermute | solution.py:115
  42.2 3.2 %shard_map.94 = (f32[384,1024]{1,0:T(8,128)S(1)}, bf16[384,1024]{1,0:T(8,128)(2,1)S(1)}, f32[8,128]{1,0:T(8,128)S(1)}) custom-call(s32[9]{0:T(128)S(1)} %fusion.plan_ref, bf16[384,1024]{1,0:T(8,128)(2,1)} %refs_0_.1, bf16[384,1024]{1,0:T(8,128)(2,1)} %collective-permute-done.7.inner_ref.outer_ref.refs_1_, ...), custom_call_target="tpu_custom_call" | custom-call | flops 1024 | bytes 1024 | tf_op jit(solution)/shard_map/pallas_call | solution.py:291
  48.8 2.3 %collective-permute-done.5.refs_0_ = bf16[400,1024]{1,0:T(8,128)(2,1)} collective-permute-done((bf16[400,1024]{1,0:T(8,128)(2,1)}, bf16[400,1024]{1,0:T(8,128)(2,1)}, u32[]{:S(2)}, u32[]{:S(2)}) %collective-permute-start.5) | collective-permute-done | bytes 819232 | tf_op jit(solution)/shard_map/ppermute | solution.py:115
  52.2 2.4 %collective-permute-start.10 = (bf16[400,1024]{1,0:T(8,128)(2,1)}, bf16[400,1024]{1,0:T(8,128)(2,1)S(1)}, u32[]{:S(2)}, u32[]{:S(2)}) collective-permute-start(bf16[400,1024]{1,0:T(8,128)(2,1)} %shard_map.95.refs_1_.refs_9_), channel_id=1, source_target_pairs={{0,2},{1,3},{2,0},{3,1},{12,14},{13,15},{14,12},{15,13},{16,18},{1... | collective-permute-start | bytes 2457608 | tf_op jit(solution)/shard_map/ppermute | solution.py:461
  56.6 3.2 %shard_map.96 = (f32[384,1024]{1,0:T(8,128)S(1)}, bf16[384,1024]{1,0:T(8,128)(2,1)S(1)}, f32[8,128]{1,0:T(8,128)S(1)}) custom-call(s32[9]{0:T(128)S(1)} %fusion.plan_ref, bf16[400,1024]{1,0:T(8,128)(2,1)} %collective-permute-done.refs_0_.refs_6_.refs_7_, bf16[400,1024]{1,0:T(8,128)(2,1)} %collective-permute-done.6.refs_1_, ...), custom_call_target="tpu_custom_call" | custom-call | flops 1024 | bytes 1024 | tf_op jit(solution)/shard_map/pallas_call | solution.py:291
  61.7 8.5 %collective-permute-done.2.outer_ref.refs_1_ = bf16[400,1024]{1,0:T(8,128)(2,1)} collective-permute-done((bf16[400,1024]{1,0:T(8,128)(2,1)}, bf16[400,1024]{1,0:T(8,128)(2,1)}, u32[]{:S(2)}, u32[]{:S(2)}) %collective-permute-start.2) | collective-permute-done | bytes 819232 | tf_op jit(solution)/shard_map/ppermute | solution.py:115
  70.2 2.0 %collective-permute-done.10.rest_1_.refs_3_ = bf16[400,1024]{1,0:T(8,128)(2,1)S(1)} collective-permute-done((bf16[400,1024]{1,0:T(8,128)(2,1)}, bf16[400,1024]{1,0:T(8,128)(2,1)S(1)}, u32[]{:S(2)}, u32[]{:S(2)}) %collective-permute-start.10) | collective-permute-done | bytes 819232 | tf_op jit(solution)/shard_map/ppermute | solution.py:461
  72.2 2.0 %shard_map.97 = bf16[192,1024]{1,0:T(8,128)(2,1)S(1)} custom-call(s32[9]{0:T(128)S(1)} %fusion.plan_ref, bf16[400,1024]{1,0:T(8,128)(2,1)} %collective-permute-done.1.refs_2_.inner_ref.refs_0_, bf16[400,1024]{1,0:T(8,128)(2,1)} %collective-permute-done.2.outer_ref.refs_1_, bf16[400,1024]{1,0:T(8,128)(2,1)} %collective-permute-done.4.rest_0_.refs_2_, ...), custom_call_target="tpu_custom_call" | custom-call | flops 1024 | bytes 1024 | tf_op jit(solution)/shard_map/pallas_call | solution.py:196
  74.8 2.9 %shard_map.98 = (f32[384,1024]{1,0:T(8,128)S(1)}, f32[8,128]{1,0:T(8,128)}) custom-call(s32[9]{0:T(128)S(1)} %fusion.plan_ref, bf16[400,1024]{1,0:T(8,128)(2,1)} %collective-permute-done.1.refs_2_.inner_ref.refs_0_, bf16[400,1024]{1,0:T(8,128)(2,1)} %collective-permute-done.2.outer_ref.refs_1_, bf16[1024,512]{1,0:T(8,128)(2,1)S(1)} %pad_maximum_fusion.refs_2_.refs_4_, ...), custom_call_target="tpu_custom_call" | custom-call | flops 1024 | bytes 1024 | tf_op jit(solution)/shard_map/pallas_call | solution.py:291
  78.9 4.0 %shard_map.102 = (f32[384,1024]{1,0:T(8,128)S(1)}, bf16[384,1024]{1,0:T(8,128)(2,1)S(1)}, f32[8,128]{1,0:T(8,128)}) custom-call(s32[9]{0:T(128)S(1)} %fusion.plan_ref, bf16[400,1024]{1,0:T(8,128)(2,1)} %collective-permute-done.3.refs_0_.refs_8_, bf16[400,1024]{1,0:T(8,128)(2,1)} %shard_map.95.refs_1_.refs_9_, ...), custom_call_target="tpu_custom_call" | custom-call | flops 1024 | bytes 1024 | tf_op jit(solution)/shard_map/pallas_call | solution.py:291
  84.8 2.0 %shard_map.101 = (f32[384,1024]{1,0:T(8,128)S(1)}, bf16[384,1024]{1,0:T(8,128)(2,1)S(1)}, f32[8,128]{1,0:T(8,128)}) custom-call(s32[9]{0:T(128)S(1)} %fusion.plan_ref, bf16[192,1024]{1,0:T(8,128)(2,1)S(1)} %collective-permute-done.12.refs_0_, bf16[192,1024]{1,0:T(8,128)(2,1)S(1)} %collective-permute-done.11.rest_2_.refs_1_, ...), custom_call_target="tpu_custom_call" | custom-call | flops 1024 | bytes 1024 | tf_op jit(solution)/shard_map/pallas_call | solution.py:291
  88.0 3.5 %shard_map.103.before_ref = f32[768,512]{1,0:T(8,128)S(1)} custom-call(s32[9]{0:T(128)S(1)} %fusion.plan_ref, bf16[384,512]{1,0:T(8,128)(2,1)S(1)} %get-tuple-element.40.refs_0_, bf16[384,512]{1,0:T(8,128)(2,1)S(1)} %get-tuple-element.41.refs_1_, f32[384,1024]{1,0:T(8,128)S(1)} %get-tuple-element.42.refs_2_, ...), custom_call_target="tpu_custom_call" | custom-call | flops 1024 | bytes 1024 | tf_op jit(solution)/shard_map/pallas_call | solution.py:377
  91.5 2.6 %shard_map.104 = (bf16[192,1024]{1,0:T(8,128)(2,1)S(1)}, f32[192,1024]{1,0:T(8,128)S(1)}, bf16[576,512]{1,0:T(8,128)(2,1)S(1)}) custom-call(s32[9]{0:T(128)S(1)} %fusion.plan_ref, f32[384,1024]{1,0:T(8,128)S(1)} %get-tuple-element.38.sums_ref, bf16[384,1024]{1,0:T(8,128)(2,1)S(1)} %collective-permute-done.16.got_ref, ...), custom_call_target="tpu_custom_call" | custom-call | flops 1024 | bytes 1024 | tf_op jit(solution)/shard_map/pallas_call | solution.py:416
  97.3 8.9 %collective-permute-done.21 = bf16[192,1024]{1,0:T(8,128)(2,1)S(1)} collective-permute-done((bf16[192,1024]{1,0:T(8,128)(2,1)S(1)}, bf16[192,1024]{1,0:T(8,128)(2,1)S(1)}, u32[]{:S(2)}, u32[]{:S(2)}) %collective-permute-start.21) | collective-permute-done | bytes 393248 | tf_op jit(solution)/shard_map/ppermute | solution.py:107
  106.3 5.8 %collective-permute-start.24 = (bf16[192,1024]{1,0:T(8,128)(2,1)S(1)}, bf16[192,1024]{1,0:T(8,128)(2,1)S(1)}, u32[]{:S(2)}, u32[]{:S(2)}) collective-permute-start(bf16[192,1024]{1,0:T(8,128)(2,1)S(1)} %add_convert_fusion.3), channel_id=1, source_target_pairs={{0,4},{12,8},{1,5},{13,9},{2,6},{14,10},{3,7},{15,11},{16,20},{28,... | collective-permute-start | bytes 1179656 | tf_op jit(solution)/shard_map/ppermute | solution.py:115
  114.7 6.8 %collective-permute-start.23 = (bf16[192,1024]{1,0:T(8,128)(2,1)S(1)}, bf16[192,1024]{1,0:T(8,128)(2,1)S(1)}, u32[]{:S(2)}, u32[]{:S(2)}) collective-permute-start(bf16[192,1024]{1,0:T(8,128)(2,1)S(1)} %add_convert_fusion.4.refs_0_), channel_id=1, source_target_pairs={{0,8},{12,4},{1,9},{13,5},{2,10},{14,6},{3,11},{15,7},{16,24},{28,... | collective-permute-start | bytes 1179656 | tf_op jit(solution)/shard_map/ppermute | solution.py:115
  125.3 2.6 %collective-permute-start.27 = (bf16[192,1024]{1,0:T(8,128)(2,1)S(1)}, bf16[192,1024]{1,0:T(8,128)(2,1)S(1)}, u32[]{:S(2)}, u32[]{:S(2)}) collective-permute-start(bf16[192,1024]{1,0:T(8,128)(2,1)S(1)} %add_convert_fusion.1), channel_id=1, source_target_pairs={{0,4},{4,0},{8,12},{12,8},{1,5},{5,1},{9,13},{13,9},{2,6},{6,2},{1... | collective-permute-start | bytes 1179656 | tf_op jit(solution)/shard_map/ppermute | solution.py:115
  127.9 2.6 %collective-permute-done.20 = bf16[192,1024]{1,0:T(8,128)(2,1)S(1)} collective-permute-done((bf16[192,1024]{1,0:T(8,128)(2,1)S(1)}, bf16[192,1024]{1,0:T(8,128)(2,1)S(1)}, u32[]{:S(2)}, u32[]{:S(2)}) %collective-permute-start.20) | collective-permute-done | bytes 393248 | tf_op jit(solution)/shard_map/ppermute | solution.py:107
  130.5 9.1 %collective-permute-done.25 = bf16[192,1024]{1,0:T(8,128)(2,1)S(1)} collective-permute-done((bf16[192,1024]{1,0:T(8,128)(2,1)S(1)}, bf16[192,1024]{1,0:T(8,128)(2,1)S(1)}, u32[]{:S(2)}, u32[]{:S(2)}) %collective-permute-start.25) | collective-permute-done | bytes 393248 | tf_op jit(solution)/shard_map/ppermute | solution.py:115
  139.9 2.5 %collective-permute-done.27 = bf16[192,1024]{1,0:T(8,128)(2,1)S(1)} collective-permute-done((bf16[192,1024]{1,0:T(8,128)(2,1)S(1)}, bf16[192,1024]{1,0:T(8,128)(2,1)S(1)}, u32[]{:S(2)}, u32[]{:S(2)}) %collective-permute-start.27) | collective-permute-done | bytes 393248 | tf_op jit(solution)/shard_map/ppermute | solution.py:115
  (108 shorter events, 44.3 us)
Async XLA Ops:
  4.5 21.4 %collective-permute-start = (bf16[400,1024]{1,0:T(8,128)(2,1)S(1)}, bf16[400,1024]{1,0:T(8,128)(2,1)}, u32[]{:S(2)}, u32[]{:S(2)}) collective-permute-start(bf16[400,1024]{1,0:T(8,128)(2,1)S(1)} %shard_map.91.refs_1_.refs_4_.refs_5_), channel_id=1, source_target_pairs={{0,4},{4,0},{8,12},{12,8},{1,5},{5,1},{9,13},{13,9},{2,6},{6,2},{1... | collective-permute-start | bytes 2457608 | tf_op jit(solution)/shard_map/ppermute | solution.py:115
  7.6 21.6 %collective-permute-start.3 = (bf16[400,1024]{1,0:T(8,128)(2,1)S(1)}, bf16[400,1024]{1,0:T(8,128)(2,1)}, u32[]{:S(2)}, u32[]{:S(2)}) collective-permute-start(bf16[400,1024]{1,0:T(8,128)(2,1)S(1)} %shard_map.91.refs_1_.refs_4_.refs_5_), channel_id=1, source_target_pairs={{4,8},{8,4},{5,9},{9,5},{6,10},{10,6},{7,11},{11,7},{20,24},{24,20... | collective-permute-start | bytes 2457608 | tf_op jit(solution)/shard_map/ppermute | solution.py:115
  9.2 21.3 %collective-permute-start.7 = (bf16[384,1024]{1,0:T(8,128)(2,1)}, bf16[384,1024]{1,0:T(8,128)(2,1)}, u32[]{:S(2)}, u32[]{:S(2)}) collective-permute-start(bf16[384,1024]{1,0:T(8,128)(2,1)} %refs_0_.1), channel_id=1, source_target_pairs={{0,2},{1,3},{2,0},{3,1},{4,6},{5,7},{6,4},{7,5},{8,10},{9,11},{10,... | collective-permute-start | bytes 2359304 | tf_op jit(solution)/shard_map/ppermute | solution.py:107
  16.8 24.1 %collective-permute-start.9 = (bf16[2048,512]{1,0:T(8,128)(2,1)}, bf16[2048,512]{1,0:T(8,128)(2,1)S(1)}, u32[]{:S(2)}, u32[]{:S(2)}) collective-permute-start(bf16[2048,512]{1,0:T(8,128)(2,1)} %shard_map.93), channel_id=1, source_target_pairs={{0,1},{1,0},{2,3},{3,2},{4,5},{5,4},{6,7},{7,6},{8,9},{9,8},{10,11... | collective-permute-start | bytes 6291464 | tf_op jit(solution)/shard_map/ppermute | solution.py:111
  26.0 25.1 %collective-permute-start.6 = (bf16[400,1024]{1,0:T(8,128)(2,1)}, bf16[400,1024]{1,0:T(8,128)(2,1)}, u32[]{:S(2)}, u32[]{:S(2)}) collective-permute-start(bf16[400,1024]{1,0:T(8,128)(2,1)} %collective-permute-done.refs_0_.refs_6_.refs_7_), channel_id=1, source_target_pairs={{0,2},{1,3},{2,0},{3,1},{4,6},{5,7},{6,4},{7,5},{8,10},{9,11},{10,... | collective-permute-start | bytes 2457608 | tf_op jit(solution)/shard_map/ppermute | solution.py:107
  27.6 11.7 %collective-permute-start.1 = (bf16[400,1024]{1,0:T(8,128)(2,1)}, bf16[400,1024]{1,0:T(8,128)(2,1)}, u32[]{:S(2)}, u32[]{:S(2)}) collective-permute-start(bf16[400,1024]{1,0:T(8,128)(2,1)} %collective-permute-done.refs_0_.refs_6_.refs_7_), channel_id=1, source_target_pairs={{4,8},{8,4},{5,9},{9,5},{6,10},{10,6},{7,11},{11,7},{20,24},{24,20... | collective-permute-start | bytes 2457608 | tf_op jit(solution)/shard_map/ppermute | solution.py:115
  29.2 21.9 %collective-permute-start.5 = (bf16[400,1024]{1,0:T(8,128)(2,1)}, bf16[400,1024]{1,0:T(8,128)(2,1)}, u32[]{:S(2)}, u32[]{:S(2)}) collective-permute-start(bf16[400,1024]{1,0:T(8,128)(2,1)} %collective-permute-done.3.refs_0_.refs_8_), channel_id=1, source_target_pairs={{4,0},{8,12},{5,1},{9,13},{6,2},{10,14},{7,3},{11,15},{20,16},{24,... | collective-permute-start | bytes 2457608 | tf_op jit(solution)/shard_map/ppermute | solution.py:115
  32.5 15.5 %collective-permute-start.8 = (bf16[192,1024]{1,0:T(8,128)(2,1)S(1)}, bf16[192,1024]{1,0:T(8,128)(2,1)S(1)}, u32[]{:S(2)}, u32[]{:S(2)}) collective-permute-start(bf16[192,1024]{1,0:T(8,128)(2,1)S(1)} %shard_map.92), channel_id=1, source_target_pairs={{0,4},{12,8},{1,5},{13,9},{2,6},{14,10},{3,7},{15,11},{16,20},{28,... | collective-permute-start | bytes 1179656 | tf_op jit(solution)/shard_map/ppermute | solution.py:115
  39.3 21.1 %collective-permute-start.4 = (bf16[400,1024]{1,0:T(8,128)(2,1)}, bf16[400,1024]{1,0:T(8,128)(2,1)}, u32[]{:S(2)}, u32[]{:S(2)}) collective-permute-start(bf16[400,1024]{1,0:T(8,128)(2,1)} %collective-permute-done.3.refs_0_.refs_8_), channel_id=1, source_target_pairs={{4,6},{5,7},{6,4},{7,5},{8,10},{9,11},{10,8},{11,9},{20,22},{21,23... | collective-permute-start | bytes 2457608 | tf_op jit(solution)/shard_map/ppermute | solution.py:461
  40.9 29.3 %collective-permute-start.2 = (bf16[400,1024]{1,0:T(8,128)(2,1)}, bf16[400,1024]{1,0:T(8,128)(2,1)}, u32[]{:S(2)}, u32[]{:S(2)}) collective-permute-start(bf16[400,1024]{1,0:T(8,128)(2,1)} %collective-permute-done.1.refs_2_.inner_ref.refs_0_), channel_id=1, source_target_pairs={{4,0},{8,12},{5,1},{9,13},{6,2},{10,14},{7,3},{11,15},{20,16},{24,... | collective-permute-start | bytes 2457608 | tf_op jit(solution)/shard_map/ppermute | solution.py:115
  52.2 20.0 %collective-permute-start.10 = (bf16[400,1024]{1,0:T(8,128)(2,1)}, bf16[400,1024]{1,0:T(8,128)(2,1)S(1)}, u32[]{:S(2)}, u32[]{:S(2)}) collective-permute-start(bf16[400,1024]{1,0:T(8,128)(2,1)} %shard_map.95.refs_1_.refs_9_), channel_id=1, source_target_pairs={{0,2},{1,3},{2,0},{3,1},{12,14},{13,15},{14,12},{15,13},{16,18},{1... | collective-permute-start | bytes 2457608 | tf_op jit(solution)/shard_map/ppermute | solution.py:461
  55.3 22.4 %collective-permute-start.14 = (bf16[384,1024]{1,0:T(8,128)(2,1)}, bf16[384,1024]{1,0:T(8,128)(2,1)S(1)}, u32[]{:S(2)}, u32[]{:S(2)}) collective-permute-start(bf16[384,1024]{1,0:T(8,128)(2,1)} %copy-done.15), channel_id=1, source_target_pairs={{0,1},{1,0},{2,3},{3,2},{4,5},{5,4},{6,7},{7,6},{8,9},{9,8},{10,11... | collective-permute-start | bytes 2359304 | tf_op jit(solution)/shard_map/ppermute | solution.py:111
  59.9 18.2 %collective-permute-start.15 = (bf16[384,1024]{1,0:T(8,128)(2,1)S(1)}, bf16[384,1024]{1,0:T(8,128)(2,1)S(1)}, u32[]{:S(2)}, u32[]{:S(2)}) collective-permute-start(bf16[384,1024]{1,0:T(8,128)(2,1)S(1)} %get-tuple-element.36), channel_id=1, source_target_pairs={{0,1},{1,0},{2,3},{3,2},{4,5},{5,4},{6,7},{7,6},{8,9},{9,8},{10,11... | collective-permute-start | bytes 2359304 | tf_op jit(solution)/shard_map/ppermute | solution.py:111
  60.4 24.4 %collective-permute-start.13 = (bf16[192,1024]{1,0:T(8,128)(2,1)S(1)}, bf16[192,1024]{1,0:T(8,128)(2,1)S(1)}, u32[]{:S(2)}, u32[]{:S(2)}) collective-permute-start(bf16[192,1024]{1,0:T(8,128)(2,1)S(1)} %collective-permute-done.11.rest_2_.refs_1_), channel_id=1, source_target_pairs={{4,0},{8,12},{5,1},{9,13},{6,2},{10,14},{7,3},{11,15},{20,16},{24,... | collective-permute-start | bytes 1179656 | tf_op jit(solution)/shard_map/ppermute | solution.py:115
  74.2 10.6 %collective-permute-start.12 = (bf16[192,1024]{1,0:T(8,128)(2,1)S(1)}, bf16[192,1024]{1,0:T(8,128)(2,1)S(1)}, u32[]{:S(2)}, u32[]{:S(2)}) collective-permute-start(bf16[192,1024]{1,0:T(8,128)(2,1)S(1)} %shard_map.97), channel_id=1, source_target_pairs={{0,2},{1,3},{2,0},{3,1},{4,6},{5,7},{6,4},{7,5},{8,10},{9,11},{10,... | collective-permute-start | bytes 1179656 | tf_op jit(solution)/shard_map/ppermute | solution.py:107
  74.8 16.7 %collective-permute-start.18 = (bf16[256,2048]{1,0:T(8,128)(2,1)S(1)}, bf16[256,2048]{1,0:T(8,128)(2,1)S(1)}, u32[]{:S(2)}, u32[]{:S(2)}) collective-permute-start(bf16[256,2048]{1,0:T(8,128)(2,1)S(1)} %copy-done.6), channel_id=1, source_target_pairs={{0,1},{1,0},{2,3},{3,2},{4,5},{5,4},{6,7},{7,6},{8,9},{9,8},{10,11... | collective-permute-start | bytes 3145736 | tf_op jit(solution)/shard_map/ppermute | solution.py:111
  94.2 12.1 %collective-permute-start.21 = (bf16[192,1024]{1,0:T(8,128)(2,1)S(1)}, bf16[192,1024]{1,0:T(8,128)(2,1)S(1)}, u32[]{:S(2)}, u32[]{:S(2)}) collective-permute-start(bf16[192,1024]{1,0:T(8,128)(2,1)S(1)} %get-tuple-element.50), channel_id=1, source_target_pairs={{0,2},{1,3},{2,0},{3,1},{4,6},{5,7},{6,4},{7,5},{8,10},{9,11},{10,... | collective-permute-start | bytes 1179656 | tf_op jit(solution)/shard_map/ppermute | solution.py:107
  96.7 17.9 %collective-permute-start.19 = (bf16[192,1024]{1,0:T(8,128)(2,1)S(1)}, bf16[192,1024]{1,0:T(8,128)(2,1)S(1)}, u32[]{:S(2)}, u32[]{:S(2)}) collective-permute-start(bf16[192,1024]{1,0:T(8,128)(2,1)S(1)} %get-tuple-element.46), channel_id=1, source_target_pairs={{0,2},{1,3},{2,0},{3,1},{4,6},{5,7},{6,4},{7,5},{8,10},{9,11},{10,... | collective-permute-start | bytes 1179656 | tf_op jit(solution)/shard_map/ppermute | solution.py:107
  106.3 17.4 %collective-permute-start.24 = (bf16[192,1024]{1,0:T(8,128)(2,1)S(1)}, bf16[192,1024]{1,0:T(8,128)(2,1)S(1)}, u32[]{:S(2)}, u32[]{:S(2)}) collective-permute-start(bf16[192,1024]{1,0:T(8,128)(2,1)S(1)} %add_convert_fusion.3), channel_id=1, source_target_pairs={{0,4},{12,8},{1,5},{13,9},{2,6},{14,10},{3,7},{15,11},{16,20},{28,... | collective-permute-start | bytes 1179656 | tf_op jit(solution)/shard_map/ppermute | solution.py:115
  112.1 13.0 %collective-permute-start.26 = (bf16[192,1024]{1,0:T(8,128)(2,1)S(1)}, bf16[192,1024]{1,0:T(8,128)(2,1)S(1)}, u32[]{:S(2)}, u32[]{:S(2)}) collective-permute-start(bf16[192,1024]{1,0:T(8,128)(2,1)S(1)} %get-tuple-element.52), channel_id=1, source_target_pairs={{0,2},{1,3},{2,0},{3,1},{4,6},{5,7},{6,4},{7,5},{8,10},{9,11},{10,... | collective-permute-start | bytes 1179656 | tf_op jit(solution)/shard_map/ppermute | solution.py:107
  113.7 14.2 %collective-permute-start.22 = (bf16[192,1024]{1,0:T(8,128)(2,1)S(1)}, bf16[192,1024]{1,0:T(8,128)(2,1)S(1)}, u32[]{:S(2)}, u32[]{:S(2)}) collective-permute-start(bf16[192,1024]{1,0:T(8,128)(2,1)S(1)} %add_convert_fusion.3), channel_id=1, source_target_pairs={{4,8},{8,4},{5,9},{9,5},{6,10},{10,6},{7,11},{11,7},{20,24},{24,20... | collective-permute-start | bytes 1179656 | tf_op jit(solution)/shard_map/ppermute | solution.py:115
  114.7 15.8 %collective-permute-start.23 = (bf16[192,1024]{1,0:T(8,128)(2,1)S(1)}, bf16[192,1024]{1,0:T(8,128)(2,1)S(1)}, u32[]{:S(2)}, u32[]{:S(2)}) collective-permute-start(bf16[192,1024]{1,0:T(8,128)(2,1)S(1)} %add_convert_fusion.4.refs_0_), channel_id=1, source_target_pairs={{0,8},{12,4},{1,9},{13,5},{2,10},{14,6},{3,11},{15,7},{16,24},{28,... | collective-permute-start | bytes 1179656 | tf_op jit(solution)/shard_map/ppermute | solution.py:115
  123.9 15.8 %collective-permute-start.25 = (bf16[192,1024]{1,0:T(8,128)(2,1)S(1)}, bf16[192,1024]{1,0:T(8,128)(2,1)S(1)}, u32[]{:S(2)}, u32[]{:S(2)}) collective-permute-start(bf16[192,1024]{1,0:T(8,128)(2,1)S(1)} %add_convert_fusion.2), channel_id=1, source_target_pairs={{4,12},{8,0},{5,13},{9,1},{6,14},{10,2},{7,15},{11,3},{20,28},{24,... | collective-permute-start | bytes 1179656 | tf_op jit(solution)/shard_map/ppermute | solution.py:115
  125.3 17.1 %collective-permute-start.27 = (bf16[192,1024]{1,0:T(8,128)(2,1)S(1)}, bf16[192,1024]{1,0:T(8,128)(2,1)S(1)}, u32[]{:S(2)}, u32[]{:S(2)}) collective-permute-start(bf16[192,1024]{1,0:T(8,128)(2,1)S(1)} %add_convert_fusion.1), channel_id=1, source_target_pairs={{0,4},{4,0},{8,12},{12,8},{1,5},{5,1},{9,13},{13,9},{2,6},{6,2},{1... | collective-permute-start | bytes 1179656 | tf_op jit(solution)/shard_map/ppermute | solution.py:115
  (27 other events, 124.4 us)

commit v22 on v20

--- a/solution.py
+++ b/solution.py
@@ -525,8 +525,9 @@
     two_out = along(passed.astype(jnp.bfloat16), TWO_OUT)
     beside = along(third, BESIDE)
     arrived = [block.astype(jnp.float32) for block in (middle, two_in, two_out)]
-    total = lax.optimization_barrier(joined(*last_chunk(second)) + sum(arrived))
-    return (total + beside.astype(jnp.float32)).astype(jnp.bfloat16)
+    total = lax.optimization_barrier(sum(arrived))
+    own_sum = joined(*last_chunk(second))
+    return (total + own_sum + beside.astype(jnp.float32)).astype(jnp.bfloat16)
 
 
 def on_device(*args):

time: 143 us -> 144 us (level)
    ppermute x13, waiting for transfers between devices: 31.7 us -> 34.4 us  [along(): return lax.ppermute(block, 'blk', route)]
    ppermute x7, waiting for transfers between devices: 11.8 us -> 9.17 us  [across_chips(): return lax.ppermute(block, 'tp', [(i, i ^ 2) for i in range(4)])]
  transfers between devices with their start and end apart: 28 -> 28, of which waited for: 10 -> 10; matrix products, arithmetic and copies ran while one was open for 7% -> 6% of each run, Pallas kernels for 18% -> 17%
where the time goes in v22:
time: 144 us; the launch traced here: 143 us
  starting transfers between devices  48.8 us (34%)
  waiting for transfers between devices  44.7 us (31%)
  Pallas kernels  29.4 us (20%)
  local copies, waits for them, and re-layouts  15.9 us (11%)
  other arithmetic  3.36 us (2%)
    ppermute x13, starting transfers between devices, along(): return lax.ppermute(block, 'blk', route)  34.5 us
    ppermute x13, waiting for transfers between devices, along(): return lax.ppermute(block, 'blk', route)  34.4 us
    pallas_call x5, Pallas kernels, partial_sums(): return on_core(body, shapes + [TOKEN], specs)(*operands, *waits)  15.2 us
    ppermute x7, waiting for transfers between devices, across_chips(): return lax.ppermute(block, 'tp', [(i, i ^ 2) for i in range(4)])  9.17 us
    ppermute x7, starting transfers between devices, across_chips(): return lax.ppermute(block, 'tp', [(i, i ^ 2) for i in range(4)])  9 us
    unnamed x46, local copies, waits for them, and re-layouts  9 us
    ppermute x2, starting transfers between devices, at_kind(): return lax.ppermute(block, ('blk', 'tp'), pairs)  4.14 us
    pallas_call x2, Pallas kernels, part_of(): pl.pallas_call(body, out_shape=shape, in_specs=[SMEM] + [ANYWHERE] * (2 +...  3.98 us
  transfers between devices with their start and end apart: 28, of which 10 were waited for; matrix products, arithmetic and copies ran while one was open for 6% of the time, Pallas kernels for 17%

profile of v22, /device:TPU:0, one launch (start us, length us, event | category | flops | bytes accessed | tf_op | source)
XLA Modules:
  0.0 142.6 jit_solution(7197844292156579315)
XLA Ops:
  4.5 3.1 %collective-permute-start = (bf16[400,1024]{1,0:T(8,128)(2,1)S(1)}, bf16[400,1024]{1,0:T(8,128)(2,1)}, u32[]{:S(2)}, u32[]{:S(2)}) collective-permute-start(bf16[400,1024]{1,0:T(8,128)(2,1)S(1)} %shard_map.91.refs_1_.refs_4_.refs_5_), channel_id=1, source_target_pairs={{0,4},{4,0},{8,12},{12,8},{1,5},{5,1},{9,13},{13,9},{2,6},{6,2},{1... | collective-permute-start | bytes 2457608 | tf_op jit(solution)/shard_map/ppermute | solution.py:115
  10.7 3.4 %dynamic-slice_bitcast_fusion.6 = (bf16[1024,256]{1,0:T(8,128)(2,1)S(1)}, bf16[1024,256]{1,0:T(8,128)(2,1)S(1)}, bf16[1024,256]{1,0:T(8,128)(2,1)S(1)}, bf16[102...) fusion(bf16[4,1024,256]{2,1,0:T(8,128)(2,1)} %bitcast.32, ...), kind=kLoop, calls=%fused_computation.17 | loop fusion | bytes 8388624 | tf_op jit(solution)/shard_map/jit(dynamic_index_in_dim)/squeeze | solution.py:443
  16.3 2.8 %dynamic-slice_bitcast_fusion.1 = (bf16[256,1024]{1,0:T(8,128)(2,1)}, bf16[256,1024]{1,0:T(8,128)(2,1)S(1)}, bf16[256,1024]{1,0:T(8,128)(2,1)S(1)}, bf16[256,1024]{1,0:T(8,128)(2,1)}) fusion(bf16[1,256,4096]{2,1,0:T(8,128)(2,1)} %param.12, s32[]{:T(128)S(6)} %select_n.39, s32[]{:T(128)S(6)} %select_n.38, s32[]{:T(128)S(6)} %select_n.37, s32[]{:T(128)S(6)} %select_n.40), kind=kLoop, calls=%fused_computation.12 | loop fusion | bytes 4194320 | tf_op jit(solution)/shard_map/dynamic_slice | solution.py:449
  19.1 6.9 %collective-permute-done.refs_0_.refs_6_.refs_7_ = bf16[400,1024]{1,0:T(8,128)(2,1)} collective-permute-done((bf16[400,1024]{1,0:T(8,128)(2,1)S(1)}, bf16[400,1024]{1,0:T(8,128)(2,1)}, u32[]{:S(2)}, u32[]{:S(2)}) %collective-permute-start) | collective-permute-done | bytes 819232 | tf_op jit(solution)/shard_map/ppermute | solution.py:115
  30.5 2.0 %shard_map.92 = bf16[192,1024]{1,0:T(8,128)(2,1)S(1)} custom-call(s32[9]{0:T(128)S(1)} %fusion.plan_ref, bf16[384,1024]{1,0:T(8,128)(2,1)} %collective-permute-done.7.inner_ref.outer_ref.refs_1_, bf16[384,1024]{1,0:T(8,128)(2,1)} %collective-permute-done.7.inner_ref.outer_ref.refs_1_), custom_call_target="tpu_custom_call" | custom-call | flops 17179869184 | bytes 1024 | tf_op jit(solution)/shard_map/pallas_call | solution.py:192
  32.5 6.5 %collective-permute-start.8 = (bf16[192,1024]{1,0:T(8,128)(2,1)S(1)}, bf16[192,1024]{1,0:T(8,128)(2,1)S(1)}, u32[]{:S(2)}, u32[]{:S(2)}) collective-permute-start(bf16[192,1024]{1,0:T(8,128)(2,1)S(1)} %shard_map.92), channel_id=1, source_target_pairs={{0,4},{12,8},{1,5},{13,9},{2,6},{14,10},{3,7},{15,11},{16,20},{28,... | collective-permute-start | bytes 1179656 | tf_op jit(solution)/shard_map/ppermute | solution.py:115
  42.2 3.2 %shard_map.94 = (f32[384,1024]{1,0:T(8,128)S(1)}, bf16[384,1024]{1,0:T(8,128)(2,1)S(1)}, f32[8,128]{1,0:T(8,128)S(1)}) custom-call(s32[9]{0:T(128)S(1)} %fusion.plan_ref, bf16[384,1024]{1,0:T(8,128)(2,1)} %refs_0_.1, bf16[384,1024]{1,0:T(8,128)(2,1)} %collective-permute-done.7.inner_ref.outer_ref.refs_1_, ...), custom_call_target="tpu_custom_call" | custom-call | flops 1024 | bytes 1024 | tf_op jit(solution)/shard_map/pallas_call | solution.py:287
  48.8 2.3 %collective-permute-done.5.refs_0_ = bf16[400,1024]{1,0:T(8,128)(2,1)} collective-permute-done((bf16[400,1024]{1,0:T(8,128)(2,1)}, bf16[400,1024]{1,0:T(8,128)(2,1)}, u32[]{:S(2)}, u32[]{:S(2)}) %collective-permute-start.5) | collective-permute-done | bytes 819232 | tf_op jit(solution)/shard_map/ppermute | solution.py:115
  51.1 2.6 %collective-permute-start.10 = (bf16[400,1024]{1,0:T(8,128)(2,1)}, bf16[400,1024]{1,0:T(8,128)(2,1)S(1)}, u32[]{:S(2)}, u32[]{:S(2)}) collective-permute-start(bf16[400,1024]{1,0:T(8,128)(2,1)} %shard_map.95.refs_1_.refs_9_), channel_id=1, source_target_pairs={{0,2},{1,3},{2,0},{3,1},{12,14},{13,15},{14,12},{15,13},{16,18},{1... | collective-permute-start | bytes 2457608 | tf_op jit(solution)/shard_map/ppermute | solution.py:457
  55.7 3.2 %shard_map.96 = (f32[384,1024]{1,0:T(8,128)S(1)}, bf16[384,1024]{1,0:T(8,128)(2,1)S(1)}, f32[8,128]{1,0:T(8,128)S(1)}) custom-call(s32[9]{0:T(128)S(1)} %fusion.plan_ref, bf16[400,1024]{1,0:T(8,128)(2,1)} %collective-permute-done.refs_0_.refs_6_.refs_7_, bf16[400,1024]{1,0:T(8,128)(2,1)} %collective-permute-done.6.refs_1_, ...), custom_call_target="tpu_custom_call" | custom-call | flops 1024 | bytes 1024 | tf_op jit(solution)/shard_map/pallas_call | solution.py:287
  60.8 9.4 %collective-permute-done.2.outer_ref.refs_1_ = bf16[400,1024]{1,0:T(8,128)(2,1)} collective-permute-done((bf16[400,1024]{1,0:T(8,128)(2,1)}, bf16[400,1024]{1,0:T(8,128)(2,1)}, u32[]{:S(2)}, u32[]{:S(2)}) %collective-permute-start.2) | collective-permute-done | bytes 819232 | tf_op jit(solution)/shard_map/ppermute | solution.py:115
  71.3 2.0 %shard_map.97 = bf16[192,1024]{1,0:T(8,128)(2,1)S(1)} custom-call(s32[9]{0:T(128)S(1)} %fusion.plan_ref, bf16[400,1024]{1,0:T(8,128)(2,1)} %collective-permute-done.1.refs_2_.inner_ref.refs_0_, bf16[400,1024]{1,0:T(8,128)(2,1)} %collective-permute-done.2.outer_ref.refs_1_, bf16[400,1024]{1,0:T(8,128)(2,1)} %collective-permute-done.4.rest_0_.refs_2_, ...), custom_call_target="tpu_custom_call" | custom-call | flops 1024 | bytes 1024 | tf_op jit(solution)/shard_map/pallas_call | solution.py:192
  73.9 2.9 %shard_map.98 = (f32[384,1024]{1,0:T(8,128)S(1)}, f32[8,128]{1,0:T(8,128)}) custom-call(s32[9]{0:T(128)S(1)} %fusion.plan_ref, bf16[400,1024]{1,0:T(8,128)(2,1)} %collective-permute-done.1.refs_2_.inner_ref.refs_0_, bf16[400,1024]{1,0:T(8,128)(2,1)} %collective-permute-done.2.outer_ref.refs_1_, bf16[1024,512]{1,0:T(8,128)(2,1)S(1)} %pad_maximum_fusion.refs_2_.refs_4_, ...), custom_call_target="tpu_custom_call" | custom-call | flops 1024 | bytes 1024 | tf_op jit(solution)/shard_map/pallas_call | solution.py:287
  78.0 4.0 %shard_map.102 = (f32[384,1024]{1,0:T(8,128)S(1)}, bf16[384,1024]{1,0:T(8,128)(2,1)S(1)}, f32[8,128]{1,0:T(8,128)}) custom-call(s32[9]{0:T(128)S(1)} %fusion.plan_ref, bf16[400,1024]{1,0:T(8,128)(2,1)} %collective-permute-done.3.refs_0_.refs_8_, bf16[400,1024]{1,0:T(8,128)(2,1)} %shard_map.95.refs_1_.refs_9_, ...), custom_call_target="tpu_custom_call" | custom-call | flops 1024 | bytes 1024 | tf_op jit(solution)/shard_map/pallas_call | solution.py:287
  84.0 2.0 %shard_map.101 = (f32[384,1024]{1,0:T(8,128)S(1)}, bf16[384,1024]{1,0:T(8,128)(2,1)S(1)}, f32[8,128]{1,0:T(8,128)}) custom-call(s32[9]{0:T(128)S(1)} %fusion.plan_ref, bf16[192,1024]{1,0:T(8,128)(2,1)S(1)} %collective-permute-done.12.refs_0_, bf16[192,1024]{1,0:T(8,128)(2,1)S(1)} %collective-permute-done.11.rest_2_.refs_1_, ...), custom_call_target="tpu_custom_call" | custom-call | flops 1024 | bytes 1024 | tf_op jit(solution)/shard_map/pallas_call | solution.py:287
  87.2 3.5 %shard_map.103.before_ref = f32[768,512]{1,0:T(8,128)S(1)} custom-call(s32[9]{0:T(128)S(1)} %fusion.plan_ref, bf16[384,512]{1,0:T(8,128)(2,1)S(1)} %get-tuple-element.40.refs_0_, bf16[384,512]{1,0:T(8,128)(2,1)S(1)} %get-tuple-element.41.refs_1_, f32[384,1024]{1,0:T(8,128)S(1)} %get-tuple-element.42.refs_2_, ...), custom_call_target="tpu_custom_call" | custom-call | flops 1024 | bytes 1024 | tf_op jit(solution)/shard_map/pallas_call | solution.py:373
  90.7 2.6 %shard_map.104 = (bf16[192,1024]{1,0:T(8,128)(2,1)S(1)}, f32[192,1024]{1,0:T(8,128)S(1)}, bf16[576,512]{1,0:T(8,128)(2,1)S(1)}) custom-call(s32[9]{0:T(128)S(1)} %fusion.plan_ref, f32[384,1024]{1,0:T(8,128)S(1)} %get-tuple-element.38.sums_ref, bf16[384,1024]{1,0:T(8,128)(2,1)S(1)} %collective-permute-done.16.got_ref, ...), custom_call_target="tpu_custom_call" | custom-call | flops 1024 | bytes 1024 | tf_op jit(solution)/shard_map/pallas_call | solution.py:412
  96.5 8.9 %collective-permute-done.19 = bf16[192,1024]{1,0:T(8,128)(2,1)S(1)} collective-permute-done((bf16[192,1024]{1,0:T(8,128)(2,1)S(1)}, bf16[192,1024]{1,0:T(8,128)(2,1)S(1)}, u32[]{:S(2)}, u32[]{:S(2)}) %collective-permute-start.19) | collective-permute-done | bytes 393248 | tf_op jit(solution)/shard_map/ppermute | solution.py:107
  105.5 5.8 %collective-permute-start.23 = (bf16[192,1024]{1,0:T(8,128)(2,1)S(1)}, bf16[192,1024]{1,0:T(8,128)(2,1)S(1)}, u32[]{:S(2)}, u32[]{:S(2)}) collective-permute-start(bf16[192,1024]{1,0:T(8,128)(2,1)S(1)} %add_convert_fusion.4), channel_id=1, source_target_pairs={{0,4},{12,8},{1,5},{13,9},{2,6},{14,10},{3,7},{15,11},{16,20},{28,... | collective-permute-start | bytes 1179656 | tf_op jit(solution)/shard_map/ppermute | solution.py:115
  113.9 6.8 %collective-permute-start.22 = (bf16[192,1024]{1,0:T(8,128)(2,1)S(1)}, bf16[192,1024]{1,0:T(8,128)(2,1)S(1)}, u32[]{:S(2)}, u32[]{:S(2)}) collective-permute-start(bf16[192,1024]{1,0:T(8,128)(2,1)S(1)} %add_convert_fusion.3.refs_0_), channel_id=1, source_target_pairs={{0,8},{12,4},{1,9},{13,5},{2,10},{14,6},{3,11},{15,7},{16,24},{28,... | collective-permute-start | bytes 1179656 | tf_op jit(solution)/shard_map/ppermute | solution.py:115
  124.5 2.6 %collective-permute-start.27 = (bf16[192,1024]{1,0:T(8,128)(2,1)S(1)}, bf16[192,1024]{1,0:T(8,128)(2,1)S(1)}, u32[]{:S(2)}, u32[]{:S(2)}) collective-permute-start(bf16[192,1024]{1,0:T(8,128)(2,1)S(1)} %add_convert_fusion.1), channel_id=1, source_target_pairs={{0,4},{4,0},{8,12},{12,8},{1,5},{5,1},{9,13},{13,9},{2,6},{6,2},{1... | collective-permute-start | bytes 1179656 | tf_op jit(solution)/shard_map/ppermute | solution.py:115
  127.1 2.6 %collective-permute-done.22 = bf16[192,1024]{1,0:T(8,128)(2,1)S(1)} collective-permute-done((bf16[192,1024]{1,0:T(8,128)(2,1)S(1)}, bf16[192,1024]{1,0:T(8,128)(2,1)S(1)}, u32[]{:S(2)}, u32[]{:S(2)}) %collective-permute-start.22) | collective-permute-done | bytes 393248 | tf_op jit(solution)/shard_map/ppermute | solution.py:115
  129.7 9.2 %collective-permute-done.24 = bf16[192,1024]{1,0:T(8,128)(2,1)S(1)} collective-permute-done((bf16[192,1024]{1,0:T(8,128)(2,1)S(1)}, bf16[192,1024]{1,0:T(8,128)(2,1)S(1)}, u32[]{:S(2)}, u32[]{:S(2)}) %collective-permute-start.24) | collective-permute-done | bytes 393248 | tf_op jit(solution)/shard_map/ppermute | solution.py:115
  139.0 2.6 %collective-permute-done.27 = bf16[192,1024]{1,0:T(8,128)(2,1)S(1)} collective-permute-done((bf16[192,1024]{1,0:T(8,128)(2,1)S(1)}, bf16[192,1024]{1,0:T(8,128)(2,1)S(1)}, u32[]{:S(2)}, u32[]{:S(2)}) %collective-permute-start.27) | collective-permute-done | bytes 393248 | tf_op jit(solution)/shard_map/ppermute | solution.py:115
  (108 shorter events, 41.4 us)
Async XLA Ops:
  4.5 21.4 %collective-permute-start = (bf16[400,1024]{1,0:T(8,128)(2,1)S(1)}, bf16[400,1024]{1,0:T(8,128)(2,1)}, u32[]{:S(2)}, u32[]{:S(2)}) collective-permute-start(bf16[400,1024]{1,0:T(8,128)(2,1)S(1)} %shard_map.91.refs_1_.refs_4_.refs_5_), channel_id=1, source_target_pairs={{0,4},{4,0},{8,12},{12,8},{1,5},{5,1},{9,13},{13,9},{2,6},{6,2},{1... | collective-permute-start | bytes 2457608 | tf_op jit(solution)/shard_map/ppermute | solution.py:115
  7.6 21.6 %collective-permute-start.3 = (bf16[400,1024]{1,0:T(8,128)(2,1)S(1)}, bf16[400,1024]{1,0:T(8,128)(2,1)}, u32[]{:S(2)}, u32[]{:S(2)}) collective-permute-start(bf16[400,1024]{1,0:T(8,128)(2,1)S(1)} %shard_map.91.refs_1_.refs_4_.refs_5_), channel_id=1, source_target_pairs={{4,8},{8,4},{5,9},{9,5},{6,10},{10,6},{7,11},{11,7},{20,24},{24,20... | collective-permute-start | bytes 2457608 | tf_op jit(solution)/shard_map/ppermute | solution.py:115
  9.2 21.3 %collective-permute-start.7 = (bf16[384,1024]{1,0:T(8,128)(2,1)}, bf16[384,1024]{1,0:T(8,128)(2,1)}, u32[]{:S(2)}, u32[]{:S(2)}) collective-permute-start(bf16[384,1024]{1,0:T(8,128)(2,1)} %refs_0_.1), channel_id=1, source_target_pairs={{0,2},{1,3},{2,0},{3,1},{4,6},{5,7},{6,4},{7,5},{8,10},{9,11},{10,... | collective-permute-start | bytes 2359304 | tf_op jit(solution)/shard_map/ppermute | solution.py:107
  15.7 25.2 %collective-permute-start.9 = (bf16[2048,512]{1,0:T(8,128)(2,1)}, bf16[2048,512]{1,0:T(8,128)(2,1)S(1)}, u32[]{:S(2)}, u32[]{:S(2)}) collective-permute-start(bf16[2048,512]{1,0:T(8,128)(2,1)} %shard_map.93), channel_id=1, source_target_pairs={{0,1},{1,0},{2,3},{3,2},{4,5},{5,4},{6,7},{7,6},{8,9},{9,8},{10,11... | collective-permute-start | bytes 6291464 | tf_op jit(solution)/shard_map/ppermute | solution.py:111
  26.0 25.1 %collective-permute-start.6 = (bf16[400,1024]{1,0:T(8,128)(2,1)}, bf16[400,1024]{1,0:T(8,128)(2,1)}, u32[]{:S(2)}, u32[]{:S(2)}) collective-permute-start(bf16[400,1024]{1,0:T(8,128)(2,1)} %collective-permute-done.refs_0_.refs_6_.refs_7_), channel_id=1, source_target_pairs={{0,2},{1,3},{2,0},{3,1},{4,6},{5,7},{6,4},{7,5},{8,10},{9,11},{10,... | collective-permute-start | bytes 2457608 | tf_op jit(solution)/shard_map/ppermute | solution.py:107
  27.6 11.7 %collective-permute-start.1 = (bf16[400,1024]{1,0:T(8,128)(2,1)}, bf16[400,1024]{1,0:T(8,128)(2,1)}, u32[]{:S(2)}, u32[]{:S(2)}) collective-permute-start(bf16[400,1024]{1,0:T(8,128)(2,1)} %collective-permute-done.refs_0_.refs_6_.refs_7_), channel_id=1, source_target_pairs={{4,8},{8,4},{5,9},{9,5},{6,10},{10,6},{7,11},{11,7},{20,24},{24,20... | collective-permute-start | bytes 2457608 | tf_op jit(solution)/shard_map/ppermute | solution.py:115
  29.2 21.9 %collective-permute-start.5 = (bf16[400,1024]{1,0:T(8,128)(2,1)}, bf16[400,1024]{1,0:T(8,128)(2,1)}, u32[]{:S(2)}, u32[]{:S(2)}) collective-permute-start(bf16[400,1024]{1,0:T(8,128)(2,1)} %collective-permute-done.3.refs_0_.refs_8_), channel_id=1, source_target_pairs={{4,0},{8,12},{5,1},{9,13},{6,2},{10,14},{7,3},{11,15},{20,16},{24,... | collective-permute-start | bytes 2457608 | tf_op jit(solution)/shard_map/ppermute | solution.py:115
  32.5 15.5 %collective-permute-start.8 = (bf16[192,1024]{1,0:T(8,128)(2,1)S(1)}, bf16[192,1024]{1,0:T(8,128)(2,1)S(1)}, u32[]{:S(2)}, u32[]{:S(2)}) collective-permute-start(bf16[192,1024]{1,0:T(8,128)(2,1)S(1)} %shard_map.92), channel_id=1, source_target_pairs={{0,4},{12,8},{1,5},{13,9},{2,6},{14,10},{3,7},{15,11},{16,20},{28,... | collective-permute-start | bytes 1179656 | tf_op jit(solution)/shard_map/ppermute | solution.py:115
  39.3 20.2 %collective-permute-start.4 = (bf16[400,1024]{1,0:T(8,128)(2,1)}, bf16[400,1024]{1,0:T(8,128)(2,1)}, u32[]{:S(2)}, u32[]{:S(2)}) collective-permute-start(bf16[400,1024]{1,0:T(8,128)(2,1)} %collective-permute-done.3.refs_0_.refs_8_), channel_id=1, source_target_pairs={{4,6},{5,7},{6,4},{7,5},{8,10},{9,11},{10,8},{11,9},{20,22},{21,23... | collective-permute-start | bytes 2457608 | tf_op jit(solution)/shard_map/ppermute | solution.py:457
  40.9 29.3 %collective-permute-start.2 = (bf16[400,1024]{1,0:T(8,128)(2,1)}, bf16[400,1024]{1,0:T(8,128)(2,1)}, u32[]{:S(2)}, u32[]{:S(2)}) collective-permute-start(bf16[400,1024]{1,0:T(8,128)(2,1)} %collective-permute-done.1.refs_2_.inner_ref.refs_0_), channel_id=1, source_target_pairs={{4,0},{8,12},{5,1},{9,13},{6,2},{10,14},{7,3},{11,15},{20,16},{24,... | collective-permute-start | bytes 2457608 | tf_op jit(solution)/shard_map/ppermute | solution.py:115
  51.1 20.1 %collective-permute-start.10 = (bf16[400,1024]{1,0:T(8,128)(2,1)}, bf16[400,1024]{1,0:T(8,128)(2,1)S(1)}, u32[]{:S(2)}, u32[]{:S(2)}) collective-permute-start(bf16[400,1024]{1,0:T(8,128)(2,1)} %shard_map.95.refs_1_.refs_9_), channel_id=1, source_target_pairs={{0,2},{1,3},{2,0},{3,1},{12,14},{13,15},{14,12},{15,13},{16,18},{1... | collective-permute-start | bytes 2457608 | tf_op jit(solution)/shard_map/ppermute | solution.py:457
  54.4 22.4 %collective-permute-start.14 = (bf16[384,1024]{1,0:T(8,128)(2,1)}, bf16[384,1024]{1,0:T(8,128)(2,1)S(1)}, u32[]{:S(2)}, u32[]{:S(2)}) collective-permute-start(bf16[384,1024]{1,0:T(8,128)(2,1)} %copy-done.15), channel_id=1, source_target_pairs={{0,1},{1,0},{2,3},{3,2},{4,5},{5,4},{6,7},{7,6},{8,9},{9,8},{10,11... | collective-permute-start | bytes 2359304 | tf_op jit(solution)/shard_map/ppermute | solution.py:111
  58.9 18.2 %collective-permute-start.15 = (bf16[384,1024]{1,0:T(8,128)(2,1)S(1)}, bf16[384,1024]{1,0:T(8,128)(2,1)S(1)}, u32[]{:S(2)}, u32[]{:S(2)}) collective-permute-start(bf16[384,1024]{1,0:T(8,128)(2,1)S(1)} %get-tuple-element.36), channel_id=1, source_target_pairs={{0,1},{1,0},{2,3},{3,2},{4,5},{5,4},{6,7},{7,6},{8,9},{9,8},{10,11... | collective-permute-start | bytes 2359304 | tf_op jit(solution)/shard_map/ppermute | solution.py:111
  59.5 24.5 %collective-permute-start.13 = (bf16[192,1024]{1,0:T(8,128)(2,1)S(1)}, bf16[192,1024]{1,0:T(8,128)(2,1)S(1)}, u32[]{:S(2)}, u32[]{:S(2)}) collective-permute-start(bf16[192,1024]{1,0:T(8,128)(2,1)S(1)} %collective-permute-done.11.rest_2_.refs_1_), channel_id=1, source_target_pairs={{4,0},{8,12},{5,1},{9,13},{6,2},{10,14},{7,3},{11,15},{20,16},{24,... | collective-permute-start | bytes 1179656 | tf_op jit(solution)/shard_map/ppermute | solution.py:115
  73.9 16.9 %collective-permute-start.18 = (bf16[256,2048]{1,0:T(8,128)(2,1)S(1)}, bf16[256,2048]{1,0:T(8,128)(2,1)S(1)}, u32[]{:S(2)}, u32[]{:S(2)}) collective-permute-start(bf16[256,2048]{1,0:T(8,128)(2,1)S(1)} %copy-done.6), channel_id=1, source_target_pairs={{0,1},{1,0},{2,3},{3,2},{4,5},{5,4},{6,7},{7,6},{8,9},{9,8},{10,11... | collective-permute-start | bytes 3145736 | tf_op jit(solution)/shard_map/ppermute | solution.py:111
  93.3 12.1 %collective-permute-start.19 = (bf16[192,1024]{1,0:T(8,128)(2,1)S(1)}, bf16[192,1024]{1,0:T(8,128)(2,1)S(1)}, u32[]{:S(2)}, u32[]{:S(2)}) collective-permute-start(bf16[192,1024]{1,0:T(8,128)(2,1)S(1)} %get-tuple-element.45), channel_id=1, source_target_pairs={{0,2},{1,3},{2,0},{3,1},{4,6},{5,7},{6,4},{7,5},{8,10},{9,11},{10,... | collective-permute-start | bytes 1179656 | tf_op jit(solution)/shard_map/ppermute | solution.py:107
  95.9 17.9 %collective-permute-start.21 = (bf16[192,1024]{1,0:T(8,128)(2,1)S(1)}, bf16[192,1024]{1,0:T(8,128)(2,1)S(1)}, u32[]{:S(2)}, u32[]{:S(2)}) collective-permute-start(bf16[192,1024]{1,0:T(8,128)(2,1)S(1)} %get-tuple-element.48), channel_id=1, source_target_pairs={{0,2},{1,3},{2,0},{3,1},{4,6},{5,7},{6,4},{7,5},{8,10},{9,11},{10,... | collective-permute-start | bytes 1179656 | tf_op jit(solution)/shard_map/ppermute | solution.py:107
  105.5 15.3 %collective-permute-start.23 = (bf16[192,1024]{1,0:T(8,128)(2,1)S(1)}, bf16[192,1024]{1,0:T(8,128)(2,1)S(1)}, u32[]{:S(2)}, u32[]{:S(2)}) collective-permute-start(bf16[192,1024]{1,0:T(8,128)(2,1)S(1)} %add_convert_fusion.4), channel_id=1, source_target_pairs={{0,4},{12,8},{1,5},{13,9},{2,6},{14,10},{3,7},{15,11},{16,20},{28,... | collective-permute-start | bytes 1179656 | tf_op jit(solution)/shard_map/ppermute | solution.py:115
  111.3 13.0 %collective-permute-start.26 = (bf16[192,1024]{1,0:T(8,128)(2,1)S(1)}, bf16[192,1024]{1,0:T(8,128)(2,1)S(1)}, u32[]{:S(2)}, u32[]{:S(2)}) collective-permute-start(bf16[192,1024]{1,0:T(8,128)(2,1)S(1)} %get-tuple-element.52), channel_id=1, source_target_pairs={{0,2},{1,3},{2,0},{3,1},{4,6},{5,7},{6,4},{7,5},{8,10},{9,11},{10,... | collective-permute-start | bytes 1179656 | tf_op jit(solution)/shard_map/ppermute | solution.py:107
  112.9 14.2 %collective-permute-start.20 = (bf16[192,1024]{1,0:T(8,128)(2,1)S(1)}, bf16[192,1024]{1,0:T(8,128)(2,1)S(1)}, u32[]{:S(2)}, u32[]{:S(2)}) collective-permute-start(bf16[192,1024]{1,0:T(8,128)(2,1)S(1)} %add_convert_fusion.4), channel_id=1, source_target_pairs={{4,8},{8,4},{5,9},{9,5},{6,10},{10,6},{7,11},{11,7},{20,24},{24,20... | collective-permute-start | bytes 1179656 | tf_op jit(solution)/shard_map/ppermute | solution.py:115
  113.9 15.7 %collective-permute-start.22 = (bf16[192,1024]{1,0:T(8,128)(2,1)S(1)}, bf16[192,1024]{1,0:T(8,128)(2,1)S(1)}, u32[]{:S(2)}, u32[]{:S(2)}) collective-permute-start(bf16[192,1024]{1,0:T(8,128)(2,1)S(1)} %add_convert_fusion.3.refs_0_), channel_id=1, source_target_pairs={{0,8},{12,4},{1,9},{13,5},{2,10},{14,6},{3,11},{15,7},{16,24},{28,... | collective-permute-start | bytes 1179656 | tf_op jit(solution)/shard_map/ppermute | solution.py:115
  120.9 17.9 %collective-permute-start.24 = (bf16[192,1024]{1,0:T(8,128)(2,1)S(1)}, bf16[192,1024]{1,0:T(8,128)(2,1)S(1)}, u32[]{:S(2)}, u32[]{:S(2)}) collective-permute-start(bf16[192,1024]{1,0:T(8,128)(2,1)S(1)} %add_convert_fusion.2), channel_id=1, source_target_pairs={{4,12},{8,0},{5,13},{9,1},{6,14},{10,2},{7,15},{11,3},{20,28},{24,... | collective-permute-start | bytes 1179656 | tf_op jit(solution)/shard_map/ppermute | solution.py:115
  122.8 16.2 %collective-permute-start.25 = (bf16[192,1024]{1,0:T(8,128)(2,1)S(1)}, bf16[192,1024]{1,0:T(8,128)(2,1)S(1)}, u32[]{:S(2)}, u32[]{:S(2)}) collective-permute-start(bf16[192,1024]{1,0:T(8,128)(2,1)S(1)} %get-tuple-element.50), channel_id=1, source_target_pairs={{0,2},{1,3},{2,0},{3,1},{4,6},{5,7},{6,4},{7,5},{8,10},{9,11},{10,... | collective-permute-start | bytes 1179656 | tf_op jit(solution)/shard_map/ppermute | solution.py:107
  124.5 17.1 %collective-permute-start.27 = (bf16[192,1024]{1,0:T(8,128)(2,1)S(1)}, bf16[192,1024]{1,0:T(8,128)(2,1)S(1)}, u32[]{:S(2)}, u32[]{:S(2)}) collective-permute-start(bf16[192,1024]{1,0:T(8,128)(2,1)S(1)} %add_convert_fusion.1), channel_id=1, source_target_pairs={{0,4},{4,0},{8,12},{12,8},{1,5},{5,1},{9,13},{13,9},{2,6},{6,2},{1... | collective-permute-start | bytes 1179656 | tf_op jit(solution)/shard_map/ppermute | solution.py:115
  (27 other events, 127.1 us)

commit v23 on v22

--- a/solution.py
+++ b/solution.py
@@ -519,13 +519,13 @@
     first, second, third = [joined(*chunk).astype(jnp.bfloat16) for chunk in chunks]
     second = lax.optimization_barrier(second)
     inward = along(first, INWARD)
-    middle = along(first, MIDDLE)
+    middle = after(along(first, MIDDLE), flops=4 * 2**30)
     two_in = along(second, TWO_IN)
     passed = second.astype(jnp.float32) + inward.astype(jnp.float32)
     two_out = along(passed.astype(jnp.bfloat16), TWO_OUT)
     beside = along(third, BESIDE)
-    arrived = [block.astype(jnp.float32) for block in (middle, two_in, two_out)]
-    total = lax.optimization_barrier(sum(arrived))
+    total = lax.optimization_barrier(two_in.astype(jnp.float32) + two_out.astype(jnp.float32))
+    total = lax.optimization_barrier(total + middle.astype(jnp.float32))
     own_sum = joined(*last_chunk(second))
     return (total + own_sum + beside.astype(jnp.float32)).astype(jnp.bfloat16)
 

time: 144 us -> 145 us (level)
  waiting for transfers between devices: 44.7 us -> 41.3 us
  starting transfers between devices: 48.8 us -> 51.2 us
  other arithmetic: 3.36 us -> 5.48 us
    ppermute x13, starting transfers between devices: 34.5 us -> 37 us  [along(): return lax.ppermute(block, 'blk', route)]
    ppermute x7, waiting for transfers between devices: 9.17 us -> 7.41 us  [across_chips(): return lax.ppermute(block, 'tp', [(i, i ^ 2) for i in range(4)])]
    ppermute x13, waiting for transfers between devices: 34.4 us -> 32.8 us  [along(): return lax.ppermute(block, 'blk', route)]
  transfers between devices with their start and end apart: 28 -> 28, of which waited for: 10 -> 9; matrix products, arithmetic and copies ran while one was open for 6% -> 7% of each run, Pallas kernels for 17% -> 17%
where the time goes in v23:
time: 145 us; the launch traced here: 144 us
  starting transfers between devices  51.2 us (35%)
  waiting for transfers between devices  41.3 us (28%)
  Pallas kernels  29.5 us (20%)
  local copies, waits for them, and re-layouts  15.9 us (11%)
  other arithmetic  5.48 us (4%)
    ppermute x13, starting transfers between devices, along(): return lax.ppermute(block, 'blk', route)  37 us
    ppermute x13, waiting for transfers between devices, along(): return lax.ppermute(block, 'blk', route)  32.8 us
    pallas_call x5, Pallas kernels, partial_sums(): return on_core(body, shapes + [TOKEN], specs)(*operands, *waits)  15.2 us
    unnamed x46, local copies, waits for them, and re-layouts  9 us
    ppermute x7, starting transfers between devices, across_chips(): return lax.ppermute(block, 'tp', [(i, i ^ 2) for i in range(4)])  8.98 us
    ppermute x7, waiting for transfers between devices, across_chips(): return lax.ppermute(block, 'tp', [(i, i ^ 2) for i in range(4)])  7.41 us
    ppermute x2, starting transfers between devices, at_kind(): return lax.ppermute(block, ('blk', 'tp'), pairs)  4.14 us
    pallas_call x2, Pallas kernels, part_of(): pl.pallas_call(body, out_shape=shape, in_specs=[SMEM] + [ANYWHERE] * (2 +...  3.98 us
  transfers between devices with their start and end apart: 28, of which 9 were waited for; matrix products, arithmetic and copies ran while one was open for 7% of the time, Pallas kernels for 17%

profile of v23, /device:TPU:0, one launch (start us, length us, event | category | flops | bytes accessed | tf_op | source)
XLA Modules:
  0.0 143.9 jit_solution(12911823831771051601)
XLA Ops:
  4.5 3.1 %collective-permute-start = (bf16[400,1024]{1,0:T(8,128)(2,1)S(1)}, bf16[400,1024]{1,0:T(8,128)(2,1)}, u32[]{:S(2)}, u32[]{:S(2)}) collective-permute-start(bf16[400,1024]{1,0:T(8,128)(2,1)S(1)} %shard_map.91.refs_1_.refs_4_.refs_5_), channel_id=1, source_target_pairs={{0,4},{4,0},{8,12},{12,8},{1,5},{5,1},{9,13},{13,9},{2,6},{6,2},{1... | collective-permute-start | bytes 2457608 | tf_op jit(solution)/shard_map/ppermute | solution.py:115
  10.7 3.4 %dynamic-slice_bitcast_fusion.6 = (bf16[1024,256]{1,0:T(8,128)(2,1)S(1)}, bf16[1024,256]{1,0:T(8,128)(2,1)S(1)}, bf16[1024,256]{1,0:T(8,128)(2,1)S(1)}, bf16[102...) fusion(bf16[4,1024,256]{2,1,0:T(8,128)(2,1)} %bitcast.32, ...), kind=kLoop, calls=%fused_computation.18 | loop fusion | bytes 8388624 | tf_op jit(solution)/shard_map/jit(dynamic_index_in_dim)/squeeze | solution.py:443
  16.3 2.8 %dynamic-slice_bitcast_fusion.1 = (bf16[256,1024]{1,0:T(8,128)(2,1)}, bf16[256,1024]{1,0:T(8,128)(2,1)S(1)}, bf16[256,1024]{1,0:T(8,128)(2,1)S(1)}, bf16[256,1024]{1,0:T(8,128)(2,1)}) fusion(bf16[1,256,4096]{2,1,0:T(8,128)(2,1)} %param.12, s32[]{:T(128)S(6)} %select_n.39, s32[]{:T(128)S(6)} %select_n.38, s32[]{:T(128)S(6)} %select_n.37, s32[]{:T(128)S(6)} %select_n.40), kind=kLoop, calls=%fused_computation.13 | loop fusion | bytes 4194320 | tf_op jit(solution)/shard_map/dynamic_slice | solution.py:449
  19.1 6.9 %collective-permute-done.refs_0_.refs_6_.refs_7_ = bf16[400,1024]{1,0:T(8,128)(2,1)} collective-permute-done((bf16[400,1024]{1,0:T(8,128)(2,1)S(1)}, bf16[400,1024]{1,0:T(8,128)(2,1)}, u32[]{:S(2)}, u32[]{:S(2)}) %collective-permute-start) | collective-permute-done | bytes 819232 | tf_op jit(solution)/shard_map/ppermute | solution.py:115
  30.5 2.0 %shard_map.92 = bf16[192,1024]{1,0:T(8,128)(2,1)S(1)} custom-call(s32[9]{0:T(128)S(1)} %fusion.plan_ref, bf16[384,1024]{1,0:T(8,128)(2,1)} %collective-permute-done.7.inner_ref.outer_ref.refs_1_, bf16[384,1024]{1,0:T(8,128)(2,1)} %collective-permute-done.7.inner_ref.outer_ref.refs_1_), custom_call_target="tpu_custom_call" | custom-call | flops 17179869184 | bytes 1024 | tf_op jit(solution)/shard_map/pallas_call | solution.py:192
  32.5 6.5 %collective-permute-start.8 = (bf16[192,1024]{1,0:T(8,128)(2,1)S(1)}, bf16[192,1024]{1,0:T(8,128)(2,1)S(1)}, u32[]{:S(2)}, u32[]{:S(2)}) collective-permute-start(bf16[192,1024]{1,0:T(8,128)(2,1)S(1)} %shard_map.92), channel_id=1, source_target_pairs={{0,4},{12,8},{1,5},{13,9},{2,6},{14,10},{3,7},{15,11},{16,20},{28,... | collective-permute-start | bytes 1179656 | tf_op jit(solution)/shard_map/ppermute | solution.py:115
  42.2 3.2 %shard_map.94 = (f32[384,1024]{1,0:T(8,128)S(1)}, bf16[384,1024]{1,0:T(8,128)(2,1)S(1)}, f32[8,128]{1,0:T(8,128)S(1)}) custom-call(s32[9]{0:T(128)S(1)} %fusion.plan_ref, bf16[384,1024]{1,0:T(8,128)(2,1)} %refs_0_.1, bf16[384,1024]{1,0:T(8,128)(2,1)} %collective-permute-done.7.inner_ref.outer_ref.refs_1_, ...), custom_call_target="tpu_custom_call" | custom-call | flops 1024 | bytes 1024 | tf_op jit(solution)/shard_map/pallas_call | solution.py:287
  48.8 2.3 %collective-permute-done.5.refs_0_ = bf16[400,1024]{1,0:T(8,128)(2,1)} collective-permute-done((bf16[400,1024]{1,0:T(8,128)(2,1)}, bf16[400,1024]{1,0:T(8,128)(2,1)}, u32[]{:S(2)}, u32[]{:S(2)}) %collective-permute-start.5) | collective-permute-done | bytes 819232 | tf_op jit(solution)/shard_map/ppermute | solution.py:115
  51.1 2.6 %collective-permute-start.10 = (bf16[400,1024]{1,0:T(8,128)(2,1)}, bf16[400,1024]{1,0:T(8,128)(2,1)S(1)}, u32[]{:S(2)}, u32[]{:S(2)}) collective-permute-start(bf16[400,1024]{1,0:T(8,128)(2,1)} %shard_map.95.refs_1_.refs_9_), channel_id=1, source_target_pairs={{0,2},{1,3},{2,0},{3,1},{12,14},{13,15},{14,12},{15,13},{16,18},{1... | collective-permute-start | bytes 2457608 | tf_op jit(solution)/shard_map/ppermute | solution.py:457
  55.7 3.2 %shard_map.96 = (f32[384,1024]{1,0:T(8,128)S(1)}, bf16[384,1024]{1,0:T(8,128)(2,1)S(1)}, f32[8,128]{1,0:T(8,128)S(1)}) custom-call(s32[9]{0:T(128)S(1)} %fusion.plan_ref, bf16[400,1024]{1,0:T(8,128)(2,1)} %collective-permute-done.refs_0_.refs_6_.refs_7_, bf16[400,1024]{1,0:T(8,128)(2,1)} %collective-permute-done.6.refs_1_, ...), custom_call_target="tpu_custom_call" | custom-call | flops 1024 | bytes 1024 | tf_op jit(solution)/shard_map/pallas_call | solution.py:287
  60.8 9.4 %collective-permute-done.2.outer_ref.refs_1_ = bf16[400,1024]{1,0:T(8,128)(2,1)} collective-permute-done((bf16[400,1024]{1,0:T(8,128)(2,1)}, bf16[400,1024]{1,0:T(8,128)(2,1)}, u32[]{:S(2)}, u32[]{:S(2)}) %collective-permute-start.2) | collective-permute-done | bytes 819232 | tf_op jit(solution)/shard_map/ppermute | solution.py:115
  71.3 2.0 %shard_map.97 = bf16[192,1024]{1,0:T(8,128)(2,1)S(1)} custom-call(s32[9]{0:T(128)S(1)} %fusion.plan_ref, bf16[400,1024]{1,0:T(8,128)(2,1)} %collective-permute-done.1.refs_2_.inner_ref.refs_0_, bf16[400,1024]{1,0:T(8,128)(2,1)} %collective-permute-done.2.outer_ref.refs_1_, bf16[400,1024]{1,0:T(8,128)(2,1)} %collective-permute-done.4.rest_0_.refs_2_, ...), custom_call_target="tpu_custom_call" | custom-call | flops 1024 | bytes 1024 | tf_op jit(solution)/shard_map/pallas_call | solution.py:192
  73.9 2.9 %shard_map.98 = (f32[384,1024]{1,0:T(8,128)S(1)}, f32[8,128]{1,0:T(8,128)}) custom-call(s32[9]{0:T(128)S(1)} %fusion.plan_ref, bf16[400,1024]{1,0:T(8,128)(2,1)} %collective-permute-done.1.refs_2_.inner_ref.refs_0_, bf16[400,1024]{1,0:T(8,128)(2,1)} %collective-permute-done.2.outer_ref.refs_1_, bf16[1024,512]{1,0:T(8,128)(2,1)S(1)} %pad_maximum_fusion.refs_2_.refs_4_, ...), custom_call_target="tpu_custom_call" | custom-call | flops 1024 | bytes 1024 | tf_op jit(solution)/shard_map/pallas_call | solution.py:287
  78.0 4.0 %shard_map.102 = (f32[384,1024]{1,0:T(8,128)S(1)}, bf16[384,1024]{1,0:T(8,128)(2,1)S(1)}, f32[8,128]{1,0:T(8,128)}) custom-call(s32[9]{0:T(128)S(1)} %fusion.plan_ref, bf16[400,1024]{1,0:T(8,128)(2,1)} %collective-permute-done.3.refs_0_.refs_8_, bf16[400,1024]{1,0:T(8,128)(2,1)} %shard_map.95.refs_1_.refs_9_, ...), custom_call_target="tpu_custom_call" | custom-call | flops 1024 | bytes 1024 | tf_op jit(solution)/shard_map/pallas_call | solution.py:287
  84.0 2.0 %shard_map.101 = (f32[384,1024]{1,0:T(8,128)S(1)}, bf16[384,1024]{1,0:T(8,128)(2,1)S(1)}, f32[8,128]{1,0:T(8,128)}) custom-call(s32[9]{0:T(128)S(1)} %fusion.plan_ref, bf16[192,1024]{1,0:T(8,128)(2,1)S(1)} %collective-permute-done.12.refs_0_, bf16[192,1024]{1,0:T(8,128)(2,1)S(1)} %collective-permute-done.11.rest_2_.refs_1_, ...), custom_call_target="tpu_custom_call" | custom-call | flops 1024 | bytes 1024 | tf_op jit(solution)/shard_map/pallas_call | solution.py:287
  87.2 3.7 %shard_map.103.before_ref = f32[768,512]{1,0:T(8,128)S(1)} custom-call(s32[9]{0:T(128)S(1)} %fusion.plan_ref, bf16[384,512]{1,0:T(8,128)(2,1)S(1)} %get-tuple-element.40.refs_0_, bf16[384,512]{1,0:T(8,128)(2,1)S(1)} %get-tuple-element.41.refs_1_, f32[384,1024]{1,0:T(8,128)S(1)} %get-tuple-element.42.refs_2_, ...), custom_call_target="tpu_custom_call" | custom-call | flops 1024 | bytes 1024 | tf_op jit(solution)/shard_map/pallas_call | solution.py:373
  90.9 2.6 %shard_map.104 = (bf16[192,1024]{1,0:T(8,128)(2,1)S(1)}, f32[192,1024]{1,0:T(8,128)S(1)}, bf16[576,512]{1,0:T(8,128)(2,1)S(1)}) custom-call(s32[9]{0:T(128)S(1)} %fusion.plan_ref, f32[384,1024]{1,0:T(8,128)S(1)} %get-tuple-element.38.sums_ref, bf16[384,1024]{1,0:T(8,128)(2,1)S(1)} %collective-permute-done.16.got_ref, ...), custom_call_target="tpu_custom_call" | custom-call | flops 1024 | bytes 1024 | tf_op jit(solution)/shard_map/pallas_call | solution.py:412
  98.2 7.4 %collective-permute-done.21 = bf16[192,1024]{1,0:T(8,128)(2,1)S(1)} collective-permute-done((bf16[192,1024]{1,0:T(8,128)(2,1)S(1)}, bf16[192,1024]{1,0:T(8,128)(2,1)S(1)}, u32[]{:S(2)}, u32[]{:S(2)}) %collective-permute-start.21) | collective-permute-done | bytes 393248 | tf_op jit(solution)/shard_map/ppermute | solution.py:107
  107.1 7.9 %collective-permute-start.22 = (bf16[192,1024]{1,0:T(8,128)(2,1)S(1)}, bf16[192,1024]{1,0:T(8,128)(2,1)S(1)}, u32[]{:S(2)}, u32[]{:S(2)}) collective-permute-start(bf16[192,1024]{1,0:T(8,128)(2,1)S(1)} %add_convert_fusion.3), channel_id=1, source_target_pairs={{0,4},{12,8},{1,5},{13,9},{2,6},{14,10},{3,7},{15,11},{16,20},{28,... | collective-permute-start | bytes 1179656 | tf_op jit(solution)/shard_map/ppermute | solution.py:115
  115.1 5.8 %collective-permute-start.20 = (bf16[192,1024]{1,0:T(8,128)(2,1)S(1)}, bf16[192,1024]{1,0:T(8,128)(2,1)S(1)}, u32[]{:S(2)}, u32[]{:S(2)}) collective-permute-start(bf16[192,1024]{1,0:T(8,128)(2,1)S(1)} %add_convert_fusion.4.refs_0_), channel_id=1, source_target_pairs={{0,8},{12,4},{1,9},{13,5},{2,10},{14,6},{3,11},{15,7},{16,24},{28,... | collective-permute-start | bytes 1179656 | tf_op jit(solution)/shard_map/ppermute | solution.py:115
  123.2 3.3 %collective-permute-start.27 = (bf16[192,1024]{1,0:T(8,128)(2,1)S(1)}, bf16[192,1024]{1,0:T(8,128)(2,1)}, u32[]{:S(2)}, u32[]{:S(2)}) collective-permute-start(bf16[192,1024]{1,0:T(8,128)(2,1)S(1)} %add_convert_fusion.1), channel_id=1, source_target_pairs={{0,4},{4,0},{8,12},{12,8},{1,5},{5,1},{9,13},{13,9},{2,6},{6,2},{1... | collective-permute-start | bytes 1179656 | tf_op jit(solution)/shard_map/ppermute | solution.py:115
  127.9 3.3 %collective-permute-done.20 = bf16[192,1024]{1,0:T(8,128)(2,1)S(1)} collective-permute-done((bf16[192,1024]{1,0:T(8,128)(2,1)S(1)}, bf16[192,1024]{1,0:T(8,128)(2,1)S(1)}, u32[]{:S(2)}, u32[]{:S(2)}) %collective-permute-start.20) | collective-permute-done | bytes 393248 | tf_op jit(solution)/shard_map/ppermute | solution.py:115
  131.2 8.5 %collective-permute-done.23 = bf16[192,1024]{1,0:T(8,128)(2,1)S(1)} collective-permute-done((bf16[192,1024]{1,0:T(8,128)(2,1)S(1)}, bf16[192,1024]{1,0:T(8,128)(2,1)S(1)}, u32[]{:S(2)}, u32[]{:S(2)}) %collective-permute-start.23) | collective-permute-done | bytes 393248 | tf_op jit(solution)/shard_map/ppermute | solution.py:115
  141.9 2.1 %add_convert_fusion = bf16[192,1024]{1,0:T(8,128)(2,1)} fusion(bf16[192,1024]{1,0:T(8,128)(2,1)} %collective-permute-done.27, f32[192,1024]{1,0:T(8,128)S(1)} %convert_add_fusion, f32[192,1024]{1,0:T(8,128)S(1)} %get-tuple-element.49, bf16[192,1024]{1,0:T(8,128)(2,1)} %collective-permute-done.25), kind=kLoop, calls=%fused_computation.5 | loop fusion | flops 1179648 | bytes 2752512 | tf_op jit(solution)/shard_map/convert_element_type | solution.py:530
  (110 shorter events, 42.8 us)
Async XLA Ops:
  4.5 21.4 %collective-permute-start = (bf16[400,1024]{1,0:T(8,128)(2,1)S(1)}, bf16[400,1024]{1,0:T(8,128)(2,1)}, u32[]{:S(2)}, u32[]{:S(2)}) collective-permute-start(bf16[400,1024]{1,0:T(8,128)(2,1)S(1)} %shard_map.91.refs_1_.refs_4_.refs_5_), channel_id=1, source_target_pairs={{0,4},{4,0},{8,12},{12,8},{1,5},{5,1},{9,13},{13,9},{2,6},{6,2},{1... | collective-permute-start | bytes 2457608 | tf_op jit(solution)/shard_map/ppermute | solution.py:115
  7.6 21.6 %collective-permute-start.3 = (bf16[400,1024]{1,0:T(8,128)(2,1)S(1)}, bf16[400,1024]{1,0:T(8,128)(2,1)}, u32[]{:S(2)}, u32[]{:S(2)}) collective-permute-start(bf16[400,1024]{1,0:T(8,128)(2,1)S(1)} %shard_map.91.refs_1_.refs_4_.refs_5_), channel_id=1, source_target_pairs={{4,8},{8,4},{5,9},{9,5},{6,10},{10,6},{7,11},{11,7},{20,24},{24,20... | collective-permute-start | bytes 2457608 | tf_op jit(solution)/shard_map/ppermute | solution.py:115
  9.2 21.3 %collective-permute-start.7 = (bf16[384,1024]{1,0:T(8,128)(2,1)}, bf16[384,1024]{1,0:T(8,128)(2,1)}, u32[]{:S(2)}, u32[]{:S(2)}) collective-permute-start(bf16[384,1024]{1,0:T(8,128)(2,1)} %refs_0_.1), channel_id=1, source_target_pairs={{0,2},{1,3},{2,0},{3,1},{4,6},{5,7},{6,4},{7,5},{8,10},{9,11},{10,... | collective-permute-start | bytes 2359304 | tf_op jit(solution)/shard_map/ppermute | solution.py:107
  15.7 25.2 %collective-permute-start.9 = (bf16[2048,512]{1,0:T(8,128)(2,1)}, bf16[2048,512]{1,0:T(8,128)(2,1)S(1)}, u32[]{:S(2)}, u32[]{:S(2)}) collective-permute-start(bf16[2048,512]{1,0:T(8,128)(2,1)} %shard_map.93), channel_id=1, source_target_pairs={{0,1},{1,0},{2,3},{3,2},{4,5},{5,4},{6,7},{7,6},{8,9},{9,8},{10,11... | collective-permute-start | bytes 6291464 | tf_op jit(solution)/shard_map/ppermute | solution.py:111
  26.0 25.1 %collective-permute-start.6 = (bf16[400,1024]{1,0:T(8,128)(2,1)}, bf16[400,1024]{1,0:T(8,128)(2,1)}, u32[]{:S(2)}, u32[]{:S(2)}) collective-permute-start(bf16[400,1024]{1,0:T(8,128)(2,1)} %collective-permute-done.refs_0_.refs_6_.refs_7_), channel_id=1, source_target_pairs={{0,2},{1,3},{2,0},{3,1},{4,6},{5,7},{6,4},{7,5},{8,10},{9,11},{10,... | collective-permute-start | bytes 2457608 | tf_op jit(solution)/shard_map/ppermute | solution.py:107
  27.6 11.7 %collective-permute-start.1 = (bf16[400,1024]{1,0:T(8,128)(2,1)}, bf16[400,1024]{1,0:T(8,128)(2,1)}, u32[]{:S(2)}, u32[]{:S(2)}) collective-permute-start(bf16[400,1024]{1,0:T(8,128)(2,1)} %collective-permute-done.refs_0_.refs_6_.refs_7_), channel_id=1, source_target_pairs={{4,8},{8,4},{5,9},{9,5},{6,10},{10,6},{7,11},{11,7},{20,24},{24,20... | collective-permute-start | bytes 2457608 | tf_op jit(solution)/shard_map/ppermute | solution.py:115
  29.2 21.9 %collective-permute-start.5 = (bf16[400,1024]{1,0:T(8,128)(2,1)}, bf16[400,1024]{1,0:T(8,128)(2,1)}, u32[]{:S(2)}, u32[]{:S(2)}) collective-permute-start(bf16[400,1024]{1,0:T(8,128)(2,1)} %collective-permute-done.3.refs_0_.refs_8_), channel_id=1, source_target_pairs={{4,0},{8,12},{5,1},{9,13},{6,2},{10,14},{7,3},{11,15},{20,16},{24,... | collective-permute-start | bytes 2457608 | tf_op jit(solution)/shard_map/ppermute | solution.py:115
  32.5 15.5 %collective-permute-start.8 = (bf16[192,1024]{1,0:T(8,128)(2,1)S(1)}, bf16[192,1024]{1,0:T(8,128)(2,1)S(1)}, u32[]{:S(2)}, u32[]{:S(2)}) collective-permute-start(bf16[192,1024]{1,0:T(8,128)(2,1)S(1)} %shard_map.92), channel_id=1, source_target_pairs={{0,4},{12,8},{1,5},{13,9},{2,6},{14,10},{3,7},{15,11},{16,20},{28,... | collective-permute-start | bytes 1179656 | tf_op jit(solution)/shard_map/ppermute | solution.py:115
  39.3 20.2 %collective-permute-start.4 = (bf16[400,1024]{1,0:T(8,128)(2,1)}, bf16[400,1024]{1,0:T(8,128)(2,1)}, u32[]{:S(2)}, u32[]{:S(2)}) collective-permute-start(bf16[400,1024]{1,0:T(8,128)(2,1)} %collective-permute-done.3.refs_0_.refs_8_), channel_id=1, source_target_pairs={{4,6},{5,7},{6,4},{7,5},{8,10},{9,11},{10,8},{11,9},{20,22},{21,23... | collective-permute-start | bytes 2457608 | tf_op jit(solution)/shard_map/ppermute | solution.py:457
  40.9 29.3 %collective-permute-start.2 = (bf16[400,1024]{1,0:T(8,128)(2,1)}, bf16[400,1024]{1,0:T(8,128)(2,1)}, u32[]{:S(2)}, u32[]{:S(2)}) collective-permute-start(bf16[400,1024]{1,0:T(8,128)(2,1)} %collective-permute-done.1.refs_2_.inner_ref.refs_0_), channel_id=1, source_target_pairs={{4,0},{8,12},{5,1},{9,13},{6,2},{10,14},{7,3},{11,15},{20,16},{24,... | collective-permute-start | bytes 2457608 | tf_op jit(solution)/shard_map/ppermute | solution.py:115
  51.1 20.1 %collective-permute-start.10 = (bf16[400,1024]{1,0:T(8,128)(2,1)}, bf16[400,1024]{1,0:T(8,128)(2,1)S(1)}, u32[]{:S(2)}, u32[]{:S(2)}) collective-permute-start(bf16[400,1024]{1,0:T(8,128)(2,1)} %shard_map.95.refs_1_.refs_9_), channel_id=1, source_target_pairs={{0,2},{1,3},{2,0},{3,1},{12,14},{13,15},{14,12},{15,13},{16,18},{1... | collective-permute-start | bytes 2457608 | tf_op jit(solution)/shard_map/ppermute | solution.py:457
  54.4 22.4 %collective-permute-start.14 = (bf16[384,1024]{1,0:T(8,128)(2,1)}, bf16[384,1024]{1,0:T(8,128)(2,1)S(1)}, u32[]{:S(2)}, u32[]{:S(2)}) collective-permute-start(bf16[384,1024]{1,0:T(8,128)(2,1)} %copy-done.15), channel_id=1, source_target_pairs={{0,1},{1,0},{2,3},{3,2},{4,5},{5,4},{6,7},{7,6},{8,9},{9,8},{10,11... | collective-permute-start | bytes 2359304 | tf_op jit(solution)/shard_map/ppermute | solution.py:111
  58.9 18.2 %collective-permute-start.15 = (bf16[384,1024]{1,0:T(8,128)(2,1)S(1)}, bf16[384,1024]{1,0:T(8,128)(2,1)S(1)}, u32[]{:S(2)}, u32[]{:S(2)}) collective-permute-start(bf16[384,1024]{1,0:T(8,128)(2,1)S(1)} %get-tuple-element.36), channel_id=1, source_target_pairs={{0,1},{1,0},{2,3},{3,2},{4,5},{5,4},{6,7},{7,6},{8,9},{9,8},{10,11... | collective-permute-start | bytes 2359304 | tf_op jit(solution)/shard_map/ppermute | solution.py:111
  59.5 24.5 %collective-permute-start.13 = (bf16[192,1024]{1,0:T(8,128)(2,1)S(1)}, bf16[192,1024]{1,0:T(8,128)(2,1)S(1)}, u32[]{:S(2)}, u32[]{:S(2)}) collective-permute-start(bf16[192,1024]{1,0:T(8,128)(2,1)S(1)} %collective-permute-done.11.rest_2_.refs_1_), channel_id=1, source_target_pairs={{4,0},{8,12},{5,1},{9,13},{6,2},{10,14},{7,3},{11,15},{20,16},{24,... | collective-permute-start | bytes 1179656 | tf_op jit(solution)/shard_map/ppermute | solution.py:115
  73.9 17.0 %collective-permute-start.18 = (bf16[256,2048]{1,0:T(8,128)(2,1)S(1)}, bf16[256,2048]{1,0:T(8,128)(2,1)S(1)}, u32[]{:S(2)}, u32[]{:S(2)}) collective-permute-start(bf16[256,2048]{1,0:T(8,128)(2,1)S(1)} %copy-done.6), channel_id=1, source_target_pairs={{0,1},{1,0},{2,3},{3,2},{4,5},{5,4},{6,7},{7,6},{8,9},{9,8},{10,11... | collective-permute-start | bytes 3145736 | tf_op jit(solution)/shard_map/ppermute | solution.py:111
  93.5 12.1 %collective-permute-start.21 = (bf16[192,1024]{1,0:T(8,128)(2,1)S(1)}, bf16[192,1024]{1,0:T(8,128)(2,1)S(1)}, u32[]{:S(2)}, u32[]{:S(2)}) collective-permute-start(bf16[192,1024]{1,0:T(8,128)(2,1)S(1)} %get-tuple-element.48), channel_id=1, source_target_pairs={{0,2},{1,3},{2,0},{3,1},{4,6},{5,7},{6,4},{7,5},{8,10},{9,11},{10,... | collective-permute-start | bytes 1179656 | tf_op jit(solution)/shard_map/ppermute | solution.py:107
  96.1 18.9 %collective-permute-start.19 = (bf16[192,1024]{1,0:T(8,128)(2,1)S(1)}, bf16[192,1024]{1,0:T(8,128)(2,1)S(1)}, u32[]{:S(2)}, u32[]{:S(2)}) collective-permute-start(bf16[192,1024]{1,0:T(8,128)(2,1)S(1)} %get-tuple-element.46), channel_id=1, source_target_pairs={{0,2},{1,3},{2,0},{3,1},{4,6},{5,7},{6,4},{7,5},{8,10},{9,11},{10,... | collective-permute-start | bytes 1179656 | tf_op jit(solution)/shard_map/ppermute | solution.py:107
  96.7 26.4 %collective-permute-start.26 = (bf16[192,1024]{1,0:T(8,128)(2,1)S(1)}, bf16[192,1024]{1,0:T(8,128)(2,1)S(1)}, u32[]{:S(2)}, u32[]{:S(2)}) collective-permute-start(bf16[192,1024]{1,0:T(8,128)(2,1)S(1)} %get-tuple-element.52), channel_id=1, source_target_pairs={{0,2},{1,3},{2,0},{3,1},{4,6},{5,7},{6,4},{7,5},{8,10},{9,11},{10,... | collective-permute-start | bytes 1179656 | tf_op jit(solution)/shard_map/ppermute | solution.py:107
  105.7 22.3 %collective-permute-start.24 = (bf16[192,1024]{1,0:T(8,128)(2,1)S(1)}, bf16[192,1024]{1,0:T(8,128)(2,1)}, u32[]{:S(2)}, u32[]{:S(2)}) collective-permute-start(bf16[192,1024]{1,0:T(8,128)(2,1)S(1)} %add_convert_fusion.3), channel_id=1, source_target_pairs={{4,8},{8,4},{5,9},{9,5},{6,10},{10,6},{7,11},{11,7},{20,24},{24,20... | collective-permute-start | bytes 1179656 | tf_op jit(solution)/shard_map/ppermute | solution.py:115
  107.1 19.4 %collective-permute-start.22 = (bf16[192,1024]{1,0:T(8,128)(2,1)S(1)}, bf16[192,1024]{1,0:T(8,128)(2,1)S(1)}, u32[]{:S(2)}, u32[]{:S(2)}) collective-permute-start(bf16[192,1024]{1,0:T(8,128)(2,1)S(1)} %add_convert_fusion.3), channel_id=1, source_target_pairs={{0,4},{12,8},{1,5},{13,9},{2,6},{14,10},{3,7},{15,11},{16,20},{28,... | collective-permute-start | bytes 1179656 | tf_op jit(solution)/shard_map/ppermute | solution.py:115
  115.1 16.1 %collective-permute-start.20 = (bf16[192,1024]{1,0:T(8,128)(2,1)S(1)}, bf16[192,1024]{1,0:T(8,128)(2,1)S(1)}, u32[]{:S(2)}, u32[]{:S(2)}) collective-permute-start(bf16[192,1024]{1,0:T(8,128)(2,1)S(1)} %add_convert_fusion.4.refs_0_), channel_id=1, source_target_pairs={{0,8},{12,4},{1,9},{13,5},{2,10},{14,6},{3,11},{15,7},{16,24},{28,... | collective-permute-start | bytes 1179656 | tf_op jit(solution)/shard_map/ppermute | solution.py:115
  121.5 19.4 %collective-permute-start.25 = (bf16[192,1024]{1,0:T(8,128)(2,1)S(1)}, bf16[192,1024]{1,0:T(8,128)(2,1)}, u32[]{:S(2)}, u32[]{:S(2)}) collective-permute-start(bf16[192,1024]{1,0:T(8,128)(2,1)S(1)} %get-tuple-element.50), channel_id=1, source_target_pairs={{0,2},{1,3},{2,0},{3,1},{4,6},{5,7},{6,4},{7,5},{8,10},{9,11},{10,... | collective-permute-start | bytes 1179656 | tf_op jit(solution)/shard_map/ppermute | solution.py:107
  123.2 18.7 %collective-permute-start.27 = (bf16[192,1024]{1,0:T(8,128)(2,1)S(1)}, bf16[192,1024]{1,0:T(8,128)(2,1)}, u32[]{:S(2)}, u32[]{:S(2)}) collective-permute-start(bf16[192,1024]{1,0:T(8,128)(2,1)S(1)} %add_convert_fusion.1), channel_id=1, source_target_pairs={{0,4},{4,0},{8,12},{12,8},{1,5},{5,1},{9,13},{13,9},{2,6},{6,2},{1... | collective-permute-start | bytes 1179656 | tf_op jit(solution)/shard_map/ppermute | solution.py:115
  126.6 13.1 %collective-permute-start.23 = (bf16[192,1024]{1,0:T(8,128)(2,1)S(1)}, bf16[192,1024]{1,0:T(8,128)(2,1)S(1)}, u32[]{:S(2)}, u32[]{:S(2)}) collective-permute-start(bf16[192,1024]{1,0:T(8,128)(2,1)S(1)} %add_convert_fusion.2), channel_id=1, source_target_pairs={{4,12},{8,0},{5,13},{9,1},{6,14},{10,2},{7,15},{11,3},{20,28},{24,... | collective-permute-start | bytes 1179656 | tf_op jit(solution)/shard_map/ppermute | solution.py:115
  (27 other events, 127.2 us)

commit v24 on v23

--- a/solution.py
+++ b/solution.py
@@ -412,9 +412,7 @@
     sent, kept, held = on_core(
         first, pair + [held_shape], specs, fact_scratch(facts[0].shape[1])
     )(plan, sums, got, *facts, before, down_own, down_lent)
-    rest = others([1, 2])
-    chunks = [(sent, kept), (rest[0], rest[1]), (rest[2], rest[3])]
-    return chunks, lambda *waits: others([3], *waits)
+    return (sent, kept), lambda index, *waits: others([index], *waits)
 
 
 def rows_travel(
@@ -509,24 +507,25 @@
         got_2,
         [(own, own), (beside, beside), second],
     )
-    chunks, last_chunk = finish(
+    first_chunk, chunk = finish(
         owned, 3, plan, sums_3, got_3, last, total, kept_down, lent_down
     )
 
     def joined(sent, kept):
         return kept + across_chips(sent).astype(jnp.float32)
 
-    first, second, third = [joined(*chunk).astype(jnp.bfloat16) for chunk in chunks]
-    second = lax.optimization_barrier(second)
+    first = joined(*first_chunk).astype(jnp.bfloat16)
+    second = lax.optimization_barrier(joined(*chunk(1)).astype(jnp.bfloat16))
+    third = joined(*chunk(2, first)).astype(jnp.bfloat16)
     inward = along(first, INWARD)
-    middle = after(along(first, MIDDLE), flops=4 * 2**30)
+    middle = after(along(first, MIDDLE), flops=2 * 2**30)
     two_in = along(second, TWO_IN)
     passed = second.astype(jnp.float32) + inward.astype(jnp.float32)
     two_out = along(passed.astype(jnp.bfloat16), TWO_OUT)
     beside = along(third, BESIDE)
     total = lax.optimization_barrier(two_in.astype(jnp.float32) + two_out.astype(jnp.float32))
     total = lax.optimization_barrier(total + middle.astype(jnp.float32))
-    own_sum = joined(*last_chunk(second))
+    own_sum = joined(*chunk(3, second))
     return (total + own_sum + beside.astype(jnp.float32)).astype(jnp.bfloat16)
 
 

time: 145 us -> 145 us (level)
  starting transfers between devices: 51.2 us -> 48.5 us
  waiting for transfers between devices: 41.3 us -> 43.1 us
    ppermute x13, starting transfers between devices: 37 us -> 34.1 us  [along(): return lax.ppermute(block, 'blk', route)]
    ppermute x7, waiting for transfers between devices: 7.41 us -> 9.33 us  [across_chips(): return lax.ppermute(block, 'tp', [(i, i ^ 2) for i in range(4)])]
    unnamed x46 -> x48, local copies, waits for them, and re-layouts: 9 us -> 9.77 us
where the time goes in v24:
time: 145 us; the launch traced here: 144 us
  starting transfers between devices  48.5 us (33%)
  waiting for transfers between devices  43.1 us (30%)
  Pallas kernels  29.6 us (20%)
  local copies, waits for them, and re-layouts  16.7 us (12%)
  other arithmetic  5.47 us (4%)
    ppermute x13, starting transfers between devices, along(): return lax.ppermute(block, 'blk', route)  34.1 us
    ppermute x13, waiting for transfers between devices, along(): return lax.ppermute(block, 'blk', route)  32.6 us
    pallas_call x5, Pallas kernels, partial_sums(): return on_core(body, shapes + [TOKEN], specs)(*operands, *waits)  15.2 us
    unnamed x48, local copies, waits for them, and re-layouts  9.77 us
    ppermute x7, waiting for transfers between devices, across_chips(): return lax.ppermute(block, 'tp', [(i, i ^ 2) for i in range(4)])  9.33 us
    ppermute x7, starting transfers between devices, across_chips(): return lax.ppermute(block, 'tp', [(i, i ^ 2) for i in range(4)])  9.01 us
    ppermute x2, starting transfers between devices, at_kind(): return lax.ppermute(block, ('blk', 'tp'), pairs)  4.15 us
    pallas_call x2, Pallas kernels, part_of(): pl.pallas_call(body, out_shape=shape, in_specs=[SMEM] + [ANYWHERE] * (2 +...  3.98 us
  transfers between devices with their start and end apart: 28, of which 9 were waited for; matrix products, arithmetic and copies ran while one was open for 7% of the time, Pallas kernels for 17%

profile of v24, /device:TPU:0, one launch (start us, length us, event | category | flops | bytes accessed | tf_op | source)
XLA Modules:
  0.0 143.7 jit_solution(10951789984342476791)
XLA Ops:
  4.5 3.1 %collective-permute-start = (bf16[400,1024]{1,0:T(8,128)(2,1)S(1)}, bf16[400,1024]{1,0:T(8,128)(2,1)}, u32[]{:S(2)}, u32[]{:S(2)}) collective-permute-start(bf16[400,1024]{1,0:T(8,128)(2,1)S(1)} %shard_map.91.refs_1_.refs_4_.refs_5_), channel_id=1, source_target_pairs={{0,4},{4,0},{8,12},{12,8},{1,5},{5,1},{9,13},{13,9},{2,6},{6,2},{1... | collective-permute-start | bytes 2457608 | tf_op jit(solution)/shard_map/ppermute | solution.py:115
  10.7 3.4 %dynamic-slice_bitcast_fusion.6 = (bf16[1024,256]{1,0:T(8,128)(2,1)S(1)}, bf16[1024,256]{1,0:T(8,128)(2,1)S(1)}, bf16[1024,256]{1,0:T(8,128)(2,1)S(1)}, bf16[102...) fusion(bf16[4,1024,256]{2,1,0:T(8,128)(2,1)} %bitcast.32, ...), kind=kLoop, calls=%fused_computation.18 | loop fusion | bytes 8388624 | tf_op jit(solution)/shard_map/jit(dynamic_index_in_dim)/squeeze | solution.py:441
  16.3 2.8 %dynamic-slice_bitcast_fusion.1 = (bf16[256,1024]{1,0:T(8,128)(2,1)}, bf16[256,1024]{1,0:T(8,128)(2,1)S(1)}, bf16[256,1024]{1,0:T(8,128)(2,1)S(1)}, bf16[256,1024]{1,0:T(8,128)(2,1)}) fusion(bf16[1,256,4096]{2,1,0:T(8,128)(2,1)} %param.12, s32[]{:T(128)S(6)} %select_n.39, s32[]{:T(128)S(6)} %select_n.38, s32[]{:T(128)S(6)} %select_n.37, s32[]{:T(128)S(6)} %select_n.40), kind=kLoop, calls=%fused_computation.13 | loop fusion | bytes 4194320 | tf_op jit(solution)/shard_map/dynamic_slice | solution.py:447
  19.1 6.9 %collective-permute-done.refs_0_.refs_6_.refs_7_ = bf16[400,1024]{1,0:T(8,128)(2,1)} collective-permute-done((bf16[400,1024]{1,0:T(8,128)(2,1)S(1)}, bf16[400,1024]{1,0:T(8,128)(2,1)}, u32[]{:S(2)}, u32[]{:S(2)}) %collective-permute-start) | collective-permute-done | bytes 819232 | tf_op jit(solution)/shard_map/ppermute | solution.py:115
  30.5 2.0 %shard_map.92 = bf16[192,1024]{1,0:T(8,128)(2,1)S(1)} custom-call(s32[9]{0:T(128)S(1)} %fusion.plan_ref, bf16[384,1024]{1,0:T(8,128)(2,1)} %collective-permute-done.7.inner_ref.outer_ref.refs_1_, bf16[384,1024]{1,0:T(8,128)(2,1)} %collective-permute-done.7.inner_ref.outer_ref.refs_1_), custom_call_target="tpu_custom_call" | custom-call | flops 17179869184 | bytes 1024 | tf_op jit(solution)/shard_map/pallas_call | solution.py:192
  32.5 6.4 %collective-permute-start.8 = (bf16[192,1024]{1,0:T(8,128)(2,1)S(1)}, bf16[192,1024]{1,0:T(8,128)(2,1)S(1)}, u32[]{:S(2)}, u32[]{:S(2)}) collective-permute-start(bf16[192,1024]{1,0:T(8,128)(2,1)S(1)} %shard_map.92), channel_id=1, source_target_pairs={{0,4},{12,8},{1,5},{13,9},{2,6},{14,10},{3,7},{15,11},{16,20},{28,... | collective-permute-start | bytes 1179656 | tf_op jit(solution)/shard_map/ppermute | solution.py:115
  42.2 3.2 %shard_map.94 = (f32[384,1024]{1,0:T(8,128)S(1)}, bf16[384,1024]{1,0:T(8,128)(2,1)S(1)}, f32[8,128]{1,0:T(8,128)S(1)}) custom-call(s32[9]{0:T(128)S(1)} %fusion.plan_ref, bf16[384,1024]{1,0:T(8,128)(2,1)} %refs_0_.1, bf16[384,1024]{1,0:T(8,128)(2,1)} %collective-permute-done.7.inner_ref.outer_ref.refs_1_, ...), custom_call_target="tpu_custom_call" | custom-call | flops 1024 | bytes 1024 | tf_op jit(solution)/shard_map/pallas_call | solution.py:287
  48.9 2.3 %collective-permute-done.5.refs_0_ = bf16[400,1024]{1,0:T(8,128)(2,1)} collective-permute-done((bf16[400,1024]{1,0:T(8,128)(2,1)}, bf16[400,1024]{1,0:T(8,128)(2,1)}, u32[]{:S(2)}, u32[]{:S(2)}) %collective-permute-start.5) | collective-permute-done | bytes 819232 | tf_op jit(solution)/shard_map/ppermute | solution.py:115
  51.1 2.6 %collective-permute-start.10 = (bf16[400,1024]{1,0:T(8,128)(2,1)}, bf16[400,1024]{1,0:T(8,128)(2,1)S(1)}, u32[]{:S(2)}, u32[]{:S(2)}) collective-permute-start(bf16[400,1024]{1,0:T(8,128)(2,1)} %shard_map.95.refs_1_.refs_9_), channel_id=1, source_target_pairs={{0,2},{1,3},{2,0},{3,1},{12,14},{13,15},{14,12},{15,13},{16,18},{1... | collective-permute-start | bytes 2457608 | tf_op jit(solution)/shard_map/ppermute | solution.py:455
  55.7 3.2 %shard_map.96 = (f32[384,1024]{1,0:T(8,128)S(1)}, bf16[384,1024]{1,0:T(8,128)(2,1)S(1)}, f32[8,128]{1,0:T(8,128)S(1)}) custom-call(s32[9]{0:T(128)S(1)} %fusion.plan_ref, bf16[400,1024]{1,0:T(8,128)(2,1)} %collective-permute-done.refs_0_.refs_6_.refs_7_, bf16[400,1024]{1,0:T(8,128)(2,1)} %collective-permute-done.6.refs_1_, ...), custom_call_target="tpu_custom_call" | custom-call | flops 1024 | bytes 1024 | tf_op jit(solution)/shard_map/pallas_call | solution.py:287
  60.8 9.4 %collective-permute-done.2.outer_ref.refs_1_ = bf16[400,1024]{1,0:T(8,128)(2,1)} collective-permute-done((bf16[400,1024]{1,0:T(8,128)(2,1)}, bf16[400,1024]{1,0:T(8,128)(2,1)}, u32[]{:S(2)}, u32[]{:S(2)}) %collective-permute-start.2) | collective-permute-done | bytes 819232 | tf_op jit(solution)/shard_map/ppermute | solution.py:115
  71.3 2.0 %shard_map.97 = bf16[192,1024]{1,0:T(8,128)(2,1)S(1)} custom-call(s32[9]{0:T(128)S(1)} %fusion.plan_ref, bf16[400,1024]{1,0:T(8,128)(2,1)} %collective-permute-done.1.refs_2_.inner_ref.refs_0_, bf16[400,1024]{1,0:T(8,128)(2,1)} %collective-permute-done.2.outer_ref.refs_1_, bf16[400,1024]{1,0:T(8,128)(2,1)} %collective-permute-done.4.rest_0_.refs_2_, ...), custom_call_target="tpu_custom_call" | custom-call | flops 1024 | bytes 1024 | tf_op jit(solution)/shard_map/pallas_call | solution.py:192
  73.9 2.9 %shard_map.98 = (f32[384,1024]{1,0:T(8,128)S(1)}, f32[8,128]{1,0:T(8,128)}) custom-call(s32[9]{0:T(128)S(1)} %fusion.plan_ref, bf16[400,1024]{1,0:T(8,128)(2,1)} %collective-permute-done.1.refs_2_.inner_ref.refs_0_, bf16[400,1024]{1,0:T(8,128)(2,1)} %collective-permute-done.2.outer_ref.refs_1_, bf16[1024,512]{1,0:T(8,128)(2,1)S(1)} %pad_maximum_fusion.refs_2_.refs_4_, ...), custom_call_target="tpu_custom_call" | custom-call | flops 1024 | bytes 1024 | tf_op jit(solution)/shard_map/pallas_call | solution.py:287
  78.0 4.0 %shard_map.102 = (f32[384,1024]{1,0:T(8,128)S(1)}, bf16[384,1024]{1,0:T(8,128)(2,1)S(1)}, f32[8,128]{1,0:T(8,128)}) custom-call(s32[9]{0:T(128)S(1)} %fusion.plan_ref, bf16[400,1024]{1,0:T(8,128)(2,1)} %collective-permute-done.3.refs_0_.refs_8_, bf16[400,1024]{1,0:T(8,128)(2,1)} %shard_map.95.refs_1_.refs_9_, ...), custom_call_target="tpu_custom_call" | custom-call | flops 1024 | bytes 1024 | tf_op jit(solution)/shard_map/pallas_call | solution.py:287
  84.0 2.0 %shard_map.101 = (f32[384,1024]{1,0:T(8,128)S(1)}, bf16[384,1024]{1,0:T(8,128)(2,1)S(1)}, f32[8,128]{1,0:T(8,128)}) custom-call(s32[9]{0:T(128)S(1)} %fusion.plan_ref, bf16[192,1024]{1,0:T(8,128)(2,1)S(1)} %collective-permute-done.12.refs_0_, bf16[192,1024]{1,0:T(8,128)(2,1)S(1)} %collective-permute-done.11.rest_2_.refs_1_, ...), custom_call_target="tpu_custom_call" | custom-call | flops 1024 | bytes 1024 | tf_op jit(solution)/shard_map/pallas_call | solution.py:287
  87.2 3.5 %shard_map.103.before_ref = f32[768,512]{1,0:T(8,128)S(1)} custom-call(s32[9]{0:T(128)S(1)} %fusion.plan_ref, bf16[384,512]{1,0:T(8,128)(2,1)S(1)} %get-tuple-element.40.refs_0_, bf16[384,512]{1,0:T(8,128)(2,1)S(1)} %get-tuple-element.41.refs_1_, f32[384,1024]{1,0:T(8,128)S(1)} %get-tuple-element.42.refs_2_, ...), custom_call_target="tpu_custom_call" | custom-call | flops 1024 | bytes 1024 | tf_op jit(solution)/shard_map/pallas_call | solution.py:373
  90.8 2.6 %shard_map.104 = (bf16[192,1024]{1,0:T(8,128)(2,1)S(1)}, f32[192,1024]{1,0:T(8,128)S(1)}, bf16[576,512]{1,0:T(8,128)(2,1)S(1)}) custom-call(s32[9]{0:T(128)S(1)} %fusion.plan_ref, f32[384,1024]{1,0:T(8,128)S(1)} %get-tuple-element.38.sums_ref, bf16[384,1024]{1,0:T(8,128)(2,1)S(1)} %collective-permute-done.16.got_ref, ...), custom_call_target="tpu_custom_call" | custom-call | flops 1024 | bytes 1024 | tf_op jit(solution)/shard_map/pallas_call | solution.py:412
  96.1 9.3 %collective-permute-done.21 = bf16[192,1024]{1,0:T(8,128)(2,1)S(1)} collective-permute-done((bf16[192,1024]{1,0:T(8,128)(2,1)S(1)}, bf16[192,1024]{1,0:T(8,128)(2,1)S(1)}, u32[]{:S(2)}, u32[]{:S(2)}) %collective-permute-start.21) | collective-permute-done | bytes 393248 | tf_op jit(solution)/shard_map/ppermute | solution.py:107
  105.5 5.8 %collective-permute-start.22 = (bf16[192,1024]{1,0:T(8,128)(2,1)S(1)}, bf16[192,1024]{1,0:T(8,128)(2,1)S(1)}, u32[]{:S(2)}, u32[]{:S(2)}) collective-permute-start(bf16[192,1024]{1,0:T(8,128)(2,1)S(1)} %add_convert_fusion.3.refs_0_), channel_id=1, source_target_pairs={{0,4},{12,8},{1,5},{13,9},{2,6},{14,10},{3,7},{15,11},{16,20},{28,... | collective-permute-start | bytes 1179656 | tf_op jit(solution)/shard_map/ppermute | solution.py:115
  114.3 6.5 %collective-permute-start.20 = (bf16[192,1024]{1,0:T(8,128)(2,1)S(1)}, bf16[192,1024]{1,0:T(8,128)(2,1)S(1)}, u32[]{:S(2)}, u32[]{:S(2)}) collective-permute-start(bf16[192,1024]{1,0:T(8,128)(2,1)S(1)} %add_convert_fusion.4.refs_0_), channel_id=1, source_target_pairs={{0,8},{12,4},{1,9},{13,5},{2,10},{14,6},{3,11},{15,7},{16,24},{28,... | collective-permute-start | bytes 1179656 | tf_op jit(solution)/shard_map/ppermute | solution.py:115
  124.5 2.6 %collective-permute-start.27 = (bf16[192,1024]{1,0:T(8,128)(2,1)S(1)}, bf16[192,1024]{1,0:T(8,128)(2,1)}, u32[]{:S(2)}, u32[]{:S(2)}) collective-permute-start(bf16[192,1024]{1,0:T(8,128)(2,1)S(1)} %add_convert_fusion.1), channel_id=1, source_target_pairs={{0,4},{4,0},{8,12},{12,8},{1,5},{5,1},{9,13},{13,9},{2,6},{6,2},{1... | collective-permute-start | bytes 1179656 | tf_op jit(solution)/shard_map/ppermute | solution.py:115
  129.8 7.8 %collective-permute-done.23 = bf16[192,1024]{1,0:T(8,128)(2,1)S(1)} collective-permute-done((bf16[192,1024]{1,0:T(8,128)(2,1)S(1)}, bf16[192,1024]{1,0:T(8,128)(2,1)S(1)}, u32[]{:S(2)}, u32[]{:S(2)}) %collective-permute-start.23) | collective-permute-done | bytes 393248 | tf_op jit(solution)/shard_map/ppermute | solution.py:115
  138.8 2.8 %collective-permute-done.27 = bf16[192,1024]{1,0:T(8,128)(2,1)} collective-permute-done((bf16[192,1024]{1,0:T(8,128)(2,1)S(1)}, bf16[192,1024]{1,0:T(8,128)(2,1)}, u32[]{:S(2)}, u32[]{:S(2)}) %collective-permute-start.27) | collective-permute-done | bytes 393248 | tf_op jit(solution)/shard_map/ppermute | solution.py:115
  141.6 2.1 %add_convert_fusion = bf16[192,1024]{1,0:T(8,128)(2,1)} fusion(bf16[192,1024]{1,0:T(8,128)(2,1)} %collective-permute-done.27, f32[192,1024]{1,0:T(8,128)S(1)} %convert_add_fusion, f32[192,1024]{1,0:T(8,128)S(1)} %get-tuple-element.49, bf16[192,1024]{1,0:T(8,128)(2,1)} %collective-permute-done.25), kind=kLoop, calls=%fused_computation.5 | loop fusion | flops 1179648 | bytes 2752512 | tf_op jit(solution)/shard_map/convert_element_type | solution.py:529
  (113 shorter events, 44.1 us)
Async XLA Ops:
  4.5 21.4 %collective-permute-start = (bf16[400,1024]{1,0:T(8,128)(2,1)S(1)}, bf16[400,1024]{1,0:T(8,128)(2,1)}, u32[]{:S(2)}, u32[]{:S(2)}) collective-permute-start(bf16[400,1024]{1,0:T(8,128)(2,1)S(1)} %shard_map.91.refs_1_.refs_4_.refs_5_), channel_id=1, source_target_pairs={{0,4},{4,0},{8,12},{12,8},{1,5},{5,1},{9,13},{13,9},{2,6},{6,2},{1... | collective-permute-start | bytes 2457608 | tf_op jit(solution)/shard_map/ppermute | solution.py:115
  7.6 21.6 %collective-permute-start.3 = (bf16[400,1024]{1,0:T(8,128)(2,1)S(1)}, bf16[400,1024]{1,0:T(8,128)(2,1)}, u32[]{:S(2)}, u32[]{:S(2)}) collective-permute-start(bf16[400,1024]{1,0:T(8,128)(2,1)S(1)} %shard_map.91.refs_1_.refs_4_.refs_5_), channel_id=1, source_target_pairs={{4,8},{8,4},{5,9},{9,5},{6,10},{10,6},{7,11},{11,7},{20,24},{24,20... | collective-permute-start | bytes 2457608 | tf_op jit(solution)/shard_map/ppermute | solution.py:115
  9.2 21.3 %collective-permute-start.7 = (bf16[384,1024]{1,0:T(8,128)(2,1)}, bf16[384,1024]{1,0:T(8,128)(2,1)}, u32[]{:S(2)}, u32[]{:S(2)}) collective-permute-start(bf16[384,1024]{1,0:T(8,128)(2,1)} %refs_0_.1), channel_id=1, source_target_pairs={{0,2},{1,3},{2,0},{3,1},{4,6},{5,7},{6,4},{7,5},{8,10},{9,11},{10,... | collective-permute-start | bytes 2359304 | tf_op jit(solution)/shard_map/ppermute | solution.py:107
  15.7 25.2 %collective-permute-start.9 = (bf16[2048,512]{1,0:T(8,128)(2,1)}, bf16[2048,512]{1,0:T(8,128)(2,1)S(1)}, u32[]{:S(2)}, u32[]{:S(2)}) collective-permute-start(bf16[2048,512]{1,0:T(8,128)(2,1)} %shard_map.93), channel_id=1, source_target_pairs={{0,1},{1,0},{2,3},{3,2},{4,5},{5,4},{6,7},{7,6},{8,9},{9,8},{10,11... | collective-permute-start | bytes 6291464 | tf_op jit(solution)/shard_map/ppermute | solution.py:111
  26.0 25.1 %collective-permute-start.6 = (bf16[400,1024]{1,0:T(8,128)(2,1)}, bf16[400,1024]{1,0:T(8,128)(2,1)}, u32[]{:S(2)}, u32[]{:S(2)}) collective-permute-start(bf16[400,1024]{1,0:T(8,128)(2,1)} %collective-permute-done.refs_0_.refs_6_.refs_7_), channel_id=1, source_target_pairs={{0,2},{1,3},{2,0},{3,1},{4,6},{5,7},{6,4},{7,5},{8,10},{9,11},{10,... | collective-permute-start | bytes 2457608 | tf_op jit(solution)/shard_map/ppermute | solution.py:107
  27.6 11.7 %collective-permute-start.1 = (bf16[400,1024]{1,0:T(8,128)(2,1)}, bf16[400,1024]{1,0:T(8,128)(2,1)}, u32[]{:S(2)}, u32[]{:S(2)}) collective-permute-start(bf16[400,1024]{1,0:T(8,128)(2,1)} %collective-permute-done.refs_0_.refs_6_.refs_7_), channel_id=1, source_target_pairs={{4,8},{8,4},{5,9},{9,5},{6,10},{10,6},{7,11},{11,7},{20,24},{24,20... | collective-permute-start | bytes 2457608 | tf_op jit(solution)/shard_map/ppermute | solution.py:115
  29.2 21.9 %collective-permute-start.5 = (bf16[400,1024]{1,0:T(8,128)(2,1)}, bf16[400,1024]{1,0:T(8,128)(2,1)}, u32[]{:S(2)}, u32[]{:S(2)}) collective-permute-start(bf16[400,1024]{1,0:T(8,128)(2,1)} %collective-permute-done.3.refs_0_.refs_8_), channel_id=1, source_target_pairs={{4,0},{8,12},{5,1},{9,13},{6,2},{10,14},{7,3},{11,15},{20,16},{24,... | collective-permute-start | bytes 2457608 | tf_op jit(solution)/shard_map/ppermute | solution.py:115
  32.5 15.6 %collective-permute-start.8 = (bf16[192,1024]{1,0:T(8,128)(2,1)S(1)}, bf16[192,1024]{1,0:T(8,128)(2,1)S(1)}, u32[]{:S(2)}, u32[]{:S(2)}) collective-permute-start(bf16[192,1024]{1,0:T(8,128)(2,1)S(1)} %shard_map.92), channel_id=1, source_target_pairs={{0,4},{12,8},{1,5},{13,9},{2,6},{14,10},{3,7},{15,11},{16,20},{28,... | collective-permute-start | bytes 1179656 | tf_op jit(solution)/shard_map/ppermute | solution.py:115
  39.3 20.2 %collective-permute-start.4 = (bf16[400,1024]{1,0:T(8,128)(2,1)}, bf16[400,1024]{1,0:T(8,128)(2,1)}, u32[]{:S(2)}, u32[]{:S(2)}) collective-permute-start(bf16[400,1024]{1,0:T(8,128)(2,1)} %collective-permute-done.3.refs_0_.refs_8_), channel_id=1, source_target_pairs={{4,6},{5,7},{6,4},{7,5},{8,10},{9,11},{10,8},{11,9},{20,22},{21,23... | collective-permute-start | bytes 2457608 | tf_op jit(solution)/shard_map/ppermute | solution.py:455
  40.9 29.3 %collective-permute-start.2 = (bf16[400,1024]{1,0:T(8,128)(2,1)}, bf16[400,1024]{1,0:T(8,128)(2,1)}, u32[]{:S(2)}, u32[]{:S(2)}) collective-permute-start(bf16[400,1024]{1,0:T(8,128)(2,1)} %collective-permute-done.1.refs_2_.inner_ref.refs_0_), channel_id=1, source_target_pairs={{4,0},{8,12},{5,1},{9,13},{6,2},{10,14},{7,3},{11,15},{20,16},{24,... | collective-permute-start | bytes 2457608 | tf_op jit(solution)/shard_map/ppermute | solution.py:115
  51.1 20.1 %collective-permute-start.10 = (bf16[400,1024]{1,0:T(8,128)(2,1)}, bf16[400,1024]{1,0:T(8,128)(2,1)S(1)}, u32[]{:S(2)}, u32[]{:S(2)}) collective-permute-start(bf16[400,1024]{1,0:T(8,128)(2,1)} %shard_map.95.refs_1_.refs_9_), channel_id=1, source_target_pairs={{0,2},{1,3},{2,0},{3,1},{12,14},{13,15},{14,12},{15,13},{16,18},{1... | collective-permute-start | bytes 2457608 | tf_op jit(solution)/shard_map/ppermute | solution.py:455
  54.4 22.4 %collective-permute-start.14 = (bf16[384,1024]{1,0:T(8,128)(2,1)}, bf16[384,1024]{1,0:T(8,128)(2,1)S(1)}, u32[]{:S(2)}, u32[]{:S(2)}) collective-permute-start(bf16[384,1024]{1,0:T(8,128)(2,1)} %copy-done.15), channel_id=1, source_target_pairs={{0,1},{1,0},{2,3},{3,2},{4,5},{5,4},{6,7},{7,6},{8,9},{9,8},{10,11... | collective-permute-start | bytes 2359304 | tf_op jit(solution)/shard_map/ppermute | solution.py:111
  58.9 18.2 %collective-permute-start.15 = (bf16[384,1024]{1,0:T(8,128)(2,1)S(1)}, bf16[384,1024]{1,0:T(8,128)(2,1)S(1)}, u32[]{:S(2)}, u32[]{:S(2)}) collective-permute-start(bf16[384,1024]{1,0:T(8,128)(2,1)S(1)} %get-tuple-element.36), channel_id=1, source_target_pairs={{0,1},{1,0},{2,3},{3,2},{4,5},{5,4},{6,7},{7,6},{8,9},{9,8},{10,11... | collective-permute-start | bytes 2359304 | tf_op jit(solution)/shard_map/ppermute | solution.py:111
  59.5 24.5 %collective-permute-start.13 = (bf16[192,1024]{1,0:T(8,128)(2,1)S(1)}, bf16[192,1024]{1,0:T(8,128)(2,1)S(1)}, u32[]{:S(2)}, u32[]{:S(2)}) collective-permute-start(bf16[192,1024]{1,0:T(8,128)(2,1)S(1)} %collective-permute-done.11.rest_2_.refs_1_), channel_id=1, source_target_pairs={{4,0},{8,12},{5,1},{9,13},{6,2},{10,14},{7,3},{11,15},{20,16},{24,... | collective-permute-start | bytes 1179656 | tf_op jit(solution)/shard_map/ppermute | solution.py:115
  73.9 16.9 %collective-permute-start.18 = (bf16[256,2048]{1,0:T(8,128)(2,1)S(1)}, bf16[256,2048]{1,0:T(8,128)(2,1)S(1)}, u32[]{:S(2)}, u32[]{:S(2)}) collective-permute-start(bf16[256,2048]{1,0:T(8,128)(2,1)S(1)} %copy-done.6), channel_id=1, source_target_pairs={{0,1},{1,0},{2,3},{3,2},{4,5},{5,4},{6,7},{7,6},{8,9},{9,8},{10,11... | collective-permute-start | bytes 3145736 | tf_op jit(solution)/shard_map/ppermute | solution.py:111
  93.4 12.1 %collective-permute-start.21 = (bf16[192,1024]{1,0:T(8,128)(2,1)S(1)}, bf16[192,1024]{1,0:T(8,128)(2,1)S(1)}, u32[]{:S(2)}, u32[]{:S(2)}) collective-permute-start(bf16[192,1024]{1,0:T(8,128)(2,1)S(1)} %get-tuple-element.48), channel_id=1, source_target_pairs={{0,2},{1,3},{2,0},{3,1},{4,6},{5,7},{6,4},{7,5},{8,10},{9,11},{10,... | collective-permute-start | bytes 1179656 | tf_op jit(solution)/shard_map/ppermute | solution.py:107
  95.5 18.7 %collective-permute-start.19 = (bf16[192,1024]{1,0:T(8,128)(2,1)S(1)}, bf16[192,1024]{1,0:T(8,128)(2,1)S(1)}, u32[]{:S(2)}, u32[]{:S(2)}) collective-permute-start(bf16[192,1024]{1,0:T(8,128)(2,1)S(1)} %get-tuple-element.46), channel_id=1, source_target_pairs={{0,2},{1,3},{2,0},{3,1},{4,6},{5,7},{6,4},{7,5},{8,10},{9,11},{10,... | collective-permute-start | bytes 1179656 | tf_op jit(solution)/shard_map/ppermute | solution.py:107
  105.5 17.4 %collective-permute-start.22 = (bf16[192,1024]{1,0:T(8,128)(2,1)S(1)}, bf16[192,1024]{1,0:T(8,128)(2,1)S(1)}, u32[]{:S(2)}, u32[]{:S(2)}) collective-permute-start(bf16[192,1024]{1,0:T(8,128)(2,1)S(1)} %add_convert_fusion.3.refs_0_), channel_id=1, source_target_pairs={{0,4},{12,8},{1,5},{13,9},{2,6},{14,10},{3,7},{15,11},{16,20},{28,... | collective-permute-start | bytes 1179656 | tf_op jit(solution)/shard_map/ppermute | solution.py:115
  111.3 15.8 %collective-permute-start.24 = (bf16[192,1024]{1,0:T(8,128)(2,1)S(1)}, bf16[192,1024]{1,0:T(8,128)(2,1)S(1)}, u32[]{:S(2)}, u32[]{:S(2)}) collective-permute-start(bf16[192,1024]{1,0:T(8,128)(2,1)S(1)} %add_convert_fusion.3.refs_0_), channel_id=1, source_target_pairs={{4,8},{8,4},{5,9},{9,5},{6,10},{10,6},{7,11},{11,7},{20,24},{24,20... | collective-permute-start | bytes 1179656 | tf_op jit(solution)/shard_map/ppermute | solution.py:115
  112.6 11.7 %collective-permute-start.26 = (bf16[192,1024]{1,0:T(8,128)(2,1)S(1)}, bf16[192,1024]{1,0:T(8,128)(2,1)S(1)}, u32[]{:S(2)}, u32[]{:S(2)}) collective-permute-start(bf16[192,1024]{1,0:T(8,128)(2,1)S(1)} %get-tuple-element.52), channel_id=1, source_target_pairs={{0,2},{1,3},{2,0},{3,1},{4,6},{5,7},{6,4},{7,5},{8,10},{9,11},{10,... | collective-permute-start | bytes 1179656 | tf_op jit(solution)/shard_map/ppermute | solution.py:107
  114.3 15.5 %collective-permute-start.20 = (bf16[192,1024]{1,0:T(8,128)(2,1)S(1)}, bf16[192,1024]{1,0:T(8,128)(2,1)S(1)}, u32[]{:S(2)}, u32[]{:S(2)}) collective-permute-start(bf16[192,1024]{1,0:T(8,128)(2,1)S(1)} %add_convert_fusion.4.refs_0_), channel_id=1, source_target_pairs={{0,8},{12,4},{1,9},{13,5},{2,10},{14,6},{3,11},{15,7},{16,24},{28,... | collective-permute-start | bytes 1179656 | tf_op jit(solution)/shard_map/ppermute | solution.py:115
  121.4 17.4 %collective-permute-start.25 = (bf16[192,1024]{1,0:T(8,128)(2,1)S(1)}, bf16[192,1024]{1,0:T(8,128)(2,1)}, u32[]{:S(2)}, u32[]{:S(2)}) collective-permute-start(bf16[192,1024]{1,0:T(8,128)(2,1)S(1)} %get-tuple-element.50), channel_id=1, source_target_pairs={{0,2},{1,3},{2,0},{3,1},{4,6},{5,7},{6,4},{7,5},{8,10},{9,11},{10,... | collective-permute-start | bytes 1179656 | tf_op jit(solution)/shard_map/ppermute | solution.py:107
  123.1 14.5 %collective-permute-start.23 = (bf16[192,1024]{1,0:T(8,128)(2,1)S(1)}, bf16[192,1024]{1,0:T(8,128)(2,1)S(1)}, u32[]{:S(2)}, u32[]{:S(2)}) collective-permute-start(bf16[192,1024]{1,0:T(8,128)(2,1)S(1)} %add_convert_fusion.2), channel_id=1, source_target_pairs={{4,12},{8,0},{5,13},{9,1},{6,14},{10,2},{7,15},{11,3},{20,28},{24,... | collective-permute-start | bytes 1179656 | tf_op jit(solution)/shard_map/ppermute | solution.py:115
  124.5 17.1 %collective-permute-start.27 = (bf16[192,1024]{1,0:T(8,128)(2,1)S(1)}, bf16[192,1024]{1,0:T(8,128)(2,1)}, u32[]{:S(2)}, u32[]{:S(2)}) collective-permute-start(bf16[192,1024]{1,0:T(8,128)(2,1)S(1)} %add_convert_fusion.1), channel_id=1, source_target_pairs={{0,4},{4,0},{8,12},{12,8},{1,5},{5,1},{9,13},{13,9},{2,6},{6,2},{1... | collective-permute-start | bytes 1179656 | tf_op jit(solution)/shard_map/ppermute | solution.py:115
  (28 other events, 127.9 us)

commit v25 on v22

--- a/solution.py
+++ b/solution.py
@@ -299,13 +299,22 @@
     return jnp.concatenate(hidden, axis=1)
 
 
-def hide(sums, got):
-    def body(sums_ref, got_ref, out_ref, token_ref):
+def hide(plan, sums, got, facts):
+    shapes = [
+        jax.ShapeDtypeStruct((sums.shape[0], sums.shape[1] // 2), jnp.bfloat16),
+        jax.ShapeDtypeStruct((FACT_ROWS, facts.shape[1]), jnp.bfloat16),
+        TOKEN,
+    ]
+
+    def body(plan_ref, sums_ref, got_ref, block_ref, out_ref, facts_ref, token_ref, sem):
+        fetch = facts_of(plan_ref, block_ref, block_ref, facts_ref, sem)
         out_ref[...] = hidden_rows(sums_ref, got_ref)
         token_ref[...] = jnp.zeros(TOKEN.shape, TOKEN.dtype)
-
-    shape = jax.ShapeDtypeStruct((sums.shape[0], sums.shape[1] // 2), jnp.bfloat16)
-    return on_core(body, [shape, TOKEN], [VMEM, VMEM])(sums, got)
+        fetch.wait()
+
+    return on_core(
+        body, shapes, [SMEM, VMEM, VMEM, ANYWHERE], [pltpu.SemaphoreType.DMA((1,))]
+    )(plan, sums, got, facts)
 
 
 def factors_of(slot, plan, facts, rows):
@@ -325,14 +334,13 @@
 
 def facts_of(plan_ref, inner_ref, outer_ref, buffer, sem):
     last = inner_ref.shape[0] - FACT_ROWS
-
-    def run(source):
-        (copy,) = copies(source, last, buffer, FACT_ROWS, 1, sem, 0)
-        copy.start()
-        copy.wait()
-
-    by_kind(plan_ref, (inner_ref, outer_ref), run)
-    return buffer
+    (fetch,) = copies(inner_ref, last, buffer, FACT_ROWS, 1, sem, 0)
+    if inner_ref is outer_ref:
+        fetch.start()
+        return fetch
+    (other,) = copies(outer_ref, last, buffer, FACT_ROWS, 1, sem, 0)
+    by_kind(plan_ref, (fetch, other), lambda copy: copy.start())
+    return fetch
 
 
 def down(held, own_ref, lent_ref, sent_ref, kept_ref):
@@ -343,35 +351,38 @@
         out[...] = result.astype(out.dtype)
 
 
-def fact_scratch(width):
-    return [pltpu.VMEM((FACT_ROWS, width), jnp.bfloat16), pltpu.SemaphoreType.DMA((1,))]
-
-
-def collect(owned, plan, hidden, sums, got, facts):
+def collect(owned, plan, hidden, facts, sums, got, third, last):
     rows, units = hidden[0].shape
-    slots = len(facts)
+    width = facts[0].shape[1]
 
     def body(plan_ref, *refs):
-        hidden_refs, refs = refs[: slots - 1], refs[slots - 1 :]
+        hidden_refs, fact_refs, refs = refs[:2], refs[2:4], refs[4:]
         sums_ref, got_ref, refs = refs[0], refs[1], refs[2:]
-        fact_refs, (out_ref, buffer, sem) = refs[: 2 * slots], refs[2 * slots :]
-        factors = []
-        for slot in range(slots):
-            facts_of(plan_ref, *fact_refs[2 * slot : 2 * slot + 2], buffer, sem)
-            factors.append(factors_of(slot, plan_ref, buffer, rows))
+        third_refs, last_refs, refs = refs[:2], refs[2:4], refs[4:]
+        out_ref, last_ref, buffer, sem, last_sem = refs
+        fetch = facts_of(plan_ref, *third_refs, buffer, sem)
+        fetch_last = facts_of(plan_ref, *last_refs, last_ref, last_sem)
+        every = [ref[...] for ref in hidden_refs] + [hidden_rows(sums_ref, got_ref)]
+        every = jnp.concatenate(every, axis=0)
+        fetch.wait()
+        factors = [
+            factors_of(slot, plan_ref, ref, rows) for slot, ref in enumerate([*fact_refs, buffer])
+        ]
         factor = jnp.concatenate([pair[0] for pair in factors], axis=1)
         owner = jnp.concatenate([pair[1] for pair in factors], axis=1)
-        every = [ref[...] for ref in hidden_refs] + [hidden_rows(sums_ref, got_ref)]
-        every = jnp.concatenate(every, axis=0)
         for index in range(4):
             span = slice(index * owned, (index + 1) * owned)
             out_ref[span, :] = chunk_rows(owned, index, plan_ref, factor, owner, every)
-
-    fact_blocks = [block for pair_of in facts for block in pair_of]
-    specs = [SMEM] + [VMEM] * (slots + 1) + [ANYWHERE] * len(fact_blocks)
-    shape = jax.ShapeDtypeStruct((4 * owned, units), jnp.float32)
-    return on_core(body, shape, specs, fact_scratch(facts[0][0].shape[1]))(
-        plan, *hidden, sums, got, *fact_blocks
+        fetch_last.wait()
+
+    shapes = [
+        jax.ShapeDtypeStruct((4 * owned, units), jnp.float32),
+        jax.ShapeDtypeStruct((FACT_ROWS, width), jnp.bfloat16),
+    ]
+    scratch = [pltpu.VMEM((FACT_ROWS, width), jnp.bfloat16)]
+    scratch += [pltpu.SemaphoreType.DMA((1,))] * 2
+    return on_core(body, shapes, [SMEM] + [VMEM] * 6 + [ANYWHERE] * 4, scratch)(
+        plan, *hidden, *facts, sums, got, *third, *last
     )
 
 
@@ -383,10 +394,9 @@
         jax.ShapeDtypeStruct((owned, width), jnp.float32),
     ]
 
-    def first(plan_ref, sums_ref, got_ref, inner_ref, outer_ref, before_ref, *refs):
-        own_ref, lent_ref, sent_ref, kept_ref, held_ref, buffer, sem = refs
-        facts_of(plan_ref, inner_ref, outer_ref, buffer, sem)
-        factor, owner = factors_of(slot, plan_ref, buffer, sums_ref.shape[0])
+    def first(plan_ref, sums_ref, got_ref, facts_ref, before_ref, *refs):
+        own_ref, lent_ref, sent_ref, kept_ref, held_ref = refs
+        factor, owner = factors_of(slot, plan_ref, facts_ref, sums_ref.shape[0])
         hidden = hidden_rows(sums_ref, got_ref)
         for index in range(4):
             rows = chunk_rows(owned, index, plan_ref, factor, owner, hidden)
@@ -408,10 +418,9 @@
         return on_core(body, pair * len(indices), [VMEM] * len(operands))(*operands)
 
     held_shape = jax.ShapeDtypeStruct((3 * owned, 2 * units), jnp.bfloat16)
-    specs = [SMEM, VMEM, VMEM, ANYWHERE, ANYWHERE] + [VMEM] * 3
-    sent, kept, held = on_core(
-        first, pair + [held_shape], specs, fact_scratch(facts[0].shape[1])
-    )(plan, sums, got, *facts, before, down_own, down_lent)
+    sent, kept, held = on_core(first, pair + [held_shape], [SMEM] + [VMEM] * 6)(
+        plan, sums, got, facts, before, down_own, down_lent
+    )
     rest = others([1, 2])
     chunks = [(sent, kept), (rest[0], rest[1]), (rest[2], rest[3])]
     return chunks, lambda *waits: others([3], *waits)
@@ -486,8 +495,8 @@
         part_of(plan, *last, 0, half, *second_far, middle_far, ready_0, ready_1)
     )
     outward_far = along(middle_far, OUTWARD)
-    hidden_0, hidden_here = hide(sums_0, got_0)
-    hidden_1, hidden_there = hide(sums_1, got_1)
+    hidden_0, facts_0, hidden_here = hide(plan, sums_0, got_0, own)
+    hidden_1, facts_1, hidden_there = hide(plan, sums_1, got_1, beside)
     sums_2, send_2, _ = partial_sums(plan, whole, [(second, second_far)], weights, (0, 1))
     got_2 = across_cores(send_2)
     near, _ = partial_sums(plan, whole, [(last,)], weights, (0,), send=False)
@@ -501,16 +510,10 @@
         waits=[hidden_here, hidden_there],
     )
     got_3 = across_cores(send_3)
-    total = collect(
-        owned,
-        plan,
-        (hidden_0, hidden_1),
-        sums_2,
-        got_2,
-        [(own, own), (beside, beside), second],
-    )
+    hidden, facts = (hidden_0, hidden_1), (facts_0, facts_1)
+    total, facts_3 = collect(owned, plan, hidden, facts, sums_2, got_2, second, last)
     chunks, last_chunk = finish(
-        owned, 3, plan, sums_3, got_3, last, total, kept_down, lent_down
+        owned, 3, plan, sums_3, got_3, facts_3, total, kept_down, lent_down
     )
 
     def joined(sent, kept):

time: 144 us -> 142 us (0.986)
  local copies, waits for them, and re-layouts: 15.9 us -> 14.2 us
    unnamed x46, local copies, waits for them, and re-layouts: 9 us -> 7.37 us
  transfers between devices with their start and end apart: 28 -> 28, of which waited for: 10 -> 9; matrix products, arithmetic and copies ran while one was open for 6% -> 7% of each run, Pallas kernels for 17% -> 18%
where the time goes in v25:
time: 142 us
  starting transfers between devices  49.1 us (35%)
  waiting for transfers between devices  44.9 us (32%)
  Pallas kernels  29.4 us (21%)
  local copies, waits for them, and re-layouts  14.2 us (10%)
  other arithmetic  3.36 us (2%)
    ppermute x13, waiting for transfers between devices, along(): return lax.ppermute(block, 'blk', route)  35 us
    ppermute x13, starting transfers between devices, along(): return lax.ppermute(block, 'blk', route)  34.9 us
    pallas_call x5, Pallas kernels, partial_sums(): return on_core(body, shapes + [TOKEN], specs)(*operands, *waits)  15.3 us
    ppermute x7, starting transfers between devices, across_chips(): return lax.ppermute(block, 'tp', [(i, i ^ 2) for i in range(4)])  9.02 us
    ppermute x7, waiting for transfers between devices, across_chips(): return lax.ppermute(block, 'tp', [(i, i ^ 2) for i in range(4)])  8.83 us
    unnamed x46, local copies, waits for them, and re-layouts  7.37 us
    pallas_call x2, Pallas kernels, part_of(): pl.pallas_call(body, out_shape=shape, in_specs=[SMEM] + [ANYWHERE] * (2 +...  4.16 us
    ppermute x2, starting transfers between devices, at_kind(): return lax.ppermute(block, ('blk', 'tp'), pairs)  4.13 us
  transfers between devices with their start and end apart: 28, of which 9 were waited for; matrix products, arithmetic and copies ran while one was open for 7% of the time, Pallas kernels for 18%

profile of v25, /device:TPU:0, one launch (start us, length us, event | category | flops | bytes accessed | tf_op | source)
XLA Modules:
  0.0 141.6 jit_solution(16389366453964262350)
XLA Ops:
  4.5 3.1 %collective-permute-start = (bf16[400,1024]{1,0:T(8,128)(2,1)S(1)}, bf16[400,1024]{1,0:T(8,128)(2,1)}, u32[]{:S(2)}, u32[]{:S(2)}) collective-permute-start(bf16[400,1024]{1,0:T(8,128)(2,1)S(1)} %shard_map.91.refs_1_.block_ref), channel_id=1, source_target_pairs={{0,4},{4,0},{8,12},{12,8},{1,5},{5,1},{9,13},{13,9},{2,6},{6,2},{1... | collective-permute-start | bytes 2457608 | tf_op jit(solution)/shard_map/ppermute | solution.py:115
  10.7 3.4 %dynamic-slice_bitcast_fusion.6 = (bf16[1024,256]{1,0:T(8,128)(2,1)S(1)}, bf16[1024,256]{1,0:T(8,128)(2,1)S(1)}, bf16[1024,256]{1,0:T(8,128)(2,1)S(1)}, bf16[102...) fusion(bf16[4,1024,256]{2,1,0:T(8,128)(2,1)} %bitcast.32, ...), kind=kLoop, calls=%fused_computation.17 | loop fusion | bytes 8388624 | tf_op jit(solution)/shard_map/jit(dynamic_index_in_dim)/squeeze | solution.py:452
  16.3 2.7 %dynamic-slice_bitcast_fusion.1 = (bf16[256,1024]{1,0:T(8,128)(2,1)}, bf16[256,1024]{1,0:T(8,128)(2,1)S(1)}, bf16[256,1024]{1,0:T(8,128)(2,1)S(1)}, bf16[256,1024]{1,0:T(8,128)(2,1)}) fusion(bf16[1,256,4096]{2,1,0:T(8,128)(2,1)} %param.12, s32[]{:T(128)S(6)} %select_n.39, s32[]{:T(128)S(6)} %select_n.38, s32[]{:T(128)S(6)} %select_n.37, s32[]{:T(128)S(6)} %select_n.40), kind=kLoop, calls=%fused_computation.12 | loop fusion | bytes 4194320 | tf_op jit(solution)/shard_map/dynamic_slice | solution.py:458
  19.1 6.9 %collective-permute-done.refs_0_.block_ref = bf16[400,1024]{1,0:T(8,128)(2,1)} collective-permute-done((bf16[400,1024]{1,0:T(8,128)(2,1)S(1)}, bf16[400,1024]{1,0:T(8,128)(2,1)}, u32[]{:S(2)}, u32[]{:S(2)}) %collective-permute-start) | collective-permute-done | bytes 819232 | tf_op jit(solution)/shard_map/ppermute | solution.py:115
  30.5 2.0 %shard_map.92 = bf16[192,1024]{1,0:T(8,128)(2,1)S(1)} custom-call(s32[9]{0:T(128)S(1)} %fusion.plan_ref, bf16[384,1024]{1,0:T(8,128)(2,1)} %collective-permute-done.7.inner_ref.outer_ref.refs_1_, bf16[384,1024]{1,0:T(8,128)(2,1)} %collective-permute-done.7.inner_ref.outer_ref.refs_1_), custom_call_target="tpu_custom_call" | custom-call | flops 17179869184 | bytes 1024 | tf_op jit(solution)/shard_map/pallas_call | solution.py:192
  32.5 6.4 %collective-permute-start.8 = (bf16[192,1024]{1,0:T(8,128)(2,1)S(1)}, bf16[192,1024]{1,0:T(8,128)(2,1)S(1)}, u32[]{:S(2)}, u32[]{:S(2)}) collective-permute-start(bf16[192,1024]{1,0:T(8,128)(2,1)S(1)} %shard_map.92), channel_id=1, source_target_pairs={{0,4},{12,8},{1,5},{13,9},{2,6},{14,10},{3,7},{15,11},{16,20},{28,... | collective-permute-start | bytes 1179656 | tf_op jit(solution)/shard_map/ppermute | solution.py:115
  42.2 3.2 %shard_map.94 = (f32[384,1024]{1,0:T(8,128)S(1)}, bf16[384,1024]{1,0:T(8,128)(2,1)S(1)}, f32[8,128]{1,0:T(8,128)S(1)}) custom-call(s32[9]{0:T(128)S(1)} %fusion.plan_ref, bf16[384,1024]{1,0:T(8,128)(2,1)} %refs_0_.1, bf16[384,1024]{1,0:T(8,128)(2,1)} %collective-permute-done.7.inner_ref.outer_ref.refs_1_, ...), custom_call_target="tpu_custom_call" | custom-call | flops 1024 | bytes 1024 | tf_op jit(solution)/shard_map/pallas_call | solution.py:287
  48.8 2.3 %collective-permute-done.5.refs_0_ = bf16[400,1024]{1,0:T(8,128)(2,1)} collective-permute-done((bf16[400,1024]{1,0:T(8,128)(2,1)}, bf16[400,1024]{1,0:T(8,128)(2,1)}, u32[]{:S(2)}, u32[]{:S(2)}) %collective-permute-start.5) | collective-permute-done | bytes 819232 | tf_op jit(solution)/shard_map/ppermute | solution.py:115
  51.1 2.6 %collective-permute-start.10 = (bf16[400,1024]{1,0:T(8,128)(2,1)}, bf16[400,1024]{1,0:T(8,128)(2,1)S(1)}, u32[]{:S(2)}, u32[]{:S(2)}) collective-permute-start(bf16[400,1024]{1,0:T(8,128)(2,1)} %shard_map.95.refs_1_.refs_7_), channel_id=1, source_target_pairs={{0,2},{1,3},{2,0},{3,1},{12,14},{13,15},{14,12},{15,13},{16,18},{1... | collective-permute-start | bytes 2457608 | tf_op jit(solution)/shard_map/ppermute | solution.py:466
  55.7 3.2 %shard_map.96 = (f32[384,1024]{1,0:T(8,128)S(1)}, bf16[384,1024]{1,0:T(8,128)(2,1)S(1)}, f32[8,128]{1,0:T(8,128)S(1)}) custom-call(s32[9]{0:T(128)S(1)} %fusion.plan_ref, bf16[400,1024]{1,0:T(8,128)(2,1)} %collective-permute-done.refs_0_.block_ref, bf16[400,1024]{1,0:T(8,128)(2,1)} %collective-permute-done.6.refs_1_, ...), custom_call_target="tpu_custom_call" | custom-call | flops 1024 | bytes 1024 | tf_op jit(solution)/shard_map/pallas_call | solution.py:287
  60.8 9.4 %collective-permute-done.2.outer_ref.refs_1_.refs_9_ = bf16[400,1024]{1,0:T(8,128)(2,1)} collective-permute-done((bf16[400,1024]{1,0:T(8,128)(2,1)}, bf16[400,1024]{1,0:T(8,128)(2,1)}, u32[]{:S(2)}, u32[]{:S(2)}) %collective-permute-start.2) | collective-permute-done | bytes 819232 | tf_op jit(solution)/shard_map/ppermute | solution.py:115
  71.3 2.2 %shard_map.97 = bf16[192,1024]{1,0:T(8,128)(2,1)S(1)} custom-call(s32[9]{0:T(128)S(1)} %fusion.plan_ref, bf16[400,1024]{1,0:T(8,128)(2,1)} %collective-permute-done.1.refs_2_.inner_ref.refs_0_.refs_8_, bf16[400,1024]{1,0:T(8,128)(2,1)} %collective-permute-done.2.outer_ref.refs_1_.refs_9_, bf16[400,1024]{1,0:T(8,128)(2,1)} %collective-permute-done.4.rest_0_.refs_2_, ...), custom_call_target="tpu_custom_call" | custom-call | flops 1024 | bytes 1024 | tf_op jit(solution)/shard_map/pallas_call | solution.py:192
  74.1 3.0 %shard_map.98 = (f32[384,1024]{1,0:T(8,128)S(1)}, f32[8,128]{1,0:T(8,128)}) custom-call(s32[9]{0:T(128)S(1)} %fusion.plan_ref, bf16[400,1024]{1,0:T(8,128)(2,1)} %collective-permute-done.1.refs_2_.inner_ref.refs_0_.refs_8_, bf16[400,1024]{1,0:T(8,128)(2,1)} %collective-permute-done.2.outer_ref.refs_1_.refs_9_, ...), custom_call_target="tpu_custom_call" | custom-call | flops 1024 | bytes 1024 | tf_op jit(solution)/shard_map/pallas_call | solution.py:287
  79.3 4.0 %shard_map.102 = (f32[384,1024]{1,0:T(8,128)S(1)}, bf16[384,1024]{1,0:T(8,128)(2,1)S(1)}, f32[8,128]{1,0:T(8,128)}) custom-call(s32[9]{0:T(128)S(1)} %fusion.plan_ref, bf16[400,1024]{1,0:T(8,128)(2,1)} %collective-permute-done.3.refs_0_.refs_6_, bf16[400,1024]{1,0:T(8,128)(2,1)} %shard_map.95.refs_1_.refs_7_, ...), custom_call_target="tpu_custom_call" | custom-call | flops 1024 | bytes 1024 | tf_op jit(solution)/shard_map/pallas_call | solution.py:287
  84.0 2.0 %shard_map.101 = (f32[384,1024]{1,0:T(8,128)S(1)}, bf16[384,1024]{1,0:T(8,128)(2,1)S(1)}, f32[8,128]{1,0:T(8,128)}) custom-call(s32[9]{0:T(128)S(1)} %fusion.plan_ref, bf16[192,1024]{1,0:T(8,128)(2,1)S(1)} %collective-permute-done.12.refs_0_, bf16[192,1024]{1,0:T(8,128)(2,1)S(1)} %collective-permute-done.11.rest_2_.refs_1_, ...), custom_call_target="tpu_custom_call" | custom-call | flops 1024 | bytes 1024 | tf_op jit(solution)/shard_map/pallas_call | solution.py:287
  86.1 2.5 %shard_map.103 = (f32[768,512]{1,0:T(8,128)S(1)}, bf16[16,1024]{1,0:T(8,128)(2,1)S(1)}) custom-call(s32[9]{0:T(128)S(1)} %fusion.plan_ref, bf16[384,512]{1,0:T(8,128)(2,1)S(1)} %get-tuple-element.44.refs_0_, bf16[384,512]{1,0:T(8,128)(2,1)S(1)} %get-tuple-element.45.refs_1_, bf16[16,1024]{1,0:T(8,128)(2,1)S(1)} %get-tuple-element.46.refs_2_, ...), custom_call_target="tpu_custom_call" | custom-call | flops 1024 | bytes 1024 | tf_op jit(solution)/shard_map/pallas_call | solution.py:384
  88.7 1.8 %shard_map.104 = (bf16[192,1024]{1,0:T(8,128)(2,1)S(1)}, f32[192,1024]{1,0:T(8,128)S(1)}, bf16[576,512]{1,0:T(8,128)(2,1)S(1)}) custom-call(s32[9]{0:T(128)S(1)} %fusion.plan_ref, f32[384,1024]{1,0:T(8,128)S(1)} %get-tuple-element.42.sums_ref, bf16[384,1024]{1,0:T(8,128)(2,1)S(1)} %collective-permute-done.16.got_ref, ...), custom_call_target="tpu_custom_call" | custom-call | flops 1024 | bytes 1024 | tf_op jit(solution)/shard_map/pallas_call | solution.py:421
  93.6 8.8 %collective-permute-done.19 = bf16[192,1024]{1,0:T(8,128)(2,1)S(1)} collective-permute-done((bf16[192,1024]{1,0:T(8,128)(2,1)S(1)}, bf16[192,1024]{1,0:T(8,128)(2,1)S(1)}, u32[]{:S(2)}, u32[]{:S(2)}) %collective-permute-start.19) | collective-permute-done | bytes 393248 | tf_op jit(solution)/shard_map/ppermute | solution.py:107
  102.5 6.0 %collective-permute-start.23 = (bf16[192,1024]{1,0:T(8,128)(2,1)S(1)}, bf16[192,1024]{1,0:T(8,128)(2,1)S(1)}, u32[]{:S(2)}, u32[]{:S(2)}) collective-permute-start(bf16[192,1024]{1,0:T(8,128)(2,1)S(1)} %add_convert_fusion.4), channel_id=1, source_target_pairs={{0,4},{12,8},{1,5},{13,9},{2,6},{14,10},{3,7},{15,11},{16,20},{28,... | collective-permute-start | bytes 1179656 | tf_op jit(solution)/shard_map/ppermute | solution.py:115
  110.9 7.1 %collective-permute-start.22 = (bf16[192,1024]{1,0:T(8,128)(2,1)S(1)}, bf16[192,1024]{1,0:T(8,128)(2,1)S(1)}, u32[]{:S(2)}, u32[]{:S(2)}) collective-permute-start(bf16[192,1024]{1,0:T(8,128)(2,1)S(1)} %add_convert_fusion.3.refs_0_), channel_id=1, source_target_pairs={{0,8},{12,4},{1,9},{13,5},{2,10},{14,6},{3,11},{15,7},{16,24},{28,... | collective-permute-start | bytes 1179656 | tf_op jit(solution)/shard_map/ppermute | solution.py:115
  121.7 2.6 %collective-permute-start.27 = (bf16[192,1024]{1,0:T(8,128)(2,1)S(1)}, bf16[192,1024]{1,0:T(8,128)(2,1)S(1)}, u32[]{:S(2)}, u32[]{:S(2)}) collective-permute-start(bf16[192,1024]{1,0:T(8,128)(2,1)S(1)} %add_convert_fusion.1), channel_id=1, source_target_pairs={{0,4},{4,0},{8,12},{12,8},{1,5},{5,1},{9,13},{13,9},{2,6},{6,2},{1... | collective-permute-start | bytes 1179656 | tf_op jit(solution)/shard_map/ppermute | solution.py:115
  124.3 3.2 %collective-permute-done.22 = bf16[192,1024]{1,0:T(8,128)(2,1)S(1)} collective-permute-done((bf16[192,1024]{1,0:T(8,128)(2,1)S(1)}, bf16[192,1024]{1,0:T(8,128)(2,1)S(1)}, u32[]{:S(2)}, u32[]{:S(2)}) %collective-permute-start.22) | collective-permute-done | bytes 393248 | tf_op jit(solution)/shard_map/ppermute | solution.py:115
  127.5 10.3 %collective-permute-done.24 = bf16[192,1024]{1,0:T(8,128)(2,1)S(1)} collective-permute-done((bf16[192,1024]{1,0:T(8,128)(2,1)S(1)}, bf16[192,1024]{1,0:T(8,128)(2,1)S(1)}, u32[]{:S(2)}, u32[]{:S(2)}) %collective-permute-start.24) | collective-permute-done | bytes 393248 | tf_op jit(solution)/shard_map/ppermute | solution.py:115
  138.1 2.5 %collective-permute-done.27 = bf16[192,1024]{1,0:T(8,128)(2,1)S(1)} collective-permute-done((bf16[192,1024]{1,0:T(8,128)(2,1)S(1)}, bf16[192,1024]{1,0:T(8,128)(2,1)S(1)}, u32[]{:S(2)}, u32[]{:S(2)}) %collective-permute-start.27) | collective-permute-done | bytes 393248 | tf_op jit(solution)/shard_map/ppermute | solution.py:115
  (108 shorter events, 39.8 us)
Async XLA Ops:
  4.5 21.4 %collective-permute-start = (bf16[400,1024]{1,0:T(8,128)(2,1)S(1)}, bf16[400,1024]{1,0:T(8,128)(2,1)}, u32[]{:S(2)}, u32[]{:S(2)}) collective-permute-start(bf16[400,1024]{1,0:T(8,128)(2,1)S(1)} %shard_map.91.refs_1_.block_ref), channel_id=1, source_target_pairs={{0,4},{4,0},{8,12},{12,8},{1,5},{5,1},{9,13},{13,9},{2,6},{6,2},{1... | collective-permute-start | bytes 2457608 | tf_op jit(solution)/shard_map/ppermute | solution.py:115
  7.6 21.6 %collective-permute-start.3 = (bf16[400,1024]{1,0:T(8,128)(2,1)S(1)}, bf16[400,1024]{1,0:T(8,128)(2,1)}, u32[]{:S(2)}, u32[]{:S(2)}) collective-permute-start(bf16[400,1024]{1,0:T(8,128)(2,1)S(1)} %shard_map.91.refs_1_.block_ref), channel_id=1, source_target_pairs={{4,8},{8,4},{5,9},{9,5},{6,10},{10,6},{7,11},{11,7},{20,24},{24,20... | collective-permute-start | bytes 2457608 | tf_op jit(solution)/shard_map/ppermute | solution.py:115
  9.2 21.3 %collective-permute-start.7 = (bf16[384,1024]{1,0:T(8,128)(2,1)}, bf16[384,1024]{1,0:T(8,128)(2,1)}, u32[]{:S(2)}, u32[]{:S(2)}) collective-permute-start(bf16[384,1024]{1,0:T(8,128)(2,1)} %refs_0_.1), channel_id=1, source_target_pairs={{0,2},{1,3},{2,0},{3,1},{4,6},{5,7},{6,4},{7,5},{8,10},{9,11},{10,... | collective-permute-start | bytes 2359304 | tf_op jit(solution)/shard_map/ppermute | solution.py:107
  15.7 25.2 %collective-permute-start.9 = (bf16[2048,512]{1,0:T(8,128)(2,1)}, bf16[2048,512]{1,0:T(8,128)(2,1)S(1)}, u32[]{:S(2)}, u32[]{:S(2)}) collective-permute-start(bf16[2048,512]{1,0:T(8,128)(2,1)} %shard_map.93), channel_id=1, source_target_pairs={{0,1},{1,0},{2,3},{3,2},{4,5},{5,4},{6,7},{7,6},{8,9},{9,8},{10,11... | collective-permute-start | bytes 6291464 | tf_op jit(solution)/shard_map/ppermute | solution.py:111
  26.0 25.1 %collective-permute-start.6 = (bf16[400,1024]{1,0:T(8,128)(2,1)}, bf16[400,1024]{1,0:T(8,128)(2,1)}, u32[]{:S(2)}, u32[]{:S(2)}) collective-permute-start(bf16[400,1024]{1,0:T(8,128)(2,1)} %collective-permute-done.refs_0_.block_ref), channel_id=1, source_target_pairs={{0,2},{1,3},{2,0},{3,1},{4,6},{5,7},{6,4},{7,5},{8,10},{9,11},{10,... | collective-permute-start | bytes 2457608 | tf_op jit(solution)/shard_map/ppermute | solution.py:107
  27.6 11.7 %collective-permute-start.1 = (bf16[400,1024]{1,0:T(8,128)(2,1)}, bf16[400,1024]{1,0:T(8,128)(2,1)}, u32[]{:S(2)}, u32[]{:S(2)}) collective-permute-start(bf16[400,1024]{1,0:T(8,128)(2,1)} %collective-permute-done.refs_0_.block_ref), channel_id=1, source_target_pairs={{4,8},{8,4},{5,9},{9,5},{6,10},{10,6},{7,11},{11,7},{20,24},{24,20... | collective-permute-start | bytes 2457608 | tf_op jit(solution)/shard_map/ppermute | solution.py:115
  29.2 21.9 %collective-permute-start.5 = (bf16[400,1024]{1,0:T(8,128)(2,1)}, bf16[400,1024]{1,0:T(8,128)(2,1)}, u32[]{:S(2)}, u32[]{:S(2)}) collective-permute-start(bf16[400,1024]{1,0:T(8,128)(2,1)} %collective-permute-done.3.refs_0_.refs_6_), channel_id=1, source_target_pairs={{4,0},{8,12},{5,1},{9,13},{6,2},{10,14},{7,3},{11,15},{20,16},{24,... | collective-permute-start | bytes 2457608 | tf_op jit(solution)/shard_map/ppermute | solution.py:115
  32.5 15.5 %collective-permute-start.8 = (bf16[192,1024]{1,0:T(8,128)(2,1)S(1)}, bf16[192,1024]{1,0:T(8,128)(2,1)S(1)}, u32[]{:S(2)}, u32[]{:S(2)}) collective-permute-start(bf16[192,1024]{1,0:T(8,128)(2,1)S(1)} %shard_map.92), channel_id=1, source_target_pairs={{0,4},{12,8},{1,5},{13,9},{2,6},{14,10},{3,7},{15,11},{16,20},{28,... | collective-permute-start | bytes 1179656 | tf_op jit(solution)/shard_map/ppermute | solution.py:115
  39.3 20.2 %collective-permute-start.4 = (bf16[400,1024]{1,0:T(8,128)(2,1)}, bf16[400,1024]{1,0:T(8,128)(2,1)}, u32[]{:S(2)}, u32[]{:S(2)}) collective-permute-start(bf16[400,1024]{1,0:T(8,128)(2,1)} %collective-permute-done.3.refs_0_.refs_6_), channel_id=1, source_target_pairs={{4,6},{5,7},{6,4},{7,5},{8,10},{9,11},{10,8},{11,9},{20,22},{21,23... | collective-permute-start | bytes 2457608 | tf_op jit(solution)/shard_map/ppermute | solution.py:466
  40.9 29.3 %collective-permute-start.2 = (bf16[400,1024]{1,0:T(8,128)(2,1)}, bf16[400,1024]{1,0:T(8,128)(2,1)}, u32[]{:S(2)}, u32[]{:S(2)}) collective-permute-start(bf16[400,1024]{1,0:T(8,128)(2,1)} %collective-permute-done.1.refs_2_.inner_ref.refs_0_.refs_8_), channel_id=1, source_target_pairs={{4,0},{8,12},{5,1},{9,13},{6,2},{10,14},{7,3},{11,15},{20,16},{24,... | collective-permute-start | bytes 2457608 | tf_op jit(solution)/shard_map/ppermute | solution.py:115
  51.1 20.1 %collective-permute-start.10 = (bf16[400,1024]{1,0:T(8,128)(2,1)}, bf16[400,1024]{1,0:T(8,128)(2,1)S(1)}, u32[]{:S(2)}, u32[]{:S(2)}) collective-permute-start(bf16[400,1024]{1,0:T(8,128)(2,1)} %shard_map.95.refs_1_.refs_7_), channel_id=1, source_target_pairs={{0,2},{1,3},{2,0},{3,1},{12,14},{13,15},{14,12},{15,13},{16,18},{1... | collective-permute-start | bytes 2457608 | tf_op jit(solution)/shard_map/ppermute | solution.py:466
  54.4 22.7 %collective-permute-start.14 = (bf16[384,1024]{1,0:T(8,128)(2,1)}, bf16[384,1024]{1,0:T(8,128)(2,1)S(1)}, u32[]{:S(2)}, u32[]{:S(2)}) collective-permute-start(bf16[384,1024]{1,0:T(8,128)(2,1)} %copy-done.15), channel_id=1, source_target_pairs={{0,1},{1,0},{2,3},{3,2},{4,5},{5,4},{6,7},{7,6},{8,9},{9,8},{10,11... | collective-permute-start | bytes 2359304 | tf_op jit(solution)/shard_map/ppermute | solution.py:111
  58.9 19.1 %collective-permute-start.15 = (bf16[384,1024]{1,0:T(8,128)(2,1)S(1)}, bf16[384,1024]{1,0:T(8,128)(2,1)S(1)}, u32[]{:S(2)}, u32[]{:S(2)}) collective-permute-start(bf16[384,1024]{1,0:T(8,128)(2,1)S(1)} %get-tuple-element.40), channel_id=1, source_target_pairs={{0,1},{1,0},{2,3},{3,2},{4,5},{5,4},{6,7},{7,6},{8,9},{9,8},{10,11... | collective-permute-start | bytes 2359304 | tf_op jit(solution)/shard_map/ppermute | solution.py:111
  59.5 24.5 %collective-permute-start.13 = (bf16[192,1024]{1,0:T(8,128)(2,1)S(1)}, bf16[192,1024]{1,0:T(8,128)(2,1)S(1)}, u32[]{:S(2)}, u32[]{:S(2)}) collective-permute-start(bf16[192,1024]{1,0:T(8,128)(2,1)S(1)} %collective-permute-done.11.rest_2_.refs_1_), channel_id=1, source_target_pairs={{4,0},{8,12},{5,1},{9,13},{6,2},{10,14},{7,3},{11,15},{20,16},{24,... | collective-permute-start | bytes 1179656 | tf_op jit(solution)/shard_map/ppermute | solution.py:115
  74.1 14.6 %collective-permute-start.18 = (bf16[256,2048]{1,0:T(8,128)(2,1)S(1)}, bf16[256,2048]{1,0:T(8,128)(2,1)S(1)}, u32[]{:S(2)}, u32[]{:S(2)}) collective-permute-start(bf16[256,2048]{1,0:T(8,128)(2,1)S(1)} %copy-done.6), channel_id=1, source_target_pairs={{0,1},{1,0},{2,3},{3,2},{4,5},{5,4},{6,7},{7,6},{8,9},{9,8},{10,11... | collective-permute-start | bytes 3145736 | tf_op jit(solution)/shard_map/ppermute | solution.py:111
  90.5 12.0 %collective-permute-start.19 = (bf16[192,1024]{1,0:T(8,128)(2,1)S(1)}, bf16[192,1024]{1,0:T(8,128)(2,1)S(1)}, u32[]{:S(2)}, u32[]{:S(2)}) collective-permute-start(bf16[192,1024]{1,0:T(8,128)(2,1)S(1)} %get-tuple-element.53), channel_id=1, source_target_pairs={{0,2},{1,3},{2,0},{3,1},{4,6},{5,7},{6,4},{7,5},{8,10},{9,11},{10,... | collective-permute-start | bytes 1179656 | tf_op jit(solution)/shard_map/ppermute | solution.py:107
  93.0 17.8 %collective-permute-start.21 = (bf16[192,1024]{1,0:T(8,128)(2,1)S(1)}, bf16[192,1024]{1,0:T(8,128)(2,1)S(1)}, u32[]{:S(2)}, u32[]{:S(2)}) collective-permute-start(bf16[192,1024]{1,0:T(8,128)(2,1)S(1)} %get-tuple-element.56), channel_id=1, source_target_pairs={{0,2},{1,3},{2,0},{3,1},{4,6},{5,7},{6,4},{7,5},{8,10},{9,11},{10,... | collective-permute-start | bytes 1179656 | tf_op jit(solution)/shard_map/ppermute | solution.py:107
  102.5 15.5 %collective-permute-start.23 = (bf16[192,1024]{1,0:T(8,128)(2,1)S(1)}, bf16[192,1024]{1,0:T(8,128)(2,1)S(1)}, u32[]{:S(2)}, u32[]{:S(2)}) collective-permute-start(bf16[192,1024]{1,0:T(8,128)(2,1)S(1)} %add_convert_fusion.4), channel_id=1, source_target_pairs={{0,4},{12,8},{1,5},{13,9},{2,6},{14,10},{3,7},{15,11},{16,20},{28,... | collective-permute-start | bytes 1179656 | tf_op jit(solution)/shard_map/ppermute | solution.py:115
  108.6 13.1 %collective-permute-start.26 = (bf16[192,1024]{1,0:T(8,128)(2,1)S(1)}, bf16[192,1024]{1,0:T(8,128)(2,1)S(1)}, u32[]{:S(2)}, u32[]{:S(2)}) collective-permute-start(bf16[192,1024]{1,0:T(8,128)(2,1)S(1)} %get-tuple-element.60), channel_id=1, source_target_pairs={{0,2},{1,3},{2,0},{3,1},{4,6},{5,7},{6,4},{7,5},{8,10},{9,11},{10,... | collective-permute-start | bytes 1179656 | tf_op jit(solution)/shard_map/ppermute | solution.py:107
  110.1 14.2 %collective-permute-start.20 = (bf16[192,1024]{1,0:T(8,128)(2,1)S(1)}, bf16[192,1024]{1,0:T(8,128)(2,1)S(1)}, u32[]{:S(2)}, u32[]{:S(2)}) collective-permute-start(bf16[192,1024]{1,0:T(8,128)(2,1)S(1)} %add_convert_fusion.4), channel_id=1, source_target_pairs={{4,8},{8,4},{5,9},{9,5},{6,10},{10,6},{7,11},{11,7},{20,24},{24,20... | collective-permute-start | bytes 1179656 | tf_op jit(solution)/shard_map/ppermute | solution.py:115
  110.9 16.6 %collective-permute-start.22 = (bf16[192,1024]{1,0:T(8,128)(2,1)S(1)}, bf16[192,1024]{1,0:T(8,128)(2,1)S(1)}, u32[]{:S(2)}, u32[]{:S(2)}) collective-permute-start(bf16[192,1024]{1,0:T(8,128)(2,1)S(1)} %add_convert_fusion.3.refs_0_), channel_id=1, source_target_pairs={{0,8},{12,4},{1,9},{13,5},{2,10},{14,6},{3,11},{15,7},{16,24},{28,... | collective-permute-start | bytes 1179656 | tf_op jit(solution)/shard_map/ppermute | solution.py:115
  118.2 19.7 %collective-permute-start.24 = (bf16[192,1024]{1,0:T(8,128)(2,1)S(1)}, bf16[192,1024]{1,0:T(8,128)(2,1)S(1)}, u32[]{:S(2)}, u32[]{:S(2)}) collective-permute-start(bf16[192,1024]{1,0:T(8,128)(2,1)S(1)} %add_convert_fusion.2), channel_id=1, source_target_pairs={{4,12},{8,0},{5,13},{9,1},{6,14},{10,2},{7,15},{11,3},{20,28},{24,... | collective-permute-start | bytes 1179656 | tf_op jit(solution)/shard_map/ppermute | solution.py:115
  120.1 18.0 %collective-permute-start.25 = (bf16[192,1024]{1,0:T(8,128)(2,1)S(1)}, bf16[192,1024]{1,0:T(8,128)(2,1)S(1)}, u32[]{:S(2)}, u32[]{:S(2)}) collective-permute-start(bf16[192,1024]{1,0:T(8,128)(2,1)S(1)} %get-tuple-element.58), channel_id=1, source_target_pairs={{0,2},{1,3},{2,0},{3,1},{4,6},{5,7},{6,4},{7,5},{8,10},{9,11},{10,... | collective-permute-start | bytes 1179656 | tf_op jit(solution)/shard_map/ppermute | solution.py:107
  121.7 18.9 %collective-permute-start.27 = (bf16[192,1024]{1,0:T(8,128)(2,1)S(1)}, bf16[192,1024]{1,0:T(8,128)(2,1)S(1)}, u32[]{:S(2)}, u32[]{:S(2)}) collective-permute-start(bf16[192,1024]{1,0:T(8,128)(2,1)S(1)} %add_convert_fusion.1), channel_id=1, source_target_pairs={{0,4},{4,0},{8,12},{12,8},{1,5},{5,1},{9,13},{13,9},{2,6},{6,2},{1... | collective-permute-start | bytes 1179656 | tf_op jit(solution)/shard_map/ppermute | solution.py:115
  (27 other events, 126.3 us)
